TPU v7x, 32 devices: a whole 2x2x4 slice. The times are simulated.
32 devices in a mesh: space: 8 (over y, x, core), dp: 4 (over z).
Axes of the slice: x: 2, y: 2, z: 4, core: 2. Of those that a mesh axis runs over, the one named last changes fastest.
Arguments:
- tokens: bfloat16 [18432, 512], P(('space', 'dp')), may hold values from -6 to 6
- gain: float32 [512], replicated, may hold values from 0.25 to 1.75
- w_in: bfloat16 [8, 512, 1024], P('space'), may hold values from -0.25 to 0.25
- w_out: bfloat16 [8, 1024, 512], P('space'), may hold values from -0.1875 to 0.1875
- expert_ids: int32 [18432, 1], P(('space', 'dp')), may hold values from 0 to 7
- gate: bfloat16 [18432], P(('space', 'dp')), may hold values from 0.25 to 1
- grad_out: bfloat16 [18432, 512], P(('space', 'dp')), may hold values from -6 to 6
Outputs:
- grad_tokens: bfloat16 [18432, 512], P(('space', 'dp'))
- grad_gate: bfloat16 [18432], P(('space', 'dp'))
- grad_w_in: float32 [8, 512, 1024], P('space', 'dp')
- grad_w_out: float32 [8, 1024, 512], P('space', 'dp')
All inputs are finite; a program needn't handle non-finite values.
Results may differ from a plain program's by a relative error of at most 0.02.
Values may be sent and summed in bfloat16 or wider, within the bound.
No kernel may reach another device: no remote copies, remote signals or barrier semaphores. Data moves between devices by JAX's collectives and lax.ppermute only.
A program may use at most 64 MiB of HBM per device.

v0:
```python
import jax
import jax.numpy as jnp
from jax import lax
from jax.sharding import PartitionSpec as P

epsilon = 1e-05


def normalize(tokens, gain):
    values = tokens.astype(jnp.float32)
    center = values - jnp.mean(values, axis=-1, keepdims=True)
    spread = lax.rsqrt(jnp.mean(center * center, axis=-1, keepdims=True) + epsilon)
    scaled = center * spread
    return (scaled, spread, (scaled * gain).astype(jnp.bfloat16))


def slot_ranks(routes, experts):
    onehot = (routes[:, None] == jnp.arange(experts, dtype=jnp.int32)[None, :]).astype(jnp.int32)
    before = jnp.cumsum(onehot, axis=0) - onehot
    return jnp.sum(before * onehot, axis=1)


def norm_backward(grad_norm, scaled, spread, gain):
    scaled_grad = grad_norm.astype(jnp.float32) * gain
    grad_mean = jnp.mean(scaled_grad, axis=-1, keepdims=True)
    grad_cross = jnp.mean(scaled_grad * scaled, axis=-1, keepdims=True)
    return spread * (scaled_grad - grad_mean - scaled * grad_cross)


def transpose_dot(left, right):
    return lax.dot_general(
        left, right, (((0,), (0,)), ((), ())), preferred_element_type=jnp.float32
    )


def right_dot(left, right):
    return lax.dot_general(
        left, right, (((1,), (1,)), ((), ())), preferred_element_type=jnp.float32
    )


def body(tokens, gain, w_in, w_out, expert_ids, gate, grad_out):
    sources = lax.axis_size("space")
    tok_rows = tokens.shape[0]
    model_width = tokens.shape[1]
    capacity = ((tok_rows * 5 // 4 + sources - 1) // sources + 7) // 8 * 8
    scaled, spread, normed = normalize(tokens, gain)
    routes = expert_ids[:, 0]
    slot_rank = slot_ranks(routes, sources)
    kept_mask = slot_rank < capacity
    target = jnp.where(kept_mask, routes * capacity + slot_rank, sources * capacity)
    row_index = jnp.minimum(target, sources * capacity - 1)
    grad_float = grad_out.astype(jnp.float32)
    weight_in = w_in[0]
    weight_out = w_out[0]

    def place_rows(rows):
        blank_rows = jnp.zeros((sources * capacity,) + rows.shape[1:], rows.dtype)
        placed = blank_rows.at[target].set(rows, mode="drop")
        return placed.reshape((sources, capacity) + rows.shape[1:])

    all_rows = sources * capacity
    delta = (gate[:, None].astype(jnp.float32) * grad_float).astype(jnp.bfloat16)
    normed_blocks, delta_blocks = (
        lax.all_to_all(place_rows(normed), "space", split_axis=0, concat_axis=0, tiled=True),
        lax.all_to_all(place_rows(delta), "space", split_axis=0, concat_axis=0, tiled=True),
    )
    normed_rows = normed_blocks.reshape(all_rows, model_width)
    delta_rows = delta_blocks.reshape(all_rows, model_width)
    preact = jnp.dot(normed_rows, weight_in, preferred_element_type=jnp.float32)
    act_float, gelu_back = jax.vjp(jax.nn.gelu, preact)
    activity = act_float.astype(jnp.bfloat16)
    token_out = jnp.dot(activity, weight_out, preferred_element_type=jnp.float32).astype(
        jnp.bfloat16
    )
    grad_activity = right_dot(delta_rows, weight_out)
    grad_preact = gelu_back(grad_activity)[0].astype(jnp.bfloat16)
    grad_normed = right_dot(grad_preact, weight_in).astype(jnp.bfloat16)
    activity, token_out, grad_preact, grad_normed = (activity, token_out, grad_preact, grad_normed)
    grad_back, out_back = (
        lax.all_to_all(
            grad_normed.reshape(sources, capacity, model_width),
            "space",
            split_axis=0,
            concat_axis=0,
            tiled=True,
        ),
        lax.all_to_all(
            token_out.reshape(sources, capacity, model_width),
            "space",
            split_axis=0,
            concat_axis=0,
            tiled=True,
        ),
    )
    token_grad = grad_back.reshape(sources * capacity, model_width)[row_index]
    token_result = out_back.reshape(sources * capacity, model_width)[row_index]
    product_sum = jnp.sum(grad_float * token_result.astype(jnp.float32), axis=1)
    grad_gate = jnp.where(kept_mask, product_sum, 0.0).astype(jnp.bfloat16)
    part_in = transpose_dot(normed_rows, grad_preact)
    part_out = transpose_dot(activity, delta_rows)
    grad_in, grad_out_weight = (
        lax.psum_scatter(
            part_in.astype(jnp.bfloat16), "dp", scatter_dimension=0, tiled=True
        ).astype(jnp.float32),
        lax.psum_scatter(
            part_out.astype(jnp.bfloat16), "dp", scatter_dimension=0, tiled=True
        ).astype(jnp.float32),
    )
    branch = jnp.where(kept_mask[:, None], norm_backward(token_grad, scaled, spread, gain), 0.0)
    grad_tokens = (grad_float + branch).astype(jnp.bfloat16)
    return (grad_tokens, grad_gate, grad_in[None], grad_out_weight[None])


def solution(mesh):
    placed = (
        P(("space", "dp"), None),
        P(),
        P("space", None, None),
        P("space", None, None),
        P(("space", "dp"), None),
        P(("space", "dp")),
        P(("space", "dp"), None),
    )
    return jax.shard_map(
        body,
        mesh=mesh,
        in_specs=placed,
        out_specs=(
            P(("space", "dp"), None),
            P(("space", "dp")),
            P("space", "dp", None),
            P("space", "dp", None),
        ),
        check_vma=False,
    )
```

profile of v0, /device:TPU:0, one launch (start us, length us, event | category | flops | bytes accessed | tf_op | source)
XLA Modules:
  0.0 123.6 jit_solution(15359349707318723510)
XLA Ops:
  7.2 1.4 %convert_reduce_fusion = f32[576]{0:T(1024)S(1)} fusion(bf16[576,512]{1,0:T(8,128)(2,1)} %param.7), kind=kLoop, calls=%fused_computation.20 | loop fusion | flops 589248 | bytes 592128 | tf_op jit(solution)/shard_map/reduce_sum | solution.py:11
  8.6 1.4 %fusion.17 = f32[576]{0:T(1024)S(1)} fusion(bf16[576,512]{1,0:T(8,128)(2,1)} %param.7, f32[576]{0:T(1024)S(1)} %broadcast_multiply_fusion.2), kind=kLoop, calls=%fused_computation.33 | loop fusion | flops 1179072 | bytes 594432 | tf_op jit(solution)/shard_map/reduce_sum | solution.py:12
  10.0 0.7 reduce
  10.7 1.4 %reduce-window.6 = s32[8,5,128]{2,0,1:T(8,128)S(1)} reduce-window(s32[8,5,128]{2,0,1:T(8,128)S(1)} %convert_bitcast_fusion, s32[]{:T(128)} %constant.9.clone.1), window={size=1x1x128 pad=0_0x0_0x127_0}, to_apply=%region_0.0 | reduce-window | flops 650240 | bytes 40964 | tf_op jit(solution)/shard_map/reduce-window
  12.7 0.7 fusion.43
  13.4 7.6 %scatter_custom_fusion.1 = bf16[768,512]{1,0:T(8,128)(2,1)} fusion(s32[576]{0:T(1024)S(1)} %get-tuple-element.7, bf16[576,512]{1,0:T(8,128)(2,1)} %param.7, f32[512]{0:T(512)} %param.8, f32[576]{0:T(1024)S(1)} %add_rsqrt_fusion, f32[576]{0:T(1024)S(1)} %broadcast_multiply_fusion.2, bf16[]{:T(256)} %constant.14.clone.1), kind=kCustom, calls=%fused_computation.46 | custom fusion | flops 1474560 | bytes 1386498 | tf_op jit(solution)/shard_map/scatter | solution.py:59
  21.0 5.3 %all-to-all-start.1 = ((bf16[8,96,512]{2,1,0:T(8,128)(2,1)}), bf16[8,96,512]{2,1,0:T(8,128)(2,1)S(1)}, u32[]{:S(2)}, u32[]{:S(2)}) async-start(bf16[8,96,512]{2,1,0:T(8,128)(2,1)} %bitcast.7), calls=%async_computation.1 | async-start | bytes 1572864 | tf_op jit(solution)/shard_map/all_to_all | solution.py:65
  26.3 9.1 %scatter_custom_fusion = bf16[768,512]{1,0:T(8,128)(2,1)} fusion(s32[576]{0:T(1024)S(1)} %get-tuple-element.7, bf16[576,512]{1,0:T(8,128)(2,1)S(1)} %copy-done.2, f32[576]{0:T(1024)S(1)} %convert_element_type.55, bf16[]{:T(256)} %constant.14.clone.1), kind=kCustom, calls=%fused_computation.45 | custom fusion | flops 884736 | bytes 1380354 | tf_op jit(solution)/shard_map/scatter | solution.py:59
  35.4 3.5 %all-to-all-done.1 = bf16[8,96,512]{2,1,0:T(8,128)(2,1)S(1)} async-done(((bf16[8,96,512]{2,1,0:T(8,128)(2,1)}), bf16[8,96,512]{2,1,0:T(8,128)(2,1)S(1)}, u32[]{:S(2)}, u32[]{:S(2)}) %all-to-all-start.1) | async-done | bytes 786464 | tf_op jit(solution)/shard_map/all_to_all | solution.py:65
  38.9 4.2 %all-to-all-start = ((bf16[8,96,512]{2,1,0:T(8,128)(2,1)}), bf16[8,96,512]{2,1,0:T(8,128)(2,1)}, u32[]{:S(2)}, u32[]{:S(2)}) async-start(bf16[8,96,512]{2,1,0:T(8,128)(2,1)} %bitcast.4), calls=%async_computation | async-start | bytes 1572864 | tf_op jit(solution)/shard_map/all_to_all | solution.py:66
  43.1 0.2 reduce-scatter.5.cloned.1.call-start
  43.3 2.6 %fusion.23 = f32[768,1024]{1,0:T(8,128)} fusion(bf16[768,512]{1,0:T(8,128)(2,1)S(1)} %bitcast.44, bf16[1,512,1024]{2,1,0:T(8,128)(2,1)S(1)} %copy-done.4), kind=kOutput, calls=%fused_computation.40 | convolution fusion | flops 805306368 | bytes 4980736 | tf_op jit(solution)/shard_map/dot_general | solution.py:70
  46.0 9.7 %all-to-all-done = bf16[8,96,512]{2,1,0:T(8,128)(2,1)} async-done(((bf16[8,96,512]{2,1,0:T(8,128)(2,1)}), bf16[8,96,512]{2,1,0:T(8,128)(2,1)}, u32[]{:S(2)}, u32[]{:S(2)}) %all-to-all-start) | async-done | bytes 786464 | tf_op jit(solution)/shard_map/all_to_all | solution.py:66
  55.7 4.4 %convolution_convert_fusion = bf16[1024,512]{1,0:T(8,128)(2,1)} fusion(bf16[768,512]{1,0:T(8,128)(2,1)} %bitcast.5, f32[768,1024]{1,0:T(8,128)} %fusion.23), kind=kOutput, calls=%fused_computation.17 | convolution fusion | flops 812908544 | bytes 4980736 | tf_op jit(solution)/shard_map/dot_general | solution.py:31
  60.1 3.9 %convolution_convert_fusion.2 = bf16[768,512]{1,0:T(8,128)(2,1)} fusion(bf16[1,1024,512]{2,1,0:T(8,128)(2,1)S(1)} %copy-done, f32[768,1024]{1,0:T(8,128)} %fusion.23), kind=kOutput, calls=%fused_computation.26 | convolution fusion | flops 812777472 | bytes 4980736 | tf_op jit(solution)/shard_map/dot_general | solution.py:73
  64.0 3.5 %all-to-all-start.3 = ((bf16[8,96,512]{2,1,0:T(8,128)(2,1)}), bf16[8,96,512]{2,1,0:T(8,128)(2,1)S(1)}, u32[]{:S(2)}, u32[]{:S(2)}) async-start(bf16[8,96,512]{2,1,0:T(8,128)(2,1)} %bitcast.12), calls=%async_computation.3 | async-start | bytes 1572864 | tf_op jit(solution)/shard_map/all_to_all | solution.py:88
  67.6 4.5 %fusion.6 = bf16[768,1024]{1,0:T(8,128)(2,1)S(1)} fusion(f32[768,1024]{1,0:T(8,128)} %fusion.23, bf16[768,512]{1,0:T(8,128)(2,1)} %bitcast.5, bf16[1,1024,512]{2,1,0:T(8,128)(2,1)S(1)} %copy-done), kind=kOutput, calls=%fused_computation.12 | convolution fusion | flops 821035008 | bytes 6553600 | tf_op jit(solution)/shard_map/dot_general | solution.py:37
  72.1 1.1 copy-done.7
  73.3 2.0 %convolution_convert_fusion.1 = bf16[512,1024]{1,0:T(8,128)(2,1)} fusion(bf16[768,512]{1,0:T(8,128)(2,1)S(1)} %bitcast.45, bf16[768,1024]{1,0:T(8,128)(2,1)S(1)} %fusion.6), kind=kOutput, calls=%fused_computation.18 | convolution fusion | flops 805830656 | bytes 3407872 | tf_op jit(solution)/shard_map/dot_general | solution.py:31
  75.2 3.6 %convolution_convert_fusion.3 = bf16[768,512]{1,0:T(8,128)(2,1)} fusion(bf16[768,1024]{1,0:T(8,128)(2,1)} %copy-done.7, bf16[1,512,1024]{2,1,0:T(8,128)(2,1)} %param.9), kind=kOutput, calls=%fused_computation.27 | convolution fusion | flops 805699584 | bytes 3407872 | tf_op jit(solution)/shard_map/dot_general | solution.py:37
  78.9 1.2 all-to-all-done.3
  80.1 3.5 %all-to-all-start.2 = ((bf16[8,96,512]{2,1,0:T(8,128)(2,1)}), bf16[8,96,512]{2,1,0:T(8,128)(2,1)S(1)}, u32[]{:S(2)}, u32[]{:S(2)}) async-start(bf16[8,96,512]{2,1,0:T(8,128)(2,1)} %bitcast.10), calls=%async_computation.2 | async-start | bytes 1572864 | tf_op jit(solution)/shard_map/all_to_all | solution.py:81
  83.7 3.3 %gather_fusion.1 = bf16[576,512]{1,0:T(8,128)(2,1)} fusion(bf16[768,512]{1,0:T(8,128)(2,1)S(1)} %bitcast.42, s32[1024]{0:T(1024)S(1)} %pad_clamp_fusion), kind=kCustom, calls=%fused_computation.1 | custom fusion | bytes 1181952 | tf_op jit(solution)/shard_map/gather | solution.py:97
  86.9 9.3 %all-to-all-done.2 = bf16[8,96,512]{2,1,0:T(8,128)(2,1)S(1)} async-done(((bf16[8,96,512]{2,1,0:T(8,128)(2,1)}), bf16[8,96,512]{2,1,0:T(8,128)(2,1)S(1)}, u32[]{:S(2)}, u32[]{:S(2)}) %all-to-all-start.2) | async-done | bytes 786464 | tf_op jit(solution)/shard_map/all_to_all | solution.py:81
  96.2 2.7 %gather_fusion = bf16[576,512]{1,0:T(8,128)(2,1)S(1)} fusion(bf16[768,512]{1,0:T(8,128)(2,1)S(1)} %bitcast.43, s32[1024]{0:T(1024)S(1)} %pad_clamp_fusion), kind=kCustom, calls=%fused_computation | custom fusion | bytes 1181952 | tf_op jit(solution)/shard_map/gather | solution.py:96
  99.0 1.6 %fusion.20 = bf16[576]{0:T(1024)(128)(2,1)S(1)} fusion(bf16[576,512]{1,0:T(8,128)(2,1)} %param.13, bf16[576,512]{1,0:T(8,128)(2,1)} %gather_fusion.1), kind=kLoop, calls=%fused_computation.36 | loop fusion | flops 1179072 | bytes 1180800 | tf_op jit(solution)/shard_map/reduce_sum | solution.py:98
  100.5 0.5 fusion.21
  101.1 0.6 select_convert_fusion
  101.7 1.4 %fusion.19 = bf16[576,512]{1,0:T(8,128)(2,1)} fusion(bf16[576,512]{1,0:T(8,128)(2,1)S(1)} %copy-done.1, bf16[576,512]{1,0:T(8,128)(2,1)S(1)} %copy-done.3, bf16[576,512]{1,0:T(8,128)(2,1)S(1)} %gather_fusion, f32[576]{0:T(1024)S(1)} %get-tuple-element.10, f32[576]{0:T(1024)S(1)} %get-tuple-element.11, f32[512]{0:T(512)S(1)} %copy-done.5, ...), kind=kLoop, calls=%fused_computation.35 | loop fusion | flops 3833856 | bytes 2371136 | tf_op jit(solution)/shard_map/convert_element_type | solution.py:111
  103.1 1.8 %bitcast_convert_fusion = f32[1,256,512]{2,1,0:T(8,128)} fusion(bf16[256,512]{1,0:T(8,128)(2,1)} %reduce-scatter.5.cloned.1.call-done), kind=kLoop, calls=%fused_computation.53 | loop fusion | flops 131072 | bytes 786432 | tf_op jit(solution)/shard_map/broadcast_in_dim | solution.py:112
  104.9 10.1 %reduce-scatter.3.cloned.1.call-done = bf16[128,1024]{1,0:T(8,128)(2,1)} async-done(((bf16[512,1024]{1,0:T(8,128)(2,1)}), bf16[128,1024]{1,0:T(8,128)(2,1)}) %reduce-scatter.3.cloned.1.call-update) | async-done | bytes 262160 | tf_op jit(solution)/shard_map/reduce_scatter | solution.py:103
  115.0 1.8 %bitcast_convert_fusion.1 = f32[1,128,1024]{2,1,0:T(8,128)} fusion(bf16[128,1024]{1,0:T(8,128)(2,1)} %reduce-scatter.3.cloned.1.call-done), kind=kLoop, calls=%fused_computation.54 | loop fusion | flops 131072 | bytes 786432 | tf_op jit(solution)/shard_map/broadcast_in_dim | solution.py:112
  (32 shorter events, 0.7 us)
Async XLA Ops:
  7.2 52.9 %copy-start = (bf16[1,1024,512]{2,1,0:T(8,128)(2,1)S(1)}, bf16[1,1024,512]{2,1,0:T(8,128)(2,1)}, u32[]{:S(2)}) copy-start(bf16[1,1024,512]{2,1,0:T(8,128)(2,1)} %param.10) | copy-start | bytes 3145732
  7.2 19.1 %copy-start.6 = (bf16[576]{0:T(1024)(128)(2,1)S(1)}, bf16[576]{0:T(1024)(128)(2,1)}, u32[]{:S(2)}) copy-start(bf16[576]{0:T(1024)(128)(2,1)} %param.12) | copy-start | bytes 3460
  7.2 19.1 %copy-start.2 = (bf16[576,512]{1,0:T(8,128)(2,1)S(1)}, bf16[576,512]{1,0:T(8,128)(2,1)}, u32[]{:S(2)}) copy-start(bf16[576,512]{1,0:T(8,128)(2,1)} %param.13) | copy-start | bytes 1769476
  21.0 22.4 %copy-start.4 = (bf16[1,512,1024]{2,1,0:T(8,128)(2,1)S(1)}, bf16[1,512,1024]{2,1,0:T(8,128)(2,1)}, u32[]{:S(2)}) copy-start(bf16[1,512,1024]{2,1,0:T(8,128)(2,1)} %param.9) | copy-start | bytes 3145732
  21.0 17.9 %all-to-all-start.1 = ((bf16[8,96,512]{2,1,0:T(8,128)(2,1)}), bf16[8,96,512]{2,1,0:T(8,128)(2,1)S(1)}, u32[]{:S(2)}, u32[]{:S(2)}) async-start(bf16[8,96,512]{2,1,0:T(8,128)(2,1)} %bitcast.7), calls=%async_computation.1 | async-start | bytes 1572864 | tf_op jit(solution)/shard_map/all_to_all | solution.py:65
  38.9 16.8 %all-to-all-start = ((bf16[8,96,512]{2,1,0:T(8,128)(2,1)}), bf16[8,96,512]{2,1,0:T(8,128)(2,1)}, u32[]{:S(2)}, u32[]{:S(2)}) async-start(bf16[8,96,512]{2,1,0:T(8,128)(2,1)} %bitcast.4), calls=%async_computation | async-start | bytes 1572864 | tf_op jit(solution)/shard_map/all_to_all | solution.py:66
  43.1 60.0 %reduce-scatter.5.cloned.1.call-start = ((), (), s32[]{:S(2)}) async-start(), calls=%async_computation.7 | async-start | bytes 1310720 | tf_op jit(solution)/shard_map/reduce_scatter | solution.py:106
  64.0 16.1 %all-to-all-start.3 = ((bf16[8,96,512]{2,1,0:T(8,128)(2,1)}), bf16[8,96,512]{2,1,0:T(8,128)(2,1)S(1)}, u32[]{:S(2)}, u32[]{:S(2)}) async-start(bf16[8,96,512]{2,1,0:T(8,128)(2,1)} %bitcast.12), calls=%async_computation.3 | async-start | bytes 1572864 | tf_op jit(solution)/shard_map/all_to_all | solution.py:88
  67.6 47.4 %reduce-scatter.3.cloned.1.call-start = ((), (), s32[]{:S(2)}) async-start(), calls=%async_computation.6 | async-start | bytes 1310720 | tf_op jit(solution)/shard_map/reduce_scatter | solution.py:103
  72.1 1.2 copy-start.7
  80.1 16.1 %all-to-all-start.2 = ((bf16[8,96,512]{2,1,0:T(8,128)(2,1)}), bf16[8,96,512]{2,1,0:T(8,128)(2,1)S(1)}, u32[]{:S(2)}, u32[]{:S(2)}) async-start(bf16[8,96,512]{2,1,0:T(8,128)(2,1)} %bitcast.10), calls=%async_computation.2 | async-start | bytes 1572864 | tf_op jit(solution)/shard_map/all_to_all | solution.py:81
  96.2 4.3 %copy-start.1 = (bf16[576,512]{1,0:T(8,128)(2,1)S(1)}, bf16[576,512]{1,0:T(8,128)(2,1)}, u32[]{:S(2)}) copy-start(bf16[576,512]{1,0:T(8,128)(2,1)} %param.7) | copy-start | bytes 1769476
  96.2 4.3 %copy-start.5 = (f32[512]{0:T(512)S(1)}, f32[512]{0:T(512)}, u32[]{:S(2)}) copy-start(f32[512]{0:T(512)} %param.8) | copy-start | bytes 6148
  99.0 2.7 %copy-start.3 = (bf16[576,512]{1,0:T(8,128)(2,1)S(1)}, bf16[576,512]{1,0:T(8,128)(2,1)}, u32[]{:S(2)}) copy-start(bf16[576,512]{1,0:T(8,128)(2,1)} %param.13) | copy-start | bytes 1769476
Sparse Core Ops, SparseCore 0:
  60.2 26.4 reduce-scatter.4
  89.2 25.8 reduce-scatter.2
where the time goes:
time: 124 us
  waiting for transfers between devices  33.9 us (27%)
  other arithmetic  30.2 us (24%)
  matrix products  21 us (17%)
  starting transfers between devices  16.9 us (14%)
  between operations  14.2 us (11%)
  local copies, waits for them, and re-layouts  7.48 us (6%)
    scatter x2, other arithmetic, place_rows(): placed = blank_rows.at[target].set(rows, mode='drop')  16.6 us
    reduce_scatter x1, waiting for transfers between devices, body(): lax.psum_scatter(part_in.astype(jnp.bfloat16), 'dp', scatter_dimension=0,...  10.1 us
    all_to_all x1, waiting for transfers between devices, body(): lax.all_to_all(place_rows(delta), 'space', split_axis=0, concat_axis=0, t...  9.72 us
    all_to_all x1, waiting for transfers between devices, body(): lax.all_to_all(grad_normed.reshape(sources, capacity, model_width), 'spac...  9.26 us
    dot_general x2, matrix products, right_dot(): lax.dot_general(left, right, (((1,), (1,)), ((), ())), preferred_element_...  8.1 us
    dot_general x2, matrix products, transpose_dot(): lax.dot_general(left, right, (((0,), (0,)), ((), ())), preferred_element_...  6.34 us
    all_to_all x1, starting transfers between devices, body(): lax.all_to_all(place_rows(normed), 'space', split_axis=0, concat_axis=0,...  5.3 us
    all_to_all x1, starting transfers between devices, body(): lax.all_to_all(place_rows(delta), 'space', split_axis=0, concat_axis=0, t...  4.21 us
  transfers between devices with their start and end apart: 6, of which 5 were waited for; matrix products, arithmetic and copies ran while one was open for 30% of the time, Pallas kernels for 0%

commit v1 on v0

v1 whole, which is shorter than its diff:
```python
import functools

import jax
import jax.numpy as jnp
from jax import lax
from jax.experimental import pallas as pl
from jax.experimental.pallas import tpu as pltpu
from jax.sharding import PartitionSpec as P

epsilon = 1e-05
F32 = jnp.float32
BF16 = jnp.bfloat16
LANES = 128
VMEM_BYTES = 56 * 1024 * 1024

vmem = pl.BlockSpec(memory_space=pltpu.VMEM)
smem = pl.BlockSpec(memory_space=pltpu.SMEM)


def dot(left, right, contract=((1,), (0,))):
    return lax.dot_general(left, right, (contract, ((), ())), preferred_element_type=F32)


def normalize(tokens):
    values = tokens.astype(F32)
    center = values - jnp.mean(values, axis=-1, keepdims=True)
    spread = lax.rsqrt(jnp.mean(center * center, axis=-1, keepdims=True) + epsilon)
    return center * spread, spread


def kernel_call(kernel, name, flops, nbytes, outs, ins, scratch=(), transcendentals=0):
    return pl.pallas_call(
        kernel,
        name=name,
        out_shape=outs,
        in_specs=ins,
        out_specs=[vmem] * len(outs),
        scratch_shapes=list(scratch),
        compiler_params=pltpu.CompilerParams(vmem_limit_bytes=VMEM_BYTES),
        cost_estimate=pl.CostEstimate(
            flops=flops, bytes_accessed=nbytes, transcendentals=transcendentals
        ),
    )


def place_kernel(sources, capacity, me, ids_ref, gate_ref, tok_ref, gain_ref, go_ref, target_ref, *outs):
    rows = sources * capacity
    tok_rows, width = tok_ref.shape
    scaled, _ = normalize(tok_ref[...])
    normed = (scaled * gain_ref[...]).astype(BF16)
    ids = ids_ref[...]
    onehot = (lax.broadcasted_iota(jnp.int32, (sources, tok_rows), 0) == ids).astype(F32)
    earlier = lax.broadcasted_iota(jnp.int32, (tok_rows, tok_rows), 0) < lax.broadcasted_iota(
        jnp.int32, (tok_rows, tok_rows), 1
    )
    before = dot(onehot.astype(BF16), jnp.where(earlier, 1.0, 0.0).astype(BF16))
    rank = jnp.sum(before * onehot, axis=0, keepdims=True).astype(jnp.int32)
    target = jnp.where(rank < capacity, jnp.bitwise_xor(ids, me[0]) * capacity + rank, -1)
    target_ref[...] = target
    hit = lax.broadcasted_iota(jnp.int32, (rows, tok_rows), 0) == target
    pick = jnp.where(hit, 1.0, 0.0).astype(BF16)
    pick_gate = jnp.where(hit, gate_ref[...].astype(F32), 0.0).astype(BF16)
    placed_normed = dot(pick, normed).astype(BF16)
    placed_delta = dot(pick_gate, go_ref[...]).astype(BF16)
    for k in range(sources):
        block = slice(k * capacity, (k + 1) * capacity)
        outs[k][:, :width] = placed_normed[block]
        outs[k][:, width:] = placed_delta[block]


def gelu_parts(value):
    root = 0.7978845608028654
    square = value * value
    tan = jnp.tanh(root * (value + 0.044715 * value * square))
    half = 0.5 * (1.0 + tan)
    slope = half + 0.5 * value * (1.0 - tan * tan) * (root * (1.0 + 3.0 * 0.044715 * square))
    return value * half, slope


def grads_kernel(sources, capacity, pieces, order, w_in_ref, w_out_ref, *refs):
    blocks = refs[:sources]
    outs_in = refs[sources : sources + pieces]
    outs_out = refs[sources + pieces : sources + 2 * pieces]
    gpre_ref, extra_ref, x_ref, d_ref, xt_ref = refs[sources + 2 * pieces :]
    width, hidden = w_in_ref.shape
    piece_d, piece_f = width // pieces, hidden // pieces
    for k in range(sources):
        block = slice(k * capacity, (k + 1) * capacity)
        x_ref[block, :] = blocks[k][:, :width]
        d_ref[block, :] = blocks[k][:, width:]
    for j in range(pieces):
        start = pl.multiple_of(order[j] * piece_d, piece_d)
        xt_ref[j * piece_d : (j + 1) * piece_d, :] = x_ref[:, pl.ds(start, piece_d)].T
    total = jnp.zeros((sources * capacity, 1), F32)
    for j in range(pieces):
        part = pl.ds(pl.multiple_of(order[j] * piece_f, piece_f), piece_f)
        delta = d_ref[...]
        preact = dot(x_ref[...], w_in_ref[:, part])
        act_float, slope = gelu_parts(preact)
        act = act_float.astype(BF16)
        grad_act = dot(delta, w_out_ref[part, :], ((1,), (1,)))
        total += jnp.sum(act.astype(F32) * grad_act, axis=1, keepdims=True)
        grad_pre = (grad_act * slope).astype(BF16)
        gpre_ref[:, part] = grad_pre
        outs_out[j][...] = dot(act.T, delta).astype(BF16)
        weight = dot(xt_ref[...], grad_pre).astype(BF16)
        for i in range(pieces):
            outs_in[i][:, part] = weight[i * piece_d : (i + 1) * piece_d]
    high = total.astype(BF16).astype(F32)
    lane = lax.broadcasted_iota(jnp.int32, extra_ref.shape, 1)
    extra_ref[...] = jnp.where(lane == 0, high, jnp.where(lane == 1, total - high, 0.0)).astype(BF16)


def back_kernel(sources, capacity, gpre_ref, w_in_ref, extra_ref, *outs):
    width = w_in_ref.shape[0]
    grad = dot(gpre_ref[...], w_in_ref[...], ((1,), (1,))).astype(BF16)
    for k in range(sources):
        block = slice(k * capacity, (k + 1) * capacity)
        outs[k][:, :width] = grad[block]
        outs[k][:, width:] = extra_ref[block, :]


def finish_kernel(sources, capacity, target_ref, gate_ref, tok_ref, gain_ref, go_ref, *refs):
    blocks = refs[:sources]
    tokens_out, gate_out, back_ref = refs[sources:]
    rows = sources * capacity
    tok_rows, width = tok_ref.shape
    for k in range(sources):
        back_ref[k * capacity : (k + 1) * capacity, :] = blocks[k][...]
    spots = jnp.broadcast_to(target_ref[...].astype(F32), (8, tok_rows)).T[:, :1].astype(jnp.int32)
    hit = lax.broadcasted_iota(jnp.int32, (tok_rows, rows), 1) == spots
    got = dot(jnp.where(hit, 1.0, 0.0).astype(BF16), back_ref[...])
    sums = got[:, width:].T
    gate_out[...] = ((sums[0:1] + sums[1:2]) / gate_ref[...].astype(F32)).astype(BF16)
    scaled, spread = normalize(tok_ref[...])
    grad = got[:, :width] * gain_ref[...]
    mean = jnp.mean(grad, axis=-1, keepdims=True)
    cross = jnp.mean(grad * scaled, axis=-1, keepdims=True)
    branch = spread * (grad - mean - scaled * cross)
    tokens_out[...] = (go_ref[...].astype(F32) + branch).astype(BF16)


def swap_blocks(blocks):
    count = len(blocks)
    return [blocks[0]] + [
        lax.ppermute(blocks[k], "space", [(i, i ^ k) for i in range(count)]) for k in range(1, count)
    ]


def add(*terms):
    return functools.reduce(jnp.add, [t.astype(F32) for t in terms])


def line_sums(first, second, third, own, place):
    swapped = lax.ppermute(first, "dp", [(0, 1), (1, 0), (2, 3), (3, 2)])
    middle = lax.ppermute(second, "dp", [(1, 2), (2, 1)])
    across = lax.ppermute(second, "dp", [(0, 2), (3, 1)])
    inner = (place == 1) | (place == 2)
    passed = jnp.where(inner, add(third, swapped), third.astype(F32)).astype(BF16)
    last = lax.ppermute(passed, "dp", [(0, 1), (3, 2), (1, 3), (2, 0)])
    kept = jnp.where(inner, 0.0, swapped.astype(F32))
    return add(own, middle, across, kept, last)


def body(tokens, gain, w_in, w_out, expert_ids, gate, grad_out):
    sources = lax.axis_size("space")
    groups = lax.axis_size("dp")
    tok_rows, width = tokens.shape
    hidden = w_in.shape[2]
    capacity = ((tok_rows * 5 // 4 + sources - 1) // sources + 7) // 8 * 8
    rows = sources * capacity
    pieces = 4
    me = lax.axis_index("space").astype(jnp.int32).reshape(1)
    place = lax.axis_index("dp").astype(jnp.int32)
    ids_row = expert_ids.reshape(1, tok_rows)
    gate_row = gate.reshape(1, tok_rows)
    gain_row = gain.reshape(1, width)
    weight_in, weight_out = w_in[0], w_out[0]
    shape = jax.ShapeDtypeStruct
    io_bytes = 2 * (2 * tok_rows * width + 2 * rows * width)

    target, *sent = kernel_call(
        functools.partial(place_kernel, sources, capacity),
        "place",
        4 * rows * tok_rows * width,
        io_bytes,
        [shape((1, tok_rows), jnp.int32)] + [shape((capacity, 2 * width), BF16)] * sources,
        [smem] + [vmem] * 5,
    )(me, ids_row, gate_row, tokens, gain_row, grad_out)
    arrived = swap_blocks(sent)

    if groups == 4:
        first = jnp.where(place % 2 == 0, 3, 0)
        second = jnp.where(place < 2, 2, 1)
        order = jnp.stack([first, second, 6 - first - second - place, place]).astype(jnp.int32)
    else:
        order = jnp.arange(pieces, dtype=jnp.int32)
    *parts, gpre, extra = kernel_call(
        functools.partial(grads_kernel, sources, capacity, pieces),
        "grads",
        8 * rows * width * hidden,
        2 * (2 * rows * width + 4 * width * hidden + rows * hidden),
        [shape((width // pieces, hidden), BF16)] * pieces
        + [shape((hidden // pieces, width), BF16)] * pieces
        + [shape((rows, hidden), BF16), shape((rows, LANES), BF16)],
        [smem] + [vmem] * (2 + sources),
        [
            pltpu.VMEM((rows, width), BF16),
            pltpu.VMEM((rows, width), BF16),
            pltpu.VMEM((width, rows), BF16),
        ],
        rows * hidden,
    )(order, weight_in, weight_out, *arrived)
    parts_in, parts_out = parts[:pieces], parts[pieces:]

    returned = kernel_call(
        functools.partial(back_kernel, sources, capacity),
        "back",
        2 * rows * width * hidden,
        2 * (rows * hidden + width * hidden + rows * width),
        [shape((capacity, width + LANES), BF16)] * sources,
        [vmem] * 3,
    )(gpre, weight_in, extra)

    if groups == 4:
        grad_w_out = line_sums(*parts_out, place)
        grad_w_in = line_sums(*parts_in, place)
    else:
        grad_w_in, grad_w_out = (
            lax.psum_scatter(
                jnp.concatenate(part), "dp", scatter_dimension=0, tiled=True
            ).astype(F32)
            for part in (parts_in, parts_out)
        )
    back = swap_blocks(returned)
    grad_tokens, grad_gate = kernel_call(
        functools.partial(finish_kernel, sources, capacity),
        "finish",
        2 * rows * tok_rows * width,
        io_bytes,
        [shape((tok_rows, width), BF16), shape((1, tok_rows), BF16)],
        [vmem] * (5 + sources),
        [pltpu.VMEM((rows, width + LANES), BF16)],
    )(target, gate_row, tokens, gain_row, grad_out, *back)
    return (grad_tokens, grad_gate.reshape(tok_rows), grad_w_in[None], grad_w_out[None])


def solution(mesh):
    placed = (
        P(("space", "dp"), None),
        P(),
        P("space", None, None),
        P("space", None, None),
        P(("space", "dp"), None),
        P(("space", "dp")),
        P(("space", "dp"), None),
    )
    return jax.shard_map(
        body,
        mesh=mesh,
        in_specs=placed,
        out_specs=(
            P(("space", "dp"), None),
            P(("space", "dp")),
            P("space", "dp", None),
            P("space", "dp", None),
        ),
        check_vma=False,
    )
```

time: 124 us -> 97.8 us (0.79)
  other arithmetic: 30.2 us -> 4.05 us
  matrix products: 21 us -> 0 us
  Pallas kernels: 0 us -> 20.1 us
  starting transfers between devices: 16.9 us -> 34.3 us
  between operations: 14.2 us -> 0.92 us
  local copies, waits for them, and re-layouts: 7.48 us -> 2.6 us
  waiting for transfers between devices: 33.9 us -> 35.5 us
    ppermute x0 -> x22, waiting for transfers between devices: none -> 35.5 us  [the longest x2 20.1 us: line_sums(): last = lax.ppermute(passed, 'dp', [(0, 1), (3, 2), (1, 3), (2, 0)])]
    ppermute x0 -> x22, starting transfers between devices: none -> 34.3 us  [the longest x14 17.9 us: swap_blocks(): lax.ppermute(blocks[k], 'space', [(i, i ^ k) for i in range(count)])]
    all_to_all x4 -> x0, waiting for transfers between devices: 23.7 us -> none  [the longest x1 9.72 us: body(): lax.all_to_all(place_rows(delta), 'space', split_axis=0, concat_axis=0, t...]
    dot_general x6 -> x0, matrix products: 21 us -> none  [the longest x2 8.1 us: right_dot(): lax.dot_general(left, right, (((1,), (1,)), ((), ())), preferred_element_...]
    pallas_call x0 -> x4, Pallas kernels: none -> 20.1 us  [the longest x1 8.3 us: body(): kernel_call(functools.partial(grads_kernel, sources, capacity, pieces), '...]
    scatter x2 -> x0, other arithmetic: 16.6 us -> none  [place_rows(): placed = blank_rows.at[target].set(rows, mode='drop')]
    all_to_all x4 -> x0, starting transfers between devices: 16.6 us -> none  [the longest x1 5.3 us: body(): lax.all_to_all(place_rows(normed), 'space', split_axis=0, concat_axis=0,...]
    reduce_scatter x2 -> x0, waiting for transfers between devices: 10.1 us -> none  [the longest x1 10.1 us: body(): lax.psum_scatter(part_in.astype(jnp.bfloat16), 'dp', scatter_dimension=0,...]
  transfers between devices with their start and end apart: 6 -> 22, of which waited for: 5 -> 6; matrix products, arithmetic and copies ran while one was open for 30% -> 3% of each run, Pallas kernels for 0% -> 8%
where the time goes in v1:
time: 97.8 us; the launch traced here: 97.5 us
  waiting for transfers between devices  35.5 us (36%)
  starting transfers between devices  34.3 us (35%)
  Pallas kernels  20.1 us (21%)
  other arithmetic  4.05 us (4%)
  local copies, waits for them, and re-layouts  2.6 us (3%)
    ppermute x2, waiting for transfers between devices, line_sums(): last = lax.ppermute(passed, 'dp', [(0, 1), (3, 2), (1, 3), (2, 0)])  20.1 us
    ppermute x14, starting transfers between devices, swap_blocks(): lax.ppermute(blocks[k], 'space', [(i, i ^ k) for i in range(count)])  17.9 us
    ppermute x14, waiting for transfers between devices, swap_blocks(): lax.ppermute(blocks[k], 'space', [(i, i ^ k) for i in range(count)])  15.4 us
    ppermute x2, starting transfers between devices, line_sums(): across = lax.ppermute(second, 'dp', [(0, 2), (3, 1)])  8.64 us
    pallas_call x1, Pallas kernels, body(): kernel_call(functools.partial(grads_kernel, sources, capacity, pieces), '...  8.3 us
    ppermute x2, starting transfers between devices, line_sums(): last = lax.ppermute(passed, 'dp', [(0, 1), (3, 2), (1, 3), (2, 0)])  4.32 us
    pallas_call x1, Pallas kernels, body(): kernel_call(functools.partial(finish_kernel, sources, capacity), 'finish'...  4.19 us
    pallas_call x1, Pallas kernels, body(): kernel_call(functools.partial(place_kernel, sources, capacity), 'place',...  3.94 us
  transfers between devices with their start and end apart: 22, of which 6 were waited for; matrix products, arithmetic and copies ran while one was open for 3% of the time, Pallas kernels for 8%

profile of v1, /device:TPU:0, one launch (start us, length us, event | category | flops | bytes accessed | tf_op | source)
XLA Modules:
  0.0 97.5 jit_solution(12713758787565137194)
XLA Ops:
  0.6 1.3 %reshape.25.gate_ref = bf16[1,576]{1,0:T(2,128)(2,1)} reshape(bf16[576]{0:T(1024)(128)(2,1)} %param.12) | data formatting | bytes 2304 | tf_op jit(solution)/shard_map/reshape | solution.py:176
  1.9 3.9 %place.1 = (s32[1,576]{1,0:T(1,128)}, bf16[96,1024]{1,0:T(8,128)(2,1)}, bf16[96,1024]{1,0:T(8,128)(2,1)}, bf16[96,1024]{1,0:T(8,128)(2,1)}, bf16[96,1024]{1,0:T(...) custom-call(s32[1]{0:T(128)} %bitcast.me, ...), custom_call_target="tpu_custom_call" | custom-call | flops 905969664 | bytes 2752512 | tf_op jit(solution)/shard_map/place/pallas_call | solution.py:182
  5.8 0.5 collective-permute-start
  6.3 2.5 %collective-permute-start.1 = (bf16[96,1024]{1,0:T(8,128)(2,1)}, bf16[96,1024]{1,0:T(8,128)(2,1)S(1)}, u32[]{:S(2)}, u32[]{:S(2)}) collective-permute-start(bf16[96,1024]{1,0:T(8,128)(2,1)} %get-tuple-element.36), channel_id=1, source_target_pairs={{0,8},{4,12},{8,0},{12,4},{16,24},{20,28},{24,16},{28,20},{1,9},{5... | collective-permute-start | bytes 589832 | tf_op jit(solution)/shard_map/ppermute | solution.py:146
  8.9 1.7 %collective-permute-start.3 = (bf16[96,1024]{1,0:T(8,128)(2,1)}, bf16[96,1024]{1,0:T(8,128)(2,1)S(1)}, u32[]{:S(2)}, u32[]{:S(2)}) collective-permute-start(bf16[96,1024]{1,0:T(8,128)(2,1)} %get-tuple-element.38), channel_id=1, source_target_pairs={{0,16},{4,20},{8,24},{12,28},{16,0},{20,4},{24,8},{28,12},{1,17},{... | collective-permute-start | bytes 589832 | tf_op jit(solution)/shard_map/ppermute | solution.py:146
  10.7 2.6 %collective-permute-start.5 = (bf16[96,1024]{1,0:T(8,128)(2,1)}, bf16[96,1024]{1,0:T(8,128)(2,1)S(1)}, u32[]{:S(2)}, u32[]{:S(2)}) collective-permute-start(bf16[96,1024]{1,0:T(8,128)(2,1)} %get-tuple-element.40), channel_id=1, source_target_pairs={{0,24},{4,28},{8,16},{12,20},{16,8},{20,12},{24,0},{28,4},{1,25},{... | collective-permute-start | bytes 589832 | tf_op jit(solution)/shard_map/ppermute | solution.py:146
  13.2 1.5 %collective-permute-done.1.refs_2_ = bf16[96,1024]{1,0:T(8,128)(2,1)S(1)} collective-permute-done((bf16[96,1024]{1,0:T(8,128)(2,1)}, bf16[96,1024]{1,0:T(8,128)(2,1)S(1)}, u32[]{:S(2)}, u32[]{:S(2)}) %collective-permute-start.1) | collective-permute-done | bytes 196640 | tf_op jit(solution)/shard_map/ppermute | solution.py:146
  14.8 1.8 %collective-permute-start.6 = (bf16[96,1024]{1,0:T(8,128)(2,1)}, bf16[96,1024]{1,0:T(8,128)(2,1)S(1)}, u32[]{:S(2)}, u32[]{:S(2)}) collective-permute-start(bf16[96,1024]{1,0:T(8,128)(2,1)} %get-tuple-element.41), channel_id=1, source_target_pairs={{0,28},{4,24},{8,20},{12,16},{16,12},{20,8},{24,4},{28,0},{1,29},{... | collective-permute-start | bytes 589832 | tf_op jit(solution)/shard_map/ppermute | solution.py:146
  16.6 0.6 pad_add_fusion.order
  17.2 1.4 %collective-permute-done.2.refs_3_ = bf16[96,1024]{1,0:T(8,128)(2,1)S(1)} collective-permute-done((bf16[96,1024]{1,0:T(8,128)(2,1)}, bf16[96,1024]{1,0:T(8,128)(2,1)S(1)}, u32[]{:S(2)}, u32[]{:S(2)}) %collective-permute-start.2) | collective-permute-done | bytes 196640 | tf_op jit(solution)/shard_map/ppermute | solution.py:146
  18.6 9.6 %collective-permute-done.4.refs_5_ = bf16[96,1024]{1,0:T(8,128)(2,1)S(1)} collective-permute-done((bf16[96,1024]{1,0:T(8,128)(2,1)}, bf16[96,1024]{1,0:T(8,128)(2,1)S(1)}, u32[]{:S(2)}, u32[]{:S(2)}) %collective-permute-start.4) | collective-permute-done | bytes 196640 | tf_op jit(solution)/shard_map/ppermute | solution.py:146
  28.3 0.6 copy-done.17
  29.1 8.3 %grads.1 = (bf16[128,1024]{1,0:T(8,128)(2,1)}, bf16[128,1024]{1,0:T(8,128)(2,1)}, bf16[128,1024]{1,0:T(8,128)(2,1)}, bf16[128,1024]{1,0:T(8,128)(2,1)}, bf16[256...) custom-call(s32[4]{0:T(128)} %pad_add_fusion.order, ...), custom_call_target="tpu_custom_call" | custom-call | flops 3221225472 | bytes 7340032 | tf_op jit(solution)/shard_map/grads/pallas_call | solution.py:198
  37.4 1.6 %collective-permute-start.16 = (bf16[128,1024]{1,0:T(8,128)(2,1)}, bf16[128,1024]{1,0:T(8,128)(2,1)S(1)}, u32[]{:S(2)}, u32[]{:S(2)}) collective-permute-start(bf16[128,1024]{1,0:T(8,128)(2,1)} %get-tuple-element.56), channel_id=1, source_target_pairs={{0,1},{1,0},{2,3},{3,2},{4,5},{5,4},{6,7},{7,6},{8,9},{9,8},{10,11... | collective-permute-start | bytes 786440 | tf_op jit(solution)/shard_map/ppermute | solution.py:155
  39.0 3.7 %back.1 = (bf16[96,640]{1,0:T(8,128)(2,1)}, bf16[96,640]{1,0:T(8,128)(2,1)}, bf16[96,640]{1,0:T(8,128)(2,1)}, bf16[96,640]{1,0:T(8,128)(2,1)}, bf16[96,640]{1,0:...) custom-call(bf16[768,1024]{1,0:T(8,128)(2,1)} %get-tuple-element.42.gpre_ref, ...), custom_call_target="tpu_custom_call" | custom-call | flops 805306368 | bytes 3407872 | tf_op jit(solution)/shard_map/back/pallas_call | solution.py:216
  43.1 1.5 %collective-permute-start.8 = (bf16[96,640]{1,0:T(8,128)(2,1)}, bf16[96,640]{1,0:T(8,128)(2,1)S(1)}, u32[]{:S(2)}, u32[]{:S(2)}) collective-permute-start(bf16[96,640]{1,0:T(8,128)(2,1)} %get-tuple-element.46), channel_id=1, source_target_pairs={{0,8},{4,12},{8,0},{12,4},{16,24},{20,28},{24,16},{28,20},{1,9},{5... | collective-permute-start | bytes 368648 | tf_op jit(solution)/shard_map/ppermute | solution.py:146
  44.6 1.7 %collective-permute-start.10 = (bf16[96,640]{1,0:T(8,128)(2,1)}, bf16[96,640]{1,0:T(8,128)(2,1)S(1)}, u32[]{:S(2)}, u32[]{:S(2)}) collective-permute-start(bf16[96,640]{1,0:T(8,128)(2,1)} %get-tuple-element.48), channel_id=1, source_target_pairs={{0,16},{4,20},{8,24},{12,28},{16,0},{20,4},{24,8},{28,12},{1,17},{... | collective-permute-start | bytes 368648 | tf_op jit(solution)/shard_map/ppermute | solution.py:146
  46.6 2.9 %collective-permute-done.8.refs_2_ = bf16[96,640]{1,0:T(8,128)(2,1)S(1)} collective-permute-done((bf16[96,640]{1,0:T(8,128)(2,1)}, bf16[96,640]{1,0:T(8,128)(2,1)S(1)}, u32[]{:S(2)}, u32[]{:S(2)}) %collective-permute-start.8) | collective-permute-done | bytes 122912 | tf_op jit(solution)/shard_map/ppermute | solution.py:146
  49.5 2.4 %collective-permute-start.12 = (bf16[96,640]{1,0:T(8,128)(2,1)}, bf16[96,640]{1,0:T(8,128)(2,1)S(1)}, u32[]{:S(2)}, u32[]{:S(2)}) collective-permute-start(bf16[96,640]{1,0:T(8,128)(2,1)} %get-tuple-element.50), channel_id=1, source_target_pairs={{0,24},{4,28},{8,16},{12,20},{16,8},{20,12},{24,0},{28,4},{1,25},{... | collective-permute-start | bytes 368648 | tf_op jit(solution)/shard_map/ppermute | solution.py:146
  51.9 2.3 %collective-permute-start.13 = (bf16[96,640]{1,0:T(8,128)(2,1)}, bf16[96,640]{1,0:T(8,128)(2,1)S(1)}, u32[]{:S(2)}, u32[]{:S(2)}) collective-permute-start(bf16[96,640]{1,0:T(8,128)(2,1)} %get-tuple-element.51), channel_id=1, source_target_pairs={{0,28},{4,24},{8,20},{12,16},{16,12},{20,8},{24,4},{28,0},{1,29},{... | collective-permute-start | bytes 368648 | tf_op jit(solution)/shard_map/ppermute | solution.py:146
  54.8 4.6 %collective-permute-start.15 = (bf16[128,1024]{1,0:T(8,128)(2,1)S(1)}, bf16[128,1024]{1,0:T(8,128)(2,1)S(1)}, u32[]{:S(2)}, u32[]{:S(2)}) collective-permute-start(bf16[128,1024]{1,0:T(8,128)(2,1)S(1)} %copy-done.12), channel_id=1, source_target_pairs={{0,2},{3,1},{4,6},{7,5},{8,10},{11,9},{12,14},{15,13},{16,18},{19,... | collective-permute-start | bytes 786440 | tf_op jit(solution)/shard_map/ppermute | solution.py:157
  59.5 0.7 collective-permute-start.14
  60.2 4.0 %collective-permute-start.19 = (bf16[256,512]{1,0:T(8,128)(2,1)S(1)}, bf16[256,512]{1,0:T(8,128)(2,1)S(1)}, u32[]{:S(2)}, u32[]{:S(2)}) collective-permute-start(bf16[256,512]{1,0:T(8,128)(2,1)S(1)} %copy-done.11), channel_id=1, source_target_pairs={{0,2},{3,1},{4,6},{7,5},{8,10},{11,9},{12,14},{15,13},{16,18},{19,... | collective-permute-start | bytes 786440 | tf_op jit(solution)/shard_map/ppermute | solution.py:157
  64.4 0.5 copy-done.10
  64.9 4.2 %finish.1 = (bf16[576,512]{1,0:T(8,128)(2,1)}, bf16[1,576]{1,0:T(2,128)(2,1)}) custom-call(s32[1,576]{1,0:T(1,128)} %get-tuple-element.33.target_ref, bf16[1,576]{1,0:T(2,128)(2,1)} %reshape.25.gate_ref, bf16[576,512]{1,0:T(8,128)(2,1)} %tok_ref.3, f32[1,512]{1,0:T(1,128)} %bitcast.14, bf16[576,512]{1,0:T(8,128)(2,1)} %go_ref.3, ...), custom_call_target="tpu_custom_call" | custom-call | flops 452984832 | bytes 2752512 | tf_op jit(solution)/shard_map/finish/pallas_call | solution.py:236
  69.1 1.3 %reduce = bf16[576]{0:T(1024)(128)(2,1)} reduce(bf16[1,576]{1,0:T(2,128)(2,1)} %get-tuple-element.53, bf16[]{:T(256)} %constant.32), dimensions={0}, to_apply=%get-tuple-element.53.reduce_sub_computation | reduce | bytes 2306 | tf_op jit(solution)/shard_map/finish/pallas_call | solution.py:236
  70.4 0.7 collective-permute-start.18
  71.2 4.3 %collective-permute-start.21 = (bf16[256,512]{1,0:T(8,128)(2,1)S(1)}, bf16[256,512]{1,0:T(8,128)(2,1)S(1)}, u32[]{:S(2)}, u32[]{:S(2)}) collective-permute-start(bf16[256,512]{1,0:T(8,128)(2,1)S(1)} %fusion.7), channel_id=1, source_target_pairs={{0,1},{3,2},{1,3},{2,0},{4,5},{7,6},{5,7},{6,4},{8,9},{11,10},{9,1... | collective-permute-start | bytes 786440 | tf_op jit(solution)/shard_map/ppermute | solution.py:160
  75.4 9.8 %collective-permute-done.17 = bf16[128,1024]{1,0:T(8,128)(2,1)S(1)} collective-permute-done((bf16[128,1024]{1,0:T(8,128)(2,1)S(1)}, bf16[128,1024]{1,0:T(8,128)(2,1)S(1)}, u32[]{:S(2)}, u32[]{:S(2)}) %collective-permute-start.17) | collective-permute-done | bytes 262176 | tf_op jit(solution)/shard_map/ppermute | solution.py:160
  85.3 1.0 %fusion.2 = f32[1,128,1024]{2,1,0:T(8,128)} fusion(bf16[128,1024]{1,0:T(8,128)(2,1)S(1)} %collective-permute-done.16, bf16[128,1024]{1,0:T(8,128)(2,1)S(1)} %collective-permute-done.17, bf16[128,1024]{1,0:T(8,128)(2,1)S(1)} %collective-permute-done.15, bf16[128,1024]{1,0:T(8,128)(2,1)S(1)} %collective-permute-done.14, bf16[128,1024]{1,0:T(8,128)(2,1)S(1)} %copy-done.1, ...), kind=kLoop, calls=%fused_computation.6 | loop fusion | flops 1310720 | bytes 1835009 | tf_op jit(solution)/shard_map/broadcast_in_dim | solution.py:245
  86.3 10.2 %collective-permute-done.21 = bf16[256,512]{1,0:T(8,128)(2,1)S(1)} collective-permute-done((bf16[256,512]{1,0:T(8,128)(2,1)S(1)}, bf16[256,512]{1,0:T(8,128)(2,1)S(1)}, u32[]{:S(2)}, u32[]{:S(2)}) %collective-permute-start.21) | collective-permute-done | bytes 262176 | tf_op jit(solution)/shard_map/ppermute | solution.py:160
  96.5 1.0 fusion.5
  (63 shorter events, 1.8 us)
Async XLA Ops:
  5.8 4.8 %collective-permute-start = (bf16[96,1024]{1,0:T(8,128)(2,1)}, bf16[96,1024]{1,0:T(8,128)(2,1)S(1)}, u32[]{:S(2)}, u32[]{:S(2)}) collective-permute-start(bf16[96,1024]{1,0:T(8,128)(2,1)} %get-tuple-element.35), channel_id=1, source_target_pairs={{0,4},{4,0},{8,12},{12,8},{16,20},{20,16},{24,28},{28,24},{1,5},{5... | collective-permute-start | bytes 589832 | tf_op jit(solution)/shard_map/ppermute | solution.py:146
  6.3 8.5 %collective-permute-start.1 = (bf16[96,1024]{1,0:T(8,128)(2,1)}, bf16[96,1024]{1,0:T(8,128)(2,1)S(1)}, u32[]{:S(2)}, u32[]{:S(2)}) collective-permute-start(bf16[96,1024]{1,0:T(8,128)(2,1)} %get-tuple-element.36), channel_id=1, source_target_pairs={{0,8},{4,12},{8,0},{12,4},{16,24},{20,28},{24,16},{28,20},{1,9},{5... | collective-permute-start | bytes 589832 | tf_op jit(solution)/shard_map/ppermute | solution.py:146
  8.8 9.8 %collective-permute-start.2 = (bf16[96,1024]{1,0:T(8,128)(2,1)}, bf16[96,1024]{1,0:T(8,128)(2,1)S(1)}, u32[]{:S(2)}, u32[]{:S(2)}) collective-permute-start(bf16[96,1024]{1,0:T(8,128)(2,1)} %get-tuple-element.37), channel_id=1, source_target_pairs={{0,12},{4,8},{8,4},{12,0},{16,28},{20,24},{24,20},{28,16},{1,13},{... | collective-permute-start | bytes 589832 | tf_op jit(solution)/shard_map/ppermute | solution.py:146
  8.9 9.7 %collective-permute-start.3 = (bf16[96,1024]{1,0:T(8,128)(2,1)}, bf16[96,1024]{1,0:T(8,128)(2,1)S(1)}, u32[]{:S(2)}, u32[]{:S(2)}) collective-permute-start(bf16[96,1024]{1,0:T(8,128)(2,1)} %get-tuple-element.38), channel_id=1, source_target_pairs={{0,16},{4,20},{8,24},{12,28},{16,0},{20,4},{24,8},{28,12},{1,17},{... | collective-permute-start | bytes 589832 | tf_op jit(solution)/shard_map/ppermute | solution.py:146
  10.7 17.6 %collective-permute-start.4 = (bf16[96,1024]{1,0:T(8,128)(2,1)}, bf16[96,1024]{1,0:T(8,128)(2,1)S(1)}, u32[]{:S(2)}, u32[]{:S(2)}) collective-permute-start(bf16[96,1024]{1,0:T(8,128)(2,1)} %get-tuple-element.39), channel_id=1, source_target_pairs={{0,20},{4,16},{8,28},{12,24},{16,4},{20,0},{24,12},{28,8},{1,21},{... | collective-permute-start | bytes 589832 | tf_op jit(solution)/shard_map/ppermute | solution.py:146
  10.7 17.6 %copy-start.13 = (bf16[96,1024]{1,0:T(8,128)(2,1)}, bf16[96,1024]{1,0:T(8,128)(2,1)S(1)}, u32[]{:S(2)}) copy-start(bf16[96,1024]{1,0:T(8,128)(2,1)S(1)} %collective-permute-done.refs_1_) | copy-start | bytes 589828
  10.7 17.6 %collective-permute-start.5 = (bf16[96,1024]{1,0:T(8,128)(2,1)}, bf16[96,1024]{1,0:T(8,128)(2,1)S(1)}, u32[]{:S(2)}, u32[]{:S(2)}) collective-permute-start(bf16[96,1024]{1,0:T(8,128)(2,1)} %get-tuple-element.40), channel_id=1, source_target_pairs={{0,24},{4,28},{8,16},{12,20},{16,8},{20,12},{24,0},{28,4},{1,25},{... | collective-permute-start | bytes 589832 | tf_op jit(solution)/shard_map/ppermute | solution.py:146
  14.8 13.5 %copy-start.14 = (bf16[96,1024]{1,0:T(8,128)(2,1)}, bf16[96,1024]{1,0:T(8,128)(2,1)S(1)}, u32[]{:S(2)}) copy-start(bf16[96,1024]{1,0:T(8,128)(2,1)S(1)} %collective-permute-done.1.refs_2_) | copy-start | bytes 589828
  14.8 13.5 %collective-permute-start.6 = (bf16[96,1024]{1,0:T(8,128)(2,1)}, bf16[96,1024]{1,0:T(8,128)(2,1)S(1)}, u32[]{:S(2)}, u32[]{:S(2)}) collective-permute-start(bf16[96,1024]{1,0:T(8,128)(2,1)} %get-tuple-element.41), channel_id=1, source_target_pairs={{0,28},{4,24},{8,20},{12,16},{16,12},{20,8},{24,4},{28,0},{1,29},{... | collective-permute-start | bytes 589832 | tf_op jit(solution)/shard_map/ppermute | solution.py:146
  37.4 17.3 %copy-start.3 = (bf16[128,1024]{1,0:T(8,128)(2,1)S(1)}, bf16[128,1024]{1,0:T(8,128)(2,1)}, u32[]{:S(2)}) copy-start(bf16[128,1024]{1,0:T(8,128)(2,1)} %get-tuple-element.57) | copy-start | bytes 786436
  37.4 16.9 %collective-permute-start.16 = (bf16[128,1024]{1,0:T(8,128)(2,1)}, bf16[128,1024]{1,0:T(8,128)(2,1)S(1)}, u32[]{:S(2)}, u32[]{:S(2)}) collective-permute-start(bf16[128,1024]{1,0:T(8,128)(2,1)} %get-tuple-element.56), channel_id=1, source_target_pairs={{0,1},{1,0},{2,3},{3,2},{4,5},{5,4},{6,7},{7,6},{8,9},{9,8},{10,11... | collective-permute-start | bytes 786440 | tf_op jit(solution)/shard_map/ppermute | solution.py:155
  39.0 15.8 %copy-start.12 = (bf16[128,1024]{1,0:T(8,128)(2,1)S(1)}, bf16[128,1024]{1,0:T(8,128)(2,1)}, u32[]{:S(2)}) copy-start(bf16[128,1024]{1,0:T(8,128)(2,1)} %get-tuple-element.55) | copy-start | bytes 786436
  39.0 21.2 %copy-start.11 = (bf16[256,512]{1,0:T(8,128)(2,1)S(1)}, bf16[256,512]{1,0:T(8,128)(2,1)}, u32[]{:S(2)}) copy-start(bf16[256,512]{1,0:T(8,128)(2,1)} %get-tuple-element.59) | copy-start | bytes 786436
  42.7 28.4 %copy-start.2 = (bf16[256,512]{1,0:T(8,128)(2,1)S(1)}, bf16[256,512]{1,0:T(8,128)(2,1)}, u32[]{:S(2)}) copy-start(bf16[256,512]{1,0:T(8,128)(2,1)} %get-tuple-element.61) | copy-start | bytes 786436
  42.7 3.6 %collective-permute-start.7 = (bf16[96,640]{1,0:T(8,128)(2,1)}, bf16[96,640]{1,0:T(8,128)(2,1)S(1)}, u32[]{:S(2)}, u32[]{:S(2)}) collective-permute-start(bf16[96,640]{1,0:T(8,128)(2,1)} %get-tuple-element.45), channel_id=1, source_target_pairs={{0,4},{4,0},{8,12},{12,8},{16,20},{20,16},{24,28},{28,24},{1,5},{5... | collective-permute-start | bytes 368648 | tf_op jit(solution)/shard_map/ppermute | solution.py:146
  43.1 6.4 %collective-permute-start.8 = (bf16[96,640]{1,0:T(8,128)(2,1)}, bf16[96,640]{1,0:T(8,128)(2,1)S(1)}, u32[]{:S(2)}, u32[]{:S(2)}) collective-permute-start(bf16[96,640]{1,0:T(8,128)(2,1)} %get-tuple-element.46), channel_id=1, source_target_pairs={{0,8},{4,12},{8,0},{12,4},{16,24},{20,28},{24,16},{28,20},{1,9},{5... | collective-permute-start | bytes 368648 | tf_op jit(solution)/shard_map/ppermute | solution.py:146
  44.6 7.3 %collective-permute-start.9 = (bf16[96,640]{1,0:T(8,128)(2,1)}, bf16[96,640]{1,0:T(8,128)(2,1)S(1)}, u32[]{:S(2)}, u32[]{:S(2)}) collective-permute-start(bf16[96,640]{1,0:T(8,128)(2,1)} %get-tuple-element.47), channel_id=1, source_target_pairs={{0,12},{4,8},{8,4},{12,0},{16,28},{20,24},{24,20},{28,16},{1,13},{... | collective-permute-start | bytes 368648 | tf_op jit(solution)/shard_map/ppermute | solution.py:146
  44.6 10.2 %collective-permute-start.10 = (bf16[96,640]{1,0:T(8,128)(2,1)}, bf16[96,640]{1,0:T(8,128)(2,1)S(1)}, u32[]{:S(2)}, u32[]{:S(2)}) collective-permute-start(bf16[96,640]{1,0:T(8,128)(2,1)} %get-tuple-element.48), channel_id=1, source_target_pairs={{0,16},{4,20},{8,24},{12,28},{16,0},{20,4},{24,8},{28,12},{1,17},{... | collective-permute-start | bytes 368648 | tf_op jit(solution)/shard_map/ppermute | solution.py:146
  46.3 18.0 %copy-start.4 = (bf16[96,640]{1,0:T(8,128)(2,1)}, bf16[96,640]{1,0:T(8,128)(2,1)S(1)}, u32[]{:S(2)}) copy-start(bf16[96,640]{1,0:T(8,128)(2,1)S(1)} %collective-permute-done.7.refs_1_) | copy-start | bytes 368644
  46.3 13.2 %collective-permute-start.11 = (bf16[96,640]{1,0:T(8,128)(2,1)}, bf16[96,640]{1,0:T(8,128)(2,1)S(1)}, u32[]{:S(2)}, u32[]{:S(2)}) collective-permute-start(bf16[96,640]{1,0:T(8,128)(2,1)} %get-tuple-element.49), channel_id=1, source_target_pairs={{0,20},{4,16},{8,28},{12,24},{16,4},{20,0},{24,12},{28,8},{1,21},{... | collective-permute-start | bytes 368648 | tf_op jit(solution)/shard_map/ppermute | solution.py:146
  49.5 14.8 %copy-start.5 = (bf16[96,640]{1,0:T(8,128)(2,1)}, bf16[96,640]{1,0:T(8,128)(2,1)S(1)}, u32[]{:S(2)}) copy-start(bf16[96,640]{1,0:T(8,128)(2,1)S(1)} %collective-permute-done.8.refs_2_) | copy-start | bytes 368644
  49.5 10.7 %collective-permute-start.12 = (bf16[96,640]{1,0:T(8,128)(2,1)}, bf16[96,640]{1,0:T(8,128)(2,1)S(1)}, u32[]{:S(2)}, u32[]{:S(2)}) collective-permute-start(bf16[96,640]{1,0:T(8,128)(2,1)} %get-tuple-element.50), channel_id=1, source_target_pairs={{0,24},{4,28},{8,16},{12,20},{16,8},{20,12},{24,0},{28,4},{1,25},{... | collective-permute-start | bytes 368648 | tf_op jit(solution)/shard_map/ppermute | solution.py:146
  51.9 12.3 %collective-permute-start.13 = (bf16[96,640]{1,0:T(8,128)(2,1)}, bf16[96,640]{1,0:T(8,128)(2,1)S(1)}, u32[]{:S(2)}, u32[]{:S(2)}) collective-permute-start(bf16[96,640]{1,0:T(8,128)(2,1)} %get-tuple-element.51), channel_id=1, source_target_pairs={{0,28},{4,24},{8,20},{12,16},{16,12},{20,8},{24,4},{28,0},{1,29},{... | collective-permute-start | bytes 368648 | tf_op jit(solution)/shard_map/ppermute | solution.py:146
  54.3 16.1 %collective-permute-start.20 = (bf16[256,512]{1,0:T(8,128)(2,1)}, bf16[256,512]{1,0:T(8,128)(2,1)S(1)}, u32[]{:S(2)}, u32[]{:S(2)}) collective-permute-start(bf16[256,512]{1,0:T(8,128)(2,1)} %get-tuple-element.60), channel_id=1, source_target_pairs={{0,1},{1,0},{2,3},{3,2},{4,5},{5,4},{6,7},{7,6},{8,9},{9,8},{10,11... | collective-permute-start | bytes 786440 | tf_op jit(solution)/shard_map/ppermute | solution.py:155
  54.8 30.5 %copy-start.1 = (bf16[128,1024]{1,0:T(8,128)(2,1)S(1)}, bf16[128,1024]{1,0:T(8,128)(2,1)}, u32[]{:S(2)}) copy-start(bf16[128,1024]{1,0:T(8,128)(2,1)} %get-tuple-element.54) | copy-start | bytes 786436
  54.8 16.3 %collective-permute-start.15 = (bf16[128,1024]{1,0:T(8,128)(2,1)S(1)}, bf16[128,1024]{1,0:T(8,128)(2,1)S(1)}, u32[]{:S(2)}, u32[]{:S(2)}) collective-permute-start(bf16[128,1024]{1,0:T(8,128)(2,1)S(1)} %copy-done.12), channel_id=1, source_target_pairs={{0,2},{3,1},{4,6},{7,5},{8,10},{11,9},{12,14},{15,13},{16,18},{19,... | collective-permute-start | bytes 786440 | tf_op jit(solution)/shard_map/ppermute | solution.py:157
  59.5 15.9 %collective-permute-start.14 = (bf16[128,1024]{1,0:T(8,128)(2,1)S(1)}, bf16[128,1024]{1,0:T(8,128)(2,1)S(1)}, u32[]{:S(2)}, u32[]{:S(2)}) collective-permute-start(bf16[128,1024]{1,0:T(8,128)(2,1)S(1)} %copy-done.12), channel_id=1, source_target_pairs={{1,2},{2,1},{5,6},{6,5},{9,10},{10,9},{13,14},{14,13},{17,18},{18,... | collective-permute-start | bytes 786440 | tf_op jit(solution)/shard_map/ppermute | solution.py:156
  60.2 26.1 %collective-permute-start.19 = (bf16[256,512]{1,0:T(8,128)(2,1)S(1)}, bf16[256,512]{1,0:T(8,128)(2,1)S(1)}, u32[]{:S(2)}, u32[]{:S(2)}) collective-permute-start(bf16[256,512]{1,0:T(8,128)(2,1)S(1)} %copy-done.11), channel_id=1, source_target_pairs={{0,2},{3,1},{4,6},{7,5},{8,10},{11,9},{12,14},{15,13},{16,18},{19,... | collective-permute-start | bytes 786440 | tf_op jit(solution)/shard_map/ppermute | solution.py:157
  64.2 21.0 %collective-permute-start.17 = (bf16[128,1024]{1,0:T(8,128)(2,1)S(1)}, bf16[128,1024]{1,0:T(8,128)(2,1)S(1)}, u32[]{:S(2)}, u32[]{:S(2)}) collective-permute-start(bf16[128,1024]{1,0:T(8,128)(2,1)S(1)} %fusion.6), channel_id=1, source_target_pairs={{0,1},{3,2},{1,3},{2,0},{4,5},{7,6},{5,7},{6,4},{8,9},{11,10},{9,1... | collective-permute-start | bytes 786440 | tf_op jit(solution)/shard_map/ppermute | solution.py:160
  69.1 27.5 %copy-start = (bf16[256,512]{1,0:T(8,128)(2,1)S(1)}, bf16[256,512]{1,0:T(8,128)(2,1)}, u32[]{:S(2)}) copy-start(bf16[256,512]{1,0:T(8,128)(2,1)} %get-tuple-element.58) | copy-start | bytes 786436
  70.4 15.9 %collective-permute-start.18 = (bf16[256,512]{1,0:T(8,128)(2,1)S(1)}, bf16[256,512]{1,0:T(8,128)(2,1)S(1)}, u32[]{:S(2)}, u32[]{:S(2)}) collective-permute-start(bf16[256,512]{1,0:T(8,128)(2,1)S(1)} %copy-done.11), channel_id=1, source_target_pairs={{1,2},{2,1},{5,6},{6,5},{9,10},{10,9},{13,14},{14,13},{17,18},{18,... | collective-permute-start | bytes 786440 | tf_op jit(solution)/shard_map/ppermute | solution.py:156
  71.2 25.3 %collective-permute-start.21 = (bf16[256,512]{1,0:T(8,128)(2,1)S(1)}, bf16[256,512]{1,0:T(8,128)(2,1)S(1)}, u32[]{:S(2)}, u32[]{:S(2)}) collective-permute-start(bf16[256,512]{1,0:T(8,128)(2,1)S(1)} %fusion.7), channel_id=1, source_target_pairs={{0,1},{3,2},{1,3},{2,0},{4,5},{7,6},{5,7},{6,4},{8,9},{11,10},{9,1... | collective-permute-start | bytes 786440 | tf_op jit(solution)/shard_map/ppermute | solution.py:160
  (10 other events, 53.2 us)

commit v2 on v1

--- a/solution.py
+++ b/solution.py
@@ -11,7 +11,7 @@
 F32 = jnp.float32
 BF16 = jnp.bfloat16
 LANES = 128
-VMEM_BYTES = 56 * 1024 * 1024
+VMEM_BYTES = 24 * 1024 * 1024
 
 vmem = pl.BlockSpec(memory_space=pltpu.VMEM)
 smem = pl.BlockSpec(memory_space=pltpu.SMEM)
@@ -55,11 +55,12 @@
     )
     before = dot(onehot.astype(BF16), jnp.where(earlier, 1.0, 0.0).astype(BF16))
     rank = jnp.sum(before * onehot, axis=0, keepdims=True).astype(jnp.int32)
-    target = jnp.where(rank < capacity, jnp.bitwise_xor(ids, me[0]) * capacity + rank, -1)
-    target_ref[...] = target
+    kept = rank < capacity
+    target_ref[...] = jnp.where(kept, ids * capacity + rank, -1)
+    target = jnp.where(kept, jnp.bitwise_xor(ids, me[0]) * capacity + rank, -1)
     hit = lax.broadcasted_iota(jnp.int32, (rows, tok_rows), 0) == target
     pick = jnp.where(hit, 1.0, 0.0).astype(BF16)
-    pick_gate = jnp.where(hit, gate_ref[...].astype(F32), 0.0).astype(BF16)
+    pick_gate = jnp.where(hit, gate_ref[...].astype(F32).reshape(1, tok_rows), 0.0).astype(BF16)
     placed_normed = dot(pick, normed).astype(BF16)
     placed_delta = dot(pick_gate, go_ref[...]).astype(BF16)
     for k in range(sources):
@@ -79,9 +80,8 @@
 
 def grads_kernel(sources, capacity, pieces, order, w_in_ref, w_out_ref, *refs):
     blocks = refs[:sources]
-    outs_in = refs[sources : sources + pieces]
-    outs_out = refs[sources + pieces : sources + 2 * pieces]
-    gpre_ref, extra_ref, x_ref, d_ref, xt_ref = refs[sources + 2 * pieces :]
+    outs = refs[sources : sources + pieces]
+    gpre_ref, extra_ref, x_ref, d_ref, xt_ref = refs[sources + pieces :]
     width, hidden = w_in_ref.shape
     piece_d, piece_f = width // pieces, hidden // pieces
     for k in range(sources):
@@ -102,36 +102,36 @@
         total += jnp.sum(act.astype(F32) * grad_act, axis=1, keepdims=True)
         grad_pre = (grad_act * slope).astype(BF16)
         gpre_ref[:, part] = grad_pre
-        outs_out[j][...] = dot(act.T, delta).astype(BF16)
+        weight = dot(act.T, delta).astype(BF16)
+        outs[j][piece_d:, :width] = weight[: piece_f // 2]
+        outs[j][piece_d:, width:] = weight[piece_f // 2 :]
         weight = dot(xt_ref[...], grad_pre).astype(BF16)
         for i in range(pieces):
-            outs_in[i][:, part] = weight[i * piece_d : (i + 1) * piece_d]
+            outs[i][:piece_d, part] = weight[i * piece_d : (i + 1) * piece_d]
     high = total.astype(BF16).astype(F32)
     lane = lax.broadcasted_iota(jnp.int32, extra_ref.shape, 1)
     extra_ref[...] = jnp.where(lane == 0, high, jnp.where(lane == 1, total - high, 0.0)).astype(BF16)
 
 
-def back_kernel(sources, capacity, gpre_ref, w_in_ref, extra_ref, *outs):
+def back_kernel(sources, capacity, me, gpre_ref, w_in_ref, extra_ref, out_ref):
     width = w_in_ref.shape[0]
     grad = dot(gpre_ref[...], w_in_ref[...], ((1,), (1,))).astype(BF16)
     for k in range(sources):
         block = slice(k * capacity, (k + 1) * capacity)
-        outs[k][:, :width] = grad[block]
-        outs[k][:, width:] = extra_ref[block, :]
-
-
-def finish_kernel(sources, capacity, target_ref, gate_ref, tok_ref, gain_ref, go_ref, *refs):
-    blocks = refs[:sources]
-    tokens_out, gate_out, back_ref = refs[sources:]
-    rows = sources * capacity
+        source = jnp.bitwise_xor(me[0], k)
+        out_ref[source, :, :width] = grad[block]
+        out_ref[source, :, width:] = extra_ref[block, :]
+
+
+def finish_kernel(target_ref, gate_ref, tok_ref, gain_ref, go_ref, back_ref, tokens_out, gate_out):
+    rows = back_ref.shape[0]
     tok_rows, width = tok_ref.shape
-    for k in range(sources):
-        back_ref[k * capacity : (k + 1) * capacity, :] = blocks[k][...]
     spots = jnp.broadcast_to(target_ref[...].astype(F32), (8, tok_rows)).T[:, :1].astype(jnp.int32)
     hit = lax.broadcasted_iota(jnp.int32, (tok_rows, rows), 1) == spots
     got = dot(jnp.where(hit, 1.0, 0.0).astype(BF16), back_ref[...])
     sums = got[:, width:].T
-    gate_out[...] = ((sums[0:1] + sums[1:2]) / gate_ref[...].astype(F32)).astype(BF16)
+    gate_row = gate_ref[...].astype(F32).reshape(1, tok_rows)
+    gate_out[...] = ((sums[0:1] + sums[1:2]) / gate_row).astype(BF16)
     scaled, spread = normalize(tok_ref[...])
     grad = got[:, :width] * gain_ref[...]
     mean = jnp.mean(grad, axis=-1, keepdims=True)
@@ -142,9 +142,10 @@
 
 def swap_blocks(blocks):
     count = len(blocks)
-    return [blocks[0]] + [
-        lax.ppermute(blocks[k], "space", [(i, i ^ k) for i in range(count)]) for k in range(1, count)
-    ]
+    swapped = list(blocks)
+    for k in reversed(range(1, count)):
+        swapped[k] = lax.ppermute(blocks[k], "space", [(i, i ^ k) for i in range(count)])
+    return swapped
 
 
 def add(*terms):
@@ -173,7 +174,6 @@
     me = lax.axis_index("space").astype(jnp.int32).reshape(1)
     place = lax.axis_index("dp").astype(jnp.int32)
     ids_row = expert_ids.reshape(1, tok_rows)
-    gate_row = gate.reshape(1, tok_rows)
     gain_row = gain.reshape(1, width)
     weight_in, weight_out = w_in[0], w_out[0]
     shape = jax.ShapeDtypeStruct
@@ -186,7 +186,7 @@
         io_bytes,
         [shape((1, tok_rows), jnp.int32)] + [shape((capacity, 2 * width), BF16)] * sources,
         [smem] + [vmem] * 5,
-    )(me, ids_row, gate_row, tokens, gain_row, grad_out)
+    )(me, ids_row, gate, tokens, gain_row, grad_out)
     arrived = swap_blocks(sent)
 
     if groups == 4:
@@ -200,8 +200,7 @@
         "grads",
         8 * rows * width * hidden,
         2 * (2 * rows * width + 4 * width * hidden + rows * hidden),
-        [shape((width // pieces, hidden), BF16)] * pieces
-        + [shape((hidden // pieces, width), BF16)] * pieces
+        [shape((width // pieces + hidden // pieces // 2, hidden), BF16)] * pieces
         + [shape((rows, hidden), BF16), shape((rows, LANES), BF16)],
         [smem] + [vmem] * (2 + sources),
         [
@@ -211,38 +210,42 @@
         ],
         rows * hidden,
     )(order, weight_in, weight_out, *arrived)
-    parts_in, parts_out = parts[:pieces], parts[pieces:]
-
-    returned = kernel_call(
+
+    (returned,) = kernel_call(
         functools.partial(back_kernel, sources, capacity),
         "back",
         2 * rows * width * hidden,
         2 * (rows * hidden + width * hidden + rows * width),
-        [shape((capacity, width + LANES), BF16)] * sources,
-        [vmem] * 3,
-    )(gpre, weight_in, extra)
+        [shape((sources, capacity, width + LANES), BF16)],
+        [smem] + [vmem] * 3,
+    )(me, gpre, weight_in, extra)
+    back = lax.all_to_all(returned, "space", split_axis=0, concat_axis=0, tiled=True)
 
     if groups == 4:
-        grad_w_out = line_sums(*parts_out, place)
-        grad_w_in = line_sums(*parts_in, place)
+        grad_w_in, grad_w_out = split_piece(line_sums(*parts, place), width, pieces)
     else:
+        parts_in, parts_out = zip(*[split_piece(part, width, pieces) for part in parts])
         grad_w_in, grad_w_out = (
             lax.psum_scatter(
                 jnp.concatenate(part), "dp", scatter_dimension=0, tiled=True
             ).astype(F32)
             for part in (parts_in, parts_out)
         )
-    back = swap_blocks(returned)
     grad_tokens, grad_gate = kernel_call(
-        functools.partial(finish_kernel, sources, capacity),
+        finish_kernel,
         "finish",
         2 * rows * tok_rows * width,
         io_bytes,
         [shape((tok_rows, width), BF16), shape((1, tok_rows), BF16)],
-        [vmem] * (5 + sources),
-        [pltpu.VMEM((rows, width + LANES), BF16)],
-    )(target, gate_row, tokens, gain_row, grad_out, *back)
+        [vmem] * 6,
+    )(target, gate, tokens, gain_row, grad_out, back.reshape(rows, width + LANES))
     return (grad_tokens, grad_gate.reshape(tok_rows), grad_w_in[None], grad_w_out[None])
+
+
+def split_piece(piece, width, pieces):
+    piece_d = width // pieces
+    lower = piece[piece_d:]
+    return piece[:piece_d], jnp.concatenate([lower[:, :width], lower[:, width:]])
 
 
 def solution(mesh):

time: 97.8 us -> 95.1 us (0.972)
  local copies, waits for them, and re-layouts: 2.6 us -> 13.1 us
  starting transfers between devices: 34.3 us -> 23.9 us
  Pallas kernels: 20.1 us -> 13.3 us
  waiting for transfers between devices: 35.5 us -> 38.1 us
  other arithmetic: 4.05 us -> 5.5 us
    unnamed x40 -> x44, local copies, waits for them, and re-layouts: 1.33 us -> 12.2 us
    ppermute x14 -> x7, starting transfers between devices: 17.9 us -> 9.24 us  [swap_blocks(): lax.ppermute(blocks[k], 'space', [(i, i ^ k) for i in range(count)])]
    ppermute x14 -> x7, waiting for transfers between devices: 15.4 us -> 11 us  [swap_blocks(): lax.ppermute(blocks[k], 'space', [(i, i ^ k) for i in range(count)])]
    all_to_all x0 -> x1, starting transfers between devices: none -> 3.87 us  [body(): lax.all_to_all(returned, 'space', split_axis=0, concat_axis=0, tiled=True)]
    all_to_all x0 -> x1, waiting for transfers between devices: none -> 3.51 us  [body(): lax.all_to_all(returned, 'space', split_axis=0, concat_axis=0, tiled=True)]
    ppermute x2 -> x1, starting transfers between devices: 8.64 us -> 5.31 us  [line_sums(): across = lax.ppermute(second, 'dp', [(0, 2), (3, 1)])]
    ppermute x2 -> x1, waiting for transfers between devices: 20.1 us -> 23.2 us  [line_sums(): last = lax.ppermute(passed, 'dp', [(0, 1), (3, 2), (1, 3), (2, 0)])]
    ppermute x2 -> x1, starting transfers between devices: 4.32 us -> 2.17 us  [line_sums(): last = lax.ppermute(passed, 'dp', [(0, 1), (3, 2), (1, 3), (2, 0)])]
  transfers between devices with their start and end apart: 22 -> 12, of which waited for: 6 -> 7; matrix products, arithmetic and copies ran while one was open for 3% -> 3% of each run, Pallas kernels for 8% -> 5%
where the time goes in v2:
time: 95.1 us; the launch traced here: 94.5 us
  waiting for transfers between devices  38.1 us (40%)
  starting transfers between devices  23.9 us (25%)
  Pallas kernels  13.3 us (14%)
  local copies, waits for them, and re-layouts  13.1 us (14%)
  other arithmetic  5.5 us (6%)
    ppermute x1, waiting for transfers between devices, line_sums(): last = lax.ppermute(passed, 'dp', [(0, 1), (3, 2), (1, 3), (2, 0)])  23.2 us
    unnamed x44, local copies, waits for them, and re-layouts  12.2 us
    ppermute x7, waiting for transfers between devices, swap_blocks(): lax.ppermute(blocks[k], 'space', [(i, i ^ k) for i in range(count)])  11 us
    ppermute x7, starting transfers between devices, swap_blocks(): lax.ppermute(blocks[k], 'space', [(i, i ^ k) for i in range(count)])  9.24 us
    pallas_call x1, Pallas kernels, body(): kernel_call(functools.partial(grads_kernel, sources, capacity, pieces), '...  6.3 us
    ppermute x1, starting transfers between devices, line_sums(): across = lax.ppermute(second, 'dp', [(0, 2), (3, 1)])  5.31 us
    all_to_all x1, starting transfers between devices, body(): lax.all_to_all(returned, 'space', split_axis=0, concat_axis=0, tiled=True)  3.87 us
    all_to_all x1, waiting for transfers between devices, body(): lax.all_to_all(returned, 'space', split_axis=0, concat_axis=0, tiled=True)  3.51 us
  transfers between devices with their start and end apart: 12, of which 7 were waited for; matrix products, arithmetic and copies ran while one was open for 3% of the time, Pallas kernels for 5%

profile of v2, /device:TPU:0, one launch (start us, length us, event | category | flops | bytes accessed | tf_op | source)
XLA Modules:
  0.0 94.5 jit_solution(11790068198216314160)
XLA Ops:
  0.6 1.1 %copy-done.1 = bf16[576,512]{1,0:T(8,128)(2,1)S(1)} copy-done((bf16[576,512]{1,0:T(8,128)(2,1)S(1)}, bf16[576,512]{1,0:T(8,128)(2,1)}, u32[]{:S(2)}) %copy-start.1) | copy-done | bytes 589848
  1.7 1.1 %copy-done.3 = bf16[576,512]{1,0:T(8,128)(2,1)S(1)} copy-done((bf16[576,512]{1,0:T(8,128)(2,1)S(1)}, bf16[576,512]{1,0:T(8,128)(2,1)}, u32[]{:S(2)}) %copy-start.3) | copy-done | bytes 589848
  2.8 0.7 copy-done.5
  3.5 0.7 copy-done.7
  4.1 0.7 copy-done.19
  4.8 2.4 %place.1 = (s32[1,576]{1,0:T(1,128)S(1)}, bf16[96,1024]{1,0:T(8,128)(2,1)S(1)}, bf16[96,1024]{1,0:T(8,128)(2,1)S(1)}, bf16[96,1024]{1,0:T(8,128)(2,1)S(1)}, bf16...) custom-call(s32[1]{0:T(128)} %bitcast.me, ...), custom_call_target="tpu_custom_call" | custom-call | flops 905969664 | bytes 2752512 | tf_op jit(solution)/shard_map/place/pallas_call | solution.py:182
  8.4 2.5 %collective-permute-start.1 = (bf16[96,1024]{1,0:T(8,128)(2,1)S(1)}, bf16[96,1024]{1,0:T(8,128)(2,1)S(1)}, u32[]{:S(2)}, u32[]{:S(2)}) collective-permute-start(bf16[96,1024]{1,0:T(8,128)(2,1)S(1)} %get-tuple-element.24), channel_id=1, source_target_pairs={{0,8},{4,12},{8,0},{12,4},{16,24},{20,28},{24,16},{28,20},{1,9},{5... | collective-permute-start | bytes 589832 | tf_op jit(solution)/shard_map/ppermute | solution.py:147
  11.0 1.7 %collective-permute-start.3 = (bf16[96,1024]{1,0:T(8,128)(2,1)}, bf16[96,1024]{1,0:T(8,128)(2,1)S(1)}, u32[]{:S(2)}, u32[]{:S(2)}) collective-permute-start(bf16[96,1024]{1,0:T(8,128)(2,1)} %get-tuple-element.26), channel_id=1, source_target_pairs={{0,16},{4,20},{8,24},{12,28},{16,0},{20,4},{24,8},{28,12},{1,17},{... | collective-permute-start | bytes 589832 | tf_op jit(solution)/shard_map/ppermute | solution.py:147
  12.7 2.6 %collective-permute-start.5 = (bf16[96,1024]{1,0:T(8,128)(2,1)S(1)}, bf16[96,1024]{1,0:T(8,128)(2,1)}, u32[]{:S(2)}, u32[]{:S(2)}) collective-permute-start(bf16[96,1024]{1,0:T(8,128)(2,1)S(1)} %get-tuple-element.28), channel_id=1, source_target_pairs={{0,24},{4,28},{8,16},{12,20},{16,8},{20,12},{24,0},{28,4},{1,25},{... | collective-permute-start | bytes 589832 | tf_op jit(solution)/shard_map/ppermute | solution.py:147
  15.3 1.3 %collective-permute-done.1.refs_2_ = bf16[96,1024]{1,0:T(8,128)(2,1)S(1)} collective-permute-done((bf16[96,1024]{1,0:T(8,128)(2,1)S(1)}, bf16[96,1024]{1,0:T(8,128)(2,1)S(1)}, u32[]{:S(2)}, u32[]{:S(2)}) %collective-permute-start.1) | collective-permute-done | bytes 196640 | tf_op jit(solution)/shard_map/ppermute | solution.py:147
  17.3 1.9 %collective-permute-start.6 = (bf16[96,1024]{1,0:T(8,128)(2,1)S(1)}, bf16[96,1024]{1,0:T(8,128)(2,1)S(1)}, u32[]{:S(2)}, u32[]{:S(2)}) collective-permute-start(bf16[96,1024]{1,0:T(8,128)(2,1)S(1)} %get-tuple-element.29), channel_id=1, source_target_pairs={{0,28},{4,24},{8,20},{12,16},{16,12},{20,8},{24,4},{28,0},{1,29},{... | collective-permute-start | bytes 589832 | tf_op jit(solution)/shard_map/ppermute | solution.py:147
  19.2 1.2 %collective-permute-done.2.refs_3_ = bf16[96,1024]{1,0:T(8,128)(2,1)S(1)} collective-permute-done((bf16[96,1024]{1,0:T(8,128)(2,1)}, bf16[96,1024]{1,0:T(8,128)(2,1)S(1)}, u32[]{:S(2)}, u32[]{:S(2)}) %collective-permute-start.2) | collective-permute-done | bytes 196640 | tf_op jit(solution)/shard_map/ppermute | solution.py:147
  21.8 8.5 %collective-permute-done.4.refs_5_ = bf16[96,1024]{1,0:T(8,128)(2,1)} collective-permute-done((bf16[96,1024]{1,0:T(8,128)(2,1)}, bf16[96,1024]{1,0:T(8,128)(2,1)}, u32[]{:S(2)}, u32[]{:S(2)}) %collective-permute-start.4) | collective-permute-done | bytes 196640 | tf_op jit(solution)/shard_map/ppermute | solution.py:147
  31.0 0.9 copy-done.12
  31.9 0.9 copy-done.14
  32.9 0.9 copy-done.16
  33.8 0.9 copy-done.18
  34.7 0.9 copy-done.21
  35.6 6.3 %grads.1 = (bf16[256,1024]{1,0:T(8,128)(2,1)}, bf16[256,1024]{1,0:T(8,128)(2,1)S(1)}, bf16[256,1024]{1,0:T(8,128)(2,1)S(1)}, bf16[256,1024]{1,0:T(8,128)(2,1)S(1...) custom-call(s32[4]{0:T(128)S(1)} %pad_add_fusion.order, bf16[512,1024]{1,0:T(8,128)(2,1)S(1)} %bitcast.15, ...), custom_call_target="tpu_custom_call" | custom-call | flops 3221225472 | bytes 7340032 | tf_op jit(solution)/shard_map/grads/pallas_call | solution.py:198
  41.9 1.9 %collective-permute-start.9 = (bf16[256,1024]{1,0:T(8,128)(2,1)}, bf16[256,1024]{1,0:T(8,128)(2,1)}, u32[]{:S(2)}, u32[]{:S(2)}) collective-permute-start(bf16[256,1024]{1,0:T(8,128)(2,1)} %get-tuple-element.36), channel_id=1, source_target_pairs={{0,1},{1,0},{2,3},{3,2},{4,5},{5,4},{6,7},{7,6},{8,9},{9,8},{10,11... | collective-permute-start | bytes 1572872 | tf_op jit(solution)/shard_map/ppermute | solution.py:156
  43.8 2.0 %back.1 = bf16[8,96,640]{2,1,0:T(8,128)(2,1)} custom-call(s32[1]{0:T(128)} %bitcast.me, bf16[768,1024]{1,0:T(8,128)(2,1)S(1)} %get-tuple-element.30.gpre_ref, bf16[512,1024]{1,0:T(8,128)(2,1)S(1)} %bitcast.16, bf16[768,128]{1,0:T(8,128)(2,1)S(1)} %get-tuple-element.31.extra_ref), custom_call_target="tpu_custom_call" | custom-call | flops 805306368 | bytes 3407872 | tf_op jit(solution)/shard_map/back/pallas_call | solution.py:214
  45.8 3.9 %all-to-all-start = ((bf16[8,96,640]{2,1,0:T(8,128)(2,1)}), bf16[8,96,640]{2,1,0:T(8,128)(2,1)S(1)}, u32[]{:S(2)}, u32[]{:S(2)}) async-start(bf16[8,96,640]{2,1,0:T(8,128)(2,1)} %back.1), calls=%async_computation | async-start | bytes 1966080 | tf_op jit(solution)/shard_map/all_to_all | solution.py:222
  49.7 5.3 %collective-permute-start.8 = (bf16[256,1024]{1,0:T(8,128)(2,1)}, bf16[256,1024]{1,0:T(8,128)(2,1)}, u32[]{:S(2)}, u32[]{:S(2)}) collective-permute-start(bf16[256,1024]{1,0:T(8,128)(2,1)} %copy-done.10), channel_id=1, source_target_pairs={{0,2},{3,1},{4,6},{7,5},{8,10},{11,9},{12,14},{15,13},{16,18},{19,... | collective-permute-start | bytes 1572872 | tf_op jit(solution)/shard_map/ppermute | solution.py:158
  55.0 1.4 %collective-permute-start.7 = (bf16[256,1024]{1,0:T(8,128)(2,1)}, bf16[256,1024]{1,0:T(8,128)(2,1)}, u32[]{:S(2)}, u32[]{:S(2)}) collective-permute-start(bf16[256,1024]{1,0:T(8,128)(2,1)} %copy-done.10), channel_id=1, source_target_pairs={{1,2},{2,1},{5,6},{6,5},{9,10},{10,9},{13,14},{14,13},{17,18},{18,... | collective-permute-start | bytes 1572872 | tf_op jit(solution)/shard_map/ppermute | solution.py:157
  56.7 2.0 %fusion.2 = bf16[256,1024]{1,0:T(8,128)(2,1)} fusion(bf16[256,1024]{1,0:T(8,128)(2,1)} %collective-permute-done.9, bf16[256,1024]{1,0:T(8,128)(2,1)S(1)} %get-tuple-element.37, pred[]{:T(512)S(6)} %or.3), kind=kLoop, calls=%fused_computation.4 | loop fusion | flops 1310720 | bytes 1572865 | tf_op jit(solution)/shard_map/convert_element_type | solution.py:160
  58.7 2.2 %collective-permute-start.10 = (bf16[256,1024]{1,0:T(8,128)(2,1)}, bf16[256,1024]{1,0:T(8,128)(2,1)}, u32[]{:S(2)}, u32[]{:S(2)}) collective-permute-start(bf16[256,1024]{1,0:T(8,128)(2,1)} %fusion.2), channel_id=1, source_target_pairs={{0,1},{3,2},{1,3},{2,0},{4,5},{7,6},{5,7},{6,4},{8,9},{11,10},{9,1... | collective-permute-start | bytes 1572872 | tf_op jit(solution)/shard_map/ppermute | solution.py:161
  60.9 3.5 %all-to-all-done = bf16[8,96,640]{2,1,0:T(8,128)(2,1)S(1)} async-done(((bf16[8,96,640]{2,1,0:T(8,128)(2,1)}), bf16[8,96,640]{2,1,0:T(8,128)(2,1)S(1)}, u32[]{:S(2)}, u32[]{:S(2)}) %all-to-all-start) | async-done | bytes 983072 | tf_op jit(solution)/shard_map/all_to_all | solution.py:222
  64.4 2.6 %finish.1 = (bf16[576,512]{1,0:T(8,128)(2,1)}, bf16[1,576]{1,0:T(2,128)(2,1)S(1)}) custom-call(s32[1,576]{1,0:T(1,128)S(1)} %get-tuple-element.21.target_ref, bf16[576]{0:T(1024)(128)(2,1)S(1)} %copy-done.6, bf16[576,512]{1,0:T(8,128)(2,1)S(1)} %copy-done.2, f32[1,512]{1,0:T(1,128)S(1)} %bitcast.18, bf16[576,512]{1,0:T(8,128)(2,1)S(1)} %copy-done.4, ...), custom_call_target="tpu_custom_call" | custom-call | flops 452984832 | bytes 2752512 | tf_op jit(solution)/shard_map/finish/pallas_call | solution.py:234
  67.7 23.2 %collective-permute-done.10 = bf16[256,1024]{1,0:T(8,128)(2,1)} collective-permute-done((bf16[256,1024]{1,0:T(8,128)(2,1)}, bf16[256,1024]{1,0:T(8,128)(2,1)}, u32[]{:S(2)}, u32[]{:S(2)}) %collective-permute-start.10) | collective-permute-done | bytes 524320 | tf_op jit(solution)/shard_map/ppermute | solution.py:161
  90.9 2.0 %fusion.1 = f32[256,1024]{1,0:T(8,128)S(1)} fusion(bf16[256,1024]{1,0:T(8,128)(2,1)} %collective-permute-done.9, bf16[256,1024]{1,0:T(8,128)(2,1)} %collective-permute-done.10, bf16[256,1024]{1,0:T(8,128)(2,1)} %collective-permute-done.8, bf16[256,1024]{1,0:T(8,128)(2,1)} %collective-permute-done.7, bf16[256,1024]{1,0:T(8,128)(2,1)S(1)} %get-tuple-element.34, ...), kind=kLoop, calls=%fused_computation.3 | loop fusion | flops 2621440 | bytes 3670017 | tf_op jit(solution)/shard_map/add | solution.py:152
  92.8 0.8 slice_bitcast_fusion
  93.7 0.8 maximum_bitcast_fusion
  (47 shorter events, 5.1 us)
Async XLA Ops:
  0.6 1.1 %copy-start.1 = (bf16[576,512]{1,0:T(8,128)(2,1)S(1)}, bf16[576,512]{1,0:T(8,128)(2,1)}, u32[]{:S(2)}) copy-start(bf16[576,512]{1,0:T(8,128)(2,1)} %tok_ref.3) | copy-start | bytes 1769476
  1.7 1.1 %copy-start.3 = (bf16[576,512]{1,0:T(8,128)(2,1)S(1)}, bf16[576,512]{1,0:T(8,128)(2,1)}, u32[]{:S(2)}) copy-start(bf16[576,512]{1,0:T(8,128)(2,1)} %go_ref.3) | copy-start | bytes 1769476
  2.8 0.7 copy-start.5
  3.5 0.7 copy-start.7
  4.1 0.7 copy-start.19
  4.8 26.2 %copy-start = (bf16[1,512,1024]{2,1,0:T(8,128)(2,1)S(1)}, bf16[1,512,1024]{2,1,0:T(8,128)(2,1)}, u32[]{:S(2)}) copy-start(bf16[1,512,1024]{2,1,0:T(8,128)(2,1)} %param.9) | copy-start | bytes 3145732
  4.8 26.2 %copy-start.9 = (bf16[1,1024,512]{2,1,0:T(8,128)(2,1)S(1)}, bf16[1,1024,512]{2,1,0:T(8,128)(2,1)}, u32[]{:S(2)}) copy-start(bf16[1,1024,512]{2,1,0:T(8,128)(2,1)} %param.10) | copy-start | bytes 3145732
  7.9 4.8 %collective-permute-start = (bf16[96,1024]{1,0:T(8,128)(2,1)S(1)}, bf16[96,1024]{1,0:T(8,128)(2,1)S(1)}, u32[]{:S(2)}, u32[]{:S(2)}) collective-permute-start(bf16[96,1024]{1,0:T(8,128)(2,1)S(1)} %get-tuple-element.23), channel_id=1, source_target_pairs={{0,4},{4,0},{8,12},{12,8},{16,20},{20,16},{24,28},{28,24},{1,5},{5... | collective-permute-start | bytes 589832 | tf_op jit(solution)/shard_map/ppermute | solution.py:147
  8.4 8.2 %collective-permute-start.1 = (bf16[96,1024]{1,0:T(8,128)(2,1)S(1)}, bf16[96,1024]{1,0:T(8,128)(2,1)S(1)}, u32[]{:S(2)}, u32[]{:S(2)}) collective-permute-start(bf16[96,1024]{1,0:T(8,128)(2,1)S(1)} %get-tuple-element.24), channel_id=1, source_target_pairs={{0,8},{4,12},{8,0},{12,4},{16,24},{20,28},{24,16},{28,20},{1,9},{5... | collective-permute-start | bytes 589832 | tf_op jit(solution)/shard_map/ppermute | solution.py:147
  10.9 9.6 %collective-permute-start.2 = (bf16[96,1024]{1,0:T(8,128)(2,1)}, bf16[96,1024]{1,0:T(8,128)(2,1)S(1)}, u32[]{:S(2)}, u32[]{:S(2)}) collective-permute-start(bf16[96,1024]{1,0:T(8,128)(2,1)} %get-tuple-element.25), channel_id=1, source_target_pairs={{0,12},{4,8},{8,4},{12,0},{16,28},{20,24},{24,20},{28,16},{1,13},{... | collective-permute-start | bytes 589832 | tf_op jit(solution)/shard_map/ppermute | solution.py:147
  11.0 10.1 %collective-permute-start.3 = (bf16[96,1024]{1,0:T(8,128)(2,1)}, bf16[96,1024]{1,0:T(8,128)(2,1)S(1)}, u32[]{:S(2)}, u32[]{:S(2)}) collective-permute-start(bf16[96,1024]{1,0:T(8,128)(2,1)} %get-tuple-element.26), channel_id=1, source_target_pairs={{0,16},{4,20},{8,24},{12,28},{16,0},{20,4},{24,8},{28,12},{1,17},{... | collective-permute-start | bytes 589832 | tf_op jit(solution)/shard_map/ppermute | solution.py:147
  12.7 17.6 %collective-permute-start.4 = (bf16[96,1024]{1,0:T(8,128)(2,1)}, bf16[96,1024]{1,0:T(8,128)(2,1)}, u32[]{:S(2)}, u32[]{:S(2)}) collective-permute-start(bf16[96,1024]{1,0:T(8,128)(2,1)} %get-tuple-element.27), channel_id=1, source_target_pairs={{0,20},{4,16},{8,28},{12,24},{16,4},{20,0},{24,12},{28,8},{1,21},{... | collective-permute-start | bytes 589832 | tf_op jit(solution)/shard_map/ppermute | solution.py:147
  12.7 17.6 %collective-permute-start.5 = (bf16[96,1024]{1,0:T(8,128)(2,1)S(1)}, bf16[96,1024]{1,0:T(8,128)(2,1)}, u32[]{:S(2)}, u32[]{:S(2)}) collective-permute-start(bf16[96,1024]{1,0:T(8,128)(2,1)S(1)} %get-tuple-element.28), channel_id=1, source_target_pairs={{0,24},{4,28},{8,16},{12,20},{16,8},{20,12},{24,0},{28,4},{1,25},{... | collective-permute-start | bytes 589832 | tf_op jit(solution)/shard_map/ppermute | solution.py:147
  16.6 0.7 copy-start.11
  17.3 13.0 %collective-permute-start.6 = (bf16[96,1024]{1,0:T(8,128)(2,1)S(1)}, bf16[96,1024]{1,0:T(8,128)(2,1)S(1)}, u32[]{:S(2)}, u32[]{:S(2)}) collective-permute-start(bf16[96,1024]{1,0:T(8,128)(2,1)S(1)} %get-tuple-element.29), channel_id=1, source_target_pairs={{0,28},{4,24},{8,20},{12,16},{16,12},{20,8},{24,4},{28,0},{1,29},{... | collective-permute-start | bytes 589832 | tf_op jit(solution)/shard_map/ppermute | solution.py:147
  21.1 0.7 copy-start.15
  30.3 0.7 copy-start.17
  31.0 0.9 copy-start.12
  31.9 0.9 copy-start.14
  32.8 0.9 copy-start.16
  33.8 0.9 copy-start.18
  34.7 0.9 copy-start.21
  41.9 1.9 %copy-start.10 = (bf16[256,1024]{1,0:T(8,128)(2,1)}, bf16[256,1024]{1,0:T(8,128)(2,1)S(1)}, u32[]{:S(2)}) copy-start(bf16[256,1024]{1,0:T(8,128)(2,1)S(1)} %get-tuple-element.35) | copy-start | bytes 1572868
  41.9 14.8 %collective-permute-start.9 = (bf16[256,1024]{1,0:T(8,128)(2,1)}, bf16[256,1024]{1,0:T(8,128)(2,1)}, u32[]{:S(2)}, u32[]{:S(2)}) collective-permute-start(bf16[256,1024]{1,0:T(8,128)(2,1)} %get-tuple-element.36), channel_id=1, source_target_pairs={{0,1},{1,0},{2,3},{3,2},{4,5},{5,4},{6,7},{7,6},{8,9},{9,8},{10,11... | collective-permute-start | bytes 1572872 | tf_op jit(solution)/shard_map/ppermute | solution.py:156
  45.8 18.6 %copy-start.2 = (bf16[576,512]{1,0:T(8,128)(2,1)S(1)}, bf16[576,512]{1,0:T(8,128)(2,1)}, u32[]{:S(2)}) copy-start(bf16[576,512]{1,0:T(8,128)(2,1)} %tok_ref.3) | copy-start | bytes 1769476
  45.8 18.6 %copy-start.4 = (bf16[576,512]{1,0:T(8,128)(2,1)S(1)}, bf16[576,512]{1,0:T(8,128)(2,1)}, u32[]{:S(2)}) copy-start(bf16[576,512]{1,0:T(8,128)(2,1)} %go_ref.3) | copy-start | bytes 1769476
  45.8 18.6 %copy-start.6 = (bf16[576]{0:T(1024)(128)(2,1)S(1)}, bf16[576]{0:T(1024)(128)(2,1)}, u32[]{:S(2)}) copy-start(bf16[576]{0:T(1024)(128)(2,1)} %gate_ref.3) | copy-start | bytes 3460
  45.8 18.6 %copy-start.8 = (f32[512]{0:T(512)S(1)}, f32[512]{0:T(512)}, u32[]{:S(2)}) copy-start(f32[512]{0:T(512)} %param.8) | copy-start | bytes 6148
  45.8 18.6 %all-to-all-start = ((bf16[8,96,640]{2,1,0:T(8,128)(2,1)}), bf16[8,96,640]{2,1,0:T(8,128)(2,1)S(1)}, u32[]{:S(2)}, u32[]{:S(2)}) async-start(bf16[8,96,640]{2,1,0:T(8,128)(2,1)} %back.1), calls=%async_computation | async-start | bytes 1966080 | tf_op jit(solution)/shard_map/all_to_all | solution.py:222
  49.7 18.0 %collective-permute-start.8 = (bf16[256,1024]{1,0:T(8,128)(2,1)}, bf16[256,1024]{1,0:T(8,128)(2,1)}, u32[]{:S(2)}, u32[]{:S(2)}) collective-permute-start(bf16[256,1024]{1,0:T(8,128)(2,1)} %copy-done.10), channel_id=1, source_target_pairs={{0,2},{3,1},{4,6},{7,5},{8,10},{11,9},{12,14},{15,13},{16,18},{19,... | collective-permute-start | bytes 1572872 | tf_op jit(solution)/shard_map/ppermute | solution.py:158
  55.0 12.7 %collective-permute-start.7 = (bf16[256,1024]{1,0:T(8,128)(2,1)}, bf16[256,1024]{1,0:T(8,128)(2,1)}, u32[]{:S(2)}, u32[]{:S(2)}) collective-permute-start(bf16[256,1024]{1,0:T(8,128)(2,1)} %copy-done.10), channel_id=1, source_target_pairs={{1,2},{2,1},{5,6},{6,5},{9,10},{10,9},{13,14},{14,13},{17,18},{18,... | collective-permute-start | bytes 1572872 | tf_op jit(solution)/shard_map/ppermute | solution.py:157
  58.7 32.1 %collective-permute-start.10 = (bf16[256,1024]{1,0:T(8,128)(2,1)}, bf16[256,1024]{1,0:T(8,128)(2,1)}, u32[]{:S(2)}, u32[]{:S(2)}) collective-permute-start(bf16[256,1024]{1,0:T(8,128)(2,1)} %fusion.2), channel_id=1, source_target_pairs={{0,1},{3,2},{1,3},{2,0},{4,5},{7,6},{5,7},{6,4},{8,9},{11,10},{9,1... | collective-permute-start | bytes 1572872 | tf_op jit(solution)/shard_map/ppermute | solution.py:161
  (2 other events, 1.3 us)

commit v3 on v2

v3 whole, which is shorter than its diff:
```python
import functools

import jax
import jax.numpy as jnp
from jax import lax
from jax.experimental import pallas as pl
from jax.experimental.pallas import tpu as pltpu
from jax.sharding import PartitionSpec as P

epsilon = 1e-05
F32 = jnp.float32
BF16 = jnp.bfloat16
LANES = 128
MIB = 1024 * 1024

vmem = pl.BlockSpec(memory_space=pltpu.VMEM)
smem = pl.BlockSpec(memory_space=pltpu.SMEM)
hbm = pl.BlockSpec(memory_space=pltpu.HBM)
anywhere = pl.BlockSpec(memory_space=pl.ANY)


def dot(left, right, contract=((1,), (0,))):
    return lax.dot_general(left, right, (contract, ((), ())), preferred_element_type=F32)


def normalize(tokens):
    values = tokens.astype(F32)
    center = values - jnp.mean(values, axis=-1, keepdims=True)
    spread = lax.rsqrt(jnp.mean(center * center, axis=-1, keepdims=True) + epsilon)
    return center * spread, spread


def kernel_call(kernel, name, flops, nbytes, outs, ins, scratch=(), places=None, vmem_mib=24):
    return pl.pallas_call(
        kernel,
        name=name,
        out_shape=outs,
        in_specs=ins,
        out_specs=places or [vmem] * len(outs),
        scratch_shapes=list(scratch),
        compiler_params=pltpu.CompilerParams(vmem_limit_bytes=vmem_mib * MIB),
        cost_estimate=pl.CostEstimate(flops=flops, bytes_accessed=nbytes, transcendentals=0),
    )


def start_copies(pairs, sems):
    copies = [pltpu.make_async_copy(src, dst, sems.at[i]) for i, (src, dst) in enumerate(pairs)]
    for copy in copies:
        copy.start()
    return copies


def place_kernel(sources, capacity, me, ids_hbm, gate_hbm, tok_hbm, gain_hbm, go_hbm, target_ref, *refs):
    outs = refs[:sources]
    ids_ref, gate_ref, tok_ref, gain_ref, go_ref, sent_ref, in_sems, out_sems = refs[sources:]
    rows = sources * capacity
    tok_rows, width = tok_ref.shape
    loads = start_copies(
        [(ids_hbm, ids_ref), (tok_hbm, tok_ref), (gain_hbm, gain_ref), (gate_hbm, gate_ref), (go_hbm, go_ref)],
        in_sems,
    )
    earlier = lax.broadcasted_iota(jnp.int32, (tok_rows, tok_rows), 0) < lax.broadcasted_iota(
        jnp.int32, (tok_rows, tok_rows), 1
    )
    earlier = jnp.where(earlier, 1.0, 0.0).astype(BF16)
    loads[0].wait()
    ids = ids_ref[...]
    onehot = (lax.broadcasted_iota(jnp.int32, (sources, tok_rows), 0) == ids).astype(F32)
    before = dot(onehot.astype(BF16), earlier)
    rank = jnp.sum(before * onehot, axis=0, keepdims=True).astype(jnp.int32)
    kept = rank < capacity
    target_ref[...] = jnp.where(kept, ids * capacity + rank, -1)
    target = jnp.where(kept, jnp.bitwise_xor(ids, me[0]) * capacity + rank, -1)
    hit = lax.broadcasted_iota(jnp.int32, (rows, tok_rows), 0) == target
    pick = jnp.where(hit, 1.0, 0.0).astype(BF16)
    loads[1].wait()
    loads[2].wait()
    scaled, _ = normalize(tok_ref[...])
    normed = (scaled * gain_ref[...]).astype(BF16)
    sent_ref[:, :width] = dot(pick, normed).astype(BF16)
    loads[3].wait()
    pick_gate = jnp.where(hit, gate_ref[...].astype(F32).reshape(1, tok_rows), 0.0).astype(BF16)
    loads[4].wait()
    sent_ref[:, width:] = dot(pick_gate, go_ref[...]).astype(BF16)
    spans = [pl.ds(j * capacity, capacity) for j in range(sources)]
    if capacity % 16:
        for j in range(sources):
            outs[j][...] = sent_ref[spans[j], :]
        return
    for copy in start_copies([(sent_ref.at[spans[j]], outs[j]) for j in range(sources)], out_sems):
        copy.wait()


def gelu_parts(value):
    root = 0.7978845608028654
    square = value * value
    tan = jnp.tanh(root * (value + 0.044715 * value * square))
    half = 0.5 * (1.0 + tan)
    slope = half + 0.5 * value * (1.0 - tan * tan) * (root * (1.0 + 3.0 * 0.044715 * square))
    return value * half, slope


def expert_chunk(rows_ref, w_in_ref, w_out_ref, part):
    width = w_in_ref.shape[0]
    delta = rows_ref[:, width:]
    preact = dot(rows_ref[:, :width], w_in_ref[:, part])
    act_float, slope = gelu_parts(preact)
    act = act_float.astype(BF16)
    grad_act = dot(delta, w_out_ref[part, :], ((1,), (1,)))
    weight = dot(act.T, delta).astype(BF16)
    total = jnp.sum(act.astype(F32) * grad_act, axis=1, keepdims=True)
    return weight, (grad_act * slope).astype(BF16), total


def early_kernel(sources, capacity, pieces, order, w_in_ref, w_out_ref, *refs):
    blocks = refs[:sources]
    first_ref, second_ref, rows_ref, gpre_ref, total_ref, sems = refs[sources:]
    piece_f = w_in_ref.shape[1] // pieces
    spans = [pl.ds(j * capacity, capacity) for j in range(sources)]
    if capacity % 16:
        for j in range(sources):
            rows_ref[spans[j], :] = blocks[j][...]
    else:
        for copy in start_copies([(blocks[j], rows_ref.at[spans[j]]) for j in range(sources)], sems):
            copy.wait()
    sums = []
    for j, out_ref in enumerate((first_ref, second_ref)):
        part = pl.ds(pl.multiple_of(order[j] * piece_f, piece_f), piece_f)
        out_ref[...], grad_pre, total = expert_chunk(rows_ref, w_in_ref, w_out_ref, part)
        gpre_ref[:, j * piece_f : (j + 1) * piece_f] = grad_pre
        sums.append(total)
    total_ref[...] = sums[0] + sums[1]


def late_kernel(
    pieces, order, w_in_ref, w_out_ref, rows_ref, half_ref, total_ref, third_ref, own_ref, *refs
):
    outs = refs[:pieces]
    gpre_ref, extra_ref, turned_ref = refs[pieces:]
    width, hidden = w_in_ref.shape
    piece_d, piece_f = width // pieces, hidden // pieces
    parts = [pl.ds(pl.multiple_of(order[j] * piece_f, piece_f), piece_f) for j in range(pieces)]
    total = total_ref[...]
    for j in range(2):
        gpre_ref[:, parts[j]] = half_ref[:, j * piece_f : (j + 1) * piece_f]
    for j, out_ref in enumerate((third_ref, own_ref)):
        out_ref[...], gpre_ref[:, parts[2 + j]], more = expert_chunk(
            rows_ref, w_in_ref, w_out_ref, parts[2 + j]
        )
        total = total + more
    for j in range(pieces):
        start = pl.multiple_of(order[j] * piece_d, piece_d)
        turned_ref[j * piece_d : (j + 1) * piece_d, :] = rows_ref[:, pl.ds(start, piece_d)].T
    for i in range(pieces):
        chunk = slice(i * piece_f, (i + 1) * piece_f)
        weight = dot(turned_ref[...], gpre_ref[:, chunk]).astype(BF16)
        for j in range(pieces):
            outs[j][:, chunk] = weight[j * piece_d : (j + 1) * piece_d]
    high = total.astype(BF16).astype(F32)
    lane = lax.broadcasted_iota(jnp.int32, extra_ref.shape, 1)
    extra_ref[...] = jnp.where(lane == 0, high, jnp.where(lane == 1, total - high, 0.0)).astype(BF16)


def back_kernel(sources, capacity, me, gpre_ref, w_in_ref, extra_ref, out_ref):
    width = w_in_ref.shape[0]
    grad = dot(gpre_ref[...], w_in_ref[...], ((1,), (1,))).astype(BF16)
    for j in range(sources):
        block = slice(j * capacity, (j + 1) * capacity)
        source = jnp.bitwise_xor(me[0], j)
        out_ref[source, :, :width] = grad[block]
        out_ref[source, :, width:] = extra_ref[block, :]


def finish_kernel(target_ref, gate_ref, tok_ref, gain_ref, go_ref, back_ref, tokens_out, gate_out):
    rows = back_ref.shape[0]
    tok_rows, width = tok_ref.shape
    spots = jnp.broadcast_to(target_ref[...].astype(F32), (8, tok_rows)).T[:, :1].astype(jnp.int32)
    hit = lax.broadcasted_iota(jnp.int32, (tok_rows, rows), 1) == spots
    got = dot(jnp.where(hit, 1.0, 0.0).astype(BF16), back_ref[...])
    sums = got[:, width:].T
    gate_row = gate_ref[...].astype(F32).reshape(1, tok_rows)
    gate_out[...] = ((sums[0:1] + sums[1:2]) / gate_row).astype(BF16).reshape(tok_rows)
    scaled, spread = normalize(tok_ref[...])
    grad = got[:, :width] * gain_ref[...]
    mean = jnp.mean(grad, axis=-1, keepdims=True)
    cross = jnp.mean(grad * scaled, axis=-1, keepdims=True)
    branch = spread * (grad - mean - scaled * cross)
    tokens_out[...] = (go_ref[...].astype(F32) + branch).astype(BF16)


def swap_blocks(blocks):
    count = len(blocks)
    return [
        blocks[j]
        if j == count - 2
        else lax.ppermute(blocks[j], "space", [(i, i ^ j ^ (count - 2)) for i in range(count)])
        for j in range(count)
    ]


def add(*terms):
    return functools.reduce(jnp.add, [t.astype(F32) for t in terms])


def line_sums(outs, ins, place, behind):
    inner = (place == 1) | (place == 2)
    sums, early = [], []
    for first, second, third, own in (outs, ins):
        if early:
            first, swapped = lax.optimization_barrier((first, swapped))
            second, behind, *early = lax.optimization_barrier((second, behind, *early))
            sums[0][1:4] = *early, jnp.where(inner, 0.0, swapped.astype(F32))
        swapped = lax.ppermute(first, "dp", [(0, 1), (1, 0), (2, 3), (3, 2)])
        middle = lax.ppermute(second, "dp", [(1, 2), (2, 1)])
        across = lax.ppermute(second, "dp", [(0, 2), (3, 1)])
        passed = jnp.where(inner, add(third, swapped), third.astype(F32)).astype(BF16)
        last = lax.ppermute(passed, "dp", [(0, 1), (3, 2), (1, 3), (2, 0)])
        early = [middle, across]
        kept = jnp.where(inner, 0.0, swapped.astype(F32))
        sums.append([own, middle, across, kept, last])
    return *[add(*terms) for terms in sums], behind


def body(tokens, gain, w_in, w_out, expert_ids, gate, grad_out):
    sources = lax.axis_size("space")
    groups = lax.axis_size("dp")
    tok_rows, width = tokens.shape
    hidden = w_in.shape[2]
    capacity = ((tok_rows * 5 // 4 + sources - 1) // sources + 7) // 8 * 8
    rows = sources * capacity
    pieces = 4
    me = (lax.axis_index("space").astype(jnp.int32) ^ (sources - 2)).reshape(1)
    place = lax.axis_index("dp").astype(jnp.int32)
    ids_row = expert_ids.reshape(1, tok_rows)
    gain_row = gain.reshape(1, width)
    weight_in, weight_out = w_in[0], w_out[0]
    shape = jax.ShapeDtypeStruct
    sems = pltpu.SemaphoreType.DMA
    block_place = vmem if capacity % 16 else anywhere
    io_bytes = 2 * (2 * tok_rows * width + 2 * rows * width)

    target, *sent = kernel_call(
        functools.partial(place_kernel, sources, capacity),
        "place",
        4 * rows * tok_rows * width,
        io_bytes,
        [shape((1, tok_rows), jnp.int32)] + [shape((capacity, 2 * width), BF16)] * sources,
        [smem] + [hbm] * 5,
        [
            pltpu.VMEM((1, tok_rows), jnp.int32),
            pltpu.VMEM((tok_rows,), BF16),
            pltpu.VMEM((tok_rows, width), BF16),
            pltpu.VMEM((1, width), F32),
            pltpu.VMEM((tok_rows, width), BF16),
            pltpu.VMEM((rows, 2 * width), BF16),
            sems((5,)),
            sems((sources,)),
        ],
        places=[vmem] + [block_place] * sources,
        vmem_mib=56,
    )(me, ids_row, gate, tokens, gain_row, grad_out)
    arrived = swap_blocks(sent)

    if groups == 4:
        first = jnp.where(place % 2 == 0, 3, 0)
        second = jnp.where(place < 2, 2, 1)
        order = jnp.stack([first, second, 6 - first - second - place, place]).astype(jnp.int32)
    else:
        order = jnp.arange(pieces, dtype=jnp.int32)
    piece_in = shape((width // pieces, hidden), BF16)
    piece_out = shape((hidden // pieces, width), BF16)
    first_out, second_out, got_rows, half, total = kernel_call(
        functools.partial(early_kernel, sources, capacity, pieces),
        "early",
        3 * rows * width * hidden,
        4 * rows * width + 4 * width * hidden,
        [
            piece_out,
            piece_out,
            shape((rows, 2 * width), BF16),
            shape((rows, hidden // pieces * 2), BF16),
            shape((rows, 1), F32),
        ],
        [smem] + [vmem] * 2 + [block_place] * sources,
        [sems((sources,))],
    )(order, weight_in, weight_out, *arrived)
    third_out, own_out, *parts_in, gpre, extra = kernel_call(
        functools.partial(late_kernel, pieces),
        "late",
        1,
        1,
        [piece_out] * 2
        + [piece_in] * pieces
        + [shape((rows, hidden), BF16), shape((rows, LANES), BF16)],
        [smem] + [vmem] * 5,
        [pltpu.VMEM((width, rows), BF16)],
    )(order, weight_in, weight_out, got_rows, half, total)
    parts_out = [first_out, second_out, third_out, own_out]

    (returned,) = kernel_call(
        functools.partial(back_kernel, sources, capacity),
        "back",
        1,
        1,
        [shape((sources, capacity, width + LANES), BF16)],
        [smem] + [vmem] * 3,
    )(me, gpre, weight_in, extra)
    if groups == 4:
        grad_w_out, grad_w_in, returned = line_sums(parts_out, parts_in, place, returned)
    else:
        grad_w_in, grad_w_out = (
            lax.psum_scatter(
                jnp.concatenate(part), "dp", scatter_dimension=0, tiled=True
            ).astype(F32)
            for part in (parts_in, parts_out)
        )
    back = lax.all_to_all(returned, "space", split_axis=0, concat_axis=0, tiled=True)
    grad_tokens, grad_gate = kernel_call(
        finish_kernel,
        "finish",
        1,
        1,
        [shape((tok_rows, width), BF16), shape((tok_rows,), BF16)],
        [vmem] * 6,
    )(target, gate, tokens, gain_row, grad_out, back.reshape(rows, width + LANES))
    return (grad_tokens, grad_gate, grad_w_in[None], grad_w_out[None])


def solution(mesh):
    placed = (
        P(("space", "dp"), None),
        P(),
        P("space", None, None),
        P("space", None, None),
        P(("space", "dp"), None),
        P(("space", "dp")),
        P(("space", "dp"), None),
    )
    return jax.shard_map(
        body,
        mesh=mesh,
        in_specs=placed,
        out_specs=(
            P(("space", "dp"), None),
            P(("space", "dp")),
            P("space", "dp", None),
            P("space", "dp", None),
        ),
        check_vma=False,
    )
```

time: 95.1 us -> 102 us (1.073)
  waiting for transfers between devices: 38.1 us -> 31.3 us
  Pallas kernels: 13.3 us -> 19.7 us
  starting transfers between devices: 23.9 us -> 28.3 us
  local copies, waits for them, and re-layouts: 13.1 us -> 16.4 us
  other arithmetic: 5.5 us -> 4.42 us
    ppermute x1 -> x2, starting transfers between devices: 5.31 us -> 11.1 us  [line_sums(): across = lax.ppermute(second, 'dp', [(0, 2), (3, 1)])]
    ppermute x1 -> x2, waiting for transfers between devices: 23.2 us -> 17.4 us  [line_sums(): last = lax.ppermute(passed, 'dp', [(0, 1), (3, 2), (1, 3), (2, 0)])]
    unnamed x44 -> x70, local copies, waits for them, and re-layouts: 12.2 us -> 16.4 us
    pallas_call x3 -> x4, Pallas kernels: 10.8 us -> 14.7 us  [the longest x1 5.62 us: body(): kernel_call(functools.partial(early_kernel, sources, capacity, pieces), '...]
    all_to_all x1, waiting for transfers between devices: 3.51 us -> 0.01 us  [body(): lax.all_to_all(returned, 'space', split_axis=0, concat_axis=0, tiled=True)]
    pallas_call x1, Pallas kernels: 2.41 us -> 4.96 us  [body(): kernel_call(functools.partial(place_kernel, sources, capacity), 'place',...]
    broadcast_in_dim x1 -> x2, other arithmetic: 0.83 us -> 3.18 us  [body(): return (grad_tokens, grad_gate, grad_w_in[None], grad_w_out[None])]
    add x1 -> x0, other arithmetic: 1.96 us -> none  [add(): return functools.reduce(jnp.add, [t.astype(F32) for t in terms])]
  transfers between devices with their start and end apart: 12 -> 16, of which waited for: 7 -> 7; matrix products, arithmetic and copies ran while one was open for 3% -> 4% of each run, Pallas kernels for 5% -> 6%
where the time goes in v3:
time: 102 us; the launch traced here: 101 us
  waiting for transfers between devices  31.3 us (31%)
  starting transfers between devices  28.3 us (28%)
  Pallas kernels  19.7 us (19%)
  local copies, waits for them, and re-layouts  16.4 us (16%)
  other arithmetic  4.42 us (4%)
    ppermute x2, waiting for transfers between devices, line_sums(): last = lax.ppermute(passed, 'dp', [(0, 1), (3, 2), (1, 3), (2, 0)])  17.4 us
    unnamed x70, local copies, waits for them, and re-layouts  16.4 us
    ppermute x7, waiting for transfers between devices, swap_blocks(): lax.ppermute(blocks[j], 'space', [(i, i ^ j ^ count - 2) for i in range(c...  12 us
    ppermute x2, starting transfers between devices, line_sums(): across = lax.ppermute(second, 'dp', [(0, 2), (3, 1)])  11.1 us
    ppermute x7, starting transfers between devices, swap_blocks(): lax.ppermute(blocks[j], 'space', [(i, i ^ j ^ count - 2) for i in range(c...  7.54 us
    pallas_call x1, Pallas kernels, body(): kernel_call(functools.partial(early_kernel, sources, capacity, pieces), '...  5.62 us
    pallas_call x1, Pallas kernels, body(): kernel_call(functools.partial(place_kernel, sources, capacity), 'place',...  4.96 us
    pallas_call x1, Pallas kernels, body(): kernel_call(functools.partial(late_kernel, pieces), 'late', 1, 1, [piece_...  4.54 us
  transfers between devices with their start and end apart: 16, of which 7 were waited for; matrix products, arithmetic and copies ran while one was open for 4% of the time, Pallas kernels for 6%

profile of v3, /device:TPU:0, one launch (start us, length us, event | category | flops | bytes accessed | tf_op | source)
XLA Modules:
  0.0 101.0 jit_solution(5519644895253351936)
XLA Ops:
  0.6 5.0 %place.1 = (s32[1,576]{1,0:T(1,128)}, bf16[96,1024]{1,0:T(8,128)(2,1)}, bf16[96,1024]{1,0:T(8,128)(2,1)}, bf16[96,1024]{1,0:T(8,128)(2,1)}, bf16[96,1024]{1,0:T(...) custom-call(s32[1]{0:T(128)} %bitcast.me, ...), custom_call_target="tpu_custom_call" | custom-call | flops 905969664 | bytes 2752512 | tf_op jit(solution)/shard_map/place/pallas_call | solution.py:242
  5.6 4.0 %collective-permute-start = (bf16[96,1024]{1,0:T(8,128)(2,1)}, bf16[96,1024]{1,0:T(8,128)(2,1)S(1)}, u32[]{:S(2)}, u32[]{:S(2)}) collective-permute-start(bf16[96,1024]{1,0:T(8,128)(2,1)} %get-tuple-element.35), channel_id=1, source_target_pairs={{0,24},{4,28},{8,16},{12,20},{16,8},{20,12},{24,0},{28,4},{1,25},{... | collective-permute-start | bytes 589832 | tf_op jit(solution)/shard_map/ppermute | solution.py:196
  9.6 1.2 %collective-permute-start.2 = (bf16[96,1024]{1,0:T(8,128)(2,1)}, bf16[96,1024]{1,0:T(8,128)(2,1)S(1)}, u32[]{:S(2)}, u32[]{:S(2)}) collective-permute-start(bf16[96,1024]{1,0:T(8,128)(2,1)} %get-tuple-element.37), channel_id=1, source_target_pairs={{0,16},{4,20},{8,24},{12,28},{16,0},{20,4},{24,8},{28,12},{1,17},{... | collective-permute-start | bytes 589832 | tf_op jit(solution)/shard_map/ppermute | solution.py:196
  11.3 1.7 %collective-permute-start.4 = (bf16[96,1024]{1,0:T(8,128)(2,1)}, bf16[96,1024]{1,0:T(8,128)(2,1)S(1)}, u32[]{:S(2)}, u32[]{:S(2)}) collective-permute-start(bf16[96,1024]{1,0:T(8,128)(2,1)} %get-tuple-element.39), channel_id=1, source_target_pairs={{0,8},{4,12},{8,0},{12,4},{16,24},{20,28},{24,16},{28,20},{1,9},{5... | collective-permute-start | bytes 589832 | tf_op jit(solution)/shard_map/ppermute | solution.py:196
  13.0 2.6 %collective-permute-done.refs_0_ = bf16[96,1024]{1,0:T(8,128)(2,1)S(1)} collective-permute-done((bf16[96,1024]{1,0:T(8,128)(2,1)}, bf16[96,1024]{1,0:T(8,128)(2,1)S(1)}, u32[]{:S(2)}, u32[]{:S(2)}) %collective-permute-start) | collective-permute-done | bytes 196640 | tf_op jit(solution)/shard_map/ppermute | solution.py:196
  16.3 3.2 %collective-permute-done.1.refs_1_ = bf16[96,1024]{1,0:T(8,128)(2,1)S(1)} collective-permute-done((bf16[96,1024]{1,0:T(8,128)(2,1)}, bf16[96,1024]{1,0:T(8,128)(2,1)S(1)}, u32[]{:S(2)}, u32[]{:S(2)}) %collective-permute-start.1) | collective-permute-done | bytes 196640 | tf_op jit(solution)/shard_map/ppermute | solution.py:196
  20.4 2.8 %collective-permute-done.2.refs_2_ = bf16[96,1024]{1,0:T(8,128)(2,1)S(1)} collective-permute-done((bf16[96,1024]{1,0:T(8,128)(2,1)}, bf16[96,1024]{1,0:T(8,128)(2,1)S(1)}, u32[]{:S(2)}, u32[]{:S(2)}) %collective-permute-start.2) | collective-permute-done | bytes 196640 | tf_op jit(solution)/shard_map/ppermute | solution.py:196
  23.8 3.4 %collective-permute-done.3.refs_3_ = bf16[96,1024]{1,0:T(8,128)(2,1)S(1)} collective-permute-done((bf16[96,1024]{1,0:T(8,128)(2,1)}, bf16[96,1024]{1,0:T(8,128)(2,1)S(1)}, u32[]{:S(2)}, u32[]{:S(2)}) %collective-permute-start.3) | collective-permute-done | bytes 196640 | tf_op jit(solution)/shard_map/ppermute | solution.py:196
  30.0 1.2 %copy-done.1 = bf16[1,1024,512]{2,1,0:T(8,128)(2,1)S(1)} copy-done((bf16[1,1024,512]{2,1,0:T(8,128)(2,1)S(1)}, bf16[1,1024,512]{2,1,0:T(8,128)(2,1)}, u32[]{:S(2)}) %copy-start.1) | copy-done | bytes 1048600
  31.2 0.9 copy-done.21
  32.2 0.9 copy-done.23
  33.1 0.9 copy-done.25
  34.0 0.9 copy-done.27
  34.9 0.9 copy-done.29
  38.6 5.6 %early.1 = (bf16[256,512]{1,0:T(8,128)(2,1)}, bf16[256,512]{1,0:T(8,128)(2,1)}, bf16[768,1024]{1,0:T(8,128)(2,1)S(1)}, bf16[768,512]{1,0:T(8,128)(2,1)S(1)}, f32[768,1]{1,0:T(8,128)S(1)}) custom-call(s32[4]{0:T(128)S(1)} %pad_add_fusion.order, bf16[512,1024]{1,0:T(8,128)(2,1)S(1)} %bitcast.14, bf16[1024,512]{1,0:T(8,128)(2,1)S(1)} %bitcast.18, ...), custom_call_target="tpu_custom_call" | custom-call | flops 1207959552 | bytes 3670016 | tf_op jit(solution)/shard_map/early/pallas_call | solution.py:272
  45.0 1.4 %collective-permute-start.7 = (bf16[256,512]{1,0:T(8,128)(2,1)}, bf16[256,512]{1,0:T(8,128)(2,1)}, u32[]{:S(2)}, u32[]{:S(2)}) collective-permute-start(bf16[256,512]{1,0:T(8,128)(2,1)} %get-tuple-element.49), channel_id=1, source_target_pairs={{1,2},{2,1},{5,6},{6,5},{9,10},{10,9},{13,14},{14,13},{17,18},{18,... | collective-permute-start | bytes 786440 | tf_op jit(solution)/shard_map/ppermute | solution.py:214
  46.4 6.4 %collective-permute-start.8 = (bf16[256,512]{1,0:T(8,128)(2,1)}, bf16[256,512]{1,0:T(8,128)(2,1)}, u32[]{:S(2)}, u32[]{:S(2)}) collective-permute-start(bf16[256,512]{1,0:T(8,128)(2,1)} %get-tuple-element.49), channel_id=1, source_target_pairs={{0,2},{3,1},{4,6},{7,5},{8,10},{11,9},{12,14},{15,13},{16,18},{19,... | collective-permute-start | bytes 786440 | tf_op jit(solution)/shard_map/ppermute | solution.py:215
  52.8 1.2 %copy-done.2 = bf16[1,1024,512]{2,1,0:T(8,128)(2,1)S(1)} copy-done((bf16[1,1024,512]{2,1,0:T(8,128)(2,1)S(1)}, bf16[1,1024,512]{2,1,0:T(8,128)(2,1)}, u32[]{:S(2)}) %copy-start.2) | copy-done | bytes 1048600
  54.0 1.0 copy-done.6
  55.0 4.5 %late.1 = (bf16[256,512]{1,0:T(8,128)(2,1)S(1)}, bf16[256,512]{1,0:T(8,128)(2,1)S(1)}, bf16[128,1024]{1,0:T(8,128)(2,1)}, bf16[128,1024]{1,0:T(8,128)(2,1)S(1)},...) custom-call(s32[4]{0:T(128)S(1)} %pad_add_fusion.order, ...), custom_call_target="tpu_custom_call" | custom-call | flops 1 | bytes 1 | tf_op jit(solution)/shard_map/late/pallas_call | solution.py:287
  59.6 2.0 %back.1 = bf16[8,96,640]{2,1,0:T(8,128)(2,1)} custom-call(s32[1]{0:T(128)} %bitcast.me, bf16[768,1024]{1,0:T(8,128)(2,1)S(1)} %get-tuple-element.47.gpre_ref, bf16[512,1024]{1,0:T(8,128)(2,1)S(1)} %bitcast.16, bf16[768,128]{1,0:T(8,128)(2,1)S(1)} %get-tuple-element.48.extra_ref), custom_call_target="tpu_custom_call" | custom-call | flops 1 | bytes 1 | tf_op jit(solution)/shard_map/back/pallas_call | solution.py:300
  61.7 1.9 %collective-permute-done.11 = bf16[256,512]{1,0:T(8,128)(2,1)} collective-permute-done((bf16[256,512]{1,0:T(8,128)(2,1)}, bf16[256,512]{1,0:T(8,128)(2,1)}, u32[]{:S(2)}, u32[]{:S(2)}) %collective-permute-start.11) | collective-permute-done | bytes 262176 | tf_op jit(solution)/shard_map/ppermute | solution.py:213
  63.6 2.5 %collective-permute-start.12 = (bf16[128,1024]{1,0:T(8,128)(2,1)}, bf16[128,1024]{1,0:T(8,128)(2,1)S(1)}, u32[]{:S(2)}, u32[]{:S(2)}) collective-permute-start(bf16[128,1024]{1,0:T(8,128)(2,1)} %get-tuple-element.57), channel_id=1, source_target_pairs={{0,1},{1,0},{2,3},{3,2},{4,5},{5,4},{6,7},{7,6},{8,9},{9,8},{10,11... | collective-permute-start | bytes 786440 | tf_op jit(solution)/shard_map/ppermute | solution.py:213
  66.1 3.7 %all-to-all-start = ((bf16[8,96,640]{2,1,0:T(8,128)(2,1)}), bf16[8,96,640]{2,1,0:T(8,128)(2,1)S(1)}, u32[]{:S(2)}, u32[]{:S(2)}) async-start(bf16[8,96,640]{2,1,0:T(8,128)(2,1)} %back.1), calls=%async_computation | async-start | bytes 1966080 | tf_op jit(solution)/shard_map/all_to_all | solution.py:317
  69.8 1.1 %fusion.4 = bf16[256,512]{1,0:T(8,128)(2,1)S(1)} fusion(bf16[256,512]{1,0:T(8,128)(2,1)} %collective-permute-done.11, bf16[256,512]{1,0:T(8,128)(2,1)S(1)} %copy-done.14, pred[]{:T(512)S(6)} %or.3), kind=kLoop, calls=%fused_computation.7 | loop fusion | flops 655360 | bytes 786433 | tf_op jit(solution)/shard_map/convert_element_type | solution.py:216
  71.1 4.7 %collective-permute-start.10 = (bf16[128,1024]{1,0:T(8,128)(2,1)S(1)}, bf16[128,1024]{1,0:T(8,128)(2,1)S(1)}, u32[]{:S(2)}, u32[]{:S(2)}) collective-permute-start(bf16[128,1024]{1,0:T(8,128)(2,1)S(1)} %copy-done.19), channel_id=1, source_target_pairs={{0,2},{3,1},{4,6},{7,5},{8,10},{11,9},{12,14},{15,13},{16,18},{19,... | collective-permute-start | bytes 786440 | tf_op jit(solution)/shard_map/ppermute | solution.py:215
  76.6 1.2 %collective-permute-start.13 = (bf16[128,1024]{1,0:T(8,128)(2,1)S(1)}, bf16[128,1024]{1,0:T(8,128)(2,1)S(1)}, u32[]{:S(2)}, u32[]{:S(2)}) collective-permute-start(bf16[128,1024]{1,0:T(8,128)(2,1)S(1)} %fusion.3), channel_id=1, source_target_pairs={{0,1},{3,2},{1,3},{2,0},{4,5},{7,6},{5,7},{6,4},{8,9},{11,10},{9,1... | collective-permute-start | bytes 786440 | tf_op jit(solution)/shard_map/ppermute | solution.py:217
  77.8 8.8 %collective-permute-done.14 = bf16[256,512]{1,0:T(8,128)(2,1)S(1)} collective-permute-done((bf16[256,512]{1,0:T(8,128)(2,1)S(1)}, bf16[256,512]{1,0:T(8,128)(2,1)S(1)}, u32[]{:S(2)}, u32[]{:S(2)}) %collective-permute-start.14) | collective-permute-done | bytes 262176 | tf_op jit(solution)/shard_map/ppermute | solution.py:217
  86.6 2.2 %add_bitcast_fusion = f32[1,256,512]{2,1,0:T(8,128)} fusion(bf16[256,512]{1,0:T(8,128)(2,1)S(1)} %collective-permute-done.14, bf16[256,512]{1,0:T(8,128)(2,1)} %collective-permute-done.11, bf16[256,512]{1,0:T(8,128)(2,1)} %collective-permute-done.8, bf16[256,512]{1,0:T(8,128)(2,1)} %collective-permute-done.7, bf16[256,512]{1,0:T(8,128)(2,1)S(1)} %copy-done.10, ...), kind=kLoop, calls=%fused_computation.8 | loop fusion | flops 1310720 | bytes 1835009 | tf_op jit(solution)/shard_map/broadcast_in_dim | solution.py:326
  88.8 8.6 %collective-permute-done.13 = bf16[128,1024]{1,0:T(8,128)(2,1)S(1)} collective-permute-done((bf16[128,1024]{1,0:T(8,128)(2,1)S(1)}, bf16[128,1024]{1,0:T(8,128)(2,1)S(1)}, u32[]{:S(2)}, u32[]{:S(2)}) %collective-permute-start.13) | collective-permute-done | bytes 262176 | tf_op jit(solution)/shard_map/ppermute | solution.py:217
  97.4 1.0 %fusion.2 = f32[1,128,1024]{2,1,0:T(8,128)} fusion(bf16[128,1024]{1,0:T(8,128)(2,1)S(1)} %collective-permute-done.12, bf16[128,1024]{1,0:T(8,128)(2,1)S(1)} %collective-permute-done.13, bf16[128,1024]{1,0:T(8,128)(2,1)S(1)} %collective-permute-done.10, bf16[128,1024]{1,0:T(8,128)(2,1)S(1)} %collective-permute-done.9, bf16[128,1024]{1,0:T(8,128)(2,1)S(1)} %copy-done.8, ...), kind=kLoop, calls=%fused_computation.5 | loop fusion | flops 1310720 | bytes 1835009 | tf_op jit(solution)/shard_map/broadcast_in_dim | solution.py:326
  98.5 2.6 %finish.1 = (bf16[576,512]{1,0:T(8,128)(2,1)}, bf16[576]{0:T(1024)(128)(2,1)}) custom-call(s32[1,576]{1,0:T(1,128)S(1)} %copy-done.15, bf16[576]{0:T(1024)(128)(2,1)S(1)} %copy-done.16, bf16[576,512]{1,0:T(8,128)(2,1)S(1)} %copy-done.3, f32[1,512]{1,0:T(1,128)S(1)} %bitcast.21, bf16[576,512]{1,0:T(8,128)(2,1)S(1)} %copy-done.4, bf16[768,640]{1,0:T(8,128)(2,1)S(1)} %bitcast.17), custom_call_target="tpu_custom_call" | custom-call | flops 1 | bytes 1 | tf_op jit(solution)/shard_map/finish/pallas_call | solution.py:318
  (80 shorter events, 10.1 us)
Async XLA Ops:
  0.6 29.4 %copy-start = (bf16[1,512,1024]{2,1,0:T(8,128)(2,1)S(1)}, bf16[1,512,1024]{2,1,0:T(8,128)(2,1)}, u32[]{:S(2)}) copy-start(bf16[1,512,1024]{2,1,0:T(8,128)(2,1)} %param.9) | copy-start | bytes 3145732
  5.6 10.0 %collective-permute-start = (bf16[96,1024]{1,0:T(8,128)(2,1)}, bf16[96,1024]{1,0:T(8,128)(2,1)S(1)}, u32[]{:S(2)}, u32[]{:S(2)}) collective-permute-start(bf16[96,1024]{1,0:T(8,128)(2,1)} %get-tuple-element.35), channel_id=1, source_target_pairs={{0,24},{4,28},{8,16},{12,20},{16,8},{20,12},{24,0},{28,4},{1,25},{... | collective-permute-start | bytes 589832 | tf_op jit(solution)/shard_map/ppermute | solution.py:196
  9.6 9.9 %collective-permute-start.1 = (bf16[96,1024]{1,0:T(8,128)(2,1)}, bf16[96,1024]{1,0:T(8,128)(2,1)S(1)}, u32[]{:S(2)}, u32[]{:S(2)}) collective-permute-start(bf16[96,1024]{1,0:T(8,128)(2,1)} %get-tuple-element.36), channel_id=1, source_target_pairs={{0,28},{4,24},{8,20},{12,16},{16,12},{20,8},{24,4},{28,0},{1,29},{... | collective-permute-start | bytes 589832 | tf_op jit(solution)/shard_map/ppermute | solution.py:196
  9.6 13.6 %collective-permute-start.2 = (bf16[96,1024]{1,0:T(8,128)(2,1)}, bf16[96,1024]{1,0:T(8,128)(2,1)S(1)}, u32[]{:S(2)}, u32[]{:S(2)}) collective-permute-start(bf16[96,1024]{1,0:T(8,128)(2,1)} %get-tuple-element.37), channel_id=1, source_target_pairs={{0,16},{4,20},{8,24},{12,28},{16,0},{20,4},{24,8},{28,12},{1,17},{... | collective-permute-start | bytes 589832 | tf_op jit(solution)/shard_map/ppermute | solution.py:196
  10.7 16.5 %collective-permute-start.3 = (bf16[96,1024]{1,0:T(8,128)(2,1)}, bf16[96,1024]{1,0:T(8,128)(2,1)S(1)}, u32[]{:S(2)}, u32[]{:S(2)}) collective-permute-start(bf16[96,1024]{1,0:T(8,128)(2,1)} %get-tuple-element.38), channel_id=1, source_target_pairs={{0,20},{4,16},{8,28},{12,24},{16,4},{20,0},{24,12},{28,8},{1,21},{... | collective-permute-start | bytes 589832 | tf_op jit(solution)/shard_map/ppermute | solution.py:196
  11.3 16.6 %collective-permute-start.4 = (bf16[96,1024]{1,0:T(8,128)(2,1)}, bf16[96,1024]{1,0:T(8,128)(2,1)S(1)}, u32[]{:S(2)}, u32[]{:S(2)}) collective-permute-start(bf16[96,1024]{1,0:T(8,128)(2,1)} %get-tuple-element.39), channel_id=1, source_target_pairs={{0,8},{4,12},{8,0},{12,4},{16,24},{20,28},{24,16},{28,20},{1,9},{5... | collective-permute-start | bytes 589832 | tf_op jit(solution)/shard_map/ppermute | solution.py:196
  16.3 12.3 %collective-permute-start.5 = (bf16[96,1024]{1,0:T(8,128)(2,1)}, bf16[96,1024]{1,0:T(8,128)(2,1)S(1)}, u32[]{:S(2)}, u32[]{:S(2)}) collective-permute-start(bf16[96,1024]{1,0:T(8,128)(2,1)} %get-tuple-element.40), channel_id=1, source_target_pairs={{0,12},{4,8},{8,4},{12,0},{16,28},{20,24},{24,20},{28,16},{1,13},{... | collective-permute-start | bytes 589832 | tf_op jit(solution)/shard_map/ppermute | solution.py:196
  20.1 9.2 %collective-permute-start.6 = (bf16[96,1024]{1,0:T(8,128)(2,1)}, bf16[96,1024]{1,0:T(8,128)(2,1)S(1)}, u32[]{:S(2)}, u32[]{:S(2)}) collective-permute-start(bf16[96,1024]{1,0:T(8,128)(2,1)} %get-tuple-element.42), channel_id=1, source_target_pairs={{0,4},{4,0},{8,12},{12,8},{16,20},{20,16},{24,28},{28,24},{1,5},{5... | collective-permute-start | bytes 589832 | tf_op jit(solution)/shard_map/ppermute | solution.py:196
  45.0 16.6 %collective-permute-start.7 = (bf16[256,512]{1,0:T(8,128)(2,1)}, bf16[256,512]{1,0:T(8,128)(2,1)}, u32[]{:S(2)}, u32[]{:S(2)}) collective-permute-start(bf16[256,512]{1,0:T(8,128)(2,1)} %get-tuple-element.49), channel_id=1, source_target_pairs={{1,2},{2,1},{5,6},{6,5},{9,10},{10,9},{13,14},{14,13},{17,18},{18,... | collective-permute-start | bytes 786440 | tf_op jit(solution)/shard_map/ppermute | solution.py:214
  46.4 15.3 %collective-permute-start.8 = (bf16[256,512]{1,0:T(8,128)(2,1)}, bf16[256,512]{1,0:T(8,128)(2,1)}, u32[]{:S(2)}, u32[]{:S(2)}) collective-permute-start(bf16[256,512]{1,0:T(8,128)(2,1)} %get-tuple-element.49), channel_id=1, source_target_pairs={{0,2},{3,1},{4,6},{7,5},{8,10},{11,9},{12,14},{15,13},{16,18},{19,... | collective-permute-start | bytes 786440 | tf_op jit(solution)/shard_map/ppermute | solution.py:215
  52.8 10.8 %collective-permute-start.11 = (bf16[256,512]{1,0:T(8,128)(2,1)}, bf16[256,512]{1,0:T(8,128)(2,1)}, u32[]{:S(2)}, u32[]{:S(2)}) collective-permute-start(bf16[256,512]{1,0:T(8,128)(2,1)} %get-tuple-element.56), channel_id=1, source_target_pairs={{0,1},{1,0},{2,3},{3,2},{4,5},{5,4},{6,7},{7,6},{8,9},{9,8},{10,11... | collective-permute-start | bytes 786440 | tf_op jit(solution)/shard_map/ppermute | solution.py:213
  59.6 2.0 %copy-start.7 = (bf16[128,1024]{1,0:T(8,128)(2,1)}, bf16[128,1024]{1,0:T(8,128)(2,1)S(1)}, u32[]{:S(2)}) copy-start(bf16[128,1024]{1,0:T(8,128)(2,1)S(1)} %get-tuple-element.53) | copy-start | bytes 786436
  59.6 2.0 %copy-start.9 = (bf16[256,512]{1,0:T(8,128)(2,1)}, bf16[256,512]{1,0:T(8,128)(2,1)S(1)}, u32[]{:S(2)}) copy-start(bf16[256,512]{1,0:T(8,128)(2,1)S(1)} %get-tuple-element.59) | copy-start | bytes 786436
  59.6 2.0 %copy-start.11 = (bf16[128,1024]{1,0:T(8,128)(2,1)}, bf16[128,1024]{1,0:T(8,128)(2,1)S(1)}, u32[]{:S(2)}) copy-start(bf16[128,1024]{1,0:T(8,128)(2,1)S(1)} %get-tuple-element.58) | copy-start | bytes 786436
  59.6 2.0 %copy-start.13 = (bf16[256,512]{1,0:T(8,128)(2,1)}, bf16[256,512]{1,0:T(8,128)(2,1)S(1)}, u32[]{:S(2)}) copy-start(bf16[256,512]{1,0:T(8,128)(2,1)S(1)} %get-tuple-element.63) | copy-start | bytes 786436
  59.6 2.0 %copy-start.18 = (bf16[128,1024]{1,0:T(8,128)(2,1)}, bf16[128,1024]{1,0:T(8,128)(2,1)S(1)}, u32[]{:S(2)}) copy-start(bf16[128,1024]{1,0:T(8,128)(2,1)S(1)} %get-tuple-element.54) | copy-start | bytes 786436
  61.6 8.2 %copy-start.14 = (bf16[256,512]{1,0:T(8,128)(2,1)S(1)}, bf16[256,512]{1,0:T(8,128)(2,1)}, u32[]{:S(2)}) copy-start(bf16[256,512]{1,0:T(8,128)(2,1)} %copy-done.13) | copy-start | bytes 786436
  61.6 9.5 %copy-start.19 = (bf16[128,1024]{1,0:T(8,128)(2,1)S(1)}, bf16[128,1024]{1,0:T(8,128)(2,1)}, u32[]{:S(2)}) copy-start(bf16[128,1024]{1,0:T(8,128)(2,1)} %copy-done.18) | copy-start | bytes 786436
  61.7 14.9 %copy-start.12 = (bf16[128,1024]{1,0:T(8,128)(2,1)S(1)}, bf16[128,1024]{1,0:T(8,128)(2,1)}, u32[]{:S(2)}) copy-start(bf16[128,1024]{1,0:T(8,128)(2,1)} %copy-done.11) | copy-start | bytes 786436
  63.6 23.0 %copy-start.10 = (bf16[256,512]{1,0:T(8,128)(2,1)S(1)}, bf16[256,512]{1,0:T(8,128)(2,1)}, u32[]{:S(2)}) copy-start(bf16[256,512]{1,0:T(8,128)(2,1)} %copy-done.9) | copy-start | bytes 786436
  63.6 12.9 %collective-permute-start.12 = (bf16[128,1024]{1,0:T(8,128)(2,1)}, bf16[128,1024]{1,0:T(8,128)(2,1)S(1)}, u32[]{:S(2)}, u32[]{:S(2)}) collective-permute-start(bf16[128,1024]{1,0:T(8,128)(2,1)} %get-tuple-element.57), channel_id=1, source_target_pairs={{0,1},{1,0},{2,3},{3,2},{4,5},{5,4},{6,7},{7,6},{8,9},{9,8},{10,11... | collective-permute-start | bytes 786440 | tf_op jit(solution)/shard_map/ppermute | solution.py:213
  66.1 32.3 %all-to-all-start = ((bf16[8,96,640]{2,1,0:T(8,128)(2,1)}), bf16[8,96,640]{2,1,0:T(8,128)(2,1)S(1)}, u32[]{:S(2)}, u32[]{:S(2)}) async-start(bf16[8,96,640]{2,1,0:T(8,128)(2,1)} %back.1), calls=%async_computation | async-start | bytes 1966080 | tf_op jit(solution)/shard_map/all_to_all | solution.py:317
  69.8 27.6 %copy-start.8 = (bf16[128,1024]{1,0:T(8,128)(2,1)S(1)}, bf16[128,1024]{1,0:T(8,128)(2,1)}, u32[]{:S(2)}) copy-start(bf16[128,1024]{1,0:T(8,128)(2,1)} %copy-done.7) | copy-start | bytes 786436
  70.9 15.7 %collective-permute-start.14 = (bf16[256,512]{1,0:T(8,128)(2,1)S(1)}, bf16[256,512]{1,0:T(8,128)(2,1)S(1)}, u32[]{:S(2)}, u32[]{:S(2)}) collective-permute-start(bf16[256,512]{1,0:T(8,128)(2,1)S(1)} %fusion.4), channel_id=1, source_target_pairs={{0,1},{3,2},{1,3},{2,0},{4,5},{7,6},{5,7},{6,4},{8,9},{11,10},{9,1... | collective-permute-start | bytes 786440 | tf_op jit(solution)/shard_map/ppermute | solution.py:217
  71.1 17.7 %collective-permute-start.10 = (bf16[128,1024]{1,0:T(8,128)(2,1)S(1)}, bf16[128,1024]{1,0:T(8,128)(2,1)S(1)}, u32[]{:S(2)}, u32[]{:S(2)}) collective-permute-start(bf16[128,1024]{1,0:T(8,128)(2,1)S(1)} %copy-done.19), channel_id=1, source_target_pairs={{0,2},{3,1},{4,6},{7,5},{8,10},{11,9},{12,14},{15,13},{16,18},{19,... | collective-permute-start | bytes 786440 | tf_op jit(solution)/shard_map/ppermute | solution.py:215
  75.8 13.0 %collective-permute-start.9 = (bf16[128,1024]{1,0:T(8,128)(2,1)S(1)}, bf16[128,1024]{1,0:T(8,128)(2,1)S(1)}, u32[]{:S(2)}, u32[]{:S(2)}) collective-permute-start(bf16[128,1024]{1,0:T(8,128)(2,1)S(1)} %copy-done.19), channel_id=1, source_target_pairs={{1,2},{2,1},{5,6},{6,5},{9,10},{10,9},{13,14},{14,13},{17,18},{18,... | collective-permute-start | bytes 786440 | tf_op jit(solution)/shard_map/ppermute | solution.py:214
  76.6 20.8 %collective-permute-start.13 = (bf16[128,1024]{1,0:T(8,128)(2,1)S(1)}, bf16[128,1024]{1,0:T(8,128)(2,1)S(1)}, u32[]{:S(2)}, u32[]{:S(2)}) collective-permute-start(bf16[128,1024]{1,0:T(8,128)(2,1)S(1)} %fusion.3), channel_id=1, source_target_pairs={{0,1},{3,2},{1,3},{2,0},{4,5},{7,6},{5,7},{6,4},{8,9},{11,10},{9,1... | collective-permute-start | bytes 786440 | tf_op jit(solution)/shard_map/ppermute | solution.py:217
  86.6 11.9 %copy-start.3 = (bf16[576,512]{1,0:T(8,128)(2,1)S(1)}, bf16[576,512]{1,0:T(8,128)(2,1)}, u32[]{:S(2)}) copy-start(bf16[576,512]{1,0:T(8,128)(2,1)} %tok_ref.1) | copy-start | bytes 1769476
  86.6 11.9 %copy-start.4 = (bf16[576,512]{1,0:T(8,128)(2,1)S(1)}, bf16[576,512]{1,0:T(8,128)(2,1)}, u32[]{:S(2)}) copy-start(bf16[576,512]{1,0:T(8,128)(2,1)} %go_ref.1) | copy-start | bytes 1769476
  86.6 11.9 %copy-start.15 = (s32[1,576]{1,0:T(1,128)S(1)}, s32[1,576]{1,0:T(1,128)}, u32[]{:S(2)}) copy-start(s32[1,576]{1,0:T(1,128)} %get-tuple-element.34.target_ref) | copy-start | bytes 6916
  86.6 11.9 %copy-start.16 = (bf16[576]{0:T(1024)(128)(2,1)S(1)}, bf16[576]{0:T(1024)(128)(2,1)}, u32[]{:S(2)}) copy-start(bf16[576]{0:T(1024)(128)(2,1)} %gate_ref.1) | copy-start | bytes 3460
  86.6 11.9 %copy-start.17 = (f32[512]{0:T(512)S(1)}, f32[512]{0:T(512)}, u32[]{:S(2)}) copy-start(f32[512]{0:T(512)} %param.8) | copy-start | bytes 6148
  (19 other events, 16.4 us)

commit v4 on v3

v4 whole, which is shorter than its diff:
```python
import functools

import jax
import jax.numpy as jnp
from jax import lax
from jax.experimental import pallas as pl
from jax.experimental.pallas import tpu as pltpu
from jax.sharding import PartitionSpec as P

epsilon = 1e-05
F32 = jnp.float32
BF16 = jnp.bfloat16
LANES = 128
LINE = 4
MIB = 1024 * 1024

vmem = pl.BlockSpec(memory_space=pltpu.VMEM)
smem = pl.BlockSpec(memory_space=pltpu.SMEM)
hbm = pl.BlockSpec(memory_space=pltpu.HBM)
anywhere = pl.BlockSpec(memory_space=pl.ANY)


def dot(left, right, contract=((1,), (0,))):
    return lax.dot_general(left, right, (contract, ((), ())), preferred_element_type=F32)


def normalize(tokens):
    values = tokens.astype(F32)
    center = values - jnp.mean(values, axis=-1, keepdims=True)
    spread = lax.rsqrt(jnp.mean(center * center, axis=-1, keepdims=True) + epsilon)
    return center * spread, spread


def kernel_call(kernel, name, flops, nbytes, outs, ins, scratch=(), places=None, vmem_mib=24):
    return pl.pallas_call(
        kernel,
        name=name,
        out_shape=outs,
        in_specs=ins,
        out_specs=places or [vmem] * len(outs),
        scratch_shapes=list(scratch),
        compiler_params=pltpu.CompilerParams(vmem_limit_bytes=vmem_mib * MIB),
        cost_estimate=pl.CostEstimate(flops=flops, bytes_accessed=nbytes, transcendentals=0),
    )


def start_copies(pairs, sems):
    copies = [pltpu.make_async_copy(src, dst, sems.at[i]) for i, (src, dst) in enumerate(pairs)]
    for copy in copies:
        copy.start()
    return copies


def block_base(me, sources):
    return jnp.bitwise_xor(me[0], sources - 2)


def place_kernel(
    sources, capacity, me, place, ids_hbm, gate_hbm, tok_hbm, gain_hbm, go_hbm, target_ref, *refs
):
    outs = refs[:sources]
    ids_ref, gate_ref, tok_ref, gain_ref, go_ref, sent_ref, in_sems, out_sems = refs[sources:]
    rows = sources * capacity
    tok_rows, width = tok_ref.shape
    loads = start_copies(
        [(ids_hbm, ids_ref), (tok_hbm, tok_ref), (gain_hbm, gain_ref), (gate_hbm, gate_ref), (go_hbm, go_ref)],
        in_sems,
    )
    mine = block_base(me, sources)
    earlier = lax.broadcasted_iota(jnp.int32, (tok_rows, tok_rows), 0) < lax.broadcasted_iota(
        jnp.int32, (tok_rows, tok_rows), 1
    )
    earlier = jnp.where(earlier, 1.0, 0.0).astype(BF16)
    for copy in loads:
        copy.wait()
    ids = ids_ref[...]
    onehot = (lax.broadcasted_iota(jnp.int32, (sources, tok_rows), 0) == ids).astype(F32)
    before = dot(onehot.astype(BF16), earlier)
    rank = jnp.sum(before * onehot, axis=0, keepdims=True).astype(jnp.int32)
    kept = rank < capacity
    target_ref[...] = jnp.where(kept, ids * capacity + rank, -1)
    target = jnp.where(kept, jnp.bitwise_xor(ids, mine) * capacity + rank, -1)
    hit = lax.broadcasted_iota(jnp.int32, (rows, tok_rows), 0) == target
    gate = gate_ref[...].astype(F32).reshape(1, tok_rows)
    scaled, _ = normalize(tok_ref[...])
    normed = (scaled * gain_ref[...]).astype(BF16)
    stores = []
    for part, (weight, values) in enumerate(((gate, go_ref[...]), (1.0, normed))):
        columns = pl.ds((1 - part) * width, width)
        sent_ref[:, columns] = dot(jnp.where(hit, weight, 0.0).astype(BF16), values).astype(BF16)
        spans = [pl.ds(j * capacity, capacity) for j in range(sources)]
        if capacity % 16:
            for j in range(sources):
                outs[j][:, columns] = sent_ref[spans[j], columns]
        else:
            stores += start_copies(
                [(sent_ref.at[spans[j], columns], outs[j].at[:, columns]) for j in range(sources)],
                out_sems.at[part],
            )
    for copy in stores:
        copy.wait()


def keep_kernel(block_ref, out_ref):
    out_ref[...] = block_ref[...]


def gelu_parts(value):
    root = 0.7978845608028654
    square = value * value
    tan = jnp.tanh(root * (value + 0.044715 * value * square))
    half = 0.5 * (1.0 + tan)
    slope = half + 0.5 * value * (1.0 - tan * tan) * (root * (1.0 + 3.0 * 0.044715 * square))
    return value * half, slope


def expert_chunk(rows_ref, w_in_ref, w_out_ref, part):
    width = w_in_ref.shape[0]
    delta = rows_ref[:, width:]
    preact = dot(rows_ref[:, :width], w_in_ref[:, part])
    act_float, slope = gelu_parts(preact)
    act = act_float.astype(BF16)
    grad_act = dot(delta, w_out_ref[part, :], ((1,), (1,)))
    weight = dot(act.T, delta).astype(BF16)
    total = jnp.sum(act.astype(F32) * grad_act, axis=1, keepdims=True)
    return weight, (grad_act * slope).astype(BF16), total


def shard_order(place):
    first = jnp.where(lax.rem(place, 2) == 0, 3, 0)
    second = jnp.where(place < 2, 2, 1)
    return [first, second, 6 - first - second - place, place]


def grads_kernel(sources, capacity, groups, place, w_in_ref, w_out_ref, *refs):
    blocks = refs[:sources]
    outs = refs[sources : sources + LINE]
    gpre_ref, extra_ref, rows_ref, turned_ref, sems = refs[sources + LINE :]
    width, hidden = w_in_ref.shape
    piece_d, piece_f = width // LINE, hidden // LINE
    order = shard_order(place[0]) if groups == LINE else list(range(LINE))
    spans = [pl.ds(j * capacity, capacity) for j in range(sources)]
    if capacity % 16:
        for j in range(sources):
            rows_ref[spans[j], :] = blocks[j][...]
    else:
        for copy in start_copies([(blocks[j], rows_ref.at[spans[j]]) for j in range(sources)], sems):
            copy.wait()
    for j in range(LINE):
        start = pl.multiple_of(order[j] * piece_d, piece_d)
        turned_ref[j * piece_d : (j + 1) * piece_d, :] = rows_ref[:, pl.ds(start, piece_d)].T
    total = jnp.zeros((sources * capacity, 1), F32)
    for j in range(LINE):
        part = pl.ds(pl.multiple_of(order[j] * piece_f, piece_f), piece_f)
        weight, grad_pre, more = expert_chunk(rows_ref, w_in_ref, w_out_ref, part)
        total += more
        gpre_ref[:, part] = grad_pre
        outs[j][piece_d:, :width] = weight[: piece_f // 2]
        outs[j][piece_d:, width:] = weight[piece_f // 2 :]
        weight = dot(turned_ref[...], grad_pre).astype(BF16)
        for i in range(LINE):
            outs[i][:piece_d, part] = weight[i * piece_d : (i + 1) * piece_d]
    high = total.astype(BF16).astype(F32)
    lane = lax.broadcasted_iota(jnp.int32, extra_ref.shape, 1)
    extra_ref[...] = jnp.where(lane == 0, high, jnp.where(lane == 1, total - high, 0.0)).astype(BF16)


def back_kernel(sources, capacity, me, gpre_ref, w_in_ref, extra_ref, out_ref):
    width = w_in_ref.shape[0]
    grad = dot(gpre_ref[...], w_in_ref[...], ((1,), (1,))).astype(BF16)
    for j in range(sources):
        block = slice(j * capacity, (j + 1) * capacity)
        source = jnp.bitwise_xor(block_base(me, sources), j)
        out_ref[source, :, :width] = grad[block]
        out_ref[source, :, width:] = extra_ref[block, :]


def finish_kernel(target_ref, gate_ref, tok_ref, gain_ref, go_ref, back_ref, tokens_out, gate_out):
    rows = back_ref.shape[0]
    tok_rows, width = tok_ref.shape
    spots = jnp.broadcast_to(target_ref[...].astype(F32), (8, tok_rows)).T[:, :1].astype(jnp.int32)
    hit = lax.broadcasted_iota(jnp.int32, (tok_rows, rows), 1) == spots
    got = dot(jnp.where(hit, 1.0, 0.0).astype(BF16), back_ref[...])
    sums = got[:, width:].T
    gate_row = gate_ref[...].astype(F32).reshape(1, tok_rows)
    gate_out[...] = ((sums[0:1] + sums[1:2]) / gate_row).astype(BF16).reshape(tok_rows)
    scaled, spread = normalize(tok_ref[...])
    grad = got[:, :width] * gain_ref[...]
    mean = jnp.mean(grad, axis=-1, keepdims=True)
    cross = jnp.mean(grad * scaled, axis=-1, keepdims=True)
    branch = spread * (grad - mean - scaled * cross)
    tokens_out[...] = (go_ref[...].astype(F32) + branch).astype(BF16)


def swap_blocks(blocks):
    count = len(blocks)
    return [
        blocks[j]
        if j == count - 2
        else lax.ppermute(blocks[j], "space", [(i, i ^ j ^ (count - 2)) for i in range(count)])
        for j in range(count)
    ]


def is_inner(place):
    return (place[0] == 1) | (place[0] == 2)


def pass_kernel(place, third_ref, swapped_ref, out_ref):
    swapped = jnp.where(is_inner(place), swapped_ref[...].astype(F32), 0.0)
    out_ref[...] = (third_ref[...].astype(F32) + swapped).astype(BF16)


def total_kernel(place, own_ref, middle_ref, across_ref, outer_ref, swapped_ref, last_ref, in_ref, out_ref):
    piece_d, half = in_ref.shape[0], out_ref.shape[0] // 2
    width = out_ref.shape[1]
    swapped = jnp.where(is_inner(place), 0.0, swapped_ref[...].astype(F32))
    total = own_ref[...].astype(F32) + swapped
    for ref in (middle_ref, across_ref, outer_ref, last_ref):
        total += ref[...].astype(F32)
    in_ref[...] = total[:piece_d]
    out_ref[:half, :] = total[piece_d:, :width]
    out_ref[half:, :] = total[piece_d:, width:]


def line_sums(place, first, second, third, own, width):
    swapped = lax.ppermute(first, "dp", [(0, 1), (1, 0), (2, 3), (3, 2)])
    middle = lax.ppermute(second, "dp", [(1, 2), (2, 1)])
    across = lax.ppermute(second, "dp", [(0, 2), (3, 1)])
    outer = lax.ppermute(third, "dp", [(0, 1), (3, 2)])
    (passed,) = kernel_call(
        pass_kernel,
        "pass",
        1,
        1,
        [jax.ShapeDtypeStruct(third.shape, BF16)],
        [smem] + [vmem] * 2,
        vmem_mib=56,
    )(place, third, swapped)
    last = lax.ppermute(passed, "dp", [(1, 3), (2, 0)])
    rows, hidden = own.shape
    piece_d = width // LINE
    return kernel_call(
        total_kernel,
        "total",
        1,
        1,
        [
            jax.ShapeDtypeStruct((piece_d, hidden), F32),
            jax.ShapeDtypeStruct((2 * (rows - piece_d), width), F32),
        ],
        [smem] + [vmem] * 6,
        vmem_mib=56,
    )(place, own, middle, across, outer, swapped, last)


def body(tokens, gain, w_in, w_out, expert_ids, gate, grad_out):
    sources = lax.axis_size("space")
    groups = lax.axis_size("dp")
    tok_rows, width = tokens.shape
    hidden = w_in.shape[2]
    capacity = ((tok_rows * 5 // 4 + sources - 1) // sources + 7) // 8 * 8
    rows = sources * capacity
    me = lax.axis_index("space").astype(jnp.int32).reshape(1)
    place = lax.axis_index("dp").astype(jnp.int32).reshape(1)
    ids_row = expert_ids.reshape(1, tok_rows)
    gain_row = gain.reshape(1, width)
    weight_in, weight_out = w_in[0], w_out[0]
    shape = jax.ShapeDtypeStruct
    sems = pltpu.SemaphoreType.DMA
    block_place = vmem if capacity % 16 else anywhere
    io_bytes = 2 * (2 * tok_rows * width + 2 * rows * width)

    target, *sent = kernel_call(
        functools.partial(place_kernel, sources, capacity),
        "place",
        4 * rows * tok_rows * width,
        io_bytes,
        [shape((1, tok_rows), jnp.int32)]
        + [shape((capacity, 2 * width), BF16)] * sources,
        [smem] * 2 + [hbm] * 5,
        [
            pltpu.VMEM((1, tok_rows), jnp.int32),
            pltpu.VMEM((tok_rows,), BF16),
            pltpu.VMEM((tok_rows, width), BF16),
            pltpu.VMEM((1, width), F32),
            pltpu.VMEM((tok_rows, width), BF16),
            pltpu.VMEM((rows, 2 * width), BF16),
            sems((5,)),
            sems((2, sources)),
        ],
        places=[vmem] + [block_place] * sources,
        vmem_mib=56,
    )(me, place, ids_row, gate, tokens, gain_row, grad_out)
    (kept,) = kernel_call(
        keep_kernel,
        "keep",
        1,
        1,
        [shape((capacity, 2 * width), BF16)],
        [vmem],
        vmem_mib=2,
    )(sent[sources - 2])
    arrived = swap_blocks(sent)
    arrived[sources - 2] = kept

    *parts, gpre, extra = kernel_call(
        functools.partial(grads_kernel, sources, capacity, groups),
        "grads",
        8 * rows * width * hidden,
        2 * (2 * rows * width + 4 * width * hidden + rows * hidden),
        [shape((width // LINE + hidden // LINE // 2, hidden), BF16)] * LINE
        + [shape((rows, hidden), BF16), shape((rows, LANES), BF16)],
        [smem] + [vmem] * 2 + [block_place] * sources,
        [
            pltpu.VMEM((rows, 2 * width), BF16),
            pltpu.VMEM((width, rows), BF16),
            sems((sources,)),
        ],
    )(place, weight_in, weight_out, *arrived)
    (returned,) = kernel_call(
        functools.partial(back_kernel, sources, capacity),
        "back",
        1,
        1,
        [shape((sources, capacity, width + LANES), BF16)],
        [smem] + [vmem] * 3,
    )(me, gpre, weight_in, extra)

    if groups == LINE:
        grad_w_in, grad_w_out = line_sums(place, *parts, width)
    else:
        parts_in, parts_out = zip(*[split_piece(part, width, LINE) for part in parts])
        grad_w_in, grad_w_out = (
            lax.psum_scatter(
                jnp.concatenate(part), "dp", scatter_dimension=0, tiled=True
            ).astype(F32)
            for part in (parts_in, parts_out)
        )
    back = lax.all_to_all(returned, "space", split_axis=0, concat_axis=0, tiled=True)
    grad_tokens, grad_gate = kernel_call(
        finish_kernel,
        "finish",
        1,
        1,
        [shape((tok_rows, width), BF16), shape((tok_rows,), BF16)],
        [vmem] * 6,
    )(target, gate, tokens, gain_row, grad_out, back.reshape(rows, width + LANES))
    return (grad_tokens, grad_gate, grad_w_in[None], grad_w_out[None])


def split_piece(piece, width, pieces):
    piece_d = width // pieces
    lower = piece[piece_d:]
    return piece[:piece_d], jnp.concatenate([lower[:, :width], lower[:, width:]])


def solution(mesh):
    placed = (
        P(("space", "dp"), None),
        P(),
        P("space", None, None),
        P("space", None, None),
        P(("space", "dp"), None),
        P(("space", "dp")),
        P(("space", "dp"), None),
    )
    return jax.shard_map(
        body,
        mesh=mesh,
        in_specs=placed,
        out_specs=(
            P(("space", "dp"), None),
            P(("space", "dp")),
            P("space", "dp", None),
            P("space", "dp", None),
        ),
        check_vma=False,
    )
```

time: 102 us -> 87.4 us (0.86)
  local copies, waits for them, and re-layouts: 16.4 us -> 1.75 us
  waiting for transfers between devices: 31.3 us -> 39.1 us
  starting transfers between devices: 28.3 us -> 23.5 us
  other arithmetic: 4.42 us -> 0 us
  Pallas kernels: 19.7 us -> 22 us
    unnamed x70 -> x20, local copies, waits for them, and re-layouts: 16.4 us -> 1.75 us
    ppermute x2, waiting for transfers between devices: 17.4 us -> 23.3 us  [the longest x1 12.7 us: line_sums(): last = lax.ppermute(passed, 'dp', [(1, 3), (2, 0)])]
    ppermute x2 -> x1, starting transfers between devices: 11.1 us -> 5.24 us  [line_sums(): across = lax.ppermute(second, 'dp', [(0, 2), (3, 1)])]
    broadcast_in_dim x2 -> x0, other arithmetic: 3.18 us -> none  [body(): return (grad_tokens, grad_gate, grad_w_in[None], grad_w_out[None])]
    pallas_call x2 -> x4, Pallas kernels: 10.2 us -> 12.6 us  [the longest x1 7.43 us: body(): kernel_call(functools.partial(grads_kernel, sources, capacity, groups), '...]
    all_to_all x1, waiting for transfers between devices: 0.01 us -> 2.24 us  [body(): lax.all_to_all(returned, 'space', split_axis=0, concat_axis=0, tiled=True)]
    ppermute x2, starting transfers between devices: 1.41 us -> 3.62 us  [the longest x1 2.34 us: line_sums(): outer = lax.ppermute(third, 'dp', [(0, 1), (3, 2)])]
    ppermute x2 -> x1, waiting for transfers between devices: 1.95 us -> 0.01 us  [line_sums(): swapped = lax.ppermute(first, 'dp', [(0, 1), (1, 0), (2, 3), (3, 2)])]
  transfers between devices with their start and end apart: 16 -> 13, of which waited for: 7 -> 8; matrix products, arithmetic and copies ran while one was open for 4% -> 0% of each run, Pallas kernels for 6% -> 8%
where the time goes in v4:
time: 87.4 us; the launch traced here: 87.1 us
  waiting for transfers between devices  39.1 us (45%)
  starting transfers between devices  23.5 us (27%)
  Pallas kernels  22 us (25%)
  local copies, waits for them, and re-layouts  1.75 us (2%)
    ppermute x7, waiting for transfers between devices, swap_blocks(): lax.ppermute(blocks[j], 'space', [(i, i ^ j ^ count - 2) for i in range(c...  13.2 us
    ppermute x1, waiting for transfers between devices, line_sums(): last = lax.ppermute(passed, 'dp', [(1, 3), (2, 0)])  12.7 us
    ppermute x1, waiting for transfers between devices, line_sums(): outer = lax.ppermute(third, 'dp', [(0, 1), (3, 2)])  10.6 us
    ppermute x7, starting transfers between devices, swap_blocks(): lax.ppermute(blocks[j], 'space', [(i, i ^ j ^ count - 2) for i in range(c...  7.51 us
    pallas_call x1, Pallas kernels, body(): kernel_call(functools.partial(grads_kernel, sources, capacity, groups), '...  7.43 us
    ppermute x1, starting transfers between devices, line_sums(): across = lax.ppermute(second, 'dp', [(0, 2), (3, 1)])  5.24 us
    pallas_call x1, Pallas kernels, body(): kernel_call(functools.partial(place_kernel, sources, capacity), 'place',...  4.8 us
    all_to_all x1, starting transfers between devices, body(): lax.all_to_all(returned, 'space', split_axis=0, concat_axis=0, tiled=True)  3.93 us
  transfers between devices with their start and end apart: 13, of which 8 were waited for; matrix products, arithmetic and copies ran while one was open for 0% of the time, Pallas kernels for 8%

profile of v4, /device:TPU:0, one launch (start us, length us, event | category | flops | bytes accessed | tf_op | source)
XLA Modules:
  0.0 87.1 jit_solution(4612759747499212580)
XLA Ops:
  0.7 4.8 %place.1 = (s32[1,576]{1,0:T(1,128)}, bf16[96,1024]{1,0:T(8,128)(2,1)}, bf16[96,1024]{1,0:T(8,128)(2,1)}, bf16[96,1024]{1,0:T(8,128)(2,1)}, bf16[96,1024]{1,0:T(...) custom-call(s32[1]{0:T(128)} %bitcast.me, ...), custom_call_target="tpu_custom_call" | custom-call | flops 905969664 | bytes 2752512 | tf_op jit(solution)/shard_map/place/pallas_call | solution.py:274
  5.5 3.9 %collective-permute-start = (bf16[96,1024]{1,0:T(8,128)(2,1)}, bf16[96,1024]{1,0:T(8,128)(2,1)S(1)}, u32[]{:S(2)}, u32[]{:S(2)}) collective-permute-start(bf16[96,1024]{1,0:T(8,128)(2,1)} %get-tuple-element.24), channel_id=1, source_target_pairs={{0,24},{4,28},{8,16},{12,20},{16,8},{20,12},{24,0},{28,4},{1,25},{... | collective-permute-start | bytes 589832 | tf_op jit(solution)/shard_map/ppermute | solution.py:200
  9.4 0.0 collective-permute-start.1
  9.4 1.2 %collective-permute-start.2 = (bf16[96,1024]{1,0:T(8,128)(2,1)}, bf16[96,1024]{1,0:T(8,128)(2,1)S(1)}, u32[]{:S(2)}, u32[]{:S(2)}) collective-permute-start(bf16[96,1024]{1,0:T(8,128)(2,1)} %get-tuple-element.26), channel_id=1, source_target_pairs={{0,16},{4,20},{8,24},{12,28},{16,0},{20,4},{24,8},{28,12},{1,17},{... | collective-permute-start | bytes 589832 | tf_op jit(solution)/shard_map/ppermute | solution.py:200
  10.6 0.6 collective-permute-start.3
  11.2 1.7 %collective-permute-start.4 = (bf16[96,1024]{1,0:T(8,128)(2,1)}, bf16[96,1024]{1,0:T(8,128)(2,1)S(1)}, u32[]{:S(2)}, u32[]{:S(2)}) collective-permute-start(bf16[96,1024]{1,0:T(8,128)(2,1)} %get-tuple-element.28), channel_id=1, source_target_pairs={{0,8},{4,12},{8,0},{12,4},{16,24},{20,28},{24,16},{28,20},{1,9},{5... | collective-permute-start | bytes 589832 | tf_op jit(solution)/shard_map/ppermute | solution.py:200
  12.8 2.6 %collective-permute-done.refs_0_ = bf16[96,1024]{1,0:T(8,128)(2,1)S(1)} collective-permute-done((bf16[96,1024]{1,0:T(8,128)(2,1)}, bf16[96,1024]{1,0:T(8,128)(2,1)S(1)}, u32[]{:S(2)}, u32[]{:S(2)}) %collective-permute-start) | collective-permute-done | bytes 196640 | tf_op jit(solution)/shard_map/ppermute | solution.py:200
  15.4 3.8 %collective-permute-done.1.refs_1_ = bf16[96,1024]{1,0:T(8,128)(2,1)S(1)} collective-permute-done((bf16[96,1024]{1,0:T(8,128)(2,1)}, bf16[96,1024]{1,0:T(8,128)(2,1)S(1)}, u32[]{:S(2)}, u32[]{:S(2)}) %collective-permute-start.1) | collective-permute-done | bytes 196640 | tf_op jit(solution)/shard_map/ppermute | solution.py:200
  19.3 0.1 collective-permute-start.6
  19.4 0.9 %copy-done.5 = bf16[96,1024]{1,0:T(8,128)(2,1)S(1)} copy-done((bf16[96,1024]{1,0:T(8,128)(2,1)S(1)}, bf16[96,1024]{1,0:T(8,128)(2,1)}, u32[]{:S(2)}) %copy-start.5) | copy-done | bytes 196632
  20.4 2.6 %collective-permute-done.2.refs_2_ = bf16[96,1024]{1,0:T(8,128)(2,1)S(1)} collective-permute-done((bf16[96,1024]{1,0:T(8,128)(2,1)}, bf16[96,1024]{1,0:T(8,128)(2,1)S(1)}, u32[]{:S(2)}, u32[]{:S(2)}) %collective-permute-start.2) | collective-permute-done | bytes 196640 | tf_op jit(solution)/shard_map/ppermute | solution.py:200
  23.0 4.1 %collective-permute-done.3.refs_3_ = bf16[96,1024]{1,0:T(8,128)(2,1)S(1)} collective-permute-done((bf16[96,1024]{1,0:T(8,128)(2,1)}, bf16[96,1024]{1,0:T(8,128)(2,1)S(1)}, u32[]{:S(2)}, u32[]{:S(2)}) %collective-permute-start.3) | collective-permute-done | bytes 196640 | tf_op jit(solution)/shard_map/ppermute | solution.py:200
  27.1 0.0 collective-permute-done.4.refs_4_
  27.1 0.0 collective-permute-done.5.refs_5_
  27.1 0.0 collective-permute-done.6.refs_7_
  27.2 7.4 %grads.1 = (bf16[256,1024]{1,0:T(8,128)(2,1)}, bf16[256,1024]{1,0:T(8,128)(2,1)S(1)}, bf16[256,1024]{1,0:T(8,128)(2,1)S(1)}, bf16[256,1024]{1,0:T(8,128)(2,1)S(1...) custom-call(s32[1]{0:T(128)} %bitcast.1.place, bf16[512,1024]{1,0:T(8,128)(2,1)S(1)} %bitcast.10, ...), custom_call_target="tpu_custom_call" | custom-call | flops 3221225472 | bytes 7340032 | tf_op jit(solution)/shard_map/grads/pallas_call | solution.py:307
  34.6 0.8 copy-done.4
  35.4 1.8 %collective-permute-start.10 = (bf16[256,1024]{1,0:T(8,128)(2,1)}, bf16[256,1024]{1,0:T(8,128)(2,1)}, u32[]{:S(2)}, u32[]{:S(2)}) collective-permute-start(bf16[256,1024]{1,0:T(8,128)(2,1)} %get-tuple-element.39), channel_id=1, source_target_pairs={{0,1},{1,0},{2,3},{3,2},{4,5},{5,4},{6,7},{7,6},{8,9},{9,8},{10,11... | collective-permute-start | bytes 1572872 | tf_op jit(solution)/shard_map/ppermute | solution.py:227
  37.2 2.0 %back.1 = bf16[8,96,640]{2,1,0:T(8,128)(2,1)} custom-call(s32[1]{0:T(128)} %bitcast.me, bf16[768,1024]{1,0:T(8,128)(2,1)S(1)} %get-tuple-element.32.gpre_ref, bf16[512,1024]{1,0:T(8,128)(2,1)S(1)} %bitcast.11, bf16[768,128]{1,0:T(8,128)(2,1)S(1)} %get-tuple-element.33.extra_ref), custom_call_target="tpu_custom_call" | custom-call | flops 1 | bytes 1 | tf_op jit(solution)/shard_map/back/pallas_call | solution.py:321
  39.2 0.0 copy-start.8
  39.2 3.9 %all-to-all-start = ((bf16[8,96,640]{2,1,0:T(8,128)(2,1)}), bf16[8,96,640]{2,1,0:T(8,128)(2,1)S(1)}, u32[]{:S(2)}, u32[]{:S(2)}) async-start(bf16[8,96,640]{2,1,0:T(8,128)(2,1)} %back.1), calls=%async_computation | async-start | bytes 1966080 | tf_op jit(solution)/shard_map/all_to_all | solution.py:340
  43.1 5.2 %collective-permute-start.8 = (bf16[256,1024]{1,0:T(8,128)(2,1)S(1)}, bf16[256,1024]{1,0:T(8,128)(2,1)}, u32[]{:S(2)}, u32[]{:S(2)}) collective-permute-start(bf16[256,1024]{1,0:T(8,128)(2,1)S(1)} %get-tuple-element.37), channel_id=1, source_target_pairs={{0,2},{3,1},{4,6},{7,5},{8,10},{11,9},{12,14},{15,13},{16,18},{19,... | collective-permute-start | bytes 1572872 | tf_op jit(solution)/shard_map/ppermute | solution.py:229
  48.4 1.4 %collective-permute-start.7 = (bf16[256,1024]{1,0:T(8,128)(2,1)S(1)}, bf16[256,1024]{1,0:T(8,128)(2,1)}, u32[]{:S(2)}, u32[]{:S(2)}) collective-permute-start(bf16[256,1024]{1,0:T(8,128)(2,1)S(1)} %get-tuple-element.37), channel_id=1, source_target_pairs={{1,2},{2,1},{5,6},{6,5},{9,10},{10,9},{13,14},{14,13},{17,18},{18,... | collective-permute-start | bytes 1572872 | tf_op jit(solution)/shard_map/ppermute | solution.py:228
  49.8 2.3 %collective-permute-start.9 = (bf16[256,1024]{1,0:T(8,128)(2,1)S(1)}, bf16[256,1024]{1,0:T(8,128)(2,1)}, u32[]{:S(2)}, u32[]{:S(2)}) collective-permute-start(bf16[256,1024]{1,0:T(8,128)(2,1)S(1)} %get-tuple-element.38.third_ref), channel_id=1, source_target_pairs={{0,1},{3,2},{4,5},{7,6},{8,9},{11,10},{12,13},{15,14},{16,17},{19,... | collective-permute-start | bytes 1572872 | tf_op jit(solution)/shard_map/ppermute | solution.py:230
  52.1 2.1 %pass.1 = bf16[256,1024]{1,0:T(8,128)(2,1)} custom-call(s32[1]{0:T(128)} %bitcast.1.place, bf16[256,1024]{1,0:T(8,128)(2,1)} %copy-done.3, bf16[256,1024]{1,0:T(8,128)(2,1)} %collective-permute-done.10.swapped_ref), custom_call_target="tpu_custom_call" | custom-call | flops 1 | bytes 1 | tf_op jit(solution)/shard_map/pass/pallas_call | solution.py:231
  54.3 1.3 %collective-permute-start.11 = (bf16[256,1024]{1,0:T(8,128)(2,1)}, bf16[256,1024]{1,0:T(8,128)(2,1)}, u32[]{:S(2)}, u32[]{:S(2)}) collective-permute-start(bf16[256,1024]{1,0:T(8,128)(2,1)} %pass.1), channel_id=1, source_target_pairs={{1,3},{2,0},{5,7},{6,4},{9,11},{10,8},{13,15},{14,12},{17,19},{18,... | collective-permute-start | bytes 1572872 | tf_op jit(solution)/shard_map/ppermute | solution.py:240
  55.6 2.2 %all-to-all-done = bf16[8,96,640]{2,1,0:T(8,128)(2,1)S(1)} async-done(((bf16[8,96,640]{2,1,0:T(8,128)(2,1)}), bf16[8,96,640]{2,1,0:T(8,128)(2,1)S(1)}, u32[]{:S(2)}, u32[]{:S(2)}) %all-to-all-start) | async-done | bytes 983072 | tf_op jit(solution)/shard_map/all_to_all | solution.py:340
  57.8 2.6 %finish.1 = (bf16[576,512]{1,0:T(8,128)(2,1)}, bf16[576]{0:T(1024)(128)(2,1)}) custom-call(s32[1,576]{1,0:T(1,128)S(1)} %copy-done.6, bf16[576]{0:T(1024)(128)(2,1)S(1)} %copy-done.7, bf16[576,512]{1,0:T(8,128)(2,1)S(1)} %copy-done.1, f32[1,512]{1,0:T(1,128)S(1)} %bitcast.13, bf16[576,512]{1,0:T(8,128)(2,1)S(1)} %copy-done.2, bf16[768,640]{1,0:T(8,128)(2,1)S(1)} %bitcast.9), custom_call_target="tpu_custom_call" | custom-call | flops 1 | bytes 1 | tf_op jit(solution)/shard_map/finish/pallas_call | solution.py:341
  60.4 0.3 collective-permute-done.8.across_ref
  60.7 10.6 %collective-permute-done.9.outer_ref = bf16[256,1024]{1,0:T(8,128)(2,1)} collective-permute-done((bf16[256,1024]{1,0:T(8,128)(2,1)S(1)}, bf16[256,1024]{1,0:T(8,128)(2,1)}, u32[]{:S(2)}, u32[]{:S(2)}) %collective-permute-start.9) | collective-permute-done | bytes 524320 | tf_op jit(solution)/shard_map/ppermute | solution.py:230
  71.3 12.7 %collective-permute-done.11.last_ref = bf16[256,1024]{1,0:T(8,128)(2,1)} collective-permute-done((bf16[256,1024]{1,0:T(8,128)(2,1)}, bf16[256,1024]{1,0:T(8,128)(2,1)}, u32[]{:S(2)}, u32[]{:S(2)}) %collective-permute-start.11) | collective-permute-done | bytes 524320 | tf_op jit(solution)/shard_map/ppermute | solution.py:240
  84.0 3.0 %total.1 = (f32[128,1024]{1,0:T(8,128)}, f32[256,512]{1,0:T(8,128)}) custom-call(s32[1]{0:T(128)} %bitcast.1.place, bf16[256,1024]{1,0:T(8,128)(2,1)} %copy-done.4, bf16[256,1024]{1,0:T(8,128)(2,1)} %collective-permute-done.7.middle_ref, bf16[256,1024]{1,0:T(8,128)(2,1)} %collective-permute-done.8.across_ref, ...), custom_call_target="tpu_custom_call" | custom-call | flops 1 | bytes 1 | tf_op jit(solution)/shard_map/total/pallas_call | solution.py:243
  (21 shorter events, 0.1 us)
Async XLA Ops:
  0.6 26.5 %copy-start = (bf16[1,512,1024]{2,1,0:T(8,128)(2,1)S(1)}, bf16[1,512,1024]{2,1,0:T(8,128)(2,1)}, u32[]{:S(2)}) copy-start(bf16[1,512,1024]{2,1,0:T(8,128)(2,1)} %param.9) | copy-start | bytes 3145732
  0.6 26.5 %copy-start.9 = (bf16[1,1024,512]{2,1,0:T(8,128)(2,1)S(1)}, bf16[1,1024,512]{2,1,0:T(8,128)(2,1)}, u32[]{:S(2)}) copy-start(bf16[1,1024,512]{2,1,0:T(8,128)(2,1)} %param.10) | copy-start | bytes 3145732
  5.5 10.0 %collective-permute-start = (bf16[96,1024]{1,0:T(8,128)(2,1)}, bf16[96,1024]{1,0:T(8,128)(2,1)S(1)}, u32[]{:S(2)}, u32[]{:S(2)}) collective-permute-start(bf16[96,1024]{1,0:T(8,128)(2,1)} %get-tuple-element.24), channel_id=1, source_target_pairs={{0,24},{4,28},{8,16},{12,20},{16,8},{20,12},{24,0},{28,4},{1,25},{... | collective-permute-start | bytes 589832 | tf_op jit(solution)/shard_map/ppermute | solution.py:200
  9.4 9.9 %collective-permute-start.1 = (bf16[96,1024]{1,0:T(8,128)(2,1)}, bf16[96,1024]{1,0:T(8,128)(2,1)S(1)}, u32[]{:S(2)}, u32[]{:S(2)}) collective-permute-start(bf16[96,1024]{1,0:T(8,128)(2,1)} %get-tuple-element.25), channel_id=1, source_target_pairs={{0,28},{4,24},{8,20},{12,16},{16,12},{20,8},{24,4},{28,0},{1,29},{... | collective-permute-start | bytes 589832 | tf_op jit(solution)/shard_map/ppermute | solution.py:200
  9.4 13.6 %collective-permute-start.2 = (bf16[96,1024]{1,0:T(8,128)(2,1)}, bf16[96,1024]{1,0:T(8,128)(2,1)S(1)}, u32[]{:S(2)}, u32[]{:S(2)}) collective-permute-start(bf16[96,1024]{1,0:T(8,128)(2,1)} %get-tuple-element.26), channel_id=1, source_target_pairs={{0,16},{4,20},{8,24},{12,28},{16,0},{20,4},{24,8},{28,12},{1,17},{... | collective-permute-start | bytes 589832 | tf_op jit(solution)/shard_map/ppermute | solution.py:200
  10.6 16.6 %collective-permute-start.3 = (bf16[96,1024]{1,0:T(8,128)(2,1)}, bf16[96,1024]{1,0:T(8,128)(2,1)S(1)}, u32[]{:S(2)}, u32[]{:S(2)}) collective-permute-start(bf16[96,1024]{1,0:T(8,128)(2,1)} %get-tuple-element.27), channel_id=1, source_target_pairs={{0,20},{4,16},{8,28},{12,24},{16,4},{20,0},{24,12},{28,8},{1,21},{... | collective-permute-start | bytes 589832 | tf_op jit(solution)/shard_map/ppermute | solution.py:200
  11.2 15.9 %collective-permute-start.4 = (bf16[96,1024]{1,0:T(8,128)(2,1)}, bf16[96,1024]{1,0:T(8,128)(2,1)S(1)}, u32[]{:S(2)}, u32[]{:S(2)}) collective-permute-start(bf16[96,1024]{1,0:T(8,128)(2,1)} %get-tuple-element.28), channel_id=1, source_target_pairs={{0,8},{4,12},{8,0},{12,4},{16,24},{20,28},{24,16},{28,20},{1,9},{5... | collective-permute-start | bytes 589832 | tf_op jit(solution)/shard_map/ppermute | solution.py:200
  15.4 11.7 %collective-permute-start.5 = (bf16[96,1024]{1,0:T(8,128)(2,1)}, bf16[96,1024]{1,0:T(8,128)(2,1)S(1)}, u32[]{:S(2)}, u32[]{:S(2)}) collective-permute-start(bf16[96,1024]{1,0:T(8,128)(2,1)} %get-tuple-element.29), channel_id=1, source_target_pairs={{0,12},{4,8},{8,4},{12,0},{16,28},{20,24},{24,20},{28,16},{1,13},{... | collective-permute-start | bytes 589832 | tf_op jit(solution)/shard_map/ppermute | solution.py:200
  19.3 7.8 %collective-permute-start.6 = (bf16[96,1024]{1,0:T(8,128)(2,1)}, bf16[96,1024]{1,0:T(8,128)(2,1)S(1)}, u32[]{:S(2)}, u32[]{:S(2)}) collective-permute-start(bf16[96,1024]{1,0:T(8,128)(2,1)} %get-tuple-element.31), channel_id=1, source_target_pairs={{0,4},{4,0},{8,12},{12,8},{16,20},{20,16},{24,28},{28,24},{1,5},{5... | collective-permute-start | bytes 589832 | tf_op jit(solution)/shard_map/ppermute | solution.py:200
  19.4 0.9 %copy-start.5 = (bf16[96,1024]{1,0:T(8,128)(2,1)S(1)}, bf16[96,1024]{1,0:T(8,128)(2,1)}, u32[]{:S(2)}) copy-start(bf16[96,1024]{1,0:T(8,128)(2,1)} %get-tuple-element.30.block_ref) | copy-start | bytes 589828
  34.6 0.8 copy-start.4
  35.4 14.4 %copy-start.3 = (bf16[256,1024]{1,0:T(8,128)(2,1)}, bf16[256,1024]{1,0:T(8,128)(2,1)S(1)}, u32[]{:S(2)}) copy-start(bf16[256,1024]{1,0:T(8,128)(2,1)S(1)} %get-tuple-element.38.third_ref) | copy-start | bytes 1572868
  35.4 16.8 %collective-permute-start.10 = (bf16[256,1024]{1,0:T(8,128)(2,1)}, bf16[256,1024]{1,0:T(8,128)(2,1)}, u32[]{:S(2)}, u32[]{:S(2)}) collective-permute-start(bf16[256,1024]{1,0:T(8,128)(2,1)} %get-tuple-element.39), channel_id=1, source_target_pairs={{0,1},{1,0},{2,3},{3,2},{4,5},{5,4},{6,7},{7,6},{8,9},{9,8},{10,11... | collective-permute-start | bytes 1572872 | tf_op jit(solution)/shard_map/ppermute | solution.py:227
  39.2 18.7 %copy-start.1 = (bf16[576,512]{1,0:T(8,128)(2,1)S(1)}, bf16[576,512]{1,0:T(8,128)(2,1)}, u32[]{:S(2)}) copy-start(bf16[576,512]{1,0:T(8,128)(2,1)} %tok_ref.1) | copy-start | bytes 1769476
  39.2 18.7 %copy-start.2 = (bf16[576,512]{1,0:T(8,128)(2,1)S(1)}, bf16[576,512]{1,0:T(8,128)(2,1)}, u32[]{:S(2)}) copy-start(bf16[576,512]{1,0:T(8,128)(2,1)} %go_ref.1) | copy-start | bytes 1769476
  39.2 18.7 %copy-start.6 = (s32[1,576]{1,0:T(1,128)S(1)}, s32[1,576]{1,0:T(1,128)}, u32[]{:S(2)}) copy-start(s32[1,576]{1,0:T(1,128)} %get-tuple-element.23.target_ref) | copy-start | bytes 6916
  39.2 18.7 %copy-start.7 = (bf16[576]{0:T(1024)(128)(2,1)S(1)}, bf16[576]{0:T(1024)(128)(2,1)}, u32[]{:S(2)}) copy-start(bf16[576]{0:T(1024)(128)(2,1)} %gate_ref.1) | copy-start | bytes 3460
  39.2 18.7 %copy-start.8 = (f32[512]{0:T(512)S(1)}, f32[512]{0:T(512)}, u32[]{:S(2)}) copy-start(f32[512]{0:T(512)} %param.8) | copy-start | bytes 6148
  39.2 18.6 %all-to-all-start = ((bf16[8,96,640]{2,1,0:T(8,128)(2,1)}), bf16[8,96,640]{2,1,0:T(8,128)(2,1)S(1)}, u32[]{:S(2)}, u32[]{:S(2)}) async-start(bf16[8,96,640]{2,1,0:T(8,128)(2,1)} %back.1), calls=%async_computation | async-start | bytes 1966080 | tf_op jit(solution)/shard_map/all_to_all | solution.py:340
  43.1 17.6 %collective-permute-start.8 = (bf16[256,1024]{1,0:T(8,128)(2,1)S(1)}, bf16[256,1024]{1,0:T(8,128)(2,1)}, u32[]{:S(2)}, u32[]{:S(2)}) collective-permute-start(bf16[256,1024]{1,0:T(8,128)(2,1)S(1)} %get-tuple-element.37), channel_id=1, source_target_pairs={{0,2},{3,1},{4,6},{7,5},{8,10},{11,9},{12,14},{15,13},{16,18},{19,... | collective-permute-start | bytes 1572872 | tf_op jit(solution)/shard_map/ppermute | solution.py:229
  48.4 12.4 %collective-permute-start.7 = (bf16[256,1024]{1,0:T(8,128)(2,1)S(1)}, bf16[256,1024]{1,0:T(8,128)(2,1)}, u32[]{:S(2)}, u32[]{:S(2)}) collective-permute-start(bf16[256,1024]{1,0:T(8,128)(2,1)S(1)} %get-tuple-element.37), channel_id=1, source_target_pairs={{1,2},{2,1},{5,6},{6,5},{9,10},{10,9},{13,14},{14,13},{17,18},{18,... | collective-permute-start | bytes 1572872 | tf_op jit(solution)/shard_map/ppermute | solution.py:228
  49.8 21.5 %collective-permute-start.9 = (bf16[256,1024]{1,0:T(8,128)(2,1)S(1)}, bf16[256,1024]{1,0:T(8,128)(2,1)}, u32[]{:S(2)}, u32[]{:S(2)}) collective-permute-start(bf16[256,1024]{1,0:T(8,128)(2,1)S(1)} %get-tuple-element.38.third_ref), channel_id=1, source_target_pairs={{0,1},{3,2},{4,5},{7,6},{8,9},{11,10},{12,13},{15,14},{16,17},{19,... | collective-permute-start | bytes 1572872 | tf_op jit(solution)/shard_map/ppermute | solution.py:230
  54.3 29.7 %collective-permute-start.11 = (bf16[256,1024]{1,0:T(8,128)(2,1)}, bf16[256,1024]{1,0:T(8,128)(2,1)}, u32[]{:S(2)}, u32[]{:S(2)}) collective-permute-start(bf16[256,1024]{1,0:T(8,128)(2,1)} %pass.1), channel_id=1, source_target_pairs={{1,3},{2,0},{5,7},{6,4},{9,11},{10,8},{13,15},{14,12},{17,19},{18,... | collective-permute-start | bytes 1572872 | tf_op jit(solution)/shard_map/ppermute | solution.py:240

commit v5 on v4

--- a/solution.py
+++ b/solution.py
@@ -107,23 +107,12 @@
 
 def gelu_parts(value):
     root = 0.7978845608028654
+    cubic = root * 0.044715
     square = value * value
-    tan = jnp.tanh(root * (value + 0.044715 * value * square))
-    half = 0.5 * (1.0 + tan)
-    slope = half + 0.5 * value * (1.0 - tan * tan) * (root * (1.0 + 3.0 * 0.044715 * square))
-    return value * half, slope
-
-
-def expert_chunk(rows_ref, w_in_ref, w_out_ref, part):
-    width = w_in_ref.shape[0]
-    delta = rows_ref[:, width:]
-    preact = dot(rows_ref[:, :width], w_in_ref[:, part])
-    act_float, slope = gelu_parts(preact)
-    act = act_float.astype(BF16)
-    grad_act = dot(delta, w_out_ref[part, :], ((1,), (1,)))
-    weight = dot(act.T, delta).astype(BF16)
-    total = jnp.sum(act.astype(F32) * grad_act, axis=1, keepdims=True)
-    return weight, (grad_act * slope).astype(BF16), total
+    tan = jnp.tanh(value * (root + cubic * square))
+    half = 0.5 + 0.5 * tan
+    act = value * half
+    return act, half + act * (1.0 - tan) * (root + 3.0 * cubic * square)
 
 
 def shard_order(place):
@@ -132,47 +121,75 @@
     return [first, second, 6 - first - second - place, place]
 
 
-def grads_kernel(sources, capacity, groups, place, w_in_ref, w_out_ref, *refs):
-    blocks = refs[:sources]
-    outs = refs[sources : sources + LINE]
-    gpre_ref, extra_ref, rows_ref, turned_ref, sems = refs[sources + LINE :]
+def expert_work(order, blocks, w_in_ref, w_out_ref, gpre_ref, extra_ref, rows_ref, turned_ref, put):
+    capacity = blocks[0].shape[0]
     width, hidden = w_in_ref.shape
     piece_d, piece_f = width // LINE, hidden // LINE
-    order = shard_order(place[0]) if groups == LINE else list(range(LINE))
-    spans = [pl.ds(j * capacity, capacity) for j in range(sources)]
-    if capacity % 16:
-        for j in range(sources):
-            rows_ref[spans[j], :] = blocks[j][...]
-    else:
-        for copy in start_copies([(blocks[j], rows_ref.at[spans[j]]) for j in range(sources)], sems):
-            copy.wait()
+    for j, block in enumerate(blocks):
+        rows_ref[j * capacity : (j + 1) * capacity, :] = block[...]
     for j in range(LINE):
         start = pl.multiple_of(order[j] * piece_d, piece_d)
         turned_ref[j * piece_d : (j + 1) * piece_d, :] = rows_ref[:, pl.ds(start, piece_d)].T
-    total = jnp.zeros((sources * capacity, 1), F32)
+    total = jnp.zeros(extra_ref.shape, F32)
     for j in range(LINE):
         part = pl.ds(pl.multiple_of(order[j] * piece_f, piece_f), piece_f)
-        weight, grad_pre, more = expert_chunk(rows_ref, w_in_ref, w_out_ref, part)
-        total += more
+        delta = rows_ref[:, width:]
+        act, slope = gelu_parts(dot(rows_ref[:, :width], w_in_ref[:, part]))
+        grad_act = dot(delta, w_out_ref[part, :], ((1,), (1,)))
+        products = act * grad_act
+        for lane in range(0, piece_f, LANES):
+            total += products[:, lane : lane + LANES]
+        grad_pre = (grad_act * slope).astype(BF16)
         gpre_ref[:, part] = grad_pre
-        outs[j][piece_d:, :width] = weight[: piece_f // 2]
-        outs[j][piece_d:, width:] = weight[piece_f // 2 :]
-        weight = dot(turned_ref[...], grad_pre).astype(BF16)
-        for i in range(LINE):
-            outs[i][:piece_d, part] = weight[i * piece_d : (i + 1) * piece_d]
+        put(j, part, dot(turned_ref[...], grad_pre), dot(act.astype(BF16).T, delta))
+    total = jnp.sum(total, axis=1, keepdims=True)
     high = total.astype(BF16).astype(F32)
     lane = lax.broadcasted_iota(jnp.int32, extra_ref.shape, 1)
     extra_ref[...] = jnp.where(lane == 0, high, jnp.where(lane == 1, total - high, 0.0)).astype(BF16)
 
 
-def back_kernel(sources, capacity, me, gpre_ref, w_in_ref, extra_ref, out_ref):
+def sooner_kernel(count, groups, place, w_in_ref, w_out_ref, *refs):
+    blocks = refs[:count]
+    sum_in_ref, sum_out_ref, gpre_ref, extra_ref, rows_ref, turned_ref = refs[count:]
+    piece_f = w_in_ref.shape[1] // LINE
+
+    def put(j, part, weight_in, weight_out):
+        sum_in_ref[:, part] = weight_in
+        sum_out_ref[j * piece_f : (j + 1) * piece_f, :] = weight_out
+
+    order = shard_order(place[0]) if groups == LINE else list(range(LINE))
+    expert_work(order, blocks, w_in_ref, w_out_ref, gpre_ref, extra_ref, rows_ref, turned_ref, put)
+
+
+def later_kernel(count, groups, place, w_in_ref, w_out_ref, sum_in_ref, sum_out_ref, *refs):
+    blocks = refs[:count]
+    outs = refs[count : count + LINE]
+    gpre_ref, extra_ref, rows_ref, turned_ref = refs[count + LINE :]
+    width, hidden = w_in_ref.shape
+    piece_d, piece_f = width // LINE, hidden // LINE
+
+    def put(j, part, weight_in, weight_out):
+        weight = (sum_out_ref[j * piece_f : (j + 1) * piece_f, :] + weight_out).astype(BF16)
+        outs[j][piece_d:, :width] = weight[: piece_f // 2]
+        outs[j][piece_d:, width:] = weight[piece_f // 2 :]
+        weight = (sum_in_ref[:, part] + weight_in).astype(BF16)
+        for i in range(LINE):
+            outs[i][:piece_d, part] = weight[i * piece_d : (i + 1) * piece_d]
+
+    order = shard_order(place[0]) if groups == LINE else list(range(LINE))
+    expert_work(order, blocks, w_in_ref, w_out_ref, gpre_ref, extra_ref, rows_ref, turned_ref, put)
+
+
+def back_kernel(sources, capacity, sets, me, w_in_ref, *refs):
+    out_ref = refs[-1]
     width = w_in_ref.shape[0]
-    grad = dot(gpre_ref[...], w_in_ref[...], ((1,), (1,))).astype(BF16)
-    for j in range(sources):
-        block = slice(j * capacity, (j + 1) * capacity)
-        source = jnp.bitwise_xor(block_base(me, sources), j)
-        out_ref[source, :, :width] = grad[block]
-        out_ref[source, :, width:] = extra_ref[block, :]
+    for members, gpre_ref, extra_ref in zip(sets, refs[0:-1:2], refs[1:-1:2]):
+        grad = dot(gpre_ref[...], w_in_ref[...], ((1,), (1,))).astype(BF16)
+        for i, j in enumerate(members):
+            block = slice(i * capacity, (i + 1) * capacity)
+            source = jnp.bitwise_xor(block_base(me, sources), j)
+            out_ref[source, :, :width] = grad[block]
+            out_ref[source, :, width:] = extra_ref[block, :]
 
 
 def finish_kernel(target_ref, gate_ref, tok_ref, gain_ref, go_ref, back_ref, tokens_out, gate_out):
@@ -206,41 +223,51 @@
     return (place[0] == 1) | (place[0] == 2)
 
 
-def pass_kernel(place, third_ref, swapped_ref, out_ref):
-    swapped = jnp.where(is_inner(place), swapped_ref[...].astype(F32), 0.0)
-    out_ref[...] = (third_ref[...].astype(F32) + swapped).astype(BF16)
-
-
-def total_kernel(place, own_ref, middle_ref, across_ref, outer_ref, swapped_ref, last_ref, in_ref, out_ref):
+def pass_kernel(place, third_ref, swapped_ref, own_ref, out_ref, sum_ref):
+    swapped = swapped_ref[...].astype(F32)
+    onward = jnp.where(is_inner(place), swapped, 0.0)
+    out_ref[...] = (third_ref[...].astype(F32) + onward).astype(BF16)
+    sum_ref[...] = own_ref[...].astype(F32) + (swapped - onward)
+
+
+def most_kernel(sum_ref, middle_ref, across_ref, outer_ref, out_ref):
+    total = sum_ref[...]
+    for ref in (middle_ref, across_ref, outer_ref):
+        total += ref[...].astype(F32)
+    out_ref[...] = total
+
+
+def total_kernel(sum_ref, last_ref, in_ref, out_ref):
     piece_d, half = in_ref.shape[0], out_ref.shape[0] // 2
     width = out_ref.shape[1]
-    swapped = jnp.where(is_inner(place), 0.0, swapped_ref[...].astype(F32))
-    total = own_ref[...].astype(F32) + swapped
-    for ref in (middle_ref, across_ref, outer_ref, last_ref):
-        total += ref[...].astype(F32)
+    total = sum_ref[...] + last_ref[...].astype(F32)
     in_ref[...] = total[:piece_d]
     out_ref[:half, :] = total[piece_d:, :width]
     out_ref[half:, :] = total[piece_d:, width:]
 
 
-def line_sums(place, first, second, third, own, width):
+def line_sums(place, first, second, third, own, width, behind):
     swapped = lax.ppermute(first, "dp", [(0, 1), (1, 0), (2, 3), (3, 2)])
     middle = lax.ppermute(second, "dp", [(1, 2), (2, 1)])
     across = lax.ppermute(second, "dp", [(0, 2), (3, 1)])
+    swapped, behind = lax.optimization_barrier((swapped, behind))
     outer = lax.ppermute(third, "dp", [(0, 1), (3, 2)])
-    (passed,) = kernel_call(
+    rows, hidden = own.shape
+    piece_d = width // LINE
+    whole = jax.ShapeDtypeStruct(own.shape, F32)
+    passed, some = kernel_call(
         pass_kernel,
         "pass",
         1,
         1,
-        [jax.ShapeDtypeStruct(third.shape, BF16)],
-        [smem] + [vmem] * 2,
-        vmem_mib=56,
-    )(place, third, swapped)
+        [jax.ShapeDtypeStruct(own.shape, BF16), whole],
+        [smem] + [vmem] * 3,
+    )(place, third, swapped, own)
     last = lax.ppermute(passed, "dp", [(1, 3), (2, 0)])
-    rows, hidden = own.shape
-    piece_d = width // LINE
-    return kernel_call(
+    (most,) = kernel_call(
+        most_kernel, "most", 1, 1, [whole], [vmem] * 4, vmem_mib=56
+    )(some, middle, across, outer)
+    sums = kernel_call(
         total_kernel,
         "total",
         1,
@@ -249,9 +276,10 @@
             jax.ShapeDtypeStruct((piece_d, hidden), F32),
             jax.ShapeDtypeStruct((2 * (rows - piece_d), width), F32),
         ],
-        [smem] + [vmem] * 6,
+        [vmem] * 2,
         vmem_mib=56,
-    )(place, own, middle, across, outer, swapped, last)
+    )(most, last)
+    return *sums, behind
 
 
 def body(tokens, gain, w_in, w_out, expert_ids, gate, grad_out):
@@ -304,31 +332,37 @@
     arrived = swap_blocks(sent)
     arrived[sources - 2] = kept
 
-    *parts, gpre, extra = kernel_call(
-        functools.partial(grads_kernel, sources, capacity, groups),
-        "grads",
-        8 * rows * width * hidden,
-        2 * (2 * rows * width + 4 * width * hidden + rows * hidden),
-        [shape((width // LINE + hidden // LINE // 2, hidden), BF16)] * LINE
-        + [shape((rows, hidden), BF16), shape((rows, LANES), BF16)],
-        [smem] + [vmem] * 2 + [block_place] * sources,
-        [
-            pltpu.VMEM((rows, 2 * width), BF16),
-            pltpu.VMEM((width, rows), BF16),
-            sems((sources,)),
-        ],
-    )(place, weight_in, weight_out, *arrived)
+    late_set = list(range(3 * sources // 8, 6 * sources // 8))
+    soon_set = [j for j in range(sources) if j not in late_set]
+
+    def work(kernel, name, members, outs, *sums):
+        count, span = len(members), len(members) * capacity
+        return kernel_call(
+            functools.partial(kernel, count, groups),
+            name,
+            8 * span * width * hidden,
+            2 * (2 * span * width + 4 * width * hidden + span * hidden),
+            outs + [shape((span, hidden), BF16), shape((span, LANES), BF16)],
+            [smem] + [vmem] * (2 + len(sums) + count),
+            [pltpu.VMEM((span, 2 * width), BF16), pltpu.VMEM((width, span), BF16)],
+        )(place, weight_in, weight_out, *sums, *[arrived[j] for j in members])
+
+    *sums, soon_gpre, soon_extra = work(
+        sooner_kernel, "sooner", soon_set, [shape((width, hidden), F32), shape((hidden, width), F32)]
+    )
+    piece = shape((width // LINE + hidden // LINE // 2, hidden), BF16)
+    *parts, late_gpre, late_extra = work(later_kernel, "later", late_set, [piece] * LINE, *sums)
     (returned,) = kernel_call(
-        functools.partial(back_kernel, sources, capacity),
+        functools.partial(back_kernel, sources, capacity, (soon_set, late_set)),
         "back",
         1,
         1,
         [shape((sources, capacity, width + LANES), BF16)],
-        [smem] + [vmem] * 3,
-    )(me, gpre, weight_in, extra)
+        [smem] + [vmem] * 5,
+    )(me, weight_in, soon_gpre, soon_extra, late_gpre, late_extra)
 
     if groups == LINE:
-        grad_w_in, grad_w_out = line_sums(place, *parts, width)
+        grad_w_in, grad_w_out, returned = line_sums(place, *parts, width, returned)
     else:
         parts_in, parts_out = zip(*[split_piece(part, width, LINE) for part in parts])
         grad_w_in, grad_w_out = (

time: 87.4 us -> 94.9 us (1.086)
  waiting for transfers between devices: 39.1 us -> 43.6 us
  local copies, waits for them, and re-layouts: 1.75 us -> 3.84 us
  starting transfers between devices: 23.5 us -> 25.2 us
    ppermute x1, waiting for transfers between devices: 0.01 us -> 10.2 us  [line_sums(): swapped = lax.ppermute(first, 'dp', [(0, 1), (1, 0), (2, 3), (3, 2)])]
    ppermute x1, waiting for transfers between devices: 10.6 us -> 16.9 us  [line_sums(): outer = lax.ppermute(third, 'dp', [(0, 1), (3, 2)])]
    ppermute x7, waiting for transfers between devices: 13.2 us -> 7.6 us  [swap_blocks(): lax.ppermute(blocks[j], 'space', [(i, i ^ j ^ count - 2) for i in range(c...]
    ppermute x1, waiting for transfers between devices: 12.7 us -> 8.88 us  [line_sums(): last = lax.ppermute(passed, 'dp', [(1, 3), (2, 0)])]
    ppermute x7, starting transfers between devices: 7.51 us -> 9.85 us  [swap_blocks(): lax.ppermute(blocks[j], 'space', [(i, i ^ j ^ count - 2) for i in range(c...]
    all_to_all x1, waiting for transfers between devices: 2.24 us -> 0.01 us  [body(): lax.all_to_all(returned, 'space', split_axis=0, concat_axis=0, tiled=True)]
    unnamed x20 -> x28, local copies, waits for them, and re-layouts: 1.75 us -> 3.84 us
    pallas_call x3 -> x5, Pallas kernels: 11.6 us -> 11.4 us  [the longest x2 6.15 us: work(): kernel_call(functools.partial(kernel, count, groups), name, 8 * span * wi...]
  transfers between devices with their start and end apart: 13 -> 13, of which waited for: 8 -> 7; matrix products, arithmetic and copies ran while one was open for 0% -> 0% of each run, Pallas kernels for 8% -> 11%
where the time goes in v5:
time: 94.9 us; the launch traced here: 94.6 us
  waiting for transfers between devices  43.6 us (46%)
  starting transfers between devices  25.2 us (27%)
  Pallas kernels  21.1 us (22%)
  local copies, waits for them, and re-layouts  3.84 us (4%)
    ppermute x1, waiting for transfers between devices, line_sums(): outer = lax.ppermute(third, 'dp', [(0, 1), (3, 2)])  16.9 us
    ppermute x1, waiting for transfers between devices, line_sums(): swapped = lax.ppermute(first, 'dp', [(0, 1), (1, 0), (2, 3), (3, 2)])  10.2 us
    ppermute x7, starting transfers between devices, swap_blocks(): lax.ppermute(blocks[j], 'space', [(i, i ^ j ^ count - 2) for i in range(c...  9.85 us
    ppermute x1, waiting for transfers between devices, line_sums(): last = lax.ppermute(passed, 'dp', [(1, 3), (2, 0)])  8.88 us
    ppermute x7, waiting for transfers between devices, swap_blocks(): lax.ppermute(blocks[j], 'space', [(i, i ^ j ^ count - 2) for i in range(c...  7.6 us
    pallas_call x2, Pallas kernels, work(): kernel_call(functools.partial(kernel, count, groups), name, 8 * span * wi...  6.15 us
    pallas_call x1, Pallas kernels, body(): kernel_call(functools.partial(place_kernel, sources, capacity), 'place',...  4.77 us
    ppermute x1, starting transfers between devices, line_sums(): across = lax.ppermute(second, 'dp', [(0, 2), (3, 1)])  4.52 us
  transfers between devices with their start and end apart: 13, of which 7 were waited for; matrix products, arithmetic and copies ran while one was open for 0% of the time, Pallas kernels for 11%

profile of v5, /device:TPU:0, one launch (start us, length us, event | category | flops | bytes accessed | tf_op | source)
XLA Modules:
  0.0 94.6 jit_solution(1468193720414403832)
XLA Ops:
  0.7 4.8 %place.1 = (s32[1,576]{1,0:T(1,128)}, bf16[96,1024]{1,0:T(8,128)(2,1)}, bf16[96,1024]{1,0:T(8,128)(2,1)}, bf16[96,1024]{1,0:T(8,128)(2,1)}, bf16[96,1024]{1,0:T(...) custom-call(s32[1]{0:T(128)} %bitcast.me, ...), custom_call_target="tpu_custom_call" | custom-call | flops 905969664 | bytes 2752512 | tf_op jit(solution)/shard_map/place/pallas_call | solution.py:302
  5.4 4.0 %collective-permute-start = (bf16[96,1024]{1,0:T(8,128)(2,1)}, bf16[96,1024]{1,0:T(8,128)(2,1)S(1)}, u32[]{:S(2)}, u32[]{:S(2)}) collective-permute-start(bf16[96,1024]{1,0:T(8,128)(2,1)} %get-tuple-element.32), channel_id=1, source_target_pairs={{0,24},{4,28},{8,16},{12,20},{16,8},{20,12},{24,0},{28,4},{1,25},{... | collective-permute-start | bytes 589832 | tf_op jit(solution)/shard_map/ppermute | solution.py:217
  9.4 1.1 %collective-permute-start.2 = (bf16[96,1024]{1,0:T(8,128)(2,1)}, bf16[96,1024]{1,0:T(8,128)(2,1)S(1)}, u32[]{:S(2)}, u32[]{:S(2)}) collective-permute-start(bf16[96,1024]{1,0:T(8,128)(2,1)} %get-tuple-element.34), channel_id=1, source_target_pairs={{0,16},{4,20},{8,24},{12,28},{16,0},{20,4},{24,8},{28,12},{1,17},{... | collective-permute-start | bytes 589832 | tf_op jit(solution)/shard_map/ppermute | solution.py:217
  10.6 0.7 collective-permute-start.3
  11.2 0.3 collective-permute-start.4
  11.6 3.9 %collective-permute-done.refs_0_ = bf16[96,1024]{1,0:T(8,128)(2,1)S(1)} collective-permute-done((bf16[96,1024]{1,0:T(8,128)(2,1)}, bf16[96,1024]{1,0:T(8,128)(2,1)S(1)}, u32[]{:S(2)}, u32[]{:S(2)}) %collective-permute-start) | collective-permute-done | bytes 196640 | tf_op jit(solution)/shard_map/ppermute | solution.py:217
  15.4 2.0 %collective-permute-start.5 = (bf16[96,1024]{1,0:T(8,128)(2,1)}, bf16[96,1024]{1,0:T(8,128)(2,1)S(1)}, u32[]{:S(2)}, u32[]{:S(2)}) collective-permute-start(bf16[96,1024]{1,0:T(8,128)(2,1)} %get-tuple-element.40), channel_id=1, source_target_pairs={{0,8},{4,12},{8,0},{12,4},{16,24},{20,28},{24,16},{28,20},{1,9},{5... | collective-permute-start | bytes 589832 | tf_op jit(solution)/shard_map/ppermute | solution.py:217
  17.4 1.8 %collective-permute-done.1.refs_1_ = bf16[96,1024]{1,0:T(8,128)(2,1)S(1)} collective-permute-done((bf16[96,1024]{1,0:T(8,128)(2,1)}, bf16[96,1024]{1,0:T(8,128)(2,1)S(1)}, u32[]{:S(2)}, u32[]{:S(2)}) %collective-permute-start.1) | collective-permute-done | bytes 196640 | tf_op jit(solution)/shard_map/ppermute | solution.py:217
  19.3 1.7 %collective-permute-start.6 = (bf16[96,1024]{1,0:T(8,128)(2,1)}, bf16[96,1024]{1,0:T(8,128)(2,1)S(1)}, u32[]{:S(2)}, u32[]{:S(2)}) collective-permute-start(bf16[96,1024]{1,0:T(8,128)(2,1)} %get-tuple-element.41), channel_id=1, source_target_pairs={{0,12},{4,8},{8,4},{12,0},{16,28},{20,24},{24,20},{28,16},{1,13},{... | collective-permute-start | bytes 589832 | tf_op jit(solution)/shard_map/ppermute | solution.py:217
  21.0 0.9 copy-done.5
  22.0 1.0 %collective-permute-done.2.refs_2_ = bf16[96,1024]{1,0:T(8,128)(2,1)S(1)} collective-permute-done((bf16[96,1024]{1,0:T(8,128)(2,1)}, bf16[96,1024]{1,0:T(8,128)(2,1)S(1)}, u32[]{:S(2)}, u32[]{:S(2)}) %collective-permute-start.2) | collective-permute-done | bytes 196640 | tf_op jit(solution)/shard_map/ppermute | solution.py:217
  23.0 3.2 %sooner.1 = (f32[512,1024]{1,0:T(8,128)S(1)}, f32[1024,512]{1,0:T(8,128)S(1)}, bf16[480,1024]{1,0:T(8,128)(2,1)S(1)}, bf16[480,128]{1,0:T(8,128)(2,1)S(1)}) custom-call(s32[1]{0:T(128)} %bitcast.1.place, bf16[512,1024]{1,0:T(8,128)(2,1)S(1)} %bitcast.9, bf16[1024,512]{1,0:T(8,128)(2,1)S(1)} %bitcast.13, bf16[96,1024]{1,0:T(8,128)(2,1)S(1)} %collective-permute-done.refs_0_, ...), custom_call_target="tpu_custom_call" | custom-call | flops 2013265920 | bytes 6160384 | tf_op jit(solution)/shard_map/sooner/pallas_call | solution.py:340
  26.2 0.8 collective-permute-done.4.refs_0_
  27.1 2.9 %later.1 = (bf16[256,1024]{1,0:T(8,128)(2,1)S(1)}, bf16[256,1024]{1,0:T(8,128)(2,1)S(1)}, bf16[256,1024]{1,0:T(8,128)(2,1)S(1)}, bf16[256,1024]{1,0:T(8,128)(2,1...) custom-call(s32[1]{0:T(128)} %bitcast.1.place, bf16[512,1024]{1,0:T(8,128)(2,1)S(1)} %bitcast.10, ...), custom_call_target="tpu_custom_call" | custom-call | flops 1207959552 | bytes 5373952 | tf_op jit(solution)/shard_map/later/pallas_call | solution.py:340
  30.0 1.9 %collective-permute-start.7 = (bf16[256,1024]{1,0:T(8,128)(2,1)S(1)}, bf16[256,1024]{1,0:T(8,128)(2,1)S(1)}, u32[]{:S(2)}, u32[]{:S(2)}) collective-permute-start(bf16[256,1024]{1,0:T(8,128)(2,1)S(1)} %get-tuple-element.42), channel_id=1, source_target_pairs={{0,1},{1,0},{2,3},{3,2},{4,5},{5,4},{6,7},{7,6},{8,9},{9,8},{10,11... | collective-permute-start | bytes 1572872 | tf_op jit(solution)/shard_map/ppermute | solution.py:250
  31.9 2.0 %back.1 = bf16[8,96,640]{2,1,0:T(8,128)(2,1)} custom-call(s32[1]{0:T(128)} %bitcast.me, bf16[512,1024]{1,0:T(8,128)(2,1)S(1)} %bitcast.11, bf16[480,1024]{1,0:T(8,128)(2,1)S(1)} %get-tuple-element.43.refs_0_, bf16[480,128]{1,0:T(8,128)(2,1)S(1)} %get-tuple-element.44.refs_1_, bf16[288,1024]{1,0:T(8,128)(2,1)S(1)} %get-tuple-element.45.refs_2_, ...), custom_call_target="tpu_custom_call" | custom-call | flops 1 | bytes 1 | tf_op jit(solution)/shard_map/back/pallas_call | solution.py:355
  33.9 10.2 %collective-permute-done.7.swapped_ref = bf16[256,1024]{1,0:T(8,128)(2,1)S(1)} collective-permute-done((bf16[256,1024]{1,0:T(8,128)(2,1)S(1)}, bf16[256,1024]{1,0:T(8,128)(2,1)S(1)}, u32[]{:S(2)}, u32[]{:S(2)}) %collective-permute-start.7) | collective-permute-done | bytes 524320 | tf_op jit(solution)/shard_map/ppermute | solution.py:250
  44.1 3.9 %all-to-all-start = ((bf16[8,96,640]{2,1,0:T(8,128)(2,1)}), bf16[8,96,640]{2,1,0:T(8,128)(2,1)S(1)}, u32[]{:S(2)}, u32[]{:S(2)}) async-start(bf16[8,96,640]{2,1,0:T(8,128)(2,1)} %back.1), calls=%async_computation | async-start | bytes 1966080 | tf_op jit(solution)/shard_map/all_to_all | solution.py:374
  48.0 4.5 %collective-permute-start.9 = (bf16[256,1024]{1,0:T(8,128)(2,1)}, bf16[256,1024]{1,0:T(8,128)(2,1)S(1)}, u32[]{:S(2)}, u32[]{:S(2)}) collective-permute-start(bf16[256,1024]{1,0:T(8,128)(2,1)} %copy-done.9), channel_id=1, source_target_pairs={{0,2},{3,1},{4,6},{7,5},{8,10},{11,9},{12,14},{15,13},{16,18},{19,... | collective-permute-start | bytes 1572872 | tf_op jit(solution)/shard_map/ppermute | solution.py:252
  52.5 0.7 collective-permute-start.8
  53.2 3.1 %collective-permute-start.10 = (bf16[256,1024]{1,0:T(8,128)(2,1)S(1)}, bf16[256,1024]{1,0:T(8,128)(2,1)S(1)}, u32[]{:S(2)}, u32[]{:S(2)}) collective-permute-start(bf16[256,1024]{1,0:T(8,128)(2,1)S(1)} %get-tuple-element.50.third_ref), channel_id=1, source_target_pairs={{0,1},{3,2},{4,5},{7,6},{8,9},{11,10},{12,13},{15,14},{16,17},{19,... | collective-permute-start | bytes 1572872 | tf_op jit(solution)/shard_map/ppermute | solution.py:254
  56.3 0.3 pass.1
  56.6 1.0 %copy-done.1 = f32[256,1024]{1,0:T(8,128)} copy-done((f32[256,1024]{1,0:T(8,128)}, f32[256,1024]{1,0:T(8,128)S(1)}, u32[]{:S(2)}) %copy-start.1) | copy-done | bytes 1048600
  57.6 1.3 %collective-permute-start.11 = (bf16[256,1024]{1,0:T(8,128)(2,1)S(1)}, bf16[256,1024]{1,0:T(8,128)(2,1)S(1)}, u32[]{:S(2)}, u32[]{:S(2)}) collective-permute-start(bf16[256,1024]{1,0:T(8,128)(2,1)S(1)} %get-tuple-element.55), channel_id=1, source_target_pairs={{1,3},{2,0},{5,7},{6,4},{9,11},{10,8},{13,15},{14,12},{17,19},{18,... | collective-permute-start | bytes 1572872 | tf_op jit(solution)/shard_map/ppermute | solution.py:266
  58.9 16.9 %collective-permute-done.10.outer_ref = bf16[256,1024]{1,0:T(8,128)(2,1)S(1)} collective-permute-done((bf16[256,1024]{1,0:T(8,128)(2,1)S(1)}, bf16[256,1024]{1,0:T(8,128)(2,1)S(1)}, u32[]{:S(2)}, u32[]{:S(2)}) %collective-permute-start.10) | collective-permute-done | bytes 524320 | tf_op jit(solution)/shard_map/ppermute | solution.py:254
  75.8 0.8 copy-done.12
  76.6 0.2 copy-done.10
  77.0 2.9 %most.1.sum_ref = f32[256,1024]{1,0:T(8,128)} custom-call(f32[256,1024]{1,0:T(8,128)} %copy-done.1, bf16[256,1024]{1,0:T(8,128)(2,1)} %copy-done.11, bf16[256,1024]{1,0:T(8,128)(2,1)} %copy-done.10, bf16[256,1024]{1,0:T(8,128)(2,1)} %copy-done.12), custom_call_target="tpu_custom_call" | custom-call | flops 1 | bytes 1 | tf_op jit(solution)/shard_map/most/pallas_call | solution.py:267
  79.9 8.9 %collective-permute-done.11.last_ref = bf16[256,1024]{1,0:T(8,128)(2,1)S(1)} collective-permute-done((bf16[256,1024]{1,0:T(8,128)(2,1)S(1)}, bf16[256,1024]{1,0:T(8,128)(2,1)S(1)}, u32[]{:S(2)}, u32[]{:S(2)}) %collective-permute-start.11) | collective-permute-done | bytes 524320 | tf_op jit(solution)/shard_map/ppermute | solution.py:266
  88.8 0.8 copy-done.13
  89.6 2.4 %total.1 = (f32[128,1024]{1,0:T(8,128)}, f32[256,512]{1,0:T(8,128)}) custom-call(f32[256,1024]{1,0:T(8,128)} %most.1.sum_ref, bf16[256,1024]{1,0:T(8,128)(2,1)} %copy-done.13), custom_call_target="tpu_custom_call" | custom-call | flops 1 | bytes 1 | tf_op jit(solution)/shard_map/total/pallas_call | solution.py:270
  92.0 2.6 %finish.1 = (bf16[576,512]{1,0:T(8,128)(2,1)}, bf16[576]{0:T(1024)(128)(2,1)}) custom-call(s32[1,576]{1,0:T(1,128)S(1)} %copy-done.6, bf16[576]{0:T(1024)(128)(2,1)S(1)} %copy-done.7, bf16[576,512]{1,0:T(8,128)(2,1)S(1)} %copy-done.3, f32[1,512]{1,0:T(1,128)S(1)} %bitcast.16, bf16[576,512]{1,0:T(8,128)(2,1)S(1)} %copy-done.4, bf16[768,640]{1,0:T(8,128)(2,1)S(1)} %bitcast.12), custom_call_target="tpu_custom_call" | custom-call | flops 1 | bytes 1 | tf_op jit(solution)/shard_map/finish/pallas_call | solution.py:375
  (31 shorter events, 0.3 us)
Async XLA Ops:
  0.6 22.4 %copy-start.2 = (bf16[1,1024,512]{2,1,0:T(8,128)(2,1)S(1)}, bf16[1,1024,512]{2,1,0:T(8,128)(2,1)}, u32[]{:S(2)}) copy-start(bf16[1,1024,512]{2,1,0:T(8,128)(2,1)} %param.10) | copy-start | bytes 3145732
  0.6 22.4 %copy-start = (bf16[1,512,1024]{2,1,0:T(8,128)(2,1)S(1)}, bf16[1,512,1024]{2,1,0:T(8,128)(2,1)}, u32[]{:S(2)}) copy-start(bf16[1,512,1024]{2,1,0:T(8,128)(2,1)} %param.9) | copy-start | bytes 3145732
  5.4 10.0 %collective-permute-start = (bf16[96,1024]{1,0:T(8,128)(2,1)}, bf16[96,1024]{1,0:T(8,128)(2,1)S(1)}, u32[]{:S(2)}, u32[]{:S(2)}) collective-permute-start(bf16[96,1024]{1,0:T(8,128)(2,1)} %get-tuple-element.32), channel_id=1, source_target_pairs={{0,24},{4,28},{8,16},{12,20},{16,8},{20,12},{24,0},{28,4},{1,25},{... | collective-permute-start | bytes 589832 | tf_op jit(solution)/shard_map/ppermute | solution.py:217
  9.4 9.9 %collective-permute-start.1 = (bf16[96,1024]{1,0:T(8,128)(2,1)}, bf16[96,1024]{1,0:T(8,128)(2,1)S(1)}, u32[]{:S(2)}, u32[]{:S(2)}) collective-permute-start(bf16[96,1024]{1,0:T(8,128)(2,1)} %get-tuple-element.33), channel_id=1, source_target_pairs={{0,28},{4,24},{8,20},{12,16},{16,12},{20,8},{24,4},{28,0},{1,29},{... | collective-permute-start | bytes 589832 | tf_op jit(solution)/shard_map/ppermute | solution.py:217
  9.4 13.6 %collective-permute-start.2 = (bf16[96,1024]{1,0:T(8,128)(2,1)}, bf16[96,1024]{1,0:T(8,128)(2,1)S(1)}, u32[]{:S(2)}, u32[]{:S(2)}) collective-permute-start(bf16[96,1024]{1,0:T(8,128)(2,1)} %get-tuple-element.34), channel_id=1, source_target_pairs={{0,16},{4,20},{8,24},{12,28},{16,0},{20,4},{24,8},{28,12},{1,17},{... | collective-permute-start | bytes 589832 | tf_op jit(solution)/shard_map/ppermute | solution.py:217
  10.6 12.4 %collective-permute-start.3 = (bf16[96,1024]{1,0:T(8,128)(2,1)}, bf16[96,1024]{1,0:T(8,128)(2,1)S(1)}, u32[]{:S(2)}, u32[]{:S(2)}) collective-permute-start(bf16[96,1024]{1,0:T(8,128)(2,1)} %get-tuple-element.36), channel_id=1, source_target_pairs={{0,4},{4,0},{8,12},{12,8},{16,20},{20,16},{24,28},{28,24},{1,5},{5... | collective-permute-start | bytes 589832 | tf_op jit(solution)/shard_map/ppermute | solution.py:217
  11.2 15.9 %collective-permute-start.4 = (bf16[96,1024]{1,0:T(8,128)(2,1)}, bf16[96,1024]{1,0:T(8,128)(2,1)S(1)}, u32[]{:S(2)}, u32[]{:S(2)}) collective-permute-start(bf16[96,1024]{1,0:T(8,128)(2,1)} %get-tuple-element.39), channel_id=1, source_target_pairs={{0,20},{4,16},{8,28},{12,24},{16,4},{20,0},{24,12},{28,8},{1,21},{... | collective-permute-start | bytes 589832 | tf_op jit(solution)/shard_map/ppermute | solution.py:217
  15.4 11.6 %collective-permute-start.5 = (bf16[96,1024]{1,0:T(8,128)(2,1)}, bf16[96,1024]{1,0:T(8,128)(2,1)S(1)}, u32[]{:S(2)}, u32[]{:S(2)}) collective-permute-start(bf16[96,1024]{1,0:T(8,128)(2,1)} %get-tuple-element.40), channel_id=1, source_target_pairs={{0,8},{4,12},{8,0},{12,4},{16,24},{20,28},{24,16},{28,20},{1,9},{5... | collective-permute-start | bytes 589832 | tf_op jit(solution)/shard_map/ppermute | solution.py:217
  19.3 7.8 %collective-permute-start.6 = (bf16[96,1024]{1,0:T(8,128)(2,1)}, bf16[96,1024]{1,0:T(8,128)(2,1)S(1)}, u32[]{:S(2)}, u32[]{:S(2)}) collective-permute-start(bf16[96,1024]{1,0:T(8,128)(2,1)} %get-tuple-element.41), channel_id=1, source_target_pairs={{0,12},{4,8},{8,4},{12,0},{16,28},{20,24},{24,20},{28,16},{1,13},{... | collective-permute-start | bytes 589832 | tf_op jit(solution)/shard_map/ppermute | solution.py:217
  21.0 0.9 copy-start.5
  30.0 3.9 %copy-start.9 = (bf16[256,1024]{1,0:T(8,128)(2,1)}, bf16[256,1024]{1,0:T(8,128)(2,1)S(1)}, u32[]{:S(2)}) copy-start(bf16[256,1024]{1,0:T(8,128)(2,1)S(1)} %get-tuple-element.54) | copy-start | bytes 1572868
  30.0 14.1 %collective-permute-start.7 = (bf16[256,1024]{1,0:T(8,128)(2,1)S(1)}, bf16[256,1024]{1,0:T(8,128)(2,1)S(1)}, u32[]{:S(2)}, u32[]{:S(2)}) collective-permute-start(bf16[256,1024]{1,0:T(8,128)(2,1)S(1)} %get-tuple-element.42), channel_id=1, source_target_pairs={{0,1},{1,0},{2,3},{3,2},{4,5},{5,4},{6,7},{7,6},{8,9},{9,8},{10,11... | collective-permute-start | bytes 1572872 | tf_op jit(solution)/shard_map/ppermute | solution.py:250
  44.1 47.9 %all-to-all-start = ((bf16[8,96,640]{2,1,0:T(8,128)(2,1)}), bf16[8,96,640]{2,1,0:T(8,128)(2,1)S(1)}, u32[]{:S(2)}, u32[]{:S(2)}) async-start(bf16[8,96,640]{2,1,0:T(8,128)(2,1)} %back.1), calls=%async_computation | async-start | bytes 1966080 | tf_op jit(solution)/shard_map/all_to_all | solution.py:374
  48.0 27.8 %collective-permute-start.9 = (bf16[256,1024]{1,0:T(8,128)(2,1)}, bf16[256,1024]{1,0:T(8,128)(2,1)S(1)}, u32[]{:S(2)}, u32[]{:S(2)}) collective-permute-start(bf16[256,1024]{1,0:T(8,128)(2,1)} %copy-done.9), channel_id=1, source_target_pairs={{0,2},{3,1},{4,6},{7,5},{8,10},{11,9},{12,14},{15,13},{16,18},{19,... | collective-permute-start | bytes 1572872 | tf_op jit(solution)/shard_map/ppermute | solution.py:252
  52.5 23.3 %collective-permute-start.8 = (bf16[256,1024]{1,0:T(8,128)(2,1)}, bf16[256,1024]{1,0:T(8,128)(2,1)S(1)}, u32[]{:S(2)}, u32[]{:S(2)}) collective-permute-start(bf16[256,1024]{1,0:T(8,128)(2,1)} %copy-done.9), channel_id=1, source_target_pairs={{1,2},{2,1},{5,6},{6,5},{9,10},{10,9},{13,14},{14,13},{17,18},{18,... | collective-permute-start | bytes 1572872 | tf_op jit(solution)/shard_map/ppermute | solution.py:251
  53.2 22.6 %collective-permute-start.10 = (bf16[256,1024]{1,0:T(8,128)(2,1)S(1)}, bf16[256,1024]{1,0:T(8,128)(2,1)S(1)}, u32[]{:S(2)}, u32[]{:S(2)}) collective-permute-start(bf16[256,1024]{1,0:T(8,128)(2,1)S(1)} %get-tuple-element.50.third_ref), channel_id=1, source_target_pairs={{0,1},{3,2},{4,5},{7,6},{8,9},{11,10},{12,13},{15,14},{16,17},{19,... | collective-permute-start | bytes 1572872 | tf_op jit(solution)/shard_map/ppermute | solution.py:254
  56.6 1.0 %copy-start.1 = (f32[256,1024]{1,0:T(8,128)}, f32[256,1024]{1,0:T(8,128)S(1)}, u32[]{:S(2)}) copy-start(f32[256,1024]{1,0:T(8,128)S(1)} %get-tuple-element.53.sum_ref) | copy-start | bytes 3145732
  57.6 31.2 %collective-permute-start.11 = (bf16[256,1024]{1,0:T(8,128)(2,1)S(1)}, bf16[256,1024]{1,0:T(8,128)(2,1)S(1)}, u32[]{:S(2)}, u32[]{:S(2)}) collective-permute-start(bf16[256,1024]{1,0:T(8,128)(2,1)S(1)} %get-tuple-element.55), channel_id=1, source_target_pairs={{1,3},{2,0},{5,7},{6,4},{9,11},{10,8},{13,15},{14,12},{17,19},{18,... | collective-permute-start | bytes 1572872 | tf_op jit(solution)/shard_map/ppermute | solution.py:266
  75.8 0.8 copy-start.12
  75.8 1.0 %copy-start.10 = (bf16[256,1024]{1,0:T(8,128)(2,1)}, bf16[256,1024]{1,0:T(8,128)(2,1)S(1)}, u32[]{:S(2)}) copy-start(bf16[256,1024]{1,0:T(8,128)(2,1)S(1)} %collective-permute-done.9.across_ref) | copy-start | bytes 1572868
  75.8 1.1 %copy-start.11 = (bf16[256,1024]{1,0:T(8,128)(2,1)}, bf16[256,1024]{1,0:T(8,128)(2,1)S(1)}, u32[]{:S(2)}) copy-start(bf16[256,1024]{1,0:T(8,128)(2,1)S(1)} %collective-permute-done.8.middle_ref) | copy-start | bytes 1572868
  76.9 15.0 %copy-start.3 = (bf16[576,512]{1,0:T(8,128)(2,1)S(1)}, bf16[576,512]{1,0:T(8,128)(2,1)}, u32[]{:S(2)}) copy-start(bf16[576,512]{1,0:T(8,128)(2,1)} %tok_ref.1) | copy-start | bytes 1769476
  77.0 15.0 %copy-start.4 = (bf16[576,512]{1,0:T(8,128)(2,1)S(1)}, bf16[576,512]{1,0:T(8,128)(2,1)}, u32[]{:S(2)}) copy-start(bf16[576,512]{1,0:T(8,128)(2,1)} %go_ref.1) | copy-start | bytes 1769476
  77.0 15.0 %copy-start.6 = (s32[1,576]{1,0:T(1,128)S(1)}, s32[1,576]{1,0:T(1,128)}, u32[]{:S(2)}) copy-start(s32[1,576]{1,0:T(1,128)} %get-tuple-element.31.target_ref) | copy-start | bytes 6916
  77.0 15.0 %copy-start.7 = (bf16[576]{0:T(1024)(128)(2,1)S(1)}, bf16[576]{0:T(1024)(128)(2,1)}, u32[]{:S(2)}) copy-start(bf16[576]{0:T(1024)(128)(2,1)} %gate_ref.1) | copy-start | bytes 3460
  77.0 15.0 %copy-start.8 = (f32[512]{0:T(512)S(1)}, f32[512]{0:T(512)}, u32[]{:S(2)}) copy-start(f32[512]{0:T(512)} %param.8) | copy-start | bytes 6148
  88.8 0.8 copy-start.13

commit v6 on v5

--- a/solution.py
+++ b/solution.py
@@ -51,10 +51,6 @@
     return copies
 
 
-def block_base(me, sources):
-    return jnp.bitwise_xor(me[0], sources - 2)
-
-
 def place_kernel(
     sources, capacity, me, place, ids_hbm, gate_hbm, tok_hbm, gain_hbm, go_hbm, target_ref, *refs
 ):
@@ -66,7 +62,7 @@
         [(ids_hbm, ids_ref), (tok_hbm, tok_ref), (gain_hbm, gain_ref), (gate_hbm, gate_ref), (go_hbm, go_ref)],
         in_sems,
     )
-    mine = block_base(me, sources)
+    mine = jnp.bitwise_xor(me[0], sources - 2)
     earlier = lax.broadcasted_iota(jnp.int32, (tok_rows, tok_rows), 0) < lax.broadcasted_iota(
         jnp.int32, (tok_rows, tok_rows), 1
     )
@@ -78,8 +74,8 @@
     before = dot(onehot.astype(BF16), earlier)
     rank = jnp.sum(before * onehot, axis=0, keepdims=True).astype(jnp.int32)
     kept = rank < capacity
-    target_ref[...] = jnp.where(kept, ids * capacity + rank, -1)
     target = jnp.where(kept, jnp.bitwise_xor(ids, mine) * capacity + rank, -1)
+    target_ref[...] = target
     hit = lax.broadcasted_iota(jnp.int32, (rows, tok_rows), 0) == target
     gate = gate_ref[...].astype(F32).reshape(1, tok_rows)
     scaled, _ = normalize(tok_ref[...])
@@ -180,20 +176,22 @@
     expert_work(order, blocks, w_in_ref, w_out_ref, gpre_ref, extra_ref, rows_ref, turned_ref, put)
 
 
-def back_kernel(sources, capacity, sets, me, w_in_ref, *refs):
-    out_ref = refs[-1]
+def back_kernel(capacity, sets, w_in_ref, *refs):
+    inputs, outs = refs[:4], refs[4:]
     width = w_in_ref.shape[0]
-    for members, gpre_ref, extra_ref in zip(sets, refs[0:-1:2], refs[1:-1:2]):
+    for members, gpre_ref, extra_ref in zip(sets, inputs[::2], inputs[1::2]):
         grad = dot(gpre_ref[...], w_in_ref[...], ((1,), (1,))).astype(BF16)
         for i, j in enumerate(members):
             block = slice(i * capacity, (i + 1) * capacity)
-            source = jnp.bitwise_xor(block_base(me, sources), j)
-            out_ref[source, :, :width] = grad[block]
-            out_ref[source, :, width:] = extra_ref[block, :]
-
-
-def finish_kernel(target_ref, gate_ref, tok_ref, gain_ref, go_ref, back_ref, tokens_out, gate_out):
-    rows = back_ref.shape[0]
+            outs[j][:, :width] = grad[block]
+            outs[j][:, width:] = extra_ref[block, :]
+
+
+def finish_kernel(target_ref, gate_ref, tok_ref, gain_ref, go_ref, *refs):
+    *blocks, tokens_out, gate_out, back_ref = refs
+    rows, capacity = back_ref.shape[0], blocks[0].shape[0]
+    for j, block in enumerate(blocks):
+        back_ref[j * capacity : (j + 1) * capacity, :] = block[...]
     tok_rows, width = tok_ref.shape
     spots = jnp.broadcast_to(target_ref[...].astype(F32), (8, tok_rows)).T[:, :1].astype(jnp.int32)
     hit = lax.broadcasted_iota(jnp.int32, (tok_rows, rows), 1) == spots
@@ -223,18 +221,14 @@
     return (place[0] == 1) | (place[0] == 2)
 
 
-def pass_kernel(place, third_ref, swapped_ref, own_ref, out_ref, sum_ref):
+def pass_kernel(place, third_ref, own_ref, swapped_ref, middle_ref, across_ref, out_ref, sum_ref):
     swapped = swapped_ref[...].astype(F32)
     onward = jnp.where(is_inner(place), swapped, 0.0)
     out_ref[...] = (third_ref[...].astype(F32) + onward).astype(BF16)
-    sum_ref[...] = own_ref[...].astype(F32) + (swapped - onward)
-
-
-def most_kernel(sum_ref, middle_ref, across_ref, outer_ref, out_ref):
-    total = sum_ref[...]
-    for ref in (middle_ref, across_ref, outer_ref):
+    total = own_ref[...].astype(F32) + (swapped - onward)
+    for ref in (middle_ref, across_ref):
         total += ref[...].astype(F32)
-    out_ref[...] = total
+    sum_ref[...] = total
 
 
 def total_kernel(sum_ref, last_ref, in_ref, out_ref):
@@ -246,27 +240,22 @@
     out_ref[half:, :] = total[piece_d:, width:]
 
 
-def line_sums(place, first, second, third, own, width, behind):
+def line_sums(place, first, second, third, own, width, ahead):
+    rows, hidden = own.shape
+    piece_d = width // LINE
     swapped = lax.ppermute(first, "dp", [(0, 1), (1, 0), (2, 3), (3, 2)])
     middle = lax.ppermute(second, "dp", [(1, 2), (2, 1)])
     across = lax.ppermute(second, "dp", [(0, 2), (3, 1)])
-    swapped, behind = lax.optimization_barrier((swapped, behind))
-    outer = lax.ppermute(third, "dp", [(0, 1), (3, 2)])
-    rows, hidden = own.shape
-    piece_d = width // LINE
-    whole = jax.ShapeDtypeStruct(own.shape, F32)
-    passed, some = kernel_call(
+    third, *ahead = lax.optimization_barrier((third, *ahead))
+    passed, most = kernel_call(
         pass_kernel,
         "pass",
         1,
         1,
-        [jax.ShapeDtypeStruct(own.shape, BF16), whole],
-        [smem] + [vmem] * 3,
-    )(place, third, swapped, own)
-    last = lax.ppermute(passed, "dp", [(1, 3), (2, 0)])
-    (most,) = kernel_call(
-        most_kernel, "most", 1, 1, [whole], [vmem] * 4, vmem_mib=56
-    )(some, middle, across, outer)
+        [jax.ShapeDtypeStruct(own.shape, BF16), jax.ShapeDtypeStruct(own.shape, F32)],
+        [smem] + [vmem] * 5,
+    )(place, third, own, swapped, middle, across)
+    last = lax.ppermute(passed, "dp", [(0, 1), (3, 2), (1, 3), (2, 0)])
     sums = kernel_call(
         total_kernel,
         "total",
@@ -277,9 +266,8 @@
             jax.ShapeDtypeStruct((2 * (rows - piece_d), width), F32),
         ],
         [vmem] * 2,
-        vmem_mib=56,
     )(most, last)
-    return *sums, behind
+    return *sums, ahead
 
 
 def body(tokens, gain, w_in, w_out, expert_ids, gate, grad_out):
@@ -352,17 +340,20 @@
     )
     piece = shape((width // LINE + hidden // LINE // 2, hidden), BF16)
     *parts, late_gpre, late_extra = work(later_kernel, "later", late_set, [piece] * LINE, *sums)
-    (returned,) = kernel_call(
-        functools.partial(back_kernel, sources, capacity, (soon_set, late_set)),
+    returned = kernel_call(
+        functools.partial(back_kernel, capacity, (soon_set, late_set)),
         "back",
         1,
         1,
-        [shape((sources, capacity, width + LANES), BF16)],
-        [smem] + [vmem] * 5,
-    )(me, weight_in, soon_gpre, soon_extra, late_gpre, late_extra)
-
+        [shape((capacity, width + LANES), BF16)] * sources,
+        [vmem] * 5,
+    )(weight_in, soon_gpre, soon_extra, late_gpre, late_extra)
+
+    back = swap_blocks(returned)
     if groups == LINE:
-        grad_w_in, grad_w_out, returned = line_sums(place, *parts, width, returned)
+        grad_w_in, grad_w_out, back[: sources // 2] = line_sums(
+            place, *parts, width, back[: sources // 2]
+        )
     else:
         parts_in, parts_out = zip(*[split_piece(part, width, LINE) for part in parts])
         grad_w_in, grad_w_out = (
@@ -371,15 +362,15 @@
             ).astype(F32)
             for part in (parts_in, parts_out)
         )
-    back = lax.all_to_all(returned, "space", split_axis=0, concat_axis=0, tiled=True)
     grad_tokens, grad_gate = kernel_call(
         finish_kernel,
         "finish",
         1,
         1,
         [shape((tok_rows, width), BF16), shape((tok_rows,), BF16)],
-        [vmem] * 6,
-    )(target, gate, tokens, gain_row, grad_out, back.reshape(rows, width + LANES))
+        [vmem] * (5 + sources),
+        [pltpu.VMEM((rows, width + LANES), BF16)],
+    )(target, gate, tokens, gain_row, grad_out, *back)
     return (grad_tokens, grad_gate, grad_w_in[None], grad_w_out[None])
 
 

time: 94.9 us -> 75.3 us (0.79)
  waiting for transfers between devices: 43.6 us -> 26.2 us
  starting transfers between devices: 25.2 us -> 31.1 us
  Pallas kernels: 21.1 us -> 16 us
  local copies, waits for them, and re-layouts: 3.84 us -> 0.96 us
    ppermute x2 -> x1, waiting for transfers between devices: 25.8 us -> 2.44 us  [line_sums(): last = lax.ppermute(passed, 'dp', [(0, 1), (3, 2), (1, 3), (2, 0)])]
    ppermute x7 -> x14, waiting for transfers between devices: 7.6 us -> 21.3 us  [swap_blocks(): lax.ppermute(blocks[j], 'space', [(i, i ^ j ^ count - 2) for i in range(c...]
    ppermute x1, waiting for transfers between devices: 10.2 us -> 0.01 us  [line_sums(): swapped = lax.ppermute(first, 'dp', [(0, 1), (1, 0), (2, 3), (3, 2)])]
    ppermute x7 -> x14, starting transfers between devices: 9.85 us -> 17.2 us  [swap_blocks(): lax.ppermute(blocks[j], 'space', [(i, i ^ j ^ count - 2) for i in range(c...]
    pallas_call x2 -> x1, Pallas kernels: 4.93 us -> 1.02 us  [body(): kernel_call(functools.partial(back_kernel, capacity, (soon_set, late_set)...]
    all_to_all x1 -> x0, starting transfers between devices: 3.9 us -> none  [body(): lax.all_to_all(returned, 'space', split_axis=0, concat_axis=0, tiled=True)]
    unnamed x28 -> x16, local copies, waits for them, and re-layouts: 3.84 us -> 0.96 us
    ppermute x1, waiting for transfers between devices: 0.01 us -> 2.48 us  [line_sums(): across = lax.ppermute(second, 'dp', [(0, 2), (3, 1)])]
  transfers between devices with their start and end apart: 13 -> 18, of which waited for: 7 -> 12; matrix products, arithmetic and copies ran while one was open for 0% -> 0% of each run, Pallas kernels for 11% -> 9%
where the time goes in v6:
time: 75.3 us; the launch traced here: 75.1 us
  starting transfers between devices  31.1 us (41%)
  waiting for transfers between devices  26.2 us (35%)
  Pallas kernels  16 us (21%)
  local copies, waits for them, and re-layouts  0.96 us (1%)
  between operations  0.79 us (1%)
    ppermute x14, waiting for transfers between devices, swap_blocks(): lax.ppermute(blocks[j], 'space', [(i, i ^ j ^ count - 2) for i in range(c...  21.3 us
    ppermute x14, starting transfers between devices, swap_blocks(): lax.ppermute(blocks[j], 'space', [(i, i ^ j ^ count - 2) for i in range(c...  17.2 us
    ppermute x1, starting transfers between devices, line_sums(): last = lax.ppermute(passed, 'dp', [(0, 1), (3, 2), (1, 3), (2, 0)])  6.8 us
    pallas_call x2, Pallas kernels, work(): kernel_call(functools.partial(kernel, count, groups), name, 8 * span * wi...  6.14 us
    pallas_call x1, Pallas kernels, body(): kernel_call(functools.partial(place_kernel, sources, capacity), 'place',...  4.75 us
    ppermute x1, starting transfers between devices, line_sums(): across = lax.ppermute(second, 'dp', [(0, 2), (3, 1)])  4.51 us
    pallas_call x1, Pallas kernels, body(): kernel_call(finish_kernel, 'finish', 1, 1, [shape((tok_rows, width), BF16...  2.61 us
    ppermute x1, waiting for transfers between devices, line_sums(): across = lax.ppermute(second, 'dp', [(0, 2), (3, 1)])  2.48 us
  transfers between devices with their start and end apart: 18, of which 12 were waited for; matrix products, arithmetic and copies ran while one was open for 0% of the time, Pallas kernels for 9%

profile of v6, /device:TPU:0, one launch (start us, length us, event | category | flops | bytes accessed | tf_op | source)
XLA Modules:
  0.0 75.1 jit_solution(4799058994647632327)
XLA Ops:
  0.7 4.7 %place.1 = (s32[1,576]{1,0:T(1,128)}, bf16[96,1024]{1,0:T(8,128)(2,1)}, bf16[96,1024]{1,0:T(8,128)(2,1)}, bf16[96,1024]{1,0:T(8,128)(2,1)}, bf16[96,1024]{1,0:T(...) custom-call(s32[1]{0:T(128)} %bitcast.me, ...), custom_call_target="tpu_custom_call" | custom-call | flops 905969664 | bytes 2752512 | tf_op jit(solution)/shard_map/place/pallas_call | solution.py:290
  5.4 3.9 %collective-permute-start = (bf16[96,1024]{1,0:T(8,128)(2,1)}, bf16[96,1024]{1,0:T(8,128)(2,1)S(1)}, u32[]{:S(2)}, u32[]{:S(2)}) collective-permute-start(bf16[96,1024]{1,0:T(8,128)(2,1)} %get-tuple-element.43), channel_id=1, source_target_pairs={{0,24},{4,28},{8,16},{12,20},{16,8},{20,12},{24,0},{28,4},{1,25},{... | collective-permute-start | bytes 589832 | tf_op jit(solution)/shard_map/ppermute | solution.py:215
  9.4 1.2 %collective-permute-start.2 = (bf16[96,1024]{1,0:T(8,128)(2,1)}, bf16[96,1024]{1,0:T(8,128)(2,1)S(1)}, u32[]{:S(2)}, u32[]{:S(2)}) collective-permute-start(bf16[96,1024]{1,0:T(8,128)(2,1)} %get-tuple-element.45), channel_id=1, source_target_pairs={{0,16},{4,20},{8,24},{12,28},{16,0},{20,4},{24,8},{28,12},{1,17},{... | collective-permute-start | bytes 589832 | tf_op jit(solution)/shard_map/ppermute | solution.py:215
  10.5 0.7 collective-permute-start.3
  11.5 3.9 %collective-permute-done.refs_0_ = bf16[96,1024]{1,0:T(8,128)(2,1)S(1)} collective-permute-done((bf16[96,1024]{1,0:T(8,128)(2,1)}, bf16[96,1024]{1,0:T(8,128)(2,1)S(1)}, u32[]{:S(2)}, u32[]{:S(2)}) %collective-permute-start) | collective-permute-done | bytes 196640 | tf_op jit(solution)/shard_map/ppermute | solution.py:215
  15.4 2.0 %collective-permute-start.5 = (bf16[96,1024]{1,0:T(8,128)(2,1)}, bf16[96,1024]{1,0:T(8,128)(2,1)S(1)}, u32[]{:S(2)}, u32[]{:S(2)}) collective-permute-start(bf16[96,1024]{1,0:T(8,128)(2,1)} %get-tuple-element.51), channel_id=1, source_target_pairs={{0,8},{4,12},{8,0},{12,4},{16,24},{20,28},{24,16},{28,20},{1,9},{5... | collective-permute-start | bytes 589832 | tf_op jit(solution)/shard_map/ppermute | solution.py:215
  17.4 1.8 %collective-permute-done.1.refs_1_ = bf16[96,1024]{1,0:T(8,128)(2,1)S(1)} collective-permute-done((bf16[96,1024]{1,0:T(8,128)(2,1)}, bf16[96,1024]{1,0:T(8,128)(2,1)S(1)}, u32[]{:S(2)}, u32[]{:S(2)}) %collective-permute-start.1) | collective-permute-done | bytes 196640 | tf_op jit(solution)/shard_map/ppermute | solution.py:215
  19.2 1.7 %collective-permute-start.6 = (bf16[96,1024]{1,0:T(8,128)(2,1)}, bf16[96,1024]{1,0:T(8,128)(2,1)S(1)}, u32[]{:S(2)}, u32[]{:S(2)}) collective-permute-start(bf16[96,1024]{1,0:T(8,128)(2,1)} %get-tuple-element.52), channel_id=1, source_target_pairs={{0,12},{4,8},{8,4},{12,0},{16,28},{20,24},{24,20},{28,16},{1,13},{... | collective-permute-start | bytes 589832 | tf_op jit(solution)/shard_map/ppermute | solution.py:215
  21.0 0.9 %copy-done.4 = bf16[96,1024]{1,0:T(8,128)(2,1)S(1)} copy-done((bf16[96,1024]{1,0:T(8,128)(2,1)S(1)}, bf16[96,1024]{1,0:T(8,128)(2,1)}, u32[]{:S(2)}) %copy-start.4) | copy-done | bytes 196632
  21.9 1.0 %collective-permute-done.2.refs_2_ = bf16[96,1024]{1,0:T(8,128)(2,1)S(1)} collective-permute-done((bf16[96,1024]{1,0:T(8,128)(2,1)}, bf16[96,1024]{1,0:T(8,128)(2,1)S(1)}, u32[]{:S(2)}, u32[]{:S(2)}) %collective-permute-start.2) | collective-permute-done | bytes 196640 | tf_op jit(solution)/shard_map/ppermute | solution.py:215
  23.0 3.2 %sooner.1 = (f32[512,1024]{1,0:T(8,128)S(1)}, f32[1024,512]{1,0:T(8,128)S(1)}, bf16[480,1024]{1,0:T(8,128)(2,1)S(1)}, bf16[480,128]{1,0:T(8,128)(2,1)S(1)}) custom-call(s32[1]{0:T(128)} %bitcast.1.place, bf16[512,1024]{1,0:T(8,128)(2,1)S(1)} %bitcast.8, bf16[1024,512]{1,0:T(8,128)(2,1)S(1)} %bitcast.11, bf16[96,1024]{1,0:T(8,128)(2,1)S(1)} %collective-permute-done.refs_0_, ...), custom_call_target="tpu_custom_call" | custom-call | flops 2013265920 | bytes 6160384 | tf_op jit(solution)/shard_map/sooner/pallas_call | solution.py:328
  26.2 0.9 %collective-permute-done.4.refs_0_ = bf16[96,1024]{1,0:T(8,128)(2,1)S(1)} collective-permute-done((bf16[96,1024]{1,0:T(8,128)(2,1)}, bf16[96,1024]{1,0:T(8,128)(2,1)S(1)}, u32[]{:S(2)}, u32[]{:S(2)}) %collective-permute-start.4) | collective-permute-done | bytes 196640 | tf_op jit(solution)/shard_map/ppermute | solution.py:215
  27.1 2.9 %later.1 = (bf16[256,1024]{1,0:T(8,128)(2,1)S(1)}, bf16[256,1024]{1,0:T(8,128)(2,1)S(1)}, bf16[256,1024]{1,0:T(8,128)(2,1)S(1)}, bf16[256,1024]{1,0:T(8,128)(2,1...) custom-call(s32[1]{0:T(128)} %bitcast.1.place, bf16[512,1024]{1,0:T(8,128)(2,1)S(1)} %bitcast.9, ...), custom_call_target="tpu_custom_call" | custom-call | flops 1207959552 | bytes 5373952 | tf_op jit(solution)/shard_map/later/pallas_call | solution.py:328
  30.0 1.8 %collective-permute-start.14 = (bf16[256,1024]{1,0:T(8,128)(2,1)S(1)}, bf16[256,1024]{1,0:T(8,128)(2,1)S(1)}, u32[]{:S(2)}, u32[]{:S(2)}) collective-permute-start(bf16[256,1024]{1,0:T(8,128)(2,1)S(1)} %get-tuple-element.74), channel_id=1, source_target_pairs={{0,1},{1,0},{2,3},{3,2},{4,5},{5,4},{6,7},{7,6},{8,9},{9,8},{10,11... | collective-permute-start | bytes 1572872 | tf_op jit(solution)/shard_map/ppermute | solution.py:246
  31.8 4.5 %collective-permute-start.16 = (bf16[256,1024]{1,0:T(8,128)(2,1)S(1)}, bf16[256,1024]{1,0:T(8,128)(2,1)S(1)}, u32[]{:S(2)}, u32[]{:S(2)}) collective-permute-start(bf16[256,1024]{1,0:T(8,128)(2,1)S(1)} %get-tuple-element.75), channel_id=1, source_target_pairs={{0,2},{3,1},{4,6},{7,5},{8,10},{11,9},{12,14},{15,13},{16,18},{19,... | collective-permute-start | bytes 1572872 | tf_op jit(solution)/shard_map/ppermute | solution.py:248
  36.3 0.7 collective-permute-start.15
  37.1 1.0 %back.1 = (bf16[96,640]{1,0:T(8,128)(2,1)S(1)}, bf16[96,640]{1,0:T(8,128)(2,1)S(1)}, bf16[96,640]{1,0:T(8,128)(2,1)S(1)}, bf16[96,640]{1,0:T(8,128)(2,1)S(1)}, b...) custom-call(bf16[512,1024]{1,0:T(8,128)(2,1)S(1)} %bitcast.10, ...), custom_call_target="tpu_custom_call" | custom-call | flops 1 | bytes 1 | tf_op jit(solution)/shard_map/back/pallas_call | solution.py:343
  38.1 2.6 %collective-permute-start.7 = (bf16[96,640]{1,0:T(8,128)(2,1)S(1)}, bf16[96,640]{1,0:T(8,128)(2,1)S(1)}, u32[]{:S(2)}, u32[]{:S(2)}) collective-permute-start(bf16[96,640]{1,0:T(8,128)(2,1)S(1)} %get-tuple-element.58), channel_id=1, source_target_pairs={{0,24},{4,28},{8,16},{12,20},{16,8},{20,12},{24,0},{28,4},{1,25},{... | collective-permute-start | bytes 368648 | tf_op jit(solution)/shard_map/ppermute | solution.py:215
  40.7 3.6 %collective-permute-done.7.refs_0_ = bf16[96,640]{1,0:T(8,128)(2,1)S(1)} collective-permute-done((bf16[96,640]{1,0:T(8,128)(2,1)S(1)}, bf16[96,640]{1,0:T(8,128)(2,1)S(1)}, u32[]{:S(2)}, u32[]{:S(2)}) %collective-permute-start.7) | collective-permute-done | bytes 122912 | tf_op jit(solution)/shard_map/ppermute | solution.py:215
  44.3 1.7 %collective-permute-start.9 = (bf16[96,640]{1,0:T(8,128)(2,1)S(1)}, bf16[96,640]{1,0:T(8,128)(2,1)S(1)}, u32[]{:S(2)}, u32[]{:S(2)}) collective-permute-start(bf16[96,640]{1,0:T(8,128)(2,1)S(1)} %get-tuple-element.60), channel_id=1, source_target_pairs={{0,16},{4,20},{8,24},{12,28},{16,0},{20,4},{24,8},{28,12},{1,17},{... | collective-permute-start | bytes 368648 | tf_op jit(solution)/shard_map/ppermute | solution.py:215
  46.0 0.7 collective-permute-done.8.refs_1_
  46.8 0.9 %collective-permute-start.10 = (bf16[96,640]{1,0:T(8,128)(2,1)S(1)}, bf16[96,640]{1,0:T(8,128)(2,1)S(1)}, u32[]{:S(2)}, u32[]{:S(2)}) collective-permute-start(bf16[96,640]{1,0:T(8,128)(2,1)S(1)} %get-tuple-element.61), channel_id=1, source_target_pairs={{0,20},{4,16},{8,28},{12,24},{16,4},{20,0},{24,12},{28,8},{1,21},{... | collective-permute-start | bytes 368648 | tf_op jit(solution)/shard_map/ppermute | solution.py:215
  47.7 1.6 %collective-permute-done.9.refs_2_ = bf16[96,640]{1,0:T(8,128)(2,1)S(1)} collective-permute-done((bf16[96,640]{1,0:T(8,128)(2,1)S(1)}, bf16[96,640]{1,0:T(8,128)(2,1)S(1)}, u32[]{:S(2)}, u32[]{:S(2)}) %collective-permute-start.9) | collective-permute-done | bytes 122912 | tf_op jit(solution)/shard_map/ppermute | solution.py:215
  49.3 2.8 %collective-permute-done.10.refs_3_ = bf16[96,640]{1,0:T(8,128)(2,1)S(1)} collective-permute-done((bf16[96,640]{1,0:T(8,128)(2,1)S(1)}, bf16[96,640]{1,0:T(8,128)(2,1)S(1)}, u32[]{:S(2)}, u32[]{:S(2)}) %collective-permute-start.10) | collective-permute-done | bytes 122912 | tf_op jit(solution)/shard_map/ppermute | solution.py:215
  52.1 2.5 %collective-permute-done.16.across_ref = bf16[256,1024]{1,0:T(8,128)(2,1)S(1)} collective-permute-done((bf16[256,1024]{1,0:T(8,128)(2,1)S(1)}, bf16[256,1024]{1,0:T(8,128)(2,1)S(1)}, u32[]{:S(2)}, u32[]{:S(2)}) %collective-permute-start.16) | collective-permute-done | bytes 524320 | tf_op jit(solution)/shard_map/ppermute | solution.py:248
  55.0 6.8 %collective-permute-start.17 = (bf16[256,1024]{1,0:T(8,128)(2,1)S(1)}, bf16[256,1024]{1,0:T(8,128)(2,1)S(1)}, u32[]{:S(2)}, u32[]{:S(2)}) collective-permute-start(bf16[256,1024]{1,0:T(8,128)(2,1)S(1)} %get-tuple-element.77), channel_id=1, source_target_pairs={{0,1},{3,2},{1,3},{2,0},{4,5},{7,6},{5,7},{6,4},{8,9},{11,10},{9,1... | collective-permute-start | bytes 1572872 | tf_op jit(solution)/shard_map/ppermute | solution.py:258
  61.8 1.5 %collective-permute-start.11 = (bf16[96,640]{1,0:T(8,128)(2,1)S(1)}, bf16[96,640]{1,0:T(8,128)(2,1)S(1)}, u32[]{:S(2)}, u32[]{:S(2)}) collective-permute-start(bf16[96,640]{1,0:T(8,128)(2,1)S(1)} %get-tuple-element.66), channel_id=1, source_target_pairs={{0,8},{4,12},{8,0},{12,4},{16,24},{20,28},{24,16},{28,20},{1,9},{5... | collective-permute-start | bytes 368648 | tf_op jit(solution)/shard_map/ppermute | solution.py:215
  63.9 3.1 %collective-permute-done.11.refs_4_ = bf16[96,640]{1,0:T(8,128)(2,1)S(1)} collective-permute-done((bf16[96,640]{1,0:T(8,128)(2,1)S(1)}, bf16[96,640]{1,0:T(8,128)(2,1)S(1)}, u32[]{:S(2)}, u32[]{:S(2)}) %collective-permute-start.11) | collective-permute-done | bytes 122912 | tf_op jit(solution)/shard_map/ppermute | solution.py:215
  67.1 1.9 %collective-permute-done.12.refs_5_ = bf16[96,640]{1,0:T(8,128)(2,1)S(1)} collective-permute-done((bf16[96,640]{1,0:T(8,128)(2,1)S(1)}, bf16[96,640]{1,0:T(8,128)(2,1)S(1)}, u32[]{:S(2)}, u32[]{:S(2)}) %collective-permute-start.12) | collective-permute-done | bytes 122912 | tf_op jit(solution)/shard_map/ppermute | solution.py:215
  69.0 2.6 %finish.1 = (bf16[576,512]{1,0:T(8,128)(2,1)}, bf16[576]{0:T(1024)(128)(2,1)}) custom-call(s32[1,576]{1,0:T(1,128)S(1)} %copy-done.5, bf16[576]{0:T(1024)(128)(2,1)S(1)} %copy-done.6, bf16[576,512]{1,0:T(8,128)(2,1)S(1)} %copy-done.2, f32[1,512]{1,0:T(1,128)S(1)} %bitcast.14, bf16[576,512]{1,0:T(8,128)(2,1)S(1)} %copy-done.3, ...), custom_call_target="tpu_custom_call" | custom-call | flops 1 | bytes 1 | tf_op jit(solution)/shard_map/finish/pallas_call | solution.py:365
  71.6 2.4 %collective-permute-done.17.last_ref = bf16[256,1024]{1,0:T(8,128)(2,1)S(1)} collective-permute-done((bf16[256,1024]{1,0:T(8,128)(2,1)S(1)}, bf16[256,1024]{1,0:T(8,128)(2,1)S(1)}, u32[]{:S(2)}, u32[]{:S(2)}) %collective-permute-start.17) | collective-permute-done | bytes 524320 | tf_op jit(solution)/shard_map/ppermute | solution.py:258
  74.0 1.1 %total.1 = (f32[128,1024]{1,0:T(8,128)}, f32[256,512]{1,0:T(8,128)}) custom-call(f32[256,1024]{1,0:T(8,128)S(1)} %get-tuple-element.76.sum_ref, bf16[256,1024]{1,0:T(8,128)(2,1)S(1)} %collective-permute-done.17.last_ref), custom_call_target="tpu_custom_call" | custom-call | flops 1 | bytes 1 | tf_op jit(solution)/shard_map/total/pallas_call | solution.py:259
  (28 shorter events, 1.4 us)
Async XLA Ops:
  0.6 22.3 %copy-start.1 = (bf16[1,1024,512]{2,1,0:T(8,128)(2,1)S(1)}, bf16[1,1024,512]{2,1,0:T(8,128)(2,1)}, u32[]{:S(2)}) copy-start(bf16[1,1024,512]{2,1,0:T(8,128)(2,1)} %param.10) | copy-start | bytes 3145732
  0.6 22.3 %copy-start = (bf16[1,512,1024]{2,1,0:T(8,128)(2,1)S(1)}, bf16[1,512,1024]{2,1,0:T(8,128)(2,1)}, u32[]{:S(2)}) copy-start(bf16[1,512,1024]{2,1,0:T(8,128)(2,1)} %param.9) | copy-start | bytes 3145732
  5.4 10.0 %collective-permute-start = (bf16[96,1024]{1,0:T(8,128)(2,1)}, bf16[96,1024]{1,0:T(8,128)(2,1)S(1)}, u32[]{:S(2)}, u32[]{:S(2)}) collective-permute-start(bf16[96,1024]{1,0:T(8,128)(2,1)} %get-tuple-element.43), channel_id=1, source_target_pairs={{0,24},{4,28},{8,16},{12,20},{16,8},{20,12},{24,0},{28,4},{1,25},{... | collective-permute-start | bytes 589832 | tf_op jit(solution)/shard_map/ppermute | solution.py:215
  9.4 9.9 %collective-permute-start.1 = (bf16[96,1024]{1,0:T(8,128)(2,1)}, bf16[96,1024]{1,0:T(8,128)(2,1)S(1)}, u32[]{:S(2)}, u32[]{:S(2)}) collective-permute-start(bf16[96,1024]{1,0:T(8,128)(2,1)} %get-tuple-element.44), channel_id=1, source_target_pairs={{0,28},{4,24},{8,20},{12,16},{16,12},{20,8},{24,4},{28,0},{1,29},{... | collective-permute-start | bytes 589832 | tf_op jit(solution)/shard_map/ppermute | solution.py:215
  9.4 13.6 %collective-permute-start.2 = (bf16[96,1024]{1,0:T(8,128)(2,1)}, bf16[96,1024]{1,0:T(8,128)(2,1)S(1)}, u32[]{:S(2)}, u32[]{:S(2)}) collective-permute-start(bf16[96,1024]{1,0:T(8,128)(2,1)} %get-tuple-element.45), channel_id=1, source_target_pairs={{0,16},{4,20},{8,24},{12,28},{16,0},{20,4},{24,8},{28,12},{1,17},{... | collective-permute-start | bytes 589832 | tf_op jit(solution)/shard_map/ppermute | solution.py:215
  10.5 12.4 %collective-permute-start.3 = (bf16[96,1024]{1,0:T(8,128)(2,1)}, bf16[96,1024]{1,0:T(8,128)(2,1)S(1)}, u32[]{:S(2)}, u32[]{:S(2)}) collective-permute-start(bf16[96,1024]{1,0:T(8,128)(2,1)} %get-tuple-element.47), channel_id=1, source_target_pairs={{0,4},{4,0},{8,12},{12,8},{16,20},{20,16},{24,28},{28,24},{1,5},{5... | collective-permute-start | bytes 589832 | tf_op jit(solution)/shard_map/ppermute | solution.py:215
  11.2 15.9 %collective-permute-start.4 = (bf16[96,1024]{1,0:T(8,128)(2,1)}, bf16[96,1024]{1,0:T(8,128)(2,1)S(1)}, u32[]{:S(2)}, u32[]{:S(2)}) collective-permute-start(bf16[96,1024]{1,0:T(8,128)(2,1)} %get-tuple-element.50), channel_id=1, source_target_pairs={{0,20},{4,16},{8,28},{12,24},{16,4},{20,0},{24,12},{28,8},{1,21},{... | collective-permute-start | bytes 589832 | tf_op jit(solution)/shard_map/ppermute | solution.py:215
  15.4 11.7 %collective-permute-start.5 = (bf16[96,1024]{1,0:T(8,128)(2,1)}, bf16[96,1024]{1,0:T(8,128)(2,1)S(1)}, u32[]{:S(2)}, u32[]{:S(2)}) collective-permute-start(bf16[96,1024]{1,0:T(8,128)(2,1)} %get-tuple-element.51), channel_id=1, source_target_pairs={{0,8},{4,12},{8,0},{12,4},{16,24},{20,28},{24,16},{28,20},{1,9},{5... | collective-permute-start | bytes 589832 | tf_op jit(solution)/shard_map/ppermute | solution.py:215
  19.2 7.8 %collective-permute-start.6 = (bf16[96,1024]{1,0:T(8,128)(2,1)}, bf16[96,1024]{1,0:T(8,128)(2,1)S(1)}, u32[]{:S(2)}, u32[]{:S(2)}) collective-permute-start(bf16[96,1024]{1,0:T(8,128)(2,1)} %get-tuple-element.52), channel_id=1, source_target_pairs={{0,12},{4,8},{8,4},{12,0},{16,28},{20,24},{24,20},{28,16},{1,13},{... | collective-permute-start | bytes 589832 | tf_op jit(solution)/shard_map/ppermute | solution.py:215
  21.0 0.9 %copy-start.4 = (bf16[96,1024]{1,0:T(8,128)(2,1)S(1)}, bf16[96,1024]{1,0:T(8,128)(2,1)}, u32[]{:S(2)}) copy-start(bf16[96,1024]{1,0:T(8,128)(2,1)} %get-tuple-element.46.block_ref) | copy-start | bytes 589828
  30.0 22.1 %collective-permute-start.14 = (bf16[256,1024]{1,0:T(8,128)(2,1)S(1)}, bf16[256,1024]{1,0:T(8,128)(2,1)S(1)}, u32[]{:S(2)}, u32[]{:S(2)}) collective-permute-start(bf16[256,1024]{1,0:T(8,128)(2,1)S(1)} %get-tuple-element.74), channel_id=1, source_target_pairs={{0,1},{1,0},{2,3},{3,2},{4,5},{5,4},{6,7},{7,6},{8,9},{9,8},{10,11... | collective-permute-start | bytes 1572872 | tf_op jit(solution)/shard_map/ppermute | solution.py:246
  31.8 22.7 %collective-permute-start.16 = (bf16[256,1024]{1,0:T(8,128)(2,1)S(1)}, bf16[256,1024]{1,0:T(8,128)(2,1)S(1)}, u32[]{:S(2)}, u32[]{:S(2)}) collective-permute-start(bf16[256,1024]{1,0:T(8,128)(2,1)S(1)} %get-tuple-element.75), channel_id=1, source_target_pairs={{0,2},{3,1},{4,6},{7,5},{8,10},{11,9},{12,14},{15,13},{16,18},{19,... | collective-permute-start | bytes 1572872 | tf_op jit(solution)/shard_map/ppermute | solution.py:248
  36.3 18.2 %collective-permute-start.15 = (bf16[256,1024]{1,0:T(8,128)(2,1)S(1)}, bf16[256,1024]{1,0:T(8,128)(2,1)S(1)}, u32[]{:S(2)}, u32[]{:S(2)}) collective-permute-start(bf16[256,1024]{1,0:T(8,128)(2,1)S(1)} %get-tuple-element.75), channel_id=1, source_target_pairs={{1,2},{2,1},{5,6},{6,5},{9,10},{10,9},{13,14},{14,13},{17,18},{18,... | collective-permute-start | bytes 1572872 | tf_op jit(solution)/shard_map/ppermute | solution.py:247
  37.0 31.9 %copy-start.2 = (bf16[576,512]{1,0:T(8,128)(2,1)S(1)}, bf16[576,512]{1,0:T(8,128)(2,1)}, u32[]{:S(2)}) copy-start(bf16[576,512]{1,0:T(8,128)(2,1)} %tok_ref.1) | copy-start | bytes 1769476
  37.1 31.9 %copy-start.3 = (bf16[576,512]{1,0:T(8,128)(2,1)S(1)}, bf16[576,512]{1,0:T(8,128)(2,1)}, u32[]{:S(2)}) copy-start(bf16[576,512]{1,0:T(8,128)(2,1)} %go_ref.1) | copy-start | bytes 1769476
  37.1 31.9 %copy-start.5 = (s32[1,576]{1,0:T(1,128)S(1)}, s32[1,576]{1,0:T(1,128)}, u32[]{:S(2)}) copy-start(s32[1,576]{1,0:T(1,128)} %get-tuple-element.42.target_ref) | copy-start | bytes 6916
  37.1 31.9 %copy-start.6 = (bf16[576]{0:T(1024)(128)(2,1)S(1)}, bf16[576]{0:T(1024)(128)(2,1)}, u32[]{:S(2)}) copy-start(bf16[576]{0:T(1024)(128)(2,1)} %gate_ref.1) | copy-start | bytes 3460
  37.1 31.9 %copy-start.7 = (f32[512]{0:T(512)S(1)}, f32[512]{0:T(512)}, u32[]{:S(2)}) copy-start(f32[512]{0:T(512)} %param.8) | copy-start | bytes 6148
  38.1 6.2 %collective-permute-start.7 = (bf16[96,640]{1,0:T(8,128)(2,1)S(1)}, bf16[96,640]{1,0:T(8,128)(2,1)S(1)}, u32[]{:S(2)}, u32[]{:S(2)}) collective-permute-start(bf16[96,640]{1,0:T(8,128)(2,1)S(1)} %get-tuple-element.58), channel_id=1, source_target_pairs={{0,24},{4,28},{8,16},{12,20},{16,8},{20,12},{24,0},{28,4},{1,25},{... | collective-permute-start | bytes 368648 | tf_op jit(solution)/shard_map/ppermute | solution.py:215
  40.7 6.1 %collective-permute-start.8 = (bf16[96,640]{1,0:T(8,128)(2,1)S(1)}, bf16[96,640]{1,0:T(8,128)(2,1)S(1)}, u32[]{:S(2)}, u32[]{:S(2)}) collective-permute-start(bf16[96,640]{1,0:T(8,128)(2,1)S(1)} %get-tuple-element.59), channel_id=1, source_target_pairs={{0,28},{4,24},{8,20},{12,16},{16,12},{20,8},{24,4},{28,0},{1,29},{... | collective-permute-start | bytes 368648 | tf_op jit(solution)/shard_map/ppermute | solution.py:215
  44.3 5.0 %collective-permute-start.9 = (bf16[96,640]{1,0:T(8,128)(2,1)S(1)}, bf16[96,640]{1,0:T(8,128)(2,1)S(1)}, u32[]{:S(2)}, u32[]{:S(2)}) collective-permute-start(bf16[96,640]{1,0:T(8,128)(2,1)S(1)} %get-tuple-element.60), channel_id=1, source_target_pairs={{0,16},{4,20},{8,24},{12,28},{16,0},{20,4},{24,8},{28,12},{1,17},{... | collective-permute-start | bytes 368648 | tf_op jit(solution)/shard_map/ppermute | solution.py:215
  46.8 5.3 %collective-permute-start.10 = (bf16[96,640]{1,0:T(8,128)(2,1)S(1)}, bf16[96,640]{1,0:T(8,128)(2,1)S(1)}, u32[]{:S(2)}, u32[]{:S(2)}) collective-permute-start(bf16[96,640]{1,0:T(8,128)(2,1)S(1)} %get-tuple-element.61), channel_id=1, source_target_pairs={{0,20},{4,16},{8,28},{12,24},{16,4},{20,0},{24,12},{28,8},{1,21},{... | collective-permute-start | bytes 368648 | tf_op jit(solution)/shard_map/ppermute | solution.py:215
  55.0 19.0 %collective-permute-start.17 = (bf16[256,1024]{1,0:T(8,128)(2,1)S(1)}, bf16[256,1024]{1,0:T(8,128)(2,1)S(1)}, u32[]{:S(2)}, u32[]{:S(2)}) collective-permute-start(bf16[256,1024]{1,0:T(8,128)(2,1)S(1)} %get-tuple-element.77), channel_id=1, source_target_pairs={{0,1},{3,2},{1,3},{2,0},{4,5},{7,6},{5,7},{6,4},{8,9},{11,10},{9,1... | collective-permute-start | bytes 1572872 | tf_op jit(solution)/shard_map/ppermute | solution.py:258
  61.8 5.3 %collective-permute-start.11 = (bf16[96,640]{1,0:T(8,128)(2,1)S(1)}, bf16[96,640]{1,0:T(8,128)(2,1)S(1)}, u32[]{:S(2)}, u32[]{:S(2)}) collective-permute-start(bf16[96,640]{1,0:T(8,128)(2,1)S(1)} %get-tuple-element.66), channel_id=1, source_target_pairs={{0,8},{4,12},{8,0},{12,4},{16,24},{20,28},{24,16},{28,20},{1,9},{5... | collective-permute-start | bytes 368648 | tf_op jit(solution)/shard_map/ppermute | solution.py:215
  63.3 5.6 %collective-permute-start.12 = (bf16[96,640]{1,0:T(8,128)(2,1)S(1)}, bf16[96,640]{1,0:T(8,128)(2,1)S(1)}, u32[]{:S(2)}, u32[]{:S(2)}) collective-permute-start(bf16[96,640]{1,0:T(8,128)(2,1)S(1)} %get-tuple-element.67), channel_id=1, source_target_pairs={{0,12},{4,8},{8,4},{12,0},{16,28},{20,24},{24,20},{28,16},{1,13},{... | collective-permute-start | bytes 368648 | tf_op jit(solution)/shard_map/ppermute | solution.py:215
  63.3 5.6 %collective-permute-start.13 = (bf16[96,640]{1,0:T(8,128)(2,1)S(1)}, bf16[96,640]{1,0:T(8,128)(2,1)S(1)}, u32[]{:S(2)}, u32[]{:S(2)}) collective-permute-start(bf16[96,640]{1,0:T(8,128)(2,1)S(1)} %get-tuple-element.69), channel_id=1, source_target_pairs={{0,4},{4,0},{8,12},{12,8},{16,20},{20,16},{24,28},{28,24},{1,5},{5... | collective-permute-start | bytes 368648 | tf_op jit(solution)/shard_map/ppermute | solution.py:215

commit v7 on v6

--- a/solution.py
+++ b/solution.py
@@ -55,27 +55,40 @@
     sources, capacity, me, place, ids_hbm, gate_hbm, tok_hbm, gain_hbm, go_hbm, target_ref, *refs
 ):
     outs = refs[:sources]
-    ids_ref, gate_ref, tok_ref, gain_ref, go_ref, sent_ref, in_sems, out_sems = refs[sources:]
+    wide_ref, ids_ref, gate_ref, tok_ref, gain_ref, go_ref, sent_ref, in_sems, out_sems = refs[sources:]
     rows = sources * capacity
     tok_rows, width = tok_ref.shape
     loads = start_copies(
         [(ids_hbm, ids_ref), (tok_hbm, tok_ref), (gain_hbm, gain_ref), (gate_hbm, gate_ref), (go_hbm, go_ref)],
         in_sems,
     )
-    mine = jnp.bitwise_xor(me[0], sources - 2)
-    earlier = lax.broadcasted_iota(jnp.int32, (tok_rows, tok_rows), 0) < lax.broadcasted_iota(
-        jnp.int32, (tok_rows, tok_rows), 1
+    earlier = lax.broadcasted_iota(jnp.int32, (LANES, LANES), 0) < lax.broadcasted_iota(
+        jnp.int32, (LANES, LANES), 1
     )
     earlier = jnp.where(earlier, 1.0, 0.0).astype(BF16)
-    for copy in loads:
+    loads[0].wait()
+    chunks = range(0, tok_rows, LANES)
+    wide_ref[...] = jnp.full_like(wide_ref, -1)
+    wide_ref[:, :tok_rows] = ids_ref[...]
+    ids = [wide_ref[:, c : c + LANES] for c in chunks]
+    expert = lax.broadcasted_iota(jnp.int32, (sources, LANES), 0)
+    onehots = [jnp.where(expert == chunk, 1.0, 0.0) for chunk in ids]
+    within = dot(jnp.concatenate(onehots).astype(BF16), earlier)
+    base = jnp.zeros((sources, 1), F32)
+    for i, (c, chunk, onehot) in enumerate(zip(chunks, ids, onehots)):
+        before = within[i * sources : (i + 1) * sources] + base
+        base += jnp.sum(onehot, axis=1, keepdims=True)
+        rank = jnp.sum(before * onehot, axis=0, keepdims=True).astype(jnp.int32)
+        away = jnp.bitwise_xor(chunk, me[0])
+        block = jnp.zeros_like(away)
+        for j, k in enumerate(block_order(sources)):
+            block = jnp.where(away == k, j, block)
+        end = min(LANES, tok_rows - c)
+        target = jnp.where(rank < capacity, block * capacity + rank, -1)
+        target_ref[:, c : c + end] = target[:, :end]
+    target = target_ref[...]
+    for copy in loads[1:]:
         copy.wait()
-    ids = ids_ref[...]
-    onehot = (lax.broadcasted_iota(jnp.int32, (sources, tok_rows), 0) == ids).astype(F32)
-    before = dot(onehot.astype(BF16), earlier)
-    rank = jnp.sum(before * onehot, axis=0, keepdims=True).astype(jnp.int32)
-    kept = rank < capacity
-    target = jnp.where(kept, jnp.bitwise_xor(ids, mine) * capacity + rank, -1)
-    target_ref[...] = target
     hit = lax.broadcasted_iota(jnp.int32, (rows, tok_rows), 0) == target
     gate = gate_ref[...].astype(F32).reshape(1, tok_rows)
     scaled, _ = normalize(tok_ref[...])
@@ -207,13 +220,16 @@
     tokens_out[...] = (go_ref[...].astype(F32) + branch).astype(BF16)
 
 
+def block_order(sources):
+    same = sorted(range(2, sources, 2), key=lambda k: (k.bit_count(), -k))
+    return same + list(range(sources - 1, 1, -2)) + [1, 0]
+
+
 def swap_blocks(blocks):
     count = len(blocks)
     return [
-        blocks[j]
-        if j == count - 2
-        else lax.ppermute(blocks[j], "space", [(i, i ^ j ^ (count - 2)) for i in range(count)])
-        for j in range(count)
+        lax.ppermute(block, "space", [(i, i ^ k) for i in range(count)]) if k else block
+        for block, k in zip(blocks, block_order(count))
     ]
 
 
@@ -221,12 +237,12 @@
     return (place[0] == 1) | (place[0] == 2)
 
 
-def pass_kernel(place, third_ref, own_ref, swapped_ref, middle_ref, across_ref, out_ref, sum_ref):
+def pass_kernel(place, third_ref, own_ref, swapped_ref, across_ref, middle_ref, out_ref, sum_ref):
     swapped = swapped_ref[...].astype(F32)
     onward = jnp.where(is_inner(place), swapped, 0.0)
     out_ref[...] = (third_ref[...].astype(F32) + onward).astype(BF16)
     total = own_ref[...].astype(F32) + (swapped - onward)
-    for ref in (middle_ref, across_ref):
+    for ref in (across_ref, middle_ref):
         total += ref[...].astype(F32)
     sum_ref[...] = total
 
@@ -244,8 +260,8 @@
     rows, hidden = own.shape
     piece_d = width // LINE
     swapped = lax.ppermute(first, "dp", [(0, 1), (1, 0), (2, 3), (3, 2)])
+    across = lax.ppermute(second, "dp", [(0, 2), (3, 1)])
     middle = lax.ppermute(second, "dp", [(1, 2), (2, 1)])
-    across = lax.ppermute(second, "dp", [(0, 2), (3, 1)])
     third, *ahead = lax.optimization_barrier((third, *ahead))
     passed, most = kernel_call(
         pass_kernel,
@@ -254,7 +270,7 @@
         1,
         [jax.ShapeDtypeStruct(own.shape, BF16), jax.ShapeDtypeStruct(own.shape, F32)],
         [smem] + [vmem] * 5,
-    )(place, third, own, swapped, middle, across)
+    )(place, third, own, swapped, across, middle)
     last = lax.ppermute(passed, "dp", [(0, 1), (3, 2), (1, 3), (2, 0)])
     sums = kernel_call(
         total_kernel,
@@ -296,6 +312,7 @@
         + [shape((capacity, 2 * width), BF16)] * sources,
         [smem] * 2 + [hbm] * 5,
         [
+            pltpu.VMEM((1, pl.cdiv(tok_rows, LANES) * LANES), jnp.int32),
             pltpu.VMEM((1, tok_rows), jnp.int32),
             pltpu.VMEM((tok_rows,), BF16),
             pltpu.VMEM((tok_rows, width), BF16),
@@ -316,9 +333,9 @@
         [shape((capacity, 2 * width), BF16)],
         [vmem],
         vmem_mib=2,
-    )(sent[sources - 2])
+    )(sent[-1])
     arrived = swap_blocks(sent)
-    arrived[sources - 2] = kept
+    arrived[-1] = kept
 
     late_set = list(range(3 * sources // 8, 6 * sources // 8))
     soon_set = [j for j in range(sources) if j not in late_set]

time: 75.3 us -> 74.1 us (0.984)
  starting transfers between devices: 31.1 us -> 29.9 us
    ppermute x1, waiting for transfers between devices: 2.44 us -> 3.96 us  [line_sums(): last = lax.ppermute(passed, 'dp', [(0, 1), (3, 2), (1, 3), (2, 0)])]
    ppermute x1, starting transfers between devices: 6.8 us -> 5.52 us  [line_sums(): last = lax.ppermute(passed, 'dp', [(0, 1), (3, 2), (1, 3), (2, 0)])]
    ppermute x1, starting transfers between devices: 4.51 us -> 5.76 us  [line_sums(): across = lax.ppermute(second, 'dp', [(0, 2), (3, 1)])]
    ppermute x14, starting transfers between devices: 17.2 us -> 16.1 us  [swap_blocks(): lax.ppermute(block, 'space', [(i, i ^ k) for i in range(count)])]
where the time goes in v7:
time: 74.1 us; the launch traced here: 73.9 us
  starting transfers between devices  29.9 us (40%)
  waiting for transfers between devices  26.4 us (36%)
  Pallas kernels  15.8 us (21%)
  local copies, waits for them, and re-layouts  0.96 us (1%)
  between operations  0.79 us (1%)
    ppermute x14, waiting for transfers between devices, swap_blocks(): lax.ppermute(block, 'space', [(i, i ^ k) for i in range(count)])  20.6 us
    ppermute x14, starting transfers between devices, swap_blocks(): lax.ppermute(block, 'space', [(i, i ^ k) for i in range(count)])  16.1 us
    pallas_call x2, Pallas kernels, work(): kernel_call(functools.partial(kernel, count, groups), name, 8 * span * wi...  6.15 us
    ppermute x1, starting transfers between devices, line_sums(): across = lax.ppermute(second, 'dp', [(0, 2), (3, 1)])  5.76 us
    ppermute x1, starting transfers between devices, line_sums(): last = lax.ppermute(passed, 'dp', [(0, 1), (3, 2), (1, 3), (2, 0)])  5.52 us
    pallas_call x1, Pallas kernels, body(): kernel_call(functools.partial(place_kernel, sources, capacity), 'place',...  4.52 us
    ppermute x1, waiting for transfers between devices, line_sums(): last = lax.ppermute(passed, 'dp', [(0, 1), (3, 2), (1, 3), (2, 0)])  3.96 us
    pallas_call x1, Pallas kernels, body(): kernel_call(finish_kernel, 'finish', 1, 1, [shape((tok_rows, width), BF16...  2.61 us
  transfers between devices with their start and end apart: 18, of which 12 were waited for; matrix products, arithmetic and copies ran while one was open for 0% of the time, Pallas kernels for 9%

profile of v7, /device:TPU:0, one launch (start us, length us, event | category | flops | bytes accessed | tf_op | source)
XLA Modules:
  0.0 73.9 jit_solution(1095364429804711211)
XLA Ops:
  0.7 4.5 %place.1 = (s32[1,576]{1,0:T(1,128)}, bf16[96,1024]{1,0:T(8,128)(2,1)}, bf16[96,1024]{1,0:T(8,128)(2,1)}, bf16[96,1024]{1,0:T(8,128)(2,1)}, bf16[96,1024]{1,0:T(...) custom-call(s32[1]{0:T(128)} %bitcast.me, ...), custom_call_target="tpu_custom_call" | custom-call | flops 905969664 | bytes 2752512 | tf_op jit(solution)/shard_map/place/pallas_call | solution.py:306
  5.2 3.0 %collective-permute-start = (bf16[96,1024]{1,0:T(8,128)(2,1)}, bf16[96,1024]{1,0:T(8,128)(2,1)S(1)}, u32[]{:S(2)}, u32[]{:S(2)}) collective-permute-start(bf16[96,1024]{1,0:T(8,128)(2,1)} %get-tuple-element.43), channel_id=1, source_target_pairs={{0,16},{4,20},{8,24},{12,28},{16,0},{20,4},{24,8},{28,12},{1,17},{... | collective-permute-start | bytes 589832 | tf_op jit(solution)/shard_map/ppermute | solution.py:231
  8.2 1.5 %collective-permute-start.1 = (bf16[96,1024]{1,0:T(8,128)(2,1)}, bf16[96,1024]{1,0:T(8,128)(2,1)S(1)}, u32[]{:S(2)}, u32[]{:S(2)}) collective-permute-start(bf16[96,1024]{1,0:T(8,128)(2,1)} %get-tuple-element.44), channel_id=1, source_target_pairs={{0,8},{4,12},{8,0},{12,4},{16,24},{20,28},{24,16},{28,20},{1,9},{5... | collective-permute-start | bytes 589832 | tf_op jit(solution)/shard_map/ppermute | solution.py:231
  9.8 3.0 %collective-permute-start.4 = (bf16[96,1024]{1,0:T(8,128)(2,1)}, bf16[96,1024]{1,0:T(8,128)(2,1)S(1)}, u32[]{:S(2)}, u32[]{:S(2)}) collective-permute-start(bf16[96,1024]{1,0:T(8,128)(2,1)} %get-tuple-element.50), channel_id=1, source_target_pairs={{0,28},{4,24},{8,20},{12,16},{16,12},{20,8},{24,4},{28,0},{1,29},{... | collective-permute-start | bytes 589832 | tf_op jit(solution)/shard_map/ppermute | solution.py:231
  12.8 0.6 collective-permute-done.refs_0_
  13.3 0.3 collective-permute-start.5
  13.6 2.6 %collective-permute-done.1.refs_1_ = bf16[96,1024]{1,0:T(8,128)(2,1)S(1)} collective-permute-done((bf16[96,1024]{1,0:T(8,128)(2,1)}, bf16[96,1024]{1,0:T(8,128)(2,1)S(1)}, u32[]{:S(2)}, u32[]{:S(2)}) %collective-permute-start.1) | collective-permute-done | bytes 196640 | tf_op jit(solution)/shard_map/ppermute | solution.py:231
  16.3 0.3 collective-permute-start.6
  16.6 0.9 %copy-done.4 = bf16[96,1024]{1,0:T(8,128)(2,1)S(1)} copy-done((bf16[96,1024]{1,0:T(8,128)(2,1)S(1)}, bf16[96,1024]{1,0:T(8,128)(2,1)}, u32[]{:S(2)}) %copy-start.4) | copy-done | bytes 196632
  17.5 2.5 %collective-permute-done.2.refs_2_ = bf16[96,1024]{1,0:T(8,128)(2,1)S(1)} collective-permute-done((bf16[96,1024]{1,0:T(8,128)(2,1)}, bf16[96,1024]{1,0:T(8,128)(2,1)S(1)}, u32[]{:S(2)}, u32[]{:S(2)}) %collective-permute-start.2) | collective-permute-done | bytes 196640 | tf_op jit(solution)/shard_map/ppermute | solution.py:231
  20.1 3.2 %sooner.1 = (f32[512,1024]{1,0:T(8,128)S(1)}, f32[1024,512]{1,0:T(8,128)S(1)}, bf16[480,1024]{1,0:T(8,128)(2,1)S(1)}, bf16[480,128]{1,0:T(8,128)(2,1)S(1)}) custom-call(s32[1]{0:T(128)} %bitcast.1.place, bf16[512,1024]{1,0:T(8,128)(2,1)S(1)} %bitcast.8, bf16[1024,512]{1,0:T(8,128)(2,1)S(1)} %bitcast.11, bf16[96,1024]{1,0:T(8,128)(2,1)S(1)} %collective-permute-done.refs_0_, ...), custom_call_target="tpu_custom_call" | custom-call | flops 2013265920 | bytes 6160384 | tf_op jit(solution)/shard_map/sooner/pallas_call | solution.py:345
  23.3 0.5 collective-permute-done.4.refs_0_
  23.9 3.3 %collective-permute-done.5.refs_1_ = bf16[96,1024]{1,0:T(8,128)(2,1)S(1)} collective-permute-done((bf16[96,1024]{1,0:T(8,128)(2,1)}, bf16[96,1024]{1,0:T(8,128)(2,1)S(1)}, u32[]{:S(2)}, u32[]{:S(2)}) %collective-permute-start.5) | collective-permute-done | bytes 196640 | tf_op jit(solution)/shard_map/ppermute | solution.py:231
  27.2 2.9 %later.1 = (bf16[256,1024]{1,0:T(8,128)(2,1)S(1)}, bf16[256,1024]{1,0:T(8,128)(2,1)S(1)}, bf16[256,1024]{1,0:T(8,128)(2,1)S(1)}, bf16[256,1024]{1,0:T(8,128)(2,1...) custom-call(s32[1]{0:T(128)} %bitcast.1.place, bf16[512,1024]{1,0:T(8,128)(2,1)S(1)} %bitcast.9, ...), custom_call_target="tpu_custom_call" | custom-call | flops 1207959552 | bytes 5373952 | tf_op jit(solution)/shard_map/later/pallas_call | solution.py:345
  30.1 1.8 %collective-permute-start.14 = (bf16[256,1024]{1,0:T(8,128)(2,1)S(1)}, bf16[256,1024]{1,0:T(8,128)(2,1)S(1)}, u32[]{:S(2)}, u32[]{:S(2)}) collective-permute-start(bf16[256,1024]{1,0:T(8,128)(2,1)S(1)} %get-tuple-element.74), channel_id=1, source_target_pairs={{0,1},{1,0},{2,3},{3,2},{4,5},{5,4},{6,7},{7,6},{8,9},{9,8},{10,11... | collective-permute-start | bytes 1572872 | tf_op jit(solution)/shard_map/ppermute | solution.py:262
  31.9 0.7 collective-permute-start.16
  32.6 5.8 %collective-permute-start.15 = (bf16[256,1024]{1,0:T(8,128)(2,1)S(1)}, bf16[256,1024]{1,0:T(8,128)(2,1)S(1)}, u32[]{:S(2)}, u32[]{:S(2)}) collective-permute-start(bf16[256,1024]{1,0:T(8,128)(2,1)S(1)} %get-tuple-element.75), channel_id=1, source_target_pairs={{0,2},{3,1},{4,6},{7,5},{8,10},{11,9},{12,14},{15,13},{16,18},{19,... | collective-permute-start | bytes 1572872 | tf_op jit(solution)/shard_map/ppermute | solution.py:263
  38.4 1.0 %back.1 = (bf16[96,640]{1,0:T(8,128)(2,1)S(1)}, bf16[96,640]{1,0:T(8,128)(2,1)S(1)}, bf16[96,640]{1,0:T(8,128)(2,1)S(1)}, bf16[96,640]{1,0:T(8,128)(2,1)S(1)}, b...) custom-call(bf16[512,1024]{1,0:T(8,128)(2,1)S(1)} %bitcast.10, ...), custom_call_target="tpu_custom_call" | custom-call | flops 1 | bytes 1 | tf_op jit(solution)/shard_map/back/pallas_call | solution.py:360
  39.5 1.5 %collective-permute-start.7 = (bf16[96,640]{1,0:T(8,128)(2,1)S(1)}, bf16[96,640]{1,0:T(8,128)(2,1)S(1)}, u32[]{:S(2)}, u32[]{:S(2)}) collective-permute-start(bf16[96,640]{1,0:T(8,128)(2,1)S(1)} %get-tuple-element.58), channel_id=1, source_target_pairs={{0,16},{4,20},{8,24},{12,28},{16,0},{20,4},{24,8},{28,12},{1,17},{... | collective-permute-start | bytes 368648 | tf_op jit(solution)/shard_map/ppermute | solution.py:231
  41.0 1.5 %collective-permute-start.8 = (bf16[96,640]{1,0:T(8,128)(2,1)S(1)}, bf16[96,640]{1,0:T(8,128)(2,1)S(1)}, u32[]{:S(2)}, u32[]{:S(2)}) collective-permute-start(bf16[96,640]{1,0:T(8,128)(2,1)S(1)} %get-tuple-element.59), channel_id=1, source_target_pairs={{0,8},{4,12},{8,0},{12,4},{16,24},{20,28},{24,16},{28,20},{1,9},{5... | collective-permute-start | bytes 368648 | tf_op jit(solution)/shard_map/ppermute | solution.py:231
  42.5 1.9 %collective-permute-done.7.refs_0_ = bf16[96,640]{1,0:T(8,128)(2,1)S(1)} collective-permute-done((bf16[96,640]{1,0:T(8,128)(2,1)S(1)}, bf16[96,640]{1,0:T(8,128)(2,1)S(1)}, u32[]{:S(2)}, u32[]{:S(2)}) %collective-permute-start.7) | collective-permute-done | bytes 122912 | tf_op jit(solution)/shard_map/ppermute | solution.py:231
  44.4 2.4 %collective-permute-start.9 = (bf16[96,640]{1,0:T(8,128)(2,1)S(1)}, bf16[96,640]{1,0:T(8,128)(2,1)S(1)}, u32[]{:S(2)}, u32[]{:S(2)}) collective-permute-start(bf16[96,640]{1,0:T(8,128)(2,1)S(1)} %get-tuple-element.60), channel_id=1, source_target_pairs={{0,24},{4,28},{8,16},{12,20},{16,8},{20,12},{24,0},{28,4},{1,25},{... | collective-permute-start | bytes 368648 | tf_op jit(solution)/shard_map/ppermute | solution.py:231
  46.8 3.7 %collective-permute-done.9.refs_2_ = bf16[96,640]{1,0:T(8,128)(2,1)S(1)} collective-permute-done((bf16[96,640]{1,0:T(8,128)(2,1)S(1)}, bf16[96,640]{1,0:T(8,128)(2,1)S(1)}, u32[]{:S(2)}, u32[]{:S(2)}) %collective-permute-start.9) | collective-permute-done | bytes 122912 | tf_op jit(solution)/shard_map/ppermute | solution.py:231
  50.5 2.3 %collective-permute-done.10.refs_3_ = bf16[96,640]{1,0:T(8,128)(2,1)S(1)} collective-permute-done((bf16[96,640]{1,0:T(8,128)(2,1)S(1)}, bf16[96,640]{1,0:T(8,128)(2,1)S(1)}, u32[]{:S(2)}, u32[]{:S(2)}) %collective-permute-start.10) | collective-permute-done | bytes 122912 | tf_op jit(solution)/shard_map/ppermute | solution.py:231
  52.8 1.8 %collective-permute-done.15.across_ref = bf16[256,1024]{1,0:T(8,128)(2,1)S(1)} collective-permute-done((bf16[256,1024]{1,0:T(8,128)(2,1)S(1)}, bf16[256,1024]{1,0:T(8,128)(2,1)S(1)}, u32[]{:S(2)}, u32[]{:S(2)}) %collective-permute-start.15) | collective-permute-done | bytes 524320 | tf_op jit(solution)/shard_map/ppermute | solution.py:263
  54.7 0.4 pass.1
  55.1 5.5 %collective-permute-start.17 = (bf16[256,1024]{1,0:T(8,128)(2,1)S(1)}, bf16[256,1024]{1,0:T(8,128)(2,1)S(1)}, u32[]{:S(2)}, u32[]{:S(2)}) collective-permute-start(bf16[256,1024]{1,0:T(8,128)(2,1)S(1)} %get-tuple-element.77), channel_id=1, source_target_pairs={{0,1},{3,2},{1,3},{2,0},{4,5},{7,6},{5,7},{6,4},{8,9},{11,10},{9,1... | collective-permute-start | bytes 1572872 | tf_op jit(solution)/shard_map/ppermute | solution.py:274
  60.6 2.5 %collective-permute-start.12 = (bf16[96,640]{1,0:T(8,128)(2,1)S(1)}, bf16[96,640]{1,0:T(8,128)(2,1)S(1)}, u32[]{:S(2)}, u32[]{:S(2)}) collective-permute-start(bf16[96,640]{1,0:T(8,128)(2,1)S(1)} %get-tuple-element.67), channel_id=1, source_target_pairs={{0,12},{4,8},{8,4},{12,0},{16,28},{20,24},{24,20},{28,16},{1,13},{... | collective-permute-start | bytes 368648 | tf_op jit(solution)/shard_map/ppermute | solution.py:231
  63.1 3.0 %collective-permute-done.11.refs_4_ = bf16[96,640]{1,0:T(8,128)(2,1)S(1)} collective-permute-done((bf16[96,640]{1,0:T(8,128)(2,1)S(1)}, bf16[96,640]{1,0:T(8,128)(2,1)S(1)}, u32[]{:S(2)}, u32[]{:S(2)}) %collective-permute-start.11) | collective-permute-done | bytes 122912 | tf_op jit(solution)/shard_map/ppermute | solution.py:231
  66.2 2.6 %finish.1 = (bf16[576,512]{1,0:T(8,128)(2,1)}, bf16[576]{0:T(1024)(128)(2,1)}) custom-call(s32[1,576]{1,0:T(1,128)S(1)} %copy-done.5, bf16[576]{0:T(1024)(128)(2,1)S(1)} %copy-done.6, bf16[576,512]{1,0:T(8,128)(2,1)S(1)} %copy-done.2, f32[1,512]{1,0:T(1,128)S(1)} %bitcast.14, bf16[576,512]{1,0:T(8,128)(2,1)S(1)} %copy-done.3, ...), custom_call_target="tpu_custom_call" | custom-call | flops 1 | bytes 1 | tf_op jit(solution)/shard_map/finish/pallas_call | solution.py:382
  68.9 4.0 %collective-permute-done.17.last_ref = bf16[256,1024]{1,0:T(8,128)(2,1)S(1)} collective-permute-done((bf16[256,1024]{1,0:T(8,128)(2,1)S(1)}, bf16[256,1024]{1,0:T(8,128)(2,1)S(1)}, u32[]{:S(2)}, u32[]{:S(2)}) %collective-permute-start.17) | collective-permute-done | bytes 524320 | tf_op jit(solution)/shard_map/ppermute | solution.py:274
  72.8 1.1 %total.1 = (f32[128,1024]{1,0:T(8,128)}, f32[256,512]{1,0:T(8,128)}) custom-call(f32[256,1024]{1,0:T(8,128)S(1)} %get-tuple-element.76.sum_ref, bf16[256,1024]{1,0:T(8,128)(2,1)S(1)} %collective-permute-done.17.last_ref), custom_call_target="tpu_custom_call" | custom-call | flops 1 | bytes 1 | tf_op jit(solution)/shard_map/total/pallas_call | solution.py:275
  (28 shorter events, 0.2 us)
Async XLA Ops:
  0.6 19.4 %copy-start.1 = (bf16[1,1024,512]{2,1,0:T(8,128)(2,1)S(1)}, bf16[1,1024,512]{2,1,0:T(8,128)(2,1)}, u32[]{:S(2)}) copy-start(bf16[1,1024,512]{2,1,0:T(8,128)(2,1)} %param.10) | copy-start | bytes 3145732
  0.6 19.4 %copy-start = (bf16[1,512,1024]{2,1,0:T(8,128)(2,1)S(1)}, bf16[1,512,1024]{2,1,0:T(8,128)(2,1)}, u32[]{:S(2)}) copy-start(bf16[1,512,1024]{2,1,0:T(8,128)(2,1)} %param.9) | copy-start | bytes 3145732
  5.2 8.1 %collective-permute-start = (bf16[96,1024]{1,0:T(8,128)(2,1)}, bf16[96,1024]{1,0:T(8,128)(2,1)S(1)}, u32[]{:S(2)}, u32[]{:S(2)}) collective-permute-start(bf16[96,1024]{1,0:T(8,128)(2,1)} %get-tuple-element.43), channel_id=1, source_target_pairs={{0,16},{4,20},{8,24},{12,28},{16,0},{20,4},{24,8},{28,12},{1,17},{... | collective-permute-start | bytes 589832 | tf_op jit(solution)/shard_map/ppermute | solution.py:231
  8.2 8.0 %collective-permute-start.1 = (bf16[96,1024]{1,0:T(8,128)(2,1)}, bf16[96,1024]{1,0:T(8,128)(2,1)S(1)}, u32[]{:S(2)}, u32[]{:S(2)}) collective-permute-start(bf16[96,1024]{1,0:T(8,128)(2,1)} %get-tuple-element.44), channel_id=1, source_target_pairs={{0,8},{4,12},{8,0},{12,4},{16,24},{20,28},{24,16},{28,20},{1,9},{5... | collective-permute-start | bytes 589832 | tf_op jit(solution)/shard_map/ppermute | solution.py:231
  9.7 10.3 %collective-permute-start.2 = (bf16[96,1024]{1,0:T(8,128)(2,1)}, bf16[96,1024]{1,0:T(8,128)(2,1)S(1)}, u32[]{:S(2)}, u32[]{:S(2)}) collective-permute-start(bf16[96,1024]{1,0:T(8,128)(2,1)} %get-tuple-element.45), channel_id=1, source_target_pairs={{0,24},{4,28},{8,16},{12,20},{16,8},{20,12},{24,0},{28,4},{1,25},{... | collective-permute-start | bytes 589832 | tf_op jit(solution)/shard_map/ppermute | solution.py:231
  9.8 10.3 %collective-permute-start.3 = (bf16[96,1024]{1,0:T(8,128)(2,1)}, bf16[96,1024]{1,0:T(8,128)(2,1)S(1)}, u32[]{:S(2)}, u32[]{:S(2)}) collective-permute-start(bf16[96,1024]{1,0:T(8,128)(2,1)} %get-tuple-element.46), channel_id=1, source_target_pairs={{0,4},{4,0},{8,12},{12,8},{16,20},{20,16},{24,28},{28,24},{1,5},{5... | collective-permute-start | bytes 589832 | tf_op jit(solution)/shard_map/ppermute | solution.py:231
  9.8 14.1 %collective-permute-start.4 = (bf16[96,1024]{1,0:T(8,128)(2,1)}, bf16[96,1024]{1,0:T(8,128)(2,1)S(1)}, u32[]{:S(2)}, u32[]{:S(2)}) collective-permute-start(bf16[96,1024]{1,0:T(8,128)(2,1)} %get-tuple-element.50), channel_id=1, source_target_pairs={{0,28},{4,24},{8,20},{12,16},{16,12},{20,8},{24,4},{28,0},{1,29},{... | collective-permute-start | bytes 589832 | tf_op jit(solution)/shard_map/ppermute | solution.py:231
  13.3 13.8 %collective-permute-start.5 = (bf16[96,1024]{1,0:T(8,128)(2,1)}, bf16[96,1024]{1,0:T(8,128)(2,1)S(1)}, u32[]{:S(2)}, u32[]{:S(2)}) collective-permute-start(bf16[96,1024]{1,0:T(8,128)(2,1)} %get-tuple-element.51), channel_id=1, source_target_pairs={{0,20},{4,16},{8,28},{12,24},{16,4},{20,0},{24,12},{28,8},{1,21},{... | collective-permute-start | bytes 589832 | tf_op jit(solution)/shard_map/ppermute | solution.py:231
  16.3 10.9 %collective-permute-start.6 = (bf16[96,1024]{1,0:T(8,128)(2,1)}, bf16[96,1024]{1,0:T(8,128)(2,1)S(1)}, u32[]{:S(2)}, u32[]{:S(2)}) collective-permute-start(bf16[96,1024]{1,0:T(8,128)(2,1)} %get-tuple-element.52), channel_id=1, source_target_pairs={{0,12},{4,8},{8,4},{12,0},{16,28},{20,24},{24,20},{28,16},{1,13},{... | collective-permute-start | bytes 589832 | tf_op jit(solution)/shard_map/ppermute | solution.py:231
  16.6 0.9 %copy-start.4 = (bf16[96,1024]{1,0:T(8,128)(2,1)S(1)}, bf16[96,1024]{1,0:T(8,128)(2,1)}, u32[]{:S(2)}) copy-start(bf16[96,1024]{1,0:T(8,128)(2,1)} %get-tuple-element.47.block_ref) | copy-start | bytes 589828
  30.1 22.7 %collective-permute-start.14 = (bf16[256,1024]{1,0:T(8,128)(2,1)S(1)}, bf16[256,1024]{1,0:T(8,128)(2,1)S(1)}, u32[]{:S(2)}, u32[]{:S(2)}) collective-permute-start(bf16[256,1024]{1,0:T(8,128)(2,1)S(1)} %get-tuple-element.74), channel_id=1, source_target_pairs={{0,1},{1,0},{2,3},{3,2},{4,5},{5,4},{6,7},{7,6},{8,9},{9,8},{10,11... | collective-permute-start | bytes 1572872 | tf_op jit(solution)/shard_map/ppermute | solution.py:262
  31.9 20.9 %collective-permute-start.16 = (bf16[256,1024]{1,0:T(8,128)(2,1)S(1)}, bf16[256,1024]{1,0:T(8,128)(2,1)S(1)}, u32[]{:S(2)}, u32[]{:S(2)}) collective-permute-start(bf16[256,1024]{1,0:T(8,128)(2,1)S(1)} %get-tuple-element.75), channel_id=1, source_target_pairs={{1,2},{2,1},{5,6},{6,5},{9,10},{10,9},{13,14},{14,13},{17,18},{18,... | collective-permute-start | bytes 1572872 | tf_op jit(solution)/shard_map/ppermute | solution.py:264
  32.6 22.1 %collective-permute-start.15 = (bf16[256,1024]{1,0:T(8,128)(2,1)S(1)}, bf16[256,1024]{1,0:T(8,128)(2,1)S(1)}, u32[]{:S(2)}, u32[]{:S(2)}) collective-permute-start(bf16[256,1024]{1,0:T(8,128)(2,1)S(1)} %get-tuple-element.75), channel_id=1, source_target_pairs={{0,2},{3,1},{4,6},{7,5},{8,10},{11,9},{12,14},{15,13},{16,18},{19,... | collective-permute-start | bytes 1572872 | tf_op jit(solution)/shard_map/ppermute | solution.py:263
  38.4 27.8 %copy-start.2 = (bf16[576,512]{1,0:T(8,128)(2,1)S(1)}, bf16[576,512]{1,0:T(8,128)(2,1)}, u32[]{:S(2)}) copy-start(bf16[576,512]{1,0:T(8,128)(2,1)} %tok_ref.1) | copy-start | bytes 1769476
  38.4 27.8 %copy-start.3 = (bf16[576,512]{1,0:T(8,128)(2,1)S(1)}, bf16[576,512]{1,0:T(8,128)(2,1)}, u32[]{:S(2)}) copy-start(bf16[576,512]{1,0:T(8,128)(2,1)} %go_ref.1) | copy-start | bytes 1769476
  38.4 27.8 %copy-start.5 = (s32[1,576]{1,0:T(1,128)S(1)}, s32[1,576]{1,0:T(1,128)}, u32[]{:S(2)}) copy-start(s32[1,576]{1,0:T(1,128)} %get-tuple-element.42.target_ref) | copy-start | bytes 6916
  38.4 27.8 %copy-start.6 = (bf16[576]{0:T(1024)(128)(2,1)S(1)}, bf16[576]{0:T(1024)(128)(2,1)}, u32[]{:S(2)}) copy-start(bf16[576]{0:T(1024)(128)(2,1)} %gate_ref.1) | copy-start | bytes 3460
  38.4 27.8 %copy-start.7 = (f32[512]{0:T(512)S(1)}, f32[512]{0:T(512)}, u32[]{:S(2)}) copy-start(f32[512]{0:T(512)} %param.8) | copy-start | bytes 6148
  39.5 4.9 %collective-permute-start.7 = (bf16[96,640]{1,0:T(8,128)(2,1)S(1)}, bf16[96,640]{1,0:T(8,128)(2,1)S(1)}, u32[]{:S(2)}, u32[]{:S(2)}) collective-permute-start(bf16[96,640]{1,0:T(8,128)(2,1)S(1)} %get-tuple-element.58), channel_id=1, source_target_pairs={{0,16},{4,20},{8,24},{12,28},{16,0},{20,4},{24,8},{28,12},{1,17},{... | collective-permute-start | bytes 368648 | tf_op jit(solution)/shard_map/ppermute | solution.py:231
  41.0 5.8 %collective-permute-start.8 = (bf16[96,640]{1,0:T(8,128)(2,1)S(1)}, bf16[96,640]{1,0:T(8,128)(2,1)S(1)}, u32[]{:S(2)}, u32[]{:S(2)}) collective-permute-start(bf16[96,640]{1,0:T(8,128)(2,1)S(1)} %get-tuple-element.59), channel_id=1, source_target_pairs={{0,8},{4,12},{8,0},{12,4},{16,24},{20,28},{24,16},{28,20},{1,9},{5... | collective-permute-start | bytes 368648 | tf_op jit(solution)/shard_map/ppermute | solution.py:231
  44.4 6.1 %collective-permute-start.9 = (bf16[96,640]{1,0:T(8,128)(2,1)S(1)}, bf16[96,640]{1,0:T(8,128)(2,1)S(1)}, u32[]{:S(2)}, u32[]{:S(2)}) collective-permute-start(bf16[96,640]{1,0:T(8,128)(2,1)S(1)} %get-tuple-element.60), channel_id=1, source_target_pairs={{0,24},{4,28},{8,16},{12,20},{16,8},{20,12},{24,0},{28,4},{1,25},{... | collective-permute-start | bytes 368648 | tf_op jit(solution)/shard_map/ppermute | solution.py:231
  46.8 6.0 %collective-permute-start.10 = (bf16[96,640]{1,0:T(8,128)(2,1)S(1)}, bf16[96,640]{1,0:T(8,128)(2,1)S(1)}, u32[]{:S(2)}, u32[]{:S(2)}) collective-permute-start(bf16[96,640]{1,0:T(8,128)(2,1)S(1)} %get-tuple-element.61), channel_id=1, source_target_pairs={{0,28},{4,24},{8,20},{12,16},{16,12},{20,8},{24,4},{28,0},{1,29},{... | collective-permute-start | bytes 368648 | tf_op jit(solution)/shard_map/ppermute | solution.py:231
  55.1 17.7 %collective-permute-start.17 = (bf16[256,1024]{1,0:T(8,128)(2,1)S(1)}, bf16[256,1024]{1,0:T(8,128)(2,1)S(1)}, u32[]{:S(2)}, u32[]{:S(2)}) collective-permute-start(bf16[256,1024]{1,0:T(8,128)(2,1)S(1)} %get-tuple-element.77), channel_id=1, source_target_pairs={{0,1},{3,2},{1,3},{2,0},{4,5},{7,6},{5,7},{6,4},{8,9},{11,10},{9,1... | collective-permute-start | bytes 1572872 | tf_op jit(solution)/shard_map/ppermute | solution.py:274
  60.6 5.5 %collective-permute-start.11 = (bf16[96,640]{1,0:T(8,128)(2,1)S(1)}, bf16[96,640]{1,0:T(8,128)(2,1)S(1)}, u32[]{:S(2)}, u32[]{:S(2)}) collective-permute-start(bf16[96,640]{1,0:T(8,128)(2,1)S(1)} %get-tuple-element.66), channel_id=1, source_target_pairs={{0,20},{4,16},{8,28},{12,24},{16,4},{20,0},{24,12},{28,8},{1,21},{... | collective-permute-start | bytes 368648 | tf_op jit(solution)/shard_map/ppermute | solution.py:231
  60.6 5.6 %collective-permute-start.12 = (bf16[96,640]{1,0:T(8,128)(2,1)S(1)}, bf16[96,640]{1,0:T(8,128)(2,1)S(1)}, u32[]{:S(2)}, u32[]{:S(2)}) collective-permute-start(bf16[96,640]{1,0:T(8,128)(2,1)S(1)} %get-tuple-element.67), channel_id=1, source_target_pairs={{0,12},{4,8},{8,4},{12,0},{16,28},{20,24},{24,20},{28,16},{1,13},{... | collective-permute-start | bytes 368648 | tf_op jit(solution)/shard_map/ppermute | solution.py:231
  63.1 3.1 %collective-permute-start.13 = (bf16[96,640]{1,0:T(8,128)(2,1)S(1)}, bf16[96,640]{1,0:T(8,128)(2,1)S(1)}, u32[]{:S(2)}, u32[]{:S(2)}) collective-permute-start(bf16[96,640]{1,0:T(8,128)(2,1)S(1)} %get-tuple-element.68), channel_id=1, source_target_pairs={{0,4},{4,0},{8,12},{12,8},{16,20},{20,16},{24,28},{28,24},{1,5},{5... | collective-permute-start | bytes 368648 | tf_op jit(solution)/shard_map/ppermute | solution.py:231

commit v8 on v7

--- a/solution.py
+++ b/solution.py
@@ -125,9 +125,8 @@
 
 
 def shard_order(place):
-    first = jnp.where(lax.rem(place, 2) == 0, 3, 0)
-    second = jnp.where(place < 2, 2, 1)
-    return [first, second, 6 - first - second - place, place]
+    second = jnp.where(place < 2, 2 - 2 * place, 7 - 2 * place)
+    return [3 - place, second, 3 - second, place]
 
 
 def expert_work(order, blocks, w_in_ref, w_out_ref, gpre_ref, extra_ref, rows_ref, turned_ref, put):
@@ -225,53 +224,51 @@
     return same + list(range(sources - 1, 1, -2)) + [1, 0]
 
 
-def swap_blocks(blocks):
-    count = len(blocks)
+def swap_blocks(blocks, order):
+    devices = range(lax.axis_size("space"))
     return [
-        lax.ppermute(block, "space", [(i, i ^ k) for i in range(count)]) if k else block
-        for block, k in zip(blocks, block_order(count))
+        lax.ppermute(block, "space", [(i, i ^ k) for i in devices]) if k else block
+        for block, k in zip(blocks, order)
     ]
 
 
-def is_inner(place):
-    return (place[0] == 1) | (place[0] == 2)
-
-
-def pass_kernel(place, third_ref, own_ref, swapped_ref, across_ref, middle_ref, out_ref, sum_ref):
-    swapped = swapped_ref[...].astype(F32)
-    onward = jnp.where(is_inner(place), swapped, 0.0)
-    out_ref[...] = (third_ref[...].astype(F32) + onward).astype(BF16)
-    total = own_ref[...].astype(F32) + (swapped - onward)
-    for ref in (across_ref, middle_ref):
-        total += ref[...].astype(F32)
-    sum_ref[...] = total
-
-
-def total_kernel(sum_ref, last_ref, in_ref, out_ref):
+def pass_kernel(place, up_ref, down_ref, third_ref, own_ref, out_ref, sum_ref):
+    up, down = up_ref[...].astype(F32), down_ref[...].astype(F32)
+    low = place[0] == 1
+    out_ref[...] = (third_ref[...].astype(F32) + jnp.where(low, up, down)).astype(BF16)
+    sum_ref[...] = own_ref[...].astype(F32) + jnp.where(low, down, up)
+
+
+def total_kernel(sum_ref, cycle_ref, last_ref, in_ref, out_ref):
     piece_d, half = in_ref.shape[0], out_ref.shape[0] // 2
     width = out_ref.shape[1]
-    total = sum_ref[...] + last_ref[...].astype(F32)
+    total = sum_ref[...] + cycle_ref[...].astype(F32) + last_ref[...].astype(F32)
     in_ref[...] = total[:piece_d]
     out_ref[:half, :] = total[piece_d:, :width]
     out_ref[half:, :] = total[piece_d:, width:]
 
 
-def line_sums(place, first, second, third, own, width, ahead):
+def line_sums(place, first, second, third, own, width, returned):
     rows, hidden = own.shape
     piece_d = width // LINE
-    swapped = lax.ppermute(first, "dp", [(0, 1), (1, 0), (2, 3), (3, 2)])
-    across = lax.ppermute(second, "dp", [(0, 2), (3, 1)])
-    middle = lax.ppermute(second, "dp", [(1, 2), (2, 1)])
-    third, *ahead = lax.optimization_barrier((third, *ahead))
+    half = len(returned) // 2
+    order = block_order(len(returned))
+    up = lax.ppermute(first, "dp", [(0, 1), (1, 2)])
+    down = lax.ppermute(first, "dp", [(3, 2), (2, 1)])
+    cycle = lax.ppermute(second, "dp", [(0, 2), (1, 0), (2, 3), (3, 1)])
+    back = swap_blocks(returned[:half], order[:half])
+    third, *back = lax.optimization_barrier((third, *back))
     passed, most = kernel_call(
         pass_kernel,
         "pass",
         1,
         1,
         [jax.ShapeDtypeStruct(own.shape, BF16), jax.ShapeDtypeStruct(own.shape, F32)],
-        [smem] + [vmem] * 5,
-    )(place, third, own, swapped, across, middle)
+        [smem] + [vmem] * 4,
+    )(place, up, down, third, own)
     last = lax.ppermute(passed, "dp", [(0, 1), (3, 2), (1, 3), (2, 0)])
+    cycle, *rest = lax.optimization_barrier((cycle, *returned[half:]))
+    back += swap_blocks(rest, order[half:])
     sums = kernel_call(
         total_kernel,
         "total",
@@ -281,9 +278,9 @@
             jax.ShapeDtypeStruct((piece_d, hidden), F32),
             jax.ShapeDtypeStruct((2 * (rows - piece_d), width), F32),
         ],
-        [vmem] * 2,
-    )(most, last)
-    return *sums, ahead
+        [vmem] * 3,
+    )(most, cycle, last)
+    return *sums, back
 
 
 def body(tokens, gain, w_in, w_out, expert_ids, gate, grad_out):
@@ -334,7 +331,7 @@
         [vmem],
         vmem_mib=2,
     )(sent[-1])
-    arrived = swap_blocks(sent)
+    arrived = swap_blocks(sent, block_order(sources))
     arrived[-1] = kept
 
     late_set = list(range(3 * sources // 8, 6 * sources // 8))
@@ -366,12 +363,10 @@
         [vmem] * 5,
     )(weight_in, soon_gpre, soon_extra, late_gpre, late_extra)
 
-    back = swap_blocks(returned)
     if groups == LINE:
-        grad_w_in, grad_w_out, back[: sources // 2] = line_sums(
-            place, *parts, width, back[: sources // 2]
-        )
+        grad_w_in, grad_w_out, back = line_sums(place, *parts, width, returned)
     else:
+        back = swap_blocks(returned, block_order(sources))
         parts_in, parts_out = zip(*[split_piece(part, width, LINE) for part in parts])
         grad_w_in, grad_w_out = (
             lax.psum_scatter(

time: 74.1 us -> 71.9 us (0.970)
  waiting for transfers between devices: 26.4 us -> 20.8 us
  starting transfers between devices: 29.9 us -> 33.4 us
    ppermute x1, starting transfers between devices: 5.52 us -> 11 us  [line_sums(): last = lax.ppermute(passed, 'dp', [(0, 1), (3, 2), (1, 3), (2, 0)])]
    ppermute x17, waiting for transfers between devices: 22.4 us -> 19.5 us  [the longest x14 19.5 us: swap_blocks(): lax.ppermute(block, 'space', [(i, i ^ k) for i in devices])]
    ppermute x1, waiting for transfers between devices: 3.96 us -> 1.24 us  [line_sums(): last = lax.ppermute(passed, 'dp', [(0, 1), (3, 2), (1, 3), (2, 0)])]
    ppermute x17, starting transfers between devices: 24.4 us -> 22.4 us  [the longest x14 16 us: swap_blocks(): lax.ppermute(block, 'space', [(i, i ^ k) for i in devices])]
  transfers between devices with their start and end apart: 18 -> 18, of which waited for: 12 -> 11; matrix products, arithmetic and copies ran while one was open for 0% -> 0% of each run, Pallas kernels for 9% -> 10%
where the time goes in v8:
time: 71.9 us; the launch traced here: 71.7 us
  starting transfers between devices  33.4 us (46%)
  waiting for transfers between devices  20.8 us (29%)
  Pallas kernels  15.7 us (22%)
  local copies, waits for them, and re-layouts  0.96 us (1%)
  between operations  0.79 us (1%)
    ppermute x14, waiting for transfers between devices, swap_blocks(): lax.ppermute(block, 'space', [(i, i ^ k) for i in devices])  19.5 us
    ppermute x14, starting transfers between devices, swap_blocks(): lax.ppermute(block, 'space', [(i, i ^ k) for i in devices])  16 us
    ppermute x1, starting transfers between devices, line_sums(): last = lax.ppermute(passed, 'dp', [(0, 1), (3, 2), (1, 3), (2, 0)])  11 us
    pallas_call x2, Pallas kernels, work(): kernel_call(functools.partial(kernel, count, groups), name, 8 * span * wi...  6.15 us
    pallas_call x1, Pallas kernels, body(): kernel_call(functools.partial(place_kernel, sources, capacity), 'place',...  4.52 us
    ppermute x1, starting transfers between devices, line_sums(): up = lax.ppermute(first, 'dp', [(0, 1), (1, 2)])  4.31 us
    pallas_call x1, Pallas kernels, body(): kernel_call(finish_kernel, 'finish', 1, 1, [shape((tok_rows, width), BF16...  2.59 us
  transfers between devices with their start and end apart: 18, of which 11 were waited for; matrix products, arithmetic and copies ran while one was open for 0% of the time, Pallas kernels for 10%

profile of v8, /device:TPU:0, one launch (start us, length us, event | category | flops | bytes accessed | tf_op | source)
XLA Modules:
  0.0 71.7 jit_solution(18199560362461312622)
XLA Ops:
  0.7 4.5 %place.1 = (s32[1,576]{1,0:T(1,128)}, bf16[96,1024]{1,0:T(8,128)(2,1)}, bf16[96,1024]{1,0:T(8,128)(2,1)}, bf16[96,1024]{1,0:T(8,128)(2,1)}, bf16[96,1024]{1,0:T(...) custom-call(s32[1]{0:T(128)} %bitcast.me, ...), custom_call_target="tpu_custom_call" | custom-call | flops 905969664 | bytes 2752512 | tf_op jit(solution)/shard_map/place/pallas_call | solution.py:303
  5.2 3.0 %collective-permute-start = (bf16[96,1024]{1,0:T(8,128)(2,1)}, bf16[96,1024]{1,0:T(8,128)(2,1)S(1)}, u32[]{:S(2)}, u32[]{:S(2)}) collective-permute-start(bf16[96,1024]{1,0:T(8,128)(2,1)} %get-tuple-element.48), channel_id=1, source_target_pairs={{0,16},{4,20},{8,24},{12,28},{16,0},{20,4},{24,8},{28,12},{1,17},{... | collective-permute-start | bytes 589832 | tf_op jit(solution)/shard_map/ppermute | solution.py:230
  8.2 1.5 %collective-permute-start.1 = (bf16[96,1024]{1,0:T(8,128)(2,1)}, bf16[96,1024]{1,0:T(8,128)(2,1)S(1)}, u32[]{:S(2)}, u32[]{:S(2)}) collective-permute-start(bf16[96,1024]{1,0:T(8,128)(2,1)} %get-tuple-element.49), channel_id=1, source_target_pairs={{0,8},{4,12},{8,0},{12,4},{16,24},{20,28},{24,16},{28,20},{1,9},{5... | collective-permute-start | bytes 589832 | tf_op jit(solution)/shard_map/ppermute | solution.py:230
  9.8 3.0 %collective-permute-start.4 = (bf16[96,1024]{1,0:T(8,128)(2,1)}, bf16[96,1024]{1,0:T(8,128)(2,1)S(1)}, u32[]{:S(2)}, u32[]{:S(2)}) collective-permute-start(bf16[96,1024]{1,0:T(8,128)(2,1)} %get-tuple-element.55), channel_id=1, source_target_pairs={{0,28},{4,24},{8,20},{12,16},{16,12},{20,8},{24,4},{28,0},{1,29},{... | collective-permute-start | bytes 589832 | tf_op jit(solution)/shard_map/ppermute | solution.py:230
  12.8 0.6 collective-permute-done.refs_0_
  13.3 0.3 collective-permute-start.5
  13.6 2.6 %collective-permute-done.1.refs_1_ = bf16[96,1024]{1,0:T(8,128)(2,1)S(1)} collective-permute-done((bf16[96,1024]{1,0:T(8,128)(2,1)}, bf16[96,1024]{1,0:T(8,128)(2,1)S(1)}, u32[]{:S(2)}, u32[]{:S(2)}) %collective-permute-start.1) | collective-permute-done | bytes 196640 | tf_op jit(solution)/shard_map/ppermute | solution.py:230
  16.3 0.3 collective-permute-start.6
  16.6 0.9 %copy-done.4 = bf16[96,1024]{1,0:T(8,128)(2,1)S(1)} copy-done((bf16[96,1024]{1,0:T(8,128)(2,1)S(1)}, bf16[96,1024]{1,0:T(8,128)(2,1)}, u32[]{:S(2)}) %copy-start.4) | copy-done | bytes 196632
  17.5 2.5 %collective-permute-done.2.refs_2_ = bf16[96,1024]{1,0:T(8,128)(2,1)S(1)} collective-permute-done((bf16[96,1024]{1,0:T(8,128)(2,1)}, bf16[96,1024]{1,0:T(8,128)(2,1)S(1)}, u32[]{:S(2)}, u32[]{:S(2)}) %collective-permute-start.2) | collective-permute-done | bytes 196640 | tf_op jit(solution)/shard_map/ppermute | solution.py:230
  20.1 3.2 %sooner.1 = (f32[512,1024]{1,0:T(8,128)S(1)}, f32[1024,512]{1,0:T(8,128)S(1)}, bf16[480,1024]{1,0:T(8,128)(2,1)S(1)}, bf16[480,128]{1,0:T(8,128)(2,1)S(1)}) custom-call(s32[1]{0:T(128)} %bitcast.1.place, bf16[512,1024]{1,0:T(8,128)(2,1)S(1)} %bitcast.8, bf16[1024,512]{1,0:T(8,128)(2,1)S(1)} %bitcast.11, bf16[96,1024]{1,0:T(8,128)(2,1)S(1)} %collective-permute-done.refs_0_, ...), custom_call_target="tpu_custom_call" | custom-call | flops 2013265920 | bytes 6160384 | tf_op jit(solution)/shard_map/sooner/pallas_call | solution.py:342
  23.3 0.5 collective-permute-done.4.refs_0_
  23.9 3.3 %collective-permute-done.5.refs_1_ = bf16[96,1024]{1,0:T(8,128)(2,1)S(1)} collective-permute-done((bf16[96,1024]{1,0:T(8,128)(2,1)}, bf16[96,1024]{1,0:T(8,128)(2,1)S(1)}, u32[]{:S(2)}, u32[]{:S(2)}) %collective-permute-start.5) | collective-permute-done | bytes 196640 | tf_op jit(solution)/shard_map/ppermute | solution.py:230
  27.2 2.9 %later.1 = (bf16[256,1024]{1,0:T(8,128)(2,1)S(1)}, bf16[256,1024]{1,0:T(8,128)(2,1)S(1)}, bf16[256,1024]{1,0:T(8,128)(2,1)S(1)}, bf16[256,1024]{1,0:T(8,128)(2,1...) custom-call(s32[1]{0:T(128)} %bitcast.1.place, bf16[512,1024]{1,0:T(8,128)(2,1)S(1)} %bitcast.9, ...), custom_call_target="tpu_custom_call" | custom-call | flops 1207959552 | bytes 5373952 | tf_op jit(solution)/shard_map/later/pallas_call | solution.py:342
  30.1 0.7 collective-permute-start.16
  30.8 4.3 %collective-permute-start.15 = (bf16[256,1024]{1,0:T(8,128)(2,1)S(1)}, bf16[256,1024]{1,0:T(8,128)(2,1)S(1)}, u32[]{:S(2)}, u32[]{:S(2)}) collective-permute-start(bf16[256,1024]{1,0:T(8,128)(2,1)S(1)} %get-tuple-element.82), channel_id=1, source_target_pairs={{0,1},{1,2},{4,5},{5,6},{8,9},{9,10},{12,13},{13,14},{16,17},{17,1... | collective-permute-start | bytes 1572872 | tf_op jit(solution)/shard_map/ppermute | solution.py:256
  35.2 1.0 %back.1 = (bf16[96,640]{1,0:T(8,128)(2,1)S(1)}, bf16[96,640]{1,0:T(8,128)(2,1)S(1)}, bf16[96,640]{1,0:T(8,128)(2,1)S(1)}, bf16[96,640]{1,0:T(8,128)(2,1)S(1)}, b...) custom-call(bf16[512,1024]{1,0:T(8,128)(2,1)S(1)} %bitcast.10, ...), custom_call_target="tpu_custom_call" | custom-call | flops 1 | bytes 1 | tf_op jit(solution)/shard_map/back/pallas_call | solution.py:357
  36.2 1.5 %collective-permute-start.7 = (bf16[96,640]{1,0:T(8,128)(2,1)S(1)}, bf16[96,640]{1,0:T(8,128)(2,1)S(1)}, u32[]{:S(2)}, u32[]{:S(2)}) collective-permute-start(bf16[96,640]{1,0:T(8,128)(2,1)S(1)} %get-tuple-element.63), channel_id=1, source_target_pairs={{0,16},{4,20},{8,24},{12,28},{16,0},{20,4},{24,8},{28,12},{1,17},{... | collective-permute-start | bytes 368648 | tf_op jit(solution)/shard_map/ppermute | solution.py:230
  37.7 1.5 %collective-permute-start.8 = (bf16[96,640]{1,0:T(8,128)(2,1)S(1)}, bf16[96,640]{1,0:T(8,128)(2,1)S(1)}, u32[]{:S(2)}, u32[]{:S(2)}) collective-permute-start(bf16[96,640]{1,0:T(8,128)(2,1)S(1)} %get-tuple-element.64), channel_id=1, source_target_pairs={{0,8},{4,12},{8,0},{12,4},{16,24},{20,28},{24,16},{28,20},{1,9},{5... | collective-permute-start | bytes 368648 | tf_op jit(solution)/shard_map/ppermute | solution.py:230
  39.2 1.4 %collective-permute-start.11 = (bf16[256,1024]{1,0:T(8,128)(2,1)S(1)}, bf16[256,1024]{1,0:T(8,128)(2,1)S(1)}, u32[]{:S(2)}, u32[]{:S(2)}) collective-permute-start(bf16[256,1024]{1,0:T(8,128)(2,1)S(1)} %get-tuple-element.71), channel_id=1, source_target_pairs={{0,2},{1,0},{2,3},{3,1},{4,6},{5,4},{6,7},{7,5},{8,10},{9,8},{10,1... | collective-permute-start | bytes 1572872 | tf_op jit(solution)/shard_map/ppermute | solution.py:258
  40.6 0.7 collective-permute-done.7.refs_0_
  41.3 2.2 %collective-permute-start.9 = (bf16[96,640]{1,0:T(8,128)(2,1)S(1)}, bf16[96,640]{1,0:T(8,128)(2,1)S(1)}, u32[]{:S(2)}, u32[]{:S(2)}) collective-permute-start(bf16[96,640]{1,0:T(8,128)(2,1)S(1)} %get-tuple-element.65), channel_id=1, source_target_pairs={{0,24},{4,28},{8,16},{12,20},{16,8},{20,12},{24,0},{28,4},{1,25},{... | collective-permute-start | bytes 368648 | tf_op jit(solution)/shard_map/ppermute | solution.py:230
  43.6 3.6 %collective-permute-done.9.refs_2_ = bf16[96,640]{1,0:T(8,128)(2,1)S(1)} collective-permute-done((bf16[96,640]{1,0:T(8,128)(2,1)S(1)}, bf16[96,640]{1,0:T(8,128)(2,1)S(1)}, u32[]{:S(2)}, u32[]{:S(2)}) %collective-permute-start.9) | collective-permute-done | bytes 122912 | tf_op jit(solution)/shard_map/ppermute | solution.py:230
  47.2 2.6 %collective-permute-done.10.refs_3_ = bf16[96,640]{1,0:T(8,128)(2,1)S(1)} collective-permute-done((bf16[96,640]{1,0:T(8,128)(2,1)S(1)}, bf16[96,640]{1,0:T(8,128)(2,1)S(1)}, u32[]{:S(2)}, u32[]{:S(2)}) %collective-permute-start.10) | collective-permute-done | bytes 122912 | tf_op jit(solution)/shard_map/ppermute | solution.py:230
  49.7 0.4 pass.1
  50.1 11.0 %collective-permute-start.17 = (bf16[256,1024]{1,0:T(8,128)(2,1)S(1)}, bf16[256,1024]{1,0:T(8,128)(2,1)S(1)}, u32[]{:S(2)}, u32[]{:S(2)}) collective-permute-start(bf16[256,1024]{1,0:T(8,128)(2,1)S(1)} %get-tuple-element.87), channel_id=1, source_target_pairs={{0,1},{3,2},{1,3},{2,0},{4,5},{7,6},{5,7},{6,4},{8,9},{11,10},{9,1... | collective-permute-start | bytes 1572872 | tf_op jit(solution)/shard_map/ppermute | solution.py:269
  61.1 2.5 %collective-permute-start.13 = (bf16[96,640]{1,0:T(8,128)(2,1)S(1)}, bf16[96,640]{1,0:T(8,128)(2,1)S(1)}, u32[]{:S(2)}, u32[]{:S(2)}) collective-permute-start(bf16[96,640]{1,0:T(8,128)(2,1)S(1)} %get-tuple-element.77), channel_id=1, source_target_pairs={{0,12},{4,8},{8,4},{12,0},{16,28},{20,24},{24,20},{28,16},{1,13},{... | collective-permute-start | bytes 368648 | tf_op jit(solution)/shard_map/ppermute | solution.py:230
  63.7 3.0 %collective-permute-done.12.refs_4_ = bf16[96,640]{1,0:T(8,128)(2,1)S(1)} collective-permute-done((bf16[96,640]{1,0:T(8,128)(2,1)S(1)}, bf16[96,640]{1,0:T(8,128)(2,1)S(1)}, u32[]{:S(2)}, u32[]{:S(2)}) %collective-permute-start.12) | collective-permute-done | bytes 122912 | tf_op jit(solution)/shard_map/ppermute | solution.py:230
  66.6 0.1 collective-permute-done.13.refs_5_
  66.8 2.6 %finish.1 = (bf16[576,512]{1,0:T(8,128)(2,1)}, bf16[576]{0:T(1024)(128)(2,1)}) custom-call(s32[1,576]{1,0:T(1,128)S(1)} %copy-done.5, bf16[576]{0:T(1024)(128)(2,1)S(1)} %copy-done.6, bf16[576,512]{1,0:T(8,128)(2,1)S(1)} %copy-done.2, f32[1,512]{1,0:T(1,128)S(1)} %bitcast.14, bf16[576,512]{1,0:T(8,128)(2,1)S(1)} %copy-done.3, ...), custom_call_target="tpu_custom_call" | custom-call | flops 1 | bytes 1 | tf_op jit(solution)/shard_map/finish/pallas_call | solution.py:377
  69.4 1.2 %collective-permute-done.17.last_ref = bf16[256,1024]{1,0:T(8,128)(2,1)S(1)} collective-permute-done((bf16[256,1024]{1,0:T(8,128)(2,1)S(1)}, bf16[256,1024]{1,0:T(8,128)(2,1)S(1)}, u32[]{:S(2)}, u32[]{:S(2)}) %collective-permute-start.17) | collective-permute-done | bytes 524320 | tf_op jit(solution)/shard_map/ppermute | solution.py:269
  70.6 1.1 %total.1 = (f32[128,1024]{1,0:T(8,128)}, f32[256,512]{1,0:T(8,128)}) custom-call(f32[256,1024]{1,0:T(8,128)S(1)} %get-tuple-element.85.sum_ref, bf16[256,1024]{1,0:T(8,128)(2,1)S(1)} %collective-permute-done.11.cycle_ref, bf16[256,1024]{1,0:T(8,128)(2,1)S(1)} %collective-permute-done.17.last_ref), custom_call_target="tpu_custom_call" | custom-call | flops 1 | bytes 1 | tf_op jit(solution)/shard_map/total/pallas_call | solution.py:272
  (28 shorter events, 0.1 us)
Async XLA Ops:
  0.6 19.4 %copy-start.1 = (bf16[1,1024,512]{2,1,0:T(8,128)(2,1)S(1)}, bf16[1,1024,512]{2,1,0:T(8,128)(2,1)}, u32[]{:S(2)}) copy-start(bf16[1,1024,512]{2,1,0:T(8,128)(2,1)} %param.10) | copy-start | bytes 3145732
  0.6 19.4 %copy-start = (bf16[1,512,1024]{2,1,0:T(8,128)(2,1)S(1)}, bf16[1,512,1024]{2,1,0:T(8,128)(2,1)}, u32[]{:S(2)}) copy-start(bf16[1,512,1024]{2,1,0:T(8,128)(2,1)} %param.9) | copy-start | bytes 3145732
  5.2 8.1 %collective-permute-start = (bf16[96,1024]{1,0:T(8,128)(2,1)}, bf16[96,1024]{1,0:T(8,128)(2,1)S(1)}, u32[]{:S(2)}, u32[]{:S(2)}) collective-permute-start(bf16[96,1024]{1,0:T(8,128)(2,1)} %get-tuple-element.48), channel_id=1, source_target_pairs={{0,16},{4,20},{8,24},{12,28},{16,0},{20,4},{24,8},{28,12},{1,17},{... | collective-permute-start | bytes 589832 | tf_op jit(solution)/shard_map/ppermute | solution.py:230
  8.2 8.0 %collective-permute-start.1 = (bf16[96,1024]{1,0:T(8,128)(2,1)}, bf16[96,1024]{1,0:T(8,128)(2,1)S(1)}, u32[]{:S(2)}, u32[]{:S(2)}) collective-permute-start(bf16[96,1024]{1,0:T(8,128)(2,1)} %get-tuple-element.49), channel_id=1, source_target_pairs={{0,8},{4,12},{8,0},{12,4},{16,24},{20,28},{24,16},{28,20},{1,9},{5... | collective-permute-start | bytes 589832 | tf_op jit(solution)/shard_map/ppermute | solution.py:230
  9.7 10.3 %collective-permute-start.2 = (bf16[96,1024]{1,0:T(8,128)(2,1)}, bf16[96,1024]{1,0:T(8,128)(2,1)S(1)}, u32[]{:S(2)}, u32[]{:S(2)}) collective-permute-start(bf16[96,1024]{1,0:T(8,128)(2,1)} %get-tuple-element.50), channel_id=1, source_target_pairs={{0,24},{4,28},{8,16},{12,20},{16,8},{20,12},{24,0},{28,4},{1,25},{... | collective-permute-start | bytes 589832 | tf_op jit(solution)/shard_map/ppermute | solution.py:230
  9.8 10.3 %collective-permute-start.3 = (bf16[96,1024]{1,0:T(8,128)(2,1)}, bf16[96,1024]{1,0:T(8,128)(2,1)S(1)}, u32[]{:S(2)}, u32[]{:S(2)}) collective-permute-start(bf16[96,1024]{1,0:T(8,128)(2,1)} %get-tuple-element.51), channel_id=1, source_target_pairs={{0,4},{4,0},{8,12},{12,8},{16,20},{20,16},{24,28},{28,24},{1,5},{5... | collective-permute-start | bytes 589832 | tf_op jit(solution)/shard_map/ppermute | solution.py:230
  9.8 14.1 %collective-permute-start.4 = (bf16[96,1024]{1,0:T(8,128)(2,1)}, bf16[96,1024]{1,0:T(8,128)(2,1)S(1)}, u32[]{:S(2)}, u32[]{:S(2)}) collective-permute-start(bf16[96,1024]{1,0:T(8,128)(2,1)} %get-tuple-element.55), channel_id=1, source_target_pairs={{0,28},{4,24},{8,20},{12,16},{16,12},{20,8},{24,4},{28,0},{1,29},{... | collective-permute-start | bytes 589832 | tf_op jit(solution)/shard_map/ppermute | solution.py:230
  13.3 13.8 %collective-permute-start.5 = (bf16[96,1024]{1,0:T(8,128)(2,1)}, bf16[96,1024]{1,0:T(8,128)(2,1)S(1)}, u32[]{:S(2)}, u32[]{:S(2)}) collective-permute-start(bf16[96,1024]{1,0:T(8,128)(2,1)} %get-tuple-element.56), channel_id=1, source_target_pairs={{0,20},{4,16},{8,28},{12,24},{16,4},{20,0},{24,12},{28,8},{1,21},{... | collective-permute-start | bytes 589832 | tf_op jit(solution)/shard_map/ppermute | solution.py:230
  16.3 10.9 %collective-permute-start.6 = (bf16[96,1024]{1,0:T(8,128)(2,1)}, bf16[96,1024]{1,0:T(8,128)(2,1)S(1)}, u32[]{:S(2)}, u32[]{:S(2)}) collective-permute-start(bf16[96,1024]{1,0:T(8,128)(2,1)} %get-tuple-element.57), channel_id=1, source_target_pairs={{0,12},{4,8},{8,4},{12,0},{16,28},{20,24},{24,20},{28,16},{1,13},{... | collective-permute-start | bytes 589832 | tf_op jit(solution)/shard_map/ppermute | solution.py:230
  16.6 0.9 %copy-start.4 = (bf16[96,1024]{1,0:T(8,128)(2,1)S(1)}, bf16[96,1024]{1,0:T(8,128)(2,1)}, u32[]{:S(2)}) copy-start(bf16[96,1024]{1,0:T(8,128)(2,1)} %get-tuple-element.52.block_ref) | copy-start | bytes 589828
  30.1 19.6 %collective-permute-start.16 = (bf16[256,1024]{1,0:T(8,128)(2,1)S(1)}, bf16[256,1024]{1,0:T(8,128)(2,1)S(1)}, u32[]{:S(2)}, u32[]{:S(2)}) collective-permute-start(bf16[256,1024]{1,0:T(8,128)(2,1)S(1)} %get-tuple-element.82), channel_id=1, source_target_pairs={{3,2},{2,1},{7,6},{6,5},{11,10},{10,9},{15,14},{14,13},{19,18},{18... | collective-permute-start | bytes 1572872 | tf_op jit(solution)/shard_map/ppermute | solution.py:257
  30.8 18.9 %collective-permute-start.15 = (bf16[256,1024]{1,0:T(8,128)(2,1)S(1)}, bf16[256,1024]{1,0:T(8,128)(2,1)S(1)}, u32[]{:S(2)}, u32[]{:S(2)}) collective-permute-start(bf16[256,1024]{1,0:T(8,128)(2,1)S(1)} %get-tuple-element.82), channel_id=1, source_target_pairs={{0,1},{1,2},{4,5},{5,6},{8,9},{9,10},{12,13},{13,14},{16,17},{17,1... | collective-permute-start | bytes 1572872 | tf_op jit(solution)/shard_map/ppermute | solution.py:256
  35.1 31.6 %copy-start.2 = (bf16[576,512]{1,0:T(8,128)(2,1)S(1)}, bf16[576,512]{1,0:T(8,128)(2,1)}, u32[]{:S(2)}) copy-start(bf16[576,512]{1,0:T(8,128)(2,1)} %tok_ref.1) | copy-start | bytes 1769476
  35.1 31.6 %copy-start.3 = (bf16[576,512]{1,0:T(8,128)(2,1)S(1)}, bf16[576,512]{1,0:T(8,128)(2,1)}, u32[]{:S(2)}) copy-start(bf16[576,512]{1,0:T(8,128)(2,1)} %go_ref.1) | copy-start | bytes 1769476
  35.1 31.6 %copy-start.5 = (s32[1,576]{1,0:T(1,128)S(1)}, s32[1,576]{1,0:T(1,128)}, u32[]{:S(2)}) copy-start(s32[1,576]{1,0:T(1,128)} %get-tuple-element.47.target_ref) | copy-start | bytes 6916
  35.1 31.6 %copy-start.6 = (bf16[576]{0:T(1024)(128)(2,1)S(1)}, bf16[576]{0:T(1024)(128)(2,1)}, u32[]{:S(2)}) copy-start(bf16[576]{0:T(1024)(128)(2,1)} %gate_ref.1) | copy-start | bytes 3460
  35.1 31.6 %copy-start.7 = (f32[512]{0:T(512)S(1)}, f32[512]{0:T(512)}, u32[]{:S(2)}) copy-start(f32[512]{0:T(512)} %param.8) | copy-start | bytes 6148
  36.2 5.1 %collective-permute-start.7 = (bf16[96,640]{1,0:T(8,128)(2,1)S(1)}, bf16[96,640]{1,0:T(8,128)(2,1)S(1)}, u32[]{:S(2)}, u32[]{:S(2)}) collective-permute-start(bf16[96,640]{1,0:T(8,128)(2,1)S(1)} %get-tuple-element.63), channel_id=1, source_target_pairs={{0,16},{4,20},{8,24},{12,28},{16,0},{20,4},{24,8},{28,12},{1,17},{... | collective-permute-start | bytes 368648 | tf_op jit(solution)/shard_map/ppermute | solution.py:230
  37.7 5.8 %collective-permute-start.8 = (bf16[96,640]{1,0:T(8,128)(2,1)S(1)}, bf16[96,640]{1,0:T(8,128)(2,1)S(1)}, u32[]{:S(2)}, u32[]{:S(2)}) collective-permute-start(bf16[96,640]{1,0:T(8,128)(2,1)S(1)} %get-tuple-element.64), channel_id=1, source_target_pairs={{0,8},{4,12},{8,0},{12,4},{16,24},{20,28},{24,16},{28,20},{1,9},{5... | collective-permute-start | bytes 368648 | tf_op jit(solution)/shard_map/ppermute | solution.py:230
  39.2 21.9 %collective-permute-start.11 = (bf16[256,1024]{1,0:T(8,128)(2,1)S(1)}, bf16[256,1024]{1,0:T(8,128)(2,1)S(1)}, u32[]{:S(2)}, u32[]{:S(2)}) collective-permute-start(bf16[256,1024]{1,0:T(8,128)(2,1)S(1)} %get-tuple-element.71), channel_id=1, source_target_pairs={{0,2},{1,0},{2,3},{3,1},{4,6},{5,4},{6,7},{7,5},{8,10},{9,8},{10,1... | collective-permute-start | bytes 1572872 | tf_op jit(solution)/shard_map/ppermute | solution.py:258
  41.3 5.8 %collective-permute-start.9 = (bf16[96,640]{1,0:T(8,128)(2,1)S(1)}, bf16[96,640]{1,0:T(8,128)(2,1)S(1)}, u32[]{:S(2)}, u32[]{:S(2)}) collective-permute-start(bf16[96,640]{1,0:T(8,128)(2,1)S(1)} %get-tuple-element.65), channel_id=1, source_target_pairs={{0,24},{4,28},{8,16},{12,20},{16,8},{20,12},{24,0},{28,4},{1,25},{... | collective-permute-start | bytes 368648 | tf_op jit(solution)/shard_map/ppermute | solution.py:230
  43.6 6.2 %collective-permute-start.10 = (bf16[96,640]{1,0:T(8,128)(2,1)S(1)}, bf16[96,640]{1,0:T(8,128)(2,1)S(1)}, u32[]{:S(2)}, u32[]{:S(2)}) collective-permute-start(bf16[96,640]{1,0:T(8,128)(2,1)S(1)} %get-tuple-element.66), channel_id=1, source_target_pairs={{0,28},{4,24},{8,20},{12,16},{16,12},{20,8},{24,4},{28,0},{1,29},{... | collective-permute-start | bytes 368648 | tf_op jit(solution)/shard_map/ppermute | solution.py:230
  50.1 20.5 %collective-permute-start.17 = (bf16[256,1024]{1,0:T(8,128)(2,1)S(1)}, bf16[256,1024]{1,0:T(8,128)(2,1)S(1)}, u32[]{:S(2)}, u32[]{:S(2)}) collective-permute-start(bf16[256,1024]{1,0:T(8,128)(2,1)S(1)} %get-tuple-element.87), channel_id=1, source_target_pairs={{0,1},{3,2},{1,3},{2,0},{4,5},{7,6},{5,7},{6,4},{8,9},{11,10},{9,1... | collective-permute-start | bytes 1572872 | tf_op jit(solution)/shard_map/ppermute | solution.py:269
  61.1 5.5 %collective-permute-start.12 = (bf16[96,640]{1,0:T(8,128)(2,1)S(1)}, bf16[96,640]{1,0:T(8,128)(2,1)S(1)}, u32[]{:S(2)}, u32[]{:S(2)}) collective-permute-start(bf16[96,640]{1,0:T(8,128)(2,1)S(1)} %get-tuple-element.76), channel_id=1, source_target_pairs={{0,20},{4,16},{8,28},{12,24},{16,4},{20,0},{24,12},{28,8},{1,21},{... | collective-permute-start | bytes 368648 | tf_op jit(solution)/shard_map/ppermute | solution.py:230
  61.1 5.6 %collective-permute-start.13 = (bf16[96,640]{1,0:T(8,128)(2,1)S(1)}, bf16[96,640]{1,0:T(8,128)(2,1)S(1)}, u32[]{:S(2)}, u32[]{:S(2)}) collective-permute-start(bf16[96,640]{1,0:T(8,128)(2,1)S(1)} %get-tuple-element.77), channel_id=1, source_target_pairs={{0,12},{4,8},{8,4},{12,0},{16,28},{20,24},{24,20},{28,16},{1,13},{... | collective-permute-start | bytes 368648 | tf_op jit(solution)/shard_map/ppermute | solution.py:230
  63.7 3.1 %collective-permute-start.14 = (bf16[96,640]{1,0:T(8,128)(2,1)S(1)}, bf16[96,640]{1,0:T(8,128)(2,1)S(1)}, u32[]{:S(2)}, u32[]{:S(2)}) collective-permute-start(bf16[96,640]{1,0:T(8,128)(2,1)S(1)} %get-tuple-element.78), channel_id=1, source_target_pairs={{0,4},{4,0},{8,12},{12,8},{16,20},{20,16},{24,28},{28,24},{1,5},{5... | collective-permute-start | bytes 368648 | tf_op jit(solution)/shard_map/ppermute | solution.py:230

commit v9 on v8

--- a/solution.py
+++ b/solution.py
@@ -51,13 +51,37 @@
     return copies
 
 
+def put_blocks(first, target, gate, tok_ref, gain_ref, go_ref, sent_ref, outs, sems):
+    capacity, width = outs[0].shape[0], tok_ref.shape[1]
+    count = len(outs)
+    hit = lax.broadcasted_iota(jnp.int32, (count * capacity, target.shape[1]), 0) == (
+        target - first * capacity
+    )
+    gate = gate.astype(F32).reshape(target.shape)
+    scaled, _ = normalize(tok_ref[...])
+    normed = (scaled * gain_ref[...]).astype(BF16)
+    spans = [pl.ds(j * capacity, capacity) for j in range(count)]
+    stores = []
+    for part, (weight, values) in enumerate(((gate, go_ref[...]), (1.0, normed))):
+        columns = pl.ds((1 - part) * width, width)
+        sent_ref[:, columns] = dot(jnp.where(hit, weight, 0.0).astype(BF16), values).astype(BF16)
+        if capacity % 16:
+            for j in range(count):
+                outs[j][:, columns] = sent_ref[spans[j], columns]
+        else:
+            stores += start_copies(
+                [(sent_ref.at[spans[j], columns], outs[j].at[:, columns]) for j in range(count)],
+                sems.at[part],
+            )
+    for copy in stores:
+        copy.wait()
+
+
 def place_kernel(
     sources, capacity, me, place, ids_hbm, gate_hbm, tok_hbm, gain_hbm, go_hbm, target_ref, *refs
 ):
-    outs = refs[:sources]
-    wide_ref, ids_ref, gate_ref, tok_ref, gain_ref, go_ref, sent_ref, in_sems, out_sems = refs[sources:]
-    rows = sources * capacity
-    tok_rows, width = tok_ref.shape
+    *outs, wide_ref, ids_ref, gate_ref, tok_ref, gain_ref, go_ref, sent_ref, in_sems, out_sems = refs
+    tok_rows = tok_ref.shape[0]
     loads = start_copies(
         [(ids_hbm, ids_ref), (tok_hbm, tok_ref), (gain_hbm, gain_ref), (gate_hbm, gate_ref), (go_hbm, go_ref)],
         in_sems,
@@ -86,28 +110,14 @@
         end = min(LANES, tok_rows - c)
         target = jnp.where(rank < capacity, block * capacity + rank, -1)
         target_ref[:, c : c + end] = target[:, :end]
-    target = target_ref[...]
     for copy in loads[1:]:
         copy.wait()
-    hit = lax.broadcasted_iota(jnp.int32, (rows, tok_rows), 0) == target
-    gate = gate_ref[...].astype(F32).reshape(1, tok_rows)
-    scaled, _ = normalize(tok_ref[...])
-    normed = (scaled * gain_ref[...]).astype(BF16)
-    stores = []
-    for part, (weight, values) in enumerate(((gate, go_ref[...]), (1.0, normed))):
-        columns = pl.ds((1 - part) * width, width)
-        sent_ref[:, columns] = dot(jnp.where(hit, weight, 0.0).astype(BF16), values).astype(BF16)
-        spans = [pl.ds(j * capacity, capacity) for j in range(sources)]
-        if capacity % 16:
-            for j in range(sources):
-                outs[j][:, columns] = sent_ref[spans[j], columns]
-        else:
-            stores += start_copies(
-                [(sent_ref.at[spans[j], columns], outs[j].at[:, columns]) for j in range(sources)],
-                out_sems.at[part],
-            )
-    for copy in stores:
-        copy.wait()
+    put_blocks(0, target_ref[...], gate_ref[...], tok_ref, gain_ref, go_ref, sent_ref, outs, out_sems)
+
+
+def rest_kernel(first, target_ref, gate_ref, tok_ref, gain_ref, go_ref, *refs):
+    *outs, sent_ref, sems = refs
+    put_blocks(first, target_ref[...], gate_ref[...], tok_ref, gain_ref, go_ref, sent_ref, outs, sems)
 
 
 def keep_kernel(block_ref, out_ref):
@@ -125,8 +135,9 @@
 
 
 def shard_order(place):
-    second = jnp.where(place < 2, 2 - 2 * place, 7 - 2 * place)
-    return [3 - place, second, 3 - second, place]
+    first = jnp.where(lax.rem(place, 2) == 0, 3, 0)
+    second = jnp.where(place < 2, 2, 1)
+    return [first, second, 6 - first - second - place, place]
 
 
 def expert_work(order, blocks, w_in_ref, w_out_ref, gpre_ref, extra_ref, rows_ref, turned_ref, put):
@@ -232,17 +243,21 @@
     ]
 
 
-def pass_kernel(place, up_ref, down_ref, third_ref, own_ref, out_ref, sum_ref):
-    up, down = up_ref[...].astype(F32), down_ref[...].astype(F32)
-    low = place[0] == 1
-    out_ref[...] = (third_ref[...].astype(F32) + jnp.where(low, up, down)).astype(BF16)
-    sum_ref[...] = own_ref[...].astype(F32) + jnp.where(low, down, up)
-
-
-def total_kernel(sum_ref, cycle_ref, last_ref, in_ref, out_ref):
+def start_kernel(own_ref, middle_ref, out_ref):
+    out_ref[...] = own_ref[...].astype(F32) + middle_ref[...].astype(F32)
+
+
+def pass_kernel(place, swapped_ref, third_ref, sum_ref, out_ref, more_ref):
+    swapped = swapped_ref[...].astype(F32)
+    onward = jnp.where((place[0] == 1) | (place[0] == 2), swapped, 0.0)
+    out_ref[...] = (third_ref[...].astype(F32) + onward).astype(BF16)
+    more_ref[...] = sum_ref[...] + (swapped - onward)
+
+
+def total_kernel(sum_ref, across_ref, last_ref, in_ref, out_ref):
     piece_d, half = in_ref.shape[0], out_ref.shape[0] // 2
     width = out_ref.shape[1]
-    total = sum_ref[...] + cycle_ref[...].astype(F32) + last_ref[...].astype(F32)
+    total = sum_ref[...] + across_ref[...].astype(F32) + last_ref[...].astype(F32)
     in_ref[...] = total[:piece_d]
     out_ref[:half, :] = total[piece_d:, :width]
     out_ref[half:, :] = total[piece_d:, width:]
@@ -253,21 +268,24 @@
     piece_d = width // LINE
     half = len(returned) // 2
     order = block_order(len(returned))
-    up = lax.ppermute(first, "dp", [(0, 1), (1, 2)])
-    down = lax.ppermute(first, "dp", [(3, 2), (2, 1)])
-    cycle = lax.ppermute(second, "dp", [(0, 2), (1, 0), (2, 3), (3, 1)])
+    middle = lax.ppermute(second, "dp", [(1, 2), (2, 1)])
+    swapped = lax.ppermute(first, "dp", [(0, 1), (1, 0), (2, 3), (3, 2)])
+    across = lax.ppermute(second, "dp", [(0, 2), (3, 1)])
     back = swap_blocks(returned[:half], order[:half])
     third, *back = lax.optimization_barrier((third, *back))
+    (some,) = kernel_call(
+        start_kernel, "start", 1, 1, [jax.ShapeDtypeStruct(own.shape, F32)], [vmem] * 2
+    )(own, middle)
     passed, most = kernel_call(
         pass_kernel,
         "pass",
         1,
         1,
         [jax.ShapeDtypeStruct(own.shape, BF16), jax.ShapeDtypeStruct(own.shape, F32)],
-        [smem] + [vmem] * 4,
-    )(place, up, down, third, own)
+        [smem] + [vmem] * 3,
+    )(place, swapped, third, some)
     last = lax.ppermute(passed, "dp", [(0, 1), (3, 2), (1, 3), (2, 0)])
-    cycle, *rest = lax.optimization_barrier((cycle, *returned[half:]))
+    across, *rest = lax.optimization_barrier((across, *returned[half:]))
     back += swap_blocks(rest, order[half:])
     sums = kernel_call(
         total_kernel,
@@ -279,7 +297,7 @@
             jax.ShapeDtypeStruct((2 * (rows - piece_d), width), F32),
         ],
         [vmem] * 3,
-    )(most, cycle, last)
+    )(most, across, last)
     return *sums, back
 
 
@@ -300,13 +318,14 @@
     block_place = vmem if capacity % 16 else anywhere
     io_bytes = 2 * (2 * tok_rows * width + 2 * rows * width)
 
+    soon = sources // 2
+    blocks = [shape((capacity, 2 * width), BF16)] * soon
     target, *sent = kernel_call(
         functools.partial(place_kernel, sources, capacity),
         "place",
-        4 * rows * tok_rows * width,
+        2 * rows * tok_rows * width,
         io_bytes,
-        [shape((1, tok_rows), jnp.int32)]
-        + [shape((capacity, 2 * width), BF16)] * sources,
+        [shape((1, tok_rows), jnp.int32)] + blocks,
         [smem] * 2 + [hbm] * 5,
         [
             pltpu.VMEM((1, pl.cdiv(tok_rows, LANES) * LANES), jnp.int32),
@@ -315,13 +334,24 @@
             pltpu.VMEM((tok_rows, width), BF16),
             pltpu.VMEM((1, width), F32),
             pltpu.VMEM((tok_rows, width), BF16),
-            pltpu.VMEM((rows, 2 * width), BF16),
+            pltpu.VMEM((soon * capacity, 2 * width), BF16),
             sems((5,)),
-            sems((2, sources)),
+            sems((2, soon)),
         ],
-        places=[vmem] + [block_place] * sources,
+        places=[vmem] + [block_place] * soon,
         vmem_mib=56,
     )(me, place, ids_row, gate, tokens, gain_row, grad_out)
+    sent += kernel_call(
+        functools.partial(rest_kernel, soon),
+        "rest",
+        1,
+        1,
+        blocks,
+        [vmem] * 5,
+        [pltpu.VMEM((soon * capacity, 2 * width), BF16), sems((2, soon))],
+        places=[block_place] * soon,
+        vmem_mib=16,
+    )(target, gate, tokens, gain_row, grad_out)
     (kept,) = kernel_call(
         keep_kernel,
         "keep",
@@ -334,7 +364,7 @@
     arrived = swap_blocks(sent, block_order(sources))
     arrived[-1] = kept
 
-    late_set = list(range(3 * sources // 8, 6 * sources // 8))
+    late_set = list(range(sources // 2, 3 * sources // 4))
     soon_set = [j for j in range(sources) if j not in late_set]
 
     def work(kernel, name, members, outs, *sums):

time: 71.9 us -> 71.7 us (level)
  starting transfers between devices: 33.4 us -> 22.8 us
  waiting for transfers between devices: 20.8 us -> 29.4 us
  local copies, waits for them, and re-layouts: 0.96 us -> 2.07 us
  Pallas kernels: 15.7 us -> 16.5 us
    ppermute x1, starting transfers between devices: 11 us -> 0.54 us  [line_sums(): last = lax.ppermute(passed, 'dp', [(0, 1), (3, 2), (1, 3), (2, 0)])]
    ppermute x3, waiting for transfers between devices: 0.01 us -> 7.31 us  [the longest x1 7.3 us: line_sums(): across = lax.ppermute(second, 'dp', [(0, 2), (3, 1)])]
    ppermute x1, waiting for transfers between devices: 1.24 us -> 4.3 us  [line_sums(): last = lax.ppermute(passed, 'dp', [(0, 1), (3, 2), (1, 3), (2, 0)])]
    ppermute x14, waiting for transfers between devices: 19.5 us -> 17.7 us  [swap_blocks(): lax.ppermute(block, 'space', [(i, i ^ k) for i in devices])]
    pallas_call x0 -> x2, Pallas kernels: none -> 1.42 us  [the longest x1 1.31 us: body(): kernel_call(functools.partial(rest_kernel, soon), 'rest', 1, 1, blocks, [...]
    unnamed x16 -> x20, local copies, waits for them, and re-layouts: 0.96 us -> 2.07 us
  transfers between devices with their start and end apart: 18 -> 18, of which waited for: 11 -> 9; matrix products, arithmetic and copies ran while one was open for 0% -> 0% of each run, Pallas kernels for 10% -> 13%
where the time goes in v9:
time: 71.7 us; the launch traced here: 71.5 us
  waiting for transfers between devices  29.4 us (41%)
  starting transfers between devices  22.8 us (32%)
  Pallas kernels  16.5 us (23%)
  local copies, waits for them, and re-layouts  2.07 us (3%)
  between operations  0.8 us (1%)
    ppermute x14, waiting for transfers between devices, swap_blocks(): lax.ppermute(block, 'space', [(i, i ^ k) for i in devices])  17.7 us
    ppermute x14, starting transfers between devices, swap_blocks(): lax.ppermute(block, 'space', [(i, i ^ k) for i in devices])  15.3 us
    ppermute x1, waiting for transfers between devices, line_sums(): across = lax.ppermute(second, 'dp', [(0, 2), (3, 1)])  7.3 us
    pallas_call x2, Pallas kernels, work(): kernel_call(functools.partial(kernel, count, groups), name, 8 * span * wi...  6.11 us
    ppermute x1, starting transfers between devices, line_sums(): swapped = lax.ppermute(first, 'dp', [(0, 1), (1, 0), (2, 3), (3, 2)])  4.46 us
    ppermute x1, waiting for transfers between devices, line_sums(): last = lax.ppermute(passed, 'dp', [(0, 1), (3, 2), (1, 3), (2, 0)])  4.3 us
    pallas_call x1, Pallas kernels, body(): kernel_call(functools.partial(place_kernel, sources, capacity), 'place',...  3.81 us
    pallas_call x1, Pallas kernels, body(): kernel_call(finish_kernel, 'finish', 1, 1, [shape((tok_rows, width), BF16...  2.59 us
  transfers between devices with their start and end apart: 18, of which 9 were waited for; matrix products, arithmetic and copies ran while one was open for 0% of the time, Pallas kernels for 13%

profile of v9, /device:TPU:0, one launch (start us, length us, event | category | flops | bytes accessed | tf_op | source)
XLA Modules:
  0.0 71.5 jit_solution(15726074338704653994)
XLA Ops:
  0.7 3.8 %place.1 = (s32[1,576]{1,0:T(1,128)}, bf16[96,1024]{1,0:T(8,128)(2,1)}, bf16[96,1024]{1,0:T(8,128)(2,1)}, bf16[96,1024]{1,0:T(8,128)(2,1)}, bf16[96,1024]{1,0:T(8,128)(2,1)}) custom-call(s32[1]{0:T(128)} %bitcast.me, s32[1]{0:T(128)} %bitcast.1.place, s32[1,576]{1,0:T(1,128)} %bitcast.18, bf16[576]{0:T(1024)(128)(2,1)} %gate_ref.3, ...), custom_call_target="tpu_custom_call" | custom-call | flops 452984832 | bytes 2752512 | tf_op jit(solution)/shard_map/place/pallas_call | solution.py:323
  4.5 3.0 %collective-permute-start = (bf16[96,1024]{1,0:T(8,128)(2,1)}, bf16[96,1024]{1,0:T(8,128)(2,1)S(1)}, u32[]{:S(2)}, u32[]{:S(2)}) collective-permute-start(bf16[96,1024]{1,0:T(8,128)(2,1)} %get-tuple-element.48), channel_id=1, source_target_pairs={{0,16},{4,20},{8,24},{12,28},{16,0},{20,4},{24,8},{28,12},{1,17},{... | collective-permute-start | bytes 589832 | tf_op jit(solution)/shard_map/ppermute | solution.py:241
  7.5 1.5 %collective-permute-start.1 = (bf16[96,1024]{1,0:T(8,128)(2,1)}, bf16[96,1024]{1,0:T(8,128)(2,1)S(1)}, u32[]{:S(2)}, u32[]{:S(2)}) collective-permute-start(bf16[96,1024]{1,0:T(8,128)(2,1)} %get-tuple-element.49), channel_id=1, source_target_pairs={{0,8},{4,12},{8,0},{12,4},{16,24},{20,28},{24,16},{28,20},{1,9},{5... | collective-permute-start | bytes 589832 | tf_op jit(solution)/shard_map/ppermute | solution.py:241
  9.1 1.5 %collective-permute-start.3 = (bf16[96,1024]{1,0:T(8,128)(2,1)}, bf16[96,1024]{1,0:T(8,128)(2,1)S(1)}, u32[]{:S(2)}, u32[]{:S(2)}) collective-permute-start(bf16[96,1024]{1,0:T(8,128)(2,1)} %get-tuple-element.51), channel_id=1, source_target_pairs={{0,28},{4,24},{8,20},{12,16},{16,12},{20,8},{24,4},{28,0},{1,29},{... | collective-permute-start | bytes 589832 | tf_op jit(solution)/shard_map/ppermute | solution.py:241
  10.5 0.7 copy-done.4
  11.2 0.7 copy-done.6
  11.9 0.7 copy-done.8
  12.6 1.3 %rest.1 = (bf16[96,1024]{1,0:T(8,128)(2,1)S(1)}, bf16[96,1024]{1,0:T(8,128)(2,1)S(1)}, bf16[96,1024]{1,0:T(8,128)(2,1)S(1)}, bf16[96,1024]{1,0:T(8,128)(2,1)S(1)}) custom-call(s32[1,576]{1,0:T(1,128)S(1)} %copy-done.4, bf16[576]{0:T(1024)(128)(2,1)S(1)} %copy-done.6, bf16[576,512]{1,0:T(8,128)(2,1)S(1)} %copy-done.1, f32[1,512]{1,0:T(1,128)S(1)} %bitcast.14, ...), custom_call_target="tpu_custom_call" | custom-call | flops 1 | bytes 1 | tf_op jit(solution)/shard_map/rest/pallas_call | solution.py:344
  13.9 1.6 %collective-permute-start.4 = (bf16[96,1024]{1,0:T(8,128)(2,1)S(1)}, bf16[96,1024]{1,0:T(8,128)(2,1)S(1)}, u32[]{:S(2)}, u32[]{:S(2)}) collective-permute-start(bf16[96,1024]{1,0:T(8,128)(2,1)S(1)} %get-tuple-element.52), channel_id=1, source_target_pairs={{0,4},{4,0},{8,12},{12,8},{16,20},{20,16},{24,28},{28,24},{1,5},{5... | collective-permute-start | bytes 589832 | tf_op jit(solution)/shard_map/ppermute | solution.py:241
  15.9 3.4 %collective-permute-done.2.refs_2_ = bf16[96,1024]{1,0:T(8,128)(2,1)S(1)} collective-permute-done((bf16[96,1024]{1,0:T(8,128)(2,1)}, bf16[96,1024]{1,0:T(8,128)(2,1)S(1)}, u32[]{:S(2)}, u32[]{:S(2)}) %collective-permute-start.2) | collective-permute-done | bytes 196640 | tf_op jit(solution)/shard_map/ppermute | solution.py:241
  19.3 3.8 %collective-permute-done.3.refs_3_ = bf16[96,1024]{1,0:T(8,128)(2,1)S(1)} collective-permute-done((bf16[96,1024]{1,0:T(8,128)(2,1)}, bf16[96,1024]{1,0:T(8,128)(2,1)S(1)}, u32[]{:S(2)}, u32[]{:S(2)}) %collective-permute-start.3) | collective-permute-done | bytes 196640 | tf_op jit(solution)/shard_map/ppermute | solution.py:241
  23.2 4.0 %sooner.1 = (f32[512,1024]{1,0:T(8,128)S(1)}, f32[1024,512]{1,0:T(8,128)S(1)}, bf16[576,1024]{1,0:T(8,128)(2,1)S(1)}, bf16[576,128]{1,0:T(8,128)(2,1)S(1)}) custom-call(s32[1]{0:T(128)} %bitcast.1.place, bf16[512,1024]{1,0:T(8,128)(2,1)S(1)} %bitcast.8, bf16[1024,512]{1,0:T(8,128)(2,1)S(1)} %bitcast.11, bf16[96,1024]{1,0:T(8,128)(2,1)S(1)} %collective-permute-done.refs_0_, ...), custom_call_target="tpu_custom_call" | custom-call | flops 2415919104 | bytes 6553600 | tf_op jit(solution)/shard_map/sooner/pallas_call | solution.py:372
  27.2 2.1 %later.1 = (bf16[256,1024]{1,0:T(8,128)(2,1)S(1)}, bf16[256,1024]{1,0:T(8,128)(2,1)S(1)}, bf16[256,1024]{1,0:T(8,128)(2,1)S(1)}, bf16[256,1024]{1,0:T(8,128)(2,1...) custom-call(s32[1]{0:T(128)} %bitcast.1.place, bf16[512,1024]{1,0:T(8,128)(2,1)S(1)} %bitcast.9, ...), custom_call_target="tpu_custom_call" | custom-call | flops 805306368 | bytes 4980736 | tf_op jit(solution)/shard_map/later/pallas_call | solution.py:372
  29.3 0.7 collective-permute-start.16
  30.0 4.5 %collective-permute-start.15 = (bf16[256,1024]{1,0:T(8,128)(2,1)S(1)}, bf16[256,1024]{1,0:T(8,128)(2,1)S(1)}, u32[]{:S(2)}, u32[]{:S(2)}) collective-permute-start(bf16[256,1024]{1,0:T(8,128)(2,1)S(1)} %get-tuple-element.82), channel_id=1, source_target_pairs={{0,1},{1,0},{2,3},{3,2},{4,5},{5,4},{6,7},{7,6},{8,9},{9,8},{10,11... | collective-permute-start | bytes 1572872 | tf_op jit(solution)/shard_map/ppermute | solution.py:272
  34.5 1.1 %back.1 = (bf16[96,640]{1,0:T(8,128)(2,1)S(1)}, bf16[96,640]{1,0:T(8,128)(2,1)S(1)}, bf16[96,640]{1,0:T(8,128)(2,1)S(1)}, bf16[96,640]{1,0:T(8,128)(2,1)S(1)}, b...) custom-call(bf16[512,1024]{1,0:T(8,128)(2,1)S(1)} %bitcast.10, ...), custom_call_target="tpu_custom_call" | custom-call | flops 1 | bytes 1 | tf_op jit(solution)/shard_map/back/pallas_call | solution.py:387
  35.6 1.1 %collective-permute-start.7 = (bf16[96,640]{1,0:T(8,128)(2,1)S(1)}, bf16[96,640]{1,0:T(8,128)(2,1)S(1)}, u32[]{:S(2)}, u32[]{:S(2)}) collective-permute-start(bf16[96,640]{1,0:T(8,128)(2,1)S(1)} %get-tuple-element.63), channel_id=1, source_target_pairs={{0,16},{4,20},{8,24},{12,28},{16,0},{20,4},{24,8},{28,12},{1,17},{... | collective-permute-start | bytes 368648 | tf_op jit(solution)/shard_map/ppermute | solution.py:241
  36.6 1.5 %collective-permute-start.8 = (bf16[96,640]{1,0:T(8,128)(2,1)S(1)}, bf16[96,640]{1,0:T(8,128)(2,1)S(1)}, u32[]{:S(2)}, u32[]{:S(2)}) collective-permute-start(bf16[96,640]{1,0:T(8,128)(2,1)S(1)} %get-tuple-element.64), channel_id=1, source_target_pairs={{0,8},{4,12},{8,0},{12,4},{16,24},{20,28},{24,16},{28,20},{1,9},{5... | collective-permute-start | bytes 368648 | tf_op jit(solution)/shard_map/ppermute | solution.py:241
  38.1 1.8 %collective-permute-start.11 = (bf16[256,1024]{1,0:T(8,128)(2,1)S(1)}, bf16[256,1024]{1,0:T(8,128)(2,1)S(1)}, u32[]{:S(2)}, u32[]{:S(2)}) collective-permute-start(bf16[256,1024]{1,0:T(8,128)(2,1)S(1)} %get-tuple-element.71), channel_id=1, source_target_pairs={{0,2},{3,1},{4,6},{7,5},{8,10},{11,9},{12,14},{15,13},{16,18},{19,... | collective-permute-start | bytes 1572872 | tf_op jit(solution)/shard_map/ppermute | solution.py:273
  40.0 1.0 %collective-permute-done.7.refs_0_ = bf16[96,640]{1,0:T(8,128)(2,1)S(1)} collective-permute-done((bf16[96,640]{1,0:T(8,128)(2,1)S(1)}, bf16[96,640]{1,0:T(8,128)(2,1)S(1)}, u32[]{:S(2)}, u32[]{:S(2)}) %collective-permute-start.7) | collective-permute-done | bytes 122912 | tf_op jit(solution)/shard_map/ppermute | solution.py:241
  41.0 2.4 %collective-permute-start.9 = (bf16[96,640]{1,0:T(8,128)(2,1)S(1)}, bf16[96,640]{1,0:T(8,128)(2,1)S(1)}, u32[]{:S(2)}, u32[]{:S(2)}) collective-permute-start(bf16[96,640]{1,0:T(8,128)(2,1)S(1)} %get-tuple-element.65), channel_id=1, source_target_pairs={{0,24},{4,28},{8,16},{12,20},{16,8},{20,12},{24,0},{28,4},{1,25},{... | collective-permute-start | bytes 368648 | tf_op jit(solution)/shard_map/ppermute | solution.py:241
  43.4 3.7 %collective-permute-done.9.refs_2_ = bf16[96,640]{1,0:T(8,128)(2,1)S(1)} collective-permute-done((bf16[96,640]{1,0:T(8,128)(2,1)S(1)}, bf16[96,640]{1,0:T(8,128)(2,1)S(1)}, u32[]{:S(2)}, u32[]{:S(2)}) %collective-permute-start.9) | collective-permute-done | bytes 122912 | tf_op jit(solution)/shard_map/ppermute | solution.py:241
  47.1 2.5 %collective-permute-done.10.refs_3_ = bf16[96,640]{1,0:T(8,128)(2,1)S(1)} collective-permute-done((bf16[96,640]{1,0:T(8,128)(2,1)S(1)}, bf16[96,640]{1,0:T(8,128)(2,1)S(1)}, u32[]{:S(2)}, u32[]{:S(2)}) %collective-permute-start.10) | collective-permute-done | bytes 122912 | tf_op jit(solution)/shard_map/ppermute | solution.py:241
  49.8 0.3 pass.1
  50.1 0.5 collective-permute-start.17
  50.7 7.3 %collective-permute-done.11.across_ref = bf16[256,1024]{1,0:T(8,128)(2,1)S(1)} collective-permute-done((bf16[256,1024]{1,0:T(8,128)(2,1)S(1)}, bf16[256,1024]{1,0:T(8,128)(2,1)S(1)}, u32[]{:S(2)}, u32[]{:S(2)}) %collective-permute-start.11) | collective-permute-done | bytes 524320 | tf_op jit(solution)/shard_map/ppermute | solution.py:273
  58.0 0.6 collective-permute-start.12
  58.6 1.7 %collective-permute-start.13 = (bf16[96,640]{1,0:T(8,128)(2,1)S(1)}, bf16[96,640]{1,0:T(8,128)(2,1)S(1)}, u32[]{:S(2)}, u32[]{:S(2)}) collective-permute-start(bf16[96,640]{1,0:T(8,128)(2,1)S(1)} %get-tuple-element.77), channel_id=1, source_target_pairs={{0,12},{4,8},{8,4},{12,0},{16,28},{20,24},{24,20},{28,16},{1,13},{... | collective-permute-start | bytes 368648 | tf_op jit(solution)/shard_map/ppermute | solution.py:241
  60.3 3.0 %collective-permute-done.12.refs_4_ = bf16[96,640]{1,0:T(8,128)(2,1)S(1)} collective-permute-done((bf16[96,640]{1,0:T(8,128)(2,1)S(1)}, bf16[96,640]{1,0:T(8,128)(2,1)S(1)}, u32[]{:S(2)}, u32[]{:S(2)}) %collective-permute-start.12) | collective-permute-done | bytes 122912 | tf_op jit(solution)/shard_map/ppermute | solution.py:241
  63.5 2.6 %finish.1 = (bf16[576,512]{1,0:T(8,128)(2,1)}, bf16[576]{0:T(1024)(128)(2,1)}) custom-call(s32[1,576]{1,0:T(1,128)S(1)} %copy-done.5, bf16[576]{0:T(1024)(128)(2,1)S(1)} %copy-done.7, bf16[576,512]{1,0:T(8,128)(2,1)S(1)} %copy-done.1, f32[1,512]{1,0:T(1,128)S(1)} %bitcast.15, bf16[576,512]{1,0:T(8,128)(2,1)S(1)} %copy-done.2, ...), custom_call_target="tpu_custom_call" | custom-call | flops 1 | bytes 1 | tf_op jit(solution)/shard_map/finish/pallas_call | solution.py:407
  66.1 4.3 %collective-permute-done.17.last_ref = bf16[256,1024]{1,0:T(8,128)(2,1)S(1)} collective-permute-done((bf16[256,1024]{1,0:T(8,128)(2,1)S(1)}, bf16[256,1024]{1,0:T(8,128)(2,1)S(1)}, u32[]{:S(2)}, u32[]{:S(2)}) %collective-permute-start.17) | collective-permute-done | bytes 524320 | tf_op jit(solution)/shard_map/ppermute | solution.py:287
  70.4 1.1 %total.1 = (f32[128,1024]{1,0:T(8,128)}, f32[256,512]{1,0:T(8,128)}) custom-call(f32[256,1024]{1,0:T(8,128)S(1)} %get-tuple-element.85.sum_ref, bf16[256,1024]{1,0:T(8,128)(2,1)S(1)} %collective-permute-done.11.across_ref, bf16[256,1024]{1,0:T(8,128)(2,1)S(1)} %collective-permute-done.17.last_ref), custom_call_target="tpu_custom_call" | custom-call | flops 1 | bytes 1 | tf_op jit(solution)/shard_map/total/pallas_call | solution.py:290
  (34 shorter events, 0.9 us)
Async XLA Ops:
  0.6 9.9 %copy-start.2 = (bf16[576,512]{1,0:T(8,128)(2,1)S(1)}, bf16[576,512]{1,0:T(8,128)(2,1)}, u32[]{:S(2)}) copy-start(bf16[576,512]{1,0:T(8,128)(2,1)} %go_ref.3) | copy-start | bytes 1769476
  0.6 9.9 %copy-start.1 = (bf16[576,512]{1,0:T(8,128)(2,1)S(1)}, bf16[576,512]{1,0:T(8,128)(2,1)}, u32[]{:S(2)}) copy-start(bf16[576,512]{1,0:T(8,128)(2,1)} %tok_ref.3) | copy-start | bytes 1769476
  0.7 22.5 %copy-start.3 = (bf16[1,1024,512]{2,1,0:T(8,128)(2,1)S(1)}, bf16[1,1024,512]{2,1,0:T(8,128)(2,1)}, u32[]{:S(2)}) copy-start(bf16[1,1024,512]{2,1,0:T(8,128)(2,1)} %param.10) | copy-start | bytes 3145732
  0.7 22.5 %copy-start = (bf16[1,512,1024]{2,1,0:T(8,128)(2,1)S(1)}, bf16[1,512,1024]{2,1,0:T(8,128)(2,1)}, u32[]{:S(2)}) copy-start(bf16[1,512,1024]{2,1,0:T(8,128)(2,1)} %param.9) | copy-start | bytes 3145732
  4.5 11.0 %collective-permute-start = (bf16[96,1024]{1,0:T(8,128)(2,1)}, bf16[96,1024]{1,0:T(8,128)(2,1)S(1)}, u32[]{:S(2)}, u32[]{:S(2)}) collective-permute-start(bf16[96,1024]{1,0:T(8,128)(2,1)} %get-tuple-element.48), channel_id=1, source_target_pairs={{0,16},{4,20},{8,24},{12,28},{16,0},{20,4},{24,8},{28,12},{1,17},{... | collective-permute-start | bytes 589832 | tf_op jit(solution)/shard_map/ppermute | solution.py:241
  7.5 8.2 %collective-permute-start.1 = (bf16[96,1024]{1,0:T(8,128)(2,1)}, bf16[96,1024]{1,0:T(8,128)(2,1)S(1)}, u32[]{:S(2)}, u32[]{:S(2)}) collective-permute-start(bf16[96,1024]{1,0:T(8,128)(2,1)} %get-tuple-element.49), channel_id=1, source_target_pairs={{0,8},{4,12},{8,0},{12,4},{16,24},{20,28},{24,16},{28,20},{1,9},{5... | collective-permute-start | bytes 589832 | tf_op jit(solution)/shard_map/ppermute | solution.py:241
  9.0 10.3 %collective-permute-start.2 = (bf16[96,1024]{1,0:T(8,128)(2,1)}, bf16[96,1024]{1,0:T(8,128)(2,1)S(1)}, u32[]{:S(2)}, u32[]{:S(2)}) collective-permute-start(bf16[96,1024]{1,0:T(8,128)(2,1)} %get-tuple-element.50), channel_id=1, source_target_pairs={{0,24},{4,28},{8,16},{12,20},{16,8},{20,12},{24,0},{28,4},{1,25},{... | collective-permute-start | bytes 589832 | tf_op jit(solution)/shard_map/ppermute | solution.py:241
  9.1 14.1 %collective-permute-start.3 = (bf16[96,1024]{1,0:T(8,128)(2,1)}, bf16[96,1024]{1,0:T(8,128)(2,1)S(1)}, u32[]{:S(2)}, u32[]{:S(2)}) collective-permute-start(bf16[96,1024]{1,0:T(8,128)(2,1)} %get-tuple-element.51), channel_id=1, source_target_pairs={{0,28},{4,24},{8,20},{12,16},{16,12},{20,8},{24,4},{28,0},{1,29},{... | collective-permute-start | bytes 589832 | tf_op jit(solution)/shard_map/ppermute | solution.py:241
  10.5 0.7 copy-start.4
  11.2 0.7 copy-start.6
  11.9 0.7 copy-start.8
  13.9 9.2 %collective-permute-start.4 = (bf16[96,1024]{1,0:T(8,128)(2,1)S(1)}, bf16[96,1024]{1,0:T(8,128)(2,1)S(1)}, u32[]{:S(2)}, u32[]{:S(2)}) collective-permute-start(bf16[96,1024]{1,0:T(8,128)(2,1)S(1)} %get-tuple-element.52), channel_id=1, source_target_pairs={{0,4},{4,0},{8,12},{12,8},{16,20},{20,16},{24,28},{28,24},{1,5},{5... | collective-permute-start | bytes 589832 | tf_op jit(solution)/shard_map/ppermute | solution.py:241
  15.5 11.6 %collective-permute-start.5 = (bf16[96,1024]{1,0:T(8,128)(2,1)S(1)}, bf16[96,1024]{1,0:T(8,128)(2,1)S(1)}, u32[]{:S(2)}, u32[]{:S(2)}) collective-permute-start(bf16[96,1024]{1,0:T(8,128)(2,1)S(1)} %get-tuple-element.56), channel_id=1, source_target_pairs={{0,20},{4,16},{8,28},{12,24},{16,4},{20,0},{24,12},{28,8},{1,21},{... | collective-permute-start | bytes 589832 | tf_op jit(solution)/shard_map/ppermute | solution.py:241
  15.7 11.4 %collective-permute-start.6 = (bf16[96,1024]{1,0:T(8,128)(2,1)S(1)}, bf16[96,1024]{1,0:T(8,128)(2,1)S(1)}, u32[]{:S(2)}, u32[]{:S(2)}) collective-permute-start(bf16[96,1024]{1,0:T(8,128)(2,1)S(1)} %get-tuple-element.57), channel_id=1, source_target_pairs={{0,12},{4,8},{8,4},{12,0},{16,28},{20,24},{24,20},{28,16},{1,13},{... | collective-permute-start | bytes 589832 | tf_op jit(solution)/shard_map/ppermute | solution.py:241
  29.3 20.4 %collective-permute-start.16 = (bf16[256,1024]{1,0:T(8,128)(2,1)S(1)}, bf16[256,1024]{1,0:T(8,128)(2,1)S(1)}, u32[]{:S(2)}, u32[]{:S(2)}) collective-permute-start(bf16[256,1024]{1,0:T(8,128)(2,1)S(1)} %get-tuple-element.71), channel_id=1, source_target_pairs={{1,2},{2,1},{5,6},{6,5},{9,10},{10,9},{13,14},{14,13},{17,18},{18,... | collective-permute-start | bytes 1572872 | tf_op jit(solution)/shard_map/ppermute | solution.py:271
  30.0 19.8 %collective-permute-start.15 = (bf16[256,1024]{1,0:T(8,128)(2,1)S(1)}, bf16[256,1024]{1,0:T(8,128)(2,1)S(1)}, u32[]{:S(2)}, u32[]{:S(2)}) collective-permute-start(bf16[256,1024]{1,0:T(8,128)(2,1)S(1)} %get-tuple-element.82), channel_id=1, source_target_pairs={{0,1},{1,0},{2,3},{3,2},{4,5},{5,4},{6,7},{7,6},{8,9},{9,8},{10,11... | collective-permute-start | bytes 1572872 | tf_op jit(solution)/shard_map/ppermute | solution.py:272
  35.6 5.4 %collective-permute-start.7 = (bf16[96,640]{1,0:T(8,128)(2,1)S(1)}, bf16[96,640]{1,0:T(8,128)(2,1)S(1)}, u32[]{:S(2)}, u32[]{:S(2)}) collective-permute-start(bf16[96,640]{1,0:T(8,128)(2,1)S(1)} %get-tuple-element.63), channel_id=1, source_target_pairs={{0,16},{4,20},{8,24},{12,28},{16,0},{20,4},{24,8},{28,12},{1,17},{... | collective-permute-start | bytes 368648 | tf_op jit(solution)/shard_map/ppermute | solution.py:241
  36.6 6.8 %collective-permute-start.8 = (bf16[96,640]{1,0:T(8,128)(2,1)S(1)}, bf16[96,640]{1,0:T(8,128)(2,1)S(1)}, u32[]{:S(2)}, u32[]{:S(2)}) collective-permute-start(bf16[96,640]{1,0:T(8,128)(2,1)S(1)} %get-tuple-element.64), channel_id=1, source_target_pairs={{0,8},{4,12},{8,0},{12,4},{16,24},{20,28},{24,16},{28,20},{1,9},{5... | collective-permute-start | bytes 368648 | tf_op jit(solution)/shard_map/ppermute | solution.py:241
  38.1 19.9 %collective-permute-start.11 = (bf16[256,1024]{1,0:T(8,128)(2,1)S(1)}, bf16[256,1024]{1,0:T(8,128)(2,1)S(1)}, u32[]{:S(2)}, u32[]{:S(2)}) collective-permute-start(bf16[256,1024]{1,0:T(8,128)(2,1)S(1)} %get-tuple-element.71), channel_id=1, source_target_pairs={{0,2},{3,1},{4,6},{7,5},{8,10},{11,9},{12,14},{15,13},{16,18},{19,... | collective-permute-start | bytes 1572872 | tf_op jit(solution)/shard_map/ppermute | solution.py:273
  41.0 6.2 %collective-permute-start.9 = (bf16[96,640]{1,0:T(8,128)(2,1)S(1)}, bf16[96,640]{1,0:T(8,128)(2,1)S(1)}, u32[]{:S(2)}, u32[]{:S(2)}) collective-permute-start(bf16[96,640]{1,0:T(8,128)(2,1)S(1)} %get-tuple-element.65), channel_id=1, source_target_pairs={{0,24},{4,28},{8,16},{12,20},{16,8},{20,12},{24,0},{28,4},{1,25},{... | collective-permute-start | bytes 368648 | tf_op jit(solution)/shard_map/ppermute | solution.py:241
  43.4 6.3 %collective-permute-start.10 = (bf16[96,640]{1,0:T(8,128)(2,1)S(1)}, bf16[96,640]{1,0:T(8,128)(2,1)S(1)}, u32[]{:S(2)}, u32[]{:S(2)}) collective-permute-start(bf16[96,640]{1,0:T(8,128)(2,1)S(1)} %get-tuple-element.66), channel_id=1, source_target_pairs={{0,28},{4,24},{8,20},{12,16},{16,12},{20,8},{24,4},{28,0},{1,29},{... | collective-permute-start | bytes 368648 | tf_op jit(solution)/shard_map/ppermute | solution.py:241
  49.7 13.8 %copy-start.5 = (s32[1,576]{1,0:T(1,128)S(1)}, s32[1,576]{1,0:T(1,128)}, u32[]{:S(2)}) copy-start(s32[1,576]{1,0:T(1,128)} %get-tuple-element.47.target_ref) | copy-start | bytes 6916
  49.7 13.8 %copy-start.7 = (bf16[576]{0:T(1024)(128)(2,1)S(1)}, bf16[576]{0:T(1024)(128)(2,1)}, u32[]{:S(2)}) copy-start(bf16[576]{0:T(1024)(128)(2,1)} %gate_ref.3) | copy-start | bytes 3460
  49.7 13.8 %copy-start.9 = (f32[512]{0:T(512)S(1)}, f32[512]{0:T(512)}, u32[]{:S(2)}) copy-start(f32[512]{0:T(512)} %param.8) | copy-start | bytes 6148
  50.1 20.3 %collective-permute-start.17 = (bf16[256,1024]{1,0:T(8,128)(2,1)S(1)}, bf16[256,1024]{1,0:T(8,128)(2,1)S(1)}, u32[]{:S(2)}, u32[]{:S(2)}) collective-permute-start(bf16[256,1024]{1,0:T(8,128)(2,1)S(1)} %get-tuple-element.87), channel_id=1, source_target_pairs={{0,1},{3,2},{1,3},{2,0},{4,5},{7,6},{5,7},{6,4},{8,9},{11,10},{9,1... | collective-permute-start | bytes 1572872 | tf_op jit(solution)/shard_map/ppermute | solution.py:287
  58.0 5.2 %collective-permute-start.12 = (bf16[96,640]{1,0:T(8,128)(2,1)S(1)}, bf16[96,640]{1,0:T(8,128)(2,1)S(1)}, u32[]{:S(2)}, u32[]{:S(2)}) collective-permute-start(bf16[96,640]{1,0:T(8,128)(2,1)S(1)} %get-tuple-element.76), channel_id=1, source_target_pairs={{0,20},{4,16},{8,28},{12,24},{16,4},{20,0},{24,12},{28,8},{1,21},{... | collective-permute-start | bytes 368648 | tf_op jit(solution)/shard_map/ppermute | solution.py:241
  58.6 4.9 %collective-permute-start.13 = (bf16[96,640]{1,0:T(8,128)(2,1)S(1)}, bf16[96,640]{1,0:T(8,128)(2,1)S(1)}, u32[]{:S(2)}, u32[]{:S(2)}) collective-permute-start(bf16[96,640]{1,0:T(8,128)(2,1)S(1)} %get-tuple-element.77), channel_id=1, source_target_pairs={{0,12},{4,8},{8,4},{12,0},{16,28},{20,24},{24,20},{28,16},{1,13},{... | collective-permute-start | bytes 368648 | tf_op jit(solution)/shard_map/ppermute | solution.py:241
  60.3 3.3 %collective-permute-start.14 = (bf16[96,640]{1,0:T(8,128)(2,1)S(1)}, bf16[96,640]{1,0:T(8,128)(2,1)S(1)}, u32[]{:S(2)}, u32[]{:S(2)}) collective-permute-start(bf16[96,640]{1,0:T(8,128)(2,1)S(1)} %get-tuple-element.78), channel_id=1, source_target_pairs={{0,4},{4,0},{8,12},{12,8},{16,20},{20,16},{24,28},{28,24},{1,5},{5... | collective-permute-start | bytes 368648 | tf_op jit(solution)/shard_map/ppermute | solution.py:241

commit v10 on v9

--- a/solution.py
+++ b/solution.py
@@ -180,6 +180,20 @@
     expert_work(order, blocks, w_in_ref, w_out_ref, gpre_ref, extra_ref, rows_ref, turned_ref, put)
 
 
+def next_kernel(count, groups, place, w_in_ref, w_out_ref, old_in_ref, old_out_ref, *refs):
+    blocks = refs[:count]
+    sum_in_ref, sum_out_ref, gpre_ref, extra_ref, rows_ref, turned_ref = refs[count:]
+    piece_f = w_in_ref.shape[1] // LINE
+
+    def put(j, part, weight_in, weight_out):
+        chunk = slice(j * piece_f, (j + 1) * piece_f)
+        sum_in_ref[:, part] = old_in_ref[:, part] + weight_in
+        sum_out_ref[chunk, :] = old_out_ref[chunk, :] + weight_out
+
+    order = shard_order(place[0]) if groups == LINE else list(range(LINE))
+    expert_work(order, blocks, w_in_ref, w_out_ref, gpre_ref, extra_ref, rows_ref, turned_ref, put)
+
+
 def later_kernel(count, groups, place, w_in_ref, w_out_ref, sum_in_ref, sum_out_ref, *refs):
     blocks = refs[:count]
     outs = refs[count : count + LINE]
@@ -200,7 +214,7 @@
 
 
 def back_kernel(capacity, sets, w_in_ref, *refs):
-    inputs, outs = refs[:4], refs[4:]
+    inputs, outs = refs[: 2 * len(sets)], refs[2 * len(sets) :]
     width = w_in_ref.shape[0]
     for members, gpre_ref, extra_ref in zip(sets, inputs[::2], inputs[1::2]):
         grad = dot(gpre_ref[...], w_in_ref[...], ((1,), (1,))).astype(BF16)
@@ -243,15 +257,11 @@
     ]
 
 
-def start_kernel(own_ref, middle_ref, out_ref):
-    out_ref[...] = own_ref[...].astype(F32) + middle_ref[...].astype(F32)
-
-
-def pass_kernel(place, swapped_ref, third_ref, sum_ref, out_ref, more_ref):
-    swapped = swapped_ref[...].astype(F32)
-    onward = jnp.where((place[0] == 1) | (place[0] == 2), swapped, 0.0)
-    out_ref[...] = (third_ref[...].astype(F32) + onward).astype(BF16)
-    more_ref[...] = sum_ref[...] + (swapped - onward)
+def pass_kernel(place, swapped_ref, middle_ref, third_ref, own_ref, out_ref, sum_ref):
+    inner = (place[0] == 1) | (place[0] == 2)
+    swapped, middle = swapped_ref[...].astype(F32), middle_ref[...].astype(F32)
+    out_ref[...] = (third_ref[...].astype(F32) + jnp.where(inner, swapped, 0.0)).astype(BF16)
+    sum_ref[...] = own_ref[...].astype(F32) + jnp.where(inner, middle, swapped)
 
 
 def total_kernel(sum_ref, across_ref, last_ref, in_ref, out_ref):
@@ -268,22 +278,19 @@
     piece_d = width // LINE
     half = len(returned) // 2
     order = block_order(len(returned))
-    middle = lax.ppermute(second, "dp", [(1, 2), (2, 1)])
+    middle = lax.ppermute(second, "dp", [(0, 0), (1, 2), (2, 1), (3, 3)])
     swapped = lax.ppermute(first, "dp", [(0, 1), (1, 0), (2, 3), (3, 2)])
     across = lax.ppermute(second, "dp", [(0, 2), (3, 1)])
     back = swap_blocks(returned[:half], order[:half])
     third, *back = lax.optimization_barrier((third, *back))
-    (some,) = kernel_call(
-        start_kernel, "start", 1, 1, [jax.ShapeDtypeStruct(own.shape, F32)], [vmem] * 2
-    )(own, middle)
     passed, most = kernel_call(
         pass_kernel,
         "pass",
         1,
         1,
         [jax.ShapeDtypeStruct(own.shape, BF16), jax.ShapeDtypeStruct(own.shape, F32)],
-        [smem] + [vmem] * 3,
-    )(place, swapped, third, some)
+        [smem] + [vmem] * 4,
+    )(place, swapped, middle, third, own)
     last = lax.ppermute(passed, "dp", [(0, 1), (3, 2), (1, 3), (2, 0)])
     across, *rest = lax.optimization_barrier((across, *returned[half:]))
     back += swap_blocks(rest, order[half:])
@@ -364,8 +371,9 @@
     arrived = swap_blocks(sent, block_order(sources))
     arrived[-1] = kept
 
+    next_set = list(range(3 * sources // 8, sources // 2))
     late_set = list(range(sources // 2, 3 * sources // 4))
-    soon_set = [j for j in range(sources) if j not in late_set]
+    soon_set = [j for j in range(sources) if j not in next_set + late_set]
 
     def work(kernel, name, members, outs, *sums):
         count, span = len(members), len(members) * capacity
@@ -379,19 +387,19 @@
             [pltpu.VMEM((span, 2 * width), BF16), pltpu.VMEM((width, span), BF16)],
         )(place, weight_in, weight_out, *sums, *[arrived[j] for j in members])
 
-    *sums, soon_gpre, soon_extra = work(
-        sooner_kernel, "sooner", soon_set, [shape((width, hidden), F32), shape((hidden, width), F32)]
-    )
+    sums_shape = [shape((width, hidden), F32), shape((hidden, width), F32)]
+    *sums, soon_gpre, soon_extra = work(sooner_kernel, "sooner", soon_set, sums_shape)
+    *sums, next_gpre, next_extra = work(next_kernel, "next", next_set, sums_shape, *sums)
     piece = shape((width // LINE + hidden // LINE // 2, hidden), BF16)
     *parts, late_gpre, late_extra = work(later_kernel, "later", late_set, [piece] * LINE, *sums)
     returned = kernel_call(
-        functools.partial(back_kernel, capacity, (soon_set, late_set)),
+        functools.partial(back_kernel, capacity, (soon_set, next_set, late_set)),
         "back",
         1,
         1,
         [shape((capacity, width + LANES), BF16)] * sources,
-        [vmem] * 5,
-    )(weight_in, soon_gpre, soon_extra, late_gpre, late_extra)
+        [vmem] * 7,
+    )(weight_in, soon_gpre, soon_extra, next_gpre, next_extra, late_gpre, late_extra)
 
     if groups == LINE:
         grad_w_in, grad_w_out, back = line_sums(place, *parts, width, returned)

time: 71.7 us -> 72.5 us (1.011)
  waiting for transfers between devices: 29.4 us -> 18 us
  starting transfers between devices: 22.8 us -> 33.6 us
  Pallas kernels: 16.5 us -> 17.8 us
    ppermute x1, starting transfers between devices: 0.54 us -> 10.3 us  [line_sums(): last = lax.ppermute(passed, 'dp', [(0, 1), (3, 2), (1, 3), (2, 0)])]
    ppermute x1, waiting for transfers between devices: 7.3 us -> 0.01 us  [line_sums(): across = lax.ppermute(second, 'dp', [(0, 2), (3, 1)])]
    ppermute x1, starting transfers between devices: 1.82 us -> 5.75 us  [line_sums(): across = lax.ppermute(second, 'dp', [(0, 2), (3, 1)])]
    ppermute x14, waiting for transfers between devices: 17.7 us -> 14.2 us  [swap_blocks(): lax.ppermute(block, 'space', [(i, i ^ k) for i in devices])]
    ppermute x1, starting transfers between devices: 4.46 us -> 1.79 us  [line_sums(): swapped = lax.ppermute(first, 'dp', [(0, 1), (1, 0), (2, 3), (3, 2)])]
    pallas_call x2 -> x3, Pallas kernels: 6.11 us -> 7.32 us  [work(): kernel_call(functools.partial(kernel, count, groups), name, 8 * span * wi...]
  transfers between devices with their start and end apart: 18 -> 18, of which waited for: 9 -> 7; matrix products, arithmetic and copies ran while one was open for 0% -> 0% of each run, Pallas kernels for 13% -> 15%
where the time goes in v10:
time: 72.5 us; the launch traced here: 72.3 us
  starting transfers between devices  33.6 us (46%)
  waiting for transfers between devices  18 us (25%)
  Pallas kernels  17.8 us (25%)
  local copies, waits for them, and re-layouts  2.07 us (3%)
  between operations  0.82 us (1%)
    ppermute x14, starting transfers between devices, swap_blocks(): lax.ppermute(block, 'space', [(i, i ^ k) for i in devices])  15.2 us
    ppermute x14, waiting for transfers between devices, swap_blocks(): lax.ppermute(block, 'space', [(i, i ^ k) for i in devices])  14.2 us
    ppermute x1, starting transfers between devices, line_sums(): last = lax.ppermute(passed, 'dp', [(0, 1), (3, 2), (1, 3), (2, 0)])  10.3 us
    pallas_call x3, Pallas kernels, work(): kernel_call(functools.partial(kernel, count, groups), name, 8 * span * wi...  7.32 us
    ppermute x1, starting transfers between devices, line_sums(): across = lax.ppermute(second, 'dp', [(0, 2), (3, 1)])  5.75 us
    pallas_call x1, Pallas kernels, body(): kernel_call(functools.partial(place_kernel, sources, capacity), 'place',...  3.8 us
    ppermute x1, waiting for transfers between devices, line_sums(): last = lax.ppermute(passed, 'dp', [(0, 1), (3, 2), (1, 3), (2, 0)])  3.8 us
    pallas_call x1, Pallas kernels, body(): kernel_call(finish_kernel, 'finish', 1, 1, [shape((tok_rows, width), BF16...  2.59 us
  transfers between devices with their start and end apart: 18, of which 7 were waited for; matrix products, arithmetic and copies ran while one was open for 0% of the time, Pallas kernels for 15%

profile of v10, /device:TPU:0, one launch (start us, length us, event | category | flops | bytes accessed | tf_op | source)
XLA Modules:
  0.0 72.3 jit_solution(3246163665499683983)
XLA Ops:
  0.7 3.8 %place.1 = (s32[1,576]{1,0:T(1,128)}, bf16[96,1024]{1,0:T(8,128)(2,1)}, bf16[96,1024]{1,0:T(8,128)(2,1)}, bf16[96,1024]{1,0:T(8,128)(2,1)}, bf16[96,1024]{1,0:T(8,128)(2,1)}) custom-call(s32[1]{0:T(128)} %bitcast.me, s32[1]{0:T(128)} %bitcast.1.place, s32[1,576]{1,0:T(1,128)} %bitcast.20, bf16[576]{0:T(1024)(128)(2,1)} %gate_ref.3, ...), custom_call_target="tpu_custom_call" | custom-call | flops 452984832 | bytes 2752512 | tf_op jit(solution)/shard_map/place/pallas_call | solution.py:330
  4.5 3.0 %collective-permute-start = (bf16[96,1024]{1,0:T(8,128)(2,1)}, bf16[96,1024]{1,0:T(8,128)(2,1)S(1)}, u32[]{:S(2)}, u32[]{:S(2)}) collective-permute-start(bf16[96,1024]{1,0:T(8,128)(2,1)} %get-tuple-element.52), channel_id=1, source_target_pairs={{0,16},{4,20},{8,24},{12,28},{16,0},{20,4},{24,8},{28,12},{1,17},{... | collective-permute-start | bytes 589832 | tf_op jit(solution)/shard_map/ppermute | solution.py:255
  7.5 1.5 %collective-permute-start.1 = (bf16[96,1024]{1,0:T(8,128)(2,1)}, bf16[96,1024]{1,0:T(8,128)(2,1)S(1)}, u32[]{:S(2)}, u32[]{:S(2)}) collective-permute-start(bf16[96,1024]{1,0:T(8,128)(2,1)} %get-tuple-element.53), channel_id=1, source_target_pairs={{0,8},{4,12},{8,0},{12,4},{16,24},{20,28},{24,16},{28,20},{1,9},{5... | collective-permute-start | bytes 589832 | tf_op jit(solution)/shard_map/ppermute | solution.py:255
  9.1 0.7 copy-done.4
  9.7 0.7 copy-done.6
  10.4 0.7 copy-done.8
  11.1 1.3 %rest.1 = (bf16[96,1024]{1,0:T(8,128)(2,1)S(1)}, bf16[96,1024]{1,0:T(8,128)(2,1)S(1)}, bf16[96,1024]{1,0:T(8,128)(2,1)S(1)}, bf16[96,1024]{1,0:T(8,128)(2,1)S(1)}) custom-call(s32[1,576]{1,0:T(1,128)S(1)} %copy-done.4, bf16[576]{0:T(1024)(128)(2,1)S(1)} %copy-done.6, bf16[576,512]{1,0:T(8,128)(2,1)S(1)} %copy-done.2, f32[1,512]{1,0:T(1,128)S(1)} %bitcast.16, ...), custom_call_target="tpu_custom_call" | custom-call | flops 1 | bytes 1 | tf_op jit(solution)/shard_map/rest/pallas_call | solution.py:351
  12.5 3.0 %collective-permute-start.4 = (bf16[96,1024]{1,0:T(8,128)(2,1)}, bf16[96,1024]{1,0:T(8,128)(2,1)S(1)}, u32[]{:S(2)}, u32[]{:S(2)}) collective-permute-start(bf16[96,1024]{1,0:T(8,128)(2,1)} %get-tuple-element.59), channel_id=1, source_target_pairs={{0,28},{4,24},{8,20},{12,16},{16,12},{20,8},{24,4},{28,0},{1,29},{... | collective-permute-start | bytes 589832 | tf_op jit(solution)/shard_map/ppermute | solution.py:255
  15.5 0.3 collective-permute-start.5
  15.9 3.4 %collective-permute-done.2.refs_2_ = bf16[96,1024]{1,0:T(8,128)(2,1)S(1)} collective-permute-done((bf16[96,1024]{1,0:T(8,128)(2,1)}, bf16[96,1024]{1,0:T(8,128)(2,1)S(1)}, u32[]{:S(2)}, u32[]{:S(2)}) %collective-permute-start.2) | collective-permute-done | bytes 196640 | tf_op jit(solution)/shard_map/ppermute | solution.py:255
  19.3 3.2 %sooner.1 = (f32[512,1024]{1,0:T(8,128)S(1)}, f32[1024,512]{1,0:T(8,128)S(1)}, bf16[480,1024]{1,0:T(8,128)(2,1)S(1)}, bf16[480,128]{1,0:T(8,128)(2,1)S(1)}) custom-call(s32[1]{0:T(128)} %bitcast.1.place, bf16[512,1024]{1,0:T(8,128)(2,1)S(1)} %bitcast.8, bf16[1024,512]{1,0:T(8,128)(2,1)S(1)} %bitcast.12, bf16[96,1024]{1,0:T(8,128)(2,1)S(1)} %collective-permute-done.refs_0_, ...), custom_call_target="tpu_custom_call" | custom-call | flops 2013265920 | bytes 6160384 | tf_op jit(solution)/shard_map/sooner/pallas_call | solution.py:380
  22.6 0.2 collective-permute-done.4.refs_0_
  22.8 2.0 %next.1 = (f32[512,1024]{1,0:T(8,128)S(1)}, f32[1024,512]{1,0:T(8,128)S(1)}, bf16[96,1024]{1,0:T(8,128)(2,1)S(1)}, bf16[96,128]{1,0:T(8,128)(2,1)S(1)}) custom-call(s32[1]{0:T(128)} %bitcast.1.place, bf16[512,1024]{1,0:T(8,128)(2,1)S(1)} %bitcast.9, bf16[1024,512]{1,0:T(8,128)(2,1)S(1)} %bitcast.13, f32[512,1024]{1,0:T(8,128)S(1)} %get-tuple-element.57.old_in_ref, ...), custom_call_target="tpu_custom_call" | custom-call | flops 402653184 | bytes 4587520 | tf_op jit(solution)/shard_map/next/pallas_call | solution.py:380
  24.7 1.8 %collective-permute-done.5.refs_0_ = bf16[96,1024]{1,0:T(8,128)(2,1)S(1)} collective-permute-done((bf16[96,1024]{1,0:T(8,128)(2,1)S(1)}, bf16[96,1024]{1,0:T(8,128)(2,1)S(1)}, u32[]{:S(2)}, u32[]{:S(2)}) %collective-permute-start.5) | collective-permute-done | bytes 196640 | tf_op jit(solution)/shard_map/ppermute | solution.py:255
  26.5 2.1 %later.1 = (bf16[256,1024]{1,0:T(8,128)(2,1)S(1)}, bf16[256,1024]{1,0:T(8,128)(2,1)S(1)}, bf16[256,1024]{1,0:T(8,128)(2,1)S(1)}, bf16[256,1024]{1,0:T(8,128)(2,1...) custom-call(s32[1]{0:T(128)} %bitcast.1.place, bf16[512,1024]{1,0:T(8,128)(2,1)S(1)} %bitcast.10, ...), custom_call_target="tpu_custom_call" | custom-call | flops 805306368 | bytes 4980736 | tf_op jit(solution)/shard_map/later/pallas_call | solution.py:380
  28.6 1.8 %collective-permute-start.15 = (bf16[256,1024]{1,0:T(8,128)(2,1)S(1)}, bf16[256,1024]{1,0:T(8,128)(2,1)S(1)}, u32[]{:S(2)}, u32[]{:S(2)}) collective-permute-start(bf16[256,1024]{1,0:T(8,128)(2,1)S(1)} %get-tuple-element.90), channel_id=1, source_target_pairs={{0,1},{1,0},{2,3},{3,2},{4,5},{5,4},{6,7},{7,6},{8,9},{9,8},{10,11... | collective-permute-start | bytes 1572872 | tf_op jit(solution)/shard_map/ppermute | solution.py:282
  30.4 0.7 collective-permute-start.16
  31.1 1.3 %back.1 = (bf16[96,640]{1,0:T(8,128)(2,1)S(1)}, bf16[96,640]{1,0:T(8,128)(2,1)S(1)}, bf16[96,640]{1,0:T(8,128)(2,1)S(1)}, bf16[96,640]{1,0:T(8,128)(2,1)S(1)}, b...) custom-call(bf16[512,1024]{1,0:T(8,128)(2,1)S(1)} %bitcast.11, ...), custom_call_target="tpu_custom_call" | custom-call | flops 1 | bytes 1 | tf_op jit(solution)/shard_map/back/pallas_call | solution.py:395
  32.5 1.6 %collective-permute-start.7 = (bf16[96,640]{1,0:T(8,128)(2,1)S(1)}, bf16[96,640]{1,0:T(8,128)(2,1)S(1)}, u32[]{:S(2)}, u32[]{:S(2)}) collective-permute-start(bf16[96,640]{1,0:T(8,128)(2,1)S(1)} %get-tuple-element.71), channel_id=1, source_target_pairs={{0,16},{4,20},{8,24},{12,28},{16,0},{20,4},{24,8},{28,12},{1,17},{... | collective-permute-start | bytes 368648 | tf_op jit(solution)/shard_map/ppermute | solution.py:255
  34.1 1.5 %collective-permute-start.8 = (bf16[96,640]{1,0:T(8,128)(2,1)S(1)}, bf16[96,640]{1,0:T(8,128)(2,1)S(1)}, u32[]{:S(2)}, u32[]{:S(2)}) collective-permute-start(bf16[96,640]{1,0:T(8,128)(2,1)S(1)} %get-tuple-element.72), channel_id=1, source_target_pairs={{0,8},{4,12},{8,0},{12,4},{16,24},{20,28},{24,16},{28,20},{1,9},{5... | collective-permute-start | bytes 368648 | tf_op jit(solution)/shard_map/ppermute | solution.py:255
  35.6 5.7 %collective-permute-start.11 = (bf16[256,1024]{1,0:T(8,128)(2,1)S(1)}, bf16[256,1024]{1,0:T(8,128)(2,1)S(1)}, u32[]{:S(2)}, u32[]{:S(2)}) collective-permute-start(bf16[256,1024]{1,0:T(8,128)(2,1)S(1)} %get-tuple-element.79), channel_id=1, source_target_pairs={{0,2},{3,1},{4,6},{7,5},{8,10},{11,9},{12,14},{15,13},{16,18},{19,... | collective-permute-start | bytes 1572872 | tf_op jit(solution)/shard_map/ppermute | solution.py:283
  41.3 0.5 collective-permute-start.9
  41.9 0.8 %collective-permute-start.10 = (bf16[96,640]{1,0:T(8,128)(2,1)S(1)}, bf16[96,640]{1,0:T(8,128)(2,1)S(1)}, u32[]{:S(2)}, u32[]{:S(2)}) collective-permute-start(bf16[96,640]{1,0:T(8,128)(2,1)S(1)} %get-tuple-element.74), channel_id=1, source_target_pairs={{0,28},{4,24},{8,20},{12,16},{16,12},{20,8},{24,4},{28,0},{1,29},{... | collective-permute-start | bytes 368648 | tf_op jit(solution)/shard_map/ppermute | solution.py:255
  42.6 5.8 %collective-permute-done.9.refs_2_ = bf16[96,640]{1,0:T(8,128)(2,1)S(1)} collective-permute-done((bf16[96,640]{1,0:T(8,128)(2,1)S(1)}, bf16[96,640]{1,0:T(8,128)(2,1)S(1)}, u32[]{:S(2)}, u32[]{:S(2)}) %collective-permute-start.9) | collective-permute-done | bytes 122912 | tf_op jit(solution)/shard_map/ppermute | solution.py:255
  48.4 0.3 pass.1
  48.7 10.3 %collective-permute-start.17 = (bf16[256,1024]{1,0:T(8,128)(2,1)S(1)}, bf16[256,1024]{1,0:T(8,128)(2,1)S(1)}, u32[]{:S(2)}, u32[]{:S(2)}) collective-permute-start(bf16[256,1024]{1,0:T(8,128)(2,1)S(1)} %get-tuple-element.95), channel_id=1, source_target_pairs={{0,1},{3,2},{1,3},{2,0},{4,5},{7,6},{5,7},{6,4},{8,9},{11,10},{9,1... | collective-permute-start | bytes 1572872 | tf_op jit(solution)/shard_map/ppermute | solution.py:294
  59.1 2.6 %collective-permute-start.13 = (bf16[96,640]{1,0:T(8,128)(2,1)S(1)}, bf16[96,640]{1,0:T(8,128)(2,1)S(1)}, u32[]{:S(2)}, u32[]{:S(2)}) collective-permute-start(bf16[96,640]{1,0:T(8,128)(2,1)S(1)} %get-tuple-element.85), channel_id=1, source_target_pairs={{0,12},{4,8},{8,4},{12,0},{16,28},{20,24},{24,20},{28,16},{1,13},{... | collective-permute-start | bytes 368648 | tf_op jit(solution)/shard_map/ppermute | solution.py:255
  61.7 2.8 %collective-permute-done.12.refs_4_ = bf16[96,640]{1,0:T(8,128)(2,1)S(1)} collective-permute-done((bf16[96,640]{1,0:T(8,128)(2,1)S(1)}, bf16[96,640]{1,0:T(8,128)(2,1)S(1)}, u32[]{:S(2)}, u32[]{:S(2)}) %collective-permute-start.12) | collective-permute-done | bytes 122912 | tf_op jit(solution)/shard_map/ppermute | solution.py:255
  64.6 0.2 collective-permute-done.13.refs_5_
  64.8 2.6 %finish.1 = (bf16[576,512]{1,0:T(8,128)(2,1)}, bf16[576]{0:T(1024)(128)(2,1)}) custom-call(s32[1,576]{1,0:T(1,128)S(1)} %copy-done.5, bf16[576]{0:T(1024)(128)(2,1)S(1)} %copy-done.7, bf16[576,512]{1,0:T(8,128)(2,1)S(1)} %copy-done.2, f32[1,512]{1,0:T(1,128)S(1)} %bitcast.17, bf16[576,512]{1,0:T(8,128)(2,1)S(1)} %copy-done.3, ...), custom_call_target="tpu_custom_call" | custom-call | flops 1 | bytes 1 | tf_op jit(solution)/shard_map/finish/pallas_call | solution.py:415
  67.4 3.8 %collective-permute-done.17.last_ref = bf16[256,1024]{1,0:T(8,128)(2,1)S(1)} collective-permute-done((bf16[256,1024]{1,0:T(8,128)(2,1)S(1)}, bf16[256,1024]{1,0:T(8,128)(2,1)S(1)}, u32[]{:S(2)}, u32[]{:S(2)}) %collective-permute-start.17) | collective-permute-done | bytes 524320 | tf_op jit(solution)/shard_map/ppermute | solution.py:294
  71.2 1.1 %total.1 = (f32[128,1024]{1,0:T(8,128)}, f32[256,512]{1,0:T(8,128)}) custom-call(f32[256,1024]{1,0:T(8,128)S(1)} %get-tuple-element.93.sum_ref, bf16[256,1024]{1,0:T(8,128)(2,1)S(1)} %collective-permute-done.11.across_ref, bf16[256,1024]{1,0:T(8,128)(2,1)S(1)} %collective-permute-done.17.last_ref), custom_call_target="tpu_custom_call" | custom-call | flops 1 | bytes 1 | tf_op jit(solution)/shard_map/total/pallas_call | solution.py:297
  (34 shorter events, 0.5 us)
Async XLA Ops:
  0.6 8.4 %copy-start.3 = (bf16[576,512]{1,0:T(8,128)(2,1)S(1)}, bf16[576,512]{1,0:T(8,128)(2,1)}, u32[]{:S(2)}) copy-start(bf16[576,512]{1,0:T(8,128)(2,1)} %go_ref.3) | copy-start | bytes 1769476
  0.6 8.4 %copy-start.2 = (bf16[576,512]{1,0:T(8,128)(2,1)S(1)}, bf16[576,512]{1,0:T(8,128)(2,1)}, u32[]{:S(2)}) copy-start(bf16[576,512]{1,0:T(8,128)(2,1)} %tok_ref.3) | copy-start | bytes 1769476
  0.7 18.7 %copy-start.1 = (bf16[1,1024,512]{2,1,0:T(8,128)(2,1)S(1)}, bf16[1,1024,512]{2,1,0:T(8,128)(2,1)}, u32[]{:S(2)}) copy-start(bf16[1,1024,512]{2,1,0:T(8,128)(2,1)} %param.10) | copy-start | bytes 3145732
  0.7 18.7 %copy-start = (bf16[1,512,1024]{2,1,0:T(8,128)(2,1)S(1)}, bf16[1,512,1024]{2,1,0:T(8,128)(2,1)}, u32[]{:S(2)}) copy-start(bf16[1,512,1024]{2,1,0:T(8,128)(2,1)} %param.9) | copy-start | bytes 3145732
  4.5 11.0 %collective-permute-start = (bf16[96,1024]{1,0:T(8,128)(2,1)}, bf16[96,1024]{1,0:T(8,128)(2,1)S(1)}, u32[]{:S(2)}, u32[]{:S(2)}) collective-permute-start(bf16[96,1024]{1,0:T(8,128)(2,1)} %get-tuple-element.52), channel_id=1, source_target_pairs={{0,16},{4,20},{8,24},{12,28},{16,0},{20,4},{24,8},{28,12},{1,17},{... | collective-permute-start | bytes 589832 | tf_op jit(solution)/shard_map/ppermute | solution.py:255
  7.5 8.3 %collective-permute-start.1 = (bf16[96,1024]{1,0:T(8,128)(2,1)}, bf16[96,1024]{1,0:T(8,128)(2,1)S(1)}, u32[]{:S(2)}, u32[]{:S(2)}) collective-permute-start(bf16[96,1024]{1,0:T(8,128)(2,1)} %get-tuple-element.53), channel_id=1, source_target_pairs={{0,8},{4,12},{8,0},{12,4},{16,24},{20,28},{24,16},{28,20},{1,9},{5... | collective-permute-start | bytes 589832 | tf_op jit(solution)/shard_map/ppermute | solution.py:255
  9.0 10.3 %collective-permute-start.2 = (bf16[96,1024]{1,0:T(8,128)(2,1)}, bf16[96,1024]{1,0:T(8,128)(2,1)S(1)}, u32[]{:S(2)}, u32[]{:S(2)}) collective-permute-start(bf16[96,1024]{1,0:T(8,128)(2,1)} %get-tuple-element.54), channel_id=1, source_target_pairs={{0,24},{4,28},{8,16},{12,20},{16,8},{20,12},{24,0},{28,4},{1,25},{... | collective-permute-start | bytes 589832 | tf_op jit(solution)/shard_map/ppermute | solution.py:255
  9.1 0.7 copy-start.4
  9.7 0.7 copy-start.6
  10.4 0.7 copy-start.8
  12.4 6.9 %collective-permute-start.3 = (bf16[96,1024]{1,0:T(8,128)(2,1)S(1)}, bf16[96,1024]{1,0:T(8,128)(2,1)S(1)}, u32[]{:S(2)}, u32[]{:S(2)}) collective-permute-start(bf16[96,1024]{1,0:T(8,128)(2,1)S(1)} %get-tuple-element.55), channel_id=1, source_target_pairs={{0,4},{4,0},{8,12},{12,8},{16,20},{20,16},{24,28},{28,24},{1,5},{5... | collective-permute-start | bytes 589832 | tf_op jit(solution)/shard_map/ppermute | solution.py:255
  12.5 10.3 %collective-permute-start.4 = (bf16[96,1024]{1,0:T(8,128)(2,1)}, bf16[96,1024]{1,0:T(8,128)(2,1)S(1)}, u32[]{:S(2)}, u32[]{:S(2)}) collective-permute-start(bf16[96,1024]{1,0:T(8,128)(2,1)} %get-tuple-element.59), channel_id=1, source_target_pairs={{0,28},{4,24},{8,20},{12,16},{16,12},{20,8},{24,4},{28,0},{1,29},{... | collective-permute-start | bytes 589832 | tf_op jit(solution)/shard_map/ppermute | solution.py:255
  15.5 11.0 %collective-permute-start.5 = (bf16[96,1024]{1,0:T(8,128)(2,1)S(1)}, bf16[96,1024]{1,0:T(8,128)(2,1)S(1)}, u32[]{:S(2)}, u32[]{:S(2)}) collective-permute-start(bf16[96,1024]{1,0:T(8,128)(2,1)S(1)} %get-tuple-element.62), channel_id=1, source_target_pairs={{0,20},{4,16},{8,28},{12,24},{16,4},{20,0},{24,12},{28,8},{1,21},{... | collective-permute-start | bytes 589832 | tf_op jit(solution)/shard_map/ppermute | solution.py:255
  15.8 10.7 %collective-permute-start.6 = (bf16[96,1024]{1,0:T(8,128)(2,1)S(1)}, bf16[96,1024]{1,0:T(8,128)(2,1)S(1)}, u32[]{:S(2)}, u32[]{:S(2)}) collective-permute-start(bf16[96,1024]{1,0:T(8,128)(2,1)S(1)} %get-tuple-element.63), channel_id=1, source_target_pairs={{0,12},{4,8},{8,4},{12,0},{16,28},{20,24},{24,20},{28,16},{1,13},{... | collective-permute-start | bytes 589832 | tf_op jit(solution)/shard_map/ppermute | solution.py:255
  28.6 19.8 %collective-permute-start.15 = (bf16[256,1024]{1,0:T(8,128)(2,1)S(1)}, bf16[256,1024]{1,0:T(8,128)(2,1)S(1)}, u32[]{:S(2)}, u32[]{:S(2)}) collective-permute-start(bf16[256,1024]{1,0:T(8,128)(2,1)S(1)} %get-tuple-element.90), channel_id=1, source_target_pairs={{0,1},{1,0},{2,3},{3,2},{4,5},{5,4},{6,7},{7,6},{8,9},{9,8},{10,11... | collective-permute-start | bytes 1572872 | tf_op jit(solution)/shard_map/ppermute | solution.py:282
  30.4 18.0 %collective-permute-start.16 = (bf16[256,1024]{1,0:T(8,128)(2,1)S(1)}, bf16[256,1024]{1,0:T(8,128)(2,1)S(1)}, u32[]{:S(2)}, u32[]{:S(2)}) collective-permute-start(bf16[256,1024]{1,0:T(8,128)(2,1)S(1)} %get-tuple-element.79), channel_id=1, source_target_pairs={{0,0},{1,2},{2,1},{3,3},{4,4},{5,6},{6,5},{7,7},{8,8},{9,10},{10,9... | collective-permute-start | bytes 1572872 | tf_op jit(solution)/shard_map/ppermute | solution.py:281
  31.1 33.7 %copy-start.5 = (s32[1,576]{1,0:T(1,128)S(1)}, s32[1,576]{1,0:T(1,128)}, u32[]{:S(2)}) copy-start(s32[1,576]{1,0:T(1,128)} %get-tuple-element.51.target_ref) | copy-start | bytes 6916
  31.1 33.7 %copy-start.7 = (bf16[576]{0:T(1024)(128)(2,1)S(1)}, bf16[576]{0:T(1024)(128)(2,1)}, u32[]{:S(2)}) copy-start(bf16[576]{0:T(1024)(128)(2,1)} %gate_ref.3) | copy-start | bytes 3460
  31.1 33.7 %copy-start.9 = (f32[512]{0:T(512)S(1)}, f32[512]{0:T(512)}, u32[]{:S(2)}) copy-start(f32[512]{0:T(512)} %param.8) | copy-start | bytes 6148
  32.5 8.8 %collective-permute-start.7 = (bf16[96,640]{1,0:T(8,128)(2,1)S(1)}, bf16[96,640]{1,0:T(8,128)(2,1)S(1)}, u32[]{:S(2)}, u32[]{:S(2)}) collective-permute-start(bf16[96,640]{1,0:T(8,128)(2,1)S(1)} %get-tuple-element.71), channel_id=1, source_target_pairs={{0,16},{4,20},{8,24},{12,28},{16,0},{20,4},{24,8},{28,12},{1,17},{... | collective-permute-start | bytes 368648 | tf_op jit(solution)/shard_map/ppermute | solution.py:255
  34.1 7.8 %collective-permute-start.8 = (bf16[96,640]{1,0:T(8,128)(2,1)S(1)}, bf16[96,640]{1,0:T(8,128)(2,1)S(1)}, u32[]{:S(2)}, u32[]{:S(2)}) collective-permute-start(bf16[96,640]{1,0:T(8,128)(2,1)S(1)} %get-tuple-element.72), channel_id=1, source_target_pairs={{0,8},{4,12},{8,0},{12,4},{16,24},{20,28},{24,16},{28,20},{1,9},{5... | collective-permute-start | bytes 368648 | tf_op jit(solution)/shard_map/ppermute | solution.py:255
  35.6 23.5 %collective-permute-start.11 = (bf16[256,1024]{1,0:T(8,128)(2,1)S(1)}, bf16[256,1024]{1,0:T(8,128)(2,1)S(1)}, u32[]{:S(2)}, u32[]{:S(2)}) collective-permute-start(bf16[256,1024]{1,0:T(8,128)(2,1)S(1)} %get-tuple-element.79), channel_id=1, source_target_pairs={{0,2},{3,1},{4,6},{7,5},{8,10},{11,9},{12,14},{15,13},{16,18},{19,... | collective-permute-start | bytes 1572872 | tf_op jit(solution)/shard_map/ppermute | solution.py:283
  41.3 7.1 %collective-permute-start.9 = (bf16[96,640]{1,0:T(8,128)(2,1)S(1)}, bf16[96,640]{1,0:T(8,128)(2,1)S(1)}, u32[]{:S(2)}, u32[]{:S(2)}) collective-permute-start(bf16[96,640]{1,0:T(8,128)(2,1)S(1)} %get-tuple-element.73), channel_id=1, source_target_pairs={{0,24},{4,28},{8,16},{12,20},{16,8},{20,12},{24,0},{28,4},{1,25},{... | collective-permute-start | bytes 368648 | tf_op jit(solution)/shard_map/ppermute | solution.py:255
  41.9 6.5 %collective-permute-start.10 = (bf16[96,640]{1,0:T(8,128)(2,1)S(1)}, bf16[96,640]{1,0:T(8,128)(2,1)S(1)}, u32[]{:S(2)}, u32[]{:S(2)}) collective-permute-start(bf16[96,640]{1,0:T(8,128)(2,1)S(1)} %get-tuple-element.74), channel_id=1, source_target_pairs={{0,28},{4,24},{8,20},{12,16},{16,12},{20,8},{24,4},{28,0},{1,29},{... | collective-permute-start | bytes 368648 | tf_op jit(solution)/shard_map/ppermute | solution.py:255
  48.7 22.5 %collective-permute-start.17 = (bf16[256,1024]{1,0:T(8,128)(2,1)S(1)}, bf16[256,1024]{1,0:T(8,128)(2,1)S(1)}, u32[]{:S(2)}, u32[]{:S(2)}) collective-permute-start(bf16[256,1024]{1,0:T(8,128)(2,1)S(1)} %get-tuple-element.95), channel_id=1, source_target_pairs={{0,1},{3,2},{1,3},{2,0},{4,5},{7,6},{5,7},{6,4},{8,9},{11,10},{9,1... | collective-permute-start | bytes 1572872 | tf_op jit(solution)/shard_map/ppermute | solution.py:294
  59.0 5.6 %collective-permute-start.12 = (bf16[96,640]{1,0:T(8,128)(2,1)S(1)}, bf16[96,640]{1,0:T(8,128)(2,1)S(1)}, u32[]{:S(2)}, u32[]{:S(2)}) collective-permute-start(bf16[96,640]{1,0:T(8,128)(2,1)S(1)} %get-tuple-element.84), channel_id=1, source_target_pairs={{0,20},{4,16},{8,28},{12,24},{16,4},{20,0},{24,12},{28,8},{1,21},{... | collective-permute-start | bytes 368648 | tf_op jit(solution)/shard_map/ppermute | solution.py:255
  59.1 5.7 %collective-permute-start.13 = (bf16[96,640]{1,0:T(8,128)(2,1)S(1)}, bf16[96,640]{1,0:T(8,128)(2,1)S(1)}, u32[]{:S(2)}, u32[]{:S(2)}) collective-permute-start(bf16[96,640]{1,0:T(8,128)(2,1)S(1)} %get-tuple-element.85), channel_id=1, source_target_pairs={{0,12},{4,8},{8,4},{12,0},{16,28},{20,24},{24,20},{28,16},{1,13},{... | collective-permute-start | bytes 368648 | tf_op jit(solution)/shard_map/ppermute | solution.py:255
  61.7 3.1 %collective-permute-start.14 = (bf16[96,640]{1,0:T(8,128)(2,1)S(1)}, bf16[96,640]{1,0:T(8,128)(2,1)S(1)}, u32[]{:S(2)}, u32[]{:S(2)}) collective-permute-start(bf16[96,640]{1,0:T(8,128)(2,1)S(1)} %get-tuple-element.86), channel_id=1, source_target_pairs={{0,4},{4,0},{8,12},{12,8},{16,20},{20,16},{24,28},{28,24},{1,5},{5... | collective-permute-start | bytes 368648 | tf_op jit(solution)/shard_map/ppermute | solution.py:255

commit v11 on v10

--- a/solution.py
+++ b/solution.py
@@ -276,12 +276,13 @@
 def line_sums(place, first, second, third, own, width, returned):
     rows, hidden = own.shape
     piece_d = width // LINE
-    half = len(returned) // 2
+    ahead = 3 * len(returned) // 8
     order = block_order(len(returned))
     middle = lax.ppermute(second, "dp", [(0, 0), (1, 2), (2, 1), (3, 3)])
     swapped = lax.ppermute(first, "dp", [(0, 1), (1, 0), (2, 3), (3, 2)])
+    back = swap_blocks(returned[:ahead], order[:ahead])
+    second, back[0] = lax.optimization_barrier((second, back[0]))
     across = lax.ppermute(second, "dp", [(0, 2), (3, 1)])
-    back = swap_blocks(returned[:half], order[:half])
     third, *back = lax.optimization_barrier((third, *back))
     passed, most = kernel_call(
         pass_kernel,
@@ -292,8 +293,8 @@
         [smem] + [vmem] * 4,
     )(place, swapped, middle, third, own)
     last = lax.ppermute(passed, "dp", [(0, 1), (3, 2), (1, 3), (2, 0)])
-    across, *rest = lax.optimization_barrier((across, *returned[half:]))
-    back += swap_blocks(rest, order[half:])
+    across, *rest = lax.optimization_barrier((across, *returned[ahead:]))
+    back += swap_blocks(rest, order[ahead:])
     sums = kernel_call(
         total_kernel,
         "total",

time: 72.5 us -> 72.5 us (level)
  starting transfers between devices: 33.6 us -> 31.9 us
  waiting for transfers between devices: 18 us -> 19.7 us
    ppermute x14, waiting for transfers between devices: 14.2 us -> 19.1 us  [swap_blocks(): lax.ppermute(block, 'space', [(i, i ^ k) for i in devices])]
    ppermute x1, waiting for transfers between devices: 3.8 us -> 0.54 us  [line_sums(): last = lax.ppermute(passed, 'dp', [(0, 1), (3, 2), (1, 3), (2, 0)])]
    ppermute x1, starting transfers between devices: 10.3 us -> 7.73 us  [line_sums(): last = lax.ppermute(passed, 'dp', [(0, 1), (3, 2), (1, 3), (2, 0)])]
    ppermute x14, starting transfers between devices: 15.2 us -> 16 us  [swap_blocks(): lax.ppermute(block, 'space', [(i, i ^ k) for i in devices])]
  transfers between devices with their start and end apart: 18 -> 18, of which waited for: 7 -> 9; matrix products, arithmetic and copies ran while one was open for 0% -> 0% of each run, Pallas kernels for 15% -> 15%
where the time goes in v11:
time: 72.5 us; the launch traced here: 72.3 us
  starting transfers between devices  31.9 us (44%)
  waiting for transfers between devices  19.7 us (27%)
  Pallas kernels  17.8 us (25%)
  local copies, waits for them, and re-layouts  2.07 us (3%)
  between operations  0.81 us (1%)
    ppermute x14, waiting for transfers between devices, swap_blocks(): lax.ppermute(block, 'space', [(i, i ^ k) for i in devices])  19.1 us
    ppermute x14, starting transfers between devices, swap_blocks(): lax.ppermute(block, 'space', [(i, i ^ k) for i in devices])  16 us
    ppermute x1, starting transfers between devices, line_sums(): last = lax.ppermute(passed, 'dp', [(0, 1), (3, 2), (1, 3), (2, 0)])  7.73 us
    pallas_call x3, Pallas kernels, work(): kernel_call(functools.partial(kernel, count, groups), name, 8 * span * wi...  7.32 us
    ppermute x1, starting transfers between devices, line_sums(): across = lax.ppermute(second, 'dp', [(0, 2), (3, 1)])  5.75 us
    pallas_call x1, Pallas kernels, body(): kernel_call(functools.partial(place_kernel, sources, capacity), 'place',...  3.8 us
    pallas_call x1, Pallas kernels, body(): kernel_call(finish_kernel, 'finish', 1, 1, [shape((tok_rows, width), BF16...  2.59 us
    unnamed x20, local copies, waits for them, and re-layouts  2.07 us
  transfers between devices with their start and end apart: 18, of which 9 were waited for; matrix products, arithmetic and copies ran while one was open for 0% of the time, Pallas kernels for 15%

profile of v11, /device:TPU:0, one launch (start us, length us, event | category | flops | bytes accessed | tf_op | source)
XLA Modules:
  0.0 72.3 jit_solution(13523965115277701637)
XLA Ops:
  0.7 3.8 %place.1 = (s32[1,576]{1,0:T(1,128)}, bf16[96,1024]{1,0:T(8,128)(2,1)}, bf16[96,1024]{1,0:T(8,128)(2,1)}, bf16[96,1024]{1,0:T(8,128)(2,1)}, bf16[96,1024]{1,0:T(8,128)(2,1)}) custom-call(s32[1]{0:T(128)} %bitcast.me, s32[1]{0:T(128)} %bitcast.1.place, s32[1,576]{1,0:T(1,128)} %bitcast.20, bf16[576]{0:T(1024)(128)(2,1)} %gate_ref.3, ...), custom_call_target="tpu_custom_call" | custom-call | flops 452984832 | bytes 2752512 | tf_op jit(solution)/shard_map/place/pallas_call | solution.py:331
  4.5 3.0 %collective-permute-start = (bf16[96,1024]{1,0:T(8,128)(2,1)}, bf16[96,1024]{1,0:T(8,128)(2,1)S(1)}, u32[]{:S(2)}, u32[]{:S(2)}) collective-permute-start(bf16[96,1024]{1,0:T(8,128)(2,1)} %get-tuple-element.54), channel_id=1, source_target_pairs={{0,16},{4,20},{8,24},{12,28},{16,0},{20,4},{24,8},{28,12},{1,17},{... | collective-permute-start | bytes 589832 | tf_op jit(solution)/shard_map/ppermute | solution.py:255
  7.5 1.5 %collective-permute-start.1 = (bf16[96,1024]{1,0:T(8,128)(2,1)}, bf16[96,1024]{1,0:T(8,128)(2,1)S(1)}, u32[]{:S(2)}, u32[]{:S(2)}) collective-permute-start(bf16[96,1024]{1,0:T(8,128)(2,1)} %get-tuple-element.55), channel_id=1, source_target_pairs={{0,8},{4,12},{8,0},{12,4},{16,24},{20,28},{24,16},{28,20},{1,9},{5... | collective-permute-start | bytes 589832 | tf_op jit(solution)/shard_map/ppermute | solution.py:255
  9.1 0.7 copy-done.4
  9.7 0.7 copy-done.6
  10.4 0.7 copy-done.8
  11.1 1.3 %rest.1 = (bf16[96,1024]{1,0:T(8,128)(2,1)S(1)}, bf16[96,1024]{1,0:T(8,128)(2,1)S(1)}, bf16[96,1024]{1,0:T(8,128)(2,1)S(1)}, bf16[96,1024]{1,0:T(8,128)(2,1)S(1)}) custom-call(s32[1,576]{1,0:T(1,128)S(1)} %copy-done.4, bf16[576]{0:T(1024)(128)(2,1)S(1)} %copy-done.6, bf16[576,512]{1,0:T(8,128)(2,1)S(1)} %copy-done.2, f32[1,512]{1,0:T(1,128)S(1)} %bitcast.16, ...), custom_call_target="tpu_custom_call" | custom-call | flops 1 | bytes 1 | tf_op jit(solution)/shard_map/rest/pallas_call | solution.py:352
  12.5 3.0 %collective-permute-start.4 = (bf16[96,1024]{1,0:T(8,128)(2,1)}, bf16[96,1024]{1,0:T(8,128)(2,1)S(1)}, u32[]{:S(2)}, u32[]{:S(2)}) collective-permute-start(bf16[96,1024]{1,0:T(8,128)(2,1)} %get-tuple-element.61), channel_id=1, source_target_pairs={{0,28},{4,24},{8,20},{12,16},{16,12},{20,8},{24,4},{28,0},{1,29},{... | collective-permute-start | bytes 589832 | tf_op jit(solution)/shard_map/ppermute | solution.py:255
  15.9 3.4 %collective-permute-done.2.refs_2_ = bf16[96,1024]{1,0:T(8,128)(2,1)S(1)} collective-permute-done((bf16[96,1024]{1,0:T(8,128)(2,1)}, bf16[96,1024]{1,0:T(8,128)(2,1)S(1)}, u32[]{:S(2)}, u32[]{:S(2)}) %collective-permute-start.2) | collective-permute-done | bytes 196640 | tf_op jit(solution)/shard_map/ppermute | solution.py:255
  19.3 3.2 %sooner.1 = (f32[512,1024]{1,0:T(8,128)S(1)}, f32[1024,512]{1,0:T(8,128)S(1)}, bf16[480,1024]{1,0:T(8,128)(2,1)S(1)}, bf16[480,128]{1,0:T(8,128)(2,1)S(1)}) custom-call(s32[1]{0:T(128)} %bitcast.1.place, bf16[512,1024]{1,0:T(8,128)(2,1)S(1)} %bitcast.8, bf16[1024,512]{1,0:T(8,128)(2,1)S(1)} %bitcast.12, bf16[96,1024]{1,0:T(8,128)(2,1)S(1)} %collective-permute-done.refs_0_, ...), custom_call_target="tpu_custom_call" | custom-call | flops 2013265920 | bytes 6160384 | tf_op jit(solution)/shard_map/sooner/pallas_call | solution.py:381
  22.8 2.0 %next.1 = (f32[512,1024]{1,0:T(8,128)S(1)}, f32[1024,512]{1,0:T(8,128)S(1)}, bf16[96,1024]{1,0:T(8,128)(2,1)S(1)}, bf16[96,128]{1,0:T(8,128)(2,1)S(1)}) custom-call(s32[1]{0:T(128)} %bitcast.1.place, bf16[512,1024]{1,0:T(8,128)(2,1)S(1)} %bitcast.9, bf16[1024,512]{1,0:T(8,128)(2,1)S(1)} %bitcast.13, f32[512,1024]{1,0:T(8,128)S(1)} %get-tuple-element.59.old_in_ref, ...), custom_call_target="tpu_custom_call" | custom-call | flops 402653184 | bytes 4587520 | tf_op jit(solution)/shard_map/next/pallas_call | solution.py:381
  24.7 1.8 %collective-permute-done.5.refs_0_ = bf16[96,1024]{1,0:T(8,128)(2,1)S(1)} collective-permute-done((bf16[96,1024]{1,0:T(8,128)(2,1)S(1)}, bf16[96,1024]{1,0:T(8,128)(2,1)S(1)}, u32[]{:S(2)}, u32[]{:S(2)}) %collective-permute-start.5) | collective-permute-done | bytes 196640 | tf_op jit(solution)/shard_map/ppermute | solution.py:255
  26.5 2.1 %later.1 = (bf16[256,1024]{1,0:T(8,128)(2,1)S(1)}, bf16[256,1024]{1,0:T(8,128)(2,1)S(1)}, bf16[256,1024]{1,0:T(8,128)(2,1)S(1)}, bf16[256,1024]{1,0:T(8,128)(2,1...) custom-call(s32[1]{0:T(128)} %bitcast.1.place, bf16[512,1024]{1,0:T(8,128)(2,1)S(1)} %bitcast.10, ...), custom_call_target="tpu_custom_call" | custom-call | flops 805306368 | bytes 4980736 | tf_op jit(solution)/shard_map/later/pallas_call | solution.py:381
  28.6 1.8 %collective-permute-start.15 = (bf16[256,1024]{1,0:T(8,128)(2,1)S(1)}, bf16[256,1024]{1,0:T(8,128)(2,1)S(1)}, u32[]{:S(2)}, u32[]{:S(2)}) collective-permute-start(bf16[256,1024]{1,0:T(8,128)(2,1)S(1)} %get-tuple-element.94), channel_id=1, source_target_pairs={{0,1},{1,0},{2,3},{3,2},{4,5},{5,4},{6,7},{7,6},{8,9},{9,8},{10,11... | collective-permute-start | bytes 1572872 | tf_op jit(solution)/shard_map/ppermute | solution.py:282
  30.4 0.7 collective-permute-start.16
  31.1 1.3 %back.1 = (bf16[96,640]{1,0:T(8,128)(2,1)S(1)}, bf16[96,640]{1,0:T(8,128)(2,1)S(1)}, bf16[96,640]{1,0:T(8,128)(2,1)S(1)}, bf16[96,640]{1,0:T(8,128)(2,1)S(1)}, b...) custom-call(bf16[512,1024]{1,0:T(8,128)(2,1)S(1)} %bitcast.11, ...), custom_call_target="tpu_custom_call" | custom-call | flops 1 | bytes 1 | tf_op jit(solution)/shard_map/back/pallas_call | solution.py:396
  32.5 1.6 %collective-permute-start.7 = (bf16[96,640]{1,0:T(8,128)(2,1)S(1)}, bf16[96,640]{1,0:T(8,128)(2,1)S(1)}, u32[]{:S(2)}, u32[]{:S(2)}) collective-permute-start(bf16[96,640]{1,0:T(8,128)(2,1)S(1)} %get-tuple-element.74), channel_id=1, source_target_pairs={{0,16},{4,20},{8,24},{12,28},{16,0},{20,4},{24,8},{28,12},{1,17},{... | collective-permute-start | bytes 368648 | tf_op jit(solution)/shard_map/ppermute | solution.py:255
  34.1 3.5 %collective-permute-done.7.refs_0_ = bf16[96,640]{1,0:T(8,128)(2,1)S(1)} collective-permute-done((bf16[96,640]{1,0:T(8,128)(2,1)S(1)}, bf16[96,640]{1,0:T(8,128)(2,1)S(1)}, u32[]{:S(2)}, u32[]{:S(2)}) %collective-permute-start.7) | collective-permute-done | bytes 122912 | tf_op jit(solution)/shard_map/ppermute | solution.py:255
  37.6 5.8 %collective-permute-start.10 = (bf16[256,1024]{1,0:T(8,128)(2,1)S(1)}, bf16[256,1024]{1,0:T(8,128)(2,1)S(1)}, u32[]{:S(2)}, u32[]{:S(2)}) collective-permute-start(bf16[256,1024]{1,0:T(8,128)(2,1)S(1)} %get-tuple-element.81), channel_id=1, source_target_pairs={{0,2},{3,1},{4,6},{7,5},{8,10},{11,9},{12,14},{15,13},{16,18},{19,... | collective-permute-start | bytes 1572872 | tf_op jit(solution)/shard_map/ppermute | solution.py:285
  43.4 1.6 %collective-permute-start.8 = (bf16[96,640]{1,0:T(8,128)(2,1)S(1)}, bf16[96,640]{1,0:T(8,128)(2,1)S(1)}, u32[]{:S(2)}, u32[]{:S(2)}) collective-permute-start(bf16[96,640]{1,0:T(8,128)(2,1)S(1)} %get-tuple-element.76), channel_id=1, source_target_pairs={{0,8},{4,12},{8,0},{12,4},{16,24},{20,28},{24,16},{28,20},{1,9},{5... | collective-permute-start | bytes 368648 | tf_op jit(solution)/shard_map/ppermute | solution.py:255
  44.9 1.5 %collective-permute-start.9 = (bf16[96,640]{1,0:T(8,128)(2,1)S(1)}, bf16[96,640]{1,0:T(8,128)(2,1)S(1)}, u32[]{:S(2)}, u32[]{:S(2)}) collective-permute-start(bf16[96,640]{1,0:T(8,128)(2,1)S(1)} %get-tuple-element.77), channel_id=1, source_target_pairs={{0,24},{4,28},{8,16},{12,20},{16,8},{20,12},{24,0},{28,4},{1,25},{... | collective-permute-start | bytes 368648 | tf_op jit(solution)/shard_map/ppermute | solution.py:255
  46.4 3.1 %collective-permute-done.8.refs_1_ = bf16[96,640]{1,0:T(8,128)(2,1)S(1)} collective-permute-done((bf16[96,640]{1,0:T(8,128)(2,1)S(1)}, bf16[96,640]{1,0:T(8,128)(2,1)S(1)}, u32[]{:S(2)}, u32[]{:S(2)}) %collective-permute-start.8) | collective-permute-done | bytes 122912 | tf_op jit(solution)/shard_map/ppermute | solution.py:255
  49.5 1.4 %collective-permute-done.9.refs_2_ = bf16[96,640]{1,0:T(8,128)(2,1)S(1)} collective-permute-done((bf16[96,640]{1,0:T(8,128)(2,1)S(1)}, bf16[96,640]{1,0:T(8,128)(2,1)S(1)}, u32[]{:S(2)}, u32[]{:S(2)}) %collective-permute-start.9) | collective-permute-done | bytes 122912 | tf_op jit(solution)/shard_map/ppermute | solution.py:255
  51.3 7.7 %collective-permute-start.17 = (bf16[256,1024]{1,0:T(8,128)(2,1)S(1)}, bf16[256,1024]{1,0:T(8,128)(2,1)S(1)}, u32[]{:S(2)}, u32[]{:S(2)}) collective-permute-start(bf16[256,1024]{1,0:T(8,128)(2,1)S(1)} %get-tuple-element.99), channel_id=1, source_target_pairs={{0,1},{3,2},{1,3},{2,0},{4,5},{7,6},{5,7},{6,4},{8,9},{11,10},{9,1... | collective-permute-start | bytes 1572872 | tf_op jit(solution)/shard_map/ppermute | solution.py:295
  59.0 1.1 %collective-permute-start.11 = (bf16[96,640]{1,0:T(8,128)(2,1)S(1)}, bf16[96,640]{1,0:T(8,128)(2,1)S(1)}, u32[]{:S(2)}, u32[]{:S(2)}) collective-permute-start(bf16[96,640]{1,0:T(8,128)(2,1)S(1)} %get-tuple-element.87), channel_id=1, source_target_pairs={{0,28},{4,24},{8,20},{12,16},{16,12},{20,8},{24,4},{28,0},{1,29},{... | collective-permute-start | bytes 368648 | tf_op jit(solution)/shard_map/ppermute | solution.py:255
  60.1 1.6 %collective-permute-start.12 = (bf16[96,640]{1,0:T(8,128)(2,1)S(1)}, bf16[96,640]{1,0:T(8,128)(2,1)S(1)}, u32[]{:S(2)}, u32[]{:S(2)}) collective-permute-start(bf16[96,640]{1,0:T(8,128)(2,1)S(1)} %get-tuple-element.88), channel_id=1, source_target_pairs={{0,20},{4,16},{8,28},{12,24},{16,4},{20,0},{24,12},{28,8},{1,21},{... | collective-permute-start | bytes 368648 | tf_op jit(solution)/shard_map/ppermute | solution.py:255
  61.7 0.6 collective-permute-start.14
  62.3 3.2 %collective-permute-done.11.refs_3_ = bf16[96,640]{1,0:T(8,128)(2,1)S(1)} collective-permute-done((bf16[96,640]{1,0:T(8,128)(2,1)S(1)}, bf16[96,640]{1,0:T(8,128)(2,1)S(1)}, u32[]{:S(2)}, u32[]{:S(2)}) %collective-permute-start.11) | collective-permute-done | bytes 122912 | tf_op jit(solution)/shard_map/ppermute | solution.py:255
  65.5 2.5 %collective-permute-done.12.refs_4_ = bf16[96,640]{1,0:T(8,128)(2,1)S(1)} collective-permute-done((bf16[96,640]{1,0:T(8,128)(2,1)S(1)}, bf16[96,640]{1,0:T(8,128)(2,1)S(1)}, u32[]{:S(2)}, u32[]{:S(2)}) %collective-permute-start.12) | collective-permute-done | bytes 122912 | tf_op jit(solution)/shard_map/ppermute | solution.py:255
  68.1 2.6 %finish.1 = (bf16[576,512]{1,0:T(8,128)(2,1)}, bf16[576]{0:T(1024)(128)(2,1)}) custom-call(s32[1,576]{1,0:T(1,128)S(1)} %copy-done.5, bf16[576]{0:T(1024)(128)(2,1)S(1)} %copy-done.7, bf16[576,512]{1,0:T(8,128)(2,1)S(1)} %copy-done.2, f32[1,512]{1,0:T(1,128)S(1)} %bitcast.17, bf16[576,512]{1,0:T(8,128)(2,1)S(1)} %copy-done.3, ...), custom_call_target="tpu_custom_call" | custom-call | flops 1 | bytes 1 | tf_op jit(solution)/shard_map/finish/pallas_call | solution.py:416
  70.7 0.5 collective-permute-done.17.last_ref
  71.2 1.1 %total.1 = (f32[128,1024]{1,0:T(8,128)}, f32[256,512]{1,0:T(8,128)}) custom-call(f32[256,1024]{1,0:T(8,128)S(1)} %get-tuple-element.97.sum_ref, bf16[256,1024]{1,0:T(8,128)(2,1)S(1)} %collective-permute-done.10.across_ref, bf16[256,1024]{1,0:T(8,128)(2,1)S(1)} %collective-permute-done.17.last_ref), custom_call_target="tpu_custom_call" | custom-call | flops 1 | bytes 1 | tf_op jit(solution)/shard_map/total/pallas_call | solution.py:298
  (34 shorter events, 1.2 us)
Async XLA Ops:
  0.6 8.4 %copy-start.3 = (bf16[576,512]{1,0:T(8,128)(2,1)S(1)}, bf16[576,512]{1,0:T(8,128)(2,1)}, u32[]{:S(2)}) copy-start(bf16[576,512]{1,0:T(8,128)(2,1)} %go_ref.3) | copy-start | bytes 1769476
  0.6 8.4 %copy-start.2 = (bf16[576,512]{1,0:T(8,128)(2,1)S(1)}, bf16[576,512]{1,0:T(8,128)(2,1)}, u32[]{:S(2)}) copy-start(bf16[576,512]{1,0:T(8,128)(2,1)} %tok_ref.3) | copy-start | bytes 1769476
  0.7 18.7 %copy-start.1 = (bf16[1,1024,512]{2,1,0:T(8,128)(2,1)S(1)}, bf16[1,1024,512]{2,1,0:T(8,128)(2,1)}, u32[]{:S(2)}) copy-start(bf16[1,1024,512]{2,1,0:T(8,128)(2,1)} %param.10) | copy-start | bytes 3145732
  0.7 18.7 %copy-start = (bf16[1,512,1024]{2,1,0:T(8,128)(2,1)S(1)}, bf16[1,512,1024]{2,1,0:T(8,128)(2,1)}, u32[]{:S(2)}) copy-start(bf16[1,512,1024]{2,1,0:T(8,128)(2,1)} %param.9) | copy-start | bytes 3145732
  4.5 11.0 %collective-permute-start = (bf16[96,1024]{1,0:T(8,128)(2,1)}, bf16[96,1024]{1,0:T(8,128)(2,1)S(1)}, u32[]{:S(2)}, u32[]{:S(2)}) collective-permute-start(bf16[96,1024]{1,0:T(8,128)(2,1)} %get-tuple-element.54), channel_id=1, source_target_pairs={{0,16},{4,20},{8,24},{12,28},{16,0},{20,4},{24,8},{28,12},{1,17},{... | collective-permute-start | bytes 589832 | tf_op jit(solution)/shard_map/ppermute | solution.py:255
  7.5 8.3 %collective-permute-start.1 = (bf16[96,1024]{1,0:T(8,128)(2,1)}, bf16[96,1024]{1,0:T(8,128)(2,1)S(1)}, u32[]{:S(2)}, u32[]{:S(2)}) collective-permute-start(bf16[96,1024]{1,0:T(8,128)(2,1)} %get-tuple-element.55), channel_id=1, source_target_pairs={{0,8},{4,12},{8,0},{12,4},{16,24},{20,28},{24,16},{28,20},{1,9},{5... | collective-permute-start | bytes 589832 | tf_op jit(solution)/shard_map/ppermute | solution.py:255
  9.0 10.3 %collective-permute-start.2 = (bf16[96,1024]{1,0:T(8,128)(2,1)}, bf16[96,1024]{1,0:T(8,128)(2,1)S(1)}, u32[]{:S(2)}, u32[]{:S(2)}) collective-permute-start(bf16[96,1024]{1,0:T(8,128)(2,1)} %get-tuple-element.56), channel_id=1, source_target_pairs={{0,24},{4,28},{8,16},{12,20},{16,8},{20,12},{24,0},{28,4},{1,25},{... | collective-permute-start | bytes 589832 | tf_op jit(solution)/shard_map/ppermute | solution.py:255
  9.1 0.7 copy-start.4
  9.7 0.7 copy-start.6
  10.4 0.7 copy-start.8
  12.4 6.9 %collective-permute-start.3 = (bf16[96,1024]{1,0:T(8,128)(2,1)S(1)}, bf16[96,1024]{1,0:T(8,128)(2,1)S(1)}, u32[]{:S(2)}, u32[]{:S(2)}) collective-permute-start(bf16[96,1024]{1,0:T(8,128)(2,1)S(1)} %get-tuple-element.57), channel_id=1, source_target_pairs={{0,4},{4,0},{8,12},{12,8},{16,20},{20,16},{24,28},{28,24},{1,5},{5... | collective-permute-start | bytes 589832 | tf_op jit(solution)/shard_map/ppermute | solution.py:255
  12.5 10.3 %collective-permute-start.4 = (bf16[96,1024]{1,0:T(8,128)(2,1)}, bf16[96,1024]{1,0:T(8,128)(2,1)S(1)}, u32[]{:S(2)}, u32[]{:S(2)}) collective-permute-start(bf16[96,1024]{1,0:T(8,128)(2,1)} %get-tuple-element.61), channel_id=1, source_target_pairs={{0,28},{4,24},{8,20},{12,16},{16,12},{20,8},{24,4},{28,0},{1,29},{... | collective-permute-start | bytes 589832 | tf_op jit(solution)/shard_map/ppermute | solution.py:255
  15.5 11.0 %collective-permute-start.5 = (bf16[96,1024]{1,0:T(8,128)(2,1)S(1)}, bf16[96,1024]{1,0:T(8,128)(2,1)S(1)}, u32[]{:S(2)}, u32[]{:S(2)}) collective-permute-start(bf16[96,1024]{1,0:T(8,128)(2,1)S(1)} %get-tuple-element.64), channel_id=1, source_target_pairs={{0,20},{4,16},{8,28},{12,24},{16,4},{20,0},{24,12},{28,8},{1,21},{... | collective-permute-start | bytes 589832 | tf_op jit(solution)/shard_map/ppermute | solution.py:255
  15.8 10.7 %collective-permute-start.6 = (bf16[96,1024]{1,0:T(8,128)(2,1)S(1)}, bf16[96,1024]{1,0:T(8,128)(2,1)S(1)}, u32[]{:S(2)}, u32[]{:S(2)}) collective-permute-start(bf16[96,1024]{1,0:T(8,128)(2,1)S(1)} %get-tuple-element.65), channel_id=1, source_target_pairs={{0,12},{4,8},{8,4},{12,0},{16,28},{20,24},{24,20},{28,16},{1,13},{... | collective-permute-start | bytes 589832 | tf_op jit(solution)/shard_map/ppermute | solution.py:255
  28.6 22.3 %collective-permute-start.15 = (bf16[256,1024]{1,0:T(8,128)(2,1)S(1)}, bf16[256,1024]{1,0:T(8,128)(2,1)S(1)}, u32[]{:S(2)}, u32[]{:S(2)}) collective-permute-start(bf16[256,1024]{1,0:T(8,128)(2,1)S(1)} %get-tuple-element.94), channel_id=1, source_target_pairs={{0,1},{1,0},{2,3},{3,2},{4,5},{5,4},{6,7},{7,6},{8,9},{9,8},{10,11... | collective-permute-start | bytes 1572872 | tf_op jit(solution)/shard_map/ppermute | solution.py:282
  30.4 20.5 %collective-permute-start.16 = (bf16[256,1024]{1,0:T(8,128)(2,1)S(1)}, bf16[256,1024]{1,0:T(8,128)(2,1)S(1)}, u32[]{:S(2)}, u32[]{:S(2)}) collective-permute-start(bf16[256,1024]{1,0:T(8,128)(2,1)S(1)} %get-tuple-element.81), channel_id=1, source_target_pairs={{0,0},{1,2},{2,1},{3,3},{4,4},{5,6},{6,5},{7,7},{8,8},{9,10},{10,9... | collective-permute-start | bytes 1572872 | tf_op jit(solution)/shard_map/ppermute | solution.py:281
  31.1 37.0 %copy-start.5 = (s32[1,576]{1,0:T(1,128)S(1)}, s32[1,576]{1,0:T(1,128)}, u32[]{:S(2)}) copy-start(s32[1,576]{1,0:T(1,128)} %get-tuple-element.53.target_ref) | copy-start | bytes 6916
  31.1 37.0 %copy-start.7 = (bf16[576]{0:T(1024)(128)(2,1)S(1)}, bf16[576]{0:T(1024)(128)(2,1)}, u32[]{:S(2)}) copy-start(bf16[576]{0:T(1024)(128)(2,1)} %gate_ref.3) | copy-start | bytes 3460
  31.1 37.0 %copy-start.9 = (f32[512]{0:T(512)S(1)}, f32[512]{0:T(512)}, u32[]{:S(2)}) copy-start(f32[512]{0:T(512)} %param.8) | copy-start | bytes 6148
  32.5 5.1 %collective-permute-start.7 = (bf16[96,640]{1,0:T(8,128)(2,1)S(1)}, bf16[96,640]{1,0:T(8,128)(2,1)S(1)}, u32[]{:S(2)}, u32[]{:S(2)}) collective-permute-start(bf16[96,640]{1,0:T(8,128)(2,1)S(1)} %get-tuple-element.74), channel_id=1, source_target_pairs={{0,16},{4,20},{8,24},{12,28},{16,0},{20,4},{24,8},{28,12},{1,17},{... | collective-permute-start | bytes 368648 | tf_op jit(solution)/shard_map/ppermute | solution.py:255
  37.6 21.4 %collective-permute-start.10 = (bf16[256,1024]{1,0:T(8,128)(2,1)S(1)}, bf16[256,1024]{1,0:T(8,128)(2,1)S(1)}, u32[]{:S(2)}, u32[]{:S(2)}) collective-permute-start(bf16[256,1024]{1,0:T(8,128)(2,1)S(1)} %get-tuple-element.81), channel_id=1, source_target_pairs={{0,2},{3,1},{4,6},{7,5},{8,10},{11,9},{12,14},{15,13},{16,18},{19,... | collective-permute-start | bytes 1572872 | tf_op jit(solution)/shard_map/ppermute | solution.py:285
  43.4 6.1 %collective-permute-start.8 = (bf16[96,640]{1,0:T(8,128)(2,1)S(1)}, bf16[96,640]{1,0:T(8,128)(2,1)S(1)}, u32[]{:S(2)}, u32[]{:S(2)}) collective-permute-start(bf16[96,640]{1,0:T(8,128)(2,1)S(1)} %get-tuple-element.76), channel_id=1, source_target_pairs={{0,8},{4,12},{8,0},{12,4},{16,24},{20,28},{24,16},{28,20},{1,9},{5... | collective-permute-start | bytes 368648 | tf_op jit(solution)/shard_map/ppermute | solution.py:255
  44.9 6.0 %collective-permute-start.9 = (bf16[96,640]{1,0:T(8,128)(2,1)S(1)}, bf16[96,640]{1,0:T(8,128)(2,1)S(1)}, u32[]{:S(2)}, u32[]{:S(2)}) collective-permute-start(bf16[96,640]{1,0:T(8,128)(2,1)S(1)} %get-tuple-element.77), channel_id=1, source_target_pairs={{0,24},{4,28},{8,16},{12,20},{16,8},{20,12},{24,0},{28,4},{1,25},{... | collective-permute-start | bytes 368648 | tf_op jit(solution)/shard_map/ppermute | solution.py:255
  51.3 20.0 %collective-permute-start.17 = (bf16[256,1024]{1,0:T(8,128)(2,1)S(1)}, bf16[256,1024]{1,0:T(8,128)(2,1)S(1)}, u32[]{:S(2)}, u32[]{:S(2)}) collective-permute-start(bf16[256,1024]{1,0:T(8,128)(2,1)S(1)} %get-tuple-element.99), channel_id=1, source_target_pairs={{0,1},{3,2},{1,3},{2,0},{4,5},{7,6},{5,7},{6,4},{8,9},{11,10},{9,1... | collective-permute-start | bytes 1572872 | tf_op jit(solution)/shard_map/ppermute | solution.py:295
  59.0 6.5 %collective-permute-start.11 = (bf16[96,640]{1,0:T(8,128)(2,1)S(1)}, bf16[96,640]{1,0:T(8,128)(2,1)S(1)}, u32[]{:S(2)}, u32[]{:S(2)}) collective-permute-start(bf16[96,640]{1,0:T(8,128)(2,1)S(1)} %get-tuple-element.87), channel_id=1, source_target_pairs={{0,28},{4,24},{8,20},{12,16},{16,12},{20,8},{24,4},{28,0},{1,29},{... | collective-permute-start | bytes 368648 | tf_op jit(solution)/shard_map/ppermute | solution.py:255
  60.1 8.0 %collective-permute-start.12 = (bf16[96,640]{1,0:T(8,128)(2,1)S(1)}, bf16[96,640]{1,0:T(8,128)(2,1)S(1)}, u32[]{:S(2)}, u32[]{:S(2)}) collective-permute-start(bf16[96,640]{1,0:T(8,128)(2,1)S(1)} %get-tuple-element.88), channel_id=1, source_target_pairs={{0,20},{4,16},{8,28},{12,24},{16,4},{20,0},{24,12},{28,8},{1,21},{... | collective-permute-start | bytes 368648 | tf_op jit(solution)/shard_map/ppermute | solution.py:255
  61.7 6.4 %collective-permute-start.13 = (bf16[96,640]{1,0:T(8,128)(2,1)S(1)}, bf16[96,640]{1,0:T(8,128)(2,1)S(1)}, u32[]{:S(2)}, u32[]{:S(2)}) collective-permute-start(bf16[96,640]{1,0:T(8,128)(2,1)S(1)} %get-tuple-element.89), channel_id=1, source_target_pairs={{0,12},{4,8},{8,4},{12,0},{16,28},{20,24},{24,20},{28,16},{1,13},{... | collective-permute-start | bytes 368648 | tf_op jit(solution)/shard_map/ppermute | solution.py:255
  61.7 6.3 %collective-permute-start.14 = (bf16[96,640]{1,0:T(8,128)(2,1)S(1)}, bf16[96,640]{1,0:T(8,128)(2,1)S(1)}, u32[]{:S(2)}, u32[]{:S(2)}) collective-permute-start(bf16[96,640]{1,0:T(8,128)(2,1)S(1)} %get-tuple-element.90), channel_id=1, source_target_pairs={{0,4},{4,0},{8,12},{12,8},{16,20},{20,16},{24,28},{28,24},{1,5},{5... | collective-permute-start | bytes 368648 | tf_op jit(solution)/shard_map/ppermute | solution.py:255

commit v12 on v11

--- a/solution.py
+++ b/solution.py
@@ -135,9 +135,8 @@
 
 
 def shard_order(place):
-    first = jnp.where(lax.rem(place, 2) == 0, 3, 0)
-    second = jnp.where(place < 2, 2, 1)
-    return [first, second, 6 - first - second - place, place]
+    second = jnp.where(place < 2, 2 - 2 * place, 7 - 2 * place)
+    return [3 - place, second, 3 - second, place]
 
 
 def expert_work(order, blocks, w_in_ref, w_out_ref, gpre_ref, extra_ref, rows_ref, turned_ref, put):
@@ -257,32 +256,29 @@
     ]
 
 
-def pass_kernel(place, swapped_ref, middle_ref, third_ref, own_ref, out_ref, sum_ref):
-    inner = (place[0] == 1) | (place[0] == 2)
-    swapped, middle = swapped_ref[...].astype(F32), middle_ref[...].astype(F32)
-    out_ref[...] = (third_ref[...].astype(F32) + jnp.where(inner, swapped, 0.0)).astype(BF16)
-    sum_ref[...] = own_ref[...].astype(F32) + jnp.where(inner, middle, swapped)
-
-
-def total_kernel(sum_ref, across_ref, last_ref, in_ref, out_ref):
+def pass_kernel(middle_ref, inward_ref, third_ref, own_ref, out_ref, sum_ref):
+    out_ref[...] = (third_ref[...].astype(F32) + inward_ref[...].astype(F32)).astype(BF16)
+    sum_ref[...] = own_ref[...].astype(F32) + middle_ref[...].astype(F32)
+
+
+def total_kernel(sum_ref, cycle_ref, last_ref, in_ref, out_ref):
     piece_d, half = in_ref.shape[0], out_ref.shape[0] // 2
     width = out_ref.shape[1]
-    total = sum_ref[...] + across_ref[...].astype(F32) + last_ref[...].astype(F32)
+    total = sum_ref[...] + cycle_ref[...].astype(F32) + last_ref[...].astype(F32)
     in_ref[...] = total[:piece_d]
     out_ref[:half, :] = total[piece_d:, :width]
     out_ref[half:, :] = total[piece_d:, width:]
 
 
-def line_sums(place, first, second, third, own, width, returned):
+def line_sums(first, second, third, own, width, returned):
     rows, hidden = own.shape
     piece_d = width // LINE
     ahead = 3 * len(returned) // 8
     order = block_order(len(returned))
-    middle = lax.ppermute(second, "dp", [(0, 0), (1, 2), (2, 1), (3, 3)])
-    swapped = lax.ppermute(first, "dp", [(0, 1), (1, 0), (2, 3), (3, 2)])
+    inward = lax.ppermute(first, "dp", [(0, 1), (3, 2)])
+    middle = lax.ppermute(first, "dp", [(1, 2), (2, 1)])
+    cycle = lax.ppermute(second, "dp", [(0, 2), (1, 0), (2, 3), (3, 1)])
     back = swap_blocks(returned[:ahead], order[:ahead])
-    second, back[0] = lax.optimization_barrier((second, back[0]))
-    across = lax.ppermute(second, "dp", [(0, 2), (3, 1)])
     third, *back = lax.optimization_barrier((third, *back))
     passed, most = kernel_call(
         pass_kernel,
@@ -290,10 +286,10 @@
         1,
         1,
         [jax.ShapeDtypeStruct(own.shape, BF16), jax.ShapeDtypeStruct(own.shape, F32)],
-        [smem] + [vmem] * 4,
-    )(place, swapped, middle, third, own)
+        [vmem] * 4,
+    )(middle, inward, third, own)
     last = lax.ppermute(passed, "dp", [(0, 1), (3, 2), (1, 3), (2, 0)])
-    across, *rest = lax.optimization_barrier((across, *returned[ahead:]))
+    cycle, *rest = lax.optimization_barrier((cycle, *returned[ahead:]))
     back += swap_blocks(rest, order[ahead:])
     sums = kernel_call(
         total_kernel,
@@ -305,7 +301,7 @@
             jax.ShapeDtypeStruct((2 * (rows - piece_d), width), F32),
         ],
         [vmem] * 3,
-    )(most, across, last)
+    )(most, cycle, last)
     return *sums, back
 
 
@@ -403,7 +399,7 @@
     )(weight_in, soon_gpre, soon_extra, next_gpre, next_extra, late_gpre, late_extra)
 
     if groups == LINE:
-        grad_w_in, grad_w_out, back = line_sums(place, *parts, width, returned)
+        grad_w_in, grad_w_out, back = line_sums(*parts, width, returned)
     else:
         back = swap_blocks(returned, block_order(sources))
         parts_in, parts_out = zip(*[split_piece(part, width, LINE) for part in parts])

time: 72.5 us -> 72.7 us (level)
  starting transfers between devices: 31.9 us -> 36.6 us
  waiting for transfers between devices: 19.7 us -> 15.3 us
    ppermute x1, starting transfers between devices: 7.73 us -> 13.3 us  [line_sums(): last = lax.ppermute(passed, 'dp', [(0, 1), (3, 2), (1, 3), (2, 0)])]
    ppermute x14, waiting for transfers between devices: 19.1 us -> 14.6 us  [swap_blocks(): lax.ppermute(block, 'space', [(i, i ^ k) for i in devices])]
    ppermute x3, starting transfers between devices: 8.22 us -> 6.39 us  [the longest x1 3.66 us: line_sums(): inward = lax.ppermute(first, 'dp', [(0, 1), (3, 2)])]
    ppermute x14, starting transfers between devices: 16 us -> 16.9 us  [swap_blocks(): lax.ppermute(block, 'space', [(i, i ^ k) for i in devices])]
  transfers between devices with their start and end apart: 18 -> 18, of which waited for: 9 -> 8; matrix products, arithmetic and copies ran while one was open for 0% -> 0% of each run, Pallas kernels for 15% -> 15%
where the time goes in v12:
time: 72.7 us; the launch traced here: 72.5 us
  starting transfers between devices  36.6 us (50%)
  Pallas kernels  17.7 us (24%)
  waiting for transfers between devices  15.3 us (21%)
  local copies, waits for them, and re-layouts  2.07 us (3%)
  between operations  0.81 us (1%)
    ppermute x14, starting transfers between devices, swap_blocks(): lax.ppermute(block, 'space', [(i, i ^ k) for i in devices])  16.9 us
    ppermute x14, waiting for transfers between devices, swap_blocks(): lax.ppermute(block, 'space', [(i, i ^ k) for i in devices])  14.6 us
    ppermute x1, starting transfers between devices, line_sums(): last = lax.ppermute(passed, 'dp', [(0, 1), (3, 2), (1, 3), (2, 0)])  13.3 us
    pallas_call x3, Pallas kernels, work(): kernel_call(functools.partial(kernel, count, groups), name, 8 * span * wi...  7.32 us
    pallas_call x1, Pallas kernels, body(): kernel_call(functools.partial(place_kernel, sources, capacity), 'place',...  3.8 us
    ppermute x1, starting transfers between devices, line_sums(): inward = lax.ppermute(first, 'dp', [(0, 1), (3, 2)])  3.66 us
    pallas_call x1, Pallas kernels, body(): kernel_call(finish_kernel, 'finish', 1, 1, [shape((tok_rows, width), BF16...  2.6 us
    unnamed x20, local copies, waits for them, and re-layouts  2.07 us
  transfers between devices with their start and end apart: 18, of which 8 were waited for; matrix products, arithmetic and copies ran while one was open for 0% of the time, Pallas kernels for 15%

profile of v12, /device:TPU:0, one launch (start us, length us, event | category | flops | bytes accessed | tf_op | source)
XLA Modules:
  0.0 72.5 jit_solution(172184384809828782)
XLA Ops:
  0.7 3.8 %place.1 = (s32[1,576]{1,0:T(1,128)}, bf16[96,1024]{1,0:T(8,128)(2,1)}, bf16[96,1024]{1,0:T(8,128)(2,1)}, bf16[96,1024]{1,0:T(8,128)(2,1)}, bf16[96,1024]{1,0:T(8,128)(2,1)}) custom-call(s32[1]{0:T(128)} %bitcast.me, s32[1]{0:T(128)} %bitcast.1.place, s32[1,576]{1,0:T(1,128)} %bitcast.20, bf16[576]{0:T(1024)(128)(2,1)} %gate_ref.3, ...), custom_call_target="tpu_custom_call" | custom-call | flops 452984832 | bytes 2752512 | tf_op jit(solution)/shard_map/place/pallas_call | solution.py:327
  4.5 3.0 %collective-permute-start = (bf16[96,1024]{1,0:T(8,128)(2,1)}, bf16[96,1024]{1,0:T(8,128)(2,1)S(1)}, u32[]{:S(2)}, u32[]{:S(2)}) collective-permute-start(bf16[96,1024]{1,0:T(8,128)(2,1)} %get-tuple-element.52), channel_id=1, source_target_pairs={{0,16},{4,20},{8,24},{12,28},{16,0},{20,4},{24,8},{28,12},{1,17},{... | collective-permute-start | bytes 589832 | tf_op jit(solution)/shard_map/ppermute | solution.py:254
  7.5 1.5 %collective-permute-start.1 = (bf16[96,1024]{1,0:T(8,128)(2,1)}, bf16[96,1024]{1,0:T(8,128)(2,1)S(1)}, u32[]{:S(2)}, u32[]{:S(2)}) collective-permute-start(bf16[96,1024]{1,0:T(8,128)(2,1)} %get-tuple-element.53), channel_id=1, source_target_pairs={{0,8},{4,12},{8,0},{12,4},{16,24},{20,28},{24,16},{28,20},{1,9},{5... | collective-permute-start | bytes 589832 | tf_op jit(solution)/shard_map/ppermute | solution.py:254
  9.1 0.7 copy-done.4
  9.7 0.7 copy-done.6
  10.4 0.7 copy-done.8
  11.1 1.3 %rest.1 = (bf16[96,1024]{1,0:T(8,128)(2,1)S(1)}, bf16[96,1024]{1,0:T(8,128)(2,1)S(1)}, bf16[96,1024]{1,0:T(8,128)(2,1)S(1)}, bf16[96,1024]{1,0:T(8,128)(2,1)S(1)}) custom-call(s32[1,576]{1,0:T(1,128)S(1)} %copy-done.4, bf16[576]{0:T(1024)(128)(2,1)S(1)} %copy-done.6, bf16[576,512]{1,0:T(8,128)(2,1)S(1)} %copy-done.2, f32[1,512]{1,0:T(1,128)S(1)} %bitcast.16, ...), custom_call_target="tpu_custom_call" | custom-call | flops 1 | bytes 1 | tf_op jit(solution)/shard_map/rest/pallas_call | solution.py:348
  12.5 3.0 %collective-permute-start.4 = (bf16[96,1024]{1,0:T(8,128)(2,1)}, bf16[96,1024]{1,0:T(8,128)(2,1)S(1)}, u32[]{:S(2)}, u32[]{:S(2)}) collective-permute-start(bf16[96,1024]{1,0:T(8,128)(2,1)} %get-tuple-element.59), channel_id=1, source_target_pairs={{0,28},{4,24},{8,20},{12,16},{16,12},{20,8},{24,4},{28,0},{1,29},{... | collective-permute-start | bytes 589832 | tf_op jit(solution)/shard_map/ppermute | solution.py:254
  15.5 0.3 collective-permute-start.5
  15.9 3.4 %collective-permute-done.2.refs_2_ = bf16[96,1024]{1,0:T(8,128)(2,1)S(1)} collective-permute-done((bf16[96,1024]{1,0:T(8,128)(2,1)}, bf16[96,1024]{1,0:T(8,128)(2,1)S(1)}, u32[]{:S(2)}, u32[]{:S(2)}) %collective-permute-start.2) | collective-permute-done | bytes 196640 | tf_op jit(solution)/shard_map/ppermute | solution.py:254
  19.3 3.2 %sooner.1 = (f32[512,1024]{1,0:T(8,128)S(1)}, f32[1024,512]{1,0:T(8,128)S(1)}, bf16[480,1024]{1,0:T(8,128)(2,1)S(1)}, bf16[480,128]{1,0:T(8,128)(2,1)S(1)}) custom-call(s32[1]{0:T(128)} %bitcast.1.place, bf16[512,1024]{1,0:T(8,128)(2,1)S(1)} %bitcast.8, bf16[1024,512]{1,0:T(8,128)(2,1)S(1)} %bitcast.12, bf16[96,1024]{1,0:T(8,128)(2,1)S(1)} %collective-permute-done.refs_0_, ...), custom_call_target="tpu_custom_call" | custom-call | flops 2013265920 | bytes 6160384 | tf_op jit(solution)/shard_map/sooner/pallas_call | solution.py:377
  22.8 2.0 %next.1 = (f32[512,1024]{1,0:T(8,128)S(1)}, f32[1024,512]{1,0:T(8,128)S(1)}, bf16[96,1024]{1,0:T(8,128)(2,1)S(1)}, bf16[96,128]{1,0:T(8,128)(2,1)S(1)}) custom-call(s32[1]{0:T(128)} %bitcast.1.place, bf16[512,1024]{1,0:T(8,128)(2,1)S(1)} %bitcast.9, bf16[1024,512]{1,0:T(8,128)(2,1)S(1)} %bitcast.13, f32[512,1024]{1,0:T(8,128)S(1)} %get-tuple-element.57.old_in_ref, ...), custom_call_target="tpu_custom_call" | custom-call | flops 402653184 | bytes 4587520 | tf_op jit(solution)/shard_map/next/pallas_call | solution.py:377
  24.7 1.8 %collective-permute-done.5.refs_0_ = bf16[96,1024]{1,0:T(8,128)(2,1)S(1)} collective-permute-done((bf16[96,1024]{1,0:T(8,128)(2,1)S(1)}, bf16[96,1024]{1,0:T(8,128)(2,1)S(1)}, u32[]{:S(2)}, u32[]{:S(2)}) %collective-permute-start.5) | collective-permute-done | bytes 196640 | tf_op jit(solution)/shard_map/ppermute | solution.py:254
  26.5 2.1 %later.1 = (bf16[256,1024]{1,0:T(8,128)(2,1)S(1)}, bf16[256,1024]{1,0:T(8,128)(2,1)S(1)}, bf16[256,1024]{1,0:T(8,128)(2,1)S(1)}, bf16[256,1024]{1,0:T(8,128)(2,1...) custom-call(s32[1]{0:T(128)} %bitcast.1.place, bf16[512,1024]{1,0:T(8,128)(2,1)S(1)} %bitcast.10, ...), custom_call_target="tpu_custom_call" | custom-call | flops 805306368 | bytes 4980736 | tf_op jit(solution)/shard_map/later/pallas_call | solution.py:377
  28.6 3.7 %collective-permute-start.16 = (bf16[256,1024]{1,0:T(8,128)(2,1)S(1)}, bf16[256,1024]{1,0:T(8,128)(2,1)S(1)}, u32[]{:S(2)}, u32[]{:S(2)}) collective-permute-start(bf16[256,1024]{1,0:T(8,128)(2,1)S(1)} %get-tuple-element.90), channel_id=1, source_target_pairs={{0,1},{3,2},{4,5},{7,6},{8,9},{11,10},{12,13},{15,14},{16,17},{19,... | collective-permute-start | bytes 1572872 | tf_op jit(solution)/shard_map/ppermute | solution.py:278
  32.3 0.7 collective-permute-start.15
  33.0 1.3 %back.1 = (bf16[96,640]{1,0:T(8,128)(2,1)S(1)}, bf16[96,640]{1,0:T(8,128)(2,1)S(1)}, bf16[96,640]{1,0:T(8,128)(2,1)S(1)}, bf16[96,640]{1,0:T(8,128)(2,1)S(1)}, b...) custom-call(bf16[512,1024]{1,0:T(8,128)(2,1)S(1)} %bitcast.11, ...), custom_call_target="tpu_custom_call" | custom-call | flops 1 | bytes 1 | tf_op jit(solution)/shard_map/back/pallas_call | solution.py:392
  34.4 1.6 %collective-permute-start.7 = (bf16[96,640]{1,0:T(8,128)(2,1)S(1)}, bf16[96,640]{1,0:T(8,128)(2,1)S(1)}, u32[]{:S(2)}, u32[]{:S(2)}) collective-permute-start(bf16[96,640]{1,0:T(8,128)(2,1)S(1)} %get-tuple-element.71), channel_id=1, source_target_pairs={{0,16},{4,20},{8,24},{12,28},{16,0},{20,4},{24,8},{28,12},{1,17},{... | collective-permute-start | bytes 368648 | tf_op jit(solution)/shard_map/ppermute | solution.py:254
  36.0 2.0 %collective-permute-start.10 = (bf16[256,1024]{1,0:T(8,128)(2,1)S(1)}, bf16[256,1024]{1,0:T(8,128)(2,1)S(1)}, u32[]{:S(2)}, u32[]{:S(2)}) collective-permute-start(bf16[256,1024]{1,0:T(8,128)(2,1)S(1)} %get-tuple-element.77), channel_id=1, source_target_pairs={{0,2},{1,0},{2,3},{3,1},{4,6},{5,4},{6,7},{7,5},{8,10},{9,8},{10,1... | collective-permute-start | bytes 1572872 | tf_op jit(solution)/shard_map/ppermute | solution.py:280
  38.0 1.5 %collective-permute-start.8 = (bf16[96,640]{1,0:T(8,128)(2,1)S(1)}, bf16[96,640]{1,0:T(8,128)(2,1)S(1)}, u32[]{:S(2)}, u32[]{:S(2)}) collective-permute-start(bf16[96,640]{1,0:T(8,128)(2,1)S(1)} %get-tuple-element.72), channel_id=1, source_target_pairs={{0,8},{4,12},{8,0},{12,4},{16,24},{20,28},{24,16},{28,20},{1,9},{5... | collective-permute-start | bytes 368648 | tf_op jit(solution)/shard_map/ppermute | solution.py:254
  39.5 2.5 %collective-permute-start.9 = (bf16[96,640]{1,0:T(8,128)(2,1)S(1)}, bf16[96,640]{1,0:T(8,128)(2,1)S(1)}, u32[]{:S(2)}, u32[]{:S(2)}) collective-permute-start(bf16[96,640]{1,0:T(8,128)(2,1)S(1)} %get-tuple-element.73), channel_id=1, source_target_pairs={{0,24},{4,28},{8,16},{12,20},{16,8},{20,12},{24,0},{28,4},{1,25},{... | collective-permute-start | bytes 368648 | tf_op jit(solution)/shard_map/ppermute | solution.py:254
  41.9 1.9 %collective-permute-done.8.refs_1_ = bf16[96,640]{1,0:T(8,128)(2,1)S(1)} collective-permute-done((bf16[96,640]{1,0:T(8,128)(2,1)S(1)}, bf16[96,640]{1,0:T(8,128)(2,1)S(1)}, u32[]{:S(2)}, u32[]{:S(2)}) %collective-permute-start.8) | collective-permute-done | bytes 122912 | tf_op jit(solution)/shard_map/ppermute | solution.py:254
  43.8 1.6 %collective-permute-done.9.refs_2_ = bf16[96,640]{1,0:T(8,128)(2,1)S(1)} collective-permute-done((bf16[96,640]{1,0:T(8,128)(2,1)S(1)}, bf16[96,640]{1,0:T(8,128)(2,1)S(1)}, u32[]{:S(2)}, u32[]{:S(2)}) %collective-permute-start.9) | collective-permute-done | bytes 122912 | tf_op jit(solution)/shard_map/ppermute | solution.py:254
  45.5 0.2 pass.1
  45.7 13.3 %collective-permute-start.17 = (bf16[256,1024]{1,0:T(8,128)(2,1)S(1)}, bf16[256,1024]{1,0:T(8,128)(2,1)S(1)}, u32[]{:S(2)}, u32[]{:S(2)}) collective-permute-start(bf16[256,1024]{1,0:T(8,128)(2,1)S(1)} %get-tuple-element.95), channel_id=1, source_target_pairs={{0,1},{3,2},{1,3},{2,0},{4,5},{7,6},{5,7},{6,4},{8,9},{11,10},{9,1... | collective-permute-start | bytes 1572872 | tf_op jit(solution)/shard_map/ppermute | solution.py:291
  59.0 2.7 %collective-permute-start.12 = (bf16[96,640]{1,0:T(8,128)(2,1)S(1)}, bf16[96,640]{1,0:T(8,128)(2,1)S(1)}, u32[]{:S(2)}, u32[]{:S(2)}) collective-permute-start(bf16[96,640]{1,0:T(8,128)(2,1)S(1)} %get-tuple-element.84), channel_id=1, source_target_pairs={{0,20},{4,16},{8,28},{12,24},{16,4},{20,0},{24,12},{28,8},{1,21},{... | collective-permute-start | bytes 368648 | tf_op jit(solution)/shard_map/ppermute | solution.py:254
  61.7 0.6 collective-permute-start.14
  62.3 3.2 %collective-permute-done.11.refs_3_ = bf16[96,640]{1,0:T(8,128)(2,1)S(1)} collective-permute-done((bf16[96,640]{1,0:T(8,128)(2,1)S(1)}, bf16[96,640]{1,0:T(8,128)(2,1)S(1)}, u32[]{:S(2)}, u32[]{:S(2)}) %collective-permute-start.11) | collective-permute-done | bytes 122912 | tf_op jit(solution)/shard_map/ppermute | solution.py:254
  65.5 2.5 %collective-permute-done.12.refs_4_ = bf16[96,640]{1,0:T(8,128)(2,1)S(1)} collective-permute-done((bf16[96,640]{1,0:T(8,128)(2,1)S(1)}, bf16[96,640]{1,0:T(8,128)(2,1)S(1)}, u32[]{:S(2)}, u32[]{:S(2)}) %collective-permute-start.12) | collective-permute-done | bytes 122912 | tf_op jit(solution)/shard_map/ppermute | solution.py:254
  68.1 2.6 %finish.1 = (bf16[576,512]{1,0:T(8,128)(2,1)}, bf16[576]{0:T(1024)(128)(2,1)}) custom-call(s32[1,576]{1,0:T(1,128)S(1)} %copy-done.5, bf16[576]{0:T(1024)(128)(2,1)S(1)} %copy-done.7, bf16[576,512]{1,0:T(8,128)(2,1)S(1)} %copy-done.2, f32[1,512]{1,0:T(1,128)S(1)} %bitcast.17, bf16[576,512]{1,0:T(8,128)(2,1)S(1)} %copy-done.3, ...), custom_call_target="tpu_custom_call" | custom-call | flops 1 | bytes 1 | tf_op jit(solution)/shard_map/finish/pallas_call | solution.py:412
  70.7 0.7 collective-permute-done.17.last_ref
  71.4 1.1 %total.1 = (f32[128,1024]{1,0:T(8,128)}, f32[256,512]{1,0:T(8,128)}) custom-call(f32[256,1024]{1,0:T(8,128)S(1)} %get-tuple-element.93.sum_ref, bf16[256,1024]{1,0:T(8,128)(2,1)S(1)} %collective-permute-done.10.cycle_ref, bf16[256,1024]{1,0:T(8,128)(2,1)S(1)} %collective-permute-done.17.last_ref), custom_call_target="tpu_custom_call" | custom-call | flops 1 | bytes 1 | tf_op jit(solution)/shard_map/total/pallas_call | solution.py:294
  (34 shorter events, 0.6 us)
Async XLA Ops:
  0.6 8.4 %copy-start.3 = (bf16[576,512]{1,0:T(8,128)(2,1)S(1)}, bf16[576,512]{1,0:T(8,128)(2,1)}, u32[]{:S(2)}) copy-start(bf16[576,512]{1,0:T(8,128)(2,1)} %go_ref.3) | copy-start | bytes 1769476
  0.6 8.4 %copy-start.2 = (bf16[576,512]{1,0:T(8,128)(2,1)S(1)}, bf16[576,512]{1,0:T(8,128)(2,1)}, u32[]{:S(2)}) copy-start(bf16[576,512]{1,0:T(8,128)(2,1)} %tok_ref.3) | copy-start | bytes 1769476
  0.7 18.7 %copy-start.1 = (bf16[1,1024,512]{2,1,0:T(8,128)(2,1)S(1)}, bf16[1,1024,512]{2,1,0:T(8,128)(2,1)}, u32[]{:S(2)}) copy-start(bf16[1,1024,512]{2,1,0:T(8,128)(2,1)} %param.10) | copy-start | bytes 3145732
  0.7 18.7 %copy-start = (bf16[1,512,1024]{2,1,0:T(8,128)(2,1)S(1)}, bf16[1,512,1024]{2,1,0:T(8,128)(2,1)}, u32[]{:S(2)}) copy-start(bf16[1,512,1024]{2,1,0:T(8,128)(2,1)} %param.9) | copy-start | bytes 3145732
  4.5 11.0 %collective-permute-start = (bf16[96,1024]{1,0:T(8,128)(2,1)}, bf16[96,1024]{1,0:T(8,128)(2,1)S(1)}, u32[]{:S(2)}, u32[]{:S(2)}) collective-permute-start(bf16[96,1024]{1,0:T(8,128)(2,1)} %get-tuple-element.52), channel_id=1, source_target_pairs={{0,16},{4,20},{8,24},{12,28},{16,0},{20,4},{24,8},{28,12},{1,17},{... | collective-permute-start | bytes 589832 | tf_op jit(solution)/shard_map/ppermute | solution.py:254
  7.5 8.3 %collective-permute-start.1 = (bf16[96,1024]{1,0:T(8,128)(2,1)}, bf16[96,1024]{1,0:T(8,128)(2,1)S(1)}, u32[]{:S(2)}, u32[]{:S(2)}) collective-permute-start(bf16[96,1024]{1,0:T(8,128)(2,1)} %get-tuple-element.53), channel_id=1, source_target_pairs={{0,8},{4,12},{8,0},{12,4},{16,24},{20,28},{24,16},{28,20},{1,9},{5... | collective-permute-start | bytes 589832 | tf_op jit(solution)/shard_map/ppermute | solution.py:254
  9.0 10.3 %collective-permute-start.2 = (bf16[96,1024]{1,0:T(8,128)(2,1)}, bf16[96,1024]{1,0:T(8,128)(2,1)S(1)}, u32[]{:S(2)}, u32[]{:S(2)}) collective-permute-start(bf16[96,1024]{1,0:T(8,128)(2,1)} %get-tuple-element.54), channel_id=1, source_target_pairs={{0,24},{4,28},{8,16},{12,20},{16,8},{20,12},{24,0},{28,4},{1,25},{... | collective-permute-start | bytes 589832 | tf_op jit(solution)/shard_map/ppermute | solution.py:254
  9.1 0.7 copy-start.4
  9.7 0.7 copy-start.6
  10.4 0.7 copy-start.8
  12.4 6.9 %collective-permute-start.3 = (bf16[96,1024]{1,0:T(8,128)(2,1)S(1)}, bf16[96,1024]{1,0:T(8,128)(2,1)S(1)}, u32[]{:S(2)}, u32[]{:S(2)}) collective-permute-start(bf16[96,1024]{1,0:T(8,128)(2,1)S(1)} %get-tuple-element.55), channel_id=1, source_target_pairs={{0,4},{4,0},{8,12},{12,8},{16,20},{20,16},{24,28},{28,24},{1,5},{5... | collective-permute-start | bytes 589832 | tf_op jit(solution)/shard_map/ppermute | solution.py:254
  12.5 10.3 %collective-permute-start.4 = (bf16[96,1024]{1,0:T(8,128)(2,1)}, bf16[96,1024]{1,0:T(8,128)(2,1)S(1)}, u32[]{:S(2)}, u32[]{:S(2)}) collective-permute-start(bf16[96,1024]{1,0:T(8,128)(2,1)} %get-tuple-element.59), channel_id=1, source_target_pairs={{0,28},{4,24},{8,20},{12,16},{16,12},{20,8},{24,4},{28,0},{1,29},{... | collective-permute-start | bytes 589832 | tf_op jit(solution)/shard_map/ppermute | solution.py:254
  15.5 11.0 %collective-permute-start.5 = (bf16[96,1024]{1,0:T(8,128)(2,1)S(1)}, bf16[96,1024]{1,0:T(8,128)(2,1)S(1)}, u32[]{:S(2)}, u32[]{:S(2)}) collective-permute-start(bf16[96,1024]{1,0:T(8,128)(2,1)S(1)} %get-tuple-element.62), channel_id=1, source_target_pairs={{0,20},{4,16},{8,28},{12,24},{16,4},{20,0},{24,12},{28,8},{1,21},{... | collective-permute-start | bytes 589832 | tf_op jit(solution)/shard_map/ppermute | solution.py:254
  15.8 10.7 %collective-permute-start.6 = (bf16[96,1024]{1,0:T(8,128)(2,1)S(1)}, bf16[96,1024]{1,0:T(8,128)(2,1)S(1)}, u32[]{:S(2)}, u32[]{:S(2)}) collective-permute-start(bf16[96,1024]{1,0:T(8,128)(2,1)S(1)} %get-tuple-element.63), channel_id=1, source_target_pairs={{0,12},{4,8},{8,4},{12,0},{16,28},{20,24},{24,20},{28,16},{1,13},{... | collective-permute-start | bytes 589832 | tf_op jit(solution)/shard_map/ppermute | solution.py:254
  28.6 16.8 %collective-permute-start.16 = (bf16[256,1024]{1,0:T(8,128)(2,1)S(1)}, bf16[256,1024]{1,0:T(8,128)(2,1)S(1)}, u32[]{:S(2)}, u32[]{:S(2)}) collective-permute-start(bf16[256,1024]{1,0:T(8,128)(2,1)S(1)} %get-tuple-element.90), channel_id=1, source_target_pairs={{0,1},{3,2},{4,5},{7,6},{8,9},{11,10},{12,13},{15,14},{16,17},{19,... | collective-permute-start | bytes 1572872 | tf_op jit(solution)/shard_map/ppermute | solution.py:278
  32.3 13.2 %collective-permute-start.15 = (bf16[256,1024]{1,0:T(8,128)(2,1)S(1)}, bf16[256,1024]{1,0:T(8,128)(2,1)S(1)}, u32[]{:S(2)}, u32[]{:S(2)}) collective-permute-start(bf16[256,1024]{1,0:T(8,128)(2,1)S(1)} %get-tuple-element.90), channel_id=1, source_target_pairs={{1,2},{2,1},{5,6},{6,5},{9,10},{10,9},{13,14},{14,13},{17,18},{18,... | collective-permute-start | bytes 1572872 | tf_op jit(solution)/shard_map/ppermute | solution.py:279
  33.0 35.1 %copy-start.5 = (s32[1,576]{1,0:T(1,128)S(1)}, s32[1,576]{1,0:T(1,128)}, u32[]{:S(2)}) copy-start(s32[1,576]{1,0:T(1,128)} %get-tuple-element.51.target_ref) | copy-start | bytes 6916
  33.0 35.1 %copy-start.7 = (bf16[576]{0:T(1024)(128)(2,1)S(1)}, bf16[576]{0:T(1024)(128)(2,1)}, u32[]{:S(2)}) copy-start(bf16[576]{0:T(1024)(128)(2,1)} %gate_ref.3) | copy-start | bytes 3460
  33.0 35.1 %copy-start.9 = (f32[512]{0:T(512)S(1)}, f32[512]{0:T(512)}, u32[]{:S(2)}) copy-start(f32[512]{0:T(512)} %param.8) | copy-start | bytes 6148
  34.4 5.1 %collective-permute-start.7 = (bf16[96,640]{1,0:T(8,128)(2,1)S(1)}, bf16[96,640]{1,0:T(8,128)(2,1)S(1)}, u32[]{:S(2)}, u32[]{:S(2)}) collective-permute-start(bf16[96,640]{1,0:T(8,128)(2,1)S(1)} %get-tuple-element.71), channel_id=1, source_target_pairs={{0,16},{4,20},{8,24},{12,28},{16,0},{20,4},{24,8},{28,12},{1,17},{... | collective-permute-start | bytes 368648 | tf_op jit(solution)/shard_map/ppermute | solution.py:254
  36.0 23.0 %collective-permute-start.10 = (bf16[256,1024]{1,0:T(8,128)(2,1)S(1)}, bf16[256,1024]{1,0:T(8,128)(2,1)S(1)}, u32[]{:S(2)}, u32[]{:S(2)}) collective-permute-start(bf16[256,1024]{1,0:T(8,128)(2,1)S(1)} %get-tuple-element.77), channel_id=1, source_target_pairs={{0,2},{1,0},{2,3},{3,1},{4,6},{5,4},{6,7},{7,5},{8,10},{9,8},{10,1... | collective-permute-start | bytes 1572872 | tf_op jit(solution)/shard_map/ppermute | solution.py:280
  38.0 5.8 %collective-permute-start.8 = (bf16[96,640]{1,0:T(8,128)(2,1)S(1)}, bf16[96,640]{1,0:T(8,128)(2,1)S(1)}, u32[]{:S(2)}, u32[]{:S(2)}) collective-permute-start(bf16[96,640]{1,0:T(8,128)(2,1)S(1)} %get-tuple-element.72), channel_id=1, source_target_pairs={{0,8},{4,12},{8,0},{12,4},{16,24},{20,28},{24,16},{28,20},{1,9},{5... | collective-permute-start | bytes 368648 | tf_op jit(solution)/shard_map/ppermute | solution.py:254
  39.5 5.9 %collective-permute-start.9 = (bf16[96,640]{1,0:T(8,128)(2,1)S(1)}, bf16[96,640]{1,0:T(8,128)(2,1)S(1)}, u32[]{:S(2)}, u32[]{:S(2)}) collective-permute-start(bf16[96,640]{1,0:T(8,128)(2,1)S(1)} %get-tuple-element.73), channel_id=1, source_target_pairs={{0,24},{4,28},{8,16},{12,20},{16,8},{20,12},{24,0},{28,4},{1,25},{... | collective-permute-start | bytes 368648 | tf_op jit(solution)/shard_map/ppermute | solution.py:254
  45.7 25.7 %collective-permute-start.17 = (bf16[256,1024]{1,0:T(8,128)(2,1)S(1)}, bf16[256,1024]{1,0:T(8,128)(2,1)S(1)}, u32[]{:S(2)}, u32[]{:S(2)}) collective-permute-start(bf16[256,1024]{1,0:T(8,128)(2,1)S(1)} %get-tuple-element.95), channel_id=1, source_target_pairs={{0,1},{3,2},{1,3},{2,0},{4,5},{7,6},{5,7},{6,4},{8,9},{11,10},{9,1... | collective-permute-start | bytes 1572872 | tf_op jit(solution)/shard_map/ppermute | solution.py:291
  59.0 6.5 %collective-permute-start.11 = (bf16[96,640]{1,0:T(8,128)(2,1)S(1)}, bf16[96,640]{1,0:T(8,128)(2,1)S(1)}, u32[]{:S(2)}, u32[]{:S(2)}) collective-permute-start(bf16[96,640]{1,0:T(8,128)(2,1)S(1)} %get-tuple-element.83), channel_id=1, source_target_pairs={{0,28},{4,24},{8,20},{12,16},{16,12},{20,8},{24,4},{28,0},{1,29},{... | collective-permute-start | bytes 368648 | tf_op jit(solution)/shard_map/ppermute | solution.py:254
  59.0 9.0 %collective-permute-start.12 = (bf16[96,640]{1,0:T(8,128)(2,1)S(1)}, bf16[96,640]{1,0:T(8,128)(2,1)S(1)}, u32[]{:S(2)}, u32[]{:S(2)}) collective-permute-start(bf16[96,640]{1,0:T(8,128)(2,1)S(1)} %get-tuple-element.84), channel_id=1, source_target_pairs={{0,20},{4,16},{8,28},{12,24},{16,4},{20,0},{24,12},{28,8},{1,21},{... | collective-permute-start | bytes 368648 | tf_op jit(solution)/shard_map/ppermute | solution.py:254
  61.7 6.4 %collective-permute-start.13 = (bf16[96,640]{1,0:T(8,128)(2,1)S(1)}, bf16[96,640]{1,0:T(8,128)(2,1)S(1)}, u32[]{:S(2)}, u32[]{:S(2)}) collective-permute-start(bf16[96,640]{1,0:T(8,128)(2,1)S(1)} %get-tuple-element.85), channel_id=1, source_target_pairs={{0,12},{4,8},{8,4},{12,0},{16,28},{20,24},{24,20},{28,16},{1,13},{... | collective-permute-start | bytes 368648 | tf_op jit(solution)/shard_map/ppermute | solution.py:254
  61.7 6.3 %collective-permute-start.14 = (bf16[96,640]{1,0:T(8,128)(2,1)S(1)}, bf16[96,640]{1,0:T(8,128)(2,1)S(1)}, u32[]{:S(2)}, u32[]{:S(2)}) collective-permute-start(bf16[96,640]{1,0:T(8,128)(2,1)S(1)} %get-tuple-element.86), channel_id=1, source_target_pairs={{0,4},{4,0},{8,12},{12,8},{16,20},{20,16},{24,28},{28,24},{1,5},{5... | collective-permute-start | bytes 368648 | tf_op jit(solution)/shard_map/ppermute | solution.py:254

commit v13 on v12

--- a/solution.py
+++ b/solution.py
@@ -273,12 +273,13 @@
 def line_sums(first, second, third, own, width, returned):
     rows, hidden = own.shape
     piece_d = width // LINE
-    ahead = 3 * len(returned) // 8
+    ahead = len(returned) // 4
     order = block_order(len(returned))
     inward = lax.ppermute(first, "dp", [(0, 1), (3, 2)])
     middle = lax.ppermute(first, "dp", [(1, 2), (2, 1)])
+    back = swap_blocks(returned[:ahead], order[:ahead])
+    second, back[0] = lax.optimization_barrier((second, back[0]))
     cycle = lax.ppermute(second, "dp", [(0, 2), (1, 0), (2, 3), (3, 1)])
-    back = swap_blocks(returned[:ahead], order[:ahead])
     third, *back = lax.optimization_barrier((third, *back))
     passed, most = kernel_call(
         pass_kernel,
@@ -288,8 +289,8 @@
         [jax.ShapeDtypeStruct(own.shape, BF16), jax.ShapeDtypeStruct(own.shape, F32)],
         [vmem] * 4,
     )(middle, inward, third, own)
+    passed, *rest = lax.optimization_barrier((passed, *returned[ahead:]))
     last = lax.ppermute(passed, "dp", [(0, 1), (3, 2), (1, 3), (2, 0)])
-    cycle, *rest = lax.optimization_barrier((cycle, *returned[ahead:]))
     back += swap_blocks(rest, order[ahead:])
     sums = kernel_call(
         total_kernel,

time: 72.7 us -> 74.4 us (1.023)
  waiting for transfers between devices: 15.3 us -> 17.7 us
    ppermute x1, waiting for transfers between devices: 0.01 us -> 1.65 us  [line_sums(): inward = lax.ppermute(first, 'dp', [(0, 1), (3, 2)])]
    ppermute x14, starting transfers between devices: 16.9 us -> 15.3 us  [swap_blocks(): lax.ppermute(block, 'space', [(i, i ^ k) for i in devices])]
    ppermute x14, waiting for transfers between devices: 14.6 us -> 16.1 us  [swap_blocks(): lax.ppermute(block, 'space', [(i, i ^ k) for i in devices])]
    ppermute x1, starting transfers between devices: 13.3 us -> 14.2 us  [line_sums(): last = lax.ppermute(passed, 'dp', [(0, 1), (3, 2), (1, 3), (2, 0)])]
  transfers between devices with their start and end apart: 18 -> 18, of which waited for: 8 -> 10; matrix products, arithmetic and copies ran while one was open for 0% -> 0% of each run, Pallas kernels for 15% -> 14%
where the time goes in v13:
time: 74.4 us; the launch traced here: 74.2 us
  starting transfers between devices  35.9 us (48%)
  Pallas kernels  17.7 us (24%)
  waiting for transfers between devices  17.7 us (24%)
  local copies, waits for them, and re-layouts  2.07 us (3%)
  between operations  0.81 us (1%)
    ppermute x14, waiting for transfers between devices, swap_blocks(): lax.ppermute(block, 'space', [(i, i ^ k) for i in devices])  16.1 us
    ppermute x14, starting transfers between devices, swap_blocks(): lax.ppermute(block, 'space', [(i, i ^ k) for i in devices])  15.3 us
    ppermute x1, starting transfers between devices, line_sums(): last = lax.ppermute(passed, 'dp', [(0, 1), (3, 2), (1, 3), (2, 0)])  14.2 us
    pallas_call x3, Pallas kernels, work(): kernel_call(functools.partial(kernel, count, groups), name, 8 * span * wi...  7.32 us
    pallas_call x1, Pallas kernels, body(): kernel_call(functools.partial(place_kernel, sources, capacity), 'place',...  3.8 us
    ppermute x1, starting transfers between devices, line_sums(): inward = lax.ppermute(first, 'dp', [(0, 1), (3, 2)])  3.66 us
    pallas_call x1, Pallas kernels, body(): kernel_call(finish_kernel, 'finish', 1, 1, [shape((tok_rows, width), BF16...  2.6 us
    unnamed x20, local copies, waits for them, and re-layouts  2.07 us
  transfers between devices with their start and end apart: 18, of which 10 were waited for; matrix products, arithmetic and copies ran while one was open for 0% of the time, Pallas kernels for 14%

profile of v13, /device:TPU:0, one launch (start us, length us, event | category | flops | bytes accessed | tf_op | source)
XLA Modules:
  0.0 74.2 jit_solution(12979417586092686631)
XLA Ops:
  0.7 3.8 %place.1 = (s32[1,576]{1,0:T(1,128)}, bf16[96,1024]{1,0:T(8,128)(2,1)}, bf16[96,1024]{1,0:T(8,128)(2,1)}, bf16[96,1024]{1,0:T(8,128)(2,1)}, bf16[96,1024]{1,0:T(8,128)(2,1)}) custom-call(s32[1]{0:T(128)} %bitcast.me, s32[1]{0:T(128)} %bitcast.1.place, s32[1,576]{1,0:T(1,128)} %bitcast.20, bf16[576]{0:T(1024)(128)(2,1)} %gate_ref.3, ...), custom_call_target="tpu_custom_call" | custom-call | flops 452984832 | bytes 2752512 | tf_op jit(solution)/shard_map/place/pallas_call | solution.py:328
  4.5 3.0 %collective-permute-start = (bf16[96,1024]{1,0:T(8,128)(2,1)}, bf16[96,1024]{1,0:T(8,128)(2,1)S(1)}, u32[]{:S(2)}, u32[]{:S(2)}) collective-permute-start(bf16[96,1024]{1,0:T(8,128)(2,1)} %get-tuple-element.54), channel_id=1, source_target_pairs={{0,16},{4,20},{8,24},{12,28},{16,0},{20,4},{24,8},{28,12},{1,17},{... | collective-permute-start | bytes 589832 | tf_op jit(solution)/shard_map/ppermute | solution.py:254
  7.5 1.5 %collective-permute-start.1 = (bf16[96,1024]{1,0:T(8,128)(2,1)}, bf16[96,1024]{1,0:T(8,128)(2,1)S(1)}, u32[]{:S(2)}, u32[]{:S(2)}) collective-permute-start(bf16[96,1024]{1,0:T(8,128)(2,1)} %get-tuple-element.55), channel_id=1, source_target_pairs={{0,8},{4,12},{8,0},{12,4},{16,24},{20,28},{24,16},{28,20},{1,9},{5... | collective-permute-start | bytes 589832 | tf_op jit(solution)/shard_map/ppermute | solution.py:254
  9.1 0.7 copy-done.4
  9.7 0.7 copy-done.6
  10.4 0.7 copy-done.8
  11.1 1.3 %rest.1 = (bf16[96,1024]{1,0:T(8,128)(2,1)S(1)}, bf16[96,1024]{1,0:T(8,128)(2,1)S(1)}, bf16[96,1024]{1,0:T(8,128)(2,1)S(1)}, bf16[96,1024]{1,0:T(8,128)(2,1)S(1)}) custom-call(s32[1,576]{1,0:T(1,128)S(1)} %copy-done.4, bf16[576]{0:T(1024)(128)(2,1)S(1)} %copy-done.6, bf16[576,512]{1,0:T(8,128)(2,1)S(1)} %copy-done.2, f32[1,512]{1,0:T(1,128)S(1)} %bitcast.16, ...), custom_call_target="tpu_custom_call" | custom-call | flops 1 | bytes 1 | tf_op jit(solution)/shard_map/rest/pallas_call | solution.py:349
  12.5 3.0 %collective-permute-start.4 = (bf16[96,1024]{1,0:T(8,128)(2,1)}, bf16[96,1024]{1,0:T(8,128)(2,1)S(1)}, u32[]{:S(2)}, u32[]{:S(2)}) collective-permute-start(bf16[96,1024]{1,0:T(8,128)(2,1)} %get-tuple-element.61), channel_id=1, source_target_pairs={{0,28},{4,24},{8,20},{12,16},{16,12},{20,8},{24,4},{28,0},{1,29},{... | collective-permute-start | bytes 589832 | tf_op jit(solution)/shard_map/ppermute | solution.py:254
  15.5 0.3 collective-permute-start.5
  15.9 3.4 %collective-permute-done.2.refs_2_ = bf16[96,1024]{1,0:T(8,128)(2,1)S(1)} collective-permute-done((bf16[96,1024]{1,0:T(8,128)(2,1)}, bf16[96,1024]{1,0:T(8,128)(2,1)S(1)}, u32[]{:S(2)}, u32[]{:S(2)}) %collective-permute-start.2) | collective-permute-done | bytes 196640 | tf_op jit(solution)/shard_map/ppermute | solution.py:254
  19.3 3.2 %sooner.1 = (f32[512,1024]{1,0:T(8,128)S(1)}, f32[1024,512]{1,0:T(8,128)S(1)}, bf16[480,1024]{1,0:T(8,128)(2,1)S(1)}, bf16[480,128]{1,0:T(8,128)(2,1)S(1)}) custom-call(s32[1]{0:T(128)} %bitcast.1.place, bf16[512,1024]{1,0:T(8,128)(2,1)S(1)} %bitcast.8, bf16[1024,512]{1,0:T(8,128)(2,1)S(1)} %bitcast.12, bf16[96,1024]{1,0:T(8,128)(2,1)S(1)} %collective-permute-done.refs_0_, ...), custom_call_target="tpu_custom_call" | custom-call | flops 2013265920 | bytes 6160384 | tf_op jit(solution)/shard_map/sooner/pallas_call | solution.py:378
  22.8 2.0 %next.1 = (f32[512,1024]{1,0:T(8,128)S(1)}, f32[1024,512]{1,0:T(8,128)S(1)}, bf16[96,1024]{1,0:T(8,128)(2,1)S(1)}, bf16[96,128]{1,0:T(8,128)(2,1)S(1)}) custom-call(s32[1]{0:T(128)} %bitcast.1.place, bf16[512,1024]{1,0:T(8,128)(2,1)S(1)} %bitcast.9, bf16[1024,512]{1,0:T(8,128)(2,1)S(1)} %bitcast.13, f32[512,1024]{1,0:T(8,128)S(1)} %get-tuple-element.59.old_in_ref, ...), custom_call_target="tpu_custom_call" | custom-call | flops 402653184 | bytes 4587520 | tf_op jit(solution)/shard_map/next/pallas_call | solution.py:378
  24.7 1.8 %collective-permute-done.5.refs_0_ = bf16[96,1024]{1,0:T(8,128)(2,1)S(1)} collective-permute-done((bf16[96,1024]{1,0:T(8,128)(2,1)S(1)}, bf16[96,1024]{1,0:T(8,128)(2,1)S(1)}, u32[]{:S(2)}, u32[]{:S(2)}) %collective-permute-start.5) | collective-permute-done | bytes 196640 | tf_op jit(solution)/shard_map/ppermute | solution.py:254
  26.5 2.1 %later.1 = (bf16[256,1024]{1,0:T(8,128)(2,1)S(1)}, bf16[256,1024]{1,0:T(8,128)(2,1)S(1)}, bf16[256,1024]{1,0:T(8,128)(2,1)S(1)}, bf16[256,1024]{1,0:T(8,128)(2,1...) custom-call(s32[1]{0:T(128)} %bitcast.1.place, bf16[512,1024]{1,0:T(8,128)(2,1)S(1)} %bitcast.10, ...), custom_call_target="tpu_custom_call" | custom-call | flops 805306368 | bytes 4980736 | tf_op jit(solution)/shard_map/later/pallas_call | solution.py:378
  28.6 3.7 %collective-permute-start.10 = (bf16[256,1024]{1,0:T(8,128)(2,1)S(1)}, bf16[256,1024]{1,0:T(8,128)(2,1)S(1)}, u32[]{:S(2)}, u32[]{:S(2)}) collective-permute-start(bf16[256,1024]{1,0:T(8,128)(2,1)S(1)} %get-tuple-element.79), channel_id=1, source_target_pairs={{0,1},{3,2},{4,5},{7,6},{8,9},{11,10},{12,13},{15,14},{16,17},{19,... | collective-permute-start | bytes 1572872 | tf_op jit(solution)/shard_map/ppermute | solution.py:278
  32.3 0.7 collective-permute-start.9
  33.0 1.3 %back.1 = (bf16[96,640]{1,0:T(8,128)(2,1)S(1)}, bf16[96,640]{1,0:T(8,128)(2,1)S(1)}, bf16[96,640]{1,0:T(8,128)(2,1)S(1)}, bf16[96,640]{1,0:T(8,128)(2,1)S(1)}, b...) custom-call(bf16[512,1024]{1,0:T(8,128)(2,1)S(1)} %bitcast.11, ...), custom_call_target="tpu_custom_call" | custom-call | flops 1 | bytes 1 | tf_op jit(solution)/shard_map/back/pallas_call | solution.py:393
  34.4 1.6 %collective-permute-start.7 = (bf16[96,640]{1,0:T(8,128)(2,1)S(1)}, bf16[96,640]{1,0:T(8,128)(2,1)S(1)}, u32[]{:S(2)}, u32[]{:S(2)}) collective-permute-start(bf16[96,640]{1,0:T(8,128)(2,1)S(1)} %get-tuple-element.74), channel_id=1, source_target_pairs={{0,16},{4,20},{8,24},{12,28},{16,0},{20,4},{24,8},{28,12},{1,17},{... | collective-permute-start | bytes 368648 | tf_op jit(solution)/shard_map/ppermute | solution.py:254
  36.0 1.5 %collective-permute-start.8 = (bf16[96,640]{1,0:T(8,128)(2,1)S(1)}, bf16[96,640]{1,0:T(8,128)(2,1)S(1)}, u32[]{:S(2)}, u32[]{:S(2)}) collective-permute-start(bf16[96,640]{1,0:T(8,128)(2,1)S(1)} %get-tuple-element.76), channel_id=1, source_target_pairs={{0,8},{4,12},{8,0},{12,4},{16,24},{20,28},{24,16},{28,20},{1,9},{5... | collective-permute-start | bytes 368648 | tf_op jit(solution)/shard_map/ppermute | solution.py:254
  37.5 2.0 %collective-permute-done.7.refs_0_ = bf16[96,640]{1,0:T(8,128)(2,1)S(1)} collective-permute-done((bf16[96,640]{1,0:T(8,128)(2,1)S(1)}, bf16[96,640]{1,0:T(8,128)(2,1)S(1)}, u32[]{:S(2)}, u32[]{:S(2)}) %collective-permute-start.7) | collective-permute-done | bytes 122912 | tf_op jit(solution)/shard_map/ppermute | solution.py:254
  39.5 1.3 %collective-permute-done.8.refs_1_ = bf16[96,640]{1,0:T(8,128)(2,1)S(1)} collective-permute-done((bf16[96,640]{1,0:T(8,128)(2,1)S(1)}, bf16[96,640]{1,0:T(8,128)(2,1)S(1)}, u32[]{:S(2)}, u32[]{:S(2)}) %collective-permute-start.8) | collective-permute-done | bytes 122912 | tf_op jit(solution)/shard_map/ppermute | solution.py:254
  40.8 2.0 %collective-permute-start.16 = (bf16[256,1024]{1,0:T(8,128)(2,1)S(1)}, bf16[256,1024]{1,0:T(8,128)(2,1)S(1)}, u32[]{:S(2)}, u32[]{:S(2)}) collective-permute-start(bf16[256,1024]{1,0:T(8,128)(2,1)S(1)} %get-tuple-element.98), channel_id=1, source_target_pairs={{0,2},{1,0},{2,3},{3,1},{4,6},{5,4},{6,7},{7,5},{8,10},{9,8},{10,1... | collective-permute-start | bytes 1572872 | tf_op jit(solution)/shard_map/ppermute | solution.py:282
  42.9 1.7 %collective-permute-done.10.inward_ref = bf16[256,1024]{1,0:T(8,128)(2,1)S(1)} collective-permute-done((bf16[256,1024]{1,0:T(8,128)(2,1)S(1)}, bf16[256,1024]{1,0:T(8,128)(2,1)S(1)}, u32[]{:S(2)}, u32[]{:S(2)}) %collective-permute-start.10) | collective-permute-done | bytes 524320 | tf_op jit(solution)/shard_map/ppermute | solution.py:278
  44.8 14.2 %collective-permute-start.17 = (bf16[256,1024]{1,0:T(8,128)(2,1)S(1)}, bf16[256,1024]{1,0:T(8,128)(2,1)S(1)}, u32[]{:S(2)}, u32[]{:S(2)}) collective-permute-start(bf16[256,1024]{1,0:T(8,128)(2,1)S(1)} %get-tuple-element.99), channel_id=1, source_target_pairs={{0,1},{3,2},{1,3},{2,0},{4,5},{7,6},{5,7},{6,4},{8,9},{11,10},{9,1... | collective-permute-start | bytes 1572872 | tf_op jit(solution)/shard_map/ppermute | solution.py:293
  59.0 2.4 %collective-permute-start.11 = (bf16[96,640]{1,0:T(8,128)(2,1)S(1)}, bf16[96,640]{1,0:T(8,128)(2,1)S(1)}, u32[]{:S(2)}, u32[]{:S(2)}) collective-permute-start(bf16[96,640]{1,0:T(8,128)(2,1)S(1)} %get-tuple-element.89), channel_id=1, source_target_pairs={{0,24},{4,28},{8,16},{12,20},{16,8},{20,12},{24,0},{28,4},{1,25},{... | collective-permute-start | bytes 368648 | tf_op jit(solution)/shard_map/ppermute | solution.py:254
  61.4 1.7 %collective-permute-start.13 = (bf16[96,640]{1,0:T(8,128)(2,1)S(1)}, bf16[96,640]{1,0:T(8,128)(2,1)S(1)}, u32[]{:S(2)}, u32[]{:S(2)}) collective-permute-start(bf16[96,640]{1,0:T(8,128)(2,1)S(1)} %get-tuple-element.91), channel_id=1, source_target_pairs={{0,20},{4,16},{8,28},{12,24},{16,4},{20,0},{24,12},{28,8},{1,21},{... | collective-permute-start | bytes 368648 | tf_op jit(solution)/shard_map/ppermute | solution.py:254
  63.2 1.9 %collective-permute-done.11.refs_2_ = bf16[96,640]{1,0:T(8,128)(2,1)S(1)} collective-permute-done((bf16[96,640]{1,0:T(8,128)(2,1)S(1)}, bf16[96,640]{1,0:T(8,128)(2,1)S(1)}, u32[]{:S(2)}, u32[]{:S(2)}) %collective-permute-start.11) | collective-permute-done | bytes 122912 | tf_op jit(solution)/shard_map/ppermute | solution.py:254
  65.1 2.4 %collective-permute-done.12.refs_3_ = bf16[96,640]{1,0:T(8,128)(2,1)S(1)} collective-permute-done((bf16[96,640]{1,0:T(8,128)(2,1)S(1)}, bf16[96,640]{1,0:T(8,128)(2,1)S(1)}, u32[]{:S(2)}, u32[]{:S(2)}) %collective-permute-start.12) | collective-permute-done | bytes 122912 | tf_op jit(solution)/shard_map/ppermute | solution.py:254
  67.5 2.5 %collective-permute-done.13.refs_4_ = bf16[96,640]{1,0:T(8,128)(2,1)S(1)} collective-permute-done((bf16[96,640]{1,0:T(8,128)(2,1)S(1)}, bf16[96,640]{1,0:T(8,128)(2,1)S(1)}, u32[]{:S(2)}, u32[]{:S(2)}) %collective-permute-start.13) | collective-permute-done | bytes 122912 | tf_op jit(solution)/shard_map/ppermute | solution.py:254
  70.0 0.5 collective-permute-done.14.refs_5_
  70.5 2.6 %finish.1 = (bf16[576,512]{1,0:T(8,128)(2,1)}, bf16[576]{0:T(1024)(128)(2,1)}) custom-call(s32[1,576]{1,0:T(1,128)S(1)} %copy-done.5, bf16[576]{0:T(1024)(128)(2,1)S(1)} %copy-done.7, bf16[576,512]{1,0:T(8,128)(2,1)S(1)} %copy-done.2, f32[1,512]{1,0:T(1,128)S(1)} %bitcast.17, bf16[576,512]{1,0:T(8,128)(2,1)S(1)} %copy-done.3, ...), custom_call_target="tpu_custom_call" | custom-call | flops 1 | bytes 1 | tf_op jit(solution)/shard_map/finish/pallas_call | solution.py:413
  73.1 1.1 %total.1 = (f32[128,1024]{1,0:T(8,128)}, f32[256,512]{1,0:T(8,128)}) custom-call(f32[256,1024]{1,0:T(8,128)S(1)} %get-tuple-element.97.sum_ref, bf16[256,1024]{1,0:T(8,128)(2,1)S(1)} %collective-permute-done.16.cycle_ref, bf16[256,1024]{1,0:T(8,128)(2,1)S(1)} %collective-permute-done.17.last_ref), custom_call_target="tpu_custom_call" | custom-call | flops 1 | bytes 1 | tf_op jit(solution)/shard_map/total/pallas_call | solution.py:295
  (34 shorter events, 0.7 us)
Async XLA Ops:
  0.6 8.4 %copy-start.3 = (bf16[576,512]{1,0:T(8,128)(2,1)S(1)}, bf16[576,512]{1,0:T(8,128)(2,1)}, u32[]{:S(2)}) copy-start(bf16[576,512]{1,0:T(8,128)(2,1)} %go_ref.3) | copy-start | bytes 1769476
  0.6 8.4 %copy-start.2 = (bf16[576,512]{1,0:T(8,128)(2,1)S(1)}, bf16[576,512]{1,0:T(8,128)(2,1)}, u32[]{:S(2)}) copy-start(bf16[576,512]{1,0:T(8,128)(2,1)} %tok_ref.3) | copy-start | bytes 1769476
  0.7 18.7 %copy-start.1 = (bf16[1,1024,512]{2,1,0:T(8,128)(2,1)S(1)}, bf16[1,1024,512]{2,1,0:T(8,128)(2,1)}, u32[]{:S(2)}) copy-start(bf16[1,1024,512]{2,1,0:T(8,128)(2,1)} %param.10) | copy-start | bytes 3145732
  0.7 18.7 %copy-start = (bf16[1,512,1024]{2,1,0:T(8,128)(2,1)S(1)}, bf16[1,512,1024]{2,1,0:T(8,128)(2,1)}, u32[]{:S(2)}) copy-start(bf16[1,512,1024]{2,1,0:T(8,128)(2,1)} %param.9) | copy-start | bytes 3145732
  4.5 11.0 %collective-permute-start = (bf16[96,1024]{1,0:T(8,128)(2,1)}, bf16[96,1024]{1,0:T(8,128)(2,1)S(1)}, u32[]{:S(2)}, u32[]{:S(2)}) collective-permute-start(bf16[96,1024]{1,0:T(8,128)(2,1)} %get-tuple-element.54), channel_id=1, source_target_pairs={{0,16},{4,20},{8,24},{12,28},{16,0},{20,4},{24,8},{28,12},{1,17},{... | collective-permute-start | bytes 589832 | tf_op jit(solution)/shard_map/ppermute | solution.py:254
  7.5 8.3 %collective-permute-start.1 = (bf16[96,1024]{1,0:T(8,128)(2,1)}, bf16[96,1024]{1,0:T(8,128)(2,1)S(1)}, u32[]{:S(2)}, u32[]{:S(2)}) collective-permute-start(bf16[96,1024]{1,0:T(8,128)(2,1)} %get-tuple-element.55), channel_id=1, source_target_pairs={{0,8},{4,12},{8,0},{12,4},{16,24},{20,28},{24,16},{28,20},{1,9},{5... | collective-permute-start | bytes 589832 | tf_op jit(solution)/shard_map/ppermute | solution.py:254
  9.0 10.3 %collective-permute-start.2 = (bf16[96,1024]{1,0:T(8,128)(2,1)}, bf16[96,1024]{1,0:T(8,128)(2,1)S(1)}, u32[]{:S(2)}, u32[]{:S(2)}) collective-permute-start(bf16[96,1024]{1,0:T(8,128)(2,1)} %get-tuple-element.56), channel_id=1, source_target_pairs={{0,24},{4,28},{8,16},{12,20},{16,8},{20,12},{24,0},{28,4},{1,25},{... | collective-permute-start | bytes 589832 | tf_op jit(solution)/shard_map/ppermute | solution.py:254
  9.1 0.7 copy-start.4
  9.7 0.7 copy-start.6
  10.4 0.7 copy-start.8
  12.4 6.9 %collective-permute-start.3 = (bf16[96,1024]{1,0:T(8,128)(2,1)S(1)}, bf16[96,1024]{1,0:T(8,128)(2,1)S(1)}, u32[]{:S(2)}, u32[]{:S(2)}) collective-permute-start(bf16[96,1024]{1,0:T(8,128)(2,1)S(1)} %get-tuple-element.57), channel_id=1, source_target_pairs={{0,4},{4,0},{8,12},{12,8},{16,20},{20,16},{24,28},{28,24},{1,5},{5... | collective-permute-start | bytes 589832 | tf_op jit(solution)/shard_map/ppermute | solution.py:254
  12.5 10.3 %collective-permute-start.4 = (bf16[96,1024]{1,0:T(8,128)(2,1)}, bf16[96,1024]{1,0:T(8,128)(2,1)S(1)}, u32[]{:S(2)}, u32[]{:S(2)}) collective-permute-start(bf16[96,1024]{1,0:T(8,128)(2,1)} %get-tuple-element.61), channel_id=1, source_target_pairs={{0,28},{4,24},{8,20},{12,16},{16,12},{20,8},{24,4},{28,0},{1,29},{... | collective-permute-start | bytes 589832 | tf_op jit(solution)/shard_map/ppermute | solution.py:254
  15.5 11.0 %collective-permute-start.5 = (bf16[96,1024]{1,0:T(8,128)(2,1)S(1)}, bf16[96,1024]{1,0:T(8,128)(2,1)S(1)}, u32[]{:S(2)}, u32[]{:S(2)}) collective-permute-start(bf16[96,1024]{1,0:T(8,128)(2,1)S(1)} %get-tuple-element.64), channel_id=1, source_target_pairs={{0,20},{4,16},{8,28},{12,24},{16,4},{20,0},{24,12},{28,8},{1,21},{... | collective-permute-start | bytes 589832 | tf_op jit(solution)/shard_map/ppermute | solution.py:254
  15.8 10.7 %collective-permute-start.6 = (bf16[96,1024]{1,0:T(8,128)(2,1)S(1)}, bf16[96,1024]{1,0:T(8,128)(2,1)S(1)}, u32[]{:S(2)}, u32[]{:S(2)}) collective-permute-start(bf16[96,1024]{1,0:T(8,128)(2,1)S(1)} %get-tuple-element.65), channel_id=1, source_target_pairs={{0,12},{4,8},{8,4},{12,0},{16,28},{20,24},{24,20},{28,16},{1,13},{... | collective-permute-start | bytes 589832 | tf_op jit(solution)/shard_map/ppermute | solution.py:254
  28.6 15.9 %collective-permute-start.10 = (bf16[256,1024]{1,0:T(8,128)(2,1)S(1)}, bf16[256,1024]{1,0:T(8,128)(2,1)S(1)}, u32[]{:S(2)}, u32[]{:S(2)}) collective-permute-start(bf16[256,1024]{1,0:T(8,128)(2,1)S(1)} %get-tuple-element.79), channel_id=1, source_target_pairs={{0,1},{3,2},{4,5},{7,6},{8,9},{11,10},{12,13},{15,14},{16,17},{19,... | collective-permute-start | bytes 1572872 | tf_op jit(solution)/shard_map/ppermute | solution.py:278
  32.3 12.2 %collective-permute-start.9 = (bf16[256,1024]{1,0:T(8,128)(2,1)S(1)}, bf16[256,1024]{1,0:T(8,128)(2,1)S(1)}, u32[]{:S(2)}, u32[]{:S(2)}) collective-permute-start(bf16[256,1024]{1,0:T(8,128)(2,1)S(1)} %get-tuple-element.79), channel_id=1, source_target_pairs={{1,2},{2,1},{5,6},{6,5},{9,10},{10,9},{13,14},{14,13},{17,18},{18,... | collective-permute-start | bytes 1572872 | tf_op jit(solution)/shard_map/ppermute | solution.py:279
  33.0 37.5 %copy-start.5 = (s32[1,576]{1,0:T(1,128)S(1)}, s32[1,576]{1,0:T(1,128)}, u32[]{:S(2)}) copy-start(s32[1,576]{1,0:T(1,128)} %get-tuple-element.53.target_ref) | copy-start | bytes 6916
  33.0 37.5 %copy-start.7 = (bf16[576]{0:T(1024)(128)(2,1)S(1)}, bf16[576]{0:T(1024)(128)(2,1)}, u32[]{:S(2)}) copy-start(bf16[576]{0:T(1024)(128)(2,1)} %gate_ref.3) | copy-start | bytes 3460
  33.0 37.5 %copy-start.9 = (f32[512]{0:T(512)S(1)}, f32[512]{0:T(512)}, u32[]{:S(2)}) copy-start(f32[512]{0:T(512)} %param.8) | copy-start | bytes 6148
  34.4 5.1 %collective-permute-start.7 = (bf16[96,640]{1,0:T(8,128)(2,1)S(1)}, bf16[96,640]{1,0:T(8,128)(2,1)S(1)}, u32[]{:S(2)}, u32[]{:S(2)}) collective-permute-start(bf16[96,640]{1,0:T(8,128)(2,1)S(1)} %get-tuple-element.74), channel_id=1, source_target_pairs={{0,16},{4,20},{8,24},{12,28},{16,0},{20,4},{24,8},{28,12},{1,17},{... | collective-permute-start | bytes 368648 | tf_op jit(solution)/shard_map/ppermute | solution.py:254
  36.0 4.9 %collective-permute-start.8 = (bf16[96,640]{1,0:T(8,128)(2,1)S(1)}, bf16[96,640]{1,0:T(8,128)(2,1)S(1)}, u32[]{:S(2)}, u32[]{:S(2)}) collective-permute-start(bf16[96,640]{1,0:T(8,128)(2,1)S(1)} %get-tuple-element.76), channel_id=1, source_target_pairs={{0,8},{4,12},{8,0},{12,4},{16,24},{20,28},{24,16},{28,20},{1,9},{5... | collective-permute-start | bytes 368648 | tf_op jit(solution)/shard_map/ppermute | solution.py:254
  40.8 32.3 %collective-permute-start.16 = (bf16[256,1024]{1,0:T(8,128)(2,1)S(1)}, bf16[256,1024]{1,0:T(8,128)(2,1)S(1)}, u32[]{:S(2)}, u32[]{:S(2)}) collective-permute-start(bf16[256,1024]{1,0:T(8,128)(2,1)S(1)} %get-tuple-element.98), channel_id=1, source_target_pairs={{0,2},{1,0},{2,3},{3,1},{4,6},{5,4},{6,7},{7,5},{8,10},{9,8},{10,1... | collective-permute-start | bytes 1572872 | tf_op jit(solution)/shard_map/ppermute | solution.py:282
  44.8 28.4 %collective-permute-start.17 = (bf16[256,1024]{1,0:T(8,128)(2,1)S(1)}, bf16[256,1024]{1,0:T(8,128)(2,1)S(1)}, u32[]{:S(2)}, u32[]{:S(2)}) collective-permute-start(bf16[256,1024]{1,0:T(8,128)(2,1)S(1)} %get-tuple-element.99), channel_id=1, source_target_pairs={{0,1},{3,2},{1,3},{2,0},{4,5},{7,6},{5,7},{6,4},{8,9},{11,10},{9,1... | collective-permute-start | bytes 1572872 | tf_op jit(solution)/shard_map/ppermute | solution.py:293
  59.0 6.1 %collective-permute-start.11 = (bf16[96,640]{1,0:T(8,128)(2,1)S(1)}, bf16[96,640]{1,0:T(8,128)(2,1)S(1)}, u32[]{:S(2)}, u32[]{:S(2)}) collective-permute-start(bf16[96,640]{1,0:T(8,128)(2,1)S(1)} %get-tuple-element.89), channel_id=1, source_target_pairs={{0,24},{4,28},{8,16},{12,20},{16,8},{20,12},{24,0},{28,4},{1,25},{... | collective-permute-start | bytes 368648 | tf_op jit(solution)/shard_map/ppermute | solution.py:254
  61.4 6.1 %collective-permute-start.12 = (bf16[96,640]{1,0:T(8,128)(2,1)S(1)}, bf16[96,640]{1,0:T(8,128)(2,1)S(1)}, u32[]{:S(2)}, u32[]{:S(2)}) collective-permute-start(bf16[96,640]{1,0:T(8,128)(2,1)S(1)} %get-tuple-element.90), channel_id=1, source_target_pairs={{0,28},{4,24},{8,20},{12,16},{16,12},{20,8},{24,4},{28,0},{1,29},{... | collective-permute-start | bytes 368648 | tf_op jit(solution)/shard_map/ppermute | solution.py:254
  61.4 8.5 %collective-permute-start.13 = (bf16[96,640]{1,0:T(8,128)(2,1)S(1)}, bf16[96,640]{1,0:T(8,128)(2,1)S(1)}, u32[]{:S(2)}, u32[]{:S(2)}) collective-permute-start(bf16[96,640]{1,0:T(8,128)(2,1)S(1)} %get-tuple-element.91), channel_id=1, source_target_pairs={{0,20},{4,16},{8,28},{12,24},{16,4},{20,0},{24,12},{28,8},{1,21},{... | collective-permute-start | bytes 368648 | tf_op jit(solution)/shard_map/ppermute | solution.py:254
  65.1 5.4 %collective-permute-start.14 = (bf16[96,640]{1,0:T(8,128)(2,1)S(1)}, bf16[96,640]{1,0:T(8,128)(2,1)S(1)}, u32[]{:S(2)}, u32[]{:S(2)}) collective-permute-start(bf16[96,640]{1,0:T(8,128)(2,1)S(1)} %get-tuple-element.92), channel_id=1, source_target_pairs={{0,12},{4,8},{8,4},{12,0},{16,28},{20,24},{24,20},{28,16},{1,13},{... | collective-permute-start | bytes 368648 | tf_op jit(solution)/shard_map/ppermute | solution.py:254
  67.5 3.0 %collective-permute-start.15 = (bf16[96,640]{1,0:T(8,128)(2,1)S(1)}, bf16[96,640]{1,0:T(8,128)(2,1)S(1)}, u32[]{:S(2)}, u32[]{:S(2)}) collective-permute-start(bf16[96,640]{1,0:T(8,128)(2,1)S(1)} %get-tuple-element.93), channel_id=1, source_target_pairs={{0,4},{4,0},{8,12},{12,8},{16,20},{20,16},{24,28},{28,24},{1,5},{5... | collective-permute-start | bytes 368648 | tf_op jit(solution)/shard_map/ppermute | solution.py:254

commit v14 on v13

--- a/solution.py
+++ b/solution.py
@@ -196,7 +196,7 @@
 def later_kernel(count, groups, place, w_in_ref, w_out_ref, sum_in_ref, sum_out_ref, *refs):
     blocks = refs[:count]
     outs = refs[count : count + LINE]
-    gpre_ref, extra_ref, rows_ref, turned_ref = refs[count + LINE :]
+    upper_ref, lower_ref, gpre_ref, extra_ref, rows_ref, turned_ref = refs[count + LINE :]
     width, hidden = w_in_ref.shape
     piece_d, piece_f = width // LINE, hidden // LINE
 
@@ -210,6 +210,9 @@
 
     order = shard_order(place[0]) if groups == LINE else list(range(LINE))
     expert_work(order, blocks, w_in_ref, w_out_ref, gpre_ref, extra_ref, rows_ref, turned_ref, put)
+    cut = upper_ref.shape[0]
+    upper_ref[...] = outs[0][:cut, :]
+    lower_ref[...] = outs[0][cut:, :]
 
 
 def back_kernel(capacity, sets, w_in_ref, *refs):
@@ -256,39 +259,40 @@
     ]
 
 
-def pass_kernel(middle_ref, inward_ref, third_ref, own_ref, out_ref, sum_ref):
+def pass_kernel(above_ref, inward_ref, third_ref, own_ref, out_ref, sum_ref):
+    cut = above_ref.shape[0]
     out_ref[...] = (third_ref[...].astype(F32) + inward_ref[...].astype(F32)).astype(BF16)
-    sum_ref[...] = own_ref[...].astype(F32) + middle_ref[...].astype(F32)
-
-
-def total_kernel(sum_ref, cycle_ref, last_ref, in_ref, out_ref):
+    sum_ref[:cut, :] = own_ref[:cut, :].astype(F32) + above_ref[...].astype(F32)
+    sum_ref[cut:, :] = own_ref[cut:, :].astype(F32)
+
+
+def total_kernel(sum_ref, below_ref, cycle_ref, last_ref, in_ref, out_ref):
     piece_d, half = in_ref.shape[0], out_ref.shape[0] // 2
     width = out_ref.shape[1]
+    cut = sum_ref.shape[0] - below_ref.shape[0]
     total = sum_ref[...] + cycle_ref[...].astype(F32) + last_ref[...].astype(F32)
+    total = jnp.concatenate([total[:cut], total[cut:] + below_ref[...].astype(F32)])
     in_ref[...] = total[:piece_d]
     out_ref[:half, :] = total[piece_d:, :width]
     out_ref[half:, :] = total[piece_d:, width:]
 
 
-def line_sums(first, second, third, own, width, returned):
+def line_sums(first, second, third, own, upper, lower, width, returned):
     rows, hidden = own.shape
     piece_d = width // LINE
     ahead = len(returned) // 4
     order = block_order(len(returned))
     inward = lax.ppermute(first, "dp", [(0, 1), (3, 2)])
-    middle = lax.ppermute(first, "dp", [(1, 2), (2, 1)])
+    above = lax.ppermute(upper, "dp", [(1, 2), (2, 1)])
+    below = lax.ppermute(lower, "dp", [(1, 2), (2, 1)])
     back = swap_blocks(returned[:ahead], order[:ahead])
     second, back[0] = lax.optimization_barrier((second, back[0]))
     cycle = lax.ppermute(second, "dp", [(0, 2), (1, 0), (2, 3), (3, 1)])
     third, *back = lax.optimization_barrier((third, *back))
+    shape = functools.partial(jax.ShapeDtypeStruct, own.shape)
     passed, most = kernel_call(
-        pass_kernel,
-        "pass",
-        1,
-        1,
-        [jax.ShapeDtypeStruct(own.shape, BF16), jax.ShapeDtypeStruct(own.shape, F32)],
-        [vmem] * 4,
-    )(middle, inward, third, own)
+        pass_kernel, "pass", 1, 1, [shape(BF16), shape(F32)], [vmem] * 4
+    )(above, inward, third, own)
     passed, *rest = lax.optimization_barrier((passed, *returned[ahead:]))
     last = lax.ppermute(passed, "dp", [(0, 1), (3, 2), (1, 3), (2, 0)])
     back += swap_blocks(rest, order[ahead:])
@@ -301,8 +305,8 @@
             jax.ShapeDtypeStruct((piece_d, hidden), F32),
             jax.ShapeDtypeStruct((2 * (rows - piece_d), width), F32),
         ],
-        [vmem] * 3,
-    )(most, cycle, last)
+        [vmem] * 4,
+    )(most, below, cycle, last)
     return *sums, back
 
 
@@ -389,7 +393,11 @@
     *sums, soon_gpre, soon_extra = work(sooner_kernel, "sooner", soon_set, sums_shape)
     *sums, next_gpre, next_extra = work(next_kernel, "next", next_set, sums_shape, *sums)
     piece = shape((width // LINE + hidden // LINE // 2, hidden), BF16)
-    *parts, late_gpre, late_extra = work(later_kernel, "later", late_set, [piece] * LINE, *sums)
+    cut = 3 * piece.shape[0] // 4
+    cut_pieces = [shape((cut, hidden), BF16), shape((piece.shape[0] - cut, hidden), BF16)]
+    *parts, late_gpre, late_extra = work(
+        later_kernel, "later", late_set, [piece] * LINE + cut_pieces, *sums
+    )
     returned = kernel_call(
         functools.partial(back_kernel, capacity, (soon_set, next_set, late_set)),
         "back",
@@ -403,7 +411,7 @@
         grad_w_in, grad_w_out, back = line_sums(*parts, width, returned)
     else:
         back = swap_blocks(returned, block_order(sources))
-        parts_in, parts_out = zip(*[split_piece(part, width, LINE) for part in parts])
+        parts_in, parts_out = zip(*[split_piece(part, width, LINE) for part in parts[:LINE]])
         grad_w_in, grad_w_out = (
             lax.psum_scatter(
                 jnp.concatenate(part), "dp", scatter_dimension=0, tiled=True

time: 74.4 us -> 70.9 us (0.953)
  starting transfers between devices: 35.9 us -> 26 us
  waiting for transfers between devices: 17.7 us -> 23.7 us
    ppermute x1, starting transfers between devices: 14.2 us -> 2.53 us  [line_sums(): last = lax.ppermute(passed, 'dp', [(0, 1), (3, 2), (1, 3), (2, 0)])]
    ppermute x1, waiting for transfers between devices: 0.01 us -> 5.54 us  [line_sums(): last = lax.ppermute(passed, 'dp', [(0, 1), (3, 2), (1, 3), (2, 0)])]
    ppermute x14, starting transfers between devices: 15.3 us -> 16.4 us  [swap_blocks(): lax.ppermute(block, 'space', [(i, i ^ k) for i in devices])]
  transfers between devices with their start and end apart: 18 -> 19, of which waited for: 10 -> 11; matrix products, arithmetic and copies ran while one was open for 0% -> 0% of each run, Pallas kernels for 14% -> 15%
where the time goes in v14:
time: 70.9 us; the launch traced here: 70.3 us
  starting transfers between devices  26 us (37%)
  waiting for transfers between devices  23.7 us (33%)
  Pallas kernels  17.7 us (25%)
  local copies, waits for them, and re-layouts  2.06 us (3%)
  between operations  0.81 us (1%)
    ppermute x14, waiting for transfers between devices, swap_blocks(): lax.ppermute(block, 'space', [(i, i ^ k) for i in devices])  16.5 us
    ppermute x14, starting transfers between devices, swap_blocks(): lax.ppermute(block, 'space', [(i, i ^ k) for i in devices])  16.4 us
    pallas_call x3, Pallas kernels, work(): kernel_call(functools.partial(kernel, count, groups), name, 8 * span * wi...  7.32 us
    ppermute x1, waiting for transfers between devices, line_sums(): last = lax.ppermute(passed, 'dp', [(0, 1), (3, 2), (1, 3), (2, 0)])  5.54 us
    pallas_call x1, Pallas kernels, body(): kernel_call(functools.partial(place_kernel, sources, capacity), 'place',...  3.79 us
    ppermute x1, starting transfers between devices, line_sums(): inward = lax.ppermute(first, 'dp', [(0, 1), (3, 2)])  3.66 us
    pallas_call x1, Pallas kernels, body(): kernel_call(finish_kernel, 'finish', 1, 1, [shape((tok_rows, width), BF16...  2.59 us
    ppermute x1, starting transfers between devices, line_sums(): last = lax.ppermute(passed, 'dp', [(0, 1), (3, 2), (1, 3), (2, 0)])  2.53 us
  transfers between devices with their start and end apart: 19, of which 11 were waited for; matrix products, arithmetic and copies ran while one was open for 0% of the time, Pallas kernels for 15%

profile of v14, /device:TPU:0, one launch (start us, length us, event | category | flops | bytes accessed | tf_op | source)
XLA Modules:
  0.0 70.3 jit_solution(207520383772058534)
XLA Ops:
  0.7 3.8 %place.1 = (s32[1,576]{1,0:T(1,128)}, bf16[96,1024]{1,0:T(8,128)(2,1)}, bf16[96,1024]{1,0:T(8,128)(2,1)}, bf16[96,1024]{1,0:T(8,128)(2,1)}, bf16[96,1024]{1,0:T(8,128)(2,1)}) custom-call(s32[1]{0:T(128)} %bitcast.me, s32[1]{0:T(128)} %bitcast.1.place, s32[1,576]{1,0:T(1,128)} %bitcast.20, bf16[576]{0:T(1024)(128)(2,1)} %gate_ref.3, ...), custom_call_target="tpu_custom_call" | custom-call | flops 452984832 | bytes 2752512 | tf_op jit(solution)/shard_map/place/pallas_call | solution.py:332
  4.5 3.0 %collective-permute-start = (bf16[96,1024]{1,0:T(8,128)(2,1)}, bf16[96,1024]{1,0:T(8,128)(2,1)S(1)}, u32[]{:S(2)}, u32[]{:S(2)}) collective-permute-start(bf16[96,1024]{1,0:T(8,128)(2,1)} %get-tuple-element.56), channel_id=1, source_target_pairs={{0,16},{4,20},{8,24},{12,28},{16,0},{20,4},{24,8},{28,12},{1,17},{... | collective-permute-start | bytes 589832 | tf_op jit(solution)/shard_map/ppermute | solution.py:257
  7.5 1.5 %collective-permute-start.1 = (bf16[96,1024]{1,0:T(8,128)(2,1)}, bf16[96,1024]{1,0:T(8,128)(2,1)S(1)}, u32[]{:S(2)}, u32[]{:S(2)}) collective-permute-start(bf16[96,1024]{1,0:T(8,128)(2,1)} %get-tuple-element.57), channel_id=1, source_target_pairs={{0,8},{4,12},{8,0},{12,4},{16,24},{20,28},{24,16},{28,20},{1,9},{5... | collective-permute-start | bytes 589832 | tf_op jit(solution)/shard_map/ppermute | solution.py:257
  9.7 0.7 copy-done.6
  10.4 0.7 copy-done.8
  11.1 1.3 %rest.1 = (bf16[96,1024]{1,0:T(8,128)(2,1)S(1)}, bf16[96,1024]{1,0:T(8,128)(2,1)S(1)}, bf16[96,1024]{1,0:T(8,128)(2,1)S(1)}, bf16[96,1024]{1,0:T(8,128)(2,1)S(1)}) custom-call(s32[1,576]{1,0:T(1,128)S(1)} %copy-done.4, bf16[576]{0:T(1024)(128)(2,1)S(1)} %copy-done.6, bf16[576,512]{1,0:T(8,128)(2,1)S(1)} %copy-done.2, f32[1,512]{1,0:T(1,128)S(1)} %bitcast.16, ...), custom_call_target="tpu_custom_call" | custom-call | flops 1 | bytes 1 | tf_op jit(solution)/shard_map/rest/pallas_call | solution.py:353
  12.5 3.0 %collective-permute-start.4 = (bf16[96,1024]{1,0:T(8,128)(2,1)}, bf16[96,1024]{1,0:T(8,128)(2,1)S(1)}, u32[]{:S(2)}, u32[]{:S(2)}) collective-permute-start(bf16[96,1024]{1,0:T(8,128)(2,1)} %get-tuple-element.63), channel_id=1, source_target_pairs={{0,28},{4,24},{8,20},{12,16},{16,12},{20,8},{24,4},{28,0},{1,29},{... | collective-permute-start | bytes 589832 | tf_op jit(solution)/shard_map/ppermute | solution.py:257
  15.9 3.4 %collective-permute-done.2.refs_2_ = bf16[96,1024]{1,0:T(8,128)(2,1)S(1)} collective-permute-done((bf16[96,1024]{1,0:T(8,128)(2,1)}, bf16[96,1024]{1,0:T(8,128)(2,1)S(1)}, u32[]{:S(2)}, u32[]{:S(2)}) %collective-permute-start.2) | collective-permute-done | bytes 196640 | tf_op jit(solution)/shard_map/ppermute | solution.py:257
  19.3 3.2 %sooner.1 = (f32[512,1024]{1,0:T(8,128)S(1)}, f32[1024,512]{1,0:T(8,128)S(1)}, bf16[480,1024]{1,0:T(8,128)(2,1)S(1)}, bf16[480,128]{1,0:T(8,128)(2,1)S(1)}) custom-call(s32[1]{0:T(128)} %bitcast.1.place, bf16[512,1024]{1,0:T(8,128)(2,1)S(1)} %bitcast.8, bf16[1024,512]{1,0:T(8,128)(2,1)S(1)} %bitcast.12, bf16[96,1024]{1,0:T(8,128)(2,1)S(1)} %collective-permute-done.refs_0_, ...), custom_call_target="tpu_custom_call" | custom-call | flops 2013265920 | bytes 6160384 | tf_op jit(solution)/shard_map/sooner/pallas_call | solution.py:382
  22.8 2.0 %next.1 = (f32[512,1024]{1,0:T(8,128)S(1)}, f32[1024,512]{1,0:T(8,128)S(1)}, bf16[96,1024]{1,0:T(8,128)(2,1)S(1)}, bf16[96,128]{1,0:T(8,128)(2,1)S(1)}) custom-call(s32[1]{0:T(128)} %bitcast.1.place, bf16[512,1024]{1,0:T(8,128)(2,1)S(1)} %bitcast.9, bf16[1024,512]{1,0:T(8,128)(2,1)S(1)} %bitcast.13, f32[512,1024]{1,0:T(8,128)S(1)} %get-tuple-element.61.old_in_ref, ...), custom_call_target="tpu_custom_call" | custom-call | flops 402653184 | bytes 4587520 | tf_op jit(solution)/shard_map/next/pallas_call | solution.py:382
  24.7 1.7 %collective-permute-done.5.refs_0_ = bf16[96,1024]{1,0:T(8,128)(2,1)S(1)} collective-permute-done((bf16[96,1024]{1,0:T(8,128)(2,1)S(1)}, bf16[96,1024]{1,0:T(8,128)(2,1)S(1)}, u32[]{:S(2)}, u32[]{:S(2)}) %collective-permute-start.5) | collective-permute-done | bytes 196640 | tf_op jit(solution)/shard_map/ppermute | solution.py:257
  26.5 2.1 %later.1 = (bf16[256,1024]{1,0:T(8,128)(2,1)S(1)}, bf16[256,1024]{1,0:T(8,128)(2,1)S(1)}, bf16[256,1024]{1,0:T(8,128)(2,1)S(1)}, bf16[256,1024]{1,0:T(8,128)(2,1...) custom-call(s32[1]{0:T(128)} %bitcast.1.place, ...), custom_call_target="tpu_custom_call" | custom-call | flops 805306368 | bytes 4980736 | tf_op jit(solution)/shard_map/later/pallas_call | solution.py:382
  28.6 3.7 %collective-permute-start.10 = (bf16[256,1024]{1,0:T(8,128)(2,1)S(1)}, bf16[256,1024]{1,0:T(8,128)(2,1)S(1)}, u32[]{:S(2)}, u32[]{:S(2)}) collective-permute-start(bf16[256,1024]{1,0:T(8,128)(2,1)S(1)} %get-tuple-element.82), channel_id=1, source_target_pairs={{0,1},{3,2},{4,5},{7,6},{8,9},{11,10},{12,13},{15,14},{16,17},{19,... | collective-permute-start | bytes 1572872 | tf_op jit(solution)/shard_map/ppermute | solution.py:285
  32.3 0.7 collective-permute-start.9
  33.0 1.3 %back.1 = (bf16[96,640]{1,0:T(8,128)(2,1)S(1)}, bf16[96,640]{1,0:T(8,128)(2,1)S(1)}, bf16[96,640]{1,0:T(8,128)(2,1)S(1)}, bf16[96,640]{1,0:T(8,128)(2,1)S(1)}, b...) custom-call(bf16[512,1024]{1,0:T(8,128)(2,1)S(1)} %bitcast.11, ...), custom_call_target="tpu_custom_call" | custom-call | flops 1 | bytes 1 | tf_op jit(solution)/shard_map/back/pallas_call | solution.py:401
  34.4 1.6 %collective-permute-start.7 = (bf16[96,640]{1,0:T(8,128)(2,1)S(1)}, bf16[96,640]{1,0:T(8,128)(2,1)S(1)}, u32[]{:S(2)}, u32[]{:S(2)}) collective-permute-start(bf16[96,640]{1,0:T(8,128)(2,1)S(1)} %get-tuple-element.76), channel_id=1, source_target_pairs={{0,16},{4,20},{8,24},{12,28},{16,0},{20,4},{24,8},{28,12},{1,17},{... | collective-permute-start | bytes 368648 | tf_op jit(solution)/shard_map/ppermute | solution.py:257
  35.9 1.5 %collective-permute-start.8 = (bf16[96,640]{1,0:T(8,128)(2,1)S(1)}, bf16[96,640]{1,0:T(8,128)(2,1)S(1)}, u32[]{:S(2)}, u32[]{:S(2)}) collective-permute-start(bf16[96,640]{1,0:T(8,128)(2,1)S(1)} %get-tuple-element.78), channel_id=1, source_target_pairs={{0,8},{4,12},{8,0},{12,4},{16,24},{20,28},{24,16},{28,20},{1,9},{5... | collective-permute-start | bytes 368648 | tf_op jit(solution)/shard_map/ppermute | solution.py:257
  37.4 2.0 %collective-permute-done.7.refs_0_ = bf16[96,640]{1,0:T(8,128)(2,1)S(1)} collective-permute-done((bf16[96,640]{1,0:T(8,128)(2,1)S(1)}, bf16[96,640]{1,0:T(8,128)(2,1)S(1)}, u32[]{:S(2)}, u32[]{:S(2)}) %collective-permute-start.7) | collective-permute-done | bytes 122912 | tf_op jit(solution)/shard_map/ppermute | solution.py:257
  39.5 1.3 %collective-permute-done.8.refs_1_ = bf16[96,640]{1,0:T(8,128)(2,1)S(1)} collective-permute-done((bf16[96,640]{1,0:T(8,128)(2,1)S(1)}, bf16[96,640]{1,0:T(8,128)(2,1)S(1)}, u32[]{:S(2)}, u32[]{:S(2)}) %collective-permute-start.8) | collective-permute-done | bytes 122912 | tf_op jit(solution)/shard_map/ppermute | solution.py:257
  40.8 2.0 %collective-permute-start.17 = (bf16[256,1024]{1,0:T(8,128)(2,1)S(1)}, bf16[256,1024]{1,0:T(8,128)(2,1)S(1)}, u32[]{:S(2)}, u32[]{:S(2)}) collective-permute-start(bf16[256,1024]{1,0:T(8,128)(2,1)S(1)} %get-tuple-element.102), channel_id=1, source_target_pairs={{0,2},{1,0},{2,3},{3,1},{4,6},{5,4},{6,7},{7,5},{8,10},{9,8},{10,1... | collective-permute-start | bytes 1572872 | tf_op jit(solution)/shard_map/ppermute | solution.py:290
  42.9 1.6 %collective-permute-done.10.inward_ref = bf16[256,1024]{1,0:T(8,128)(2,1)S(1)} collective-permute-done((bf16[256,1024]{1,0:T(8,128)(2,1)S(1)}, bf16[256,1024]{1,0:T(8,128)(2,1)S(1)}, u32[]{:S(2)}, u32[]{:S(2)}) %collective-permute-start.10) | collective-permute-done | bytes 524320 | tf_op jit(solution)/shard_map/ppermute | solution.py:285
  44.7 2.5 %collective-permute-start.18 = (bf16[256,1024]{1,0:T(8,128)(2,1)S(1)}, bf16[256,1024]{1,0:T(8,128)(2,1)S(1)}, u32[]{:S(2)}, u32[]{:S(2)}) collective-permute-start(bf16[256,1024]{1,0:T(8,128)(2,1)S(1)} %get-tuple-element.103), channel_id=1, source_target_pairs={{0,1},{3,2},{1,3},{2,0},{4,5},{7,6},{5,7},{6,4},{8,9},{11,10},{9,1... | collective-permute-start | bytes 1572872 | tf_op jit(solution)/shard_map/ppermute | solution.py:297
  47.3 2.4 %collective-permute-start.11 = (bf16[96,640]{1,0:T(8,128)(2,1)S(1)}, bf16[96,640]{1,0:T(8,128)(2,1)S(1)}, u32[]{:S(2)}, u32[]{:S(2)}) collective-permute-start(bf16[96,640]{1,0:T(8,128)(2,1)S(1)} %get-tuple-element.92), channel_id=1, source_target_pairs={{0,24},{4,28},{8,16},{12,20},{16,8},{20,12},{24,0},{28,4},{1,25},{... | collective-permute-start | bytes 368648 | tf_op jit(solution)/shard_map/ppermute | solution.py:257
  49.7 1.7 %collective-permute-start.13 = (bf16[96,640]{1,0:T(8,128)(2,1)S(1)}, bf16[96,640]{1,0:T(8,128)(2,1)S(1)}, u32[]{:S(2)}, u32[]{:S(2)}) collective-permute-start(bf16[96,640]{1,0:T(8,128)(2,1)S(1)} %get-tuple-element.94), channel_id=1, source_target_pairs={{0,20},{4,16},{8,28},{12,24},{16,4},{20,0},{24,12},{28,8},{1,21},{... | collective-permute-start | bytes 368648 | tf_op jit(solution)/shard_map/ppermute | solution.py:257
  51.4 1.9 %collective-permute-done.11.refs_2_ = bf16[96,640]{1,0:T(8,128)(2,1)S(1)} collective-permute-done((bf16[96,640]{1,0:T(8,128)(2,1)S(1)}, bf16[96,640]{1,0:T(8,128)(2,1)S(1)}, u32[]{:S(2)}, u32[]{:S(2)}) %collective-permute-start.11) | collective-permute-done | bytes 122912 | tf_op jit(solution)/shard_map/ppermute | solution.py:257
  54.0 1.7 %collective-permute-done.12.refs_3_ = bf16[96,640]{1,0:T(8,128)(2,1)S(1)} collective-permute-done((bf16[96,640]{1,0:T(8,128)(2,1)S(1)}, bf16[96,640]{1,0:T(8,128)(2,1)S(1)}, u32[]{:S(2)}, u32[]{:S(2)}) %collective-permute-start.12) | collective-permute-done | bytes 122912 | tf_op jit(solution)/shard_map/ppermute | solution.py:257
  55.8 0.9 %collective-permute-start.14 = (bf16[96,640]{1,0:T(8,128)(2,1)S(1)}, bf16[96,640]{1,0:T(8,128)(2,1)S(1)}, u32[]{:S(2)}, u32[]{:S(2)}) collective-permute-start(bf16[96,640]{1,0:T(8,128)(2,1)S(1)} %get-tuple-element.95), channel_id=1, source_target_pairs={{0,12},{4,8},{8,4},{12,0},{16,28},{20,24},{24,20},{28,16},{1,13},{... | collective-permute-start | bytes 368648 | tf_op jit(solution)/shard_map/ppermute | solution.py:257
  56.7 1.5 %collective-permute-done.13.refs_4_ = bf16[96,640]{1,0:T(8,128)(2,1)S(1)} collective-permute-done((bf16[96,640]{1,0:T(8,128)(2,1)S(1)}, bf16[96,640]{1,0:T(8,128)(2,1)S(1)}, u32[]{:S(2)}, u32[]{:S(2)}) %collective-permute-start.13) | collective-permute-done | bytes 122912 | tf_op jit(solution)/shard_map/ppermute | solution.py:257
  58.4 2.6 %collective-permute-done.14.refs_5_ = bf16[96,640]{1,0:T(8,128)(2,1)S(1)} collective-permute-done((bf16[96,640]{1,0:T(8,128)(2,1)S(1)}, bf16[96,640]{1,0:T(8,128)(2,1)S(1)}, u32[]{:S(2)}, u32[]{:S(2)}) %collective-permute-start.14) | collective-permute-done | bytes 122912 | tf_op jit(solution)/shard_map/ppermute | solution.py:257
  61.0 2.6 %finish.1 = (bf16[576,512]{1,0:T(8,128)(2,1)}, bf16[576]{0:T(1024)(128)(2,1)}) custom-call(s32[1,576]{1,0:T(1,128)S(1)} %copy-done.5, bf16[576]{0:T(1024)(128)(2,1)S(1)} %copy-done.7, bf16[576,512]{1,0:T(8,128)(2,1)S(1)} %copy-done.2, f32[1,512]{1,0:T(1,128)S(1)} %bitcast.17, bf16[576,512]{1,0:T(8,128)(2,1)S(1)} %copy-done.3, ...), custom_call_target="tpu_custom_call" | custom-call | flops 1 | bytes 1 | tf_op jit(solution)/shard_map/finish/pallas_call | solution.py:421
  63.6 5.5 %collective-permute-done.18.last_ref = bf16[256,1024]{1,0:T(8,128)(2,1)S(1)} collective-permute-done((bf16[256,1024]{1,0:T(8,128)(2,1)S(1)}, bf16[256,1024]{1,0:T(8,128)(2,1)S(1)}, u32[]{:S(2)}, u32[]{:S(2)}) %collective-permute-start.18) | collective-permute-done | bytes 524320 | tf_op jit(solution)/shard_map/ppermute | solution.py:297
  69.2 1.1 %total.1 = (f32[128,1024]{1,0:T(8,128)}, f32[256,512]{1,0:T(8,128)}) custom-call(f32[256,1024]{1,0:T(8,128)S(1)} %get-tuple-element.100.sum_ref, bf16[64,1024]{1,0:T(8,128)(2,1)S(1)} %collective-permute-done.16.below_ref, bf16[256,1024]{1,0:T(8,128)(2,1)S(1)} %collective-permute-done.17.cycle_ref, bf16[256,1024]{1,0:T(8,128)(2,1)S(1)} %collective-permute-done.18.last_ref), custom_call_target="tpu_custom_call" | custom-call | flops 1 | bytes 1 | tf_op jit(solution)/shard_map/total/pallas_call | solution.py:299
  (36 shorter events, 2.5 us)
Async XLA Ops:
  0.6 8.4 %copy-start.3 = (bf16[576,512]{1,0:T(8,128)(2,1)S(1)}, bf16[576,512]{1,0:T(8,128)(2,1)}, u32[]{:S(2)}) copy-start(bf16[576,512]{1,0:T(8,128)(2,1)} %go_ref.3) | copy-start | bytes 1769476
  0.6 8.4 %copy-start.2 = (bf16[576,512]{1,0:T(8,128)(2,1)S(1)}, bf16[576,512]{1,0:T(8,128)(2,1)}, u32[]{:S(2)}) copy-start(bf16[576,512]{1,0:T(8,128)(2,1)} %tok_ref.3) | copy-start | bytes 1769476
  0.7 18.7 %copy-start.1 = (bf16[1,1024,512]{2,1,0:T(8,128)(2,1)S(1)}, bf16[1,1024,512]{2,1,0:T(8,128)(2,1)}, u32[]{:S(2)}) copy-start(bf16[1,1024,512]{2,1,0:T(8,128)(2,1)} %param.10) | copy-start | bytes 3145732
  0.7 18.7 %copy-start = (bf16[1,512,1024]{2,1,0:T(8,128)(2,1)S(1)}, bf16[1,512,1024]{2,1,0:T(8,128)(2,1)}, u32[]{:S(2)}) copy-start(bf16[1,512,1024]{2,1,0:T(8,128)(2,1)} %param.9) | copy-start | bytes 3145732
  4.5 11.0 %collective-permute-start = (bf16[96,1024]{1,0:T(8,128)(2,1)}, bf16[96,1024]{1,0:T(8,128)(2,1)S(1)}, u32[]{:S(2)}, u32[]{:S(2)}) collective-permute-start(bf16[96,1024]{1,0:T(8,128)(2,1)} %get-tuple-element.56), channel_id=1, source_target_pairs={{0,16},{4,20},{8,24},{12,28},{16,0},{20,4},{24,8},{28,12},{1,17},{... | collective-permute-start | bytes 589832 | tf_op jit(solution)/shard_map/ppermute | solution.py:257
  7.5 8.2 %collective-permute-start.1 = (bf16[96,1024]{1,0:T(8,128)(2,1)}, bf16[96,1024]{1,0:T(8,128)(2,1)S(1)}, u32[]{:S(2)}, u32[]{:S(2)}) collective-permute-start(bf16[96,1024]{1,0:T(8,128)(2,1)} %get-tuple-element.57), channel_id=1, source_target_pairs={{0,8},{4,12},{8,0},{12,4},{16,24},{20,28},{24,16},{28,20},{1,9},{5... | collective-permute-start | bytes 589832 | tf_op jit(solution)/shard_map/ppermute | solution.py:257
  9.0 10.3 %collective-permute-start.2 = (bf16[96,1024]{1,0:T(8,128)(2,1)}, bf16[96,1024]{1,0:T(8,128)(2,1)S(1)}, u32[]{:S(2)}, u32[]{:S(2)}) collective-permute-start(bf16[96,1024]{1,0:T(8,128)(2,1)} %get-tuple-element.58), channel_id=1, source_target_pairs={{0,24},{4,28},{8,16},{12,20},{16,8},{20,12},{24,0},{28,4},{1,25},{... | collective-permute-start | bytes 589832 | tf_op jit(solution)/shard_map/ppermute | solution.py:257
  9.1 0.7 copy-start.4
  9.7 0.7 copy-start.6
  10.4 0.7 copy-start.8
  12.4 6.9 %collective-permute-start.3 = (bf16[96,1024]{1,0:T(8,128)(2,1)S(1)}, bf16[96,1024]{1,0:T(8,128)(2,1)S(1)}, u32[]{:S(2)}, u32[]{:S(2)}) collective-permute-start(bf16[96,1024]{1,0:T(8,128)(2,1)S(1)} %get-tuple-element.59), channel_id=1, source_target_pairs={{0,4},{4,0},{8,12},{12,8},{16,20},{20,16},{24,28},{28,24},{1,5},{5... | collective-permute-start | bytes 589832 | tf_op jit(solution)/shard_map/ppermute | solution.py:257
  12.5 10.3 %collective-permute-start.4 = (bf16[96,1024]{1,0:T(8,128)(2,1)}, bf16[96,1024]{1,0:T(8,128)(2,1)S(1)}, u32[]{:S(2)}, u32[]{:S(2)}) collective-permute-start(bf16[96,1024]{1,0:T(8,128)(2,1)} %get-tuple-element.63), channel_id=1, source_target_pairs={{0,28},{4,24},{8,20},{12,16},{16,12},{20,8},{24,4},{28,0},{1,29},{... | collective-permute-start | bytes 589832 | tf_op jit(solution)/shard_map/ppermute | solution.py:257
  15.5 11.0 %collective-permute-start.5 = (bf16[96,1024]{1,0:T(8,128)(2,1)S(1)}, bf16[96,1024]{1,0:T(8,128)(2,1)S(1)}, u32[]{:S(2)}, u32[]{:S(2)}) collective-permute-start(bf16[96,1024]{1,0:T(8,128)(2,1)S(1)} %get-tuple-element.66), channel_id=1, source_target_pairs={{0,20},{4,16},{8,28},{12,24},{16,4},{20,0},{24,12},{28,8},{1,21},{... | collective-permute-start | bytes 589832 | tf_op jit(solution)/shard_map/ppermute | solution.py:257
  15.7 10.8 %collective-permute-start.6 = (bf16[96,1024]{1,0:T(8,128)(2,1)S(1)}, bf16[96,1024]{1,0:T(8,128)(2,1)S(1)}, u32[]{:S(2)}, u32[]{:S(2)}) collective-permute-start(bf16[96,1024]{1,0:T(8,128)(2,1)S(1)} %get-tuple-element.67), channel_id=1, source_target_pairs={{0,12},{4,8},{8,4},{12,0},{16,28},{20,24},{24,20},{28,16},{1,13},{... | collective-permute-start | bytes 589832 | tf_op jit(solution)/shard_map/ppermute | solution.py:257
  28.6 15.9 %collective-permute-start.10 = (bf16[256,1024]{1,0:T(8,128)(2,1)S(1)}, bf16[256,1024]{1,0:T(8,128)(2,1)S(1)}, u32[]{:S(2)}, u32[]{:S(2)}) collective-permute-start(bf16[256,1024]{1,0:T(8,128)(2,1)S(1)} %get-tuple-element.82), channel_id=1, source_target_pairs={{0,1},{3,2},{4,5},{7,6},{8,9},{11,10},{12,13},{15,14},{16,17},{19,... | collective-permute-start | bytes 1572872 | tf_op jit(solution)/shard_map/ppermute | solution.py:285
  32.3 10.6 %collective-permute-start.9 = (bf16[192,1024]{1,0:T(8,128)(2,1)S(1)}, bf16[192,1024]{1,0:T(8,128)(2,1)S(1)}, u32[]{:S(2)}, u32[]{:S(2)}) collective-permute-start(bf16[192,1024]{1,0:T(8,128)(2,1)S(1)} %get-tuple-element.81), channel_id=1, source_target_pairs={{1,2},{2,1},{5,6},{6,5},{9,10},{10,9},{13,14},{14,13},{17,18},{18,... | collective-permute-start | bytes 1179656 | tf_op jit(solution)/shard_map/ppermute | solution.py:286
  33.0 28.1 %copy-start.5 = (s32[1,576]{1,0:T(1,128)S(1)}, s32[1,576]{1,0:T(1,128)}, u32[]{:S(2)}) copy-start(s32[1,576]{1,0:T(1,128)} %get-tuple-element.55.target_ref) | copy-start | bytes 6916
  33.0 28.1 %copy-start.7 = (bf16[576]{0:T(1024)(128)(2,1)S(1)}, bf16[576]{0:T(1024)(128)(2,1)}, u32[]{:S(2)}) copy-start(bf16[576]{0:T(1024)(128)(2,1)} %gate_ref.3) | copy-start | bytes 3460
  33.0 28.0 %copy-start.9 = (f32[512]{0:T(512)S(1)}, f32[512]{0:T(512)}, u32[]{:S(2)}) copy-start(f32[512]{0:T(512)} %param.8) | copy-start | bytes 6148
  34.4 5.1 %collective-permute-start.7 = (bf16[96,640]{1,0:T(8,128)(2,1)S(1)}, bf16[96,640]{1,0:T(8,128)(2,1)S(1)}, u32[]{:S(2)}, u32[]{:S(2)}) collective-permute-start(bf16[96,640]{1,0:T(8,128)(2,1)S(1)} %get-tuple-element.76), channel_id=1, source_target_pairs={{0,16},{4,20},{8,24},{12,28},{16,0},{20,4},{24,8},{28,12},{1,17},{... | collective-permute-start | bytes 368648 | tf_op jit(solution)/shard_map/ppermute | solution.py:257
  35.9 4.9 %collective-permute-start.8 = (bf16[96,640]{1,0:T(8,128)(2,1)S(1)}, bf16[96,640]{1,0:T(8,128)(2,1)S(1)}, u32[]{:S(2)}, u32[]{:S(2)}) collective-permute-start(bf16[96,640]{1,0:T(8,128)(2,1)S(1)} %get-tuple-element.78), channel_id=1, source_target_pairs={{0,8},{4,12},{8,0},{12,4},{16,24},{20,28},{24,16},{28,20},{1,9},{5... | collective-permute-start | bytes 368648 | tf_op jit(solution)/shard_map/ppermute | solution.py:257
  40.8 22.8 %collective-permute-start.17 = (bf16[256,1024]{1,0:T(8,128)(2,1)S(1)}, bf16[256,1024]{1,0:T(8,128)(2,1)S(1)}, u32[]{:S(2)}, u32[]{:S(2)}) collective-permute-start(bf16[256,1024]{1,0:T(8,128)(2,1)S(1)} %get-tuple-element.102), channel_id=1, source_target_pairs={{0,2},{1,0},{2,3},{3,1},{4,6},{5,4},{6,7},{7,5},{8,10},{9,8},{10,1... | collective-permute-start | bytes 1572872 | tf_op jit(solution)/shard_map/ppermute | solution.py:290
  44.7 24.5 %collective-permute-start.18 = (bf16[256,1024]{1,0:T(8,128)(2,1)S(1)}, bf16[256,1024]{1,0:T(8,128)(2,1)S(1)}, u32[]{:S(2)}, u32[]{:S(2)}) collective-permute-start(bf16[256,1024]{1,0:T(8,128)(2,1)S(1)} %get-tuple-element.103), channel_id=1, source_target_pairs={{0,1},{3,2},{1,3},{2,0},{4,5},{7,6},{5,7},{6,4},{8,9},{11,10},{9,1... | collective-permute-start | bytes 1572872 | tf_op jit(solution)/shard_map/ppermute | solution.py:297
  47.3 6.1 %collective-permute-start.11 = (bf16[96,640]{1,0:T(8,128)(2,1)S(1)}, bf16[96,640]{1,0:T(8,128)(2,1)S(1)}, u32[]{:S(2)}, u32[]{:S(2)}) collective-permute-start(bf16[96,640]{1,0:T(8,128)(2,1)S(1)} %get-tuple-element.92), channel_id=1, source_target_pairs={{0,24},{4,28},{8,16},{12,20},{16,8},{20,12},{24,0},{28,4},{1,25},{... | collective-permute-start | bytes 368648 | tf_op jit(solution)/shard_map/ppermute | solution.py:257
  49.7 6.1 %collective-permute-start.12 = (bf16[96,640]{1,0:T(8,128)(2,1)S(1)}, bf16[96,640]{1,0:T(8,128)(2,1)S(1)}, u32[]{:S(2)}, u32[]{:S(2)}) collective-permute-start(bf16[96,640]{1,0:T(8,128)(2,1)S(1)} %get-tuple-element.93), channel_id=1, source_target_pairs={{0,28},{4,24},{8,20},{12,16},{16,12},{20,8},{24,4},{28,0},{1,29},{... | collective-permute-start | bytes 368648 | tf_op jit(solution)/shard_map/ppermute | solution.py:257
  49.7 8.5 %collective-permute-start.13 = (bf16[96,640]{1,0:T(8,128)(2,1)S(1)}, bf16[96,640]{1,0:T(8,128)(2,1)S(1)}, u32[]{:S(2)}, u32[]{:S(2)}) collective-permute-start(bf16[96,640]{1,0:T(8,128)(2,1)S(1)} %get-tuple-element.94), channel_id=1, source_target_pairs={{0,20},{4,16},{8,28},{12,24},{16,4},{20,0},{24,12},{28,8},{1,21},{... | collective-permute-start | bytes 368648 | tf_op jit(solution)/shard_map/ppermute | solution.py:257
  53.4 10.3 %collective-permute-start.16 = (bf16[64,1024]{1,0:T(8,128)(2,1)S(1)}, bf16[64,1024]{1,0:T(8,128)(2,1)S(1)}, u32[]{:S(2)}, u32[]{:S(2)}) collective-permute-start(bf16[64,1024]{1,0:T(8,128)(2,1)S(1)} %get-tuple-element.101), channel_id=1, source_target_pairs={{1,2},{2,1},{5,6},{6,5},{9,10},{10,9},{13,14},{14,13},{17,18},{18,... | collective-permute-start | bytes 393224 | tf_op jit(solution)/shard_map/ppermute | solution.py:287
  55.8 5.2 %collective-permute-start.14 = (bf16[96,640]{1,0:T(8,128)(2,1)S(1)}, bf16[96,640]{1,0:T(8,128)(2,1)S(1)}, u32[]{:S(2)}, u32[]{:S(2)}) collective-permute-start(bf16[96,640]{1,0:T(8,128)(2,1)S(1)} %get-tuple-element.95), channel_id=1, source_target_pairs={{0,12},{4,8},{8,4},{12,0},{16,28},{20,24},{24,20},{28,16},{1,13},{... | collective-permute-start | bytes 368648 | tf_op jit(solution)/shard_map/ppermute | solution.py:257
  58.2 2.8 %collective-permute-start.15 = (bf16[96,640]{1,0:T(8,128)(2,1)S(1)}, bf16[96,640]{1,0:T(8,128)(2,1)S(1)}, u32[]{:S(2)}, u32[]{:S(2)}) collective-permute-start(bf16[96,640]{1,0:T(8,128)(2,1)S(1)} %get-tuple-element.96), channel_id=1, source_target_pairs={{0,4},{4,0},{8,12},{12,8},{16,20},{20,16},{24,28},{28,24},{1,5},{5... | collective-permute-start | bytes 368648 | tf_op jit(solution)/shard_map/ppermute | solution.py:257

commit v15 on v14

--- a/solution.py
+++ b/solution.py
@@ -266,15 +266,21 @@
     sum_ref[cut:, :] = own_ref[cut:, :].astype(F32)
 
 
-def total_kernel(sum_ref, below_ref, cycle_ref, last_ref, in_ref, out_ref):
+def total_kernel(sum_ref, below_ref, cycle_ref, last_ref, in_hbm, out_hbm, in_ref, out_ref, sems):
     piece_d, half = in_ref.shape[0], out_ref.shape[0] // 2
     width = out_ref.shape[1]
     cut = sum_ref.shape[0] - below_ref.shape[0]
-    total = sum_ref[...] + cycle_ref[...].astype(F32) + last_ref[...].astype(F32)
-    total = jnp.concatenate([total[:cut], total[cut:] + below_ref[...].astype(F32)])
-    in_ref[...] = total[:piece_d]
-    out_ref[:half, :] = total[piece_d:, :width]
-    out_ref[half:, :] = total[piece_d:, width:]
+    in_ref[...] = (
+        sum_ref[:piece_d, :] + cycle_ref[:piece_d, :].astype(F32) + last_ref[:piece_d, :].astype(F32)
+    )
+    copies = start_copies([(in_ref, in_hbm)], sems.at[0])
+    total = sum_ref[piece_d:, :] + cycle_ref[piece_d:, :].astype(F32) + last_ref[piece_d:, :].astype(F32)
+    split = cut - piece_d
+    total = jnp.concatenate([total[:split], total[split:] + below_ref[...].astype(F32)])
+    out_ref[:half, :] = total[:, :width]
+    out_ref[half:, :] = total[:, width:]
+    for copy in copies + start_copies([(out_ref, out_hbm)], sems.at[1]):
+        copy.wait()
 
 
 def line_sums(first, second, third, own, upper, lower, width, returned):
@@ -296,16 +302,16 @@
     passed, *rest = lax.optimization_barrier((passed, *returned[ahead:]))
     last = lax.ppermute(passed, "dp", [(0, 1), (3, 2), (1, 3), (2, 0)])
     back += swap_blocks(rest, order[ahead:])
+    ends = (piece_d, hidden), (2 * (rows - piece_d), width)
     sums = kernel_call(
         total_kernel,
         "total",
         1,
         1,
-        [
-            jax.ShapeDtypeStruct((piece_d, hidden), F32),
-            jax.ShapeDtypeStruct((2 * (rows - piece_d), width), F32),
-        ],
+        [jax.ShapeDtypeStruct(end, F32) for end in ends],
         [vmem] * 4,
+        [pltpu.VMEM(end, F32) for end in ends] + [pltpu.SemaphoreType.DMA((2, 1))],
+        places=[hbm] * 2,
     )(most, below, cycle, last)
     return *sums, back
 
@@ -393,7 +399,7 @@
     *sums, soon_gpre, soon_extra = work(sooner_kernel, "sooner", soon_set, sums_shape)
     *sums, next_gpre, next_extra = work(next_kernel, "next", next_set, sums_shape, *sums)
     piece = shape((width // LINE + hidden // LINE // 2, hidden), BF16)
-    cut = 3 * piece.shape[0] // 4
+    cut = 7 * piece.shape[0] // 8
     cut_pieces = [shape((cut, hidden), BF16), shape((piece.shape[0] - cut, hidden), BF16)]
     *parts, late_gpre, late_extra = work(
         later_kernel, "later", late_set, [piece] * LINE + cut_pieces, *sums

time: 70.9 us -> 70.5 us (level)
  starting transfers between devices: 26 us -> 24.8 us
  waiting for transfers between devices: 23.7 us -> 24.8 us
    ppermute x1, waiting for transfers between devices: 5.54 us -> 7.63 us  [line_sums(): last = lax.ppermute(passed, 'dp', [(0, 1), (3, 2), (1, 3), (2, 0)])]
    ppermute x14, starting transfers between devices: 16.4 us -> 15.3 us  [swap_blocks(): lax.ppermute(block, 'space', [(i, i ^ k) for i in devices])]
    ppermute x14, waiting for transfers between devices: 16.5 us -> 15.5 us  [swap_blocks(): lax.ppermute(block, 'space', [(i, i ^ k) for i in devices])]
  transfers between devices with their start and end apart: 19 -> 19, of which waited for: 11 -> 10; matrix products, arithmetic and copies ran while one was open for 0% -> 0% of each run, Pallas kernels for 15% -> 15%
where the time goes in v15:
time: 70.5 us; the launch traced here: 70.2 us
  starting transfers between devices  24.8 us (35%)
  waiting for transfers between devices  24.8 us (35%)
  Pallas kernels  17.7 us (25%)
  local copies, waits for them, and re-layouts  2.06 us (3%)
  between operations  0.84 us (1%)
    ppermute x14, waiting for transfers between devices, swap_blocks(): lax.ppermute(block, 'space', [(i, i ^ k) for i in devices])  15.5 us
    ppermute x14, starting transfers between devices, swap_blocks(): lax.ppermute(block, 'space', [(i, i ^ k) for i in devices])  15.3 us
    ppermute x1, waiting for transfers between devices, line_sums(): last = lax.ppermute(passed, 'dp', [(0, 1), (3, 2), (1, 3), (2, 0)])  7.63 us
    pallas_call x3, Pallas kernels, work(): kernel_call(functools.partial(kernel, count, groups), name, 8 * span * wi...  7.32 us
    pallas_call x1, Pallas kernels, body(): kernel_call(functools.partial(place_kernel, sources, capacity), 'place',...  3.79 us
    ppermute x1, starting transfers between devices, line_sums(): inward = lax.ppermute(first, 'dp', [(0, 1), (3, 2)])  3.66 us
    pallas_call x1, Pallas kernels, body(): kernel_call(finish_kernel, 'finish', 1, 1, [shape((tok_rows, width), BF16...  2.59 us
    ppermute x1, starting transfers between devices, line_sums(): last = lax.ppermute(passed, 'dp', [(0, 1), (3, 2), (1, 3), (2, 0)])  2.53 us
  transfers between devices with their start and end apart: 19, of which 10 were waited for; matrix products, arithmetic and copies ran while one was open for 0% of the time, Pallas kernels for 15%

profile of v15, /device:TPU:0, one launch (start us, length us, event | category | flops | bytes accessed | tf_op | source)
XLA Modules:
  0.0 70.2 jit_solution(2209620540036477433)
XLA Ops:
  0.7 3.8 %place.1 = (s32[1,576]{1,0:T(1,128)}, bf16[96,1024]{1,0:T(8,128)(2,1)}, bf16[96,1024]{1,0:T(8,128)(2,1)}, bf16[96,1024]{1,0:T(8,128)(2,1)}, bf16[96,1024]{1,0:T(8,128)(2,1)}) custom-call(s32[1]{0:T(128)} %bitcast.me, s32[1]{0:T(128)} %bitcast.1.place, s32[1,576]{1,0:T(1,128)} %bitcast.20, bf16[576]{0:T(1024)(128)(2,1)} %gate_ref.3, ...), custom_call_target="tpu_custom_call" | custom-call | flops 452984832 | bytes 2752512 | tf_op jit(solution)/shard_map/place/pallas_call | solution.py:338
  4.5 3.0 %collective-permute-start = (bf16[96,1024]{1,0:T(8,128)(2,1)}, bf16[96,1024]{1,0:T(8,128)(2,1)S(1)}, u32[]{:S(2)}, u32[]{:S(2)}) collective-permute-start(bf16[96,1024]{1,0:T(8,128)(2,1)} %get-tuple-element.56), channel_id=1, source_target_pairs={{0,16},{4,20},{8,24},{12,28},{16,0},{20,4},{24,8},{28,12},{1,17},{... | collective-permute-start | bytes 589832 | tf_op jit(solution)/shard_map/ppermute | solution.py:257
  7.5 1.5 %collective-permute-start.1 = (bf16[96,1024]{1,0:T(8,128)(2,1)}, bf16[96,1024]{1,0:T(8,128)(2,1)S(1)}, u32[]{:S(2)}, u32[]{:S(2)}) collective-permute-start(bf16[96,1024]{1,0:T(8,128)(2,1)} %get-tuple-element.57), channel_id=1, source_target_pairs={{0,8},{4,12},{8,0},{12,4},{16,24},{20,28},{24,16},{28,20},{1,9},{5... | collective-permute-start | bytes 589832 | tf_op jit(solution)/shard_map/ppermute | solution.py:257
  9.1 0.7 copy-done.4
  9.7 0.7 copy-done.6
  10.4 0.7 copy-done.8
  11.1 1.3 %rest.1 = (bf16[96,1024]{1,0:T(8,128)(2,1)S(1)}, bf16[96,1024]{1,0:T(8,128)(2,1)S(1)}, bf16[96,1024]{1,0:T(8,128)(2,1)S(1)}, bf16[96,1024]{1,0:T(8,128)(2,1)S(1)}) custom-call(s32[1,576]{1,0:T(1,128)S(1)} %copy-done.4, bf16[576]{0:T(1024)(128)(2,1)S(1)} %copy-done.6, bf16[576,512]{1,0:T(8,128)(2,1)S(1)} %copy-done.2, f32[1,512]{1,0:T(1,128)S(1)} %bitcast.16, ...), custom_call_target="tpu_custom_call" | custom-call | flops 1 | bytes 1 | tf_op jit(solution)/shard_map/rest/pallas_call | solution.py:359
  12.5 3.0 %collective-permute-start.4 = (bf16[96,1024]{1,0:T(8,128)(2,1)}, bf16[96,1024]{1,0:T(8,128)(2,1)S(1)}, u32[]{:S(2)}, u32[]{:S(2)}) collective-permute-start(bf16[96,1024]{1,0:T(8,128)(2,1)} %get-tuple-element.63), channel_id=1, source_target_pairs={{0,28},{4,24},{8,20},{12,16},{16,12},{20,8},{24,4},{28,0},{1,29},{... | collective-permute-start | bytes 589832 | tf_op jit(solution)/shard_map/ppermute | solution.py:257
  15.9 3.4 %collective-permute-done.2.refs_2_ = bf16[96,1024]{1,0:T(8,128)(2,1)S(1)} collective-permute-done((bf16[96,1024]{1,0:T(8,128)(2,1)}, bf16[96,1024]{1,0:T(8,128)(2,1)S(1)}, u32[]{:S(2)}, u32[]{:S(2)}) %collective-permute-start.2) | collective-permute-done | bytes 196640 | tf_op jit(solution)/shard_map/ppermute | solution.py:257
  19.3 3.2 %sooner.1 = (f32[512,1024]{1,0:T(8,128)S(1)}, f32[1024,512]{1,0:T(8,128)S(1)}, bf16[480,1024]{1,0:T(8,128)(2,1)S(1)}, bf16[480,128]{1,0:T(8,128)(2,1)S(1)}) custom-call(s32[1]{0:T(128)} %bitcast.1.place, bf16[512,1024]{1,0:T(8,128)(2,1)S(1)} %bitcast.8, bf16[1024,512]{1,0:T(8,128)(2,1)S(1)} %bitcast.12, bf16[96,1024]{1,0:T(8,128)(2,1)S(1)} %collective-permute-done.refs_0_, ...), custom_call_target="tpu_custom_call" | custom-call | flops 2013265920 | bytes 6160384 | tf_op jit(solution)/shard_map/sooner/pallas_call | solution.py:388
  22.8 2.0 %next.1 = (f32[512,1024]{1,0:T(8,128)S(1)}, f32[1024,512]{1,0:T(8,128)S(1)}, bf16[96,1024]{1,0:T(8,128)(2,1)S(1)}, bf16[96,128]{1,0:T(8,128)(2,1)S(1)}) custom-call(s32[1]{0:T(128)} %bitcast.1.place, bf16[512,1024]{1,0:T(8,128)(2,1)S(1)} %bitcast.9, bf16[1024,512]{1,0:T(8,128)(2,1)S(1)} %bitcast.13, f32[512,1024]{1,0:T(8,128)S(1)} %get-tuple-element.61.old_in_ref, ...), custom_call_target="tpu_custom_call" | custom-call | flops 402653184 | bytes 4587520 | tf_op jit(solution)/shard_map/next/pallas_call | solution.py:388
  24.7 1.7 %collective-permute-done.5.refs_0_ = bf16[96,1024]{1,0:T(8,128)(2,1)S(1)} collective-permute-done((bf16[96,1024]{1,0:T(8,128)(2,1)S(1)}, bf16[96,1024]{1,0:T(8,128)(2,1)S(1)}, u32[]{:S(2)}, u32[]{:S(2)}) %collective-permute-start.5) | collective-permute-done | bytes 196640 | tf_op jit(solution)/shard_map/ppermute | solution.py:257
  26.5 2.1 %later.1 = (bf16[256,1024]{1,0:T(8,128)(2,1)S(1)}, bf16[256,1024]{1,0:T(8,128)(2,1)S(1)}, bf16[256,1024]{1,0:T(8,128)(2,1)S(1)}, bf16[256,1024]{1,0:T(8,128)(2,1...) custom-call(s32[1]{0:T(128)} %bitcast.1.place, ...), custom_call_target="tpu_custom_call" | custom-call | flops 805306368 | bytes 4980736 | tf_op jit(solution)/shard_map/later/pallas_call | solution.py:388
  28.6 3.7 %collective-permute-start.10 = (bf16[256,1024]{1,0:T(8,128)(2,1)S(1)}, bf16[256,1024]{1,0:T(8,128)(2,1)S(1)}, u32[]{:S(2)}, u32[]{:S(2)}) collective-permute-start(bf16[256,1024]{1,0:T(8,128)(2,1)S(1)} %get-tuple-element.82), channel_id=1, source_target_pairs={{0,1},{3,2},{4,5},{7,6},{8,9},{11,10},{12,13},{15,14},{16,17},{19,... | collective-permute-start | bytes 1572872 | tf_op jit(solution)/shard_map/ppermute | solution.py:291
  32.3 0.7 collective-permute-start.9
  33.0 1.4 %back.1 = (bf16[96,640]{1,0:T(8,128)(2,1)S(1)}, bf16[96,640]{1,0:T(8,128)(2,1)S(1)}, bf16[96,640]{1,0:T(8,128)(2,1)S(1)}, bf16[96,640]{1,0:T(8,128)(2,1)S(1)}, b...) custom-call(bf16[512,1024]{1,0:T(8,128)(2,1)S(1)} %bitcast.11, ...), custom_call_target="tpu_custom_call" | custom-call | flops 1 | bytes 1 | tf_op jit(solution)/shard_map/back/pallas_call | solution.py:407
  34.4 1.6 %collective-permute-start.7 = (bf16[96,640]{1,0:T(8,128)(2,1)S(1)}, bf16[96,640]{1,0:T(8,128)(2,1)S(1)}, u32[]{:S(2)}, u32[]{:S(2)}) collective-permute-start(bf16[96,640]{1,0:T(8,128)(2,1)S(1)} %get-tuple-element.76), channel_id=1, source_target_pairs={{0,16},{4,20},{8,24},{12,28},{16,0},{20,4},{24,8},{28,12},{1,17},{... | collective-permute-start | bytes 368648 | tf_op jit(solution)/shard_map/ppermute | solution.py:257
  35.9 1.5 %collective-permute-start.8 = (bf16[96,640]{1,0:T(8,128)(2,1)S(1)}, bf16[96,640]{1,0:T(8,128)(2,1)S(1)}, u32[]{:S(2)}, u32[]{:S(2)}) collective-permute-start(bf16[96,640]{1,0:T(8,128)(2,1)S(1)} %get-tuple-element.78), channel_id=1, source_target_pairs={{0,8},{4,12},{8,0},{12,4},{16,24},{20,28},{24,16},{28,20},{1,9},{5... | collective-permute-start | bytes 368648 | tf_op jit(solution)/shard_map/ppermute | solution.py:257
  37.4 2.0 %collective-permute-done.7.refs_0_ = bf16[96,640]{1,0:T(8,128)(2,1)S(1)} collective-permute-done((bf16[96,640]{1,0:T(8,128)(2,1)S(1)}, bf16[96,640]{1,0:T(8,128)(2,1)S(1)}, u32[]{:S(2)}, u32[]{:S(2)}) %collective-permute-start.7) | collective-permute-done | bytes 122912 | tf_op jit(solution)/shard_map/ppermute | solution.py:257
  39.5 1.3 %collective-permute-done.8.refs_1_ = bf16[96,640]{1,0:T(8,128)(2,1)S(1)} collective-permute-done((bf16[96,640]{1,0:T(8,128)(2,1)S(1)}, bf16[96,640]{1,0:T(8,128)(2,1)S(1)}, u32[]{:S(2)}, u32[]{:S(2)}) %collective-permute-start.8) | collective-permute-done | bytes 122912 | tf_op jit(solution)/shard_map/ppermute | solution.py:257
  40.8 2.0 %collective-permute-start.17 = (bf16[256,1024]{1,0:T(8,128)(2,1)S(1)}, bf16[256,1024]{1,0:T(8,128)(2,1)S(1)}, u32[]{:S(2)}, u32[]{:S(2)}) collective-permute-start(bf16[256,1024]{1,0:T(8,128)(2,1)S(1)} %get-tuple-element.102), channel_id=1, source_target_pairs={{0,2},{1,0},{2,3},{3,1},{4,6},{5,4},{6,7},{7,5},{8,10},{9,8},{10,1... | collective-permute-start | bytes 1572872 | tf_op jit(solution)/shard_map/ppermute | solution.py:296
  42.9 1.6 %collective-permute-done.10.inward_ref = bf16[256,1024]{1,0:T(8,128)(2,1)S(1)} collective-permute-done((bf16[256,1024]{1,0:T(8,128)(2,1)S(1)}, bf16[256,1024]{1,0:T(8,128)(2,1)S(1)}, u32[]{:S(2)}, u32[]{:S(2)}) %collective-permute-start.10) | collective-permute-done | bytes 524320 | tf_op jit(solution)/shard_map/ppermute | solution.py:291
  44.7 2.5 %collective-permute-start.18 = (bf16[256,1024]{1,0:T(8,128)(2,1)S(1)}, bf16[256,1024]{1,0:T(8,128)(2,1)S(1)}, u32[]{:S(2)}, u32[]{:S(2)}) collective-permute-start(bf16[256,1024]{1,0:T(8,128)(2,1)S(1)} %get-tuple-element.103), channel_id=1, source_target_pairs={{0,1},{3,2},{1,3},{2,0},{4,5},{7,6},{5,7},{6,4},{8,9},{11,10},{9,1... | collective-permute-start | bytes 1572872 | tf_op jit(solution)/shard_map/ppermute | solution.py:303
  47.3 2.4 %collective-permute-start.11 = (bf16[96,640]{1,0:T(8,128)(2,1)S(1)}, bf16[96,640]{1,0:T(8,128)(2,1)S(1)}, u32[]{:S(2)}, u32[]{:S(2)}) collective-permute-start(bf16[96,640]{1,0:T(8,128)(2,1)S(1)} %get-tuple-element.92), channel_id=1, source_target_pairs={{0,24},{4,28},{8,16},{12,20},{16,8},{20,12},{24,0},{28,4},{1,25},{... | collective-permute-start | bytes 368648 | tf_op jit(solution)/shard_map/ppermute | solution.py:257
  49.7 1.7 %collective-permute-start.13 = (bf16[96,640]{1,0:T(8,128)(2,1)S(1)}, bf16[96,640]{1,0:T(8,128)(2,1)S(1)}, u32[]{:S(2)}, u32[]{:S(2)}) collective-permute-start(bf16[96,640]{1,0:T(8,128)(2,1)S(1)} %get-tuple-element.94), channel_id=1, source_target_pairs={{0,20},{4,16},{8,28},{12,24},{16,4},{20,0},{24,12},{28,8},{1,21},{... | collective-permute-start | bytes 368648 | tf_op jit(solution)/shard_map/ppermute | solution.py:257
  51.4 1.9 %collective-permute-done.11.refs_2_ = bf16[96,640]{1,0:T(8,128)(2,1)S(1)} collective-permute-done((bf16[96,640]{1,0:T(8,128)(2,1)S(1)}, bf16[96,640]{1,0:T(8,128)(2,1)S(1)}, u32[]{:S(2)}, u32[]{:S(2)}) %collective-permute-start.11) | collective-permute-done | bytes 122912 | tf_op jit(solution)/shard_map/ppermute | solution.py:257
  53.4 2.4 %collective-permute-done.12.refs_3_ = bf16[96,640]{1,0:T(8,128)(2,1)S(1)} collective-permute-done((bf16[96,640]{1,0:T(8,128)(2,1)S(1)}, bf16[96,640]{1,0:T(8,128)(2,1)S(1)}, u32[]{:S(2)}, u32[]{:S(2)}) %collective-permute-start.12) | collective-permute-done | bytes 122912 | tf_op jit(solution)/shard_map/ppermute | solution.py:257
  55.8 2.5 %collective-permute-done.13.refs_4_ = bf16[96,640]{1,0:T(8,128)(2,1)S(1)} collective-permute-done((bf16[96,640]{1,0:T(8,128)(2,1)S(1)}, bf16[96,640]{1,0:T(8,128)(2,1)S(1)}, u32[]{:S(2)}, u32[]{:S(2)}) %collective-permute-start.13) | collective-permute-done | bytes 122912 | tf_op jit(solution)/shard_map/ppermute | solution.py:257
  58.2 0.7 collective-permute-start.16
  59.0 2.6 %finish.1 = (bf16[576,512]{1,0:T(8,128)(2,1)}, bf16[576]{0:T(1024)(128)(2,1)}) custom-call(s32[1,576]{1,0:T(1,128)S(1)} %copy-done.5, bf16[576]{0:T(1024)(128)(2,1)S(1)} %copy-done.7, bf16[576,512]{1,0:T(8,128)(2,1)S(1)} %copy-done.2, f32[1,512]{1,0:T(1,128)S(1)} %bitcast.17, bf16[576,512]{1,0:T(8,128)(2,1)S(1)} %copy-done.3, ...), custom_call_target="tpu_custom_call" | custom-call | flops 1 | bytes 1 | tf_op jit(solution)/shard_map/finish/pallas_call | solution.py:427
  61.6 7.6 %collective-permute-done.18.last_ref = bf16[256,1024]{1,0:T(8,128)(2,1)S(1)} collective-permute-done((bf16[256,1024]{1,0:T(8,128)(2,1)S(1)}, bf16[256,1024]{1,0:T(8,128)(2,1)S(1)}, u32[]{:S(2)}, u32[]{:S(2)}) %collective-permute-start.18) | collective-permute-done | bytes 524320 | tf_op jit(solution)/shard_map/ppermute | solution.py:303
  69.2 1.1 %total.1 = (f32[128,1024]{1,0:T(8,128)}, f32[256,512]{1,0:T(8,128)}) custom-call(f32[256,1024]{1,0:T(8,128)S(1)} %get-tuple-element.100.sum_ref, bf16[32,1024]{1,0:T(8,128)(2,1)S(1)} %collective-permute-done.16.below_ref, bf16[256,1024]{1,0:T(8,128)(2,1)S(1)} %collective-permute-done.17.cycle_ref, bf16[256,1024]{1,0:T(8,128)(2,1)S(1)} %collective-permute-done.18.last_ref), custom_call_target="tpu_custom_call" | custom-call | flops 1 | bytes 1 | tf_op jit(solution)/shard_map/total/pallas_call | solution.py:306
  (36 shorter events, 1.0 us)
Async XLA Ops:
  0.6 8.4 %copy-start.3 = (bf16[576,512]{1,0:T(8,128)(2,1)S(1)}, bf16[576,512]{1,0:T(8,128)(2,1)}, u32[]{:S(2)}) copy-start(bf16[576,512]{1,0:T(8,128)(2,1)} %go_ref.3) | copy-start | bytes 1769476
  0.6 8.4 %copy-start.2 = (bf16[576,512]{1,0:T(8,128)(2,1)S(1)}, bf16[576,512]{1,0:T(8,128)(2,1)}, u32[]{:S(2)}) copy-start(bf16[576,512]{1,0:T(8,128)(2,1)} %tok_ref.3) | copy-start | bytes 1769476
  0.7 18.7 %copy-start.1 = (bf16[1,1024,512]{2,1,0:T(8,128)(2,1)S(1)}, bf16[1,1024,512]{2,1,0:T(8,128)(2,1)}, u32[]{:S(2)}) copy-start(bf16[1,1024,512]{2,1,0:T(8,128)(2,1)} %param.10) | copy-start | bytes 3145732
  0.7 18.7 %copy-start = (bf16[1,512,1024]{2,1,0:T(8,128)(2,1)S(1)}, bf16[1,512,1024]{2,1,0:T(8,128)(2,1)}, u32[]{:S(2)}) copy-start(bf16[1,512,1024]{2,1,0:T(8,128)(2,1)} %param.9) | copy-start | bytes 3145732
  4.5 11.0 %collective-permute-start = (bf16[96,1024]{1,0:T(8,128)(2,1)}, bf16[96,1024]{1,0:T(8,128)(2,1)S(1)}, u32[]{:S(2)}, u32[]{:S(2)}) collective-permute-start(bf16[96,1024]{1,0:T(8,128)(2,1)} %get-tuple-element.56), channel_id=1, source_target_pairs={{0,16},{4,20},{8,24},{12,28},{16,0},{20,4},{24,8},{28,12},{1,17},{... | collective-permute-start | bytes 589832 | tf_op jit(solution)/shard_map/ppermute | solution.py:257
  7.5 8.2 %collective-permute-start.1 = (bf16[96,1024]{1,0:T(8,128)(2,1)}, bf16[96,1024]{1,0:T(8,128)(2,1)S(1)}, u32[]{:S(2)}, u32[]{:S(2)}) collective-permute-start(bf16[96,1024]{1,0:T(8,128)(2,1)} %get-tuple-element.57), channel_id=1, source_target_pairs={{0,8},{4,12},{8,0},{12,4},{16,24},{20,28},{24,16},{28,20},{1,9},{5... | collective-permute-start | bytes 589832 | tf_op jit(solution)/shard_map/ppermute | solution.py:257
  9.0 10.3 %collective-permute-start.2 = (bf16[96,1024]{1,0:T(8,128)(2,1)}, bf16[96,1024]{1,0:T(8,128)(2,1)S(1)}, u32[]{:S(2)}, u32[]{:S(2)}) collective-permute-start(bf16[96,1024]{1,0:T(8,128)(2,1)} %get-tuple-element.58), channel_id=1, source_target_pairs={{0,24},{4,28},{8,16},{12,20},{16,8},{20,12},{24,0},{28,4},{1,25},{... | collective-permute-start | bytes 589832 | tf_op jit(solution)/shard_map/ppermute | solution.py:257
  9.1 0.7 copy-start.4
  9.7 0.7 copy-start.6
  10.4 0.7 copy-start.8
  12.4 6.9 %collective-permute-start.3 = (bf16[96,1024]{1,0:T(8,128)(2,1)S(1)}, bf16[96,1024]{1,0:T(8,128)(2,1)S(1)}, u32[]{:S(2)}, u32[]{:S(2)}) collective-permute-start(bf16[96,1024]{1,0:T(8,128)(2,1)S(1)} %get-tuple-element.59), channel_id=1, source_target_pairs={{0,4},{4,0},{8,12},{12,8},{16,20},{20,16},{24,28},{28,24},{1,5},{5... | collective-permute-start | bytes 589832 | tf_op jit(solution)/shard_map/ppermute | solution.py:257
  12.5 10.3 %collective-permute-start.4 = (bf16[96,1024]{1,0:T(8,128)(2,1)}, bf16[96,1024]{1,0:T(8,128)(2,1)S(1)}, u32[]{:S(2)}, u32[]{:S(2)}) collective-permute-start(bf16[96,1024]{1,0:T(8,128)(2,1)} %get-tuple-element.63), channel_id=1, source_target_pairs={{0,28},{4,24},{8,20},{12,16},{16,12},{20,8},{24,4},{28,0},{1,29},{... | collective-permute-start | bytes 589832 | tf_op jit(solution)/shard_map/ppermute | solution.py:257
  15.5 11.0 %collective-permute-start.5 = (bf16[96,1024]{1,0:T(8,128)(2,1)S(1)}, bf16[96,1024]{1,0:T(8,128)(2,1)S(1)}, u32[]{:S(2)}, u32[]{:S(2)}) collective-permute-start(bf16[96,1024]{1,0:T(8,128)(2,1)S(1)} %get-tuple-element.66), channel_id=1, source_target_pairs={{0,20},{4,16},{8,28},{12,24},{16,4},{20,0},{24,12},{28,8},{1,21},{... | collective-permute-start | bytes 589832 | tf_op jit(solution)/shard_map/ppermute | solution.py:257
  15.7 10.8 %collective-permute-start.6 = (bf16[96,1024]{1,0:T(8,128)(2,1)S(1)}, bf16[96,1024]{1,0:T(8,128)(2,1)S(1)}, u32[]{:S(2)}, u32[]{:S(2)}) collective-permute-start(bf16[96,1024]{1,0:T(8,128)(2,1)S(1)} %get-tuple-element.67), channel_id=1, source_target_pairs={{0,12},{4,8},{8,4},{12,0},{16,28},{20,24},{24,20},{28,16},{1,13},{... | collective-permute-start | bytes 589832 | tf_op jit(solution)/shard_map/ppermute | solution.py:257
  28.6 15.9 %collective-permute-start.10 = (bf16[256,1024]{1,0:T(8,128)(2,1)S(1)}, bf16[256,1024]{1,0:T(8,128)(2,1)S(1)}, u32[]{:S(2)}, u32[]{:S(2)}) collective-permute-start(bf16[256,1024]{1,0:T(8,128)(2,1)S(1)} %get-tuple-element.82), channel_id=1, source_target_pairs={{0,1},{3,2},{4,5},{7,6},{8,9},{11,10},{12,13},{15,14},{16,17},{19,... | collective-permute-start | bytes 1572872 | tf_op jit(solution)/shard_map/ppermute | solution.py:291
  32.3 10.6 %collective-permute-start.9 = (bf16[224,1024]{1,0:T(8,128)(2,1)S(1)}, bf16[224,1024]{1,0:T(8,128)(2,1)S(1)}, u32[]{:S(2)}, u32[]{:S(2)}) collective-permute-start(bf16[224,1024]{1,0:T(8,128)(2,1)S(1)} %get-tuple-element.81), channel_id=1, source_target_pairs={{1,2},{2,1},{5,6},{6,5},{9,10},{10,9},{13,14},{14,13},{17,18},{18,... | collective-permute-start | bytes 1376264 | tf_op jit(solution)/shard_map/ppermute | solution.py:292
  33.0 26.0 %copy-start.5 = (s32[1,576]{1,0:T(1,128)S(1)}, s32[1,576]{1,0:T(1,128)}, u32[]{:S(2)}) copy-start(s32[1,576]{1,0:T(1,128)} %get-tuple-element.55.target_ref) | copy-start | bytes 6916
  33.0 26.0 %copy-start.7 = (bf16[576]{0:T(1024)(128)(2,1)S(1)}, bf16[576]{0:T(1024)(128)(2,1)}, u32[]{:S(2)}) copy-start(bf16[576]{0:T(1024)(128)(2,1)} %gate_ref.3) | copy-start | bytes 3460
  33.0 26.0 %copy-start.9 = (f32[512]{0:T(512)S(1)}, f32[512]{0:T(512)}, u32[]{:S(2)}) copy-start(f32[512]{0:T(512)} %param.8) | copy-start | bytes 6148
  34.4 5.1 %collective-permute-start.7 = (bf16[96,640]{1,0:T(8,128)(2,1)S(1)}, bf16[96,640]{1,0:T(8,128)(2,1)S(1)}, u32[]{:S(2)}, u32[]{:S(2)}) collective-permute-start(bf16[96,640]{1,0:T(8,128)(2,1)S(1)} %get-tuple-element.76), channel_id=1, source_target_pairs={{0,16},{4,20},{8,24},{12,28},{16,0},{20,4},{24,8},{28,12},{1,17},{... | collective-permute-start | bytes 368648 | tf_op jit(solution)/shard_map/ppermute | solution.py:257
  35.9 4.9 %collective-permute-start.8 = (bf16[96,640]{1,0:T(8,128)(2,1)S(1)}, bf16[96,640]{1,0:T(8,128)(2,1)S(1)}, u32[]{:S(2)}, u32[]{:S(2)}) collective-permute-start(bf16[96,640]{1,0:T(8,128)(2,1)S(1)} %get-tuple-element.78), channel_id=1, source_target_pairs={{0,8},{4,12},{8,0},{12,4},{16,24},{20,28},{24,16},{28,20},{1,9},{5... | collective-permute-start | bytes 368648 | tf_op jit(solution)/shard_map/ppermute | solution.py:257
  40.8 20.7 %collective-permute-start.17 = (bf16[256,1024]{1,0:T(8,128)(2,1)S(1)}, bf16[256,1024]{1,0:T(8,128)(2,1)S(1)}, u32[]{:S(2)}, u32[]{:S(2)}) collective-permute-start(bf16[256,1024]{1,0:T(8,128)(2,1)S(1)} %get-tuple-element.102), channel_id=1, source_target_pairs={{0,2},{1,0},{2,3},{3,1},{4,6},{5,4},{6,7},{7,5},{8,10},{9,8},{10,1... | collective-permute-start | bytes 1572872 | tf_op jit(solution)/shard_map/ppermute | solution.py:296
  44.7 24.4 %collective-permute-start.18 = (bf16[256,1024]{1,0:T(8,128)(2,1)S(1)}, bf16[256,1024]{1,0:T(8,128)(2,1)S(1)}, u32[]{:S(2)}, u32[]{:S(2)}) collective-permute-start(bf16[256,1024]{1,0:T(8,128)(2,1)S(1)} %get-tuple-element.103), channel_id=1, source_target_pairs={{0,1},{3,2},{1,3},{2,0},{4,5},{7,6},{5,7},{6,4},{8,9},{11,10},{9,1... | collective-permute-start | bytes 1572872 | tf_op jit(solution)/shard_map/ppermute | solution.py:303
  47.3 6.1 %collective-permute-start.11 = (bf16[96,640]{1,0:T(8,128)(2,1)S(1)}, bf16[96,640]{1,0:T(8,128)(2,1)S(1)}, u32[]{:S(2)}, u32[]{:S(2)}) collective-permute-start(bf16[96,640]{1,0:T(8,128)(2,1)S(1)} %get-tuple-element.92), channel_id=1, source_target_pairs={{0,24},{4,28},{8,16},{12,20},{16,8},{20,12},{24,0},{28,4},{1,25},{... | collective-permute-start | bytes 368648 | tf_op jit(solution)/shard_map/ppermute | solution.py:257
  49.7 6.1 %collective-permute-start.12 = (bf16[96,640]{1,0:T(8,128)(2,1)S(1)}, bf16[96,640]{1,0:T(8,128)(2,1)S(1)}, u32[]{:S(2)}, u32[]{:S(2)}) collective-permute-start(bf16[96,640]{1,0:T(8,128)(2,1)S(1)} %get-tuple-element.93), channel_id=1, source_target_pairs={{0,28},{4,24},{8,20},{12,16},{16,12},{20,8},{24,4},{28,0},{1,29},{... | collective-permute-start | bytes 368648 | tf_op jit(solution)/shard_map/ppermute | solution.py:257
  49.7 8.5 %collective-permute-start.13 = (bf16[96,640]{1,0:T(8,128)(2,1)S(1)}, bf16[96,640]{1,0:T(8,128)(2,1)S(1)}, u32[]{:S(2)}, u32[]{:S(2)}) collective-permute-start(bf16[96,640]{1,0:T(8,128)(2,1)S(1)} %get-tuple-element.94), channel_id=1, source_target_pairs={{0,20},{4,16},{8,28},{12,24},{16,4},{20,0},{24,12},{28,8},{1,21},{... | collective-permute-start | bytes 368648 | tf_op jit(solution)/shard_map/ppermute | solution.py:257
  53.4 5.5 %collective-permute-start.14 = (bf16[96,640]{1,0:T(8,128)(2,1)S(1)}, bf16[96,640]{1,0:T(8,128)(2,1)S(1)}, u32[]{:S(2)}, u32[]{:S(2)}) collective-permute-start(bf16[96,640]{1,0:T(8,128)(2,1)S(1)} %get-tuple-element.95), channel_id=1, source_target_pairs={{0,12},{4,8},{8,4},{12,0},{16,28},{20,24},{24,20},{28,16},{1,13},{... | collective-permute-start | bytes 368648 | tf_op jit(solution)/shard_map/ppermute | solution.py:257
  55.8 3.1 %collective-permute-start.15 = (bf16[96,640]{1,0:T(8,128)(2,1)S(1)}, bf16[96,640]{1,0:T(8,128)(2,1)S(1)}, u32[]{:S(2)}, u32[]{:S(2)}) collective-permute-start(bf16[96,640]{1,0:T(8,128)(2,1)S(1)} %get-tuple-element.96), channel_id=1, source_target_pairs={{0,4},{4,0},{8,12},{12,8},{16,20},{20,16},{24,28},{28,24},{1,5},{5... | collective-permute-start | bytes 368648 | tf_op jit(solution)/shard_map/ppermute | solution.py:257
  58.2 3.3 %collective-permute-start.16 = (bf16[32,1024]{1,0:T(8,128)(2,1)S(1)}, bf16[32,1024]{1,0:T(8,128)(2,1)S(1)}, u32[]{:S(2)}, u32[]{:S(2)}) collective-permute-start(bf16[32,1024]{1,0:T(8,128)(2,1)S(1)} %get-tuple-element.101), channel_id=1, source_target_pairs={{1,2},{2,1},{5,6},{6,5},{9,10},{10,9},{13,14},{14,13},{17,18},{18,... | collective-permute-start | bytes 196616 | tf_op jit(solution)/shard_map/ppermute | solution.py:293

commit v16 on v15

--- a/solution.py
+++ b/solution.py
@@ -135,8 +135,9 @@
 
 
 def shard_order(place):
-    second = jnp.where(place < 2, 2 - 2 * place, 7 - 2 * place)
-    return [3 - place, second, 3 - second, place]
+    first = jnp.where(lax.rem(place, 2) == 0, 3, 0)
+    second = jnp.where(place < 2, 2, 1)
+    return [first, second, 6 - first - second - place, place]
 
 
 def expert_work(order, blocks, w_in_ref, w_out_ref, gpre_ref, extra_ref, rows_ref, turned_ref, put):
@@ -211,8 +212,8 @@
     order = shard_order(place[0]) if groups == LINE else list(range(LINE))
     expert_work(order, blocks, w_in_ref, w_out_ref, gpre_ref, extra_ref, rows_ref, turned_ref, put)
     cut = upper_ref.shape[0]
-    upper_ref[...] = outs[0][:cut, :]
-    lower_ref[...] = outs[0][cut:, :]
+    upper_ref[...] = outs[1][:cut, :]
+    lower_ref[...] = outs[1][cut:, :]
 
 
 def back_kernel(capacity, sets, w_in_ref, *refs):
@@ -259,48 +260,64 @@
     ]
 
 
-def pass_kernel(above_ref, inward_ref, third_ref, own_ref, out_ref, sum_ref):
+def pass_kernel(
+    place, swapped_ref, above_ref, quarter_ref, third_ref, own_ref, lower_ref, out_ref, sum_ref, on_ref
+):
+    inner = (place[0] == 1) | (place[0] == 2)
     cut = above_ref.shape[0]
-    out_ref[...] = (third_ref[...].astype(F32) + inward_ref[...].astype(F32)).astype(BF16)
-    sum_ref[:cut, :] = own_ref[:cut, :].astype(F32) + above_ref[...].astype(F32)
-    sum_ref[cut:, :] = own_ref[cut:, :].astype(F32)
-
-
-def total_kernel(sum_ref, below_ref, cycle_ref, last_ref, in_hbm, out_hbm, in_ref, out_ref, sems):
+    swapped = swapped_ref[...].astype(F32)
+    out_ref[...] = (third_ref[...].astype(F32) + jnp.where(inner, swapped, 0.0)).astype(BF16)
+    total = own_ref[...].astype(F32) + jnp.where(inner, 0.0, swapped)
+    sum_ref[:cut, :] = total[:cut] + jnp.where(inner, above_ref[...].astype(F32), 0.0)
+    sum_ref[cut:, :] = total[cut:]
+    on_ref[...] = (lower_ref[...].astype(F32) + quarter_ref[...].astype(F32)).astype(BF16)
+
+
+def total_kernel(sum_ref, below_ref, across_ref, last_ref, in_hbm, out_hbm, in_ref, out_ref, sems):
     piece_d, half = in_ref.shape[0], out_ref.shape[0] // 2
     width = out_ref.shape[1]
-    cut = sum_ref.shape[0] - below_ref.shape[0]
-    in_ref[...] = (
-        sum_ref[:piece_d, :] + cycle_ref[:piece_d, :].astype(F32) + last_ref[:piece_d, :].astype(F32)
-    )
+    cut = across_ref.shape[0]
+
+    def part(start, end, more):
+        return sum_ref[start:end, :] + last_ref[start:end, :].astype(F32) + more.astype(F32)
+
+    in_ref[...] = part(0, piece_d, across_ref[:piece_d, :])
     copies = start_copies([(in_ref, in_hbm)], sems.at[0])
-    total = sum_ref[piece_d:, :] + cycle_ref[piece_d:, :].astype(F32) + last_ref[piece_d:, :].astype(F32)
-    split = cut - piece_d
-    total = jnp.concatenate([total[:split], total[split:] + below_ref[...].astype(F32)])
+    total = jnp.concatenate(
+        [part(piece_d, cut, across_ref[piece_d:, :]), part(cut, sum_ref.shape[0], below_ref[...])]
+    )
     out_ref[:half, :] = total[:, :width]
     out_ref[half:, :] = total[:, width:]
     for copy in copies + start_copies([(out_ref, out_hbm)], sems.at[1]):
         copy.wait()
 
 
-def line_sums(first, second, third, own, upper, lower, width, returned):
+def line_sums(place, first, third, own, upper, lower, width, returned):
     rows, hidden = own.shape
     piece_d = width // LINE
-    ahead = len(returned) // 4
+    ahead = 3 * len(returned) // 8
     order = block_order(len(returned))
-    inward = lax.ppermute(first, "dp", [(0, 1), (3, 2)])
+    swap = [(0, 1), (1, 0), (2, 3), (3, 2)]
+    swapped = lax.ppermute(first, "dp", swap)
     above = lax.ppermute(upper, "dp", [(1, 2), (2, 1)])
-    below = lax.ppermute(lower, "dp", [(1, 2), (2, 1)])
+    quarter = lax.ppermute(lower, "dp", swap)
     back = swap_blocks(returned[:ahead], order[:ahead])
-    second, back[0] = lax.optimization_barrier((second, back[0]))
-    cycle = lax.ppermute(second, "dp", [(0, 2), (1, 0), (2, 3), (3, 1)])
+    upper, back[0] = lax.optimization_barrier((upper, back[0]))
+    across = lax.ppermute(upper, "dp", [(0, 2), (3, 1)])
     third, *back = lax.optimization_barrier((third, *back))
     shape = functools.partial(jax.ShapeDtypeStruct, own.shape)
-    passed, most = kernel_call(
-        pass_kernel, "pass", 1, 1, [shape(BF16), shape(F32)], [vmem] * 4
-    )(above, inward, third, own)
+    passed, most, onward = kernel_call(
+        pass_kernel,
+        "pass",
+        1,
+        1,
+        [shape(BF16), shape(F32), jax.ShapeDtypeStruct(lower.shape, BF16)],
+        [smem] + [vmem] * 6,
+    )(place, swapped, above, quarter, third, own, lower)
     passed, *rest = lax.optimization_barrier((passed, *returned[ahead:]))
     last = lax.ppermute(passed, "dp", [(0, 1), (3, 2), (1, 3), (2, 0)])
+    below = lax.ppermute(onward, "dp", [(1, 2), (2, 1)])
+    across, rest[-2] = lax.optimization_barrier((across, rest[-2]))
     back += swap_blocks(rest, order[ahead:])
     ends = (piece_d, hidden), (2 * (rows - piece_d), width)
     sums = kernel_call(
@@ -312,7 +329,7 @@
         [vmem] * 4,
         [pltpu.VMEM(end, F32) for end in ends] + [pltpu.SemaphoreType.DMA((2, 1))],
         places=[hbm] * 2,
-    )(most, below, cycle, last)
+    )(most, below, across, last)
     return *sums, back
 
 
@@ -399,7 +416,7 @@
     *sums, soon_gpre, soon_extra = work(sooner_kernel, "sooner", soon_set, sums_shape)
     *sums, next_gpre, next_extra = work(next_kernel, "next", next_set, sums_shape, *sums)
     piece = shape((width // LINE + hidden // LINE // 2, hidden), BF16)
-    cut = 7 * piece.shape[0] // 8
+    cut = 3 * piece.shape[0] // 4
     cut_pieces = [shape((cut, hidden), BF16), shape((piece.shape[0] - cut, hidden), BF16)]
     *parts, late_gpre, late_extra = work(
         later_kernel, "later", late_set, [piece] * LINE + cut_pieces, *sums
@@ -414,7 +431,9 @@
     )(weight_in, soon_gpre, soon_extra, next_gpre, next_extra, late_gpre, late_extra)
 
     if groups == LINE:
-        grad_w_in, grad_w_out, back = line_sums(*parts, width, returned)
+        grad_w_in, grad_w_out, back = line_sums(
+            place, parts[0], *parts[2:], width, returned
+        )
     else:
         back = swap_blocks(returned, block_order(sources))
         parts_in, parts_out = zip(*[split_piece(part, width, LINE) for part in parts[:LINE]])

time: 70.5 us -> 72.2 us (1.024)
  the two profiles are of different devices: /device:TPU:0 before, /device:TPU:9 now
where the time goes in v16:
time: 72.2 us; the launch traced here: 72 us
  starting transfers between devices  31.2 us (43%)
  waiting for transfers between devices  19.4 us (27%)
  Pallas kernels  18.6 us (26%)
  local copies, waits for them, and re-layouts  2.06 us (3%)
  between operations  0.81 us (1%)
    ppermute x14, starting transfers between devices, swap_blocks(): lax.ppermute(block, 'space', [(i, i ^ k) for i in devices])  21.1 us
    ppermute x14, waiting for transfers between devices, swap_blocks(): lax.ppermute(block, 'space', [(i, i ^ k) for i in devices])  13 us
    pallas_call x3, Pallas kernels, work(): kernel_call(functools.partial(kernel, count, groups), name, 8 * span * wi...  8.06 us
    ppermute x1, waiting for transfers between devices, line_sums(): across = lax.ppermute(upper, 'dp', [(0, 2), (3, 1)])  5.03 us
    ppermute x1, starting transfers between devices, line_sums(): above = lax.ppermute(upper, 'dp', [(1, 2), (2, 1)])  4.49 us
    pallas_call x1, Pallas kernels, body(): kernel_call(functools.partial(place_kernel, sources, capacity), 'place',...  3.79 us
    pallas_call x1, Pallas kernels, body(): kernel_call(finish_kernel, 'finish', 1, 1, [shape((tok_rows, width), BF16...  2.59 us
    ppermute x1, starting transfers between devices, line_sums(): last = lax.ppermute(passed, 'dp', [(0, 1), (3, 2), (1, 3), (2, 0)])  2.38 us
  transfers between devices with their start and end apart: 20, of which 8 were waited for; matrix products, arithmetic and copies ran while one was open for 0% of the time, Pallas kernels for 15%

profile of v16, /device:TPU:9, one launch (start us, length us, event | category | flops | bytes accessed | tf_op | source)
XLA Modules:
  0.0 72.0 jit_solution(15967702663469951119)
XLA Ops:
  0.7 3.8 %place.1 = (s32[1,576]{1,0:T(1,128)}, bf16[96,1024]{1,0:T(8,128)(2,1)}, bf16[96,1024]{1,0:T(8,128)(2,1)}, bf16[96,1024]{1,0:T(8,128)(2,1)}, bf16[96,1024]{1,0:T(8,128)(2,1)}) custom-call(s32[1]{0:T(128)} %bitcast.me, s32[1]{0:T(128)} %bitcast.1.place, s32[1,576]{1,0:T(1,128)} %bitcast.20, bf16[576]{0:T(1024)(128)(2,1)} %gate_ref.3, ...), custom_call_target="tpu_custom_call" | custom-call | flops 452984832 | bytes 2752512 | tf_op jit(solution)/shard_map/place/pallas_call | solution.py:355
  4.5 1.3 %collective-permute-start = (bf16[96,1024]{1,0:T(8,128)(2,1)}, bf16[96,1024]{1,0:T(8,128)(2,1)S(1)}, u32[]{:S(2)}, u32[]{:S(2)}) collective-permute-start(bf16[96,1024]{1,0:T(8,128)(2,1)} %get-tuple-element.58), channel_id=1, source_target_pairs={{0,16},{4,20},{8,24},{12,28},{16,0},{20,4},{24,8},{28,12},{1,17},{... | collective-permute-start | bytes 589832 | tf_op jit(solution)/shard_map/ppermute | solution.py:258
  5.8 1.2 %collective-permute-start.1 = (bf16[96,1024]{1,0:T(8,128)(2,1)}, bf16[96,1024]{1,0:T(8,128)(2,1)S(1)}, u32[]{:S(2)}, u32[]{:S(2)}) collective-permute-start(bf16[96,1024]{1,0:T(8,128)(2,1)} %get-tuple-element.59), channel_id=1, source_target_pairs={{0,8},{4,12},{8,0},{12,4},{16,24},{20,28},{24,16},{28,20},{1,9},{5... | collective-permute-start | bytes 589832 | tf_op jit(solution)/shard_map/ppermute | solution.py:258
  9.2 1.3 %rest.1 = (bf16[96,1024]{1,0:T(8,128)(2,1)S(1)}, bf16[96,1024]{1,0:T(8,128)(2,1)S(1)}, bf16[96,1024]{1,0:T(8,128)(2,1)S(1)}, bf16[96,1024]{1,0:T(8,128)(2,1)S(1)}) custom-call(s32[1,576]{1,0:T(1,128)S(1)} %copy-done.4, bf16[576]{0:T(1024)(128)(2,1)S(1)} %copy-done.6, bf16[576,512]{1,0:T(8,128)(2,1)S(1)} %copy-done.2, f32[1,512]{1,0:T(1,128)S(1)} %bitcast.16, ...), custom_call_target="tpu_custom_call" | custom-call | flops 1 | bytes 1 | tf_op jit(solution)/shard_map/rest/pallas_call | solution.py:376
  10.5 1.6 %collective-permute-start.3 = (bf16[96,1024]{1,0:T(8,128)(2,1)S(1)}, bf16[96,1024]{1,0:T(8,128)(2,1)S(1)}, u32[]{:S(2)}, u32[]{:S(2)}) collective-permute-start(bf16[96,1024]{1,0:T(8,128)(2,1)S(1)} %get-tuple-element.61), channel_id=1, source_target_pairs={{0,4},{4,0},{8,12},{12,8},{16,20},{20,16},{24,28},{28,24},{1,5},{5... | collective-permute-start | bytes 589832 | tf_op jit(solution)/shard_map/ppermute | solution.py:258
  12.1 2.1 %collective-permute-start.4 = (bf16[96,1024]{1,0:T(8,128)(2,1)}, bf16[96,1024]{1,0:T(8,128)(2,1)S(1)}, u32[]{:S(2)}, u32[]{:S(2)}) collective-permute-start(bf16[96,1024]{1,0:T(8,128)(2,1)} %get-tuple-element.65), channel_id=1, source_target_pairs={{0,28},{4,24},{8,20},{12,16},{16,12},{20,8},{24,4},{28,0},{1,29},{... | collective-permute-start | bytes 589832 | tf_op jit(solution)/shard_map/ppermute | solution.py:258
  14.9 1.0 %collective-permute-start.6 = (bf16[96,1024]{1,0:T(8,128)(2,1)S(1)}, bf16[96,1024]{1,0:T(8,128)(2,1)S(1)}, u32[]{:S(2)}, u32[]{:S(2)}) collective-permute-start(bf16[96,1024]{1,0:T(8,128)(2,1)S(1)} %get-tuple-element.69), channel_id=1, source_target_pairs={{0,12},{4,8},{8,4},{12,0},{16,28},{20,24},{24,20},{28,16},{1,13},{... | collective-permute-start | bytes 589832 | tf_op jit(solution)/shard_map/ppermute | solution.py:258
  15.9 3.3 %sooner.1 = (f32[512,1024]{1,0:T(8,128)S(1)}, f32[1024,512]{1,0:T(8,128)S(1)}, bf16[480,1024]{1,0:T(8,128)(2,1)S(1)}, bf16[480,128]{1,0:T(8,128)(2,1)S(1)}) custom-call(s32[1]{0:T(128)} %bitcast.1.place, bf16[512,1024]{1,0:T(8,128)(2,1)S(1)} %bitcast.8, bf16[1024,512]{1,0:T(8,128)(2,1)S(1)} %bitcast.12, bf16[96,1024]{1,0:T(8,128)(2,1)S(1)} %collective-permute-done.refs_0_, ...), custom_call_target="tpu_custom_call" | custom-call | flops 2013265920 | bytes 6160384 | tf_op jit(solution)/shard_map/sooner/pallas_call | solution.py:405
  19.1 3.0 %collective-permute-done.4.refs_0_ = bf16[96,1024]{1,0:T(8,128)(2,1)S(1)} collective-permute-done((bf16[96,1024]{1,0:T(8,128)(2,1)}, bf16[96,1024]{1,0:T(8,128)(2,1)S(1)}, u32[]{:S(2)}, u32[]{:S(2)}) %collective-permute-start.4) | collective-permute-done | bytes 196640 | tf_op jit(solution)/shard_map/ppermute | solution.py:258
  22.1 2.0 %next.1 = (f32[512,1024]{1,0:T(8,128)S(1)}, f32[1024,512]{1,0:T(8,128)S(1)}, bf16[96,1024]{1,0:T(8,128)(2,1)S(1)}, bf16[96,128]{1,0:T(8,128)(2,1)S(1)}) custom-call(s32[1]{0:T(128)} %bitcast.1.place, bf16[512,1024]{1,0:T(8,128)(2,1)S(1)} %bitcast.9, bf16[1024,512]{1,0:T(8,128)(2,1)S(1)} %bitcast.13, f32[512,1024]{1,0:T(8,128)S(1)} %get-tuple-element.63.old_in_ref, ...), custom_call_target="tpu_custom_call" | custom-call | flops 402653184 | bytes 4587520 | tf_op jit(solution)/shard_map/next/pallas_call | solution.py:405
  24.1 1.4 %collective-permute-done.5.refs_0_ = bf16[96,1024]{1,0:T(8,128)(2,1)S(1)} collective-permute-done((bf16[96,1024]{1,0:T(8,128)(2,1)S(1)}, bf16[96,1024]{1,0:T(8,128)(2,1)S(1)}, u32[]{:S(2)}, u32[]{:S(2)}) %collective-permute-start.5) | collective-permute-done | bytes 196640 | tf_op jit(solution)/shard_map/ppermute | solution.py:258
  25.5 2.8 %later.1 = (bf16[256,1024]{1,0:T(8,128)(2,1)S(1)}, bf16[256,1024]{1,0:T(8,128)(2,1)}, bf16[256,1024]{1,0:T(8,128)(2,1)S(1)}, bf16[256,1024]{1,0:T(8,128)(2,1)S(1...) custom-call(s32[1]{0:T(128)} %bitcast.1.place, ...), custom_call_target="tpu_custom_call" | custom-call | flops 805306368 | bytes 4980736 | tf_op jit(solution)/shard_map/later/pallas_call | solution.py:405
  28.3 4.5 %collective-permute-start.11 = (bf16[192,1024]{1,0:T(8,128)(2,1)S(1)}, bf16[192,1024]{1,0:T(8,128)(2,1)S(1)}, u32[]{:S(2)}, u32[]{:S(2)}) collective-permute-start(bf16[192,1024]{1,0:T(8,128)(2,1)S(1)} %get-tuple-element.98), channel_id=1, source_target_pairs={{1,2},{2,1},{5,6},{6,5},{9,10},{10,9},{13,14},{14,13},{17,18},{18,... | collective-permute-start | bytes 1179656 | tf_op jit(solution)/shard_map/ppermute | solution.py:302
  32.8 1.3 %back.1 = (bf16[96,640]{1,0:T(8,128)(2,1)S(1)}, bf16[96,640]{1,0:T(8,128)(2,1)S(1)}, bf16[96,640]{1,0:T(8,128)(2,1)S(1)}, bf16[96,640]{1,0:T(8,128)(2,1)S(1)}, b...) custom-call(bf16[512,1024]{1,0:T(8,128)(2,1)S(1)} %bitcast.11, ...), custom_call_target="tpu_custom_call" | custom-call | flops 1 | bytes 1 | tf_op jit(solution)/shard_map/back/pallas_call | solution.py:424
  34.2 1.3 %collective-permute-start.7 = (bf16[96,640]{1,0:T(8,128)(2,1)S(1)}, bf16[96,640]{1,0:T(8,128)(2,1)S(1)}, u32[]{:S(2)}, u32[]{:S(2)}) collective-permute-start(bf16[96,640]{1,0:T(8,128)(2,1)S(1)} %get-tuple-element.78), channel_id=1, source_target_pairs={{0,16},{4,20},{8,24},{12,28},{16,0},{20,4},{24,8},{28,12},{1,17},{... | collective-permute-start | bytes 368648 | tf_op jit(solution)/shard_map/ppermute | solution.py:258
  35.5 1.2 %collective-permute-start.8 = (bf16[96,640]{1,0:T(8,128)(2,1)S(1)}, bf16[96,640]{1,0:T(8,128)(2,1)S(1)}, u32[]{:S(2)}, u32[]{:S(2)}) collective-permute-start(bf16[96,640]{1,0:T(8,128)(2,1)S(1)} %get-tuple-element.80), channel_id=1, source_target_pairs={{0,8},{4,12},{8,0},{12,4},{16,24},{20,28},{24,16},{28,20},{1,9},{5... | collective-permute-start | bytes 368648 | tf_op jit(solution)/shard_map/ppermute | solution.py:258
  36.7 1.6 %collective-permute-done.7.refs_0_ = bf16[96,640]{1,0:T(8,128)(2,1)S(1)} collective-permute-done((bf16[96,640]{1,0:T(8,128)(2,1)S(1)}, bf16[96,640]{1,0:T(8,128)(2,1)S(1)}, u32[]{:S(2)}, u32[]{:S(2)}) %collective-permute-start.7) | collective-permute-done | bytes 122912 | tf_op jit(solution)/shard_map/ppermute | solution.py:258
  38.3 2.2 %collective-permute-start.9 = (bf16[96,640]{1,0:T(8,128)(2,1)S(1)}, bf16[96,640]{1,0:T(8,128)(2,1)S(1)}, u32[]{:S(2)}, u32[]{:S(2)}) collective-permute-start(bf16[96,640]{1,0:T(8,128)(2,1)S(1)} %get-tuple-element.81), channel_id=1, source_target_pairs={{0,24},{4,28},{8,16},{12,20},{16,8},{20,12},{24,0},{28,4},{1,25},{... | collective-permute-start | bytes 368648 | tf_op jit(solution)/shard_map/ppermute | solution.py:258
  40.5 1.3 %collective-permute-start.16 = (bf16[192,1024]{1,0:T(8,128)(2,1)S(1)}, bf16[192,1024]{1,0:T(8,128)(2,1)S(1)}, u32[]{:S(2)}, u32[]{:S(2)}) collective-permute-start(bf16[192,1024]{1,0:T(8,128)(2,1)S(1)} %get-tuple-element.98), channel_id=1, source_target_pairs={{0,2},{3,1},{4,6},{7,5},{8,10},{11,9},{12,14},{15,13},{16,18},{19,... | collective-permute-start | bytes 1179656 | tf_op jit(solution)/shard_map/ppermute | solution.py:306
  41.7 1.2 %collective-permute-done.9.refs_2_ = bf16[96,640]{1,0:T(8,128)(2,1)S(1)} collective-permute-done((bf16[96,640]{1,0:T(8,128)(2,1)S(1)}, bf16[96,640]{1,0:T(8,128)(2,1)S(1)}, u32[]{:S(2)}, u32[]{:S(2)}) %collective-permute-start.9) | collective-permute-done | bytes 122912 | tf_op jit(solution)/shard_map/ppermute | solution.py:258
  42.9 1.3 %collective-permute-done.12.quarter_ref = bf16[64,1024]{1,0:T(8,128)(2,1)S(1)} collective-permute-done((bf16[64,1024]{1,0:T(8,128)(2,1)S(1)}, bf16[64,1024]{1,0:T(8,128)(2,1)S(1)}, u32[]{:S(2)}, u32[]{:S(2)}) %collective-permute-start.12) | collective-permute-done | bytes 131104 | tf_op jit(solution)/shard_map/ppermute | solution.py:303
  44.6 2.4 %collective-permute-start.19 = (bf16[256,1024]{1,0:T(8,128)(2,1)S(1)}, bf16[256,1024]{1,0:T(8,128)(2,1)S(1)}, u32[]{:S(2)}, u32[]{:S(2)}) collective-permute-start(bf16[256,1024]{1,0:T(8,128)(2,1)S(1)} %get-tuple-element.107), channel_id=1, source_target_pairs={{0,1},{3,2},{1,3},{2,0},{4,5},{7,6},{5,7},{6,4},{8,9},{11,10},{9,1... | collective-permute-start | bytes 1572872 | tf_op jit(solution)/shard_map/ppermute | solution.py:318
  47.0 5.0 %collective-permute-done.16.across_ref = bf16[192,1024]{1,0:T(8,128)(2,1)S(1)} collective-permute-done((bf16[192,1024]{1,0:T(8,128)(2,1)S(1)}, bf16[192,1024]{1,0:T(8,128)(2,1)S(1)}, u32[]{:S(2)}, u32[]{:S(2)}) %collective-permute-start.16) | collective-permute-done | bytes 393248 | tf_op jit(solution)/shard_map/ppermute | solution.py:306
  52.0 5.4 %collective-permute-start.17 = (bf16[96,640]{1,0:T(8,128)(2,1)S(1)}, bf16[96,640]{1,0:T(8,128)(2,1)S(1)}, u32[]{:S(2)}, u32[]{:S(2)}) collective-permute-start(bf16[96,640]{1,0:T(8,128)(2,1)S(1)} %get-tuple-element.100), channel_id=1, source_target_pairs={{0,4},{4,0},{8,12},{12,8},{16,20},{20,16},{24,28},{28,24},{1,5},{5... | collective-permute-start | bytes 368648 | tf_op jit(solution)/shard_map/ppermute | solution.py:258
  57.4 1.9 %collective-permute-start.18 = (bf16[64,1024]{1,0:T(8,128)(2,1)S(1)}, bf16[64,1024]{1,0:T(8,128)(2,1)S(1)}, u32[]{:S(2)}, u32[]{:S(2)}) collective-permute-start(bf16[64,1024]{1,0:T(8,128)(2,1)S(1)} %get-tuple-element.105), channel_id=1, source_target_pairs={{1,2},{2,1},{5,6},{6,5},{9,10},{10,9},{13,14},{14,13},{17,18},{18,... | collective-permute-start | bytes 393224 | tf_op jit(solution)/shard_map/ppermute | solution.py:319
  59.3 0.9 %collective-permute-start.13 = (bf16[96,640]{1,0:T(8,128)(2,1)S(1)}, bf16[96,640]{1,0:T(8,128)(2,1)S(1)}, u32[]{:S(2)}, u32[]{:S(2)}) collective-permute-start(bf16[96,640]{1,0:T(8,128)(2,1)S(1)} %get-tuple-element.95), channel_id=1, source_target_pairs={{0,28},{4,24},{8,20},{12,16},{16,12},{20,8},{24,4},{28,0},{1,29},{... | collective-permute-start | bytes 368648 | tf_op jit(solution)/shard_map/ppermute | solution.py:258
  60.2 0.9 %collective-permute-start.14 = (bf16[96,640]{1,0:T(8,128)(2,1)S(1)}, bf16[96,640]{1,0:T(8,128)(2,1)S(1)}, u32[]{:S(2)}, u32[]{:S(2)}) collective-permute-start(bf16[96,640]{1,0:T(8,128)(2,1)S(1)} %get-tuple-element.96), channel_id=1, source_target_pairs={{0,20},{4,16},{8,28},{12,24},{16,4},{20,0},{24,12},{28,8},{1,21},{... | collective-permute-start | bytes 368648 | tf_op jit(solution)/shard_map/ppermute | solution.py:258
  61.1 1.3 %collective-permute-start.15 = (bf16[96,640]{1,0:T(8,128)(2,1)S(1)}, bf16[96,640]{1,0:T(8,128)(2,1)S(1)}, u32[]{:S(2)}, u32[]{:S(2)}) collective-permute-start(bf16[96,640]{1,0:T(8,128)(2,1)S(1)} %get-tuple-element.97), channel_id=1, source_target_pairs={{0,12},{4,8},{8,4},{12,0},{16,28},{20,24},{24,20},{28,16},{1,13},{... | collective-permute-start | bytes 368648 | tf_op jit(solution)/shard_map/ppermute | solution.py:258
  62.4 3.5 %collective-permute-done.13.refs_3_ = bf16[96,640]{1,0:T(8,128)(2,1)S(1)} collective-permute-done((bf16[96,640]{1,0:T(8,128)(2,1)S(1)}, bf16[96,640]{1,0:T(8,128)(2,1)S(1)}, u32[]{:S(2)}, u32[]{:S(2)}) %collective-permute-start.13) | collective-permute-done | bytes 122912 | tf_op jit(solution)/shard_map/ppermute | solution.py:258
  65.9 2.4 %collective-permute-done.14.refs_4_ = bf16[96,640]{1,0:T(8,128)(2,1)S(1)} collective-permute-done((bf16[96,640]{1,0:T(8,128)(2,1)S(1)}, bf16[96,640]{1,0:T(8,128)(2,1)S(1)}, u32[]{:S(2)}, u32[]{:S(2)}) %collective-permute-start.14) | collective-permute-done | bytes 122912 | tf_op jit(solution)/shard_map/ppermute | solution.py:258
  68.3 2.6 %finish.1 = (bf16[576,512]{1,0:T(8,128)(2,1)}, bf16[576]{0:T(1024)(128)(2,1)}) custom-call(s32[1,576]{1,0:T(1,128)S(1)} %copy-done.5, bf16[576]{0:T(1024)(128)(2,1)S(1)} %copy-done.7, bf16[576,512]{1,0:T(8,128)(2,1)S(1)} %copy-done.2, f32[1,512]{1,0:T(1,128)S(1)} %bitcast.17, bf16[576,512]{1,0:T(8,128)(2,1)S(1)} %copy-done.3, ...), custom_call_target="tpu_custom_call" | custom-call | flops 1 | bytes 1 | tf_op jit(solution)/shard_map/finish/pallas_call | solution.py:446
  70.9 1.1 %total.1 = (f32[128,1024]{1,0:T(8,128)}, f32[256,512]{1,0:T(8,128)}) custom-call(f32[256,1024]{1,0:T(8,128)S(1)} %get-tuple-element.104.sum_ref, bf16[64,1024]{1,0:T(8,128)(2,1)S(1)} %collective-permute-done.18.below_ref, bf16[192,1024]{1,0:T(8,128)(2,1)S(1)} %collective-permute-done.16.across_ref, bf16[256,1024]{1,0:T(8,128)(2,1)S(1)} %collective-permute-done.19.last_ref), custom_call_target="tpu_custom_call" | custom-call | flops 1 | bytes 1 | tf_op jit(solution)/shard_map/total/pallas_call | solution.py:323
  (38 shorter events, 3.4 us)
Async XLA Ops:
  0.6 6.6 %copy-start.3 = (bf16[576,512]{1,0:T(8,128)(2,1)S(1)}, bf16[576,512]{1,0:T(8,128)(2,1)}, u32[]{:S(2)}) copy-start(bf16[576,512]{1,0:T(8,128)(2,1)} %go_ref.3) | copy-start | bytes 1769476
  0.6 6.6 %copy-start.2 = (bf16[576,512]{1,0:T(8,128)(2,1)S(1)}, bf16[576,512]{1,0:T(8,128)(2,1)}, u32[]{:S(2)}) copy-start(bf16[576,512]{1,0:T(8,128)(2,1)} %tok_ref.3) | copy-start | bytes 1769476
  0.7 15.2 %copy-start.1 = (bf16[1,1024,512]{2,1,0:T(8,128)(2,1)S(1)}, bf16[1,1024,512]{2,1,0:T(8,128)(2,1)}, u32[]{:S(2)}) copy-start(bf16[1,1024,512]{2,1,0:T(8,128)(2,1)} %param.10) | copy-start | bytes 3145732
  0.7 15.2 %copy-start = (bf16[1,512,1024]{2,1,0:T(8,128)(2,1)S(1)}, bf16[1,512,1024]{2,1,0:T(8,128)(2,1)}, u32[]{:S(2)}) copy-start(bf16[1,512,1024]{2,1,0:T(8,128)(2,1)} %param.9) | copy-start | bytes 3145732
  4.5 9.8 %collective-permute-start = (bf16[96,1024]{1,0:T(8,128)(2,1)}, bf16[96,1024]{1,0:T(8,128)(2,1)S(1)}, u32[]{:S(2)}, u32[]{:S(2)}) collective-permute-start(bf16[96,1024]{1,0:T(8,128)(2,1)} %get-tuple-element.58), channel_id=1, source_target_pairs={{0,16},{4,20},{8,24},{12,28},{16,0},{20,4},{24,8},{28,12},{1,17},{... | collective-permute-start | bytes 589832 | tf_op jit(solution)/shard_map/ppermute | solution.py:258
  5.8 9.1 %collective-permute-start.1 = (bf16[96,1024]{1,0:T(8,128)(2,1)}, bf16[96,1024]{1,0:T(8,128)(2,1)S(1)}, u32[]{:S(2)}, u32[]{:S(2)}) collective-permute-start(bf16[96,1024]{1,0:T(8,128)(2,1)} %get-tuple-element.59), channel_id=1, source_target_pairs={{0,8},{4,12},{8,0},{12,4},{16,24},{20,28},{24,16},{28,20},{1,9},{5... | collective-permute-start | bytes 589832 | tf_op jit(solution)/shard_map/ppermute | solution.py:258
  7.0 8.9 %collective-permute-start.2 = (bf16[96,1024]{1,0:T(8,128)(2,1)}, bf16[96,1024]{1,0:T(8,128)(2,1)S(1)}, u32[]{:S(2)}, u32[]{:S(2)}) collective-permute-start(bf16[96,1024]{1,0:T(8,128)(2,1)} %get-tuple-element.60), channel_id=1, source_target_pairs={{0,24},{4,28},{8,16},{12,20},{16,8},{20,12},{24,0},{28,4},{1,25},{... | collective-permute-start | bytes 589832 | tf_op jit(solution)/shard_map/ppermute | solution.py:258
  7.2 0.7 copy-start.4
  7.9 0.7 copy-start.6
  8.5 0.7 copy-start.8
  10.5 5.3 %collective-permute-start.3 = (bf16[96,1024]{1,0:T(8,128)(2,1)S(1)}, bf16[96,1024]{1,0:T(8,128)(2,1)S(1)}, u32[]{:S(2)}, u32[]{:S(2)}) collective-permute-start(bf16[96,1024]{1,0:T(8,128)(2,1)S(1)} %get-tuple-element.61), channel_id=1, source_target_pairs={{0,4},{4,0},{8,12},{12,8},{16,20},{20,16},{24,28},{28,24},{1,5},{5... | collective-permute-start | bytes 589832 | tf_op jit(solution)/shard_map/ppermute | solution.py:258
  12.1 10.0 %collective-permute-start.4 = (bf16[96,1024]{1,0:T(8,128)(2,1)}, bf16[96,1024]{1,0:T(8,128)(2,1)S(1)}, u32[]{:S(2)}, u32[]{:S(2)}) collective-permute-start(bf16[96,1024]{1,0:T(8,128)(2,1)} %get-tuple-element.65), channel_id=1, source_target_pairs={{0,28},{4,24},{8,20},{12,16},{16,12},{20,8},{24,4},{28,0},{1,29},{... | collective-permute-start | bytes 589832 | tf_op jit(solution)/shard_map/ppermute | solution.py:258
  14.3 11.2 %collective-permute-start.5 = (bf16[96,1024]{1,0:T(8,128)(2,1)S(1)}, bf16[96,1024]{1,0:T(8,128)(2,1)S(1)}, u32[]{:S(2)}, u32[]{:S(2)}) collective-permute-start(bf16[96,1024]{1,0:T(8,128)(2,1)S(1)} %get-tuple-element.68), channel_id=1, source_target_pairs={{0,20},{4,16},{8,28},{12,24},{16,4},{20,0},{24,12},{28,8},{1,21},{... | collective-permute-start | bytes 589832 | tf_op jit(solution)/shard_map/ppermute | solution.py:258
  14.9 10.6 %collective-permute-start.6 = (bf16[96,1024]{1,0:T(8,128)(2,1)S(1)}, bf16[96,1024]{1,0:T(8,128)(2,1)S(1)}, u32[]{:S(2)}, u32[]{:S(2)}) collective-permute-start(bf16[96,1024]{1,0:T(8,128)(2,1)S(1)} %get-tuple-element.69), channel_id=1, source_target_pairs={{0,12},{4,8},{8,4},{12,0},{16,28},{20,24},{24,20},{28,16},{1,13},{... | collective-permute-start | bytes 589832 | tf_op jit(solution)/shard_map/ppermute | solution.py:258
  28.3 15.9 %collective-permute-start.10 = (bf16[256,1024]{1,0:T(8,128)(2,1)S(1)}, bf16[256,1024]{1,0:T(8,128)(2,1)S(1)}, u32[]{:S(2)}, u32[]{:S(2)}) collective-permute-start(bf16[256,1024]{1,0:T(8,128)(2,1)S(1)} %get-tuple-element.85), channel_id=1, source_target_pairs={{0,1},{1,0},{2,3},{3,2},{4,5},{5,4},{6,7},{7,6},{8,9},{9,8},{10,11... | collective-permute-start | bytes 1572872 | tf_op jit(solution)/shard_map/ppermute | solution.py:301
  28.3 15.9 %collective-permute-start.11 = (bf16[192,1024]{1,0:T(8,128)(2,1)S(1)}, bf16[192,1024]{1,0:T(8,128)(2,1)S(1)}, u32[]{:S(2)}, u32[]{:S(2)}) collective-permute-start(bf16[192,1024]{1,0:T(8,128)(2,1)S(1)} %get-tuple-element.98), channel_id=1, source_target_pairs={{1,2},{2,1},{5,6},{6,5},{9,10},{10,9},{13,14},{14,13},{17,18},{18,... | collective-permute-start | bytes 1179656 | tf_op jit(solution)/shard_map/ppermute | solution.py:302
  32.8 35.5 %copy-start.5 = (s32[1,576]{1,0:T(1,128)S(1)}, s32[1,576]{1,0:T(1,128)}, u32[]{:S(2)}) copy-start(s32[1,576]{1,0:T(1,128)} %get-tuple-element.57.target_ref) | copy-start | bytes 6916
  32.8 35.5 %copy-start.7 = (bf16[576]{0:T(1024)(128)(2,1)S(1)}, bf16[576]{0:T(1024)(128)(2,1)}, u32[]{:S(2)}) copy-start(bf16[576]{0:T(1024)(128)(2,1)} %gate_ref.3) | copy-start | bytes 3460
  32.8 35.5 %copy-start.9 = (f32[512]{0:T(512)S(1)}, f32[512]{0:T(512)}, u32[]{:S(2)}) copy-start(f32[512]{0:T(512)} %param.8) | copy-start | bytes 6148
  34.2 4.1 %collective-permute-start.7 = (bf16[96,640]{1,0:T(8,128)(2,1)S(1)}, bf16[96,640]{1,0:T(8,128)(2,1)S(1)}, u32[]{:S(2)}, u32[]{:S(2)}) collective-permute-start(bf16[96,640]{1,0:T(8,128)(2,1)S(1)} %get-tuple-element.78), channel_id=1, source_target_pairs={{0,16},{4,20},{8,24},{12,28},{16,0},{20,4},{24,8},{28,12},{1,17},{... | collective-permute-start | bytes 368648 | tf_op jit(solution)/shard_map/ppermute | solution.py:258
  35.5 5.0 %collective-permute-start.8 = (bf16[96,640]{1,0:T(8,128)(2,1)S(1)}, bf16[96,640]{1,0:T(8,128)(2,1)S(1)}, u32[]{:S(2)}, u32[]{:S(2)}) collective-permute-start(bf16[96,640]{1,0:T(8,128)(2,1)S(1)} %get-tuple-element.80), channel_id=1, source_target_pairs={{0,8},{4,12},{8,0},{12,4},{16,24},{20,28},{24,16},{28,20},{1,9},{5... | collective-permute-start | bytes 368648 | tf_op jit(solution)/shard_map/ppermute | solution.py:258
  36.7 7.5 %collective-permute-start.12 = (bf16[64,1024]{1,0:T(8,128)(2,1)S(1)}, bf16[64,1024]{1,0:T(8,128)(2,1)S(1)}, u32[]{:S(2)}, u32[]{:S(2)}) collective-permute-start(bf16[64,1024]{1,0:T(8,128)(2,1)S(1)} %get-tuple-element.86.lower_ref), channel_id=1, source_target_pairs={{0,1},{1,0},{2,3},{3,2},{4,5},{5,4},{6,7},{7,6},{8,9},{9,8},{10,11... | collective-permute-start | bytes 393224 | tf_op jit(solution)/shard_map/ppermute | solution.py:303
  38.3 4.6 %collective-permute-start.9 = (bf16[96,640]{1,0:T(8,128)(2,1)S(1)}, bf16[96,640]{1,0:T(8,128)(2,1)S(1)}, u32[]{:S(2)}, u32[]{:S(2)}) collective-permute-start(bf16[96,640]{1,0:T(8,128)(2,1)S(1)} %get-tuple-element.81), channel_id=1, source_target_pairs={{0,24},{4,28},{8,16},{12,20},{16,8},{20,12},{24,0},{28,4},{1,25},{... | collective-permute-start | bytes 368648 | tf_op jit(solution)/shard_map/ppermute | solution.py:258
  40.5 11.6 %collective-permute-start.16 = (bf16[192,1024]{1,0:T(8,128)(2,1)S(1)}, bf16[192,1024]{1,0:T(8,128)(2,1)S(1)}, u32[]{:S(2)}, u32[]{:S(2)}) collective-permute-start(bf16[192,1024]{1,0:T(8,128)(2,1)S(1)} %get-tuple-element.98), channel_id=1, source_target_pairs={{0,2},{3,1},{4,6},{7,5},{8,10},{11,9},{12,14},{15,13},{16,18},{19,... | collective-permute-start | bytes 1179656 | tf_op jit(solution)/shard_map/ppermute | solution.py:306
  44.6 26.3 %collective-permute-start.19 = (bf16[256,1024]{1,0:T(8,128)(2,1)S(1)}, bf16[256,1024]{1,0:T(8,128)(2,1)S(1)}, u32[]{:S(2)}, u32[]{:S(2)}) collective-permute-start(bf16[256,1024]{1,0:T(8,128)(2,1)S(1)} %get-tuple-element.107), channel_id=1, source_target_pairs={{0,1},{3,2},{1,3},{2,0},{4,5},{7,6},{5,7},{6,4},{8,9},{11,10},{9,1... | collective-permute-start | bytes 1572872 | tf_op jit(solution)/shard_map/ppermute | solution.py:318
  52.0 9.1 %collective-permute-start.17 = (bf16[96,640]{1,0:T(8,128)(2,1)S(1)}, bf16[96,640]{1,0:T(8,128)(2,1)S(1)}, u32[]{:S(2)}, u32[]{:S(2)}) collective-permute-start(bf16[96,640]{1,0:T(8,128)(2,1)S(1)} %get-tuple-element.100), channel_id=1, source_target_pairs={{0,4},{4,0},{8,12},{12,8},{16,20},{20,16},{24,28},{28,24},{1,5},{5... | collective-permute-start | bytes 368648 | tf_op jit(solution)/shard_map/ppermute | solution.py:258
  57.4 13.5 %collective-permute-start.18 = (bf16[64,1024]{1,0:T(8,128)(2,1)S(1)}, bf16[64,1024]{1,0:T(8,128)(2,1)S(1)}, u32[]{:S(2)}, u32[]{:S(2)}) collective-permute-start(bf16[64,1024]{1,0:T(8,128)(2,1)S(1)} %get-tuple-element.105), channel_id=1, source_target_pairs={{1,2},{2,1},{5,6},{6,5},{9,10},{10,9},{13,14},{14,13},{17,18},{18,... | collective-permute-start | bytes 393224 | tf_op jit(solution)/shard_map/ppermute | solution.py:319
  59.3 6.6 %collective-permute-start.13 = (bf16[96,640]{1,0:T(8,128)(2,1)S(1)}, bf16[96,640]{1,0:T(8,128)(2,1)S(1)}, u32[]{:S(2)}, u32[]{:S(2)}) collective-permute-start(bf16[96,640]{1,0:T(8,128)(2,1)S(1)} %get-tuple-element.95), channel_id=1, source_target_pairs={{0,28},{4,24},{8,20},{12,16},{16,12},{20,8},{24,4},{28,0},{1,29},{... | collective-permute-start | bytes 368648 | tf_op jit(solution)/shard_map/ppermute | solution.py:258
  60.2 8.1 %collective-permute-start.14 = (bf16[96,640]{1,0:T(8,128)(2,1)S(1)}, bf16[96,640]{1,0:T(8,128)(2,1)S(1)}, u32[]{:S(2)}, u32[]{:S(2)}) collective-permute-start(bf16[96,640]{1,0:T(8,128)(2,1)S(1)} %get-tuple-element.96), channel_id=1, source_target_pairs={{0,20},{4,16},{8,28},{12,24},{16,4},{20,0},{24,12},{28,8},{1,21},{... | collective-permute-start | bytes 368648 | tf_op jit(solution)/shard_map/ppermute | solution.py:258
  61.1 7.2 %collective-permute-start.15 = (bf16[96,640]{1,0:T(8,128)(2,1)S(1)}, bf16[96,640]{1,0:T(8,128)(2,1)S(1)}, u32[]{:S(2)}, u32[]{:S(2)}) collective-permute-start(bf16[96,640]{1,0:T(8,128)(2,1)S(1)} %get-tuple-element.97), channel_id=1, source_target_pairs={{0,12},{4,8},{8,4},{12,0},{16,28},{20,24},{24,20},{28,16},{1,13},{... | collective-permute-start | bytes 368648 | tf_op jit(solution)/shard_map/ppermute | solution.py:258

commit v17 on v16

--- a/solution.py
+++ b/solution.py
@@ -196,8 +196,9 @@
 
 def later_kernel(count, groups, place, w_in_ref, w_out_ref, sum_in_ref, sum_out_ref, *refs):
     blocks = refs[:count]
-    outs = refs[count : count + LINE]
-    upper_ref, lower_ref, gpre_ref, extra_ref, rows_ref, turned_ref = refs[count + LINE :]
+    first_ref, third_ref, own_ref, upper_ref, lower_ref, gpre_ref, extra_ref = refs[count:-3]
+    rows_ref, turned_ref, second_ref = refs[-3:]
+    outs = (first_ref, second_ref, third_ref, own_ref)
     width, hidden = w_in_ref.shape
     piece_d, piece_f = width // LINE, hidden // LINE
 
@@ -212,8 +213,8 @@
     order = shard_order(place[0]) if groups == LINE else list(range(LINE))
     expert_work(order, blocks, w_in_ref, w_out_ref, gpre_ref, extra_ref, rows_ref, turned_ref, put)
     cut = upper_ref.shape[0]
-    upper_ref[...] = outs[1][:cut, :]
-    lower_ref[...] = outs[1][cut:, :]
+    upper_ref[...] = second_ref[:cut, :]
+    lower_ref[...] = second_ref[cut:, :]
 
 
 def back_kernel(capacity, sets, w_in_ref, *refs):
@@ -273,19 +274,20 @@
     on_ref[...] = (lower_ref[...].astype(F32) + quarter_ref[...].astype(F32)).astype(BF16)
 
 
-def total_kernel(sum_ref, below_ref, across_ref, last_ref, in_hbm, out_hbm, in_ref, out_ref, sems):
+def most_kernel(sum_ref, across_ref, out_ref):
+    cut = across_ref.shape[0]
+    out_ref[:cut, :] = sum_ref[:cut, :] + across_ref[...].astype(F32)
+    out_ref[cut:, :] = sum_ref[cut:, :]
+
+
+def total_kernel(sum_ref, below_ref, last_ref, in_hbm, out_hbm, in_ref, out_ref, sems):
     piece_d, half = in_ref.shape[0], out_ref.shape[0] // 2
     width = out_ref.shape[1]
-    cut = across_ref.shape[0]
-
-    def part(start, end, more):
-        return sum_ref[start:end, :] + last_ref[start:end, :].astype(F32) + more.astype(F32)
-
-    in_ref[...] = part(0, piece_d, across_ref[:piece_d, :])
+    split = sum_ref.shape[0] - below_ref.shape[0] - piece_d
+    in_ref[...] = sum_ref[:piece_d, :] + last_ref[:piece_d, :].astype(F32)
     copies = start_copies([(in_ref, in_hbm)], sems.at[0])
-    total = jnp.concatenate(
-        [part(piece_d, cut, across_ref[piece_d:, :]), part(cut, sum_ref.shape[0], below_ref[...])]
-    )
+    total = sum_ref[piece_d:, :] + last_ref[piece_d:, :].astype(F32)
+    total = jnp.concatenate([total[:split], total[split:] + below_ref[...].astype(F32)])
     out_ref[:half, :] = total[:, :width]
     out_ref[half:, :] = total[:, width:]
     for copy in copies + start_copies([(out_ref, out_hbm)], sems.at[1]):
@@ -295,7 +297,7 @@
 def line_sums(place, first, third, own, upper, lower, width, returned):
     rows, hidden = own.shape
     piece_d = width // LINE
-    ahead = 3 * len(returned) // 8
+    ahead = 2 * len(returned) // 8
     order = block_order(len(returned))
     swap = [(0, 1), (1, 0), (2, 3), (3, 2)]
     swapped = lax.ppermute(first, "dp", swap)
@@ -317,8 +319,8 @@
     passed, *rest = lax.optimization_barrier((passed, *returned[ahead:]))
     last = lax.ppermute(passed, "dp", [(0, 1), (3, 2), (1, 3), (2, 0)])
     below = lax.ppermute(onward, "dp", [(1, 2), (2, 1)])
-    across, rest[-2] = lax.optimization_barrier((across, rest[-2]))
     back += swap_blocks(rest, order[ahead:])
+    (most,) = kernel_call(most_kernel, "most", 32 * rows * width * hidden, 1, [shape(F32)], [vmem] * 2)(most, across)
     ends = (piece_d, hidden), (2 * (rows - piece_d), width)
     sums = kernel_call(
         total_kernel,
@@ -326,10 +328,10 @@
         1,
         1,
         [jax.ShapeDtypeStruct(end, F32) for end in ends],
-        [vmem] * 4,
+        [vmem] * 3,
         [pltpu.VMEM(end, F32) for end in ends] + [pltpu.SemaphoreType.DMA((2, 1))],
         places=[hbm] * 2,
-    )(most, below, across, last)
+    )(most, below, last)
     return *sums, back
 
 
@@ -400,7 +402,7 @@
     late_set = list(range(sources // 2, 3 * sources // 4))
     soon_set = [j for j in range(sources) if j not in next_set + late_set]
 
-    def work(kernel, name, members, outs, *sums):
+    def work(kernel, name, members, outs, *sums, scratch=()):
         count, span = len(members), len(members) * capacity
         return kernel_call(
             functools.partial(kernel, count, groups),
@@ -409,7 +411,7 @@
             2 * (2 * span * width + 4 * width * hidden + span * hidden),
             outs + [shape((span, hidden), BF16), shape((span, LANES), BF16)],
             [smem] + [vmem] * (2 + len(sums) + count),
-            [pltpu.VMEM((span, 2 * width), BF16), pltpu.VMEM((width, span), BF16)],
+            [pltpu.VMEM((span, 2 * width), BF16), pltpu.VMEM((width, span), BF16), *scratch],
         )(place, weight_in, weight_out, *sums, *[arrived[j] for j in members])
 
     sums_shape = [shape((width, hidden), F32), shape((hidden, width), F32)]
@@ -419,7 +421,12 @@
     cut = 3 * piece.shape[0] // 4
     cut_pieces = [shape((cut, hidden), BF16), shape((piece.shape[0] - cut, hidden), BF16)]
     *parts, late_gpre, late_extra = work(
-        later_kernel, "later", late_set, [piece] * LINE + cut_pieces, *sums
+        later_kernel,
+        "later",
+        late_set,
+        [piece] * (LINE - 1) + cut_pieces,
+        *sums,
+        scratch=[pltpu.VMEM(piece.shape, BF16)],
     )
     returned = kernel_call(
         functools.partial(back_kernel, capacity, (soon_set, next_set, late_set)),
@@ -432,11 +439,12 @@
 
     if groups == LINE:
         grad_w_in, grad_w_out, back = line_sums(
-            place, parts[0], *parts[2:], width, returned
+            place, *parts, width, returned
         )
     else:
         back = swap_blocks(returned, block_order(sources))
-        parts_in, parts_out = zip(*[split_piece(part, width, LINE) for part in parts[:LINE]])
+        pieces = [parts[0], jnp.concatenate(parts[LINE - 1 :]), *parts[1 : LINE - 1]]
+        parts_in, parts_out = zip(*[split_piece(part, width, LINE) for part in pieces])
         grad_w_in, grad_w_out = (
             lax.psum_scatter(
                 jnp.concatenate(part), "dp", scatter_dimension=0, tiled=True

time: 72.2 us -> 74.5 us (1.032)
  the two profiles are of different devices: /device:TPU:9 before, /device:TPU:0 now
where the time goes in v17:
time: 74.5 us; the launch traced here: 73.8 us
  starting transfers between devices  28.1 us (38%)
  waiting for transfers between devices  24.8 us (33%)
  Pallas kernels  17.9 us (24%)
  local copies, waits for them, and re-layouts  2.06 us (3%)
  between operations  0.83 us (1%)
    ppermute x14, starting transfers between devices, swap_blocks(): lax.ppermute(block, 'space', [(i, i ^ k) for i in devices])  16.7 us
    ppermute x14, waiting for transfers between devices, swap_blocks(): lax.ppermute(block, 'space', [(i, i ^ k) for i in devices])  15.5 us
    pallas_call x3, Pallas kernels, work(): kernel_call(functools.partial(kernel, count, groups), name, 8 * span * wi...  7.32 us
    ppermute x1, starting transfers between devices, line_sums(): across = lax.ppermute(upper, 'dp', [(0, 2), (3, 1)])  5.76 us
    ppermute x1, waiting for transfers between devices, line_sums(): quarter = lax.ppermute(lower, 'dp', swap)  5.25 us
    ppermute x1, waiting for transfers between devices, line_sums(): last = lax.ppermute(passed, 'dp', [(0, 1), (3, 2), (1, 3), (2, 0)])  4.13 us
    pallas_call x1, Pallas kernels, body(): kernel_call(functools.partial(place_kernel, sources, capacity), 'place',...  3.79 us
    pallas_call x1, Pallas kernels, body(): kernel_call(finish_kernel, 'finish', 1, 1, [shape((tok_rows, width), BF16...  2.59 us
  transfers between devices with their start and end apart: 20, of which 10 were waited for; matrix products, arithmetic and copies ran while one was open for 0% of the time, Pallas kernels for 15%

profile of v17, /device:TPU:0, one launch (start us, length us, event | category | flops | bytes accessed | tf_op | source)
XLA Modules:
  0.0 73.8 jit_solution(9958847014898607553)
XLA Ops:
  0.7 3.8 %place.1 = (s32[1,576]{1,0:T(1,128)}, bf16[96,1024]{1,0:T(8,128)(2,1)}, bf16[96,1024]{1,0:T(8,128)(2,1)}, bf16[96,1024]{1,0:T(8,128)(2,1)}, bf16[96,1024]{1,0:T(8,128)(2,1)}) custom-call(s32[1]{0:T(128)} %bitcast.me, s32[1]{0:T(128)} %bitcast.1.place, s32[1,576]{1,0:T(1,128)} %bitcast.20, bf16[576]{0:T(1024)(128)(2,1)} %gate_ref.3, ...), custom_call_target="tpu_custom_call" | custom-call | flops 452984832 | bytes 2752512 | tf_op jit(solution)/shard_map/place/pallas_call | solution.py:357
  4.5 3.0 %collective-permute-start = (bf16[96,1024]{1,0:T(8,128)(2,1)}, bf16[96,1024]{1,0:T(8,128)(2,1)S(1)}, u32[]{:S(2)}, u32[]{:S(2)}) collective-permute-start(bf16[96,1024]{1,0:T(8,128)(2,1)} %get-tuple-element.56), channel_id=1, source_target_pairs={{0,16},{4,20},{8,24},{12,28},{16,0},{20,4},{24,8},{28,12},{1,17},{... | collective-permute-start | bytes 589832 | tf_op jit(solution)/shard_map/ppermute | solution.py:259
  7.5 1.5 %collective-permute-start.1 = (bf16[96,1024]{1,0:T(8,128)(2,1)}, bf16[96,1024]{1,0:T(8,128)(2,1)S(1)}, u32[]{:S(2)}, u32[]{:S(2)}) collective-permute-start(bf16[96,1024]{1,0:T(8,128)(2,1)} %get-tuple-element.57), channel_id=1, source_target_pairs={{0,8},{4,12},{8,0},{12,4},{16,24},{20,28},{24,16},{28,20},{1,9},{5... | collective-permute-start | bytes 589832 | tf_op jit(solution)/shard_map/ppermute | solution.py:259
  9.1 0.7 copy-done.4
  9.7 0.7 copy-done.6
  10.4 0.7 copy-done.8
  11.1 1.3 %rest.1 = (bf16[96,1024]{1,0:T(8,128)(2,1)S(1)}, bf16[96,1024]{1,0:T(8,128)(2,1)S(1)}, bf16[96,1024]{1,0:T(8,128)(2,1)S(1)}, bf16[96,1024]{1,0:T(8,128)(2,1)S(1)}) custom-call(s32[1,576]{1,0:T(1,128)S(1)} %copy-done.4, bf16[576]{0:T(1024)(128)(2,1)S(1)} %copy-done.6, bf16[576,512]{1,0:T(8,128)(2,1)S(1)} %copy-done.2, f32[1,512]{1,0:T(1,128)S(1)} %bitcast.16, ...), custom_call_target="tpu_custom_call" | custom-call | flops 1 | bytes 1 | tf_op jit(solution)/shard_map/rest/pallas_call | solution.py:378
  12.5 3.0 %collective-permute-start.4 = (bf16[96,1024]{1,0:T(8,128)(2,1)}, bf16[96,1024]{1,0:T(8,128)(2,1)S(1)}, u32[]{:S(2)}, u32[]{:S(2)}) collective-permute-start(bf16[96,1024]{1,0:T(8,128)(2,1)} %get-tuple-element.63), channel_id=1, source_target_pairs={{0,28},{4,24},{8,20},{12,16},{16,12},{20,8},{24,4},{28,0},{1,29},{... | collective-permute-start | bytes 589832 | tf_op jit(solution)/shard_map/ppermute | solution.py:259
  15.9 3.4 %collective-permute-done.2.refs_2_ = bf16[96,1024]{1,0:T(8,128)(2,1)S(1)} collective-permute-done((bf16[96,1024]{1,0:T(8,128)(2,1)}, bf16[96,1024]{1,0:T(8,128)(2,1)S(1)}, u32[]{:S(2)}, u32[]{:S(2)}) %collective-permute-start.2) | collective-permute-done | bytes 196640 | tf_op jit(solution)/shard_map/ppermute | solution.py:259
  19.3 3.2 %sooner.1 = (f32[512,1024]{1,0:T(8,128)S(1)}, f32[1024,512]{1,0:T(8,128)S(1)}, bf16[480,1024]{1,0:T(8,128)(2,1)S(1)}, bf16[480,128]{1,0:T(8,128)(2,1)S(1)}) custom-call(s32[1]{0:T(128)} %bitcast.1.place, bf16[512,1024]{1,0:T(8,128)(2,1)S(1)} %bitcast.8, bf16[1024,512]{1,0:T(8,128)(2,1)S(1)} %bitcast.12, bf16[96,1024]{1,0:T(8,128)(2,1)S(1)} %collective-permute-done.refs_0_, ...), custom_call_target="tpu_custom_call" | custom-call | flops 2013265920 | bytes 6160384 | tf_op jit(solution)/shard_map/sooner/pallas_call | solution.py:407
  22.8 2.0 %next.1 = (f32[512,1024]{1,0:T(8,128)S(1)}, f32[1024,512]{1,0:T(8,128)S(1)}, bf16[96,1024]{1,0:T(8,128)(2,1)S(1)}, bf16[96,128]{1,0:T(8,128)(2,1)S(1)}) custom-call(s32[1]{0:T(128)} %bitcast.1.place, bf16[512,1024]{1,0:T(8,128)(2,1)S(1)} %bitcast.9, bf16[1024,512]{1,0:T(8,128)(2,1)S(1)} %bitcast.13, f32[512,1024]{1,0:T(8,128)S(1)} %get-tuple-element.61.old_in_ref, ...), custom_call_target="tpu_custom_call" | custom-call | flops 402653184 | bytes 4587520 | tf_op jit(solution)/shard_map/next/pallas_call | solution.py:407
  24.7 1.7 %collective-permute-done.5.refs_0_ = bf16[96,1024]{1,0:T(8,128)(2,1)S(1)} collective-permute-done((bf16[96,1024]{1,0:T(8,128)(2,1)S(1)}, bf16[96,1024]{1,0:T(8,128)(2,1)S(1)}, u32[]{:S(2)}, u32[]{:S(2)}) %collective-permute-start.5) | collective-permute-done | bytes 196640 | tf_op jit(solution)/shard_map/ppermute | solution.py:259
  26.5 2.1 %later.1 = (bf16[256,1024]{1,0:T(8,128)(2,1)S(1)}, bf16[256,1024]{1,0:T(8,128)(2,1)S(1)}, bf16[256,1024]{1,0:T(8,128)(2,1)S(1)}, bf16[192,1024]{1,0:T(8,128)(2,1...) custom-call(s32[1]{0:T(128)} %bitcast.1.place, ...), custom_call_target="tpu_custom_call" | custom-call | flops 805306368 | bytes 4980736 | tf_op jit(solution)/shard_map/later/pallas_call | solution.py:407
  28.6 1.8 %collective-permute-start.9 = (bf16[256,1024]{1,0:T(8,128)(2,1)S(1)}, bf16[256,1024]{1,0:T(8,128)(2,1)S(1)}, u32[]{:S(2)}, u32[]{:S(2)}) collective-permute-start(bf16[256,1024]{1,0:T(8,128)(2,1)S(1)} %get-tuple-element.81), channel_id=1, source_target_pairs={{0,1},{1,0},{2,3},{3,2},{4,5},{5,4},{6,7},{7,6},{8,9},{9,8},{10,11... | collective-permute-start | bytes 1572872 | tf_op jit(solution)/shard_map/ppermute | solution.py:303
  30.4 0.7 collective-permute-start.10
  31.1 1.3 %back.1 = (bf16[96,640]{1,0:T(8,128)(2,1)S(1)}, bf16[96,640]{1,0:T(8,128)(2,1)S(1)}, bf16[96,640]{1,0:T(8,128)(2,1)S(1)}, bf16[96,640]{1,0:T(8,128)(2,1)S(1)}, b...) custom-call(bf16[512,1024]{1,0:T(8,128)(2,1)S(1)} %bitcast.11, ...), custom_call_target="tpu_custom_call" | custom-call | flops 1 | bytes 1 | tf_op jit(solution)/shard_map/back/pallas_call | solution.py:431
  32.4 1.6 %collective-permute-start.7 = (bf16[96,640]{1,0:T(8,128)(2,1)S(1)}, bf16[96,640]{1,0:T(8,128)(2,1)S(1)}, u32[]{:S(2)}, u32[]{:S(2)}) collective-permute-start(bf16[96,640]{1,0:T(8,128)(2,1)S(1)} %get-tuple-element.76), channel_id=1, source_target_pairs={{0,16},{4,20},{8,24},{12,28},{16,0},{20,4},{24,8},{28,12},{1,17},{... | collective-permute-start | bytes 368648 | tf_op jit(solution)/shard_map/ppermute | solution.py:259
  34.0 3.5 %collective-permute-done.7.refs_0_ = bf16[96,640]{1,0:T(8,128)(2,1)S(1)} collective-permute-done((bf16[96,640]{1,0:T(8,128)(2,1)S(1)}, bf16[96,640]{1,0:T(8,128)(2,1)S(1)}, u32[]{:S(2)}, u32[]{:S(2)}) %collective-permute-start.7) | collective-permute-done | bytes 122912 | tf_op jit(solution)/shard_map/ppermute | solution.py:259
  37.5 5.8 %collective-permute-start.17 = (bf16[192,1024]{1,0:T(8,128)(2,1)S(1)}, bf16[192,1024]{1,0:T(8,128)(2,1)S(1)}, u32[]{:S(2)}, u32[]{:S(2)}) collective-permute-start(bf16[192,1024]{1,0:T(8,128)(2,1)S(1)} %get-tuple-element.101), channel_id=1, source_target_pairs={{0,2},{3,1},{4,6},{7,5},{8,10},{11,9},{12,14},{15,13},{16,18},{19,... | collective-permute-start | bytes 1179656 | tf_op jit(solution)/shard_map/ppermute | solution.py:308
  43.4 1.5 %collective-permute-start.8 = (bf16[96,640]{1,0:T(8,128)(2,1)S(1)}, bf16[96,640]{1,0:T(8,128)(2,1)S(1)}, u32[]{:S(2)}, u32[]{:S(2)}) collective-permute-start(bf16[96,640]{1,0:T(8,128)(2,1)S(1)} %get-tuple-element.78), channel_id=1, source_target_pairs={{0,8},{4,12},{8,0},{12,4},{16,24},{20,28},{24,16},{28,20},{1,9},{5... | collective-permute-start | bytes 368648 | tf_op jit(solution)/shard_map/ppermute | solution.py:259
  44.9 3.4 %collective-permute-done.8.refs_1_ = bf16[96,640]{1,0:T(8,128)(2,1)S(1)} collective-permute-done((bf16[96,640]{1,0:T(8,128)(2,1)S(1)}, bf16[96,640]{1,0:T(8,128)(2,1)S(1)}, u32[]{:S(2)}, u32[]{:S(2)}) %collective-permute-start.8) | collective-permute-done | bytes 122912 | tf_op jit(solution)/shard_map/ppermute | solution.py:259
  48.3 5.2 %collective-permute-done.11.quarter_ref = bf16[64,1024]{1,0:T(8,128)(2,1)S(1)} collective-permute-done((bf16[64,1024]{1,0:T(8,128)(2,1)S(1)}, bf16[64,1024]{1,0:T(8,128)(2,1)S(1)}, u32[]{:S(2)}, u32[]{:S(2)}) %collective-permute-start.11) | collective-permute-done | bytes 131104 | tf_op jit(solution)/shard_map/ppermute | solution.py:305
  54.0 2.5 %collective-permute-start.12 = (bf16[96,640]{1,0:T(8,128)(2,1)S(1)}, bf16[96,640]{1,0:T(8,128)(2,1)S(1)}, u32[]{:S(2)}, u32[]{:S(2)}) collective-permute-start(bf16[96,640]{1,0:T(8,128)(2,1)S(1)} %get-tuple-element.92), channel_id=1, source_target_pairs={{0,24},{4,28},{8,16},{12,20},{16,8},{20,12},{24,0},{28,4},{1,25},{... | collective-permute-start | bytes 368648 | tf_op jit(solution)/shard_map/ppermute | solution.py:259
  56.5 2.5 %collective-permute-start.19 = (bf16[256,1024]{1,0:T(8,128)(2,1)S(1)}, bf16[256,1024]{1,0:T(8,128)(2,1)S(1)}, u32[]{:S(2)}, u32[]{:S(2)}) collective-permute-start(bf16[256,1024]{1,0:T(8,128)(2,1)S(1)} %get-tuple-element.103), channel_id=1, source_target_pairs={{0,1},{3,2},{1,3},{2,0},{4,5},{7,6},{5,7},{6,4},{8,9},{11,10},{9,1... | collective-permute-start | bytes 1572872 | tf_op jit(solution)/shard_map/ppermute | solution.py:320
  59.0 1.4 %collective-permute-start.14 = (bf16[96,640]{1,0:T(8,128)(2,1)S(1)}, bf16[96,640]{1,0:T(8,128)(2,1)S(1)}, u32[]{:S(2)}, u32[]{:S(2)}) collective-permute-start(bf16[96,640]{1,0:T(8,128)(2,1)S(1)} %get-tuple-element.94), channel_id=1, source_target_pairs={{0,20},{4,16},{8,28},{12,24},{16,4},{20,0},{24,12},{28,8},{1,21},{... | collective-permute-start | bytes 368648 | tf_op jit(solution)/shard_map/ppermute | solution.py:259
  60.5 1.6 %collective-permute-start.16 = (bf16[96,640]{1,0:T(8,128)(2,1)S(1)}, bf16[96,640]{1,0:T(8,128)(2,1)S(1)}, u32[]{:S(2)}, u32[]{:S(2)}) collective-permute-start(bf16[96,640]{1,0:T(8,128)(2,1)S(1)} %get-tuple-element.96), channel_id=1, source_target_pairs={{0,4},{4,0},{8,12},{12,8},{16,20},{20,16},{24,28},{28,24},{1,5},{5... | collective-permute-start | bytes 368648 | tf_op jit(solution)/shard_map/ppermute | solution.py:259
  62.5 0.7 collective-permute-start.18
  63.3 1.7 %collective-permute-done.14.refs_4_ = bf16[96,640]{1,0:T(8,128)(2,1)S(1)} collective-permute-done((bf16[96,640]{1,0:T(8,128)(2,1)S(1)}, bf16[96,640]{1,0:T(8,128)(2,1)S(1)}, u32[]{:S(2)}, u32[]{:S(2)}) %collective-permute-start.14) | collective-permute-done | bytes 122912 | tf_op jit(solution)/shard_map/ppermute | solution.py:259
  65.1 0.9 %collective-permute-done.15.refs_5_ = bf16[96,640]{1,0:T(8,128)(2,1)S(1)} collective-permute-done((bf16[96,640]{1,0:T(8,128)(2,1)S(1)}, bf16[96,640]{1,0:T(8,128)(2,1)S(1)}, u32[]{:S(2)}, u32[]{:S(2)}) %collective-permute-start.15) | collective-permute-done | bytes 122912 | tf_op jit(solution)/shard_map/ppermute | solution.py:259
  66.0 2.6 %finish.1 = (bf16[576,512]{1,0:T(8,128)(2,1)}, bf16[576]{0:T(1024)(128)(2,1)}) custom-call(s32[1,576]{1,0:T(1,128)S(1)} %copy-done.5, bf16[576]{0:T(1024)(128)(2,1)S(1)} %copy-done.7, bf16[576,512]{1,0:T(8,128)(2,1)S(1)} %copy-done.2, f32[1,512]{1,0:T(1,128)S(1)} %bitcast.17, bf16[576,512]{1,0:T(8,128)(2,1)S(1)} %copy-done.3, ...), custom_call_target="tpu_custom_call" | custom-call | flops 1 | bytes 1 | tf_op jit(solution)/shard_map/finish/pallas_call | solution.py:454
  68.6 4.1 %collective-permute-done.19.last_ref = bf16[256,1024]{1,0:T(8,128)(2,1)S(1)} collective-permute-done((bf16[256,1024]{1,0:T(8,128)(2,1)S(1)}, bf16[256,1024]{1,0:T(8,128)(2,1)S(1)}, u32[]{:S(2)}, u32[]{:S(2)}) %collective-permute-start.19) | collective-permute-done | bytes 524320 | tf_op jit(solution)/shard_map/ppermute | solution.py:320
  72.8 1.0 %total.1 = (f32[128,1024]{1,0:T(8,128)}, f32[256,512]{1,0:T(8,128)}) custom-call(f32[256,1024]{1,0:T(8,128)S(1)} %most.1.sum_ref, bf16[64,1024]{1,0:T(8,128)(2,1)S(1)} %collective-permute-done.18.below_ref, bf16[256,1024]{1,0:T(8,128)(2,1)S(1)} %collective-permute-done.19.last_ref), custom_call_target="tpu_custom_call" | custom-call | flops 1 | bytes 1 | tf_op jit(solution)/shard_map/total/pallas_call | solution.py:325
  (39 shorter events, 1.9 us)
Async XLA Ops:
  0.6 8.4 %copy-start.3 = (bf16[576,512]{1,0:T(8,128)(2,1)S(1)}, bf16[576,512]{1,0:T(8,128)(2,1)}, u32[]{:S(2)}) copy-start(bf16[576,512]{1,0:T(8,128)(2,1)} %go_ref.3) | copy-start | bytes 1769476
  0.6 8.4 %copy-start.2 = (bf16[576,512]{1,0:T(8,128)(2,1)S(1)}, bf16[576,512]{1,0:T(8,128)(2,1)}, u32[]{:S(2)}) copy-start(bf16[576,512]{1,0:T(8,128)(2,1)} %tok_ref.3) | copy-start | bytes 1769476
  0.7 18.7 %copy-start.1 = (bf16[1,1024,512]{2,1,0:T(8,128)(2,1)S(1)}, bf16[1,1024,512]{2,1,0:T(8,128)(2,1)}, u32[]{:S(2)}) copy-start(bf16[1,1024,512]{2,1,0:T(8,128)(2,1)} %param.10) | copy-start | bytes 3145732
  0.7 18.7 %copy-start = (bf16[1,512,1024]{2,1,0:T(8,128)(2,1)S(1)}, bf16[1,512,1024]{2,1,0:T(8,128)(2,1)}, u32[]{:S(2)}) copy-start(bf16[1,512,1024]{2,1,0:T(8,128)(2,1)} %param.9) | copy-start | bytes 3145732
  4.5 11.0 %collective-permute-start = (bf16[96,1024]{1,0:T(8,128)(2,1)}, bf16[96,1024]{1,0:T(8,128)(2,1)S(1)}, u32[]{:S(2)}, u32[]{:S(2)}) collective-permute-start(bf16[96,1024]{1,0:T(8,128)(2,1)} %get-tuple-element.56), channel_id=1, source_target_pairs={{0,16},{4,20},{8,24},{12,28},{16,0},{20,4},{24,8},{28,12},{1,17},{... | collective-permute-start | bytes 589832 | tf_op jit(solution)/shard_map/ppermute | solution.py:259
  7.5 8.2 %collective-permute-start.1 = (bf16[96,1024]{1,0:T(8,128)(2,1)}, bf16[96,1024]{1,0:T(8,128)(2,1)S(1)}, u32[]{:S(2)}, u32[]{:S(2)}) collective-permute-start(bf16[96,1024]{1,0:T(8,128)(2,1)} %get-tuple-element.57), channel_id=1, source_target_pairs={{0,8},{4,12},{8,0},{12,4},{16,24},{20,28},{24,16},{28,20},{1,9},{5... | collective-permute-start | bytes 589832 | tf_op jit(solution)/shard_map/ppermute | solution.py:259
  9.0 10.3 %collective-permute-start.2 = (bf16[96,1024]{1,0:T(8,128)(2,1)}, bf16[96,1024]{1,0:T(8,128)(2,1)S(1)}, u32[]{:S(2)}, u32[]{:S(2)}) collective-permute-start(bf16[96,1024]{1,0:T(8,128)(2,1)} %get-tuple-element.58), channel_id=1, source_target_pairs={{0,24},{4,28},{8,16},{12,20},{16,8},{20,12},{24,0},{28,4},{1,25},{... | collective-permute-start | bytes 589832 | tf_op jit(solution)/shard_map/ppermute | solution.py:259
  9.1 0.7 copy-start.4
  9.7 0.7 copy-start.6
  10.4 0.7 copy-start.8
  12.4 6.9 %collective-permute-start.3 = (bf16[96,1024]{1,0:T(8,128)(2,1)S(1)}, bf16[96,1024]{1,0:T(8,128)(2,1)S(1)}, u32[]{:S(2)}, u32[]{:S(2)}) collective-permute-start(bf16[96,1024]{1,0:T(8,128)(2,1)S(1)} %get-tuple-element.59), channel_id=1, source_target_pairs={{0,4},{4,0},{8,12},{12,8},{16,20},{20,16},{24,28},{28,24},{1,5},{5... | collective-permute-start | bytes 589832 | tf_op jit(solution)/shard_map/ppermute | solution.py:259
  12.5 10.3 %collective-permute-start.4 = (bf16[96,1024]{1,0:T(8,128)(2,1)}, bf16[96,1024]{1,0:T(8,128)(2,1)S(1)}, u32[]{:S(2)}, u32[]{:S(2)}) collective-permute-start(bf16[96,1024]{1,0:T(8,128)(2,1)} %get-tuple-element.63), channel_id=1, source_target_pairs={{0,28},{4,24},{8,20},{12,16},{16,12},{20,8},{24,4},{28,0},{1,29},{... | collective-permute-start | bytes 589832 | tf_op jit(solution)/shard_map/ppermute | solution.py:259
  15.5 11.0 %collective-permute-start.5 = (bf16[96,1024]{1,0:T(8,128)(2,1)S(1)}, bf16[96,1024]{1,0:T(8,128)(2,1)S(1)}, u32[]{:S(2)}, u32[]{:S(2)}) collective-permute-start(bf16[96,1024]{1,0:T(8,128)(2,1)S(1)} %get-tuple-element.66), channel_id=1, source_target_pairs={{0,20},{4,16},{8,28},{12,24},{16,4},{20,0},{24,12},{28,8},{1,21},{... | collective-permute-start | bytes 589832 | tf_op jit(solution)/shard_map/ppermute | solution.py:259
  15.7 10.7 %collective-permute-start.6 = (bf16[96,1024]{1,0:T(8,128)(2,1)S(1)}, bf16[96,1024]{1,0:T(8,128)(2,1)S(1)}, u32[]{:S(2)}, u32[]{:S(2)}) collective-permute-start(bf16[96,1024]{1,0:T(8,128)(2,1)S(1)} %get-tuple-element.67), channel_id=1, source_target_pairs={{0,12},{4,8},{8,4},{12,0},{16,28},{20,24},{24,20},{28,16},{1,13},{... | collective-permute-start | bytes 589832 | tf_op jit(solution)/shard_map/ppermute | solution.py:259
  28.6 25.0 %collective-permute-start.9 = (bf16[256,1024]{1,0:T(8,128)(2,1)S(1)}, bf16[256,1024]{1,0:T(8,128)(2,1)S(1)}, u32[]{:S(2)}, u32[]{:S(2)}) collective-permute-start(bf16[256,1024]{1,0:T(8,128)(2,1)S(1)} %get-tuple-element.81), channel_id=1, source_target_pairs={{0,1},{1,0},{2,3},{3,2},{4,5},{5,4},{6,7},{7,6},{8,9},{9,8},{10,11... | collective-permute-start | bytes 1572872 | tf_op jit(solution)/shard_map/ppermute | solution.py:303
  30.4 23.2 %collective-permute-start.10 = (bf16[192,1024]{1,0:T(8,128)(2,1)S(1)}, bf16[192,1024]{1,0:T(8,128)(2,1)S(1)}, u32[]{:S(2)}, u32[]{:S(2)}) collective-permute-start(bf16[192,1024]{1,0:T(8,128)(2,1)S(1)} %get-tuple-element.101), channel_id=1, source_target_pairs={{1,2},{2,1},{5,6},{6,5},{9,10},{10,9},{13,14},{14,13},{17,18},{18,... | collective-permute-start | bytes 1179656 | tf_op jit(solution)/shard_map/ppermute | solution.py:304
  32.4 5.1 %collective-permute-start.7 = (bf16[96,640]{1,0:T(8,128)(2,1)S(1)}, bf16[96,640]{1,0:T(8,128)(2,1)S(1)}, u32[]{:S(2)}, u32[]{:S(2)}) collective-permute-start(bf16[96,640]{1,0:T(8,128)(2,1)S(1)} %get-tuple-element.76), channel_id=1, source_target_pairs={{0,16},{4,20},{8,24},{12,28},{16,0},{20,4},{24,8},{28,12},{1,17},{... | collective-permute-start | bytes 368648 | tf_op jit(solution)/shard_map/ppermute | solution.py:259
  37.5 22.9 %collective-permute-start.17 = (bf16[192,1024]{1,0:T(8,128)(2,1)S(1)}, bf16[192,1024]{1,0:T(8,128)(2,1)S(1)}, u32[]{:S(2)}, u32[]{:S(2)}) collective-permute-start(bf16[192,1024]{1,0:T(8,128)(2,1)S(1)} %get-tuple-element.101), channel_id=1, source_target_pairs={{0,2},{3,1},{4,6},{7,5},{8,10},{11,9},{12,14},{15,13},{16,18},{19,... | collective-permute-start | bytes 1179656 | tf_op jit(solution)/shard_map/ppermute | solution.py:308
  43.3 10.3 %collective-permute-start.11 = (bf16[64,1024]{1,0:T(8,128)(2,1)S(1)}, bf16[64,1024]{1,0:T(8,128)(2,1)S(1)}, u32[]{:S(2)}, u32[]{:S(2)}) collective-permute-start(bf16[64,1024]{1,0:T(8,128)(2,1)S(1)} %get-tuple-element.82.lower_ref), channel_id=1, source_target_pairs={{0,1},{1,0},{2,3},{3,2},{4,5},{5,4},{6,7},{7,6},{8,9},{9,8},{10,11... | collective-permute-start | bytes 393224 | tf_op jit(solution)/shard_map/ppermute | solution.py:305
  43.4 4.9 %collective-permute-start.8 = (bf16[96,640]{1,0:T(8,128)(2,1)S(1)}, bf16[96,640]{1,0:T(8,128)(2,1)S(1)}, u32[]{:S(2)}, u32[]{:S(2)}) collective-permute-start(bf16[96,640]{1,0:T(8,128)(2,1)S(1)} %get-tuple-element.78), channel_id=1, source_target_pairs={{0,8},{4,12},{8,0},{12,4},{16,24},{20,28},{24,16},{28,20},{1,9},{5... | collective-permute-start | bytes 368648 | tf_op jit(solution)/shard_map/ppermute | solution.py:259
  54.0 6.4 %collective-permute-start.12 = (bf16[96,640]{1,0:T(8,128)(2,1)S(1)}, bf16[96,640]{1,0:T(8,128)(2,1)S(1)}, u32[]{:S(2)}, u32[]{:S(2)}) collective-permute-start(bf16[96,640]{1,0:T(8,128)(2,1)S(1)} %get-tuple-element.92), channel_id=1, source_target_pairs={{0,24},{4,28},{8,16},{12,20},{16,8},{20,12},{24,0},{28,4},{1,25},{... | collective-permute-start | bytes 368648 | tf_op jit(solution)/shard_map/ppermute | solution.py:259
  56.5 6.0 %collective-permute-start.13 = (bf16[96,640]{1,0:T(8,128)(2,1)S(1)}, bf16[96,640]{1,0:T(8,128)(2,1)S(1)}, u32[]{:S(2)}, u32[]{:S(2)}) collective-permute-start(bf16[96,640]{1,0:T(8,128)(2,1)S(1)} %get-tuple-element.93), channel_id=1, source_target_pairs={{0,28},{4,24},{8,20},{12,16},{16,12},{20,8},{24,4},{28,0},{1,29},{... | collective-permute-start | bytes 368648 | tf_op jit(solution)/shard_map/ppermute | solution.py:259
  56.5 16.2 %collective-permute-start.19 = (bf16[256,1024]{1,0:T(8,128)(2,1)S(1)}, bf16[256,1024]{1,0:T(8,128)(2,1)S(1)}, u32[]{:S(2)}, u32[]{:S(2)}) collective-permute-start(bf16[256,1024]{1,0:T(8,128)(2,1)S(1)} %get-tuple-element.103), channel_id=1, source_target_pairs={{0,1},{3,2},{1,3},{2,0},{4,5},{7,6},{5,7},{6,4},{8,9},{11,10},{9,1... | collective-permute-start | bytes 1572872 | tf_op jit(solution)/shard_map/ppermute | solution.py:320
  59.0 6.1 %collective-permute-start.14 = (bf16[96,640]{1,0:T(8,128)(2,1)S(1)}, bf16[96,640]{1,0:T(8,128)(2,1)S(1)}, u32[]{:S(2)}, u32[]{:S(2)}) collective-permute-start(bf16[96,640]{1,0:T(8,128)(2,1)S(1)} %get-tuple-element.94), channel_id=1, source_target_pairs={{0,20},{4,16},{8,28},{12,24},{16,4},{20,0},{24,12},{28,8},{1,21},{... | collective-permute-start | bytes 368648 | tf_op jit(solution)/shard_map/ppermute | solution.py:259
  60.4 5.6 %collective-permute-start.15 = (bf16[96,640]{1,0:T(8,128)(2,1)S(1)}, bf16[96,640]{1,0:T(8,128)(2,1)S(1)}, u32[]{:S(2)}, u32[]{:S(2)}) collective-permute-start(bf16[96,640]{1,0:T(8,128)(2,1)S(1)} %get-tuple-element.95), channel_id=1, source_target_pairs={{0,12},{4,8},{8,4},{12,0},{16,28},{20,24},{24,20},{28,16},{1,13},{... | collective-permute-start | bytes 368648 | tf_op jit(solution)/shard_map/ppermute | solution.py:259
  60.5 5.6 %collective-permute-start.16 = (bf16[96,640]{1,0:T(8,128)(2,1)S(1)}, bf16[96,640]{1,0:T(8,128)(2,1)S(1)}, u32[]{:S(2)}, u32[]{:S(2)}) collective-permute-start(bf16[96,640]{1,0:T(8,128)(2,1)S(1)} %get-tuple-element.96), channel_id=1, source_target_pairs={{0,4},{4,0},{8,12},{12,8},{16,20},{20,16},{24,28},{28,24},{1,5},{5... | collective-permute-start | bytes 368648 | tf_op jit(solution)/shard_map/ppermute | solution.py:259
  62.5 6.1 %collective-permute-start.18 = (bf16[64,1024]{1,0:T(8,128)(2,1)S(1)}, bf16[64,1024]{1,0:T(8,128)(2,1)S(1)}, u32[]{:S(2)}, u32[]{:S(2)}) collective-permute-start(bf16[64,1024]{1,0:T(8,128)(2,1)S(1)} %get-tuple-element.102), channel_id=1, source_target_pairs={{1,2},{2,1},{5,6},{6,5},{9,10},{10,9},{13,14},{14,13},{17,18},{18,... | collective-permute-start | bytes 393224 | tf_op jit(solution)/shard_map/ppermute | solution.py:321
  63.2 2.8 %copy-start.5 = (s32[1,576]{1,0:T(1,128)S(1)}, s32[1,576]{1,0:T(1,128)}, u32[]{:S(2)}) copy-start(s32[1,576]{1,0:T(1,128)} %get-tuple-element.55.target_ref) | copy-start | bytes 6916
  63.2 2.8 %copy-start.7 = (bf16[576]{0:T(1024)(128)(2,1)S(1)}, bf16[576]{0:T(1024)(128)(2,1)}, u32[]{:S(2)}) copy-start(bf16[576]{0:T(1024)(128)(2,1)} %gate_ref.3) | copy-start | bytes 3460
  63.2 2.8 %copy-start.9 = (f32[512]{0:T(512)S(1)}, f32[512]{0:T(512)}, u32[]{:S(2)}) copy-start(f32[512]{0:T(512)} %param.8) | copy-start | bytes 6148

commit v18 on v17

--- a/solution.py
+++ b/solution.py
@@ -304,7 +304,7 @@
     above = lax.ppermute(upper, "dp", [(1, 2), (2, 1)])
     quarter = lax.ppermute(lower, "dp", swap)
     back = swap_blocks(returned[:ahead], order[:ahead])
-    upper, back[0] = lax.optimization_barrier((upper, back[0]))
+    upper, quarter = lax.optimization_barrier((upper, quarter))
     across = lax.ppermute(upper, "dp", [(0, 2), (3, 1)])
     third, *back = lax.optimization_barrier((third, *back))
     shape = functools.partial(jax.ShapeDtypeStruct, own.shape)

time: 74.5 us -> 77.1 us (1.035)
  waiting for transfers between devices: 24.8 us -> 31.7 us
  starting transfers between devices: 28.1 us -> 23.5 us
    ppermute x1, waiting for transfers between devices: 5.25 us -> 14 us  [line_sums(): quarter = lax.ppermute(lower, 'dp', swap)]
    ppermute x1, starting transfers between devices: 2.48 us -> 0.01 us  [line_sums(): last = lax.ppermute(passed, 'dp', [(0, 1), (3, 2), (1, 3), (2, 0)])]
    ppermute x14, starting transfers between devices: 16.7 us -> 15.4 us  [swap_blocks(): lax.ppermute(block, 'space', [(i, i ^ k) for i in devices])]
    ppermute x1, starting transfers between devices: 5.76 us -> 4.67 us  [line_sums(): across = lax.ppermute(upper, 'dp', [(0, 2), (3, 1)])]
    ppermute x1, waiting for transfers between devices: 4.13 us -> 3.05 us  [line_sums(): last = lax.ppermute(passed, 'dp', [(0, 1), (3, 2), (1, 3), (2, 0)])]
    ppermute x14, waiting for transfers between devices: 15.5 us -> 14.6 us  [swap_blocks(): lax.ppermute(block, 'space', [(i, i ^ k) for i in devices])]
where the time goes in v18:
time: 77.1 us; the launch traced here: 76 us
  waiting for transfers between devices  31.7 us (41%)
  starting transfers between devices  23.5 us (30%)
  Pallas kernels  18 us (23%)
  local copies, waits for them, and re-layouts  2.06 us (3%)
  between operations  0.83 us (1%)
    ppermute x14, starting transfers between devices, swap_blocks(): lax.ppermute(block, 'space', [(i, i ^ k) for i in devices])  15.4 us
    ppermute x14, waiting for transfers between devices, swap_blocks(): lax.ppermute(block, 'space', [(i, i ^ k) for i in devices])  14.6 us
    ppermute x1, waiting for transfers between devices, line_sums(): quarter = lax.ppermute(lower, 'dp', swap)  14 us
    pallas_call x3, Pallas kernels, work(): kernel_call(functools.partial(kernel, count, groups), name, 8 * span * wi...  7.32 us
    ppermute x1, starting transfers between devices, line_sums(): across = lax.ppermute(upper, 'dp', [(0, 2), (3, 1)])  4.67 us
    pallas_call x1, Pallas kernels, body(): kernel_call(functools.partial(place_kernel, sources, capacity), 'place',...  3.79 us
    ppermute x1, waiting for transfers between devices, line_sums(): last = lax.ppermute(passed, 'dp', [(0, 1), (3, 2), (1, 3), (2, 0)])  3.05 us
    pallas_call x1, Pallas kernels, body(): kernel_call(finish_kernel, 'finish', 1, 1, [shape((tok_rows, width), BF16...  2.59 us
  transfers between devices with their start and end apart: 20, of which 10 were waited for; matrix products, arithmetic and copies ran while one was open for 0% of the time, Pallas kernels for 15%

profile of v18, /device:TPU:0, one launch (start us, length us, event | category | flops | bytes accessed | tf_op | source)
XLA Modules:
  0.0 76.0 jit_solution(8598798618337786098)
XLA Ops:
  0.7 3.8 %place.1 = (s32[1,576]{1,0:T(1,128)}, bf16[96,1024]{1,0:T(8,128)(2,1)}, bf16[96,1024]{1,0:T(8,128)(2,1)}, bf16[96,1024]{1,0:T(8,128)(2,1)}, bf16[96,1024]{1,0:T(8,128)(2,1)}) custom-call(s32[1]{0:T(128)} %bitcast.me, s32[1]{0:T(128)} %bitcast.1.place, s32[1,576]{1,0:T(1,128)} %bitcast.20, bf16[576]{0:T(1024)(128)(2,1)} %gate_ref.3, ...), custom_call_target="tpu_custom_call" | custom-call | flops 452984832 | bytes 2752512 | tf_op jit(solution)/shard_map/place/pallas_call | solution.py:357
  4.5 3.0 %collective-permute-start = (bf16[96,1024]{1,0:T(8,128)(2,1)}, bf16[96,1024]{1,0:T(8,128)(2,1)S(1)}, u32[]{:S(2)}, u32[]{:S(2)}) collective-permute-start(bf16[96,1024]{1,0:T(8,128)(2,1)} %get-tuple-element.56), channel_id=1, source_target_pairs={{0,16},{4,20},{8,24},{12,28},{16,0},{20,4},{24,8},{28,12},{1,17},{... | collective-permute-start | bytes 589832 | tf_op jit(solution)/shard_map/ppermute | solution.py:259
  7.5 1.5 %collective-permute-start.1 = (bf16[96,1024]{1,0:T(8,128)(2,1)}, bf16[96,1024]{1,0:T(8,128)(2,1)S(1)}, u32[]{:S(2)}, u32[]{:S(2)}) collective-permute-start(bf16[96,1024]{1,0:T(8,128)(2,1)} %get-tuple-element.57), channel_id=1, source_target_pairs={{0,8},{4,12},{8,0},{12,4},{16,24},{20,28},{24,16},{28,20},{1,9},{5... | collective-permute-start | bytes 589832 | tf_op jit(solution)/shard_map/ppermute | solution.py:259
  9.1 0.7 copy-done.4
  9.7 0.7 copy-done.6
  10.4 0.7 copy-done.8
  11.1 1.3 %rest.1 = (bf16[96,1024]{1,0:T(8,128)(2,1)S(1)}, bf16[96,1024]{1,0:T(8,128)(2,1)S(1)}, bf16[96,1024]{1,0:T(8,128)(2,1)S(1)}, bf16[96,1024]{1,0:T(8,128)(2,1)S(1)}) custom-call(s32[1,576]{1,0:T(1,128)S(1)} %copy-done.4, bf16[576]{0:T(1024)(128)(2,1)S(1)} %copy-done.6, bf16[576,512]{1,0:T(8,128)(2,1)S(1)} %copy-done.2, f32[1,512]{1,0:T(1,128)S(1)} %bitcast.16, ...), custom_call_target="tpu_custom_call" | custom-call | flops 1 | bytes 1 | tf_op jit(solution)/shard_map/rest/pallas_call | solution.py:378
  12.5 3.0 %collective-permute-start.4 = (bf16[96,1024]{1,0:T(8,128)(2,1)}, bf16[96,1024]{1,0:T(8,128)(2,1)S(1)}, u32[]{:S(2)}, u32[]{:S(2)}) collective-permute-start(bf16[96,1024]{1,0:T(8,128)(2,1)} %get-tuple-element.63), channel_id=1, source_target_pairs={{0,28},{4,24},{8,20},{12,16},{16,12},{20,8},{24,4},{28,0},{1,29},{... | collective-permute-start | bytes 589832 | tf_op jit(solution)/shard_map/ppermute | solution.py:259
  15.9 3.4 %collective-permute-done.2.refs_2_ = bf16[96,1024]{1,0:T(8,128)(2,1)S(1)} collective-permute-done((bf16[96,1024]{1,0:T(8,128)(2,1)}, bf16[96,1024]{1,0:T(8,128)(2,1)S(1)}, u32[]{:S(2)}, u32[]{:S(2)}) %collective-permute-start.2) | collective-permute-done | bytes 196640 | tf_op jit(solution)/shard_map/ppermute | solution.py:259
  19.3 3.2 %sooner.1 = (f32[512,1024]{1,0:T(8,128)S(1)}, f32[1024,512]{1,0:T(8,128)S(1)}, bf16[480,1024]{1,0:T(8,128)(2,1)S(1)}, bf16[480,128]{1,0:T(8,128)(2,1)S(1)}) custom-call(s32[1]{0:T(128)} %bitcast.1.place, bf16[512,1024]{1,0:T(8,128)(2,1)S(1)} %bitcast.8, bf16[1024,512]{1,0:T(8,128)(2,1)S(1)} %bitcast.12, bf16[96,1024]{1,0:T(8,128)(2,1)S(1)} %collective-permute-done.refs_0_, ...), custom_call_target="tpu_custom_call" | custom-call | flops 2013265920 | bytes 6160384 | tf_op jit(solution)/shard_map/sooner/pallas_call | solution.py:407
  22.8 2.0 %next.1 = (f32[512,1024]{1,0:T(8,128)S(1)}, f32[1024,512]{1,0:T(8,128)S(1)}, bf16[96,1024]{1,0:T(8,128)(2,1)S(1)}, bf16[96,128]{1,0:T(8,128)(2,1)S(1)}) custom-call(s32[1]{0:T(128)} %bitcast.1.place, bf16[512,1024]{1,0:T(8,128)(2,1)S(1)} %bitcast.9, bf16[1024,512]{1,0:T(8,128)(2,1)S(1)} %bitcast.13, f32[512,1024]{1,0:T(8,128)S(1)} %get-tuple-element.61.old_in_ref, ...), custom_call_target="tpu_custom_call" | custom-call | flops 402653184 | bytes 4587520 | tf_op jit(solution)/shard_map/next/pallas_call | solution.py:407
  24.7 1.7 %collective-permute-done.5.refs_0_ = bf16[96,1024]{1,0:T(8,128)(2,1)S(1)} collective-permute-done((bf16[96,1024]{1,0:T(8,128)(2,1)S(1)}, bf16[96,1024]{1,0:T(8,128)(2,1)S(1)}, u32[]{:S(2)}, u32[]{:S(2)}) %collective-permute-start.5) | collective-permute-done | bytes 196640 | tf_op jit(solution)/shard_map/ppermute | solution.py:259
  26.5 2.1 %later.1 = (bf16[256,1024]{1,0:T(8,128)(2,1)S(1)}, bf16[256,1024]{1,0:T(8,128)(2,1)S(1)}, bf16[256,1024]{1,0:T(8,128)(2,1)S(1)}, bf16[192,1024]{1,0:T(8,128)(2,1...) custom-call(s32[1]{0:T(128)} %bitcast.1.place, ...), custom_call_target="tpu_custom_call" | custom-call | flops 805306368 | bytes 4980736 | tf_op jit(solution)/shard_map/later/pallas_call | solution.py:407
  28.6 1.8 %collective-permute-start.9 = (bf16[256,1024]{1,0:T(8,128)(2,1)S(1)}, bf16[256,1024]{1,0:T(8,128)(2,1)S(1)}, u32[]{:S(2)}, u32[]{:S(2)}) collective-permute-start(bf16[256,1024]{1,0:T(8,128)(2,1)S(1)} %get-tuple-element.79), channel_id=1, source_target_pairs={{0,1},{1,0},{2,3},{3,2},{4,5},{5,4},{6,7},{7,6},{8,9},{9,8},{10,11... | collective-permute-start | bytes 1572872 | tf_op jit(solution)/shard_map/ppermute | solution.py:303
  30.7 0.7 collective-permute-start.10
  31.4 14.0 %collective-permute-done.11.quarter_ref = bf16[64,1024]{1,0:T(8,128)(2,1)S(1)} collective-permute-done((bf16[64,1024]{1,0:T(8,128)(2,1)S(1)}, bf16[64,1024]{1,0:T(8,128)(2,1)S(1)}, u32[]{:S(2)}, u32[]{:S(2)}) %collective-permute-start.11) | collective-permute-done | bytes 131104 | tf_op jit(solution)/shard_map/ppermute | solution.py:305
  45.4 4.7 %collective-permute-start.17 = (bf16[192,1024]{1,0:T(8,128)(2,1)S(1)}, bf16[192,1024]{1,0:T(8,128)(2,1)S(1)}, u32[]{:S(2)}, u32[]{:S(2)}) collective-permute-start(bf16[192,1024]{1,0:T(8,128)(2,1)S(1)} %get-tuple-element.101), channel_id=1, source_target_pairs={{0,2},{3,1},{4,6},{7,5},{8,10},{11,9},{12,14},{15,13},{16,18},{19,... | collective-permute-start | bytes 1179656 | tf_op jit(solution)/shard_map/ppermute | solution.py:308
  50.1 1.3 %back.1 = (bf16[96,640]{1,0:T(8,128)(2,1)S(1)}, bf16[96,640]{1,0:T(8,128)(2,1)S(1)}, bf16[96,640]{1,0:T(8,128)(2,1)S(1)}, bf16[96,640]{1,0:T(8,128)(2,1)S(1)}, b...) custom-call(bf16[512,1024]{1,0:T(8,128)(2,1)S(1)} %bitcast.11, ...), custom_call_target="tpu_custom_call" | custom-call | flops 1 | bytes 1 | tf_op jit(solution)/shard_map/back/pallas_call | solution.py:431
  51.4 1.6 %collective-permute-start.7 = (bf16[96,640]{1,0:T(8,128)(2,1)S(1)}, bf16[96,640]{1,0:T(8,128)(2,1)S(1)}, u32[]{:S(2)}, u32[]{:S(2)}) collective-permute-start(bf16[96,640]{1,0:T(8,128)(2,1)S(1)} %get-tuple-element.75), channel_id=1, source_target_pairs={{0,16},{4,20},{8,24},{12,28},{16,0},{20,4},{24,8},{28,12},{1,17},{... | collective-permute-start | bytes 368648 | tf_op jit(solution)/shard_map/ppermute | solution.py:259
  53.0 1.5 %collective-permute-start.8 = (bf16[96,640]{1,0:T(8,128)(2,1)S(1)}, bf16[96,640]{1,0:T(8,128)(2,1)S(1)}, u32[]{:S(2)}, u32[]{:S(2)}) collective-permute-start(bf16[96,640]{1,0:T(8,128)(2,1)S(1)} %get-tuple-element.76), channel_id=1, source_target_pairs={{0,8},{4,12},{8,0},{12,4},{16,24},{20,28},{24,16},{28,20},{1,9},{5... | collective-permute-start | bytes 368648 | tf_op jit(solution)/shard_map/ppermute | solution.py:259
  54.5 1.9 %collective-permute-done.7.refs_0_ = bf16[96,640]{1,0:T(8,128)(2,1)S(1)} collective-permute-done((bf16[96,640]{1,0:T(8,128)(2,1)S(1)}, bf16[96,640]{1,0:T(8,128)(2,1)S(1)}, u32[]{:S(2)}, u32[]{:S(2)}) %collective-permute-start.7) | collective-permute-done | bytes 122912 | tf_op jit(solution)/shard_map/ppermute | solution.py:259
  56.4 1.5 %collective-permute-done.8.refs_1_ = bf16[96,640]{1,0:T(8,128)(2,1)S(1)} collective-permute-done((bf16[96,640]{1,0:T(8,128)(2,1)S(1)}, bf16[96,640]{1,0:T(8,128)(2,1)S(1)}, u32[]{:S(2)}, u32[]{:S(2)}) %collective-permute-start.8) | collective-permute-done | bytes 122912 | tf_op jit(solution)/shard_map/ppermute | solution.py:259
  58.3 1.5 %collective-permute-start.12 = (bf16[96,640]{1,0:T(8,128)(2,1)S(1)}, bf16[96,640]{1,0:T(8,128)(2,1)S(1)}, u32[]{:S(2)}, u32[]{:S(2)}) collective-permute-start(bf16[96,640]{1,0:T(8,128)(2,1)S(1)} %get-tuple-element.92), channel_id=1, source_target_pairs={{0,24},{4,28},{8,16},{12,20},{16,8},{20,12},{24,0},{28,4},{1,25},{... | collective-permute-start | bytes 368648 | tf_op jit(solution)/shard_map/ppermute | solution.py:259
  59.8 1.7 %collective-permute-start.14 = (bf16[96,640]{1,0:T(8,128)(2,1)S(1)}, bf16[96,640]{1,0:T(8,128)(2,1)S(1)}, u32[]{:S(2)}, u32[]{:S(2)}) collective-permute-start(bf16[96,640]{1,0:T(8,128)(2,1)S(1)} %get-tuple-element.94), channel_id=1, source_target_pairs={{0,20},{4,16},{8,28},{12,24},{16,4},{20,0},{24,12},{28,8},{1,21},{... | collective-permute-start | bytes 368648 | tf_op jit(solution)/shard_map/ppermute | solution.py:259
  61.6 1.1 %collective-permute-start.15 = (bf16[96,640]{1,0:T(8,128)(2,1)S(1)}, bf16[96,640]{1,0:T(8,128)(2,1)S(1)}, u32[]{:S(2)}, u32[]{:S(2)}) collective-permute-start(bf16[96,640]{1,0:T(8,128)(2,1)S(1)} %get-tuple-element.95), channel_id=1, source_target_pairs={{0,12},{4,8},{8,4},{12,0},{16,28},{20,24},{24,20},{28,16},{1,13},{... | collective-permute-start | bytes 368648 | tf_op jit(solution)/shard_map/ppermute | solution.py:259
  62.6 2.1 %collective-permute-done.12.refs_2_ = bf16[96,640]{1,0:T(8,128)(2,1)S(1)} collective-permute-done((bf16[96,640]{1,0:T(8,128)(2,1)S(1)}, bf16[96,640]{1,0:T(8,128)(2,1)S(1)}, u32[]{:S(2)}, u32[]{:S(2)}) %collective-permute-start.12) | collective-permute-done | bytes 122912 | tf_op jit(solution)/shard_map/ppermute | solution.py:259
  64.8 1.7 %collective-permute-done.13.refs_3_ = bf16[96,640]{1,0:T(8,128)(2,1)S(1)} collective-permute-done((bf16[96,640]{1,0:T(8,128)(2,1)S(1)}, bf16[96,640]{1,0:T(8,128)(2,1)S(1)}, u32[]{:S(2)}, u32[]{:S(2)}) %collective-permute-start.13) | collective-permute-done | bytes 122912 | tf_op jit(solution)/shard_map/ppermute | solution.py:259
  66.4 0.7 collective-permute-start.18
  67.2 2.0 %collective-permute-done.14.refs_4_ = bf16[96,640]{1,0:T(8,128)(2,1)S(1)} collective-permute-done((bf16[96,640]{1,0:T(8,128)(2,1)S(1)}, bf16[96,640]{1,0:T(8,128)(2,1)S(1)}, u32[]{:S(2)}, u32[]{:S(2)}) %collective-permute-start.14) | collective-permute-done | bytes 122912 | tf_op jit(solution)/shard_map/ppermute | solution.py:259
  69.3 2.6 %finish.1 = (bf16[576,512]{1,0:T(8,128)(2,1)}, bf16[576]{0:T(1024)(128)(2,1)}) custom-call(s32[1,576]{1,0:T(1,128)S(1)} %copy-done.5, bf16[576]{0:T(1024)(128)(2,1)S(1)} %copy-done.7, bf16[576,512]{1,0:T(8,128)(2,1)S(1)} %copy-done.2, f32[1,512]{1,0:T(1,128)S(1)} %bitcast.17, bf16[576,512]{1,0:T(8,128)(2,1)S(1)} %copy-done.3, ...), custom_call_target="tpu_custom_call" | custom-call | flops 1 | bytes 1 | tf_op jit(solution)/shard_map/finish/pallas_call | solution.py:454
  71.9 3.1 %collective-permute-done.19.last_ref = bf16[256,1024]{1,0:T(8,128)(2,1)S(1)} collective-permute-done((bf16[256,1024]{1,0:T(8,128)(2,1)S(1)}, bf16[256,1024]{1,0:T(8,128)(2,1)S(1)}, u32[]{:S(2)}, u32[]{:S(2)}) %collective-permute-start.19) | collective-permute-done | bytes 524320 | tf_op jit(solution)/shard_map/ppermute | solution.py:320
  74.9 1.0 %total.1 = (f32[128,1024]{1,0:T(8,128)}, f32[256,512]{1,0:T(8,128)}) custom-call(f32[256,1024]{1,0:T(8,128)S(1)} %most.1.sum_ref, bf16[64,1024]{1,0:T(8,128)(2,1)S(1)} %collective-permute-done.18.below_ref, bf16[256,1024]{1,0:T(8,128)(2,1)S(1)} %collective-permute-done.19.last_ref), custom_call_target="tpu_custom_call" | custom-call | flops 1 | bytes 1 | tf_op jit(solution)/shard_map/total/pallas_call | solution.py:325
  (39 shorter events, 1.6 us)
Async XLA Ops:
  0.6 8.4 %copy-start.3 = (bf16[576,512]{1,0:T(8,128)(2,1)S(1)}, bf16[576,512]{1,0:T(8,128)(2,1)}, u32[]{:S(2)}) copy-start(bf16[576,512]{1,0:T(8,128)(2,1)} %go_ref.3) | copy-start | bytes 1769476
  0.6 8.4 %copy-start.2 = (bf16[576,512]{1,0:T(8,128)(2,1)S(1)}, bf16[576,512]{1,0:T(8,128)(2,1)}, u32[]{:S(2)}) copy-start(bf16[576,512]{1,0:T(8,128)(2,1)} %tok_ref.3) | copy-start | bytes 1769476
  0.7 18.7 %copy-start.1 = (bf16[1,1024,512]{2,1,0:T(8,128)(2,1)S(1)}, bf16[1,1024,512]{2,1,0:T(8,128)(2,1)}, u32[]{:S(2)}) copy-start(bf16[1,1024,512]{2,1,0:T(8,128)(2,1)} %param.10) | copy-start | bytes 3145732
  0.7 18.7 %copy-start = (bf16[1,512,1024]{2,1,0:T(8,128)(2,1)S(1)}, bf16[1,512,1024]{2,1,0:T(8,128)(2,1)}, u32[]{:S(2)}) copy-start(bf16[1,512,1024]{2,1,0:T(8,128)(2,1)} %param.9) | copy-start | bytes 3145732
  4.5 11.0 %collective-permute-start = (bf16[96,1024]{1,0:T(8,128)(2,1)}, bf16[96,1024]{1,0:T(8,128)(2,1)S(1)}, u32[]{:S(2)}, u32[]{:S(2)}) collective-permute-start(bf16[96,1024]{1,0:T(8,128)(2,1)} %get-tuple-element.56), channel_id=1, source_target_pairs={{0,16},{4,20},{8,24},{12,28},{16,0},{20,4},{24,8},{28,12},{1,17},{... | collective-permute-start | bytes 589832 | tf_op jit(solution)/shard_map/ppermute | solution.py:259
  7.5 8.2 %collective-permute-start.1 = (bf16[96,1024]{1,0:T(8,128)(2,1)}, bf16[96,1024]{1,0:T(8,128)(2,1)S(1)}, u32[]{:S(2)}, u32[]{:S(2)}) collective-permute-start(bf16[96,1024]{1,0:T(8,128)(2,1)} %get-tuple-element.57), channel_id=1, source_target_pairs={{0,8},{4,12},{8,0},{12,4},{16,24},{20,28},{24,16},{28,20},{1,9},{5... | collective-permute-start | bytes 589832 | tf_op jit(solution)/shard_map/ppermute | solution.py:259
  9.0 10.3 %collective-permute-start.2 = (bf16[96,1024]{1,0:T(8,128)(2,1)}, bf16[96,1024]{1,0:T(8,128)(2,1)S(1)}, u32[]{:S(2)}, u32[]{:S(2)}) collective-permute-start(bf16[96,1024]{1,0:T(8,128)(2,1)} %get-tuple-element.58), channel_id=1, source_target_pairs={{0,24},{4,28},{8,16},{12,20},{16,8},{20,12},{24,0},{28,4},{1,25},{... | collective-permute-start | bytes 589832 | tf_op jit(solution)/shard_map/ppermute | solution.py:259
  9.1 0.7 copy-start.4
  9.7 0.7 copy-start.6
  10.4 0.7 copy-start.8
  12.4 6.9 %collective-permute-start.3 = (bf16[96,1024]{1,0:T(8,128)(2,1)S(1)}, bf16[96,1024]{1,0:T(8,128)(2,1)S(1)}, u32[]{:S(2)}, u32[]{:S(2)}) collective-permute-start(bf16[96,1024]{1,0:T(8,128)(2,1)S(1)} %get-tuple-element.59), channel_id=1, source_target_pairs={{0,4},{4,0},{8,12},{12,8},{16,20},{20,16},{24,28},{28,24},{1,5},{5... | collective-permute-start | bytes 589832 | tf_op jit(solution)/shard_map/ppermute | solution.py:259
  12.5 10.3 %collective-permute-start.4 = (bf16[96,1024]{1,0:T(8,128)(2,1)}, bf16[96,1024]{1,0:T(8,128)(2,1)S(1)}, u32[]{:S(2)}, u32[]{:S(2)}) collective-permute-start(bf16[96,1024]{1,0:T(8,128)(2,1)} %get-tuple-element.63), channel_id=1, source_target_pairs={{0,28},{4,24},{8,20},{12,16},{16,12},{20,8},{24,4},{28,0},{1,29},{... | collective-permute-start | bytes 589832 | tf_op jit(solution)/shard_map/ppermute | solution.py:259
  15.5 11.0 %collective-permute-start.5 = (bf16[96,1024]{1,0:T(8,128)(2,1)S(1)}, bf16[96,1024]{1,0:T(8,128)(2,1)S(1)}, u32[]{:S(2)}, u32[]{:S(2)}) collective-permute-start(bf16[96,1024]{1,0:T(8,128)(2,1)S(1)} %get-tuple-element.66), channel_id=1, source_target_pairs={{0,20},{4,16},{8,28},{12,24},{16,4},{20,0},{24,12},{28,8},{1,21},{... | collective-permute-start | bytes 589832 | tf_op jit(solution)/shard_map/ppermute | solution.py:259
  15.7 10.7 %collective-permute-start.6 = (bf16[96,1024]{1,0:T(8,128)(2,1)S(1)}, bf16[96,1024]{1,0:T(8,128)(2,1)S(1)}, u32[]{:S(2)}, u32[]{:S(2)}) collective-permute-start(bf16[96,1024]{1,0:T(8,128)(2,1)S(1)} %get-tuple-element.67), channel_id=1, source_target_pairs={{0,12},{4,8},{8,4},{12,0},{16,28},{20,24},{24,20},{28,16},{1,13},{... | collective-permute-start | bytes 589832 | tf_op jit(solution)/shard_map/ppermute | solution.py:259
  28.6 29.3 %collective-permute-start.9 = (bf16[256,1024]{1,0:T(8,128)(2,1)S(1)}, bf16[256,1024]{1,0:T(8,128)(2,1)S(1)}, u32[]{:S(2)}, u32[]{:S(2)}) collective-permute-start(bf16[256,1024]{1,0:T(8,128)(2,1)S(1)} %get-tuple-element.79), channel_id=1, source_target_pairs={{0,1},{1,0},{2,3},{3,2},{4,5},{5,4},{6,7},{7,6},{8,9},{9,8},{10,11... | collective-permute-start | bytes 1572872 | tf_op jit(solution)/shard_map/ppermute | solution.py:303
  30.4 15.0 %collective-permute-start.11 = (bf16[64,1024]{1,0:T(8,128)(2,1)S(1)}, bf16[64,1024]{1,0:T(8,128)(2,1)S(1)}, u32[]{:S(2)}, u32[]{:S(2)}) collective-permute-start(bf16[64,1024]{1,0:T(8,128)(2,1)S(1)} %get-tuple-element.81.lower_ref), channel_id=1, source_target_pairs={{0,1},{1,0},{2,3},{3,2},{4,5},{5,4},{6,7},{7,6},{8,9},{9,8},{10,11... | collective-permute-start | bytes 393224 | tf_op jit(solution)/shard_map/ppermute | solution.py:305
  30.7 27.2 %collective-permute-start.10 = (bf16[192,1024]{1,0:T(8,128)(2,1)S(1)}, bf16[192,1024]{1,0:T(8,128)(2,1)S(1)}, u32[]{:S(2)}, u32[]{:S(2)}) collective-permute-start(bf16[192,1024]{1,0:T(8,128)(2,1)S(1)} %get-tuple-element.101), channel_id=1, source_target_pairs={{1,2},{2,1},{5,6},{6,5},{9,10},{10,9},{13,14},{14,13},{17,18},{18,... | collective-permute-start | bytes 1179656 | tf_op jit(solution)/shard_map/ppermute | solution.py:304
  45.4 16.1 %collective-permute-start.17 = (bf16[192,1024]{1,0:T(8,128)(2,1)S(1)}, bf16[192,1024]{1,0:T(8,128)(2,1)S(1)}, u32[]{:S(2)}, u32[]{:S(2)}) collective-permute-start(bf16[192,1024]{1,0:T(8,128)(2,1)S(1)} %get-tuple-element.101), channel_id=1, source_target_pairs={{0,2},{3,1},{4,6},{7,5},{8,10},{11,9},{12,14},{15,13},{16,18},{19,... | collective-permute-start | bytes 1179656 | tf_op jit(solution)/shard_map/ppermute | solution.py:308
  51.4 4.9 %collective-permute-start.7 = (bf16[96,640]{1,0:T(8,128)(2,1)S(1)}, bf16[96,640]{1,0:T(8,128)(2,1)S(1)}, u32[]{:S(2)}, u32[]{:S(2)}) collective-permute-start(bf16[96,640]{1,0:T(8,128)(2,1)S(1)} %get-tuple-element.75), channel_id=1, source_target_pairs={{0,16},{4,20},{8,24},{12,28},{16,0},{20,4},{24,8},{28,12},{1,17},{... | collective-permute-start | bytes 368648 | tf_op jit(solution)/shard_map/ppermute | solution.py:259
  53.0 4.9 %collective-permute-start.8 = (bf16[96,640]{1,0:T(8,128)(2,1)S(1)}, bf16[96,640]{1,0:T(8,128)(2,1)S(1)}, u32[]{:S(2)}, u32[]{:S(2)}) collective-permute-start(bf16[96,640]{1,0:T(8,128)(2,1)S(1)} %get-tuple-element.76), channel_id=1, source_target_pairs={{0,8},{4,12},{8,0},{12,4},{16,24},{20,28},{24,16},{28,20},{1,9},{5... | collective-permute-start | bytes 368648 | tf_op jit(solution)/shard_map/ppermute | solution.py:259
  58.3 6.4 %collective-permute-start.12 = (bf16[96,640]{1,0:T(8,128)(2,1)S(1)}, bf16[96,640]{1,0:T(8,128)(2,1)S(1)}, u32[]{:S(2)}, u32[]{:S(2)}) collective-permute-start(bf16[96,640]{1,0:T(8,128)(2,1)S(1)} %get-tuple-element.92), channel_id=1, source_target_pairs={{0,24},{4,28},{8,16},{12,20},{16,8},{20,12},{24,0},{28,4},{1,25},{... | collective-permute-start | bytes 368648 | tf_op jit(solution)/shard_map/ppermute | solution.py:259
  59.8 6.6 %collective-permute-start.13 = (bf16[96,640]{1,0:T(8,128)(2,1)S(1)}, bf16[96,640]{1,0:T(8,128)(2,1)S(1)}, u32[]{:S(2)}, u32[]{:S(2)}) collective-permute-start(bf16[96,640]{1,0:T(8,128)(2,1)S(1)} %get-tuple-element.93), channel_id=1, source_target_pairs={{0,28},{4,24},{8,20},{12,16},{16,12},{20,8},{24,4},{28,0},{1,29},{... | collective-permute-start | bytes 368648 | tf_op jit(solution)/shard_map/ppermute | solution.py:259
  59.8 15.1 %collective-permute-start.19 = (bf16[256,1024]{1,0:T(8,128)(2,1)S(1)}, bf16[256,1024]{1,0:T(8,128)(2,1)S(1)}, u32[]{:S(2)}, u32[]{:S(2)}) collective-permute-start(bf16[256,1024]{1,0:T(8,128)(2,1)S(1)} %get-tuple-element.103), channel_id=1, source_target_pairs={{0,1},{3,2},{1,3},{2,0},{4,5},{7,6},{5,7},{6,4},{8,9},{11,10},{9,1... | collective-permute-start | bytes 1572872 | tf_op jit(solution)/shard_map/ppermute | solution.py:320
  59.8 9.4 %collective-permute-start.14 = (bf16[96,640]{1,0:T(8,128)(2,1)S(1)}, bf16[96,640]{1,0:T(8,128)(2,1)S(1)}, u32[]{:S(2)}, u32[]{:S(2)}) collective-permute-start(bf16[96,640]{1,0:T(8,128)(2,1)S(1)} %get-tuple-element.94), channel_id=1, source_target_pairs={{0,20},{4,16},{8,28},{12,24},{16,4},{20,0},{24,12},{28,8},{1,21},{... | collective-permute-start | bytes 368648 | tf_op jit(solution)/shard_map/ppermute | solution.py:259
  61.6 7.7 %collective-permute-start.15 = (bf16[96,640]{1,0:T(8,128)(2,1)S(1)}, bf16[96,640]{1,0:T(8,128)(2,1)S(1)}, u32[]{:S(2)}, u32[]{:S(2)}) collective-permute-start(bf16[96,640]{1,0:T(8,128)(2,1)S(1)} %get-tuple-element.95), channel_id=1, source_target_pairs={{0,12},{4,8},{8,4},{12,0},{16,28},{20,24},{24,20},{28,16},{1,13},{... | collective-permute-start | bytes 368648 | tf_op jit(solution)/shard_map/ppermute | solution.py:259
  64.8 4.5 %collective-permute-start.16 = (bf16[96,640]{1,0:T(8,128)(2,1)S(1)}, bf16[96,640]{1,0:T(8,128)(2,1)S(1)}, u32[]{:S(2)}, u32[]{:S(2)}) collective-permute-start(bf16[96,640]{1,0:T(8,128)(2,1)S(1)} %get-tuple-element.96), channel_id=1, source_target_pairs={{0,4},{4,0},{8,12},{12,8},{16,20},{20,16},{24,28},{28,24},{1,5},{5... | collective-permute-start | bytes 368648 | tf_op jit(solution)/shard_map/ppermute | solution.py:259
  66.4 5.5 %collective-permute-start.18 = (bf16[64,1024]{1,0:T(8,128)(2,1)S(1)}, bf16[64,1024]{1,0:T(8,128)(2,1)S(1)}, u32[]{:S(2)}, u32[]{:S(2)}) collective-permute-start(bf16[64,1024]{1,0:T(8,128)(2,1)S(1)} %get-tuple-element.102), channel_id=1, source_target_pairs={{1,2},{2,1},{5,6},{6,5},{9,10},{10,9},{13,14},{14,13},{17,18},{18,... | collective-permute-start | bytes 393224 | tf_op jit(solution)/shard_map/ppermute | solution.py:321
  67.1 2.2 %copy-start.5 = (s32[1,576]{1,0:T(1,128)S(1)}, s32[1,576]{1,0:T(1,128)}, u32[]{:S(2)}) copy-start(s32[1,576]{1,0:T(1,128)} %get-tuple-element.55.target_ref) | copy-start | bytes 6916
  67.1 2.2 %copy-start.7 = (bf16[576]{0:T(1024)(128)(2,1)S(1)}, bf16[576]{0:T(1024)(128)(2,1)}, u32[]{:S(2)}) copy-start(bf16[576]{0:T(1024)(128)(2,1)} %gate_ref.3) | copy-start | bytes 3460
  67.1 2.2 %copy-start.9 = (f32[512]{0:T(512)S(1)}, f32[512]{0:T(512)}, u32[]{:S(2)}) copy-start(f32[512]{0:T(512)} %param.8) | copy-start | bytes 6148

commit v19 on v15

--- a/solution.py
+++ b/solution.py
@@ -247,7 +247,7 @@
 
 
 def block_order(sources):
-    same = sorted(range(2, sources, 2), key=lambda k: (k.bit_count(), -k))
+    same = sorted(range(2, sources, 2), key=lambda k: (k.bit_count(), k))
     return same + list(range(sources - 1, 1, -2)) + [1, 0]
 
 

time: 70.5 us -> 71.5 us (1.014)
  starting transfers between devices: 24.8 us -> 25.7 us
    ppermute x14, waiting for transfers between devices: 15.5 us -> 17.7 us  [swap_blocks(): lax.ppermute(block, 'space', [(i, i ^ k) for i in devices])]
    ppermute x1, waiting for transfers between devices: 1.65 us -> 0.01 us  [line_sums(): inward = lax.ppermute(first, 'dp', [(0, 1), (3, 2)])]
    ppermute x14, starting transfers between devices: 15.3 us -> 16.4 us  [swap_blocks(): lax.ppermute(block, 'space', [(i, i ^ k) for i in devices])]
  transfers between devices with their start and end apart: 19 -> 19, of which waited for: 10 -> 7; matrix products, arithmetic and copies ran while one was open for 0% -> 0% of each run, Pallas kernels for 15% -> 15%
where the time goes in v19:
time: 71.5 us; the launch traced here: 71.2 us
  starting transfers between devices  25.7 us (36%)
  waiting for transfers between devices  24.9 us (35%)
  Pallas kernels  17.7 us (25%)
  local copies, waits for them, and re-layouts  2.06 us (3%)
  between operations  0.88 us (1%)
    ppermute x14, waiting for transfers between devices, swap_blocks(): lax.ppermute(block, 'space', [(i, i ^ k) for i in devices])  17.7 us
    ppermute x14, starting transfers between devices, swap_blocks(): lax.ppermute(block, 'space', [(i, i ^ k) for i in devices])  16.4 us
    pallas_call x3, Pallas kernels, work(): kernel_call(functools.partial(kernel, count, groups), name, 8 * span * wi...  7.33 us
    ppermute x1, waiting for transfers between devices, line_sums(): last = lax.ppermute(passed, 'dp', [(0, 1), (3, 2), (1, 3), (2, 0)])  7.19 us
    pallas_call x1, Pallas kernels, body(): kernel_call(functools.partial(place_kernel, sources, capacity), 'place',...  3.79 us
    ppermute x1, starting transfers between devices, line_sums(): inward = lax.ppermute(first, 'dp', [(0, 1), (3, 2)])  3.51 us
    pallas_call x1, Pallas kernels, body(): kernel_call(finish_kernel, 'finish', 1, 1, [shape((tok_rows, width), BF16...  2.59 us
    ppermute x1, starting transfers between devices, line_sums(): last = lax.ppermute(passed, 'dp', [(0, 1), (3, 2), (1, 3), (2, 0)])  2.4 us
  transfers between devices with their start and end apart: 19, of which 7 were waited for; matrix products, arithmetic and copies ran while one was open for 0% of the time, Pallas kernels for 15%

profile of v19, /device:TPU:0, one launch (start us, length us, event | category | flops | bytes accessed | tf_op | source)
XLA Modules:
  0.0 71.2 jit_solution(14844708011439407518)
XLA Ops:
  0.7 3.8 %place.1 = (s32[1,576]{1,0:T(1,128)}, bf16[96,1024]{1,0:T(8,128)(2,1)}, bf16[96,1024]{1,0:T(8,128)(2,1)}, bf16[96,1024]{1,0:T(8,128)(2,1)}, bf16[96,1024]{1,0:T(8,128)(2,1)}) custom-call(s32[1]{0:T(128)} %bitcast.me, s32[1]{0:T(128)} %bitcast.1.place, s32[1,576]{1,0:T(1,128)} %bitcast.20, bf16[576]{0:T(1024)(128)(2,1)} %gate_ref.3, ...), custom_call_target="tpu_custom_call" | custom-call | flops 452984832 | bytes 2752512 | tf_op jit(solution)/shard_map/place/pallas_call | solution.py:338
  4.5 3.0 %collective-permute-start = (bf16[96,1024]{1,0:T(8,128)(2,1)}, bf16[96,1024]{1,0:T(8,128)(2,1)S(1)}, u32[]{:S(2)}, u32[]{:S(2)}) collective-permute-start(bf16[96,1024]{1,0:T(8,128)(2,1)} %get-tuple-element.56), channel_id=1, source_target_pairs={{0,8},{4,12},{8,0},{12,4},{16,24},{20,28},{24,16},{28,20},{1,9},{5... | collective-permute-start | bytes 589832 | tf_op jit(solution)/shard_map/ppermute | solution.py:257
  7.5 1.5 %collective-permute-start.1 = (bf16[96,1024]{1,0:T(8,128)(2,1)}, bf16[96,1024]{1,0:T(8,128)(2,1)S(1)}, u32[]{:S(2)}, u32[]{:S(2)}) collective-permute-start(bf16[96,1024]{1,0:T(8,128)(2,1)} %get-tuple-element.57), channel_id=1, source_target_pairs={{0,16},{4,20},{8,24},{12,28},{16,0},{20,4},{24,8},{28,12},{1,17},{... | collective-permute-start | bytes 589832 | tf_op jit(solution)/shard_map/ppermute | solution.py:257
  9.0 0.7 copy-done.4
  9.7 0.7 copy-done.6
  10.4 0.7 copy-done.8
  11.1 1.3 %rest.1 = (bf16[96,1024]{1,0:T(8,128)(2,1)S(1)}, bf16[96,1024]{1,0:T(8,128)(2,1)S(1)}, bf16[96,1024]{1,0:T(8,128)(2,1)S(1)}, bf16[96,1024]{1,0:T(8,128)(2,1)S(1)}) custom-call(s32[1,576]{1,0:T(1,128)S(1)} %copy-done.4, bf16[576]{0:T(1024)(128)(2,1)S(1)} %copy-done.6, bf16[576,512]{1,0:T(8,128)(2,1)S(1)} %copy-done.2, f32[1,512]{1,0:T(1,128)S(1)} %bitcast.16, ...), custom_call_target="tpu_custom_call" | custom-call | flops 1 | bytes 1 | tf_op jit(solution)/shard_map/rest/pallas_call | solution.py:359
  12.5 3.0 %collective-permute-start.4 = (bf16[96,1024]{1,0:T(8,128)(2,1)}, bf16[96,1024]{1,0:T(8,128)(2,1)S(1)}, u32[]{:S(2)}, u32[]{:S(2)}) collective-permute-start(bf16[96,1024]{1,0:T(8,128)(2,1)} %get-tuple-element.63), channel_id=1, source_target_pairs={{0,28},{4,24},{8,20},{12,16},{16,12},{20,8},{24,4},{28,0},{1,29},{... | collective-permute-start | bytes 589832 | tf_op jit(solution)/shard_map/ppermute | solution.py:257
  15.5 0.2 collective-permute-start.5
  15.7 6.9 %collective-permute-done.1.refs_1_ = bf16[96,1024]{1,0:T(8,128)(2,1)S(1)} collective-permute-done((bf16[96,1024]{1,0:T(8,128)(2,1)}, bf16[96,1024]{1,0:T(8,128)(2,1)S(1)}, u32[]{:S(2)}, u32[]{:S(2)}) %collective-permute-start.1) | collective-permute-done | bytes 196640 | tf_op jit(solution)/shard_map/ppermute | solution.py:257
  22.7 3.2 %sooner.1 = (f32[512,1024]{1,0:T(8,128)S(1)}, f32[1024,512]{1,0:T(8,128)S(1)}, bf16[480,1024]{1,0:T(8,128)(2,1)S(1)}, bf16[480,128]{1,0:T(8,128)(2,1)S(1)}) custom-call(s32[1]{0:T(128)} %bitcast.1.place, bf16[512,1024]{1,0:T(8,128)(2,1)S(1)} %bitcast.8, bf16[1024,512]{1,0:T(8,128)(2,1)S(1)} %bitcast.12, bf16[96,1024]{1,0:T(8,128)(2,1)S(1)} %collective-permute-done.refs_0_, ...), custom_call_target="tpu_custom_call" | custom-call | flops 2013265920 | bytes 6160384 | tf_op jit(solution)/shard_map/sooner/pallas_call | solution.py:388
  26.0 2.0 %next.1 = (f32[512,1024]{1,0:T(8,128)S(1)}, f32[1024,512]{1,0:T(8,128)S(1)}, bf16[96,1024]{1,0:T(8,128)(2,1)S(1)}, bf16[96,128]{1,0:T(8,128)(2,1)S(1)}) custom-call(s32[1]{0:T(128)} %bitcast.1.place, bf16[512,1024]{1,0:T(8,128)(2,1)S(1)} %bitcast.9, bf16[1024,512]{1,0:T(8,128)(2,1)S(1)} %bitcast.13, f32[512,1024]{1,0:T(8,128)S(1)} %get-tuple-element.61.old_in_ref, ...), custom_call_target="tpu_custom_call" | custom-call | flops 402653184 | bytes 4587520 | tf_op jit(solution)/shard_map/next/pallas_call | solution.py:388
  28.0 2.1 %later.1 = (bf16[256,1024]{1,0:T(8,128)(2,1)S(1)}, bf16[256,1024]{1,0:T(8,128)(2,1)S(1)}, bf16[256,1024]{1,0:T(8,128)(2,1)S(1)}, bf16[256,1024]{1,0:T(8,128)(2,1...) custom-call(s32[1]{0:T(128)} %bitcast.1.place, ...), custom_call_target="tpu_custom_call" | custom-call | flops 805306368 | bytes 4980736 | tf_op jit(solution)/shard_map/later/pallas_call | solution.py:388
  30.1 3.5 %collective-permute-start.10 = (bf16[256,1024]{1,0:T(8,128)(2,1)S(1)}, bf16[256,1024]{1,0:T(8,128)(2,1)S(1)}, u32[]{:S(2)}, u32[]{:S(2)}) collective-permute-start(bf16[256,1024]{1,0:T(8,128)(2,1)S(1)} %get-tuple-element.82), channel_id=1, source_target_pairs={{0,1},{3,2},{4,5},{7,6},{8,9},{11,10},{12,13},{15,14},{16,17},{19,... | collective-permute-start | bytes 1572872 | tf_op jit(solution)/shard_map/ppermute | solution.py:291
  33.6 0.7 collective-permute-start.9
  34.3 1.3 %back.1 = (bf16[96,640]{1,0:T(8,128)(2,1)S(1)}, bf16[96,640]{1,0:T(8,128)(2,1)S(1)}, bf16[96,640]{1,0:T(8,128)(2,1)S(1)}, bf16[96,640]{1,0:T(8,128)(2,1)S(1)}, b...) custom-call(bf16[512,1024]{1,0:T(8,128)(2,1)S(1)} %bitcast.11, ...), custom_call_target="tpu_custom_call" | custom-call | flops 1 | bytes 1 | tf_op jit(solution)/shard_map/back/pallas_call | solution.py:407
  35.7 0.4 collective-permute-start.7
  36.1 2.6 %collective-permute-start.8 = (bf16[96,640]{1,0:T(8,128)(2,1)S(1)}, bf16[96,640]{1,0:T(8,128)(2,1)S(1)}, u32[]{:S(2)}, u32[]{:S(2)}) collective-permute-start(bf16[96,640]{1,0:T(8,128)(2,1)S(1)} %get-tuple-element.78), channel_id=1, source_target_pairs={{0,16},{4,20},{8,24},{12,28},{16,0},{20,4},{24,8},{28,12},{1,17},{... | collective-permute-start | bytes 368648 | tf_op jit(solution)/shard_map/ppermute | solution.py:257
  38.7 2.4 %collective-permute-done.7.refs_0_ = bf16[96,640]{1,0:T(8,128)(2,1)S(1)} collective-permute-done((bf16[96,640]{1,0:T(8,128)(2,1)S(1)}, bf16[96,640]{1,0:T(8,128)(2,1)S(1)}, u32[]{:S(2)}, u32[]{:S(2)}) %collective-permute-start.7) | collective-permute-done | bytes 122912 | tf_op jit(solution)/shard_map/ppermute | solution.py:257
  41.1 1.5 %collective-permute-done.8.refs_1_ = bf16[96,640]{1,0:T(8,128)(2,1)S(1)} collective-permute-done((bf16[96,640]{1,0:T(8,128)(2,1)S(1)}, bf16[96,640]{1,0:T(8,128)(2,1)S(1)}, u32[]{:S(2)}, u32[]{:S(2)}) %collective-permute-start.8) | collective-permute-done | bytes 122912 | tf_op jit(solution)/shard_map/ppermute | solution.py:257
  42.6 2.0 %collective-permute-start.17 = (bf16[256,1024]{1,0:T(8,128)(2,1)S(1)}, bf16[256,1024]{1,0:T(8,128)(2,1)S(1)}, u32[]{:S(2)}, u32[]{:S(2)}) collective-permute-start(bf16[256,1024]{1,0:T(8,128)(2,1)S(1)} %get-tuple-element.102), channel_id=1, source_target_pairs={{0,2},{1,0},{2,3},{3,1},{4,6},{5,4},{6,7},{7,5},{8,10},{9,8},{10,1... | collective-permute-start | bytes 1572872 | tf_op jit(solution)/shard_map/ppermute | solution.py:296
  44.9 2.4 %collective-permute-start.18 = (bf16[256,1024]{1,0:T(8,128)(2,1)S(1)}, bf16[256,1024]{1,0:T(8,128)(2,1)S(1)}, u32[]{:S(2)}, u32[]{:S(2)}) collective-permute-start(bf16[256,1024]{1,0:T(8,128)(2,1)S(1)} %get-tuple-element.103), channel_id=1, source_target_pairs={{0,1},{3,2},{1,3},{2,0},{4,5},{7,6},{5,7},{6,4},{8,9},{11,10},{9,1... | collective-permute-start | bytes 1572872 | tf_op jit(solution)/shard_map/ppermute | solution.py:303
  47.3 3.2 %collective-permute-start.11 = (bf16[96,640]{1,0:T(8,128)(2,1)S(1)}, bf16[96,640]{1,0:T(8,128)(2,1)S(1)}, u32[]{:S(2)}, u32[]{:S(2)}) collective-permute-start(bf16[96,640]{1,0:T(8,128)(2,1)S(1)} %get-tuple-element.92), channel_id=1, source_target_pairs={{0,24},{4,28},{8,16},{12,20},{16,8},{20,12},{24,0},{28,4},{1,25},{... | collective-permute-start | bytes 368648 | tf_op jit(solution)/shard_map/ppermute | solution.py:257
  50.6 1.8 %collective-permute-start.13 = (bf16[96,640]{1,0:T(8,128)(2,1)S(1)}, bf16[96,640]{1,0:T(8,128)(2,1)S(1)}, u32[]{:S(2)}, u32[]{:S(2)}) collective-permute-start(bf16[96,640]{1,0:T(8,128)(2,1)S(1)} %get-tuple-element.94), channel_id=1, source_target_pairs={{0,20},{4,16},{8,28},{12,24},{16,4},{20,0},{24,12},{28,8},{1,21},{... | collective-permute-start | bytes 368648 | tf_op jit(solution)/shard_map/ppermute | solution.py:257
  52.4 2.1 %collective-permute-done.11.refs_2_ = bf16[96,640]{1,0:T(8,128)(2,1)S(1)} collective-permute-done((bf16[96,640]{1,0:T(8,128)(2,1)S(1)}, bf16[96,640]{1,0:T(8,128)(2,1)S(1)}, u32[]{:S(2)}, u32[]{:S(2)}) %collective-permute-start.11) | collective-permute-done | bytes 122912 | tf_op jit(solution)/shard_map/ppermute | solution.py:257
  54.5 2.3 %collective-permute-done.12.refs_3_ = bf16[96,640]{1,0:T(8,128)(2,1)S(1)} collective-permute-done((bf16[96,640]{1,0:T(8,128)(2,1)S(1)}, bf16[96,640]{1,0:T(8,128)(2,1)S(1)}, u32[]{:S(2)}, u32[]{:S(2)}) %collective-permute-start.12) | collective-permute-done | bytes 122912 | tf_op jit(solution)/shard_map/ppermute | solution.py:257
  56.8 0.4 collective-permute-start.15
  57.2 2.5 %collective-permute-done.13.refs_4_ = bf16[96,640]{1,0:T(8,128)(2,1)S(1)} collective-permute-done((bf16[96,640]{1,0:T(8,128)(2,1)S(1)}, bf16[96,640]{1,0:T(8,128)(2,1)S(1)}, u32[]{:S(2)}, u32[]{:S(2)}) %collective-permute-start.13) | collective-permute-done | bytes 122912 | tf_op jit(solution)/shard_map/ppermute | solution.py:257
  59.7 0.7 collective-permute-start.16
  60.4 2.6 %finish.1 = (bf16[576,512]{1,0:T(8,128)(2,1)}, bf16[576]{0:T(1024)(128)(2,1)}) custom-call(s32[1,576]{1,0:T(1,128)S(1)} %copy-done.5, bf16[576]{0:T(1024)(128)(2,1)S(1)} %copy-done.7, bf16[576,512]{1,0:T(8,128)(2,1)S(1)} %copy-done.2, f32[1,512]{1,0:T(1,128)S(1)} %bitcast.17, bf16[576,512]{1,0:T(8,128)(2,1)S(1)} %copy-done.3, ...), custom_call_target="tpu_custom_call" | custom-call | flops 1 | bytes 1 | tf_op jit(solution)/shard_map/finish/pallas_call | solution.py:427
  63.0 7.2 %collective-permute-done.18.last_ref = bf16[256,1024]{1,0:T(8,128)(2,1)S(1)} collective-permute-done((bf16[256,1024]{1,0:T(8,128)(2,1)S(1)}, bf16[256,1024]{1,0:T(8,128)(2,1)S(1)}, u32[]{:S(2)}, u32[]{:S(2)}) %collective-permute-start.18) | collective-permute-done | bytes 524320 | tf_op jit(solution)/shard_map/ppermute | solution.py:303
  70.2 1.1 %total.1 = (f32[128,1024]{1,0:T(8,128)}, f32[256,512]{1,0:T(8,128)}) custom-call(f32[256,1024]{1,0:T(8,128)S(1)} %get-tuple-element.100.sum_ref, bf16[32,1024]{1,0:T(8,128)(2,1)S(1)} %collective-permute-done.16.below_ref, bf16[256,1024]{1,0:T(8,128)(2,1)S(1)} %collective-permute-done.17.cycle_ref, bf16[256,1024]{1,0:T(8,128)(2,1)S(1)} %collective-permute-done.18.last_ref), custom_call_target="tpu_custom_call" | custom-call | flops 1 | bytes 1 | tf_op jit(solution)/shard_map/total/pallas_call | solution.py:306
  (36 shorter events, 0.5 us)
Async XLA Ops:
  0.6 8.4 %copy-start.3 = (bf16[576,512]{1,0:T(8,128)(2,1)S(1)}, bf16[576,512]{1,0:T(8,128)(2,1)}, u32[]{:S(2)}) copy-start(bf16[576,512]{1,0:T(8,128)(2,1)} %go_ref.3) | copy-start | bytes 1769476
  0.6 8.4 %copy-start.2 = (bf16[576,512]{1,0:T(8,128)(2,1)S(1)}, bf16[576,512]{1,0:T(8,128)(2,1)}, u32[]{:S(2)}) copy-start(bf16[576,512]{1,0:T(8,128)(2,1)} %tok_ref.3) | copy-start | bytes 1769476
  0.7 22.0 %copy-start.1 = (bf16[1,1024,512]{2,1,0:T(8,128)(2,1)S(1)}, bf16[1,1024,512]{2,1,0:T(8,128)(2,1)}, u32[]{:S(2)}) copy-start(bf16[1,1024,512]{2,1,0:T(8,128)(2,1)} %param.10) | copy-start | bytes 3145732
  0.7 22.0 %copy-start = (bf16[1,512,1024]{2,1,0:T(8,128)(2,1)S(1)}, bf16[1,512,1024]{2,1,0:T(8,128)(2,1)}, u32[]{:S(2)}) copy-start(bf16[1,512,1024]{2,1,0:T(8,128)(2,1)} %param.9) | copy-start | bytes 3145732
  4.5 11.0 %collective-permute-start = (bf16[96,1024]{1,0:T(8,128)(2,1)}, bf16[96,1024]{1,0:T(8,128)(2,1)S(1)}, u32[]{:S(2)}, u32[]{:S(2)}) collective-permute-start(bf16[96,1024]{1,0:T(8,128)(2,1)} %get-tuple-element.56), channel_id=1, source_target_pairs={{0,8},{4,12},{8,0},{12,4},{16,24},{20,28},{24,16},{28,20},{1,9},{5... | collective-permute-start | bytes 589832 | tf_op jit(solution)/shard_map/ppermute | solution.py:257
  7.5 15.2 %collective-permute-start.1 = (bf16[96,1024]{1,0:T(8,128)(2,1)}, bf16[96,1024]{1,0:T(8,128)(2,1)S(1)}, u32[]{:S(2)}, u32[]{:S(2)}) collective-permute-start(bf16[96,1024]{1,0:T(8,128)(2,1)} %get-tuple-element.57), channel_id=1, source_target_pairs={{0,16},{4,20},{8,24},{12,28},{16,0},{20,4},{24,8},{28,12},{1,17},{... | collective-permute-start | bytes 589832 | tf_op jit(solution)/shard_map/ppermute | solution.py:257
  9.0 13.7 %collective-permute-start.2 = (bf16[96,1024]{1,0:T(8,128)(2,1)}, bf16[96,1024]{1,0:T(8,128)(2,1)S(1)}, u32[]{:S(2)}, u32[]{:S(2)}) collective-permute-start(bf16[96,1024]{1,0:T(8,128)(2,1)} %get-tuple-element.58), channel_id=1, source_target_pairs={{0,24},{4,28},{8,16},{12,20},{16,8},{20,12},{24,0},{28,4},{1,25},{... | collective-permute-start | bytes 589832 | tf_op jit(solution)/shard_map/ppermute | solution.py:257
  9.0 0.7 copy-start.4
  9.7 0.7 copy-start.6
  10.4 0.7 copy-start.8
  12.4 10.3 %collective-permute-start.3 = (bf16[96,1024]{1,0:T(8,128)(2,1)S(1)}, bf16[96,1024]{1,0:T(8,128)(2,1)S(1)}, u32[]{:S(2)}, u32[]{:S(2)}) collective-permute-start(bf16[96,1024]{1,0:T(8,128)(2,1)S(1)} %get-tuple-element.59), channel_id=1, source_target_pairs={{0,4},{4,0},{8,12},{12,8},{16,20},{20,16},{24,28},{28,24},{1,5},{5... | collective-permute-start | bytes 589832 | tf_op jit(solution)/shard_map/ppermute | solution.py:257
  12.5 13.5 %collective-permute-start.4 = (bf16[96,1024]{1,0:T(8,128)(2,1)}, bf16[96,1024]{1,0:T(8,128)(2,1)S(1)}, u32[]{:S(2)}, u32[]{:S(2)}) collective-permute-start(bf16[96,1024]{1,0:T(8,128)(2,1)} %get-tuple-element.63), channel_id=1, source_target_pairs={{0,28},{4,24},{8,20},{12,16},{16,12},{20,8},{24,4},{28,0},{1,29},{... | collective-permute-start | bytes 589832 | tf_op jit(solution)/shard_map/ppermute | solution.py:257
  15.5 12.5 %collective-permute-start.5 = (bf16[96,1024]{1,0:T(8,128)(2,1)S(1)}, bf16[96,1024]{1,0:T(8,128)(2,1)S(1)}, u32[]{:S(2)}, u32[]{:S(2)}) collective-permute-start(bf16[96,1024]{1,0:T(8,128)(2,1)S(1)} %get-tuple-element.66), channel_id=1, source_target_pairs={{0,20},{4,16},{8,28},{12,24},{16,4},{20,0},{24,12},{28,8},{1,21},{... | collective-permute-start | bytes 589832 | tf_op jit(solution)/shard_map/ppermute | solution.py:257
  22.7 5.3 %collective-permute-start.6 = (bf16[96,1024]{1,0:T(8,128)(2,1)S(1)}, bf16[96,1024]{1,0:T(8,128)(2,1)S(1)}, u32[]{:S(2)}, u32[]{:S(2)}) collective-permute-start(bf16[96,1024]{1,0:T(8,128)(2,1)S(1)} %get-tuple-element.67), channel_id=1, source_target_pairs={{0,12},{4,8},{8,4},{12,0},{16,28},{20,24},{24,20},{28,16},{1,13},{... | collective-permute-start | bytes 589832 | tf_op jit(solution)/shard_map/ppermute | solution.py:257
  30.1 14.5 %collective-permute-start.10 = (bf16[256,1024]{1,0:T(8,128)(2,1)S(1)}, bf16[256,1024]{1,0:T(8,128)(2,1)S(1)}, u32[]{:S(2)}, u32[]{:S(2)}) collective-permute-start(bf16[256,1024]{1,0:T(8,128)(2,1)S(1)} %get-tuple-element.82), channel_id=1, source_target_pairs={{0,1},{3,2},{4,5},{7,6},{8,9},{11,10},{12,13},{15,14},{16,17},{19,... | collective-permute-start | bytes 1572872 | tf_op jit(solution)/shard_map/ppermute | solution.py:291
  33.6 11.0 %collective-permute-start.9 = (bf16[224,1024]{1,0:T(8,128)(2,1)S(1)}, bf16[224,1024]{1,0:T(8,128)(2,1)S(1)}, u32[]{:S(2)}, u32[]{:S(2)}) collective-permute-start(bf16[224,1024]{1,0:T(8,128)(2,1)S(1)} %get-tuple-element.81), channel_id=1, source_target_pairs={{1,2},{2,1},{5,6},{6,5},{9,10},{10,9},{13,14},{14,13},{17,18},{18,... | collective-permute-start | bytes 1376264 | tf_op jit(solution)/shard_map/ppermute | solution.py:292
  34.3 26.0 %copy-start.5 = (s32[1,576]{1,0:T(1,128)S(1)}, s32[1,576]{1,0:T(1,128)}, u32[]{:S(2)}) copy-start(s32[1,576]{1,0:T(1,128)} %get-tuple-element.55.target_ref) | copy-start | bytes 6916
  34.3 26.0 %copy-start.7 = (bf16[576]{0:T(1024)(128)(2,1)S(1)}, bf16[576]{0:T(1024)(128)(2,1)}, u32[]{:S(2)}) copy-start(bf16[576]{0:T(1024)(128)(2,1)} %gate_ref.3) | copy-start | bytes 3460
  34.3 26.0 %copy-start.9 = (f32[512]{0:T(512)S(1)}, f32[512]{0:T(512)}, u32[]{:S(2)}) copy-start(f32[512]{0:T(512)} %param.8) | copy-start | bytes 6148
  35.7 5.4 %collective-permute-start.7 = (bf16[96,640]{1,0:T(8,128)(2,1)S(1)}, bf16[96,640]{1,0:T(8,128)(2,1)S(1)}, u32[]{:S(2)}, u32[]{:S(2)}) collective-permute-start(bf16[96,640]{1,0:T(8,128)(2,1)S(1)} %get-tuple-element.76), channel_id=1, source_target_pairs={{0,8},{4,12},{8,0},{12,4},{16,24},{20,28},{24,16},{28,20},{1,9},{5... | collective-permute-start | bytes 368648 | tf_op jit(solution)/shard_map/ppermute | solution.py:257
  36.1 6.5 %collective-permute-start.8 = (bf16[96,640]{1,0:T(8,128)(2,1)S(1)}, bf16[96,640]{1,0:T(8,128)(2,1)S(1)}, u32[]{:S(2)}, u32[]{:S(2)}) collective-permute-start(bf16[96,640]{1,0:T(8,128)(2,1)S(1)} %get-tuple-element.78), channel_id=1, source_target_pairs={{0,16},{4,20},{8,24},{12,28},{16,0},{20,4},{24,8},{28,12},{1,17},{... | collective-permute-start | bytes 368648 | tf_op jit(solution)/shard_map/ppermute | solution.py:257
  42.6 20.4 %collective-permute-start.17 = (bf16[256,1024]{1,0:T(8,128)(2,1)S(1)}, bf16[256,1024]{1,0:T(8,128)(2,1)S(1)}, u32[]{:S(2)}, u32[]{:S(2)}) collective-permute-start(bf16[256,1024]{1,0:T(8,128)(2,1)S(1)} %get-tuple-element.102), channel_id=1, source_target_pairs={{0,2},{1,0},{2,3},{3,1},{4,6},{5,4},{6,7},{7,5},{8,10},{9,8},{10,1... | collective-permute-start | bytes 1572872 | tf_op jit(solution)/shard_map/ppermute | solution.py:296
  44.9 25.3 %collective-permute-start.18 = (bf16[256,1024]{1,0:T(8,128)(2,1)S(1)}, bf16[256,1024]{1,0:T(8,128)(2,1)S(1)}, u32[]{:S(2)}, u32[]{:S(2)}) collective-permute-start(bf16[256,1024]{1,0:T(8,128)(2,1)S(1)} %get-tuple-element.103), channel_id=1, source_target_pairs={{0,1},{3,2},{1,3},{2,0},{4,5},{7,6},{5,7},{6,4},{8,9},{11,10},{9,1... | collective-permute-start | bytes 1572872 | tf_op jit(solution)/shard_map/ppermute | solution.py:303
  47.3 7.2 %collective-permute-start.11 = (bf16[96,640]{1,0:T(8,128)(2,1)S(1)}, bf16[96,640]{1,0:T(8,128)(2,1)S(1)}, u32[]{:S(2)}, u32[]{:S(2)}) collective-permute-start(bf16[96,640]{1,0:T(8,128)(2,1)S(1)} %get-tuple-element.92), channel_id=1, source_target_pairs={{0,24},{4,28},{8,16},{12,20},{16,8},{20,12},{24,0},{28,4},{1,25},{... | collective-permute-start | bytes 368648 | tf_op jit(solution)/shard_map/ppermute | solution.py:257
  50.5 6.3 %collective-permute-start.12 = (bf16[96,640]{1,0:T(8,128)(2,1)S(1)}, bf16[96,640]{1,0:T(8,128)(2,1)S(1)}, u32[]{:S(2)}, u32[]{:S(2)}) collective-permute-start(bf16[96,640]{1,0:T(8,128)(2,1)S(1)} %get-tuple-element.93), channel_id=1, source_target_pairs={{0,28},{4,24},{8,20},{12,16},{16,12},{20,8},{24,4},{28,0},{1,29},{... | collective-permute-start | bytes 368648 | tf_op jit(solution)/shard_map/ppermute | solution.py:257
  50.6 9.1 %collective-permute-start.13 = (bf16[96,640]{1,0:T(8,128)(2,1)S(1)}, bf16[96,640]{1,0:T(8,128)(2,1)S(1)}, u32[]{:S(2)}, u32[]{:S(2)}) collective-permute-start(bf16[96,640]{1,0:T(8,128)(2,1)S(1)} %get-tuple-element.94), channel_id=1, source_target_pairs={{0,20},{4,16},{8,28},{12,24},{16,4},{20,0},{24,12},{28,8},{1,21},{... | collective-permute-start | bytes 368648 | tf_op jit(solution)/shard_map/ppermute | solution.py:257
  54.5 5.8 %collective-permute-start.14 = (bf16[96,640]{1,0:T(8,128)(2,1)S(1)}, bf16[96,640]{1,0:T(8,128)(2,1)S(1)}, u32[]{:S(2)}, u32[]{:S(2)}) collective-permute-start(bf16[96,640]{1,0:T(8,128)(2,1)S(1)} %get-tuple-element.95), channel_id=1, source_target_pairs={{0,12},{4,8},{8,4},{12,0},{16,28},{20,24},{24,20},{28,16},{1,13},{... | collective-permute-start | bytes 368648 | tf_op jit(solution)/shard_map/ppermute | solution.py:257
  56.8 3.5 %collective-permute-start.15 = (bf16[96,640]{1,0:T(8,128)(2,1)S(1)}, bf16[96,640]{1,0:T(8,128)(2,1)S(1)}, u32[]{:S(2)}, u32[]{:S(2)}) collective-permute-start(bf16[96,640]{1,0:T(8,128)(2,1)S(1)} %get-tuple-element.96), channel_id=1, source_target_pairs={{0,4},{4,0},{8,12},{12,8},{16,20},{20,16},{24,28},{28,24},{1,5},{5... | collective-permute-start | bytes 368648 | tf_op jit(solution)/shard_map/ppermute | solution.py:257
  59.7 3.3 %collective-permute-start.16 = (bf16[32,1024]{1,0:T(8,128)(2,1)S(1)}, bf16[32,1024]{1,0:T(8,128)(2,1)S(1)}, u32[]{:S(2)}, u32[]{:S(2)}) collective-permute-start(bf16[32,1024]{1,0:T(8,128)(2,1)S(1)} %get-tuple-element.101), channel_id=1, source_target_pairs={{1,2},{2,1},{5,6},{6,5},{9,10},{10,9},{13,14},{14,13},{17,18},{18,... | collective-permute-start | bytes 196616 | tf_op jit(solution)/shard_map/ppermute | solution.py:293

commit v20 on v15

--- a/solution.py
+++ b/solution.py
@@ -172,8 +172,8 @@
     piece_f = w_in_ref.shape[1] // LINE
 
     def put(j, part, weight_in, weight_out):
-        sum_in_ref[:, part] = weight_in
-        sum_out_ref[j * piece_f : (j + 1) * piece_f, :] = weight_out
+        sum_in_ref[:, part] = weight_in.astype(BF16)
+        sum_out_ref[j * piece_f : (j + 1) * piece_f, :] = weight_out.astype(BF16)
 
     order = shard_order(place[0]) if groups == LINE else list(range(LINE))
     expert_work(order, blocks, w_in_ref, w_out_ref, gpre_ref, extra_ref, rows_ref, turned_ref, put)
@@ -186,8 +186,8 @@
 
     def put(j, part, weight_in, weight_out):
         chunk = slice(j * piece_f, (j + 1) * piece_f)
-        sum_in_ref[:, part] = old_in_ref[:, part] + weight_in
-        sum_out_ref[chunk, :] = old_out_ref[chunk, :] + weight_out
+        sum_in_ref[:, part] = (old_in_ref[:, part].astype(F32) + weight_in).astype(BF16)
+        sum_out_ref[chunk, :] = (old_out_ref[chunk, :].astype(F32) + weight_out).astype(BF16)
 
     order = shard_order(place[0]) if groups == LINE else list(range(LINE))
     expert_work(order, blocks, w_in_ref, w_out_ref, gpre_ref, extra_ref, rows_ref, turned_ref, put)
@@ -201,10 +201,10 @@
     piece_d, piece_f = width // LINE, hidden // LINE
 
     def put(j, part, weight_in, weight_out):
-        weight = (sum_out_ref[j * piece_f : (j + 1) * piece_f, :] + weight_out).astype(BF16)
+        weight = (sum_out_ref[j * piece_f : (j + 1) * piece_f, :].astype(F32) + weight_out).astype(BF16)
         outs[j][piece_d:, :width] = weight[: piece_f // 2]
         outs[j][piece_d:, width:] = weight[piece_f // 2 :]
-        weight = (sum_in_ref[:, part] + weight_in).astype(BF16)
+        weight = (sum_in_ref[:, part].astype(F32) + weight_in).astype(BF16)
         for i in range(LINE):
             outs[i][:piece_d, part] = weight[i * piece_d : (i + 1) * piece_d]
 
@@ -395,7 +395,7 @@
             [pltpu.VMEM((span, 2 * width), BF16), pltpu.VMEM((width, span), BF16)],
         )(place, weight_in, weight_out, *sums, *[arrived[j] for j in members])
 
-    sums_shape = [shape((width, hidden), F32), shape((hidden, width), F32)]
+    sums_shape = [shape((width, hidden), BF16), shape((hidden, width), BF16)]
     *sums, soon_gpre, soon_extra = work(sooner_kernel, "sooner", soon_set, sums_shape)
     *sums, next_gpre, next_extra = work(next_kernel, "next", next_set, sums_shape, *sums)
     piece = shape((width // LINE + hidden // LINE // 2, hidden), BF16)

time: 70.5 us -> 70.5 us (level)
    unnamed x20 -> x18, local copies, waits for them, and re-layouts: 2.06 us -> 1.76 us
  transfers between devices with their start and end apart: 19 -> 19, of which waited for: 10 -> 11; matrix products, arithmetic and copies ran while one was open for 0% -> 0% of each run, Pallas kernels for 15% -> 15%
where the time goes in v20:
time: 70.5 us; the launch traced here: 70.2 us
  starting transfers between devices  25 us (35%)
  waiting for transfers between devices  25 us (35%)
  Pallas kernels  17.6 us (25%)
  local copies, waits for them, and re-layouts  1.76 us (2%)
  between operations  0.83 us (1%)
    ppermute x14, waiting for transfers between devices, swap_blocks(): lax.ppermute(block, 'space', [(i, i ^ k) for i in devices])  15.7 us
    ppermute x14, starting transfers between devices, swap_blocks(): lax.ppermute(block, 'space', [(i, i ^ k) for i in devices])  15.4 us
    ppermute x1, waiting for transfers between devices, line_sums(): last = lax.ppermute(passed, 'dp', [(0, 1), (3, 2), (1, 3), (2, 0)])  7.61 us
    pallas_call x3, Pallas kernels, work(): kernel_call(functools.partial(kernel, count, groups), name, 8 * span * wi...  7.29 us
    pallas_call x1, Pallas kernels, body(): kernel_call(functools.partial(place_kernel, sources, capacity), 'place',...  3.77 us
    ppermute x1, starting transfers between devices, line_sums(): inward = lax.ppermute(first, 'dp', [(0, 1), (3, 2)])  3.68 us
    pallas_call x1, Pallas kernels, body(): kernel_call(finish_kernel, 'finish', 1, 1, [shape((tok_rows, width), BF16...  2.59 us
    ppermute x1, starting transfers between devices, line_sums(): last = lax.ppermute(passed, 'dp', [(0, 1), (3, 2), (1, 3), (2, 0)])  2.53 us
  transfers between devices with their start and end apart: 19, of which 11 were waited for; matrix products, arithmetic and copies ran while one was open for 0% of the time, Pallas kernels for 15%

profile of v20, /device:TPU:0, one launch (start us, length us, event | category | flops | bytes accessed | tf_op | source)
XLA Modules:
  0.0 70.2 jit_solution(9934888307182575197)
XLA Ops:
  0.7 3.8 %place.1 = (s32[1,576]{1,0:T(1,128)}, bf16[96,1024]{1,0:T(8,128)(2,1)}, bf16[96,1024]{1,0:T(8,128)(2,1)}, bf16[96,1024]{1,0:T(8,128)(2,1)}, bf16[96,1024]{1,0:T(8,128)(2,1)}) custom-call(s32[1]{0:T(128)} %bitcast.me, s32[1]{0:T(128)} %bitcast.1.place, s32[1,576]{1,0:T(1,128)} %bitcast.20, bf16[576]{0:T(1024)(128)(2,1)} %gate_ref.3, ...), custom_call_target="tpu_custom_call" | custom-call | flops 452984832 | bytes 2752512 | tf_op jit(solution)/shard_map/place/pallas_call | solution.py:338
  4.5 3.0 %collective-permute-start = (bf16[96,1024]{1,0:T(8,128)(2,1)}, bf16[96,1024]{1,0:T(8,128)(2,1)S(1)}, u32[]{:S(2)}, u32[]{:S(2)}) collective-permute-start(bf16[96,1024]{1,0:T(8,128)(2,1)} %get-tuple-element.56), channel_id=1, source_target_pairs={{0,16},{4,20},{8,24},{12,28},{16,0},{20,4},{24,8},{28,12},{1,17},{... | collective-permute-start | bytes 589832 | tf_op jit(solution)/shard_map/ppermute | solution.py:257
  7.5 1.5 %collective-permute-start.1 = (bf16[96,1024]{1,0:T(8,128)(2,1)}, bf16[96,1024]{1,0:T(8,128)(2,1)S(1)}, u32[]{:S(2)}, u32[]{:S(2)}) collective-permute-start(bf16[96,1024]{1,0:T(8,128)(2,1)} %get-tuple-element.57), channel_id=1, source_target_pairs={{0,8},{4,12},{8,0},{12,4},{16,24},{20,28},{24,16},{28,20},{1,9},{5... | collective-permute-start | bytes 589832 | tf_op jit(solution)/shard_map/ppermute | solution.py:257
  9.1 1.1 %copy-done.3 = bf16[576,512]{1,0:T(8,128)(2,1)S(1)} copy-done((bf16[576,512]{1,0:T(8,128)(2,1)S(1)}, bf16[576,512]{1,0:T(8,128)(2,1)}, u32[]{:S(2)}) %copy-start.3) | copy-done | bytes 589848
  10.1 0.7 copy-done.5
  10.8 1.3 %rest.1 = (bf16[96,1024]{1,0:T(8,128)(2,1)S(1)}, bf16[96,1024]{1,0:T(8,128)(2,1)S(1)}, bf16[96,1024]{1,0:T(8,128)(2,1)S(1)}, bf16[96,1024]{1,0:T(8,128)(2,1)S(1)}) custom-call(s32[1,576]{1,0:T(1,128)S(1)} %copy-done.5, bf16[576]{0:T(1024)(128)(2,1)S(1)} %copy-done.7, bf16[576,512]{1,0:T(8,128)(2,1)S(1)} %copy-done.2, f32[1,512]{1,0:T(1,128)S(1)} %bitcast.16, ...), custom_call_target="tpu_custom_call" | custom-call | flops 1 | bytes 1 | tf_op jit(solution)/shard_map/rest/pallas_call | solution.py:359
  12.2 3.0 %collective-permute-start.4 = (bf16[96,1024]{1,0:T(8,128)(2,1)}, bf16[96,1024]{1,0:T(8,128)(2,1)S(1)}, u32[]{:S(2)}, u32[]{:S(2)}) collective-permute-start(bf16[96,1024]{1,0:T(8,128)(2,1)} %get-tuple-element.63), channel_id=1, source_target_pairs={{0,28},{4,24},{8,20},{12,16},{16,12},{20,8},{24,4},{28,0},{1,29},{... | collective-permute-start | bytes 589832 | tf_op jit(solution)/shard_map/ppermute | solution.py:257
  15.8 3.5 %collective-permute-done.2.refs_2_ = bf16[96,1024]{1,0:T(8,128)(2,1)S(1)} collective-permute-done((bf16[96,1024]{1,0:T(8,128)(2,1)}, bf16[96,1024]{1,0:T(8,128)(2,1)S(1)}, u32[]{:S(2)}, u32[]{:S(2)}) %collective-permute-start.2) | collective-permute-done | bytes 196640 | tf_op jit(solution)/shard_map/ppermute | solution.py:257
  19.3 3.3 %sooner.1 = (bf16[512,1024]{1,0:T(8,128)(2,1)S(1)}, bf16[1024,512]{1,0:T(8,128)(2,1)S(1)}, bf16[480,1024]{1,0:T(8,128)(2,1)S(1)}, bf16[480,128]{1,0:T(8,128)(2,1)S(1)}) custom-call(s32[1]{0:T(128)} %bitcast.1.place, bf16[512,1024]{1,0:T(8,128)(2,1)S(1)} %bitcast.8, bf16[1024,512]{1,0:T(8,128)(2,1)S(1)} %bitcast.12, ...), custom_call_target="tpu_custom_call" | custom-call | flops 2013265920 | bytes 6160384 | tf_op jit(solution)/shard_map/sooner/pallas_call | solution.py:388
  22.6 0.4 collective-permute-done.4.refs_0_
  23.0 2.0 %next.1 = (bf16[512,1024]{1,0:T(8,128)(2,1)S(1)}, bf16[1024,512]{1,0:T(8,128)(2,1)S(1)}, bf16[96,1024]{1,0:T(8,128)(2,1)S(1)}, bf16[96,128]{1,0:T(8,128)(2,1)S(1)}) custom-call(s32[1]{0:T(128)} %bitcast.1.place, bf16[512,1024]{1,0:T(8,128)(2,1)S(1)} %bitcast.9, bf16[1024,512]{1,0:T(8,128)(2,1)S(1)} %bitcast.13, ...), custom_call_target="tpu_custom_call" | custom-call | flops 402653184 | bytes 4587520 | tf_op jit(solution)/shard_map/next/pallas_call | solution.py:388
  25.0 1.5 %collective-permute-done.5.refs_0_ = bf16[96,1024]{1,0:T(8,128)(2,1)S(1)} collective-permute-done((bf16[96,1024]{1,0:T(8,128)(2,1)S(1)}, bf16[96,1024]{1,0:T(8,128)(2,1)S(1)}, u32[]{:S(2)}, u32[]{:S(2)}) %collective-permute-start.5) | collective-permute-done | bytes 196640 | tf_op jit(solution)/shard_map/ppermute | solution.py:257
  26.5 2.1 %later.1 = (bf16[256,1024]{1,0:T(8,128)(2,1)S(1)}, bf16[256,1024]{1,0:T(8,128)(2,1)S(1)}, bf16[256,1024]{1,0:T(8,128)(2,1)S(1)}, bf16[256,1024]{1,0:T(8,128)(2,1...) custom-call(s32[1]{0:T(128)} %bitcast.1.place, ...), custom_call_target="tpu_custom_call" | custom-call | flops 805306368 | bytes 4980736 | tf_op jit(solution)/shard_map/later/pallas_call | solution.py:388
  28.6 3.7 %collective-permute-start.10 = (bf16[256,1024]{1,0:T(8,128)(2,1)S(1)}, bf16[256,1024]{1,0:T(8,128)(2,1)S(1)}, u32[]{:S(2)}, u32[]{:S(2)}) collective-permute-start(bf16[256,1024]{1,0:T(8,128)(2,1)S(1)} %get-tuple-element.82), channel_id=1, source_target_pairs={{0,1},{3,2},{4,5},{7,6},{8,9},{11,10},{12,13},{15,14},{16,17},{19,... | collective-permute-start | bytes 1572872 | tf_op jit(solution)/shard_map/ppermute | solution.py:291
  32.3 0.7 collective-permute-start.9
  33.0 1.3 %back.1 = (bf16[96,640]{1,0:T(8,128)(2,1)S(1)}, bf16[96,640]{1,0:T(8,128)(2,1)S(1)}, bf16[96,640]{1,0:T(8,128)(2,1)S(1)}, bf16[96,640]{1,0:T(8,128)(2,1)S(1)}, b...) custom-call(bf16[512,1024]{1,0:T(8,128)(2,1)S(1)} %bitcast.11, ...), custom_call_target="tpu_custom_call" | custom-call | flops 1 | bytes 1 | tf_op jit(solution)/shard_map/back/pallas_call | solution.py:407
  34.3 1.6 %collective-permute-start.7 = (bf16[96,640]{1,0:T(8,128)(2,1)S(1)}, bf16[96,640]{1,0:T(8,128)(2,1)S(1)}, u32[]{:S(2)}, u32[]{:S(2)}) collective-permute-start(bf16[96,640]{1,0:T(8,128)(2,1)S(1)} %get-tuple-element.76), channel_id=1, source_target_pairs={{0,16},{4,20},{8,24},{12,28},{16,0},{20,4},{24,8},{28,12},{1,17},{... | collective-permute-start | bytes 368648 | tf_op jit(solution)/shard_map/ppermute | solution.py:257
  35.9 1.5 %collective-permute-start.8 = (bf16[96,640]{1,0:T(8,128)(2,1)S(1)}, bf16[96,640]{1,0:T(8,128)(2,1)S(1)}, u32[]{:S(2)}, u32[]{:S(2)}) collective-permute-start(bf16[96,640]{1,0:T(8,128)(2,1)S(1)} %get-tuple-element.78), channel_id=1, source_target_pairs={{0,8},{4,12},{8,0},{12,4},{16,24},{20,28},{24,16},{28,20},{1,9},{5... | collective-permute-start | bytes 368648 | tf_op jit(solution)/shard_map/ppermute | solution.py:257
  37.4 2.0 %collective-permute-done.7.refs_0_ = bf16[96,640]{1,0:T(8,128)(2,1)S(1)} collective-permute-done((bf16[96,640]{1,0:T(8,128)(2,1)S(1)}, bf16[96,640]{1,0:T(8,128)(2,1)S(1)}, u32[]{:S(2)}, u32[]{:S(2)}) %collective-permute-start.7) | collective-permute-done | bytes 122912 | tf_op jit(solution)/shard_map/ppermute | solution.py:257
  39.4 1.3 %collective-permute-done.8.refs_1_ = bf16[96,640]{1,0:T(8,128)(2,1)S(1)} collective-permute-done((bf16[96,640]{1,0:T(8,128)(2,1)S(1)}, bf16[96,640]{1,0:T(8,128)(2,1)S(1)}, u32[]{:S(2)}, u32[]{:S(2)}) %collective-permute-start.8) | collective-permute-done | bytes 122912 | tf_op jit(solution)/shard_map/ppermute | solution.py:257
  40.8 2.0 %collective-permute-start.17 = (bf16[256,1024]{1,0:T(8,128)(2,1)S(1)}, bf16[256,1024]{1,0:T(8,128)(2,1)S(1)}, u32[]{:S(2)}, u32[]{:S(2)}) collective-permute-start(bf16[256,1024]{1,0:T(8,128)(2,1)S(1)} %get-tuple-element.102), channel_id=1, source_target_pairs={{0,2},{1,0},{2,3},{3,1},{4,6},{5,4},{6,7},{7,5},{8,10},{9,8},{10,1... | collective-permute-start | bytes 1572872 | tf_op jit(solution)/shard_map/ppermute | solution.py:296
  42.8 1.7 %collective-permute-done.10.inward_ref = bf16[256,1024]{1,0:T(8,128)(2,1)S(1)} collective-permute-done((bf16[256,1024]{1,0:T(8,128)(2,1)S(1)}, bf16[256,1024]{1,0:T(8,128)(2,1)S(1)}, u32[]{:S(2)}, u32[]{:S(2)}) %collective-permute-start.10) | collective-permute-done | bytes 524320 | tf_op jit(solution)/shard_map/ppermute | solution.py:291
  44.7 2.5 %collective-permute-start.18 = (bf16[256,1024]{1,0:T(8,128)(2,1)S(1)}, bf16[256,1024]{1,0:T(8,128)(2,1)S(1)}, u32[]{:S(2)}, u32[]{:S(2)}) collective-permute-start(bf16[256,1024]{1,0:T(8,128)(2,1)S(1)} %get-tuple-element.103), channel_id=1, source_target_pairs={{0,1},{3,2},{1,3},{2,0},{4,5},{7,6},{5,7},{6,4},{8,9},{11,10},{9,1... | collective-permute-start | bytes 1572872 | tf_op jit(solution)/shard_map/ppermute | solution.py:303
  47.3 2.4 %collective-permute-start.11 = (bf16[96,640]{1,0:T(8,128)(2,1)S(1)}, bf16[96,640]{1,0:T(8,128)(2,1)S(1)}, u32[]{:S(2)}, u32[]{:S(2)}) collective-permute-start(bf16[96,640]{1,0:T(8,128)(2,1)S(1)} %get-tuple-element.92), channel_id=1, source_target_pairs={{0,24},{4,28},{8,16},{12,20},{16,8},{20,12},{24,0},{28,4},{1,25},{... | collective-permute-start | bytes 368648 | tf_op jit(solution)/shard_map/ppermute | solution.py:257
  49.7 1.7 %collective-permute-start.13 = (bf16[96,640]{1,0:T(8,128)(2,1)S(1)}, bf16[96,640]{1,0:T(8,128)(2,1)S(1)}, u32[]{:S(2)}, u32[]{:S(2)}) collective-permute-start(bf16[96,640]{1,0:T(8,128)(2,1)S(1)} %get-tuple-element.94), channel_id=1, source_target_pairs={{0,20},{4,16},{8,28},{12,24},{16,4},{20,0},{24,12},{28,8},{1,21},{... | collective-permute-start | bytes 368648 | tf_op jit(solution)/shard_map/ppermute | solution.py:257
  51.4 1.9 %collective-permute-done.11.refs_2_ = bf16[96,640]{1,0:T(8,128)(2,1)S(1)} collective-permute-done((bf16[96,640]{1,0:T(8,128)(2,1)S(1)}, bf16[96,640]{1,0:T(8,128)(2,1)S(1)}, u32[]{:S(2)}, u32[]{:S(2)}) %collective-permute-start.11) | collective-permute-done | bytes 122912 | tf_op jit(solution)/shard_map/ppermute | solution.py:257
  53.4 2.4 %collective-permute-done.12.refs_3_ = bf16[96,640]{1,0:T(8,128)(2,1)S(1)} collective-permute-done((bf16[96,640]{1,0:T(8,128)(2,1)S(1)}, bf16[96,640]{1,0:T(8,128)(2,1)S(1)}, u32[]{:S(2)}, u32[]{:S(2)}) %collective-permute-start.12) | collective-permute-done | bytes 122912 | tf_op jit(solution)/shard_map/ppermute | solution.py:257
  55.8 2.5 %collective-permute-done.13.refs_4_ = bf16[96,640]{1,0:T(8,128)(2,1)S(1)} collective-permute-done((bf16[96,640]{1,0:T(8,128)(2,1)S(1)}, bf16[96,640]{1,0:T(8,128)(2,1)S(1)}, u32[]{:S(2)}, u32[]{:S(2)}) %collective-permute-start.13) | collective-permute-done | bytes 122912 | tf_op jit(solution)/shard_map/ppermute | solution.py:257
  58.2 0.7 collective-permute-start.16
  58.9 2.6 %finish.1 = (bf16[576,512]{1,0:T(8,128)(2,1)}, bf16[576]{0:T(1024)(128)(2,1)}) custom-call(s32[1,576]{1,0:T(1,128)S(1)} %copy-done.6, bf16[576]{0:T(1024)(128)(2,1)S(1)} %copy-done.7, bf16[576,512]{1,0:T(8,128)(2,1)S(1)} %copy-done.2, f32[1,512]{1,0:T(1,128)S(1)} %bitcast.17, bf16[576,512]{1,0:T(8,128)(2,1)S(1)} %copy-done.4, ...), custom_call_target="tpu_custom_call" | custom-call | flops 1 | bytes 1 | tf_op jit(solution)/shard_map/finish/pallas_call | solution.py:427
  61.5 7.6 %collective-permute-done.18.last_ref = bf16[256,1024]{1,0:T(8,128)(2,1)S(1)} collective-permute-done((bf16[256,1024]{1,0:T(8,128)(2,1)S(1)}, bf16[256,1024]{1,0:T(8,128)(2,1)S(1)}, u32[]{:S(2)}, u32[]{:S(2)}) %collective-permute-start.18) | collective-permute-done | bytes 524320 | tf_op jit(solution)/shard_map/ppermute | solution.py:303
  69.2 1.1 %total.1 = (f32[128,1024]{1,0:T(8,128)}, f32[256,512]{1,0:T(8,128)}) custom-call(f32[256,1024]{1,0:T(8,128)S(1)} %get-tuple-element.100.sum_ref, bf16[32,1024]{1,0:T(8,128)(2,1)S(1)} %collective-permute-done.16.below_ref, bf16[256,1024]{1,0:T(8,128)(2,1)S(1)} %collective-permute-done.17.cycle_ref, bf16[256,1024]{1,0:T(8,128)(2,1)S(1)} %collective-permute-done.18.last_ref), custom_call_target="tpu_custom_call" | custom-call | flops 1 | bytes 1 | tf_op jit(solution)/shard_map/total/pallas_call | solution.py:306
  (34 shorter events, 1.0 us)
Async XLA Ops:
  0.6 8.4 %copy-start.2 = (bf16[576,512]{1,0:T(8,128)(2,1)S(1)}, bf16[576,512]{1,0:T(8,128)(2,1)}, u32[]{:S(2)}) copy-start(bf16[576,512]{1,0:T(8,128)(2,1)} %tok_ref.3) | copy-start | bytes 1769476
  0.6 8.4 %copy-start.7 = (bf16[576]{0:T(1024)(128)(2,1)S(1)}, bf16[576]{0:T(1024)(128)(2,1)}, u32[]{:S(2)}) copy-start(bf16[576]{0:T(1024)(128)(2,1)} %gate_ref.3) | copy-start | bytes 3460
  0.7 8.4 %copy-start.8 = (f32[512]{0:T(512)S(1)}, f32[512]{0:T(512)}, u32[]{:S(2)}) copy-start(f32[512]{0:T(512)} %param.8) | copy-start | bytes 6148
  0.7 18.7 %copy-start.1 = (bf16[1,1024,512]{2,1,0:T(8,128)(2,1)S(1)}, bf16[1,1024,512]{2,1,0:T(8,128)(2,1)}, u32[]{:S(2)}) copy-start(bf16[1,1024,512]{2,1,0:T(8,128)(2,1)} %param.10) | copy-start | bytes 3145732
  4.5 14.9 %copy-start = (bf16[1,512,1024]{2,1,0:T(8,128)(2,1)S(1)}, bf16[1,512,1024]{2,1,0:T(8,128)(2,1)}, u32[]{:S(2)}) copy-start(bf16[1,512,1024]{2,1,0:T(8,128)(2,1)} %param.9) | copy-start | bytes 3145732
  4.5 10.8 %collective-permute-start = (bf16[96,1024]{1,0:T(8,128)(2,1)}, bf16[96,1024]{1,0:T(8,128)(2,1)S(1)}, u32[]{:S(2)}, u32[]{:S(2)}) collective-permute-start(bf16[96,1024]{1,0:T(8,128)(2,1)} %get-tuple-element.56), channel_id=1, source_target_pairs={{0,16},{4,20},{8,24},{12,28},{16,0},{20,4},{24,8},{28,12},{1,17},{... | collective-permute-start | bytes 589832 | tf_op jit(solution)/shard_map/ppermute | solution.py:257
  7.5 8.0 %collective-permute-start.1 = (bf16[96,1024]{1,0:T(8,128)(2,1)}, bf16[96,1024]{1,0:T(8,128)(2,1)S(1)}, u32[]{:S(2)}, u32[]{:S(2)}) collective-permute-start(bf16[96,1024]{1,0:T(8,128)(2,1)} %get-tuple-element.57), channel_id=1, source_target_pairs={{0,8},{4,12},{8,0},{12,4},{16,24},{20,28},{24,16},{28,20},{1,9},{5... | collective-permute-start | bytes 589832 | tf_op jit(solution)/shard_map/ppermute | solution.py:257
  9.0 10.3 %collective-permute-start.2 = (bf16[96,1024]{1,0:T(8,128)(2,1)}, bf16[96,1024]{1,0:T(8,128)(2,1)S(1)}, u32[]{:S(2)}, u32[]{:S(2)}) collective-permute-start(bf16[96,1024]{1,0:T(8,128)(2,1)} %get-tuple-element.58), channel_id=1, source_target_pairs={{0,24},{4,28},{8,16},{12,20},{16,8},{20,12},{24,0},{28,4},{1,25},{... | collective-permute-start | bytes 589832 | tf_op jit(solution)/shard_map/ppermute | solution.py:257
  9.0 1.1 %copy-start.3 = (bf16[576,512]{1,0:T(8,128)(2,1)S(1)}, bf16[576,512]{1,0:T(8,128)(2,1)}, u32[]{:S(2)}) copy-start(bf16[576,512]{1,0:T(8,128)(2,1)} %go_ref.3) | copy-start | bytes 1769476
  10.1 0.7 copy-start.5
  12.1 7.2 %collective-permute-start.3 = (bf16[96,1024]{1,0:T(8,128)(2,1)S(1)}, bf16[96,1024]{1,0:T(8,128)(2,1)S(1)}, u32[]{:S(2)}, u32[]{:S(2)}) collective-permute-start(bf16[96,1024]{1,0:T(8,128)(2,1)S(1)} %get-tuple-element.59), channel_id=1, source_target_pairs={{0,4},{4,0},{8,12},{12,8},{16,20},{20,16},{24,28},{28,24},{1,5},{5... | collective-permute-start | bytes 589832 | tf_op jit(solution)/shard_map/ppermute | solution.py:257
  12.2 10.8 %collective-permute-start.4 = (bf16[96,1024]{1,0:T(8,128)(2,1)}, bf16[96,1024]{1,0:T(8,128)(2,1)S(1)}, u32[]{:S(2)}, u32[]{:S(2)}) collective-permute-start(bf16[96,1024]{1,0:T(8,128)(2,1)} %get-tuple-element.63), channel_id=1, source_target_pairs={{0,28},{4,24},{8,20},{12,16},{16,12},{20,8},{24,4},{28,0},{1,29},{... | collective-permute-start | bytes 589832 | tf_op jit(solution)/shard_map/ppermute | solution.py:257
  15.2 11.3 %collective-permute-start.5 = (bf16[96,1024]{1,0:T(8,128)(2,1)S(1)}, bf16[96,1024]{1,0:T(8,128)(2,1)S(1)}, u32[]{:S(2)}, u32[]{:S(2)}) collective-permute-start(bf16[96,1024]{1,0:T(8,128)(2,1)S(1)} %get-tuple-element.66), channel_id=1, source_target_pairs={{0,20},{4,16},{8,28},{12,24},{16,4},{20,0},{24,12},{28,8},{1,21},{... | collective-permute-start | bytes 589832 | tf_op jit(solution)/shard_map/ppermute | solution.py:257
  15.5 10.9 %collective-permute-start.6 = (bf16[96,1024]{1,0:T(8,128)(2,1)S(1)}, bf16[96,1024]{1,0:T(8,128)(2,1)S(1)}, u32[]{:S(2)}, u32[]{:S(2)}) collective-permute-start(bf16[96,1024]{1,0:T(8,128)(2,1)S(1)} %get-tuple-element.67), channel_id=1, source_target_pairs={{0,12},{4,8},{8,4},{12,0},{16,28},{20,24},{24,20},{28,16},{1,13},{... | collective-permute-start | bytes 589832 | tf_op jit(solution)/shard_map/ppermute | solution.py:257
  28.6 15.9 %collective-permute-start.10 = (bf16[256,1024]{1,0:T(8,128)(2,1)S(1)}, bf16[256,1024]{1,0:T(8,128)(2,1)S(1)}, u32[]{:S(2)}, u32[]{:S(2)}) collective-permute-start(bf16[256,1024]{1,0:T(8,128)(2,1)S(1)} %get-tuple-element.82), channel_id=1, source_target_pairs={{0,1},{3,2},{4,5},{7,6},{8,9},{11,10},{12,13},{15,14},{16,17},{19,... | collective-permute-start | bytes 1572872 | tf_op jit(solution)/shard_map/ppermute | solution.py:291
  32.3 10.6 %collective-permute-start.9 = (bf16[224,1024]{1,0:T(8,128)(2,1)S(1)}, bf16[224,1024]{1,0:T(8,128)(2,1)S(1)}, u32[]{:S(2)}, u32[]{:S(2)}) collective-permute-start(bf16[224,1024]{1,0:T(8,128)(2,1)S(1)} %get-tuple-element.81), channel_id=1, source_target_pairs={{1,2},{2,1},{5,6},{6,5},{9,10},{10,9},{13,14},{14,13},{17,18},{18,... | collective-permute-start | bytes 1376264 | tf_op jit(solution)/shard_map/ppermute | solution.py:292
  34.3 5.1 %collective-permute-start.7 = (bf16[96,640]{1,0:T(8,128)(2,1)S(1)}, bf16[96,640]{1,0:T(8,128)(2,1)S(1)}, u32[]{:S(2)}, u32[]{:S(2)}) collective-permute-start(bf16[96,640]{1,0:T(8,128)(2,1)S(1)} %get-tuple-element.76), channel_id=1, source_target_pairs={{0,16},{4,20},{8,24},{12,28},{16,0},{20,4},{24,8},{28,12},{1,17},{... | collective-permute-start | bytes 368648 | tf_op jit(solution)/shard_map/ppermute | solution.py:257
  35.9 4.9 %collective-permute-start.8 = (bf16[96,640]{1,0:T(8,128)(2,1)S(1)}, bf16[96,640]{1,0:T(8,128)(2,1)S(1)}, u32[]{:S(2)}, u32[]{:S(2)}) collective-permute-start(bf16[96,640]{1,0:T(8,128)(2,1)S(1)} %get-tuple-element.78), channel_id=1, source_target_pairs={{0,8},{4,12},{8,0},{12,4},{16,24},{20,28},{24,16},{28,20},{1,9},{5... | collective-permute-start | bytes 368648 | tf_op jit(solution)/shard_map/ppermute | solution.py:257
  40.8 20.8 %collective-permute-start.17 = (bf16[256,1024]{1,0:T(8,128)(2,1)S(1)}, bf16[256,1024]{1,0:T(8,128)(2,1)S(1)}, u32[]{:S(2)}, u32[]{:S(2)}) collective-permute-start(bf16[256,1024]{1,0:T(8,128)(2,1)S(1)} %get-tuple-element.102), channel_id=1, source_target_pairs={{0,2},{1,0},{2,3},{3,1},{4,6},{5,4},{6,7},{7,5},{8,10},{9,8},{10,1... | collective-permute-start | bytes 1572872 | tf_op jit(solution)/shard_map/ppermute | solution.py:296
  44.5 14.4 %copy-start.4 = (bf16[576,512]{1,0:T(8,128)(2,1)S(1)}, bf16[576,512]{1,0:T(8,128)(2,1)}, u32[]{:S(2)}) copy-start(bf16[576,512]{1,0:T(8,128)(2,1)} %go_ref.3) | copy-start | bytes 1769476
  44.7 14.2 %copy-start.6 = (s32[1,576]{1,0:T(1,128)S(1)}, s32[1,576]{1,0:T(1,128)}, u32[]{:S(2)}) copy-start(s32[1,576]{1,0:T(1,128)} %get-tuple-element.55.target_ref) | copy-start | bytes 6916
  44.7 24.4 %collective-permute-start.18 = (bf16[256,1024]{1,0:T(8,128)(2,1)S(1)}, bf16[256,1024]{1,0:T(8,128)(2,1)S(1)}, u32[]{:S(2)}, u32[]{:S(2)}) collective-permute-start(bf16[256,1024]{1,0:T(8,128)(2,1)S(1)} %get-tuple-element.103), channel_id=1, source_target_pairs={{0,1},{3,2},{1,3},{2,0},{4,5},{7,6},{5,7},{6,4},{8,9},{11,10},{9,1... | collective-permute-start | bytes 1572872 | tf_op jit(solution)/shard_map/ppermute | solution.py:303
  47.3 6.1 %collective-permute-start.11 = (bf16[96,640]{1,0:T(8,128)(2,1)S(1)}, bf16[96,640]{1,0:T(8,128)(2,1)S(1)}, u32[]{:S(2)}, u32[]{:S(2)}) collective-permute-start(bf16[96,640]{1,0:T(8,128)(2,1)S(1)} %get-tuple-element.92), channel_id=1, source_target_pairs={{0,24},{4,28},{8,16},{12,20},{16,8},{20,12},{24,0},{28,4},{1,25},{... | collective-permute-start | bytes 368648 | tf_op jit(solution)/shard_map/ppermute | solution.py:257
  49.7 6.1 %collective-permute-start.12 = (bf16[96,640]{1,0:T(8,128)(2,1)S(1)}, bf16[96,640]{1,0:T(8,128)(2,1)S(1)}, u32[]{:S(2)}, u32[]{:S(2)}) collective-permute-start(bf16[96,640]{1,0:T(8,128)(2,1)S(1)} %get-tuple-element.93), channel_id=1, source_target_pairs={{0,28},{4,24},{8,20},{12,16},{16,12},{20,8},{24,4},{28,0},{1,29},{... | collective-permute-start | bytes 368648 | tf_op jit(solution)/shard_map/ppermute | solution.py:257
  49.7 8.5 %collective-permute-start.13 = (bf16[96,640]{1,0:T(8,128)(2,1)S(1)}, bf16[96,640]{1,0:T(8,128)(2,1)S(1)}, u32[]{:S(2)}, u32[]{:S(2)}) collective-permute-start(bf16[96,640]{1,0:T(8,128)(2,1)S(1)} %get-tuple-element.94), channel_id=1, source_target_pairs={{0,20},{4,16},{8,28},{12,24},{16,4},{20,0},{24,12},{28,8},{1,21},{... | collective-permute-start | bytes 368648 | tf_op jit(solution)/shard_map/ppermute | solution.py:257
  53.4 5.5 %collective-permute-start.14 = (bf16[96,640]{1,0:T(8,128)(2,1)S(1)}, bf16[96,640]{1,0:T(8,128)(2,1)S(1)}, u32[]{:S(2)}, u32[]{:S(2)}) collective-permute-start(bf16[96,640]{1,0:T(8,128)(2,1)S(1)} %get-tuple-element.95), channel_id=1, source_target_pairs={{0,12},{4,8},{8,4},{12,0},{16,28},{20,24},{24,20},{28,16},{1,13},{... | collective-permute-start | bytes 368648 | tf_op jit(solution)/shard_map/ppermute | solution.py:257
  55.8 3.1 %collective-permute-start.15 = (bf16[96,640]{1,0:T(8,128)(2,1)S(1)}, bf16[96,640]{1,0:T(8,128)(2,1)S(1)}, u32[]{:S(2)}, u32[]{:S(2)}) collective-permute-start(bf16[96,640]{1,0:T(8,128)(2,1)S(1)} %get-tuple-element.96), channel_id=1, source_target_pairs={{0,4},{4,0},{8,12},{12,8},{16,20},{20,16},{24,28},{28,24},{1,5},{5... | collective-permute-start | bytes 368648 | tf_op jit(solution)/shard_map/ppermute | solution.py:257
  58.2 3.3 %collective-permute-start.16 = (bf16[32,1024]{1,0:T(8,128)(2,1)S(1)}, bf16[32,1024]{1,0:T(8,128)(2,1)S(1)}, u32[]{:S(2)}, u32[]{:S(2)}) collective-permute-start(bf16[32,1024]{1,0:T(8,128)(2,1)S(1)} %get-tuple-element.101), channel_id=1, source_target_pairs={{1,2},{2,1},{5,6},{6,5},{9,10},{10,9},{13,14},{14,13},{17,18},{18,... | collective-permute-start | bytes 196616 | tf_op jit(solution)/shard_map/ppermute | solution.py:293
